TPU v7x, 32 devices: a whole 2x2x4 slice. The times are simulated.
32 devices in a mesh: blk: 4 (over x, core), site: 8 (over z, y).
Axes of the slice: x: 2, y: 2, z: 4, core: 2. Of those that a mesh axis runs over, the one named last changes fastest.
Arguments:
- modes: bfloat16 [2, 1, 256, 12, 1024], P(None, None, 'blk', None, 'site'), may hold values from -0.75 to 0.75
- momenta: int32 [4, 3], replicated, may hold values from -2 to 2
Outputs:
- meson_field: float32 [128, 256, 256], P('site', 'blk')
All inputs are finite; a program needn't handle non-finite values.
Results may differ from a plain program's by a relative error of at most 0.0027.
Values may be sent and summed in bfloat16 or wider, within the bound.
No kernel may reach another device: no remote copies, remote signals or barrier semaphores. Data moves between devices by JAX's collectives and lax.ppermute only.
A program may use at most 128 MiB of HBM per device.

v0:
```python
import math

import jax
import jax.numpy as jnp
from jax import lax
from jax.sharding import PartitionSpec as P

LEXT = 48


TWO_PI = 2.0 * math.pi


def from_behind(shard, axis, by):
    devices = lax.axis_size(axis)
    return lax.ppermute(shard, axis, [(i, (i + by) % devices) for i in range(devices)])


def phase_table(momenta, first_site, site_count, extent):
    flat = first_site + jnp.arange(site_count, dtype=jnp.int32)
    coords = jnp.stack([flat % extent, flat // extent % extent, flat // (extent * extent)], 0)
    turns = jnp.mod(jnp.sum(momenta[:, :, None] * coords[None, :, :], axis=1), extent)
    angle = turns.astype(jnp.float32) * (TWO_PI / extent)
    return jnp.stack([jnp.cos(angle), jnp.sin(angle)], 1)


def apply_phase(fields, weights):
    scaled = (
        fields.astype(jnp.float32)[:, :, None, None]
        * weights[None, None, :, :, None, None, None, :]
    )
    return scaled.astype(jnp.bfloat16)


def rotate_left(phased):
    second = phased[:, :, :, 1]
    turned = jnp.stack([-second[1], second[0]], 0)
    return jnp.stack([phased[:, :, :, 0], turned], 3)


def extend(part):
    turned = jnp.stack([-part[1], part[0]], 0)
    return jnp.stack([part, turned], 0)


def conj_phased(phased):
    steps = phased.shape[1]
    grown = jnp.transpose(extend(phased), (2, 3, 4, 5, 6, 0, 1, 7, 8))
    return grown.reshape(steps, -1, 6 * phased.shape[-1])


def plain_side(fields):
    steps = fields.shape[1]
    return jnp.transpose(fields, (1, 2, 3, 0, 4, 5)).reshape(steps, -1, 6 * fields.shape[-1])


def batched_dot(first, second):
    return lax.dot_general(
        first, second, (((2,), (2,)), ((0,), (0,))), preferred_element_type=jnp.float32
    )


def split_terms(result):
    cosine_term = result[:, :, :, 0]
    sine_term = result[:, :, :, 1]
    column = jnp.arange(result.shape[-1], dtype=jnp.int32)
    signs = (1 - 2 * (column % 2)).astype(jnp.float32)
    return (cosine_term + sine_term, (cosine_term - sine_term) * signs)


def left_terms(left_own, moving, nmom):
    result = batched_dot(plain_side(moving), left_own)
    return split_terms(result.reshape(result.shape[0], result.shape[1], nmom, 2, -1))


def shards(modes, momenta):
    count = lax.axis_size("blk")
    half = count // 2
    here = lax.axis_index("blk")
    slots, steps, per_block, spin_colour, site_count = modes.shape
    nmom = momenta.shape[0]
    rows = steps * nmom * 32
    first_site = lax.axis_index("site") * site_count
    weights = phase_table(momenta, first_site, site_count, LEXT)
    fields = modes.reshape(slots, steps, per_block, 4, 3, site_count)
    left_own = conj_phased(rotate_left(apply_phase(fields, weights)))
    kept_list = []
    kept_slots = []
    pieces = []
    offsets = []
    kept_list.append(left_terms(left_own, fields, nmom)[0])
    kept_slots.append(0)
    moving = fields
    for dist in range(1, half + 1):
        moving = from_behind(moving, "blk", 1)
        kept, mirror = left_terms(left_own, moving, nmom)
        kept_list.append(kept)
        kept_slots.append(-dist % count)
        if dist < half:
            pieces.append(mirror)
            offsets.append(-dist)
    square = per_block * per_block
    kept_stack = jnp.stack(kept_list, 0).reshape(
        len(kept_list), steps, per_block, 4, nmom, per_block, 4, 2
    )
    kept_stack = jnp.transpose(kept_stack, (1, 4, 6, 3, 7, 0, 5, 2)).reshape(
        rows, len(kept_list), square
    )
    mirror_stack = jnp.stack(pieces, 0).reshape(
        len(pieces), steps, per_block, 4, nmom, per_block, 4, 2
    )
    mirror_stack = jnp.transpose(mirror_stack, (1, 4, 3, 6, 7, 0, 2, 5)).reshape(
        rows, len(pieces), square
    )
    kept_part, mirror_part = (
        lax.psum_scatter(kept_stack, "site", scatter_dimension=0, tiled=True),
        lax.psum_scatter(mirror_stack, "site", scatter_dimension=0, tiled=True),
    )
    share = kept_part.shape[0]
    empty = jnp.zeros((share, square), jnp.float32)
    placed = [empty] * count
    for index, slot in enumerate(kept_slots):
        placed[slot] = kept_part[:, index]
    for index, offset in enumerate(offsets):
        arrived = from_behind(mirror_part[:, index], "blk", offset)
        placed[-offset % count] = arrived
    whole = jnp.roll(jnp.stack(placed, 1), here, axis=1)
    whole = whole.reshape(share, count, per_block, per_block)
    return jnp.transpose(whole, (0, 2, 1, 3)).reshape(share, per_block, count * per_block)


def solution(mesh):
    placed = (P(None, None, "blk", None, "site"), P())
    return jax.shard_map(
        shards, mesh=mesh, in_specs=placed, out_specs=P("site", "blk", None), check_vma=False
    )
```

profile of v0, /device:TPU:0, one launch (start us, length us, event | category | flops | bytes accessed | tf_op | source)
XLA Modules:
  0.0 761.6 jit_solution(11874576488704781957)
XLA Ops:
  6.5 0.0 reduce-scatter.5.cloned.1.call-start
  6.5 1.3 copy.104
  7.9 0.5 collective-permute-start
  8.4 0.8 copy.73
  9.2 0.1 multiply_reduce_fusion
  9.3 0.1 fusion.16
  9.4 1.3 copy.72
  10.7 1.8 multiply_convert_fusion
  12.5 0.8 fusion.8
  13.3 1.5 maximum_bitcast_fusion.3
  14.8 3.6 fusion
  18.4 3.2 fusion.2
  21.6 0.1 copy.89
  21.7 0.0 copy-start
  21.7 4.7 maximum_bitcast_fusion.2
  26.4 0.0 copy-done
  26.4 6.6 maximum_bitcast_fusion.1
  33.1 16.5 %reshape.342 = bf16[4096,768]{1,0:T(8,128)(2,1)} reshape(bf16[1,4,2,64,4,2,2,3,128]{8,7,6,5,4,3,2,1,0:T(4,128)(2,1)} %maximum_bitcast_fusion.1) | data formatting | bytes 12582912 | tf_op jit(solution)/shard_map/reshape.6
  49.6 0.0 collective-permute-done
  49.6 0.3 reshape.346
  49.9 4.6 fusion.20
  54.5 1.8 fusion.6
  56.3 70.6 %sub.42 = f32[1,1,64,4,4,64,4,2]{3,2,7,6,5,4,1,0:T(8,128)} reshape(f32[1,256,4,1,512]{1,4,2,3,0:T(8,128)S(1)} %get-tuple-element.5) | data formatting | bytes 4194304 | tf_op jit(solution)/shard_map/sub | solution.py:68
  126.9 44.5 %multiply_bitcast_fusion = f32[1,4,4,4,2,1,64,64]{2,6,4,3,7,1,0,5:T(8,128)} fusion(f32[1,1,64,4,4,64,4,2]{3,2,7,6,5,4,1,0:T(8,128)} %sub.42, f32[64,4,2]{2,1,0:T(4,128)S(1)} %copy.89), kind=kLoop, calls=%fused_computation | loop fusion | flops 524288 | bytes 4196352 | tf_op jit(solution)/shard_map/transpose | solution.py:112
  171.3 46.5 %copy.90 = f32[1,4,4,4,2,1,64,64]{7,6,4,3,2,1,5,0:T(8,128)} copy(f32[1,4,4,4,2,1,64,64]{2,6,4,3,7,1,0,5:T(8,128)} %multiply_bitcast_fusion) | data formatting | bytes 4194304 | tf_op jit(solution)/shard_map/transpose | solution.py:112
  217.8 4.8 reshape.351
  222.6 0.0 reduce-scatter.5.cloned.1.call-update
  222.6 0.0 reduce-scatter.3.cloned.1.call-start
  222.7 0.3 reshape.344
  223.0 2.9 collective-permute-start.1
  225.9 4.6 fusion.19
  230.5 0.3 fusion.5
  230.8 70.6 %add.158 = f32[1,1,64,4,4,64,4,2]{3,2,7,6,5,4,1,0:T(8,128)} reshape(f32[1,256,4,1,512]{1,4,2,3,0:T(8,128)S(1)} %fusion.5) | data formatting | bytes 4194304 | tf_op jit(solution)/shard_map/add | solution.py:68
  301.4 0.0 copy-start.1
  301.4 46.6 %copy.85 = f32[1,1,64,4,4,64,4,2]{5,2,7,6,4,3,1,0:T(8,128)} copy(f32[1,1,64,4,4,64,4,2]{3,2,7,6,5,4,1,0:T(8,128)} %add.158) | data formatting | bytes 4194304 | tf_op jit(solution)/shard_map/add | solution.py:68
  348.0 0.0 copy-done.1
  348.1 70.6 %add.160 = f32[1,1,64,4,4,64,4,2]{3,2,7,6,5,4,1,0:T(8,128)} reshape(f32[1,256,4,1,512]{1,4,2,3,0:T(8,128)S(1)} %copy-done.1) | data formatting | bytes 4194304 | tf_op jit(solution)/shard_map/add | solution.py:68
  418.6 46.5 %copy.86 = f32[1,1,64,4,4,64,4,2]{5,2,7,6,4,3,1,0:T(8,128)} copy(f32[1,1,64,4,4,64,4,2]{3,2,7,6,5,4,1,0:T(8,128)} %add.160) | data formatting | bytes 4194304 | tf_op jit(solution)/shard_map/add | solution.py:68
  465.1 0.0 collective-permute-done.1
  465.1 0.3 reshape.348
  465.4 4.6 fusion.21
  470.1 0.3 fusion.4
  470.4 70.6 %add.162 = f32[1,1,64,4,4,64,4,2]{3,2,7,6,5,4,1,0:T(8,128)} reshape(f32[1,256,4,1,512]{1,4,2,3,0:T(8,128)S(1)} %fusion.4) | data formatting | bytes 4194304 | tf_op jit(solution)/shard_map/add | solution.py:68
  541.0 46.5 %copy.87 = f32[1,1,64,4,4,64,4,2]{5,2,7,6,4,3,1,0:T(8,128)} copy(f32[1,1,64,4,4,64,4,2]{3,2,7,6,5,4,1,0:T(8,128)} %add.162) | data formatting | bytes 4194304 | tf_op jit(solution)/shard_map/add | solution.py:68
  587.4 12.2 %maximum_bitcast_fusion = f32[1,4,4,4,2,3,64,64]{6,7,4,2,1,3,0,5:T(8,128)} fusion(f32[1,1,64,4,4,64,4,2]{5,2,7,6,4,3,1,0:T(8,128)} %copy.87, f32[1,1,64,4,4,64,4,2]{5,2,7,6,4,3,1,0:T(8,128)} %copy.86, f32[1,1,64,4,4,64,4,2]{5,2,7,6,4,3,1,0:T(8,128)} %copy.85), kind=kLoop, calls=%fused_computation.1 | loop fusion | flops 3145728 | bytes 12582912 | tf_op jit(solution)/shard_map/transpose | solution.py:106
  599.6 12.6 %copy.88 = f32[1,4,4,4,2,3,64,64]{7,6,4,3,2,1,5,0:T(8,128)} copy(f32[1,4,4,4,2,3,64,64]{6,7,4,2,1,3,0,5:T(8,128)} %maximum_bitcast_fusion) | data formatting | bytes 12582912 | tf_op jit(solution)/shard_map/transpose | solution.py:106
  612.2 10.8 %reshape.350 = f32[128,3,4096]{2,0,1:T(8,128)} reshape(f32[1,4,4,4,2,3,64,64]{7,6,4,3,2,1,5,0:T(8,128)} %copy.88) | data formatting | bytes 12582912 | tf_op jit(solution)/shard_map/reshape | solution.py:106
  623.0 0.0 reduce-scatter.3.cloned.1.call-update
  623.1 0.0 reduce-scatter.5.cloned.1.call-done
  623.1 0.3 collective-permute-start.2
  623.4 118.5 %reduce-scatter.3.cloned.1.call-done = f32[16,3,4096]{2,0,1:T(8,128)} async-done(((f32[128,3,4096]{2,0,1:T(8,128)}), f32[16,3,4096]{2,0,1:T(8,128)}) %reduce-scatter.3.cloned.1.call-update) | async-done | bytes 786448 | tf_op jit(solution)/shard_map/reduce_scatter | solution.py:116
  741.9 1.0 slice_dynamic-update-slice_fusion.4
  742.9 0.0 collective-permute-done.2
  743.0 1.0 slice_dynamic-update-slice_fusion.2
  743.9 1.0 slice_dynamic-update-slice_fusion
  744.9 1.0 slice_dynamic-update-slice_fusion.5
  745.9 1.0 slice_dynamic-update-slice_fusion.3
  746.9 1.0 slice_dynamic-update-slice_fusion.1
  747.8 0.1 constant_dynamic-slice_fusion
  747.9 0.8 reshape.352
  748.8 2.8 copy.91
  751.5 3.2 reshape.353
  (7 shorter events, 0.1 us)
Async XLA Ops:
  6.5 616.6 %reduce-scatter.5.cloned.1.call-start = ((), (), s32[]{:S(2)}) async-start(), calls=%async_computation.3 | async-start | bytes 2359296 | tf_op jit(solution)/shard_map/reduce_scatter | solution.py:117
  7.9 41.7 %collective-permute-start = (bf16[2,1,64,4,3,128]{5,4,0,3,2,1:T(4,128)(2,1)S(1)}, bf16[2,1,64,4,3,128]{5,4,0,3,2,1:T(4,128)(2,1)S(1)}, u32[]{:S(2)}, u32[]{:S(2)}) collective-permute-start(bf16[2,1,64,4,3,128]{5,4,0,3,2,1:T(4,128)(2,1)S(1)} %copy.104), channel_id=1, source_target_pairs={{0,8},{8,16},{16,24},{24,0},{1,9},{9,17},{17,25},{25,1},{2,10},{10... | collective-permute-start | bytes 1179656 | tf_op jit(solution)/shard_map/ppermute | solution.py:16
  21.7 4.7 copy-start
  222.6 519.3 %reduce-scatter.3.cloned.1.call-start = ((), (), s32[]{:S(2)}) async-start(), calls=%async_computation.2 | async-start | bytes 7077888 | tf_op jit(solution)/shard_map/reduce_scatter | solution.py:116
  223.0 242.1 %collective-permute-start.1 = (bf16[2,1,64,4,3,128]{5,4,0,3,2,1:T(4,128)(2,1)S(1)}, bf16[2,1,64,4,3,128]{5,4,0,3,2,1:T(4,128)(2,1)S(1)}, u32[]{:S(2)}, u32[]{:S(2)}) collective-permute-start(bf16[2,1,64,4,3,128]{5,4,0,3,2,1:T(4,128)(2,1)S(1)} %collective-permute-done), channel_id=1, source_target_pairs={{0,8},{8,16},{16,24},{24,0},{1,9},{9,17},{17,25},{25,1},{2,10},{10... | collective-permute-start | bytes 1179656 | tf_op jit(solution)/shard_map/ppermute | solution.py:16
  301.4 46.6 %copy-start.1 = (f32[1,256,4,1,512]{1,4,2,3,0:T(8,128)S(1)}, f32[1,256,4,1,512]{1,4,2,3,0:T(8,128)}, u32[]{:S(2)}) copy-start(f32[1,256,4,1,512]{1,4,2,3,0:T(8,128)} %get-tuple-element.6) | copy-start | bytes 6291460
  623.1 119.8 %collective-permute-start.2 = (f32[16,4096]{1,0:T(8,128)}, f32[16,4096]{1,0:T(8,128)S(1)}, u32[]{:S(2)}, u32[]{:S(2)}) collective-permute-start(f32[16,4096]{1,0:T(8,128)} %bitcast.125), channel_id=1, source_target_pairs={{0,24},{8,0},{16,8},{24,16},{1,25},{9,1},{17,9},{25,17},{2,26},{10... | collective-permute-start | bytes 786440 | tf_op jit(solution)/shard_map/ppermute | solution.py:16
Sparse Core Ops, SparseCore 0:
  222.8 70.2 reduce-scatter.4
  623.2 118.7 reduce-scatter.2
where the time goes:
time: 766 us; the launch traced here: 762 us
  local copies, waits for them, and re-layouts  530 us (69%)
  waiting for transfers between devices  119 us (16%)
  other arithmetic  81.4 us (11%)
  matrix products  13.9 us (2%)
  between operations  13.6 us (2%)
    add x6, local copies, waits for them, and re-layouts, split_terms(): return (cosine_term + sine_term, (cosine_term - sine_term) * signs)  351 us
    reduce_scatter x1, waiting for transfers between devices, shards(): lax.psum_scatter(kept_stack, 'site', scatter_dimension=0, tiled=True)  119 us
    sub x1, local copies, waits for them, and re-layouts, split_terms(): return (cosine_term + sine_term, (cosine_term - sine_term) * signs)  70.6 us
    transpose x1, local copies, waits for them, and re-layouts, shards(): jnp.transpose(mirror_stack, (1, 4, 3, 6, 7, 0, 2, 5))  46.5 us
    transpose x1, other arithmetic, shards(): jnp.transpose(mirror_stack, (1, 4, 3, 6, 7, 0, 2, 5))  44.5 us
    another operation x4, local copies, waits for them, and re-layouts  17.5 us
  transfers between devices with their start and end apart: 5, of which 1 were waited for; matrix products, arithmetic and copies ran while one was open for 58% of the time, Pallas kernels for 0%

commit v1 on v0

v1 whole, which is shorter than its diff:
```python
import functools
import math

import jax
import jax.numpy as jnp
from jax import lax
from jax.experimental import pallas as pl
from jax.experimental.pallas import tpu as pltpu
from jax.sharding import Mesh, PartitionSpec as P

LEXT = 48

TWO_PI = 2.0 * math.pi


def phase_table(momenta, first_site, site_count, extent):
    flat = first_site + jnp.arange(site_count, dtype=jnp.int32)
    coords = jnp.stack([flat % extent, flat // extent % extent, flat // (extent * extent)], 0)
    turns = jnp.mod(jnp.sum(momenta[:, :, None] * coords[None, :, :], axis=1), extent)
    angle = turns.astype(jnp.float32) * (TWO_PI / extent)
    return jnp.stack([jnp.cos(angle), jnp.sin(angle)], 1)


def left_sides(left_ref, weights_ref):
    spins, depth = left_ref.shape[2], left_ref.shape[4]
    half = depth // 2
    cosine = jnp.tile(weights_ref[0, 0:1], (1, depth // weights_ref.shape[-1]))
    sine = jnp.tile(weights_ref[0, 1:2], (1, depth // weights_ref.shape[-1]))
    cosine_rows = [[], []]
    sine_rows = [[], []]
    for spin in range(spins):
        own = left_ref[0, 0, spin].astype(jnp.float32)
        by_cos = (own * cosine).astype(jnp.bfloat16)
        by_sin = (own * sine).astype(jnp.bfloat16)
        cosine_rows[0].append(by_cos)
        cosine_rows[1].append(jnp.concatenate([-by_cos[:, half:], by_cos[:, :half]], 1))
        sine_rows[0].append(jnp.concatenate([-by_sin[:, half:], by_sin[:, :half]], 1))
        sine_rows[1].append(-by_sin)
    return (
        jnp.concatenate(cosine_rows[0] + cosine_rows[1], 0),
        jnp.concatenate(sine_rows[0] + sine_rows[1], 0),
    )


def add_terms(place_ref, weights_ref, left_ref, right_ref, field_ref):
    @pl.when(pl.program_id(0) == 0)
    def _():
        field_ref[...] = jnp.zeros_like(field_ref)

    spins = left_ref.shape[2]
    groups, columns, per_block, depth = right_ref.shape[0], *right_ref.shape[2:]
    left_cos, left_sin = left_sides(left_ref, weights_ref)
    dims = (((1,), (1,)), ((), ()))
    for column in range(columns):
        right = right_ref[:, 0, column].reshape(groups * per_block, depth)
        term = lax.dot_general(
            left_cos, right, dims, preferred_element_type=jnp.float32
        ) + lax.dot_general(left_sin, right, dims, preferred_element_type=jnp.float32)
        for part in range(2):
            for spin in range(spins):
                start = (part * spins + spin) * per_block
                field_ref[(spin * columns + column) * 2 + part] += term[start : start + per_block]


def add_terms_and_place(
    place_ref, weights_ref, left_ref, right_ref, near_ref, field_ref, total_ref
):
    add_terms(place_ref, weights_ref, left_ref, right_ref, total_ref)

    @pl.when(pl.program_id(0) == pl.num_programs(0) - 1)
    def _():
        per_block = near_ref.shape[1]
        first = place_ref[3] == 0
        for row in range(near_ref.shape[0]):
            near, far = near_ref[row], total_ref[row]
            even, odd = jnp.where(first, near, far), jnp.where(first, far, near)
            pieces = []
            for start in range(0, near.shape[1], per_block):
                pieces += [even[:, start : start + per_block], odd[:, start : start + per_block]]
            field_ref[row] = jnp.concatenate(pieces, 1)


def shards(modes, momenta):
    groups = lax.axis_size("pair")
    sites = lax.axis_size("site")
    slots, steps, per_block, spin_colour, site_count = modes.shape
    nmom = momenta.shape[0]
    share = steps * nmom * 32 // sites
    columns = min(4, share // 2)
    spins = share // (2 * columns)
    owned = lax.axis_index("site") * (share // 2)
    place = jnp.stack(
        [
            lax.axis_index("pair"),
            owned // 4 % 4 // spins,
            owned % 4 // columns,
            lax.axis_index("core"),
        ]
    ).astype(jnp.int32)

    packed = jnp.transpose(modes.reshape(slots, per_block, 4, 3, site_count), (2, 1, 0, 3, 4))
    packed = packed.reshape(4, per_block, slots * 3 * site_count)
    depth = packed.shape[-1]
    near = lax.all_gather(packed, ("pair", "site"))
    near = near.reshape(groups, sites, 4, per_block, depth)
    far = lax.ppermute(near, "core", [(0, 1), (1, 0)])

    mine = lax.dynamic_slice_in_dim(momenta, owned // 16, 1, 0)
    weights = phase_table(mine, jnp.int32(0), sites * site_count, LEXT)[0]
    weights = jnp.transpose(weights.reshape(2, sites, site_count), (1, 0, 2))

    wide = groups * per_block
    in_specs = [
        pl.BlockSpec((1, 2, site_count), lambda m, place: (m, 0, 0)),
        pl.BlockSpec(
            (1, 1, spins, per_block, depth), lambda m, place: (place[0], m, place[1], 0, 0)
        ),
        pl.BlockSpec(
            (groups, 1, columns, per_block, depth), lambda m, place: (0, m, place[2], 0, 0)
        ),
    ]
    estimate = pl.CostEstimate(
        flops=4 * share * per_block * wide * depth * sites,
        bytes_accessed=wide * sites * 4 * depth * 2,
        transcendentals=0,
    )
    params = pltpu.CompilerParams(vmem_limit_bytes=56 * 1024 * 1024)
    half = pl.pallas_call(
        add_terms,
        grid_spec=pltpu.PrefetchScalarGridSpec(
            num_scalar_prefetch=1,
            grid=(sites,),
            in_specs=in_specs,
            out_specs=pl.BlockSpec((share, per_block, wide), lambda m, place: (0, 0, 0)),
        ),
        out_shape=jax.ShapeDtypeStruct((share, per_block, wide), jnp.float32),
        compiler_params=params,
        cost_estimate=estimate,
    )(place, weights, near, near)
    return pl.pallas_call(
        add_terms_and_place,
        grid_spec=pltpu.PrefetchScalarGridSpec(
            num_scalar_prefetch=1,
            grid=(sites,),
            in_specs=in_specs
            + [pl.BlockSpec((share, per_block, wide), lambda m, place: (0, 0, 0))],
            out_specs=pl.BlockSpec((share, per_block, 2 * wide), lambda m, place: (0, 0, 0)),
            scratch_shapes=[pltpu.VMEM((share, per_block, wide), jnp.float32)],
        ),
        out_shape=jax.ShapeDtypeStruct((share, per_block, 2 * wide), jnp.float32),
        compiler_params=params,
        cost_estimate=estimate,
    )(place, weights, near, far, half)


def solution(mesh):
    count = mesh.shape["blk"]
    split = Mesh(mesh.devices.reshape(count // 2, 2, -1), ("pair", "core", "site"))
    placed = (P(None, None, ("pair", "core"), None, "site"), P())
    return jax.shard_map(
        shards,
        mesh=split,
        in_specs=placed,
        out_specs=P("site", ("pair", "core"), None),
        check_vma=False,
    )
```

time: 766 us -> 140 us (0.18)
  local copies, waits for them, and re-layouts: 530 us -> 2.44 us
  other arithmetic: 81.4 us -> 1.54 us
  Pallas kernels: 0 us -> 23.8 us
  waiting for transfers between devices: 119 us -> 98.1 us
  matrix products: 13.9 us -> 0 us
    add x6 -> x0, local copies, waits for them, and re-layouts: 351 us -> none  [split_terms(): return (cosine_term + sine_term, (cosine_term - sine_term) * signs)]
    reduce_scatter x2 -> x0, waiting for transfers between devices: 119 us -> none  [the longest x1 119 us: shards(): lax.psum_scatter(kept_stack, 'site', scatter_dimension=0, tiled=True)]
    all_gather x0 -> x1, waiting for transfers between devices: none -> 98 us  [shards(): near = lax.all_gather(packed, ('pair', 'site'))]
    sub x1 -> x0, local copies, waits for them, and re-layouts: 70.6 us -> none  [split_terms(): return (cosine_term + sine_term, (cosine_term - sine_term) * signs)]
    transpose x3 -> x1, other arithmetic: 63.3 us -> 0.61 us  [shards(): weights = jnp.transpose(weights.reshape(2, sites, site_count), (1, 0, 2))]
    transpose x3 -> x0, local copies, waits for them, and re-layouts: 61.9 us -> none  [the longest x1 46.5 us: shards(): jnp.transpose(mirror_stack, (1, 4, 3, 6, 7, 0, 2, 5))]
    pallas_call x0 -> x2, Pallas kernels: none -> 23.8 us  [the longest x1 12.2 us: shards(): pl.pallas_call(add_terms_and_place, grid_spec=pltpu.PrefetchScalarGridSpe...]
    reshape x5 -> x1, local copies, waits for them, and re-layouts: 21 us -> 1.35 us  [shards(): modes.reshape(slots, per_block, 4, 3, site_count)]
  transfers between devices with their start and end apart: 5 -> 2, of which waited for: 1 -> 1; matrix products, arithmetic and copies ran while one was open for 58% -> 1% of each run, Pallas kernels for 0% -> 8%
where the time goes in v1:
time: 140 us; the launch traced here: 139 us
  waiting for transfers between devices  98.1 us (70%)
  Pallas kernels  23.8 us (17%)
  between operations  13.4 us (10%)
  local copies, waits for them, and re-layouts  2.44 us (2%)
  other arithmetic  1.54 us (1%)
    all_gather x1, waiting for transfers between devices, shards(): near = lax.all_gather(packed, ('pair', 'site'))  98 us
    pallas_call x1, Pallas kernels, shards(): pl.pallas_call(add_terms_and_place, grid_spec=pltpu.PrefetchScalarGridSpe...  12.2 us
    pallas_call x1, Pallas kernels, shards(): pl.pallas_call(add_terms, grid_spec=pltpu.PrefetchScalarGridSpec(num_scal...  11.6 us
  transfers between devices with their start and end apart: 2, of which 1 were waited for; matrix products, arithmetic and copies ran while one was open for 1% of the time, Pallas kernels for 8%

profile of v1, /device:TPU:0, one launch (start us, length us, event | category | flops | bytes accessed | tf_op | source)
XLA Modules:
  0.0 139.2 jit_solution(5783011757030501977)
XLA Ops:
  6.5 0.0 copy-start
  6.5 0.0 all-gather.2.cloned.1.call-start
  6.5 1.3 copy.10
  7.9 1.1 all_gather_reshape.3
  9.0 0.0 all-gather.2.cloned.1.call-update
  9.0 98.0 %all-gather.2.cloned.1.call-done = bf16[16,4,64,768]{3,2,1,0:T(8,128)(2,1)} async-done(((bf16[1,4,64,768]{3,2,1,0:T(8,128)(2,1)}), bf16[16,4,64,768]{3,2,1,0:T(8,128)(2,1)}) %all-gather.2.cloned.1.call-update) | async-done | bytes 6291472 | tf_op jit(solution)/shard_map/all_gather | solution.py:104
  107.0 0.0 collective-permute-start
  107.0 0.0 copy-done
  107.0 0.7 pad_add_fusion.place_ref
  107.7 0.1 fusion
  107.9 0.1 multiply_cosine_fusion
  108.0 0.6 maximum_bitcast_fusion.weights_ref
  108.6 11.6 %shard_map.28.near_ref = f32[16,64,128]{2,1,0:T(8,128)} custom-call(s32[4]{0:T(128)} %pad_add_fusion.place_ref, f32[8,2,128]{2,1,0:T(2,128)} %maximum_bitcast_fusion.weights_ref, bf16[2,8,4,64,768]{4,3,2,1,0:T(8,128)(2,1)} %bitcast.31, bf16[2,8,4,64,768]{4,3,2,1,0:T(8,128)(2,1)} %bitcast.32), custom_call_target="tpu_custom_call" | custom-call | flops 3221225472 | bytes 6291456 | tf_op jit(solution)/shard_map/pallas_call | solution.py:128
  120.2 0.0 collective-permute-done.right_ref
  120.2 12.2 %shard_map.29 = f32[16,64,256]{2,1,0:T(8,128)} custom-call(s32[4]{0:T(128)} %pad_add_fusion.place_ref, f32[8,2,128]{2,1,0:T(2,128)} %maximum_bitcast_fusion.weights_ref, bf16[2,8,4,64,768]{4,3,2,1,0:T(8,128)(2,1)} %bitcast.33, bf16[2,8,4,64,768]{4,3,2,1,0:T(8,128)(2,1)} %collective-permute-done.right_ref, f32[16,64,128]{2,1,0:T(8,128)} %shard_map.28.near_ref), custom_call_target="tpu_custom_call" | custom-call | flops 3221225472 | bytes 6291456 | tf_op jit(solution)/shard_map/pallas_call | solution.py:140
  (4 shorter events, 0.1 us)
Async XLA Ops:
  6.5 100.5 %copy-start = (s32[4,3]{1,0:T(4,128)S(1)}, s32[4,3]{1,0:T(4,128)}, u32[]{:S(2)}) copy-start(s32[4,3]{1,0:T(4,128)} %param.3) | copy-start | bytes 148
  6.5 100.5 %all-gather.2.cloned.1.call-start = ((), (), s32[]{:S(2)}) async-start(), calls=%async_computation | async-start | bytes 6684672 | tf_op jit(solution)/shard_map/all_gather | solution.py:104
  107.0 13.1 %collective-permute-start = (bf16[2,8,4,64,768]{4,3,2,1,0:T(8,128)(2,1)}, bf16[2,8,4,64,768]{4,3,2,1,0:T(8,128)(2,1)}, u32[]{:S(2)}, u32[]{:S(2)}) collective-permute-start(bf16[2,8,4,64,768]{4,3,2,1,0:T(8,128)(2,1)} %bitcast.30), channel_id=1, source_target_pairs={{0,8},{8,0},{1,9},{9,1},{2,10},{10,2},{3,11},{11,3},{4,12},{12,4},... | collective-permute-start | bytes 18874376 | tf_op jit(solution)/shard_map/ppermute | solution.py:106
Sparse Core Ops, SparseCore 0:
  10.1 96.8 all-gather.1

commit v2 on v1

v2 whole, which is shorter than its diff:
```python
import functools
import math

import jax
import jax.numpy as jnp
from jax import lax
from jax.experimental import pallas as pl
from jax.experimental.pallas import tpu as pltpu
from jax.sharding import Mesh, PartitionSpec as P

LEXT = 48

TWO_PI = 2.0 * math.pi


def phase_table(momenta, first_site, site_count, extent):
    flat = first_site + jnp.arange(site_count, dtype=jnp.int32)
    coords = jnp.stack([flat % extent, flat // extent % extent, flat // (extent * extent)], 0)
    turns = jnp.mod(jnp.sum(momenta[:, :, None] * coords[None, :, :], axis=1), extent)
    angle = turns.astype(jnp.float32) * (TWO_PI / extent)
    return jnp.stack([jnp.cos(angle), jnp.sin(angle)], 1)


def left_sides(left_ref, weights_ref):
    spins, depth = left_ref.shape[2], left_ref.shape[4]
    half = depth // 2
    cosine = jnp.tile(weights_ref[0, 0:1], (1, depth // weights_ref.shape[-1]))
    sine = jnp.tile(weights_ref[0, 1:2], (1, depth // weights_ref.shape[-1]))
    cosine_rows = [[], []]
    sine_rows = [[], []]
    for spin in range(spins):
        own = left_ref[0, 0, spin].astype(jnp.float32)
        by_cos = (own * cosine).astype(jnp.bfloat16)
        by_sin = (own * sine).astype(jnp.bfloat16)
        cosine_rows[0].append(by_cos)
        cosine_rows[1].append(jnp.concatenate([-by_cos[:, half:], by_cos[:, :half]], 1))
        sine_rows[0].append(jnp.concatenate([-by_sin[:, half:], by_sin[:, :half]], 1))
        sine_rows[1].append(-by_sin)
    return (
        jnp.concatenate(cosine_rows[0] + cosine_rows[1], 0),
        jnp.concatenate(sine_rows[0] + sine_rows[1], 0),
    )


def add_terms(weights_ref, left_ref, right_refs, total_refs, width):
    left_cos, left_sin = left_sides(left_ref, weights_ref)
    dims = (((1,), (1,)), ((), ()))
    for right_ref, total_ref in zip(right_refs, total_refs):
        groups, columns, per_block, depth = right_ref.shape[0], *right_ref.shape[2:]
        for chunk in range(columns // width):
            right = right_ref[:, 0, chunk * width : (chunk + 1) * width]
            right = right.reshape(groups * width * per_block, depth)
            term = lax.dot_general(left_cos, right, dims, preferred_element_type=jnp.float32)
            term += lax.dot_general(left_sin, right, dims, preferred_element_type=jnp.float32)
            total_ref[chunk] += term


def start_kernel(width, place_ref, weights_ref, left_ref, near_ref, far_ref, near_out, far_out):
    @pl.when(pl.program_id(0) == 0)
    def _():
        near_out[...] = jnp.zeros_like(near_out)
        far_out[...] = jnp.zeros_like(far_out)

    add_terms(weights_ref, left_ref, [near_ref, far_ref], [near_out, far_out], width)


def next_kernel(
    width, place_ref, weights_ref, left_ref, near_ref, far_ref, near_in, far_in, near_out, far_out
):
    @pl.when(pl.program_id(0) == 0)
    def _():
        near_out[...] = near_in[...]
        far_out[...] = far_in[...]

    add_terms(weights_ref, left_ref, [near_ref, far_ref], [near_out, far_out], width)


def near_kernel(width, place_ref, weights_ref, left_ref, near_ref, near_in, near_out):
    @pl.when(pl.program_id(0) == 0)
    def _():
        near_out[...] = near_in[...]

    add_terms(weights_ref, left_ref, [near_ref], [near_out], width)


def last_kernel(
    width, place_ref, weights_ref, left_ref, far_ref, near_in, far_in, field_ref, far_total
):
    @pl.when(pl.program_id(0) == 0)
    def _():
        far_total[...] = far_in[...]

    add_terms(weights_ref, left_ref, [far_ref], [far_total], width)

    @pl.when(pl.program_id(0) == pl.num_programs(0) - 1)
    def _():
        spins = left_ref.shape[2]
        groups, columns, per_block = far_ref.shape[0], far_ref.shape[2], far_ref.shape[3]
        first = place_ref[3] == 0
        for chunk in range(columns // width):
            near, far = near_in[chunk], far_total[chunk]
            even, odd = jnp.where(first, near, far), jnp.where(first, far, near)
            for part in range(2):
                for spin in range(spins):
                    top = (part * spins + spin) * per_block
                    rows = slice(top, top + per_block)
                    for inner in range(width):
                        pieces = []
                        for group in range(groups):
                            start = (group * width + inner) * per_block
                            across = slice(start, start + per_block)
                            pieces += [even[rows, across], odd[rows, across]]
                        row = (spin * columns + chunk * width + inner) * 2 + part
                        field_ref[row] = jnp.concatenate(pieces, 1)


def shards(modes, momenta):
    groups, deep, flat = (lax.axis_size(name) for name in ("pair", "deep", "flat"))
    sites = deep * flat
    slots, steps, per_block, spin_colour, site_count = modes.shape
    share = steps * momenta.shape[0] * 32 // sites
    columns = min(4, share // 2)
    spins = share // (2 * columns)
    width = max(1, min(columns, 256 // (groups * per_block)))
    level = lax.axis_index("deep")
    owned = (level * flat + lax.axis_index("flat")) * (share // 2)
    place = [
        lax.axis_index("pair"),
        owned // 4 % 4 // spins,
        owned % 4 // columns,
        lax.axis_index("core"),
    ]
    place = jnp.stack(place + [jnp.bitwise_xor(level, d) for d in range(deep)]).astype(jnp.int32)

    packed = jnp.transpose(modes.reshape(slots, per_block, 4, 3, site_count), (2, 1, 0, 3, 4))
    packed = packed.reshape(4, per_block, slots * 3 * site_count)
    depth = packed.shape[-1]
    pieces = [packed]
    for d in range(1, deep):
        pieces.append(lax.ppermute(packed, "deep", [(i, i ^ d) for i in range(deep)]))

    nears = [
        lax.all_gather(piece, ("pair", "flat")).reshape(groups, flat, 4, per_block, depth)
        for piece in pieces
    ]

    def both(near):
        return [near, lax.ppermute(near, "core", [(0, 1), (1, 0)])]

    mine = lax.dynamic_slice_in_dim(momenta, owned // 16, 1, 0)
    weights = phase_table(mine, jnp.int32(0), sites * site_count, LEXT)[0]
    weights = jnp.transpose(weights.reshape(2, sites, site_count), (1, 0, 2))

    tall, wide = 2 * spins * per_block, groups * width * per_block
    total_shape = (columns // width, tall, wide)
    field_shape = (share, per_block, 2 * groups * per_block)
    total_spec = pl.BlockSpec(total_shape, lambda m, place: (0, 0, 0))
    total = jax.ShapeDtypeStruct(total_shape, jnp.float32)

    def call(kernel, d, near, rights, totals, out_specs, out_shape, scratch=()):
        in_specs = [
            pl.BlockSpec((1, 2, site_count), lambda m, place: (place[4 + d] * flat + m, 0, 0)),
            pl.BlockSpec(
                (1, 1, spins, per_block, depth), lambda m, place: (place[0], m, place[1], 0, 0)
            ),
        ]
        right_spec = pl.BlockSpec(
            (groups, 1, columns, per_block, depth), lambda m, place: (0, m, place[2], 0, 0)
        )
        in_specs += [right_spec] * len(rights) + [total_spec] * len(totals)
        return pl.pallas_call(
            functools.partial(kernel, width),
            grid_spec=pltpu.PrefetchScalarGridSpec(
                num_scalar_prefetch=1,
                grid=(flat,),
                in_specs=in_specs,
                out_specs=out_specs,
                scratch_shapes=scratch,
            ),
            out_shape=out_shape,
            compiler_params=pltpu.CompilerParams(vmem_limit_bytes=48 * 1024 * 1024),
            cost_estimate=pl.CostEstimate(
                flops=4 * tall * groups * per_block * columns * depth * flat * len(rights),
                bytes_accessed=groups * flat * 4 * per_block * depth * 2 * len(rights),
                transcendentals=0,
            ),
        )(place, weights, near, *rights, *totals)

    totals = call(
        start_kernel, 0, nears[0], both(nears[0]), [], [total_spec] * 2, [total] * 2
    )
    for d in range(1, deep - 1):
        near, totals = lax.optimization_barrier((nears[d], totals))
        totals = call(next_kernel, d, near, both(near), totals, [total_spec] * 2, [total] * 2)
    near, totals = lax.optimization_barrier((nears[deep - 1], totals))
    near, far = both(near)
    near_total = call(near_kernel, deep - 1, near, [near], totals[:1], total_spec, total)
    return call(
        last_kernel,
        deep - 1,
        near,
        [far],
        [near_total, totals[1]],
        pl.BlockSpec(field_shape, lambda m, place: (0, 0, 0)),
        jax.ShapeDtypeStruct(field_shape, jnp.float32),
        [pltpu.VMEM(total_shape, jnp.float32)],
    )


def solution(mesh):
    count, sites = mesh.shape["blk"], mesh.shape["site"]
    flat = 2 ** (int(math.log2(sites)) // 2)
    split = Mesh(
        mesh.devices.reshape(count // 2, 2, sites // flat, flat), ("pair", "core", "deep", "flat")
    )
    placed = (P(None, None, ("pair", "core"), None, ("deep", "flat")), P())
    return jax.shard_map(
        shards,
        mesh=split,
        in_specs=placed,
        out_specs=P(("deep", "flat"), ("pair", "core"), None),
        check_vma=False,
    )
```

time: 140 us -> 155 us (1.11)
  local copies, waits for them, and re-layouts: 2.44 us -> 12.6 us
  Pallas kernels: 23.8 us -> 14.2 us
  starting transfers between devices: 0.01 us -> 8.96 us
  waiting for transfers between devices: 98.1 us -> 105 us
    ppermute x1 -> x7, waiting for transfers between devices: 0.01 us -> 41.5 us  [the longest x3 37.7 us: shards(): lax.ppermute(packed, 'deep', [(i, i ^ d) for i in range(deep)])]
    all_gather x1 -> x4, waiting for transfers between devices: 98 us -> 63.9 us  [shards(): lax.all_gather(piece, ('pair', 'flat'))]
    unnamed x2 -> x20, local copies, waits for them, and re-layouts: 0.01 us -> 9.7 us
    pallas_call x2 -> x5, Pallas kernels: 23.8 us -> 14.2 us  [call(): pl.pallas_call(functools.partial(kernel, width), grid_spec=pltpu.Prefetch...]
    ppermute x1 -> x7, starting transfers between devices: 0.01 us -> 8.84 us  [the longest x3 8.83 us: shards(): lax.ppermute(packed, 'deep', [(i, i ^ d) for i in range(deep)])]
  transfers between devices with their start and end apart: 2 -> 11, of which waited for: 1 -> 9; matrix products, arithmetic and copies ran while one was open for 1% -> 0% of each run, Pallas kernels for 8% -> 7%
where the time goes in v2:
time: 155 us
  waiting for transfers between devices  105 us (68%)
  Pallas kernels  14.2 us (9%)
  between operations  13.3 us (9%)
  local copies, waits for them, and re-layouts  12.6 us (8%)
  starting transfers between devices  8.96 us (6%)
    all_gather x4, waiting for transfers between devices, shards(): lax.all_gather(piece, ('pair', 'flat'))  63.9 us
    ppermute x3, waiting for transfers between devices, shards(): lax.ppermute(packed, 'deep', [(i, i ^ d) for i in range(deep)])  37.7 us
    pallas_call x5, Pallas kernels, call(): pl.pallas_call(functools.partial(kernel, width), grid_spec=pltpu.Prefetch...  14.2 us
    unnamed x20, local copies, waits for them, and re-layouts  9.7 us
    ppermute x3, starting transfers between devices, shards(): lax.ppermute(packed, 'deep', [(i, i ^ d) for i in range(deep)])  8.83 us
    ppermute x4, waiting for transfers between devices, both(): return [near, lax.ppermute(near, 'core', [(0, 1), (1, 0)])]  3.83 us
  transfers between devices with their start and end apart: 11, of which 9 were waited for; matrix products, arithmetic and copies ran while one was open for 0% of the time, Pallas kernels for 7%

profile of v2, /device:TPU:0, one launch (start us, length us, event | category | flops | bytes accessed | tf_op | source)
XLA Modules:
  0.0 154.8 jit_solution(10858635867854810843)
XLA Ops:
  6.5 0.0 copy-start
  6.5 0.0 all-gather.8.cloned.1.call-start
  6.5 1.3 copy.11
  7.9 1.1 all_gather_reshape.3
  9.0 0.0 all-gather.8.cloned.1.call-update
  9.0 0.0 all-gather.14.cloned.1.call-start
  9.1 0.3 reshape.234
  9.4 3.1 %collective-permute-start.2 = (bf16[4,64,768]{2,1,0:T(8,128)(2,1)S(1)}, bf16[4,64,768]{2,1,0:T(8,128)(2,1)S(1)}, u32[]{:S(2)}, u32[]{:S(2)}) collective-permute-start(bf16[4,64,768]{2,1,0:T(8,128)(2,1)S(1)} %reshape.234), channel_id=1, source_target_pairs={{0,2},{2,0},{4,6},{6,4},{1,3},{3,1},{5,7},{7,5},{8,10},{10,8},{12,... | collective-permute-start | bytes 1179656 | tf_op jit(solution)/shard_map/ppermute | solution.py:140
  12.5 9.1 %collective-permute-done.2 = bf16[4,64,768]{2,1,0:T(8,128)(2,1)S(1)} collective-permute-done((bf16[4,64,768]{2,1,0:T(8,128)(2,1)S(1)}, bf16[4,64,768]{2,1,0:T(8,128)(2,1)S(1)}, u32[]{:S(2)}, u32[]{:S(2)}) %collective-permute-start.2) | collective-permute-done | bytes 393248 | tf_op jit(solution)/shard_map/ppermute | solution.py:140
  21.6 0.0 copy-start.8
  21.6 0.7 copy-done.8
  22.4 0.0 all-gather.14.cloned.1.call-update
  22.4 0.0 all-gather.12.cloned.1.call-start
  22.4 20.5 %all-gather.8.cloned.1.call-done = bf16[4,4,64,768]{3,2,1,0:T(8,128)(2,1)} async-done(((bf16[1,4,64,768]{3,2,1,0:T(8,128)(2,1)}), bf16[4,4,64,768]{3,2,1,0:T(8,128)(2,1)}) %all-gather.8.cloned.1.call-update) | async-done | bytes 1572880 | tf_op jit(solution)/shard_map/all_gather | solution.py:143
  42.9 0.0 collective-permute-start.3
  42.9 2.4 %collective-permute-start.1 = (bf16[4,64,768]{2,1,0:T(8,128)(2,1)S(1)}, bf16[4,64,768]{2,1,0:T(8,128)(2,1)S(1)}, u32[]{:S(2)}, u32[]{:S(2)}) collective-permute-start(bf16[4,64,768]{2,1,0:T(8,128)(2,1)S(1)} %reshape.234), channel_id=1, source_target_pairs={{0,4},{2,6},{4,0},{6,2},{1,5},{3,7},{5,1},{7,3},{8,12},{10,14},{12... | collective-permute-start | bytes 1179656 | tf_op jit(solution)/shard_map/ppermute | solution.py:140
  45.3 18.4 %collective-permute-done.1 = bf16[4,64,768]{2,1,0:T(8,128)(2,1)S(1)} collective-permute-done((bf16[4,64,768]{2,1,0:T(8,128)(2,1)S(1)}, bf16[4,64,768]{2,1,0:T(8,128)(2,1)S(1)}, u32[]{:S(2)}, u32[]{:S(2)}) %collective-permute-start.1) | collective-permute-done | bytes 393248 | tf_op jit(solution)/shard_map/ppermute | solution.py:140
  63.8 0.0 copy-start.7
  63.8 0.7 copy-done.7
  64.5 0.0 all-gather.12.cloned.1.call-update
  64.5 0.0 all-gather.10.cloned.1.call-start
  64.7 0.1 stack.52.place_ref
  64.8 0.0 copy-done
  64.8 0.1 fusion
  64.9 0.1 multiply_cosine_fusion
  65.1 0.0 collective-permute-done.3.far_ref
  65.1 0.0 copy-start.4
  65.1 1.4 copy-done.4
  66.5 3.0 %shard_map.28 = (f32[2,256,256]{2,1,0:T(8,128)S(1)}, f32[2,256,256]{2,1,0:T(8,128)S(1)}) custom-call(s32[8]{0:T(128)S(1)} %stack.52.place_ref, f32[8,2,128]{2,1,0:T(2,128)S(1)} %maximum_bitcast_fusion.weights_ref, bf16[2,2,4,64,768]{4,3,2,1,0:T(8,128)(2,1)S(1)} %bitcast.48, bf16[2,2,4,64,768]{4,3,2,1,0:T(8,128)(2,1)S(1)} %bitcast.49, ...), custom_call_target="tpu_custom_call" | custom-call | flops 1610612736 | bytes 3145728 | tf_op jit(solution)/shard_map/pallas_call | solution.py:171
  69.5 6.3 %all-gather.14.cloned.1.call-done = bf16[16,64,768]{2,1,0:T(8,128)(2,1)} async-done(((bf16[4,64,768]{2,1,0:T(8,128)(2,1)}), bf16[16,64,768]{2,1,0:T(8,128)(2,1)}) %all-gather.14.cloned.1.call-update) | async-done | bytes 1572880 | tf_op jit(solution)/shard_map/all_gather | solution.py:143
  75.8 0.0 collective-permute-start.4
  75.8 3.3 %collective-permute-start = (bf16[4,64,768]{2,1,0:T(8,128)(2,1)S(1)}, bf16[4,64,768]{2,1,0:T(8,128)(2,1)S(1)}, u32[]{:S(2)}, u32[]{:S(2)}) collective-permute-start(bf16[4,64,768]{2,1,0:T(8,128)(2,1)S(1)} %reshape.234), channel_id=1, source_target_pairs={{0,6},{2,4},{4,2},{6,0},{1,7},{3,5},{5,3},{7,1},{8,14},{10,12},{12... | collective-permute-start | bytes 1179656 | tf_op jit(solution)/shard_map/ppermute | solution.py:140
  79.1 10.1 %collective-permute-done = bf16[4,64,768]{2,1,0:T(8,128)(2,1)S(1)} collective-permute-done((bf16[4,64,768]{2,1,0:T(8,128)(2,1)S(1)}, bf16[4,64,768]{2,1,0:T(8,128)(2,1)S(1)}, u32[]{:S(2)}, u32[]{:S(2)}) %collective-permute-start) | collective-permute-done | bytes 393248 | tf_op jit(solution)/shard_map/ppermute | solution.py:140
  89.2 0.0 copy-start.9
  89.2 0.8 copy-done.9
  89.9 0.0 all-gather.10.cloned.1.call-update
  90.0 0.0 collective-permute-done.4.far_ref
  90.0 0.0 copy-start.2
  90.0 1.4 copy-done.2
  91.4 2.9 %shard_map.29 = (f32[2,256,256]{2,1,0:T(8,128)S(1)}, f32[2,256,256]{2,1,0:T(8,128)S(1)}) custom-call(s32[8]{0:T(128)S(1)} %stack.52.place_ref, f32[8,2,128]{2,1,0:T(2,128)S(1)} %maximum_bitcast_fusion.weights_ref, bf16[2,2,4,64,768]{4,3,2,1,0:T(8,128)(2,1)S(1)} %bitcast.42, bf16[2,2,4,64,768]{4,3,2,1,0:T(8,128)(2,1)S(1)} %bitcast.43, ...), custom_call_target="tpu_custom_call" | custom-call | flops 1610612736 | bytes 3145728 | tf_op jit(solution)/shard_map/pallas_call | solution.py:171
  94.3 0.0 copy-start.5
  94.4 0.8 copy-done.5
  95.1 13.5 %all-gather.12.cloned.1.call-done = bf16[16,64,768]{2,1,0:T(8,128)(2,1)} async-done(((bf16[4,64,768]{2,1,0:T(8,128)(2,1)}), bf16[16,64,768]{2,1,0:T(8,128)(2,1)}) %all-gather.12.cloned.1.call-update) | async-done | bytes 1572880 | tf_op jit(solution)/shard_map/all_gather | solution.py:143
  108.6 0.0 collective-permute-start.5
  108.6 3.6 %collective-permute-done.5.far_ref = bf16[2,2,4,64,768]{4,3,2,1,0:T(8,128)(2,1)S(1)} collective-permute-done((bf16[2,2,4,64,768]{4,3,2,1,0:T(8,128)(2,1)}, bf16[2,2,4,64,768]{4,3,2,1,0:T(8,128)(2,1)S(1)}, u32[]{:S(2)}, u32[]{:S(2)}) %collective-permute-start.5) | collective-permute-done | bytes 1572896 | tf_op jit(solution)/shard_map/ppermute | solution.py:148
  112.2 0.0 copy-start.3
  112.2 1.4 copy-done.3
  113.6 0.0 copy-start.6
  113.6 1.0 copy-done.6
  114.7 3.0 %shard_map.30 = (f32[2,256,256]{2,1,0:T(8,128)S(1)}, f32[2,256,256]{2,1,0:T(8,128)S(1)}) custom-call(s32[8]{0:T(128)S(1)} %stack.52.place_ref, f32[8,2,128]{2,1,0:T(2,128)S(1)} %maximum_bitcast_fusion.weights_ref, bf16[2,2,4,64,768]{4,3,2,1,0:T(8,128)(2,1)S(1)} %bitcast.45, bf16[2,2,4,64,768]{4,3,2,1,0:T(8,128)(2,1)S(1)} %bitcast.46, ...), custom_call_target="tpu_custom_call" | custom-call | flops 1610612736 | bytes 3145728 | tf_op jit(solution)/shard_map/pallas_call | solution.py:171
  117.7 23.7 %all-gather.10.cloned.1.call-done = bf16[16,64,768]{2,1,0:T(8,128)(2,1)} async-done(((bf16[4,64,768]{2,1,0:T(8,128)(2,1)}), bf16[16,64,768]{2,1,0:T(8,128)(2,1)}) %all-gather.10.cloned.1.call-update) | async-done | bytes 1572880 | tf_op jit(solution)/shard_map/all_gather | solution.py:143
  141.3 0.0 collective-permute-start.6
  141.3 0.0 copy-start.1
  141.3 1.4 copy-done.1
  142.7 2.0 %shard_map.31.near_in = f32[2,256,256]{2,1,0:T(8,128)S(1)} custom-call(s32[8]{0:T(128)S(1)} %stack.52.place_ref, f32[8,2,128]{2,1,0:T(2,128)S(1)} %maximum_bitcast_fusion.weights_ref, bf16[2,2,4,64,768]{4,3,2,1,0:T(8,128)(2,1)S(1)} %bitcast.38, bf16[2,2,4,64,768]{4,3,2,1,0:T(8,128)(2,1)S(1)} %bitcast.39, f32[2,256,256]{2,1,0:T(8,128)S(1)} %get-tuple-element.33.near_in), custom_call_target="tpu_custom_call" | custom-call | flops 805306368 | bytes 1572864 | tf_op jit(solution)/shard_map/pallas_call | solution.py:171
  144.7 0.2 collective-permute-done.6.far_ref
  144.9 3.3 %shard_map.32 = f32[16,64,256]{2,1,0:T(8,128)} custom-call(s32[8]{0:T(128)S(1)} %stack.52.place_ref, f32[8,2,128]{2,1,0:T(2,128)S(1)} %maximum_bitcast_fusion.weights_ref, bf16[2,2,4,64,768]{4,3,2,1,0:T(8,128)(2,1)S(1)} %bitcast.40, bf16[2,2,4,64,768]{4,3,2,1,0:T(8,128)(2,1)S(1)} %collective-permute-done.6.far_ref, f32[2,256,256]{2,1,0:T(8,128)S(1)} %shard_map.31.near_in, ...), custom_call_target="tpu_custom_call" | custom-call | flops 805306368 | bytes 1572864 | tf_op jit(solution)/shard_map/pallas_call | solution.py:171
  (5 shorter events, 0.1 us)
Async XLA Ops:
  6.5 58.2 %copy-start = (s32[4,3]{1,0:T(4,128)S(1)}, s32[4,3]{1,0:T(4,128)}, u32[]{:S(2)}) copy-start(s32[4,3]{1,0:T(4,128)} %param.3) | copy-start | bytes 148
  6.5 36.4 %all-gather.8.cloned.1.call-start = ((), (), s32[]{:S(2)}) async-start(), calls=%async_computation | async-start | bytes 1966080 | tf_op jit(solution)/shard_map/all_gather | solution.py:143
  9.0 66.7 %all-gather.14.cloned.1.call-start = ((), (), s32[]{:S(2)}) async-start(), calls=%async_computation.3 | async-start | bytes 1966080 | tf_op jit(solution)/shard_map/all_gather | solution.py:143
  9.4 12.2 %collective-permute-start.2 = (bf16[4,64,768]{2,1,0:T(8,128)(2,1)S(1)}, bf16[4,64,768]{2,1,0:T(8,128)(2,1)S(1)}, u32[]{:S(2)}, u32[]{:S(2)}) collective-permute-start(bf16[4,64,768]{2,1,0:T(8,128)(2,1)S(1)} %reshape.234), channel_id=1, source_target_pairs={{0,2},{2,0},{4,6},{6,4},{1,3},{3,1},{5,7},{7,5},{8,10},{10,8},{12,... | collective-permute-start | bytes 1179656 | tf_op jit(solution)/shard_map/ppermute | solution.py:140
  21.6 0.7 copy-start.8
  22.4 86.2 %all-gather.12.cloned.1.call-start = ((), (), s32[]{:S(2)}) async-start(), calls=%async_computation.2 | async-start | bytes 1966080 | tf_op jit(solution)/shard_map/all_gather | solution.py:143
  42.9 22.2 %collective-permute-start.3 = (bf16[2,2,4,64,768]{4,3,2,1,0:T(8,128)(2,1)}, bf16[2,2,4,64,768]{4,3,2,1,0:T(8,128)(2,1)S(1)}, u32[]{:S(2)}, u32[]{:S(2)}) collective-permute-start(bf16[2,2,4,64,768]{4,3,2,1,0:T(8,128)(2,1)} %bitcast.47), channel_id=1, source_target_pairs={{0,8},{8,0},{1,9},{9,1},{2,10},{10,2},{3,11},{11,3},{4,12},{12,4},... | collective-permute-start | bytes 4718600 | tf_op jit(solution)/shard_map/ppermute | solution.py:148
  42.9 20.9 %collective-permute-start.1 = (bf16[4,64,768]{2,1,0:T(8,128)(2,1)S(1)}, bf16[4,64,768]{2,1,0:T(8,128)(2,1)S(1)}, u32[]{:S(2)}, u32[]{:S(2)}) collective-permute-start(bf16[4,64,768]{2,1,0:T(8,128)(2,1)S(1)} %reshape.234), channel_id=1, source_target_pairs={{0,4},{2,6},{4,0},{6,2},{1,5},{3,7},{5,1},{7,3},{8,12},{10,14},{12... | collective-permute-start | bytes 1179656 | tf_op jit(solution)/shard_map/ppermute | solution.py:140
  63.8 0.7 copy-start.7
  64.5 76.8 %all-gather.10.cloned.1.call-start = ((), (), s32[]{:S(2)}) async-start(), calls=%async_computation.1 | async-start | bytes 1966080 | tf_op jit(solution)/shard_map/all_gather | solution.py:143
  65.1 1.4 copy-start.4
  75.8 14.2 %collective-permute-start.4 = (bf16[2,2,4,64,768]{4,3,2,1,0:T(8,128)(2,1)}, bf16[2,2,4,64,768]{4,3,2,1,0:T(8,128)(2,1)S(1)}, u32[]{:S(2)}, u32[]{:S(2)}) collective-permute-start(bf16[2,2,4,64,768]{4,3,2,1,0:T(8,128)(2,1)} %bitcast.41), channel_id=1, source_target_pairs={{0,8},{8,0},{1,9},{9,1},{2,10},{10,2},{3,11},{11,3},{4,12},{12,4},... | collective-permute-start | bytes 4718600 | tf_op jit(solution)/shard_map/ppermute | solution.py:148
  75.8 13.4 %collective-permute-start = (bf16[4,64,768]{2,1,0:T(8,128)(2,1)S(1)}, bf16[4,64,768]{2,1,0:T(8,128)(2,1)S(1)}, u32[]{:S(2)}, u32[]{:S(2)}) collective-permute-start(bf16[4,64,768]{2,1,0:T(8,128)(2,1)S(1)} %reshape.234), channel_id=1, source_target_pairs={{0,6},{2,4},{4,2},{6,0},{1,7},{3,5},{5,3},{7,1},{8,14},{10,12},{12... | collective-permute-start | bytes 1179656 | tf_op jit(solution)/shard_map/ppermute | solution.py:140
  89.2 0.8 copy-start.9
  90.0 1.4 copy-start.2
  94.3 0.8 copy-start.5
  108.6 3.6 %collective-permute-start.5 = (bf16[2,2,4,64,768]{4,3,2,1,0:T(8,128)(2,1)}, bf16[2,2,4,64,768]{4,3,2,1,0:T(8,128)(2,1)S(1)}, u32[]{:S(2)}, u32[]{:S(2)}) collective-permute-start(bf16[2,2,4,64,768]{4,3,2,1,0:T(8,128)(2,1)} %bitcast.44), channel_id=1, source_target_pairs={{0,8},{8,0},{1,9},{9,1},{2,10},{10,2},{3,11},{11,3},{4,12},{12,4},... | collective-permute-start | bytes 4718600 | tf_op jit(solution)/shard_map/ppermute | solution.py:148
  112.2 1.4 copy-start.3
  113.6 1.0 copy-start.6
  141.3 3.6 %collective-permute-start.6 = (bf16[2,2,4,64,768]{4,3,2,1,0:T(8,128)(2,1)}, bf16[2,2,4,64,768]{4,3,2,1,0:T(8,128)(2,1)S(1)}, u32[]{:S(2)}, u32[]{:S(2)}) collective-permute-start(bf16[2,2,4,64,768]{4,3,2,1,0:T(8,128)(2,1)} %bitcast.37), channel_id=1, source_target_pairs={{0,8},{8,0},{1,9},{9,1},{2,10},{10,2},{3,11},{11,3},{4,12},{12,4},... | collective-permute-start | bytes 4718600 | tf_op jit(solution)/shard_map/ppermute | solution.py:148
  141.3 1.4 copy-start.1
Sparse Core Ops, SparseCore 0:
  9.2 33.6 all-gather.7
  44.7 30.9 all-gather.13
  77.6 30.9 all-gather.11
  110.3 30.9 all-gather.9

commit v3 on v1

v3 whole, which is shorter than its diff:
```python
import functools
import math

import jax
import jax.numpy as jnp
from jax import lax
from jax.experimental import pallas as pl
from jax.experimental.pallas import tpu as pltpu
from jax.sharding import Mesh, PartitionSpec as P

LEXT = 48

TWO_PI = 2.0 * math.pi

AXES = ("pair", "core", "deep", "flat")


def phase_table(momenta, first_site, site_count, extent):
    flat = first_site + jnp.arange(site_count, dtype=jnp.int32)
    coords = jnp.stack([flat % extent, flat // extent % extent, flat // (extent * extent)], 0)
    turns = jnp.mod(jnp.sum(momenta[:, :, None] * coords[None, :, :], axis=1), extent)
    angle = turns.astype(jnp.float32) * (TWO_PI / extent)
    return jnp.stack([jnp.cos(angle), jnp.sin(angle)], 1)


def left_sides(owns, weights):
    depth = owns[0].shape[1]
    half = depth // 2
    cosine = jnp.tile(weights[0:1], (1, depth // weights.shape[1]))
    sine = jnp.tile(weights[1:2], (1, depth // weights.shape[1]))
    cosine_rows = [[], []]
    sine_rows = [[], []]
    for own in owns:
        own = own.astype(jnp.float32)
        by_cos = (own * cosine).astype(jnp.bfloat16)
        by_sin = (own * sine).astype(jnp.bfloat16)
        cosine_rows[0].append(by_cos)
        cosine_rows[1].append(jnp.concatenate([-by_cos[:, half:], by_cos[:, :half]], 1))
        sine_rows[0].append(jnp.concatenate([-by_sin[:, half:], by_sin[:, :half]], 1))
        sine_rows[1].append(-by_sin)
    return (
        jnp.concatenate(cosine_rows[0] + cosine_rows[1], 0),
        jnp.concatenate(sine_rows[0] + sine_rows[1], 0),
    )


def product(left_cos, left_sin, right):
    dims = (((1,), (1,)), ((), ()))
    term = lax.dot_general(left_cos, right, dims, preferred_element_type=jnp.float32)
    return term + lax.dot_general(left_sin, right, dims, preferred_element_type=jnp.float32)


def add_shards(names, has_totals, last, place_ref, weights_ref, *refs):
    refs = list(refs)
    held = {name: refs.pop(0) for name in names}
    steps = sorted({name[2] for name in names})
    sources = {}
    for dz in steps:
        for kind in ("O", "A", "B"):
            key = ("near", kind, dz)
            sources[key] = held[key] if key in held else refs.pop(0)
    totals_in = refs.pop(0) if has_totals else None
    out_ref, left_ref = refs.pop(0), refs.pop(0)
    totals_ref = refs.pop(0) if last else out_ref
    pair, core, level, beside, first_s, flat = (place_ref[i] for i in range(6))
    spins, per_block = left_ref.shape[2] // (2 * out_ref.shape[1]), out_ref.shape[1]
    if not last:
        per_block = sources[("near", "O", steps[0])].shape[1]
        spins = left_ref.shape[2] // (2 * per_block)

    if has_totals:
        totals_ref[...] = totals_in[...]
    else:
        totals_ref[...] = jnp.zeros_like(totals_ref)

    for slot, dz in enumerate(steps):
        shard = jnp.bitwise_xor(level, dz) * flat
        here = [sources[("near", "O", dz)][first_s + s] for s in range(spins)]
        there = []
        for s in range(spins):
            by_a = sources[("near", "A", dz)][first_s + s]
            by_b = sources[("near", "B", dz)][first_s + s]
            there.append(jnp.where(core == 0, by_b, by_a))
        for dy, owns in enumerate((here, there)):
            weights = weights_ref[shard + jnp.bitwise_xor(beside, dy)]
            left_cos, left_sin = left_sides(owns, weights)
            left_ref[2 * slot + dy, 0] = left_cos
            left_ref[2 * slot + dy, 1] = left_sin

    for side, kind, dz in names:
        right_ref = held[(side, kind, dz)]
        right = right_ref[...].reshape(-1, right_ref.shape[2])
        turn = core if side == "near" else 1 - core
        dx, dy = {"O": (0, 0), "A": (1 - turn, turn), "B": (turn, 1 - turn), "AB": (1, 1)}[kind]
        slot = 2 * steps.index(dz) + dy
        totals_ref[0 if side == "near" else 1, dx] += product(
            left_ref[slot, 0], left_ref[slot, 1], right
        )

    if last:
        columns = totals_ref.shape[3] // per_block
        for part in range(2):
            for spin in range(spins):
                top = (part * spins + spin) * per_block
                for column in range(columns):
                    across = pl.ds(column * per_block, per_block)
                    pieces = [
                        totals_ref[
                            jnp.bitwise_xor(core, c),
                            jnp.bitwise_xor(pair, p),
                            pl.ds(top, per_block),
                            across,
                        ]
                        for p in range(2)
                        for c in range(2)
                    ]
                    row = (spin * columns + column) * 2 + part
                    out_ref[row] = jnp.concatenate(pieces, 1)


def swap_in_windows(packed, place, weights, share):
    shape = tuple(lax.axis_size(name) for name in AXES)
    columns, per_block, depth = packed.shape
    spins = share // (2 * columns)
    tall, wide = 2 * spins * per_block, columns * per_block
    strides = (shape[1] * shape[2] * shape[3], shape[2] * shape[3], shape[3], 1)

    def move(array, target):
        pairs = []
        for p in range(shape[0]):
            for c in range(shape[1]):
                for z in range(shape[2]):
                    for y in range(shape[3]):
                        ends = (p, c, z, y), target(p, c, z, y)
                        pairs.append(
                            tuple(sum(a * b for a, b in zip(end, strides)) for end in ends)
                        )
        return lax.ppermute(array, AXES, pairs)

    def hop_a(array):
        return move(array, lambda p, c, z, y: (p ^ 1, c, z, y) if c == 0 else (p, c, z, y ^ 1))

    def hop_b(array):
        return move(array, lambda p, c, z, y: (p, c, z, y ^ 1) if c == 0 else (p ^ 1, c, z, y))

    def hop_z(array, by):
        return move(array, lambda p, c, z, y: (p, c, z ^ by, y))

    def swap(array):
        return move(array, lambda p, c, z, y: (p, c ^ 1, z, y))

    got = {("near", "O", 0): packed}
    totals = None

    def add(names, totals, last=False):
        steps = sorted({name[2] for name in names})
        extra = [
            ("near", kind, dz)
            for dz in steps
            for kind in ("O", "A", "B")
            if ("near", kind, dz) not in names
        ]
        operands = [place, weights] + [got[name] for name in list(names) + extra]
        if totals is not None:
            operands.append(totals)
        total_shape = (2, 2, tall, wide)
        out = (share, per_block, 4 * per_block) if last else total_shape
        scratch = [pltpu.VMEM((2 * len(steps), 2, tall, depth), jnp.bfloat16)]
        if last:
            scratch.append(pltpu.VMEM(total_shape, jnp.float32))
        return pl.pallas_call(
            functools.partial(add_shards, tuple(names), totals is not None, last),
            in_specs=[pl.BlockSpec(memory_space=pltpu.SMEM)]
            + [pl.BlockSpec(memory_space=pltpu.VMEM)] * (len(operands) - 1),
            out_specs=pl.BlockSpec(memory_space=pltpu.VMEM),
            out_shape=jax.ShapeDtypeStruct(out, jnp.float32),
            scratch_shapes=scratch,
            compiler_params=pltpu.CompilerParams(vmem_limit_bytes=40 * 1024 * 1024),
            cost_estimate=pl.CostEstimate(
                flops=4 * tall * wide * depth * len(names),
                bytes_accessed=wide * depth * 2 * len(names) + 8 * 4 * tall * wide,
                transcendentals=0,
            ),
        )(*operands)

    def near(kind, dz):
        return got[("near", kind, dz)]

    windows = [
        (
            {
                ("near", "A", 0): lambda: hop_a(near("O", 0)),
                ("near", "B", 0): lambda: hop_b(near("O", 0)),
                ("near", "O", 1): lambda: hop_z(near("O", 0), 1),
            },
            [("O", 0)],
            [],
        ),
        (
            {
                ("near", "O", 2): lambda: hop_z(near("O", 0), 2),
                ("near", "AB", 0): lambda: hop_b(near("A", 0)),
                ("near", "A", 1): lambda: hop_a(near("O", 1)),
                ("near", "B", 1): lambda: hop_b(near("O", 1)),
            },
            [("A", 0), ("B", 0), ("O", 1)],
            [("near", "O", 0), ("near", "A", 0), ("near", "B", 0), ("far", "O", 0)],
        ),
        (
            {
                ("near", "A", 2): lambda: hop_a(near("O", 2)),
                ("near", "B", 2): lambda: hop_b(near("O", 2)),
                ("near", "O", 3): lambda: hop_z(near("O", 2), 1),
            },
            [("AB", 0), ("A", 1), ("B", 1), ("O", 2)],
            [("near", "AB", 0), ("near", "O", 1), ("near", "A", 1), ("near", "B", 1)]
            + [("far", "A", 0), ("far", "B", 0), ("far", "O", 1)],
        ),
        (
            {
                ("near", "AB", 2): lambda: hop_b(near("A", 2)),
                ("near", "A", 3): lambda: hop_a(near("O", 3)),
                ("near", "B", 3): lambda: hop_b(near("O", 3)),
                ("near", "AB", 1): lambda: hop_z(near("AB", 0), 1),
            },
            [("A", 2), ("B", 2), ("O", 3)],
            [("far", "AB", 0), ("far", "A", 1), ("far", "B", 1)]
            + [("near", "O", 2), ("near", "A", 2), ("near", "B", 2), ("far", "O", 2)],
        ),
        (
            {("near", "AB", 3): lambda: hop_b(near("A", 3))},
            [("AB", 1), ("AB", 2), ("A", 3), ("B", 3)],
            [("near", "O", 3), ("near", "A", 3), ("near", "B", 3), ("near", "AB", 1)]
            + [("near", "AB", 2), ("far", "A", 2), ("far", "B", 2), ("far", "O", 3)],
        ),
        (
            {},
            [("AB", 3)],
            [("near", "AB", 3), ("far", "AB", 1), ("far", "AB", 2), ("far", "A", 3)]
            + [("far", "B", 3)],
        ),
    ]
    for travels, swaps, names in windows:
        new = {name: start() for name, start in travels.items()}
        for kind, dz in swaps:
            new[("far", kind, dz)] = swap(near(kind, dz))
        if names:
            totals = add(names, totals)
        got.update(new)
        got, totals = lax.optimization_barrier((got, totals))
    return add([("far", "AB", 3)], totals, last=True)


def add_terms(place_ref, weights_ref, left_ref, right_ref, field_ref):
    @pl.when(pl.program_id(0) == 0)
    def _():
        field_ref[...] = jnp.zeros_like(field_ref)

    spins = left_ref.shape[2]
    groups, columns, per_block, depth = right_ref.shape[0], *right_ref.shape[2:]
    owns = [left_ref[0, 0, spin] for spin in range(spins)]
    left_cos, left_sin = left_sides(owns, weights_ref[0])
    for column in range(columns):
        right = right_ref[:, 0, column].reshape(groups * per_block, depth)
        term = product(left_cos, left_sin, right)
        for part in range(2):
            for spin in range(spins):
                start = (part * spins + spin) * per_block
                field_ref[(spin * columns + column) * 2 + part] += term[start : start + per_block]


def gather_whole(packed, place, weights, share):
    groups, _, deep, flat = (lax.axis_size(name) for name in AXES)
    sites = deep * flat
    _, per_block, depth = packed.shape
    columns = min(4, share // 2)
    spins = share // (2 * columns)
    near = lax.all_gather(packed, ("pair", "deep", "flat"))
    near = near.reshape(groups, sites, 4, per_block, depth)
    far = lax.ppermute(near, "core", [(0, 1), (1, 0)])
    wide = groups * per_block

    def half(right):
        return pl.pallas_call(
            add_terms,
            grid_spec=pltpu.PrefetchScalarGridSpec(
                num_scalar_prefetch=1,
                grid=(sites,),
                in_specs=[
                    pl.BlockSpec((1, 2, weights.shape[2]), lambda m, place: (m, 0, 0)),
                    pl.BlockSpec(
                        (1, 1, spins, per_block, depth),
                        lambda m, place: (place[0], m, place[4] // spins, 0, 0),
                    ),
                    pl.BlockSpec(
                        (groups, 1, columns, per_block, depth),
                        lambda m, place: (0, m, place[6] // columns, 0, 0),
                    ),
                ],
                out_specs=pl.BlockSpec((share, per_block, wide), lambda m, place: (0, 0, 0)),
            ),
            out_shape=jax.ShapeDtypeStruct((share, per_block, wide), jnp.float32),
            compiler_params=pltpu.CompilerParams(vmem_limit_bytes=40 * 1024 * 1024),
        )(place, weights, near, right)

    sides = [half(right).reshape(share, per_block, groups, per_block) for right in (near, far)]
    first = lax.axis_index("core") == 0
    even, odd = (jnp.where(first, a, b) for a, b in (sides, sides[::-1]))
    return jnp.stack([even, odd], 3).reshape(share, per_block, 2 * wide)


def shards(modes, momenta):
    groups, _, deep, flat = (lax.axis_size(name) for name in AXES)
    sites = deep * flat
    slots, steps, per_block, spin_colour, site_count = modes.shape
    share = steps * momenta.shape[0] * 32 // sites
    owned = (lax.axis_index("deep") * flat + lax.axis_index("flat")) * (share // 2)
    place = [lax.axis_index(name) for name in AXES]
    place = jnp.stack(place + [owned // 4 % 4, jnp.int32(flat), owned % 4]).astype(jnp.int32)

    packed = jnp.transpose(modes.reshape(slots, per_block, 4, 3, site_count), (2, 1, 0, 3, 4))
    packed = packed.reshape(4, per_block, slots * 3 * site_count)

    mine = lax.dynamic_slice_in_dim(momenta, owned // 16, 1, 0)
    weights = phase_table(mine, jnp.int32(0), sites * site_count, LEXT)[0]
    weights = jnp.transpose(weights.reshape(2, sites, site_count), (1, 0, 2))

    if (groups, deep, flat) == (2, 4, 2) and share in (8, 16, 32):
        return swap_in_windows(packed, place, weights, share)
    return gather_whole(packed, place, weights, share)


def solution(mesh):
    count, sites = mesh.shape["blk"], mesh.shape["site"]
    flat = 2 ** (int(math.log2(sites)) // 2)
    split = Mesh(mesh.devices.reshape(count // 2, 2, sites // flat, flat), AXES)
    placed = (P(None, None, ("pair", "core"), None, ("deep", "flat")), P())
    return jax.shard_map(
        shards,
        mesh=split,
        in_specs=placed,
        out_specs=P(("deep", "flat"), ("pair", "core"), None),
        check_vma=False,
    )
```

time: 140 us -> 84.1 us (0.60)
  waiting for transfers between devices: 98.1 us -> 42.3 us
  starting transfers between devices: 0.01 us -> 24 us
  between operations: 13.4 us -> 0.21 us
  Pallas kernels: 23.8 us -> 15.3 us
    all_gather x1 -> x0, waiting for transfers between devices: 98 us -> none  [shards(): near = lax.all_gather(packed, ('pair', 'site'))]
    ppermute x1 -> x31, waiting for transfers between devices: 0.01 us -> 42.3 us  [move(): return lax.ppermute(array, AXES, pairs)]
    ppermute x1 -> x31, starting transfers between devices: 0.01 us -> 24 us  [move(): return lax.ppermute(array, AXES, pairs)]
    pallas_call x2 -> x6, Pallas kernels: 23.8 us -> 15.3 us  [add(): pl.pallas_call(functools.partial(add_shards, tuple(names), totals is not...]
  transfers between devices with their start and end apart: 2 -> 31, of which waited for: 1 -> 7; matrix products, arithmetic and copies ran while one was open for 1% -> 0% of each run, Pallas kernels for 8% -> 16%
where the time goes in v3:
time: 84.1 us; the launch traced here: 83.9 us
  waiting for transfers between devices  42.3 us (50%)
  starting transfers between devices  24 us (29%)
  Pallas kernels  15.3 us (18%)
  local copies, waits for them, and re-layouts  1.78 us (2%)
    ppermute x31, waiting for transfers between devices, move(): return lax.ppermute(array, AXES, pairs)  42.3 us
    ppermute x31, starting transfers between devices, move(): return lax.ppermute(array, AXES, pairs)  24 us
    pallas_call x6, Pallas kernels, add(): pl.pallas_call(functools.partial(add_shards, tuple(names), totals is not...  15.3 us
  transfers between devices with their start and end apart: 31, of which 7 were waited for; matrix products, arithmetic and copies ran while one was open for 0% of the time, Pallas kernels for 16%

profile of v3, /device:TPU:0, one launch (start us, length us, event | category | flops | bytes accessed | tf_op | source)
XLA Modules:
  0.0 83.9 jit_solution(15110973177882486887)
XLA Ops:
  0.0 1.3 %copy.9 = bf16[2,64,4,3,128]{4,3,0,1,2:T(4,128)(2,1)S(1)} copy(bf16[2,64,4,3,128]{4,1,3,2,0:T(8,128)(2,1)} %bitcast.32) | data formatting | bytes 786432 | tf_op jit(solution)/shard_map/reshape | solution.py:321
  1.4 0.3 reshape.222.refs_0_.refs_7_
  1.7 3.1 %collective-permute-start.3 = (bf16[4,64,768]{2,1,0:T(8,128)(2,1)S(1)}, bf16[4,64,768]{2,1,0:T(8,128)(2,1)S(1)}, u32[]{:S(2)}, u32[]{:S(2)}) collective-permute-start(bf16[4,64,768]{2,1,0:T(8,128)(2,1)S(1)} %reshape.222.refs_0_.refs_7_), channel_id=1, source_target_pairs={{0,2},{1,3},{2,0},{3,1},{4,6},{5,7},{6,4},{7,5},{8,10},{9,11},{10,... | collective-permute-start | bytes 1179656 | tf_op jit(solution)/shard_map/ppermute | solution.py:138
  4.8 1.5 %collective-permute-start.2 = (bf16[4,64,768]{2,1,0:T(8,128)(2,1)S(1)}, bf16[4,64,768]{2,1,0:T(8,128)(2,1)S(1)}, u32[]{:S(2)}, u32[]{:S(2)}) collective-permute-start(bf16[4,64,768]{2,1,0:T(8,128)(2,1)S(1)} %reshape.222.refs_0_.refs_7_), channel_id=1, source_target_pairs={{0,1},{1,0},{2,3},{3,2},{4,5},{5,4},{6,7},{7,6},{8,24},{9,25},{10,... | collective-permute-start | bytes 1179656 | tf_op jit(solution)/shard_map/ppermute | solution.py:138
  6.3 1.5 %collective-permute-start.1 = (bf16[4,64,768]{2,1,0:T(8,128)(2,1)S(1)}, bf16[4,64,768]{2,1,0:T(8,128)(2,1)S(1)}, u32[]{:S(2)}, u32[]{:S(2)}) collective-permute-start(bf16[4,64,768]{2,1,0:T(8,128)(2,1)S(1)} %reshape.222.refs_0_.refs_7_), channel_id=1, source_target_pairs={{0,16},{1,17},{2,18},{3,19},{4,20},{5,21},{6,22},{7,23},{8,9},{9,8... | collective-permute-start | bytes 1179656 | tf_op jit(solution)/shard_map/ppermute | solution.py:138
  7.8 0.0 collective-permute-start
  7.9 6.0 %collective-permute-done.3.refs_1_.refs_10_.refs_8_.refs_5_ = bf16[4,64,768]{2,1,0:T(8,128)(2,1)S(1)} collective-permute-done((bf16[4,64,768]{2,1,0:T(8,128)(2,1)S(1)}, bf16[4,64,768]{2,1,0:T(8,128)(2,1)S(1)}, u32[]{:S(2)}, u32[]{:S(2)}) %collective-permute-start.3) | collective-permute-done | bytes 393248 | tf_op jit(solution)/shard_map/ppermute | solution.py:138
  13.9 2.7 %collective-permute-done.2.refs_2_.refs_9_ = bf16[4,64,768]{2,1,0:T(8,128)(2,1)S(1)} collective-permute-done((bf16[4,64,768]{2,1,0:T(8,128)(2,1)S(1)}, bf16[4,64,768]{2,1,0:T(8,128)(2,1)S(1)}, u32[]{:S(2)}, u32[]{:S(2)}) %collective-permute-start.2) | collective-permute-done | bytes 393248 | tf_op jit(solution)/shard_map/ppermute | solution.py:138
  16.6 0.0 collective-permute-done.1.refs_1_.refs_8_
  16.6 0.0 collective-permute-done.refs_3_
  16.6 0.0 collective-permute-start.5
  16.6 2.7 %collective-permute-start.10 = (bf16[4,64,768]{2,1,0:T(8,128)(2,1)S(1)}, bf16[4,64,768]{2,1,0:T(8,128)(2,1)S(1)}, u32[]{:S(2)}, u32[]{:S(2)}) collective-permute-start(bf16[4,64,768]{2,1,0:T(8,128)(2,1)S(1)} %reshape.222.refs_0_.refs_7_), channel_id=1, source_target_pairs={{0,4},{1,5},{2,6},{3,7},{4,0},{5,1},{6,2},{7,3},{8,12},{9,13},{10,... | collective-permute-start | bytes 1179656 | tf_op jit(solution)/shard_map/ppermute | solution.py:138
  19.3 0.1 stack.44.place_ref
  19.3 0.1 fusion
  19.4 1.6 %collective-permute-start.8 = (bf16[4,64,768]{2,1,0:T(8,128)(2,1)S(1)}, bf16[4,64,768]{2,1,0:T(8,128)(2,1)S(1)}, u32[]{:S(2)}, u32[]{:S(2)}) collective-permute-start(bf16[4,64,768]{2,1,0:T(8,128)(2,1)S(1)} %collective-permute-done.1.refs_1_.refs_8_), channel_id=1, source_target_pairs={{0,1},{1,0},{2,3},{3,2},{4,5},{5,4},{6,7},{7,6},{8,24},{9,25},{10,... | collective-permute-start | bytes 1179656 | tf_op jit(solution)/shard_map/ppermute | solution.py:138
  21.0 0.0 collective-permute-start.4
  21.0 0.5 collective-permute-start.9
  21.5 0.0 collective-permute-done.5.refs_5_
  21.5 1.4 %collective-permute-start.7 = (bf16[4,64,768]{2,1,0:T(8,128)(2,1)S(1)}, bf16[4,64,768]{2,1,0:T(8,128)(2,1)S(1)}, u32[]{:S(2)}, u32[]{:S(2)}) collective-permute-start(bf16[4,64,768]{2,1,0:T(8,128)(2,1)S(1)} %collective-permute-done.3.refs_1_.refs_10_.refs_8_.refs_5_), channel_id=1, source_target_pairs={{0,16},{1,17},{2,18},{3,19},{4,20},{5,21},{6,22},{7,23},{8,9},{9,8... | collective-permute-start | bytes 1179656 | tf_op jit(solution)/shard_map/ppermute | solution.py:138
  22.9 14.3 %collective-permute-done.10.refs_3_.refs_11_.refs_8_ = bf16[4,64,768]{2,1,0:T(8,128)(2,1)S(1)} collective-permute-done((bf16[4,64,768]{2,1,0:T(8,128)(2,1)S(1)}, bf16[4,64,768]{2,1,0:T(8,128)(2,1)S(1)}, u32[]{:S(2)}, u32[]{:S(2)}) %collective-permute-start.10) | collective-permute-done | bytes 393248 | tf_op jit(solution)/shard_map/ppermute | solution.py:138
  37.3 0.1 collective-permute-start.6
  37.3 0.1 multiply_cosine_fusion
  37.5 1.8 %shard_map.28.refs_10_ = f32[2,2,256,256]{3,2,1,0:T(8,128)S(1)} custom-call(s32[7]{0:T(128)S(1)} %stack.44.place_ref, f32[8,2,128]{2,1,0:T(2,128)S(1)} %maximum_bitcast_fusion.weights_ref, bf16[4,64,768]{2,1,0:T(8,128)(2,1)S(1)} %reshape.222.refs_0_.refs_7_, bf16[4,64,768]{2,1,0:T(8,128)(2,1)S(1)} %collective-permute-done.1.refs_1_.refs_8_, ...), custom_call_target="tpu_custom_call" | custom-call | flops 805306368 | bytes 3670016 | tf_op jit(solution)/shard_map/pallas_call | solution.py:171
  39.3 0.0 collective-permute-done.8.refs_0_
  39.3 0.0 collective-permute-done.4.refs_4_
  39.3 0.0 collective-permute-done.9.refs_3_.refs_12_.refs_10_.refs_7_
  39.3 0.0 collective-permute-done.7.refs_2_.refs_11_.refs_9_.refs_6_
  39.3 0.0 collective-permute-done.6.refs_6_
  39.3 0.5 collective-permute-start.11
  39.9 0.1 collective-permute-start.12
  39.9 0.0 collective-permute-start.17
  39.9 1.6 %collective-permute-start.16 = (bf16[4,64,768]{2,1,0:T(8,128)(2,1)S(1)}, bf16[4,64,768]{2,1,0:T(8,128)(2,1)S(1)}, u32[]{:S(2)}, u32[]{:S(2)}) collective-permute-start(bf16[4,64,768]{2,1,0:T(8,128)(2,1)S(1)} %collective-permute-done.10.refs_3_.refs_11_.refs_8_), channel_id=1, source_target_pairs={{0,1},{1,0},{2,3},{3,2},{4,5},{5,4},{6,7},{7,6},{8,24},{9,25},{10,... | collective-permute-start | bytes 1179656 | tf_op jit(solution)/shard_map/ppermute | solution.py:138
  41.5 0.0 collective-permute-start.13
  41.5 0.0 collective-permute-done.11.refs_1_
  41.5 0.6 collective-permute-start.15
  42.1 0.0 collective-permute-done.12.refs_0_
  42.1 0.8 collective-permute-start.14
  42.9 2.6 %shard_map.29.refs_13_ = f32[2,2,256,256]{3,2,1,0:T(8,128)S(1)} custom-call(s32[7]{0:T(128)S(1)} %stack.44.place_ref, f32[8,2,128]{2,1,0:T(2,128)S(1)} %maximum_bitcast_fusion.weights_ref, bf16[4,64,768]{2,1,0:T(8,128)(2,1)S(1)} %collective-permute-done.8.refs_0_, bf16[4,64,768]{2,1,0:T(8,128)(2,1)S(1)} %collective-permute-done.3.refs_1_.refs_10_.refs_8_.refs_5_, ...), custom_call_target="tpu_custom_call" | custom-call | flops 1409286144 | bytes 4849664 | tf_op jit(solution)/shard_map/pallas_call | solution.py:171
  45.5 0.0 collective-permute-done.13.refs_2_
  45.5 5.9 %collective-permute-done.17.refs_0_.refs_11_.refs_1_ = bf16[4,64,768]{2,1,0:T(8,128)(2,1)S(1)} collective-permute-done((bf16[4,64,768]{2,1,0:T(8,128)(2,1)S(1)}, bf16[4,64,768]{2,1,0:T(8,128)(2,1)S(1)}, u32[]{:S(2)}, u32[]{:S(2)}) %collective-permute-start.17) | collective-permute-done | bytes 393248 | tf_op jit(solution)/shard_map/ppermute | solution.py:138
  51.4 0.0 collective-permute-done.16.refs_5_.refs_13_.refs_10_
  51.4 0.0 collective-permute-done.15.refs_4_.refs_12_.refs_9_
  51.4 0.0 collective-permute-done.14.refs_6_
  51.4 1.7 %collective-permute-start.22 = (bf16[4,64,768]{2,1,0:T(8,128)(2,1)S(1)}, bf16[4,64,768]{2,1,0:T(8,128)(2,1)S(1)}, u32[]{:S(2)}, u32[]{:S(2)}) collective-permute-start(bf16[4,64,768]{2,1,0:T(8,128)(2,1)S(1)} %collective-permute-done.8.refs_0_), channel_id=1, source_target_pairs={{0,2},{1,3},{2,0},{3,1},{4,6},{5,7},{6,4},{7,5},{8,10},{9,11},{10,... | collective-permute-start | bytes 1179656 | tf_op jit(solution)/shard_map/ppermute | solution.py:138
  53.1 0.3 collective-permute-start.19
  53.5 2.0 %collective-permute-start.23 = (bf16[4,64,768]{2,1,0:T(8,128)(2,1)S(1)}, bf16[4,64,768]{2,1,0:T(8,128)(2,1)S(1)}, u32[]{:S(2)}, u32[]{:S(2)}) collective-permute-start(bf16[4,64,768]{2,1,0:T(8,128)(2,1)S(1)} %collective-permute-done.15.refs_4_.refs_12_.refs_9_), channel_id=1, source_target_pairs={{0,1},{1,0},{2,3},{3,2},{4,5},{5,4},{6,7},{7,6},{8,24},{9,25},{10,... | collective-permute-start | bytes 1179656 | tf_op jit(solution)/shard_map/ppermute | solution.py:138
  55.5 0.0 collective-permute-start.18
  55.5 0.5 collective-permute-start.24
  56.0 7.0 %collective-permute-done.22.refs_3_ = bf16[4,64,768]{2,1,0:T(8,128)(2,1)S(1)} collective-permute-done((bf16[4,64,768]{2,1,0:T(8,128)(2,1)S(1)}, bf16[4,64,768]{2,1,0:T(8,128)(2,1)S(1)}, u32[]{:S(2)}, u32[]{:S(2)}) %collective-permute-start.22) | collective-permute-done | bytes 393248 | tf_op jit(solution)/shard_map/ppermute | solution.py:138
  63.1 0.5 collective-permute-start.21
  63.6 0.0 collective-permute-done.19.refs_6_
  63.6 0.6 collective-permute-start.20
  64.2 3.0 %shard_map.30.refs_14_ = f32[2,2,256,256]{3,2,1,0:T(8,128)S(1)} custom-call(s32[7]{0:T(128)S(1)} %stack.44.place_ref, f32[8,2,128]{2,1,0:T(2,128)S(1)} %maximum_bitcast_fusion.weights_ref, bf16[4,64,768]{2,1,0:T(8,128)(2,1)S(1)} %collective-permute-done.12.refs_0_, bf16[4,64,768]{2,1,0:T(8,128)(2,1)S(1)} %collective-permute-done.11.refs_1_, ...), custom_call_target="tpu_custom_call" | custom-call | flops 1409286144 | bytes 4849664 | tf_op jit(solution)/shard_map/pallas_call | solution.py:171
  67.2 0.0 collective-permute-done.23.refs_4_
  67.2 0.0 collective-permute-done.18.refs_5_
  67.2 3.6 %collective-permute-done.21.refs_1_.refs_12_.refs_2_ = bf16[4,64,768]{2,1,0:T(8,128)(2,1)S(1)} collective-permute-done((bf16[4,64,768]{2,1,0:T(8,128)(2,1)S(1)}, bf16[4,64,768]{2,1,0:T(8,128)(2,1)S(1)}, u32[]{:S(2)}, u32[]{:S(2)}) %collective-permute-start.21) | collective-permute-done | bytes 393248 | tf_op jit(solution)/shard_map/ppermute | solution.py:138
  70.8 0.5 collective-permute-start.27
  71.3 0.0 collective-permute-start.28
  71.3 1.9 %collective-permute-start.29 = (bf16[4,64,768]{2,1,0:T(8,128)(2,1)S(1)}, bf16[4,64,768]{2,1,0:T(8,128)(2,1)S(1)}, u32[]{:S(2)}, u32[]{:S(2)}) collective-permute-start(bf16[4,64,768]{2,1,0:T(8,128)(2,1)S(1)} %collective-permute-done.21.refs_1_.refs_12_.refs_2_), channel_id=1, source_target_pairs={{0,1},{1,0},{2,3},{3,2},{4,5},{5,4},{6,7},{7,6},{8,24},{9,25},{10,... | collective-permute-start | bytes 1179656 | tf_op jit(solution)/shard_map/ppermute | solution.py:138
  73.2 3.2 %shard_map.31.refs_14_ = f32[2,2,256,256]{3,2,1,0:T(8,128)S(1)} custom-call(s32[7]{0:T(128)S(1)} %stack.44.place_ref, f32[8,2,128]{2,1,0:T(2,128)S(1)} %maximum_bitcast_fusion.weights_ref, bf16[4,64,768]{2,1,0:T(8,128)(2,1)S(1)} %collective-permute-done.17.refs_0_.refs_11_.refs_1_, bf16[4,64,768]{2,1,0:T(8,128)(2,1)S(1)} %collective-permute-done.21.refs_1_.refs_12_.refs_2_, ...), custom_call_target="tpu_custom_call" | custom-call | flops 1610612736 | bytes 5242880 | tf_op jit(solution)/shard_map/pallas_call | solution.py:171
  76.4 0.0 collective-permute-done.28.refs_4_
  76.5 2.7 %collective-permute-done.29.refs_0_ = bf16[4,64,768]{2,1,0:T(8,128)(2,1)S(1)} collective-permute-done((bf16[4,64,768]{2,1,0:T(8,128)(2,1)S(1)}, bf16[4,64,768]{2,1,0:T(8,128)(2,1)S(1)}, u32[]{:S(2)}, u32[]{:S(2)}) %collective-permute-start.29) | collective-permute-done | bytes 393248 | tf_op jit(solution)/shard_map/ppermute | solution.py:138
  79.1 2.4 %shard_map.32.refs_4_ = f32[2,2,256,256]{3,2,1,0:T(8,128)S(1)} custom-call(s32[7]{0:T(128)S(1)} %stack.44.place_ref, f32[8,2,128]{2,1,0:T(2,128)S(1)} %maximum_bitcast_fusion.weights_ref, bf16[4,64,768]{2,1,0:T(8,128)(2,1)S(1)} %collective-permute-done.29.refs_0_, bf16[4,64,768]{2,1,0:T(8,128)(2,1)S(1)} %collective-permute-done.26.refs_1_, ...), custom_call_target="tpu_custom_call" | custom-call | flops 1006632960 | bytes 4063232 | tf_op jit(solution)/shard_map/pallas_call | solution.py:171
  81.6 2.3 %shard_map.33 = f32[16,64,256]{2,1,0:T(8,128)} custom-call(s32[7]{0:T(128)S(1)} %stack.44.place_ref, f32[8,2,128]{2,1,0:T(2,128)S(1)} %maximum_bitcast_fusion.weights_ref, bf16[4,64,768]{2,1,0:T(8,128)(2,1)S(1)} %collective-permute-done.30.refs_0_, bf16[4,64,768]{2,1,0:T(8,128)(2,1)S(1)} %collective-permute-done.17.refs_0_.refs_11_.refs_1_, ...), custom_call_target="tpu_custom_call" | custom-call | flops 201326592 | bytes 2490368 | tf_op jit(solution)/shard_map/pallas_call | solution.py:171
  (16 shorter events, 0.1 us)
Async XLA Ops:
  0.0 19.2 %copy-start = (s32[4,3]{1,0:T(4,128)S(1)}, s32[4,3]{1,0:T(4,128)}, u32[]{:S(2)}) copy-start(s32[4,3]{1,0:T(4,128)} %param.3) | copy-start | bytes 148
  1.7 12.2 %collective-permute-start.3 = (bf16[4,64,768]{2,1,0:T(8,128)(2,1)S(1)}, bf16[4,64,768]{2,1,0:T(8,128)(2,1)S(1)}, u32[]{:S(2)}, u32[]{:S(2)}) collective-permute-start(bf16[4,64,768]{2,1,0:T(8,128)(2,1)S(1)} %reshape.222.refs_0_.refs_7_), channel_id=1, source_target_pairs={{0,2},{1,3},{2,0},{3,1},{4,6},{5,7},{6,4},{7,5},{8,10},{9,11},{10,... | collective-permute-start | bytes 1179656 | tf_op jit(solution)/shard_map/ppermute | solution.py:138
  4.8 11.8 %collective-permute-start.2 = (bf16[4,64,768]{2,1,0:T(8,128)(2,1)S(1)}, bf16[4,64,768]{2,1,0:T(8,128)(2,1)S(1)}, u32[]{:S(2)}, u32[]{:S(2)}) collective-permute-start(bf16[4,64,768]{2,1,0:T(8,128)(2,1)S(1)} %reshape.222.refs_0_.refs_7_), channel_id=1, source_target_pairs={{0,1},{1,0},{2,3},{3,2},{4,5},{5,4},{6,7},{7,6},{8,24},{9,25},{10,... | collective-permute-start | bytes 1179656 | tf_op jit(solution)/shard_map/ppermute | solution.py:138
  6.3 10.3 %collective-permute-start.1 = (bf16[4,64,768]{2,1,0:T(8,128)(2,1)S(1)}, bf16[4,64,768]{2,1,0:T(8,128)(2,1)S(1)}, u32[]{:S(2)}, u32[]{:S(2)}) collective-permute-start(bf16[4,64,768]{2,1,0:T(8,128)(2,1)S(1)} %reshape.222.refs_0_.refs_7_), channel_id=1, source_target_pairs={{0,16},{1,17},{2,18},{3,19},{4,20},{5,21},{6,22},{7,23},{8,9},{9,8... | collective-permute-start | bytes 1179656 | tf_op jit(solution)/shard_map/ppermute | solution.py:138
  7.8 8.8 %collective-permute-start = (bf16[4,64,768]{2,1,0:T(8,128)(2,1)S(1)}, bf16[4,64,768]{2,1,0:T(8,128)(2,1)S(1)}, u32[]{:S(2)}, u32[]{:S(2)}) collective-permute-start(bf16[4,64,768]{2,1,0:T(8,128)(2,1)S(1)} %reshape.222.refs_0_.refs_7_), channel_id=1, source_target_pairs={{0,8},{1,9},{2,10},{3,11},{4,12},{5,13},{6,14},{7,15},{8,0},{9,1},... | collective-permute-start | bytes 1179656 | tf_op jit(solution)/shard_map/ppermute | solution.py:138
  16.6 5.0 %collective-permute-start.5 = (bf16[4,64,768]{2,1,0:T(8,128)(2,1)S(1)}, bf16[4,64,768]{2,1,0:T(8,128)(2,1)S(1)}, u32[]{:S(2)}, u32[]{:S(2)}) collective-permute-start(bf16[4,64,768]{2,1,0:T(8,128)(2,1)S(1)} %collective-permute-done.2.refs_2_.refs_9_), channel_id=1, source_target_pairs={{0,8},{1,9},{2,10},{3,11},{4,12},{5,13},{6,14},{7,15},{8,0},{9,1},... | collective-permute-start | bytes 1179656 | tf_op jit(solution)/shard_map/ppermute | solution.py:138
  16.6 20.7 %collective-permute-start.10 = (bf16[4,64,768]{2,1,0:T(8,128)(2,1)S(1)}, bf16[4,64,768]{2,1,0:T(8,128)(2,1)S(1)}, u32[]{:S(2)}, u32[]{:S(2)}) collective-permute-start(bf16[4,64,768]{2,1,0:T(8,128)(2,1)S(1)} %reshape.222.refs_0_.refs_7_), channel_id=1, source_target_pairs={{0,4},{1,5},{2,6},{3,7},{4,0},{5,1},{6,2},{7,3},{8,12},{9,13},{10,... | collective-permute-start | bytes 1179656 | tf_op jit(solution)/shard_map/ppermute | solution.py:138
  19.4 19.8 %collective-permute-start.8 = (bf16[4,64,768]{2,1,0:T(8,128)(2,1)S(1)}, bf16[4,64,768]{2,1,0:T(8,128)(2,1)S(1)}, u32[]{:S(2)}, u32[]{:S(2)}) collective-permute-start(bf16[4,64,768]{2,1,0:T(8,128)(2,1)S(1)} %collective-permute-done.1.refs_1_.refs_8_), channel_id=1, source_target_pairs={{0,1},{1,0},{2,3},{3,2},{4,5},{5,4},{6,7},{7,6},{8,24},{9,25},{10,... | collective-permute-start | bytes 1179656 | tf_op jit(solution)/shard_map/ppermute | solution.py:138
  21.0 18.3 %collective-permute-start.4 = (bf16[4,64,768]{2,1,0:T(8,128)(2,1)S(1)}, bf16[4,64,768]{2,1,0:T(8,128)(2,1)S(1)}, u32[]{:S(2)}, u32[]{:S(2)}) collective-permute-start(bf16[4,64,768]{2,1,0:T(8,128)(2,1)S(1)} %collective-permute-done.1.refs_1_.refs_8_), channel_id=1, source_target_pairs={{0,8},{1,9},{2,10},{3,11},{4,12},{5,13},{6,14},{7,15},{8,0},{9,1},... | collective-permute-start | bytes 1179656 | tf_op jit(solution)/shard_map/ppermute | solution.py:138
  21.0 18.3 %collective-permute-start.9 = (bf16[4,64,768]{2,1,0:T(8,128)(2,1)S(1)}, bf16[4,64,768]{2,1,0:T(8,128)(2,1)S(1)}, u32[]{:S(2)}, u32[]{:S(2)}) collective-permute-start(bf16[4,64,768]{2,1,0:T(8,128)(2,1)S(1)} %collective-permute-done.3.refs_1_.refs_10_.refs_8_.refs_5_), channel_id=1, source_target_pairs={{0,1},{1,0},{2,3},{3,2},{4,5},{5,4},{6,7},{7,6},{8,24},{9,25},{10,... | collective-permute-start | bytes 1179656 | tf_op jit(solution)/shard_map/ppermute | solution.py:138
  21.5 17.8 %collective-permute-start.7 = (bf16[4,64,768]{2,1,0:T(8,128)(2,1)S(1)}, bf16[4,64,768]{2,1,0:T(8,128)(2,1)S(1)}, u32[]{:S(2)}, u32[]{:S(2)}) collective-permute-start(bf16[4,64,768]{2,1,0:T(8,128)(2,1)S(1)} %collective-permute-done.3.refs_1_.refs_10_.refs_8_.refs_5_), channel_id=1, source_target_pairs={{0,16},{1,17},{2,18},{3,19},{4,20},{5,21},{6,22},{7,23},{8,9},{9,8... | collective-permute-start | bytes 1179656 | tf_op jit(solution)/shard_map/ppermute | solution.py:138
  37.3 2.1 %collective-permute-start.6 = (bf16[4,64,768]{2,1,0:T(8,128)(2,1)S(1)}, bf16[4,64,768]{2,1,0:T(8,128)(2,1)S(1)}, u32[]{:S(2)}, u32[]{:S(2)}) collective-permute-start(bf16[4,64,768]{2,1,0:T(8,128)(2,1)S(1)} %collective-permute-done.3.refs_1_.refs_10_.refs_8_.refs_5_), channel_id=1, source_target_pairs={{0,8},{1,9},{2,10},{3,11},{4,12},{5,13},{6,14},{7,15},{8,0},{9,1},... | collective-permute-start | bytes 1179656 | tf_op jit(solution)/shard_map/ppermute | solution.py:138
  39.3 2.2 %collective-permute-start.11 = (bf16[4,64,768]{2,1,0:T(8,128)(2,1)S(1)}, bf16[4,64,768]{2,1,0:T(8,128)(2,1)S(1)}, u32[]{:S(2)}, u32[]{:S(2)}) collective-permute-start(bf16[4,64,768]{2,1,0:T(8,128)(2,1)S(1)} %collective-permute-done.7.refs_2_.refs_11_.refs_9_.refs_6_), channel_id=1, source_target_pairs={{0,8},{1,9},{2,10},{3,11},{4,12},{5,13},{6,14},{7,15},{8,0},{9,1},... | collective-permute-start | bytes 1179656 | tf_op jit(solution)/shard_map/ppermute | solution.py:138
  39.9 2.3 %collective-permute-start.12 = (bf16[4,64,768]{2,1,0:T(8,128)(2,1)S(1)}, bf16[4,64,768]{2,1,0:T(8,128)(2,1)S(1)}, u32[]{:S(2)}, u32[]{:S(2)}) collective-permute-start(bf16[4,64,768]{2,1,0:T(8,128)(2,1)S(1)} %collective-permute-done.8.refs_0_), channel_id=1, source_target_pairs={{0,8},{1,9},{2,10},{3,11},{4,12},{5,13},{6,14},{7,15},{8,0},{9,1},... | collective-permute-start | bytes 1179656 | tf_op jit(solution)/shard_map/ppermute | solution.py:138
  39.9 11.5 %collective-permute-start.17 = (bf16[4,64,768]{2,1,0:T(8,128)(2,1)S(1)}, bf16[4,64,768]{2,1,0:T(8,128)(2,1)S(1)}, u32[]{:S(2)}, u32[]{:S(2)}) collective-permute-start(bf16[4,64,768]{2,1,0:T(8,128)(2,1)S(1)} %collective-permute-done.10.refs_3_.refs_11_.refs_8_), channel_id=1, source_target_pairs={{0,2},{1,3},{2,0},{3,1},{4,6},{5,7},{6,4},{7,5},{8,10},{9,11},{10,... | collective-permute-start | bytes 1179656 | tf_op jit(solution)/shard_map/ppermute | solution.py:138
  39.9 11.5 %collective-permute-start.16 = (bf16[4,64,768]{2,1,0:T(8,128)(2,1)S(1)}, bf16[4,64,768]{2,1,0:T(8,128)(2,1)S(1)}, u32[]{:S(2)}, u32[]{:S(2)}) collective-permute-start(bf16[4,64,768]{2,1,0:T(8,128)(2,1)S(1)} %collective-permute-done.10.refs_3_.refs_11_.refs_8_), channel_id=1, source_target_pairs={{0,1},{1,0},{2,3},{3,2},{4,5},{5,4},{6,7},{7,6},{8,24},{9,25},{10,... | collective-permute-start | bytes 1179656 | tf_op jit(solution)/shard_map/ppermute | solution.py:138
  41.5 4.0 %collective-permute-start.13 = (bf16[4,64,768]{2,1,0:T(8,128)(2,1)S(1)}, bf16[4,64,768]{2,1,0:T(8,128)(2,1)S(1)}, u32[]{:S(2)}, u32[]{:S(2)}) collective-permute-start(bf16[4,64,768]{2,1,0:T(8,128)(2,1)S(1)} %collective-permute-done.9.refs_3_.refs_12_.refs_10_.refs_7_), channel_id=1, source_target_pairs={{0,8},{1,9},{2,10},{3,11},{4,12},{5,13},{6,14},{7,15},{8,0},{9,1},... | collective-permute-start | bytes 1179656 | tf_op jit(solution)/shard_map/ppermute | solution.py:138
  41.5 9.9 %collective-permute-start.15 = (bf16[4,64,768]{2,1,0:T(8,128)(2,1)S(1)}, bf16[4,64,768]{2,1,0:T(8,128)(2,1)S(1)}, u32[]{:S(2)}, u32[]{:S(2)}) collective-permute-start(bf16[4,64,768]{2,1,0:T(8,128)(2,1)S(1)} %collective-permute-done.10.refs_3_.refs_11_.refs_8_), channel_id=1, source_target_pairs={{0,16},{1,17},{2,18},{3,19},{4,20},{5,21},{6,22},{7,23},{8,9},{9,8... | collective-permute-start | bytes 1179656 | tf_op jit(solution)/shard_map/ppermute | solution.py:138
  42.1 9.3 %collective-permute-start.14 = (bf16[4,64,768]{2,1,0:T(8,128)(2,1)S(1)}, bf16[4,64,768]{2,1,0:T(8,128)(2,1)S(1)}, u32[]{:S(2)}, u32[]{:S(2)}) collective-permute-start(bf16[4,64,768]{2,1,0:T(8,128)(2,1)S(1)} %collective-permute-done.10.refs_3_.refs_11_.refs_8_), channel_id=1, source_target_pairs={{0,8},{1,9},{2,10},{3,11},{4,12},{5,13},{6,14},{7,15},{8,0},{9,1},... | collective-permute-start | bytes 1179656 | tf_op jit(solution)/shard_map/ppermute | solution.py:138
  51.4 11.6 %collective-permute-start.22 = (bf16[4,64,768]{2,1,0:T(8,128)(2,1)S(1)}, bf16[4,64,768]{2,1,0:T(8,128)(2,1)S(1)}, u32[]{:S(2)}, u32[]{:S(2)}) collective-permute-start(bf16[4,64,768]{2,1,0:T(8,128)(2,1)S(1)} %collective-permute-done.8.refs_0_), channel_id=1, source_target_pairs={{0,2},{1,3},{2,0},{3,1},{4,6},{5,7},{6,4},{7,5},{8,10},{9,11},{10,... | collective-permute-start | bytes 1179656 | tf_op jit(solution)/shard_map/ppermute | solution.py:138
  53.1 10.4 %collective-permute-start.19 = (bf16[4,64,768]{2,1,0:T(8,128)(2,1)S(1)}, bf16[4,64,768]{2,1,0:T(8,128)(2,1)S(1)}, u32[]{:S(2)}, u32[]{:S(2)}) collective-permute-start(bf16[4,64,768]{2,1,0:T(8,128)(2,1)S(1)} %collective-permute-done.16.refs_5_.refs_13_.refs_10_), channel_id=1, source_target_pairs={{0,8},{1,9},{2,10},{3,11},{4,12},{5,13},{6,14},{7,15},{8,0},{9,1},... | collective-permute-start | bytes 1179656 | tf_op jit(solution)/shard_map/ppermute | solution.py:138
  53.5 13.7 %collective-permute-start.23 = (bf16[4,64,768]{2,1,0:T(8,128)(2,1)S(1)}, bf16[4,64,768]{2,1,0:T(8,128)(2,1)S(1)}, u32[]{:S(2)}, u32[]{:S(2)}) collective-permute-start(bf16[4,64,768]{2,1,0:T(8,128)(2,1)S(1)} %collective-permute-done.15.refs_4_.refs_12_.refs_9_), channel_id=1, source_target_pairs={{0,1},{1,0},{2,3},{3,2},{4,5},{5,4},{6,7},{7,6},{8,24},{9,25},{10,... | collective-permute-start | bytes 1179656 | tf_op jit(solution)/shard_map/ppermute | solution.py:138
  55.5 11.7 %collective-permute-start.18 = (bf16[4,64,768]{2,1,0:T(8,128)(2,1)S(1)}, bf16[4,64,768]{2,1,0:T(8,128)(2,1)S(1)}, u32[]{:S(2)}, u32[]{:S(2)}) collective-permute-start(bf16[4,64,768]{2,1,0:T(8,128)(2,1)S(1)} %collective-permute-done.15.refs_4_.refs_12_.refs_9_), channel_id=1, source_target_pairs={{0,8},{1,9},{2,10},{3,11},{4,12},{5,13},{6,14},{7,15},{8,0},{9,1},... | collective-permute-start | bytes 1179656 | tf_op jit(solution)/shard_map/ppermute | solution.py:138
  55.5 11.7 %collective-permute-start.24 = (bf16[4,64,768]{2,1,0:T(8,128)(2,1)S(1)}, bf16[4,64,768]{2,1,0:T(8,128)(2,1)S(1)}, u32[]{:S(2)}, u32[]{:S(2)}) collective-permute-start(bf16[4,64,768]{2,1,0:T(8,128)(2,1)S(1)} %collective-permute-done.17.refs_0_.refs_11_.refs_1_), channel_id=1, source_target_pairs={{0,1},{1,0},{2,3},{3,2},{4,5},{5,4},{6,7},{7,6},{8,24},{9,25},{10,... | collective-permute-start | bytes 1179656 | tf_op jit(solution)/shard_map/ppermute | solution.py:138
  63.1 7.8 %collective-permute-start.21 = (bf16[4,64,768]{2,1,0:T(8,128)(2,1)S(1)}, bf16[4,64,768]{2,1,0:T(8,128)(2,1)S(1)}, u32[]{:S(2)}, u32[]{:S(2)}) collective-permute-start(bf16[4,64,768]{2,1,0:T(8,128)(2,1)S(1)} %collective-permute-done.17.refs_0_.refs_11_.refs_1_), channel_id=1, source_target_pairs={{0,16},{1,17},{2,18},{3,19},{4,20},{5,21},{6,22},{7,23},{8,9},{9,8... | collective-permute-start | bytes 1179656 | tf_op jit(solution)/shard_map/ppermute | solution.py:138
  63.6 7.2 %collective-permute-start.20 = (bf16[4,64,768]{2,1,0:T(8,128)(2,1)S(1)}, bf16[4,64,768]{2,1,0:T(8,128)(2,1)S(1)}, u32[]{:S(2)}, u32[]{:S(2)}) collective-permute-start(bf16[4,64,768]{2,1,0:T(8,128)(2,1)S(1)} %collective-permute-done.17.refs_0_.refs_11_.refs_1_), channel_id=1, source_target_pairs={{0,8},{1,9},{2,10},{3,11},{4,12},{5,13},{6,14},{7,15},{8,0},{9,1},... | collective-permute-start | bytes 1179656 | tf_op jit(solution)/shard_map/ppermute | solution.py:138
  70.8 5.6 %collective-permute-start.26 = (bf16[4,64,768]{2,1,0:T(8,128)(2,1)S(1)}, bf16[4,64,768]{2,1,0:T(8,128)(2,1)S(1)}, u32[]{:S(2)}, u32[]{:S(2)}) collective-permute-start(bf16[4,64,768]{2,1,0:T(8,128)(2,1)S(1)} %collective-permute-done.22.refs_3_), channel_id=1, source_target_pairs={{0,8},{1,9},{2,10},{3,11},{4,12},{5,13},{6,14},{7,15},{8,0},{9,1},... | collective-permute-start | bytes 1179656 | tf_op jit(solution)/shard_map/ppermute | solution.py:138
  70.8 5.6 %collective-permute-start.27 = (bf16[4,64,768]{2,1,0:T(8,128)(2,1)S(1)}, bf16[4,64,768]{2,1,0:T(8,128)(2,1)S(1)}, u32[]{:S(2)}, u32[]{:S(2)}) collective-permute-start(bf16[4,64,768]{2,1,0:T(8,128)(2,1)S(1)} %collective-permute-done.23.refs_4_), channel_id=1, source_target_pairs={{0,8},{1,9},{2,10},{3,11},{4,12},{5,13},{6,14},{7,15},{8,0},{9,1},... | collective-permute-start | bytes 1179656 | tf_op jit(solution)/shard_map/ppermute | solution.py:138
  71.3 5.1 %collective-permute-start.28 = (bf16[4,64,768]{2,1,0:T(8,128)(2,1)S(1)}, bf16[4,64,768]{2,1,0:T(8,128)(2,1)S(1)}, u32[]{:S(2)}, u32[]{:S(2)}) collective-permute-start(bf16[4,64,768]{2,1,0:T(8,128)(2,1)S(1)} %collective-permute-done.24.refs_2_.refs_13_.refs_3_), channel_id=1, source_target_pairs={{0,8},{1,9},{2,10},{3,11},{4,12},{5,13},{6,14},{7,15},{8,0},{9,1},... | collective-permute-start | bytes 1179656 | tf_op jit(solution)/shard_map/ppermute | solution.py:138
  71.3 7.8 %collective-permute-start.29 = (bf16[4,64,768]{2,1,0:T(8,128)(2,1)S(1)}, bf16[4,64,768]{2,1,0:T(8,128)(2,1)S(1)}, u32[]{:S(2)}, u32[]{:S(2)}) collective-permute-start(bf16[4,64,768]{2,1,0:T(8,128)(2,1)S(1)} %collective-permute-done.21.refs_1_.refs_12_.refs_2_), channel_id=1, source_target_pairs={{0,1},{1,0},{2,3},{3,2},{4,5},{5,4},{6,7},{7,6},{8,24},{9,25},{10,... | collective-permute-start | bytes 1179656 | tf_op jit(solution)/shard_map/ppermute | solution.py:138
  73.2 5.9 %collective-permute-start.25 = (bf16[4,64,768]{2,1,0:T(8,128)(2,1)S(1)}, bf16[4,64,768]{2,1,0:T(8,128)(2,1)S(1)}, u32[]{:S(2)}, u32[]{:S(2)}) collective-permute-start(bf16[4,64,768]{2,1,0:T(8,128)(2,1)S(1)} %collective-permute-done.21.refs_1_.refs_12_.refs_2_), channel_id=1, source_target_pairs={{0,8},{1,9},{2,10},{3,11},{4,12},{5,13},{6,14},{7,15},{8,0},{9,1},... | collective-permute-start | bytes 1179656 | tf_op jit(solution)/shard_map/ppermute | solution.py:138
  79.1 2.5 %collective-permute-start.30 = (bf16[4,64,768]{2,1,0:T(8,128)(2,1)S(1)}, bf16[4,64,768]{2,1,0:T(8,128)(2,1)S(1)}, u32[]{:S(2)}, u32[]{:S(2)}) collective-permute-start(bf16[4,64,768]{2,1,0:T(8,128)(2,1)S(1)} %collective-permute-done.29.refs_0_), channel_id=1, source_target_pairs={{0,8},{1,9},{2,10},{3,11},{4,12},{5,13},{6,14},{7,15},{8,0},{9,1},... | collective-permute-start | bytes 1179656 | tf_op jit(solution)/shard_map/ppermute | solution.py:138

commit v4 on v3

--- a/solution.py
+++ b/solution.py
@@ -50,55 +50,55 @@
     return term + lax.dot_general(left_sin, right, dims, preferred_element_type=jnp.float32)
 
 
-def add_shards(names, has_totals, last, place_ref, weights_ref, *refs):
+def add_shards(names, where, has_totals, last, place_ref, weights_ref, *refs):
     refs = list(refs)
-    held = {name: refs.pop(0) for name in names}
-    steps = sorted({name[2] for name in names})
-    sources = {}
-    for dz in steps:
-        for kind in ("O", "A", "B"):
-            key = ("near", kind, dz)
-            sources[key] = held[key] if key in held else refs.pop(0)
-    totals_in = refs.pop(0) if has_totals else None
-    out_ref, left_ref = refs.pop(0), refs.pop(0)
-    totals_ref = refs.pop(0) if last else out_ref
+    scratch_ref = refs.pop() if last else None
+    left_ref, out_ref = refs.pop(), refs.pop()
+    totals_in = refs.pop() if has_totals else None
+    totals_ref = scratch_ref if last else out_ref
+
+    def shard(name):
+        index, slot = where[name]
+        return refs[index] if slot is None else refs[index].at[slot]
+
     pair, core, level, beside, first_s, flat = (place_ref[i] for i in range(6))
-    spins, per_block = left_ref.shape[2] // (2 * out_ref.shape[1]), out_ref.shape[1]
-    if not last:
-        per_block = sources[("near", "O", steps[0])].shape[1]
-        spins = left_ref.shape[2] // (2 * per_block)
+    columns, per_block, _ = shard(names[0]).shape
+    spins = left_ref.shape[2] // (2 * per_block)
 
     if has_totals:
         totals_ref[...] = totals_in[...]
     else:
         totals_ref[...] = jnp.zeros_like(totals_ref)
 
-    for slot, dz in enumerate(steps):
-        shard = jnp.bitwise_xor(level, dz) * flat
-        here = [sources[("near", "O", dz)][first_s + s] for s in range(spins)]
-        there = []
-        for s in range(spins):
-            by_a = sources[("near", "A", dz)][first_s + s]
-            by_b = sources[("near", "B", dz)][first_s + s]
-            there.append(jnp.where(core == 0, by_b, by_a))
-        for dy, owns in enumerate((here, there)):
-            weights = weights_ref[shard + jnp.bitwise_xor(beside, dy)]
-            left_cos, left_sin = left_sides(owns, weights)
-            left_ref[2 * slot + dy, 0] = left_cos
-            left_ref[2 * slot + dy, 1] = left_sin
+    slots = left_slots(names)
+    for slot, (dy, dz) in enumerate(slots):
+        site = jnp.bitwise_xor(level, dz) * flat + jnp.bitwise_xor(beside, dy)
+        if dy == 0:
+            owns = [shard(("near", "O", dz))[first_s + s] for s in range(spins)]
+        else:
+            owns = [
+                jnp.where(
+                    core == 0,
+                    shard(("near", "B", dz))[first_s + s],
+                    shard(("near", "A", dz))[first_s + s],
+                )
+                for s in range(spins)
+            ]
+        left_ref[slot, 0], left_ref[slot, 1] = left_sides(owns, weights_ref[site])
 
     for side, kind, dz in names:
-        right_ref = held[(side, kind, dz)]
-        right = right_ref[...].reshape(-1, right_ref.shape[2])
+        right = shard((side, kind, dz))[...].reshape(columns * per_block, -1)
         turn = core if side == "near" else 1 - core
         dx, dy = {"O": (0, 0), "A": (1 - turn, turn), "B": (turn, 1 - turn), "AB": (1, 1)}[kind]
-        slot = 2 * steps.index(dz) + dy
+        if kind in ("O", "AB"):
+            slot = slots.index((dy, dz))
+        else:
+            slot = slots.index((0, dz)) + dy
         totals_ref[0 if side == "near" else 1, dx] += product(
             left_ref[slot, 0], left_ref[slot, 1], right
         )
 
     if last:
-        columns = totals_ref.shape[3] // per_block
         for part in range(2):
             for spin in range(spins):
                 top = (part * spins + spin) * per_block
@@ -118,6 +118,33 @@
                     out_ref[row] = jnp.concatenate(pieces, 1)
 
 
+def route_second(place_ref, *refs):
+    stack_ref, both_ref, relayed_ref, mixed_ref = refs[6:]
+    ab0_ref, o1_ref, o2_ref = refs[3:6]
+    for slot in range(6):
+        stack_ref[slot] = refs[slot][...]
+    both_ref[0] = o1_ref[...]
+    both_ref[1] = o2_ref[...]
+    relayed_ref[0] = ab0_ref[...]
+    relayed_ref[1] = o2_ref[...]
+    mixed_ref[...] = jnp.where(place_ref[1] == 0, o2_ref[...], ab0_ref[...])
+
+
+def route_third(z1_ref, a12_ref, b12_ref, ab2_ref, stack_ref, o3_ref):
+    for slot, ref in enumerate((z1_ref, a12_ref, b12_ref)):
+        stack_ref[2 * slot] = ref[0]
+        stack_ref[2 * slot + 1] = ref[1]
+    stack_ref[6] = ab2_ref[...]
+    o3_ref[...] = z1_ref[1]
+
+
+def left_slots(names):
+    needed = set()
+    for _, kind, dz in names:
+        needed |= {"O": {(0, dz)}, "AB": {(1, dz)}}.get(kind, {(0, dz), (1, dz)})
+    return sorted(needed, key=lambda slot: (slot[1], slot[0]))
+
+
 def swap_in_windows(packed, place, weights, share):
     shape = tuple(lax.axis_size(name) for name in AXES)
     columns, per_block, depth = packed.shape
@@ -143,33 +170,49 @@
     def hop_b(array):
         return move(array, lambda p, c, z, y: (p, c, z, y ^ 1) if c == 0 else (p ^ 1, c, z, y))
 
+    def hop_ab(array):
+        return move(array, lambda p, c, z, y: (p ^ 1, c, z, y ^ 1))
+
     def hop_z(array, by):
         return move(array, lambda p, c, z, y: (p, c, z ^ by, y))
 
+    def hop_mixed(array):
+        return move(
+            array, lambda p, c, z, y: (p ^ 1, c, z, y ^ 1) if c == 0 else (p, c, z ^ 2, y)
+        )
+
     def swap(array):
         return move(array, lambda p, c, z, y: (p, c ^ 1, z, y))
 
-    got = {("near", "O", 0): packed}
-    totals = None
+    arrays = {}
+    where = {}
+
+    def put(key, array, side, kinds):
+        arrays[key] = array
+        for slot, (kind, dz) in enumerate(kinds):
+            where[(side, kind, dz)] = (key, slot if len(kinds) > 1 else None)
+
+    def near(kind, dz):
+        key, slot = where[("near", kind, dz)]
+        return arrays[key] if slot is None else arrays[key][slot]
 
     def add(names, totals, last=False):
-        steps = sorted({name[2] for name in names})
-        extra = [
-            ("near", kind, dz)
-            for dz in steps
-            for kind in ("O", "A", "B")
-            if ("near", kind, dz) not in names
-        ]
-        operands = [place, weights] + [got[name] for name in list(names) + extra]
+        slots = left_slots(names)
+        uses = list(names)
+        for dy, dz in slots:
+            uses += [("near", kind, dz) for kind in (("A", "B") if dy else ("O",))]
+        keys = sorted({where[name][0] for name in uses})
+        places = {name: (keys.index(where[name][0]), where[name][1]) for name in uses}
+        operands = [place, weights] + [arrays[key] for key in keys]
         if totals is not None:
             operands.append(totals)
         total_shape = (2, 2, tall, wide)
         out = (share, per_block, 4 * per_block) if last else total_shape
-        scratch = [pltpu.VMEM((2 * len(steps), 2, tall, depth), jnp.bfloat16)]
+        scratch = [pltpu.VMEM((len(slots), 2, tall, depth), jnp.bfloat16)]
         if last:
             scratch.append(pltpu.VMEM(total_shape, jnp.float32))
         return pl.pallas_call(
-            functools.partial(add_shards, tuple(names), totals is not None, last),
+            functools.partial(add_shards, tuple(names), places, totals is not None, last),
             in_specs=[pl.BlockSpec(memory_space=pltpu.SMEM)]
             + [pl.BlockSpec(memory_space=pltpu.VMEM)] * (len(operands) - 1),
             out_specs=pl.BlockSpec(memory_space=pltpu.VMEM),
@@ -183,72 +226,64 @@
             ),
         )(*operands)
 
-    def near(kind, dz):
-        return got[("near", kind, dz)]
-
-    windows = [
-        (
-            {
-                ("near", "A", 0): lambda: hop_a(near("O", 0)),
-                ("near", "B", 0): lambda: hop_b(near("O", 0)),
-                ("near", "O", 1): lambda: hop_z(near("O", 0), 1),
-            },
-            [("O", 0)],
-            [],
-        ),
-        (
-            {
-                ("near", "O", 2): lambda: hop_z(near("O", 0), 2),
-                ("near", "AB", 0): lambda: hop_b(near("A", 0)),
-                ("near", "A", 1): lambda: hop_a(near("O", 1)),
-                ("near", "B", 1): lambda: hop_b(near("O", 1)),
-            },
-            [("A", 0), ("B", 0), ("O", 1)],
-            [("near", "O", 0), ("near", "A", 0), ("near", "B", 0), ("far", "O", 0)],
-        ),
-        (
-            {
-                ("near", "A", 2): lambda: hop_a(near("O", 2)),
-                ("near", "B", 2): lambda: hop_b(near("O", 2)),
-                ("near", "O", 3): lambda: hop_z(near("O", 2), 1),
-            },
-            [("AB", 0), ("A", 1), ("B", 1), ("O", 2)],
-            [("near", "AB", 0), ("near", "O", 1), ("near", "A", 1), ("near", "B", 1)]
-            + [("far", "A", 0), ("far", "B", 0), ("far", "O", 1)],
-        ),
-        (
-            {
-                ("near", "AB", 2): lambda: hop_b(near("A", 2)),
-                ("near", "A", 3): lambda: hop_a(near("O", 3)),
-                ("near", "B", 3): lambda: hop_b(near("O", 3)),
-                ("near", "AB", 1): lambda: hop_z(near("AB", 0), 1),
-            },
-            [("A", 2), ("B", 2), ("O", 3)],
-            [("far", "AB", 0), ("far", "A", 1), ("far", "B", 1)]
-            + [("near", "O", 2), ("near", "A", 2), ("near", "B", 2), ("far", "O", 2)],
-        ),
-        (
-            {("near", "AB", 3): lambda: hop_b(near("A", 3))},
-            [("AB", 1), ("AB", 2), ("A", 3), ("B", 3)],
-            [("near", "O", 3), ("near", "A", 3), ("near", "B", 3), ("near", "AB", 1)]
-            + [("near", "AB", 2), ("far", "A", 2), ("far", "B", 2), ("far", "O", 3)],
-        ),
-        (
-            {},
-            [("AB", 3)],
-            [("near", "AB", 3), ("far", "AB", 1), ("far", "AB", 2), ("far", "A", 3)]
-            + [("far", "B", 3)],
-        ),
-    ]
-    for travels, swaps, names in windows:
-        new = {name: start() for name, start in travels.items()}
-        for kind, dz in swaps:
-            new[("far", kind, dz)] = swap(near(kind, dz))
-        if names:
-            totals = add(names, totals)
-        got.update(new)
-        got, totals = lax.optimization_barrier((got, totals))
-    return add([("far", "AB", 3)], totals, last=True)
+    def fence(totals):
+        nonlocal arrays
+        arrays, totals = lax.optimization_barrier((arrays, totals))
+        return totals
+
+    put("o0", packed, "near", [("O", 0)])
+
+    new = [hop_a(packed), hop_b(packed), hop_ab(packed), hop_z(packed, 1), hop_z(packed, 2)]
+    for key, array, kind in zip(
+        ("a0", "b0", "ab0", "o1", "o2"), new, (("A", 0), ("B", 0), ("AB", 0), ("O", 1), ("O", 2))
+    ):
+        put(key, array, "near", [kind])
+    place, weights = fence((place, weights))
+
+    def route(kernel, operands, counts):
+        block = pl.BlockSpec(memory_space=pltpu.VMEM)
+        first = pl.BlockSpec(memory_space=pltpu.SMEM) if operands[0] is place else block
+        shapes = [(count,) * (count > 1) + packed.shape for count in counts]
+        routed = pl.pallas_call(
+            kernel,
+            in_specs=[first] + [block] * (len(operands) - 1),
+            out_specs=[block] * len(counts),
+            out_shape=[jax.ShapeDtypeStruct(shape, packed.dtype) for shape in shapes],
+            compiler_params=pltpu.CompilerParams(vmem_limit_bytes=24 * 1024 * 1024),
+        )(*operands)
+        return fence(routed)
+
+    first = [("O", 0), ("A", 0), ("B", 0), ("AB", 0), ("O", 1), ("O", 2)]
+    stack, both, relayed, mixed = route(
+        route_second, [place] + [near(*kind) for kind in first], (6, 2, 2, 1)
+    )
+    new = [hop_z(relayed, 1), hop_a(both), hop_b(both), hop_mixed(mixed), swap(stack)]
+    totals = add([("near", *kind) for kind in first], None)
+    put("z1", new[0], "near", [("AB", 1), ("O", 3)])
+    put("a12", new[1], "near", [("A", 1), ("A", 2)])
+    put("b12", new[2], "near", [("B", 1), ("B", 2)])
+    put("ab2", new[3], "near", [("AB", 2)])
+    put("far1", new[4], "far", first)
+    totals = fence(totals)
+
+    second = [("AB", 1), ("O", 3), ("A", 1), ("A", 2), ("B", 1), ("B", 2), ("AB", 2)]
+    arrived = [arrays[key] for key in ("z1", "a12", "b12", "ab2")]
+    stack, start = route(route_third, arrived, (7, 1))
+    new = [hop_z(near("AB", 2), 1), hop_a(start), hop_b(start), swap(stack)]
+    totals = add([("near", *kind) for kind in second] + [("far", *kind) for kind in first], totals)
+    put("ab3", new[0], "near", [("AB", 3)])
+    put("a3", new[1], "near", [("A", 3)])
+    put("b3", new[2], "near", [("B", 3)])
+    put("far2", new[3], "far", second)
+    totals = fence(totals)
+
+    third = [("A", 3), ("B", 3), ("AB", 3)]
+    new = [swap(near(*kind)) for kind in third]
+    totals = add([("near", *kind) for kind in third] + [("far", *kind) for kind in second], totals)
+    for kind, array in zip(third, new):
+        put("far " + kind[0], array, "far", [kind])
+    totals = fence(totals)
+    return add([("far", *kind) for kind in third], totals, last=True)
 
 
 def add_terms(place_ref, weights_ref, left_ref, right_ref, field_ref):

time: 84.1 us -> 74.6 us (0.89)
  starting transfers between devices: 24 us -> 16.1 us
  Pallas kernels: 15.3 us -> 14.4 us
    ppermute x31 -> x17, starting transfers between devices: 24 us -> 16.1 us  [move(): return lax.ppermute(array, AXES, pairs)]
    pallas_call x6, Pallas kernels: 15.3 us -> 14.4 us  [the longest x4 13.4 us: add(): pl.pallas_call(functools.partial(add_shards, tuple(names), places, totals...]
    ppermute x31 -> x17, waiting for transfers between devices: 42.3 us -> 41.6 us  [move(): return lax.ppermute(array, AXES, pairs)]
  transfers between devices with their start and end apart: 31 -> 17, of which waited for: 7 -> 7; matrix products, arithmetic and copies ran while one was open for 0% -> 1% of each run, Pallas kernels for 16% -> 14%
where the time goes in v4:
time: 74.6 us; the launch traced here: 74.4 us
  waiting for transfers between devices  41.6 us (56%)
  starting transfers between devices  16.1 us (22%)
  Pallas kernels  14.4 us (19%)
  local copies, waits for them, and re-layouts  1.78 us (2%)
    ppermute x17, waiting for transfers between devices, move(): return lax.ppermute(array, AXES, pairs)  41.6 us
    ppermute x17, starting transfers between devices, move(): return lax.ppermute(array, AXES, pairs)  16.1 us
    pallas_call x4, Pallas kernels, add(): pl.pallas_call(functools.partial(add_shards, tuple(names), places, totals...  13.4 us
  transfers between devices with their start and end apart: 17, of which 7 were waited for; matrix products, arithmetic and copies ran while one was open for 1% of the time, Pallas kernels for 14%

profile of v4, /device:TPU:0, one launch (start us, length us, event | category | flops | bytes accessed | tf_op | source)
XLA Modules:
  0.0 74.4 jit_solution(11139461173995087081)
XLA Ops:
  0.0 0.0 copy-start
  0.0 1.3 %copy.9 = bf16[2,64,4,3,128]{4,3,0,1,2:T(4,128)(2,1)S(1)} copy(bf16[2,64,4,3,128]{4,1,3,2,0:T(8,128)(2,1)} %bitcast.32) | data formatting | bytes 786432 | tf_op jit(solution)/shard_map/reshape | solution.py:356
  1.4 0.3 reshape.222.refs_0_.refs_3_.refs_6_
  1.7 3.0 %collective-permute-start = (bf16[4,64,768]{2,1,0:T(8,128)(2,1)S(1)}, bf16[4,64,768]{2,1,0:T(8,128)(2,1)S(1)}, u32[]{:S(2)}, u32[]{:S(2)}) collective-permute-start(bf16[4,64,768]{2,1,0:T(8,128)(2,1)S(1)} %reshape.222.refs_0_.refs_3_.refs_6_), channel_id=1, source_target_pairs={{0,16},{1,17},{2,18},{3,19},{4,20},{5,21},{6,22},{7,23},{8,9},{9,8... | collective-permute-start | bytes 1179656 | tf_op jit(solution)/shard_map/ppermute | solution.py:165
  4.7 1.5 %collective-permute-start.1 = (bf16[4,64,768]{2,1,0:T(8,128)(2,1)S(1)}, bf16[4,64,768]{2,1,0:T(8,128)(2,1)S(1)}, u32[]{:S(2)}, u32[]{:S(2)}) collective-permute-start(bf16[4,64,768]{2,1,0:T(8,128)(2,1)S(1)} %reshape.222.refs_0_.refs_3_.refs_6_), channel_id=1, source_target_pairs={{0,17},{1,16},{2,19},{3,18},{4,21},{5,20},{6,23},{7,22},{8,25},{9,... | collective-permute-start | bytes 1179656 | tf_op jit(solution)/shard_map/ppermute | solution.py:165
  6.2 0.1 collective-permute-start.2
  6.2 2.0 %collective-permute-start.3 = (bf16[4,64,768]{2,1,0:T(8,128)(2,1)S(1)}, bf16[4,64,768]{2,1,0:T(8,128)(2,1)S(1)}, u32[]{:S(2)}, u32[]{:S(2)}) collective-permute-start(bf16[4,64,768]{2,1,0:T(8,128)(2,1)S(1)} %reshape.222.refs_0_.refs_3_.refs_6_), channel_id=1, source_target_pairs={{0,2},{1,3},{2,0},{3,1},{4,6},{5,7},{6,4},{7,5},{8,10},{9,11},{10,... | collective-permute-start | bytes 1179656 | tf_op jit(solution)/shard_map/ppermute | solution.py:165
  8.3 2.6 %collective-permute-start.4 = (bf16[4,64,768]{2,1,0:T(8,128)(2,1)S(1)}, bf16[4,64,768]{2,1,0:T(8,128)(2,1)S(1)}, u32[]{:S(2)}, u32[]{:S(2)}) collective-permute-start(bf16[4,64,768]{2,1,0:T(8,128)(2,1)S(1)} %reshape.222.refs_0_.refs_3_.refs_6_), channel_id=1, source_target_pairs={{0,4},{1,5},{2,6},{3,7},{4,0},{5,1},{6,2},{7,3},{8,12},{9,13},{10,... | collective-permute-start | bytes 1179656 | tf_op jit(solution)/shard_map/ppermute | solution.py:165
  10.9 0.0 copy-done
  10.9 0.1 fusion
  11.1 0.1 stack.44.place_ref
  11.2 0.1 multiply_cosine_fusion
  11.3 3.0 %collective-permute-done.refs_1_.refs_0_ = bf16[4,64,768]{2,1,0:T(8,128)(2,1)S(1)} collective-permute-done((bf16[4,64,768]{2,1,0:T(8,128)(2,1)S(1)}, bf16[4,64,768]{2,1,0:T(8,128)(2,1)S(1)}, u32[]{:S(2)}, u32[]{:S(2)}) %collective-permute-start) | collective-permute-done | bytes 393248 | tf_op jit(solution)/shard_map/ppermute | solution.py:165
  14.3 10.2 %collective-permute-done.1.refs_3_.refs_1_ = bf16[4,64,768]{2,1,0:T(8,128)(2,1)S(1)} collective-permute-done((bf16[4,64,768]{2,1,0:T(8,128)(2,1)S(1)}, bf16[4,64,768]{2,1,0:T(8,128)(2,1)S(1)}, u32[]{:S(2)}, u32[]{:S(2)}) %collective-permute-start.1) | collective-permute-done | bytes 393248 | tf_op jit(solution)/shard_map/ppermute | solution.py:165
  24.5 0.0 collective-permute-done.2.refs_2_.refs_3_
  24.5 0.3 collective-permute-done.3.refs_4_.refs_7_.refs_6_
  24.9 2.5 %collective-permute-done.4.refs_5_.refs_8_.refs_7_ = bf16[4,64,768]{2,1,0:T(8,128)(2,1)S(1)} collective-permute-done((bf16[4,64,768]{2,1,0:T(8,128)(2,1)S(1)}, bf16[4,64,768]{2,1,0:T(8,128)(2,1)S(1)}, u32[]{:S(2)}, u32[]{:S(2)}) %collective-permute-start.4) | collective-permute-done | bytes 393248 | tf_op jit(solution)/shard_map/ppermute | solution.py:165
  27.4 0.8 %shard_map.28 = (bf16[6,4,64,768]{3,2,1,0:T(8,128)(2,1)S(1)}, bf16[2,4,64,768]{3,2,1,0:T(8,128)(2,1)S(1)}, bf16[2,4,64,768]{3,2,1,0:T(8,128)(2,1)S(1)}, bf16[4,64,768]{2,1,0:T(8,128)(2,1)S(1)}) custom-call(s32[7]{0:T(128)S(1)} %stack.44.place_ref, bf16[4,64,768]{2,1,0:T(8,128)(2,1)S(1)} %reshape.222.refs_0_.refs_3_.refs_6_, ...), custom_call_target="tpu_custom_call" | custom-call | tf_op jit(solution)/shard_map/pallas_call | solution.py:247
  28.2 0.1 collective-permute-start.8
  28.3 1.6 %collective-permute-start.5 = (bf16[2,4,64,768]{3,2,1,0:T(8,128)(2,1)S(1)}, bf16[2,4,64,768]{3,2,1,0:T(8,128)(2,1)S(1)}, u32[]{:S(2)}, u32[]{:S(2)}) collective-permute-start(bf16[2,4,64,768]{3,2,1,0:T(8,128)(2,1)S(1)} %get-tuple-element.82), channel_id=1, source_target_pairs={{0,16},{1,17},{2,18},{3,19},{4,20},{5,21},{6,22},{7,23},{8,9},{9,8... | collective-permute-start | bytes 2359304 | tf_op jit(solution)/shard_map/ppermute | solution.py:165
  29.8 1.5 %collective-permute-start.7 = (bf16[2,4,64,768]{3,2,1,0:T(8,128)(2,1)S(1)}, bf16[2,4,64,768]{3,2,1,0:T(8,128)(2,1)S(1)}, u32[]{:S(2)}, u32[]{:S(2)}) collective-permute-start(bf16[2,4,64,768]{3,2,1,0:T(8,128)(2,1)S(1)} %get-tuple-element.82), channel_id=1, source_target_pairs={{0,1},{1,0},{2,3},{3,2},{4,5},{5,4},{6,7},{7,6},{8,24},{9,25},{10,... | collective-permute-start | bytes 2359304 | tf_op jit(solution)/shard_map/ppermute | solution.py:165
  31.4 0.4 collective-permute-start.9
  31.8 0.5 collective-permute-start.6
  32.3 2.5 %shard_map.29.refs_10_ = f32[2,2,256,256]{3,2,1,0:T(8,128)S(1)} custom-call(s32[7]{0:T(128)S(1)} %stack.44.place_ref, f32[8,2,128]{2,1,0:T(2,128)S(1)} %maximum_bitcast_fusion.weights_ref, bf16[4,64,768]{2,1,0:T(8,128)(2,1)S(1)} %collective-permute-done.refs_1_.refs_0_, bf16[4,64,768]{2,1,0:T(8,128)(2,1)S(1)} %collective-permute-done.1.refs_3_.refs_1_, ...), custom_call_target="tpu_custom_call" | custom-call | flops 1207959552 | bytes 4456448 | tf_op jit(solution)/shard_map/pallas_call | solution.py:214
  34.8 18.9 %collective-permute-done.6.ab2_ref.refs_2_ = bf16[4,64,768]{2,1,0:T(8,128)(2,1)S(1)} collective-permute-done((bf16[4,64,768]{2,1,0:T(8,128)(2,1)S(1)}, bf16[4,64,768]{2,1,0:T(8,128)(2,1)S(1)}, u32[]{:S(2)}, u32[]{:S(2)}) %collective-permute-start.6) | collective-permute-done | bytes 393248 | tf_op jit(solution)/shard_map/ppermute | solution.py:165
  53.6 0.0 collective-permute-done.5.a12_ref.refs_1_.refs_0_
  53.6 0.0 collective-permute-done.7.b12_ref.refs_4_.refs_3_
  53.6 1.3 %collective-permute-done.9.z1_ref.refs_9_.refs_8_.refs_5_ = bf16[2,4,64,768]{3,2,1,0:T(8,128)(2,1)S(1)} collective-permute-done((bf16[2,4,64,768]{3,2,1,0:T(8,128)(2,1)S(1)}, bf16[2,4,64,768]{3,2,1,0:T(8,128)(2,1)S(1)}, u32[]{:S(2)}, u32[]{:S(2)}) %collective-permute-start.9) | collective-permute-done | bytes 786464 | tf_op jit(solution)/shard_map/ppermute | solution.py:165
  54.9 0.0 collective-permute-done.8.refs_5_
  54.9 0.2 shard_map.30
  55.1 0.1 collective-permute-start.13
  55.2 0.6 collective-permute-start.10
  55.8 1.1 %collective-permute-start.11 = (bf16[4,64,768]{2,1,0:T(8,128)(2,1)S(1)}, bf16[4,64,768]{2,1,0:T(8,128)(2,1)S(1)}, u32[]{:S(2)}, u32[]{:S(2)}) collective-permute-start(bf16[4,64,768]{2,1,0:T(8,128)(2,1)S(1)} %collective-permute-done.6.ab2_ref.refs_2_), channel_id=1, source_target_pairs={{0,2},{1,3},{2,0},{3,1},{4,6},{5,7},{6,4},{7,5},{8,10},{9,11},{10,... | collective-permute-start | bytes 1179656 | tf_op jit(solution)/shard_map/ppermute | solution.py:165
  56.8 0.5 collective-permute-start.12
  57.4 4.3 %shard_map.31.refs_9_ = f32[2,2,256,256]{3,2,1,0:T(8,128)S(1)} custom-call(s32[7]{0:T(128)S(1)} %stack.44.place_ref, f32[8,2,128]{2,1,0:T(2,128)S(1)} %maximum_bitcast_fusion.weights_ref, bf16[4,64,768]{2,1,0:T(8,128)(2,1)S(1)} %collective-permute-done.refs_1_.refs_0_, bf16[2,4,64,768]{3,2,1,0:T(8,128)(2,1)S(1)} %collective-permute-done.5.a12_ref.refs_1_.refs_0_, ...), custom_call_target="tpu_custom_call" | custom-call | flops 2617245696 | bytes 7208960 | tf_op jit(solution)/shard_map/pallas_call | solution.py:214
  61.7 5.4 %collective-permute-done.10.refs_1_.refs_0_ = bf16[4,64,768]{2,1,0:T(8,128)(2,1)S(1)} collective-permute-done((bf16[4,64,768]{2,1,0:T(8,128)(2,1)S(1)}, bf16[4,64,768]{2,1,0:T(8,128)(2,1)S(1)}, u32[]{:S(2)}, u32[]{:S(2)}) %collective-permute-start.10) | collective-permute-done | bytes 393248 | tf_op jit(solution)/shard_map/ppermute | solution.py:165
  67.1 0.0 collective-permute-done.11.refs_2_
  67.1 0.0 collective-permute-done.12.refs_4_.refs_1_
  67.1 0.0 collective-permute-done.13.refs_5_
  67.1 0.1 collective-permute-start.14
  67.2 0.5 collective-permute-start.15
  67.7 0.1 collective-permute-start.16
  67.8 3.7 %shard_map.32.refs_6_ = f32[2,2,256,256]{3,2,1,0:T(8,128)S(1)} custom-call(s32[7]{0:T(128)S(1)} %stack.44.place_ref, f32[8,2,128]{2,1,0:T(2,128)S(1)} %maximum_bitcast_fusion.weights_ref, bf16[2,4,64,768]{3,2,1,0:T(8,128)(2,1)S(1)} %collective-permute-done.5.a12_ref.refs_1_.refs_0_, bf16[4,64,768]{2,1,0:T(8,128)(2,1)S(1)} %collective-permute-done.10.refs_1_.refs_0_, ...), custom_call_target="tpu_custom_call" | custom-call | flops 2013265920 | bytes 6029312 | tf_op jit(solution)/shard_map/pallas_call | solution.py:214
  71.5 0.0 collective-permute-done.14.refs_2_
  71.5 0.0 collective-permute-done.15.refs_3_
  71.5 0.0 collective-permute-done.16.refs_4_
  71.5 2.9 %shard_map.33 = f32[16,64,256]{2,1,0:T(8,128)} custom-call(s32[7]{0:T(128)S(1)} %stack.44.place_ref, f32[8,2,128]{2,1,0:T(2,128)S(1)} %maximum_bitcast_fusion.weights_ref, bf16[4,64,768]{2,1,0:T(8,128)(2,1)S(1)} %collective-permute-done.10.refs_1_.refs_0_, bf16[4,64,768]{2,1,0:T(8,128)(2,1)S(1)} %collective-permute-done.12.refs_4_.refs_1_, ...), custom_call_target="tpu_custom_call" | custom-call | flops 603979776 | bytes 3276800 | tf_op jit(solution)/shard_map/pallas_call | solution.py:214
  (5 shorter events, 0.1 us)
Async XLA Ops:
  0.0 10.9 %copy-start = (s32[4,3]{1,0:T(4,128)S(1)}, s32[4,3]{1,0:T(4,128)}, u32[]{:S(2)}) copy-start(s32[4,3]{1,0:T(4,128)} %param.3) | copy-start | bytes 148
  1.7 12.6 %collective-permute-start = (bf16[4,64,768]{2,1,0:T(8,128)(2,1)S(1)}, bf16[4,64,768]{2,1,0:T(8,128)(2,1)S(1)}, u32[]{:S(2)}, u32[]{:S(2)}) collective-permute-start(bf16[4,64,768]{2,1,0:T(8,128)(2,1)S(1)} %reshape.222.refs_0_.refs_3_.refs_6_), channel_id=1, source_target_pairs={{0,16},{1,17},{2,18},{3,19},{4,20},{5,21},{6,22},{7,23},{8,9},{9,8... | collective-permute-start | bytes 1179656 | tf_op jit(solution)/shard_map/ppermute | solution.py:165
  4.7 19.8 %collective-permute-start.1 = (bf16[4,64,768]{2,1,0:T(8,128)(2,1)S(1)}, bf16[4,64,768]{2,1,0:T(8,128)(2,1)S(1)}, u32[]{:S(2)}, u32[]{:S(2)}) collective-permute-start(bf16[4,64,768]{2,1,0:T(8,128)(2,1)S(1)} %reshape.222.refs_0_.refs_3_.refs_6_), channel_id=1, source_target_pairs={{0,17},{1,16},{2,19},{3,18},{4,21},{5,20},{6,23},{7,22},{8,25},{9,... | collective-permute-start | bytes 1179656 | tf_op jit(solution)/shard_map/ppermute | solution.py:165
  6.2 18.3 %collective-permute-start.2 = (bf16[4,64,768]{2,1,0:T(8,128)(2,1)S(1)}, bf16[4,64,768]{2,1,0:T(8,128)(2,1)S(1)}, u32[]{:S(2)}, u32[]{:S(2)}) collective-permute-start(bf16[4,64,768]{2,1,0:T(8,128)(2,1)S(1)} %reshape.222.refs_0_.refs_3_.refs_6_), channel_id=1, source_target_pairs={{0,1},{1,0},{2,3},{3,2},{4,5},{5,4},{6,7},{7,6},{8,24},{9,25},{10,... | collective-permute-start | bytes 1179656 | tf_op jit(solution)/shard_map/ppermute | solution.py:165
  6.2 18.6 %collective-permute-start.3 = (bf16[4,64,768]{2,1,0:T(8,128)(2,1)S(1)}, bf16[4,64,768]{2,1,0:T(8,128)(2,1)S(1)}, u32[]{:S(2)}, u32[]{:S(2)}) collective-permute-start(bf16[4,64,768]{2,1,0:T(8,128)(2,1)S(1)} %reshape.222.refs_0_.refs_3_.refs_6_), channel_id=1, source_target_pairs={{0,2},{1,3},{2,0},{3,1},{4,6},{5,7},{6,4},{7,5},{8,10},{9,11},{10,... | collective-permute-start | bytes 1179656 | tf_op jit(solution)/shard_map/ppermute | solution.py:165
  8.3 19.1 %collective-permute-start.4 = (bf16[4,64,768]{2,1,0:T(8,128)(2,1)S(1)}, bf16[4,64,768]{2,1,0:T(8,128)(2,1)S(1)}, u32[]{:S(2)}, u32[]{:S(2)}) collective-permute-start(bf16[4,64,768]{2,1,0:T(8,128)(2,1)S(1)} %reshape.222.refs_0_.refs_3_.refs_6_), channel_id=1, source_target_pairs={{0,4},{1,5},{2,6},{3,7},{4,0},{5,1},{6,2},{7,3},{8,12},{9,13},{10,... | collective-permute-start | bytes 1179656 | tf_op jit(solution)/shard_map/ppermute | solution.py:165
  28.2 26.7 %collective-permute-start.8 = (bf16[6,4,64,768]{3,2,1,0:T(8,128)(2,1)S(1)}, bf16[6,4,64,768]{3,2,1,0:T(8,128)(2,1)S(1)}, u32[]{:S(2)}, u32[]{:S(2)}) collective-permute-start(bf16[6,4,64,768]{3,2,1,0:T(8,128)(2,1)S(1)} %get-tuple-element.86), channel_id=1, source_target_pairs={{0,8},{1,9},{2,10},{3,11},{4,12},{5,13},{6,14},{7,15},{8,0},{9,1},... | collective-permute-start | bytes 7077896 | tf_op jit(solution)/shard_map/ppermute | solution.py:165
  28.3 25.3 %collective-permute-start.5 = (bf16[2,4,64,768]{3,2,1,0:T(8,128)(2,1)S(1)}, bf16[2,4,64,768]{3,2,1,0:T(8,128)(2,1)S(1)}, u32[]{:S(2)}, u32[]{:S(2)}) collective-permute-start(bf16[2,4,64,768]{3,2,1,0:T(8,128)(2,1)S(1)} %get-tuple-element.82), channel_id=1, source_target_pairs={{0,16},{1,17},{2,18},{3,19},{4,20},{5,21},{6,22},{7,23},{8,9},{9,8... | collective-permute-start | bytes 2359304 | tf_op jit(solution)/shard_map/ppermute | solution.py:165
  29.8 23.8 %collective-permute-start.7 = (bf16[2,4,64,768]{3,2,1,0:T(8,128)(2,1)S(1)}, bf16[2,4,64,768]{3,2,1,0:T(8,128)(2,1)S(1)}, u32[]{:S(2)}, u32[]{:S(2)}) collective-permute-start(bf16[2,4,64,768]{3,2,1,0:T(8,128)(2,1)S(1)} %get-tuple-element.82), channel_id=1, source_target_pairs={{0,1},{1,0},{2,3},{3,2},{4,5},{5,4},{6,7},{7,6},{8,24},{9,25},{10,... | collective-permute-start | bytes 2359304 | tf_op jit(solution)/shard_map/ppermute | solution.py:165
  31.4 23.5 %collective-permute-start.9 = (bf16[2,4,64,768]{3,2,1,0:T(8,128)(2,1)S(1)}, bf16[2,4,64,768]{3,2,1,0:T(8,128)(2,1)S(1)}, u32[]{:S(2)}, u32[]{:S(2)}) collective-permute-start(bf16[2,4,64,768]{3,2,1,0:T(8,128)(2,1)S(1)} %get-tuple-element.90), channel_id=1, source_target_pairs={{0,2},{1,3},{2,0},{3,1},{4,6},{5,7},{6,4},{7,5},{8,10},{9,11},{10,... | collective-permute-start | bytes 2359304 | tf_op jit(solution)/shard_map/ppermute | solution.py:165
  31.8 21.8 %collective-permute-start.6 = (bf16[4,64,768]{2,1,0:T(8,128)(2,1)S(1)}, bf16[4,64,768]{2,1,0:T(8,128)(2,1)S(1)}, u32[]{:S(2)}, u32[]{:S(2)}) collective-permute-start(bf16[4,64,768]{2,1,0:T(8,128)(2,1)S(1)} %get-tuple-element.84), channel_id=1, source_target_pairs={{0,17},{1,16},{2,19},{3,18},{4,21},{5,20},{6,23},{7,22},{8,12},{9,... | collective-permute-start | bytes 1179656 | tf_op jit(solution)/shard_map/ppermute | solution.py:165
  55.1 12.0 %collective-permute-start.13 = (bf16[7,4,64,768]{3,2,1,0:T(8,128)(2,1)S(1)}, bf16[7,4,64,768]{3,2,1,0:T(8,128)(2,1)S(1)}, u32[]{:S(2)}, u32[]{:S(2)}) collective-permute-start(bf16[7,4,64,768]{3,2,1,0:T(8,128)(2,1)S(1)} %get-tuple-element.110), channel_id=1, source_target_pairs={{0,8},{1,9},{2,10},{3,11},{4,12},{5,13},{6,14},{7,15},{8,0},{9,1},... | collective-permute-start | bytes 8257544 | tf_op jit(solution)/shard_map/ppermute | solution.py:165
  55.2 11.9 %collective-permute-start.10 = (bf16[4,64,768]{2,1,0:T(8,128)(2,1)S(1)}, bf16[4,64,768]{2,1,0:T(8,128)(2,1)S(1)}, u32[]{:S(2)}, u32[]{:S(2)}) collective-permute-start(bf16[4,64,768]{2,1,0:T(8,128)(2,1)S(1)} %get-tuple-element.105), channel_id=1, source_target_pairs={{0,16},{1,17},{2,18},{3,19},{4,20},{5,21},{6,22},{7,23},{8,9},{9,8... | collective-permute-start | bytes 1179656 | tf_op jit(solution)/shard_map/ppermute | solution.py:165
  55.8 11.3 %collective-permute-start.11 = (bf16[4,64,768]{2,1,0:T(8,128)(2,1)S(1)}, bf16[4,64,768]{2,1,0:T(8,128)(2,1)S(1)}, u32[]{:S(2)}, u32[]{:S(2)}) collective-permute-start(bf16[4,64,768]{2,1,0:T(8,128)(2,1)S(1)} %collective-permute-done.6.ab2_ref.refs_2_), channel_id=1, source_target_pairs={{0,2},{1,3},{2,0},{3,1},{4,6},{5,7},{6,4},{7,5},{8,10},{9,11},{10,... | collective-permute-start | bytes 1179656 | tf_op jit(solution)/shard_map/ppermute | solution.py:165
  56.8 10.3 %collective-permute-start.12 = (bf16[4,64,768]{2,1,0:T(8,128)(2,1)S(1)}, bf16[4,64,768]{2,1,0:T(8,128)(2,1)S(1)}, u32[]{:S(2)}, u32[]{:S(2)}) collective-permute-start(bf16[4,64,768]{2,1,0:T(8,128)(2,1)S(1)} %get-tuple-element.105), channel_id=1, source_target_pairs={{0,1},{1,0},{2,3},{3,2},{4,5},{5,4},{6,7},{7,6},{8,24},{9,25},{10,... | collective-permute-start | bytes 1179656 | tf_op jit(solution)/shard_map/ppermute | solution.py:165
  67.1 4.3 %collective-permute-start.14 = (bf16[4,64,768]{2,1,0:T(8,128)(2,1)S(1)}, bf16[4,64,768]{2,1,0:T(8,128)(2,1)S(1)}, u32[]{:S(2)}, u32[]{:S(2)}) collective-permute-start(bf16[4,64,768]{2,1,0:T(8,128)(2,1)S(1)} %collective-permute-done.10.refs_1_.refs_0_), channel_id=1, source_target_pairs={{0,8},{1,9},{2,10},{3,11},{4,12},{5,13},{6,14},{7,15},{8,0},{9,1},... | collective-permute-start | bytes 1179656 | tf_op jit(solution)/shard_map/ppermute | solution.py:165
  67.2 4.2 %collective-permute-start.15 = (bf16[4,64,768]{2,1,0:T(8,128)(2,1)S(1)}, bf16[4,64,768]{2,1,0:T(8,128)(2,1)S(1)}, u32[]{:S(2)}, u32[]{:S(2)}) collective-permute-start(bf16[4,64,768]{2,1,0:T(8,128)(2,1)S(1)} %collective-permute-done.11.refs_2_), channel_id=1, source_target_pairs={{0,8},{1,9},{2,10},{3,11},{4,12},{5,13},{6,14},{7,15},{8,0},{9,1},... | collective-permute-start | bytes 1179656 | tf_op jit(solution)/shard_map/ppermute | solution.py:165
  67.7 3.8 %collective-permute-start.16 = (bf16[4,64,768]{2,1,0:T(8,128)(2,1)S(1)}, bf16[4,64,768]{2,1,0:T(8,128)(2,1)S(1)}, u32[]{:S(2)}, u32[]{:S(2)}) collective-permute-start(bf16[4,64,768]{2,1,0:T(8,128)(2,1)S(1)} %collective-permute-done.12.refs_4_.refs_1_), channel_id=1, source_target_pairs={{0,8},{1,9},{2,10},{3,11},{4,12},{5,13},{6,14},{7,15},{8,0},{9,1},... | collective-permute-start | bytes 1179656 | tf_op jit(solution)/shard_map/ppermute | solution.py:165

commit v5 on v4

--- a/solution.py
+++ b/solution.py
@@ -231,13 +231,12 @@
         arrays, totals = lax.optimization_barrier((arrays, totals))
         return totals
 
-    put("o0", packed, "near", [("O", 0)])
-
-    new = [hop_a(packed), hop_b(packed), hop_ab(packed), hop_z(packed, 1), hop_z(packed, 2)]
-    for key, array, kind in zip(
-        ("a0", "b0", "ab0", "o1", "o2"), new, (("A", 0), ("B", 0), ("AB", 0), ("O", 1), ("O", 2))
-    ):
-        put(key, array, "near", [kind])
+    put("0", packed, "near", [("O", 0)])
+
+    first = [("O", 2), ("A", 0), ("O", 1), ("AB", 0), ("B", 0)]
+    new = [hop_z(packed, 2), hop_a(packed), hop_z(packed, 1), hop_ab(packed), hop_b(packed)]
+    for order, (kind, array) in enumerate(zip(first, new)):
+        put("1" + "abcde"[order], array, "near", [kind])
     place, weights = fence((place, weights))
 
     def route(kernel, operands, counts):
@@ -257,31 +256,30 @@
     stack, both, relayed, mixed = route(
         route_second, [place] + [near(*kind) for kind in first], (6, 2, 2, 1)
     )
-    new = [hop_z(relayed, 1), hop_a(both), hop_b(both), hop_mixed(mixed), swap(stack)]
+    second = [("AB", 1), ("O", 3), ("A", 1), ("A", 2), ("B", 1), ("B", 2), ("AB", 2)]
     totals = add([("near", *kind) for kind in first], None)
-    put("z1", new[0], "near", [("AB", 1), ("O", 3)])
-    put("a12", new[1], "near", [("A", 1), ("A", 2)])
-    put("b12", new[2], "near", [("B", 1), ("B", 2)])
-    put("ab2", new[3], "near", [("AB", 2)])
-    put("far1", new[4], "far", first)
+    put("2a", hop_a(both), "near", second[2:4])
+    put("2b", hop_z(relayed, 1), "near", second[0:2])
+    put("2c", hop_b(both), "near", second[4:6])
+    put("2d", hop_mixed(mixed), "near", second[6:7])
+    put("2e", swap(stack), "far", first)
     totals = fence(totals)
 
-    second = [("AB", 1), ("O", 3), ("A", 1), ("A", 2), ("B", 1), ("B", 2), ("AB", 2)]
-    arrived = [arrays[key] for key in ("z1", "a12", "b12", "ab2")]
+    arrived = [arrays[key] for key in ("2b", "2a", "2c", "2d")]
     stack, start = route(route_third, arrived, (7, 1))
-    new = [hop_z(near("AB", 2), 1), hop_a(start), hop_b(start), swap(stack)]
+    third = [("AB", 3), ("A", 3), ("B", 3)]
+    new = [hop_z(near("AB", 2), 1), hop_a(start), hop_b(start)]
+    put("3d", swap(stack), "far", second)
     totals = add([("near", *kind) for kind in second] + [("far", *kind) for kind in first], totals)
-    put("ab3", new[0], "near", [("AB", 3)])
-    put("a3", new[1], "near", [("A", 3)])
-    put("b3", new[2], "near", [("B", 3)])
-    put("far2", new[3], "far", second)
+    totals = add([("far", *kind) for kind in second], totals)
+    for order, (kind, array) in enumerate(zip(third, new)):
+        put("3" + "abc"[order], array, "near", [kind])
     totals = fence(totals)
 
-    third = [("A", 3), ("B", 3), ("AB", 3)]
     new = [swap(near(*kind)) for kind in third]
-    totals = add([("near", *kind) for kind in third] + [("far", *kind) for kind in second], totals)
-    for kind, array in zip(third, new):
-        put("far " + kind[0], array, "far", [kind])
+    totals = add([("near", *kind) for kind in third], totals)
+    for order, (kind, array) in enumerate(zip(third, new)):
+        put("4" + "abc"[order], array, "far", [kind])
     totals = fence(totals)
     return add([("far", *kind) for kind in third], totals, last=True)
 

time: 74.6 us -> 72.4 us (0.971)
  waiting for transfers between devices: 41.6 us -> 34.5 us
  starting transfers between devices: 16.1 us -> 20.5 us
    ppermute x17, waiting for transfers between devices: 41.6 us -> 34.5 us  [move(): return lax.ppermute(array, AXES, pairs)]
    ppermute x17, starting transfers between devices: 16.1 us -> 20.5 us  [move(): return lax.ppermute(array, AXES, pairs)]
    pallas_call x4 -> x5, Pallas kernels: 13.4 us -> 13.9 us  [add(): pl.pallas_call(functools.partial(add_shards, tuple(names), places, totals...]
  transfers between devices with their start and end apart: 17 -> 17, of which waited for: 7 -> 7; matrix products, arithmetic and copies ran while one was open for 1% -> 1% of each run, Pallas kernels for 14% -> 15%
where the time goes in v5:
time: 72.4 us; the launch traced here: 72.2 us
  waiting for transfers between devices  34.5 us (48%)
  starting transfers between devices  20.5 us (28%)
  Pallas kernels  14.9 us (21%)
  local copies, waits for them, and re-layouts  1.78 us (2%)
    ppermute x17, waiting for transfers between devices, move(): return lax.ppermute(array, AXES, pairs)  34.5 us
    ppermute x17, starting transfers between devices, move(): return lax.ppermute(array, AXES, pairs)  20.5 us
    pallas_call x5, Pallas kernels, add(): pl.pallas_call(functools.partial(add_shards, tuple(names), places, totals...  13.9 us
  transfers between devices with their start and end apart: 17, of which 7 were waited for; matrix products, arithmetic and copies ran while one was open for 1% of the time, Pallas kernels for 15%

profile of v5, /device:TPU:0, one launch (start us, length us, event | category | flops | bytes accessed | tf_op | source)
XLA Modules:
  0.0 72.2 jit_solution(7677508962472412005)
XLA Ops:
  0.0 0.0 copy-start
  0.0 1.3 %copy.9 = bf16[2,64,4,3,128]{4,3,0,1,2:T(4,128)(2,1)S(1)} copy(bf16[2,64,4,3,128]{4,1,3,2,0:T(8,128)(2,1)} %bitcast.32) | data formatting | bytes 786432 | tf_op jit(solution)/shard_map/reshape | solution.py:354
  1.4 0.3 reshape.222.refs_0_
  1.7 4.1 %collective-permute-start = (bf16[4,64,768]{2,1,0:T(8,128)(2,1)S(1)}, bf16[4,64,768]{2,1,0:T(8,128)(2,1)S(1)}, u32[]{:S(2)}, u32[]{:S(2)}) collective-permute-start(bf16[4,64,768]{2,1,0:T(8,128)(2,1)S(1)} %reshape.222.refs_0_), channel_id=1, source_target_pairs={{0,4},{1,5},{2,6},{3,7},{4,0},{5,1},{6,2},{7,3},{8,12},{9,13},{10,... | collective-permute-start | bytes 1179656 | tf_op jit(solution)/shard_map/ppermute | solution.py:165
  5.8 1.5 %collective-permute-start.1 = (bf16[4,64,768]{2,1,0:T(8,128)(2,1)S(1)}, bf16[4,64,768]{2,1,0:T(8,128)(2,1)S(1)}, u32[]{:S(2)}, u32[]{:S(2)}) collective-permute-start(bf16[4,64,768]{2,1,0:T(8,128)(2,1)S(1)} %reshape.222.refs_0_), channel_id=1, source_target_pairs={{0,16},{1,17},{2,18},{3,19},{4,20},{5,21},{6,22},{7,23},{8,9},{9,8... | collective-permute-start | bytes 1179656 | tf_op jit(solution)/shard_map/ppermute | solution.py:165
  7.3 1.6 %collective-permute-start.2 = (bf16[4,64,768]{2,1,0:T(8,128)(2,1)S(1)}, bf16[4,64,768]{2,1,0:T(8,128)(2,1)S(1)}, u32[]{:S(2)}, u32[]{:S(2)}) collective-permute-start(bf16[4,64,768]{2,1,0:T(8,128)(2,1)S(1)} %reshape.222.refs_0_), channel_id=1, source_target_pairs={{0,2},{1,3},{2,0},{3,1},{4,6},{5,7},{6,4},{7,5},{8,10},{9,11},{10,... | collective-permute-start | bytes 1179656 | tf_op jit(solution)/shard_map/ppermute | solution.py:165
  8.9 1.5 %collective-permute-start.3 = (bf16[4,64,768]{2,1,0:T(8,128)(2,1)S(1)}, bf16[4,64,768]{2,1,0:T(8,128)(2,1)S(1)}, u32[]{:S(2)}, u32[]{:S(2)}) collective-permute-start(bf16[4,64,768]{2,1,0:T(8,128)(2,1)S(1)} %reshape.222.refs_0_), channel_id=1, source_target_pairs={{0,17},{1,16},{2,19},{3,18},{4,21},{5,20},{6,23},{7,22},{8,25},{9,... | collective-permute-start | bytes 1179656 | tf_op jit(solution)/shard_map/ppermute | solution.py:165
  10.4 0.5 collective-permute-start.4
  10.9 0.0 copy-done
  10.9 0.1 fusion
  11.1 0.1 stack.44.place_ref
  11.2 0.1 multiply_cosine_fusion
  11.3 12.1 %collective-permute-done.refs_5_.refs_1_.refs_0_ = bf16[4,64,768]{2,1,0:T(8,128)(2,1)S(1)} collective-permute-done((bf16[4,64,768]{2,1,0:T(8,128)(2,1)S(1)}, bf16[4,64,768]{2,1,0:T(8,128)(2,1)S(1)}, u32[]{:S(2)}, u32[]{:S(2)}) %collective-permute-start) | collective-permute-done | bytes 393248 | tf_op jit(solution)/shard_map/ppermute | solution.py:165
  23.4 0.0 collective-permute-done.1.refs_1_.refs_2_
  23.4 1.4 %collective-permute-done.2.refs_4_.refs_3_.refs_1_ = bf16[4,64,768]{2,1,0:T(8,128)(2,1)S(1)} collective-permute-done((bf16[4,64,768]{2,1,0:T(8,128)(2,1)S(1)}, bf16[4,64,768]{2,1,0:T(8,128)(2,1)S(1)}, u32[]{:S(2)}, u32[]{:S(2)}) %collective-permute-start.2) | collective-permute-done | bytes 393248 | tf_op jit(solution)/shard_map/ppermute | solution.py:165
  24.9 1.3 %collective-permute-done.3.refs_3_.refs_4_ = bf16[4,64,768]{2,1,0:T(8,128)(2,1)S(1)} collective-permute-done((bf16[4,64,768]{2,1,0:T(8,128)(2,1)S(1)}, bf16[4,64,768]{2,1,0:T(8,128)(2,1)S(1)}, u32[]{:S(2)}, u32[]{:S(2)}) %collective-permute-start.3) | collective-permute-done | bytes 393248 | tf_op jit(solution)/shard_map/ppermute | solution.py:165
  26.1 0.0 collective-permute-done.4.refs_2_.refs_5_.refs_4_
  26.1 0.8 %shard_map.28 = (bf16[6,4,64,768]{3,2,1,0:T(8,128)(2,1)S(1)}, bf16[2,4,64,768]{3,2,1,0:T(8,128)(2,1)S(1)}, bf16[2,4,64,768]{3,2,1,0:T(8,128)(2,1)S(1)}, bf16[4,64,768]{2,1,0:T(8,128)(2,1)S(1)}) custom-call(s32[7]{0:T(128)S(1)} %stack.44.place_ref, bf16[4,64,768]{2,1,0:T(8,128)(2,1)S(1)} %reshape.222.refs_0_, ...), custom_call_target="tpu_custom_call" | custom-call | tf_op jit(solution)/shard_map/pallas_call | solution.py:246
  27.0 0.2 collective-permute-start.9
  27.1 1.5 %collective-permute-start.5 = (bf16[2,4,64,768]{3,2,1,0:T(8,128)(2,1)S(1)}, bf16[2,4,64,768]{3,2,1,0:T(8,128)(2,1)S(1)}, u32[]{:S(2)}, u32[]{:S(2)}) collective-permute-start(bf16[2,4,64,768]{3,2,1,0:T(8,128)(2,1)S(1)} %get-tuple-element.82), channel_id=1, source_target_pairs={{0,16},{1,17},{2,18},{3,19},{4,20},{5,21},{6,22},{7,23},{8,9},{9,8... | collective-permute-start | bytes 2359304 | tf_op jit(solution)/shard_map/ppermute | solution.py:165
  28.6 2.5 %collective-permute-start.6 = (bf16[2,4,64,768]{3,2,1,0:T(8,128)(2,1)S(1)}, bf16[2,4,64,768]{3,2,1,0:T(8,128)(2,1)S(1)}, u32[]{:S(2)}, u32[]{:S(2)}) collective-permute-start(bf16[2,4,64,768]{3,2,1,0:T(8,128)(2,1)S(1)} %get-tuple-element.83), channel_id=1, source_target_pairs={{0,2},{1,3},{2,0},{3,1},{4,6},{5,7},{6,4},{7,5},{8,10},{9,11},{10,... | collective-permute-start | bytes 2359304 | tf_op jit(solution)/shard_map/ppermute | solution.py:165
  31.2 0.5 collective-permute-start.7
  31.7 1.5 %collective-permute-start.8 = (bf16[4,64,768]{2,1,0:T(8,128)(2,1)S(1)}, bf16[4,64,768]{2,1,0:T(8,128)(2,1)S(1)}, u32[]{:S(2)}, u32[]{:S(2)}) collective-permute-start(bf16[4,64,768]{2,1,0:T(8,128)(2,1)S(1)} %get-tuple-element.84), channel_id=1, source_target_pairs={{0,17},{1,16},{2,19},{3,18},{4,21},{5,20},{6,23},{7,22},{8,12},{9,... | collective-permute-start | bytes 1179656 | tf_op jit(solution)/shard_map/ppermute | solution.py:165
  33.2 2.5 %shard_map.29.refs_10_ = f32[2,2,256,256]{3,2,1,0:T(8,128)S(1)} custom-call(s32[7]{0:T(128)S(1)} %stack.44.place_ref, f32[8,2,128]{2,1,0:T(2,128)S(1)} %maximum_bitcast_fusion.weights_ref, bf16[4,64,768]{2,1,0:T(8,128)(2,1)S(1)} %reshape.222.refs_0_, bf16[4,64,768]{2,1,0:T(8,128)(2,1)S(1)} %collective-permute-done.refs_5_.refs_1_.refs_0_, ...), custom_call_target="tpu_custom_call" | custom-call | flops 1207959552 | bytes 4456448 | tf_op jit(solution)/shard_map/pallas_call | solution.py:214
  35.6 16.9 %collective-permute-done.8.ab2_ref.refs_8_ = bf16[4,64,768]{2,1,0:T(8,128)(2,1)S(1)} collective-permute-done((bf16[4,64,768]{2,1,0:T(8,128)(2,1)S(1)}, bf16[4,64,768]{2,1,0:T(8,128)(2,1)S(1)}, u32[]{:S(2)}, u32[]{:S(2)}) %collective-permute-start.8) | collective-permute-done | bytes 393248 | tf_op jit(solution)/shard_map/ppermute | solution.py:165
  52.6 0.0 collective-permute-done.5.a12_ref.refs_5_.refs_2_
  52.6 0.0 collective-permute-done.6.z1_ref.refs_6_.refs_3_.refs_0_
  52.6 0.0 collective-permute-done.7.b12_ref.refs_7_.refs_4_
  52.6 0.0 collective-permute-done.9.refs_9_
  52.6 0.2 shard_map.30
  52.8 0.1 collective-permute-start.13
  52.9 1.8 %collective-permute-start.10 = (bf16[4,64,768]{2,1,0:T(8,128)(2,1)S(1)}, bf16[4,64,768]{2,1,0:T(8,128)(2,1)S(1)}, u32[]{:S(2)}, u32[]{:S(2)}) collective-permute-start(bf16[4,64,768]{2,1,0:T(8,128)(2,1)S(1)} %collective-permute-done.8.ab2_ref.refs_8_), channel_id=1, source_target_pairs={{0,2},{1,3},{2,0},{3,1},{4,6},{5,7},{6,4},{7,5},{8,10},{9,11},{10,... | collective-permute-start | bytes 1179656 | tf_op jit(solution)/shard_map/ppermute | solution.py:165
  54.6 1.5 %collective-permute-start.11 = (bf16[4,64,768]{2,1,0:T(8,128)(2,1)S(1)}, bf16[4,64,768]{2,1,0:T(8,128)(2,1)S(1)}, u32[]{:S(2)}, u32[]{:S(2)}) collective-permute-start(bf16[4,64,768]{2,1,0:T(8,128)(2,1)S(1)} %get-tuple-element.108), channel_id=1, source_target_pairs={{0,16},{1,17},{2,18},{3,19},{4,20},{5,21},{6,22},{7,23},{8,9},{9,8... | collective-permute-start | bytes 1179656 | tf_op jit(solution)/shard_map/ppermute | solution.py:165
  56.1 1.2 %collective-permute-start.12 = (bf16[4,64,768]{2,1,0:T(8,128)(2,1)S(1)}, bf16[4,64,768]{2,1,0:T(8,128)(2,1)S(1)}, u32[]{:S(2)}, u32[]{:S(2)}) collective-permute-start(bf16[4,64,768]{2,1,0:T(8,128)(2,1)S(1)} %get-tuple-element.108), channel_id=1, source_target_pairs={{0,1},{1,0},{2,3},{3,2},{4,5},{5,4},{6,7},{7,6},{8,24},{9,25},{10,... | collective-permute-start | bytes 1179656 | tf_op jit(solution)/shard_map/ppermute | solution.py:165
  57.3 4.3 %shard_map.31.refs_6_ = f32[2,2,256,256]{3,2,1,0:T(8,128)S(1)} custom-call(s32[7]{0:T(128)S(1)} %stack.44.place_ref, f32[8,2,128]{2,1,0:T(2,128)S(1)} %maximum_bitcast_fusion.weights_ref, bf16[4,64,768]{2,1,0:T(8,128)(2,1)S(1)} %reshape.222.refs_0_, bf16[4,64,768]{2,1,0:T(8,128)(2,1)S(1)} %collective-permute-done.refs_5_.refs_1_.refs_0_, ...), custom_call_target="tpu_custom_call" | custom-call | flops 2617245696 | bytes 7208960 | tf_op jit(solution)/shard_map/pallas_call | solution.py:214
  61.6 0.0 collective-permute-done.13.refs_5_
  61.7 2.7 %shard_map.32.refs_4_ = f32[2,2,256,256]{3,2,1,0:T(8,128)S(1)} custom-call(s32[7]{0:T(128)S(1)} %stack.44.place_ref, f32[8,2,128]{2,1,0:T(2,128)S(1)} %maximum_bitcast_fusion.weights_ref, bf16[4,64,768]{2,1,0:T(8,128)(2,1)S(1)} %collective-permute-done.refs_5_.refs_1_.refs_0_, bf16[4,64,768]{2,1,0:T(8,128)(2,1)S(1)} %collective-permute-done.2.refs_4_.refs_3_.refs_1_, ...), custom_call_target="tpu_custom_call" | custom-call | flops 1409286144 | bytes 4849664 | tf_op jit(solution)/shard_map/pallas_call | solution.py:214
  64.4 0.0 collective-permute-done.10.refs_1_
  64.4 2.1 %collective-permute-done.11.refs_2_.refs_1_ = bf16[4,64,768]{2,1,0:T(8,128)(2,1)S(1)} collective-permute-done((bf16[4,64,768]{2,1,0:T(8,128)(2,1)S(1)}, bf16[4,64,768]{2,1,0:T(8,128)(2,1)S(1)}, u32[]{:S(2)}, u32[]{:S(2)}) %collective-permute-start.11) | collective-permute-done | bytes 393248 | tf_op jit(solution)/shard_map/ppermute | solution.py:165
  66.5 0.0 collective-permute-done.12.refs_3_.refs_2_
  66.5 0.1 collective-permute-start.14
  66.6 0.4 collective-permute-start.15
  67.0 0.1 collective-permute-start.16
  67.2 1.5 %shard_map.33.refs_6_ = f32[2,2,256,256]{3,2,1,0:T(8,128)S(1)} custom-call(s32[7]{0:T(128)S(1)} %stack.44.place_ref, f32[8,2,128]{2,1,0:T(2,128)S(1)} %maximum_bitcast_fusion.weights_ref, bf16[2,4,64,768]{3,2,1,0:T(8,128)(2,1)S(1)} %collective-permute-done.6.z1_ref.refs_6_.refs_3_.refs_0_, bf16[4,64,768]{2,1,0:T(8,128)(2,1)S(1)} %collective-permute-done.10.refs_1_, ...), custom_call_target="tpu_custom_call" | custom-call | flops 603979776 | bytes 3276800 | tf_op jit(solution)/shard_map/pallas_call | solution.py:214
  68.7 0.0 collective-permute-done.14.refs_3_
  68.7 0.1 collective-permute-done.15.refs_4_
  68.8 0.6 collective-permute-done.16.refs_5_
  69.4 2.9 %shard_map.34 = f32[16,64,256]{2,1,0:T(8,128)} custom-call(s32[7]{0:T(128)S(1)} %stack.44.place_ref, f32[8,2,128]{2,1,0:T(2,128)S(1)} %maximum_bitcast_fusion.weights_ref, bf16[2,4,64,768]{3,2,1,0:T(8,128)(2,1)S(1)} %collective-permute-done.6.z1_ref.refs_6_.refs_3_.refs_0_, bf16[4,64,768]{2,1,0:T(8,128)(2,1)S(1)} %collective-permute-done.11.refs_2_.refs_1_, ...), custom_call_target="tpu_custom_call" | custom-call | flops 603979776 | bytes 3276800 | tf_op jit(solution)/shard_map/pallas_call | solution.py:214
  (5 shorter events, 0.1 us)
Async XLA Ops:
  0.0 10.9 %copy-start = (s32[4,3]{1,0:T(4,128)S(1)}, s32[4,3]{1,0:T(4,128)}, u32[]{:S(2)}) copy-start(s32[4,3]{1,0:T(4,128)} %param.3) | copy-start | bytes 148
  1.7 21.7 %collective-permute-start = (bf16[4,64,768]{2,1,0:T(8,128)(2,1)S(1)}, bf16[4,64,768]{2,1,0:T(8,128)(2,1)S(1)}, u32[]{:S(2)}, u32[]{:S(2)}) collective-permute-start(bf16[4,64,768]{2,1,0:T(8,128)(2,1)S(1)} %reshape.222.refs_0_), channel_id=1, source_target_pairs={{0,4},{1,5},{2,6},{3,7},{4,0},{5,1},{6,2},{7,3},{8,12},{9,13},{10,... | collective-permute-start | bytes 1179656 | tf_op jit(solution)/shard_map/ppermute | solution.py:165
  5.8 17.6 %collective-permute-start.1 = (bf16[4,64,768]{2,1,0:T(8,128)(2,1)S(1)}, bf16[4,64,768]{2,1,0:T(8,128)(2,1)S(1)}, u32[]{:S(2)}, u32[]{:S(2)}) collective-permute-start(bf16[4,64,768]{2,1,0:T(8,128)(2,1)S(1)} %reshape.222.refs_0_), channel_id=1, source_target_pairs={{0,16},{1,17},{2,18},{3,19},{4,20},{5,21},{6,22},{7,23},{8,9},{9,8... | collective-permute-start | bytes 1179656 | tf_op jit(solution)/shard_map/ppermute | solution.py:165
  7.3 17.6 %collective-permute-start.2 = (bf16[4,64,768]{2,1,0:T(8,128)(2,1)S(1)}, bf16[4,64,768]{2,1,0:T(8,128)(2,1)S(1)}, u32[]{:S(2)}, u32[]{:S(2)}) collective-permute-start(bf16[4,64,768]{2,1,0:T(8,128)(2,1)S(1)} %reshape.222.refs_0_), channel_id=1, source_target_pairs={{0,2},{1,3},{2,0},{3,1},{4,6},{5,7},{6,4},{7,5},{8,10},{9,11},{10,... | collective-permute-start | bytes 1179656 | tf_op jit(solution)/shard_map/ppermute | solution.py:165
  8.9 17.3 %collective-permute-start.3 = (bf16[4,64,768]{2,1,0:T(8,128)(2,1)S(1)}, bf16[4,64,768]{2,1,0:T(8,128)(2,1)S(1)}, u32[]{:S(2)}, u32[]{:S(2)}) collective-permute-start(bf16[4,64,768]{2,1,0:T(8,128)(2,1)S(1)} %reshape.222.refs_0_), channel_id=1, source_target_pairs={{0,17},{1,16},{2,19},{3,18},{4,21},{5,20},{6,23},{7,22},{8,25},{9,... | collective-permute-start | bytes 1179656 | tf_op jit(solution)/shard_map/ppermute | solution.py:165
  10.4 15.8 %collective-permute-start.4 = (bf16[4,64,768]{2,1,0:T(8,128)(2,1)S(1)}, bf16[4,64,768]{2,1,0:T(8,128)(2,1)S(1)}, u32[]{:S(2)}, u32[]{:S(2)}) collective-permute-start(bf16[4,64,768]{2,1,0:T(8,128)(2,1)S(1)} %reshape.222.refs_0_), channel_id=1, source_target_pairs={{0,1},{1,0},{2,3},{3,2},{4,5},{5,4},{6,7},{7,6},{8,24},{9,25},{10,... | collective-permute-start | bytes 1179656 | tf_op jit(solution)/shard_map/ppermute | solution.py:165
  27.0 25.6 %collective-permute-start.9 = (bf16[6,4,64,768]{3,2,1,0:T(8,128)(2,1)S(1)}, bf16[6,4,64,768]{3,2,1,0:T(8,128)(2,1)S(1)}, u32[]{:S(2)}, u32[]{:S(2)}) collective-permute-start(bf16[6,4,64,768]{3,2,1,0:T(8,128)(2,1)S(1)} %get-tuple-element.85), channel_id=1, source_target_pairs={{0,8},{1,9},{2,10},{3,11},{4,12},{5,13},{6,14},{7,15},{8,0},{9,1},... | collective-permute-start | bytes 7077896 | tf_op jit(solution)/shard_map/ppermute | solution.py:165
  27.1 25.4 %collective-permute-start.5 = (bf16[2,4,64,768]{3,2,1,0:T(8,128)(2,1)S(1)}, bf16[2,4,64,768]{3,2,1,0:T(8,128)(2,1)S(1)}, u32[]{:S(2)}, u32[]{:S(2)}) collective-permute-start(bf16[2,4,64,768]{3,2,1,0:T(8,128)(2,1)S(1)} %get-tuple-element.82), channel_id=1, source_target_pairs={{0,16},{1,17},{2,18},{3,19},{4,20},{5,21},{6,22},{7,23},{8,9},{9,8... | collective-permute-start | bytes 2359304 | tf_op jit(solution)/shard_map/ppermute | solution.py:165
  28.6 23.9 %collective-permute-start.6 = (bf16[2,4,64,768]{3,2,1,0:T(8,128)(2,1)S(1)}, bf16[2,4,64,768]{3,2,1,0:T(8,128)(2,1)S(1)}, u32[]{:S(2)}, u32[]{:S(2)}) collective-permute-start(bf16[2,4,64,768]{3,2,1,0:T(8,128)(2,1)S(1)} %get-tuple-element.83), channel_id=1, source_target_pairs={{0,2},{1,3},{2,0},{3,1},{4,6},{5,7},{6,4},{7,5},{8,10},{9,11},{10,... | collective-permute-start | bytes 2359304 | tf_op jit(solution)/shard_map/ppermute | solution.py:165
  31.2 21.4 %collective-permute-start.7 = (bf16[2,4,64,768]{3,2,1,0:T(8,128)(2,1)S(1)}, bf16[2,4,64,768]{3,2,1,0:T(8,128)(2,1)S(1)}, u32[]{:S(2)}, u32[]{:S(2)}) collective-permute-start(bf16[2,4,64,768]{3,2,1,0:T(8,128)(2,1)S(1)} %get-tuple-element.82), channel_id=1, source_target_pairs={{0,1},{1,0},{2,3},{3,2},{4,5},{5,4},{6,7},{7,6},{8,24},{9,25},{10,... | collective-permute-start | bytes 2359304 | tf_op jit(solution)/shard_map/ppermute | solution.py:165
  31.7 20.9 %collective-permute-start.8 = (bf16[4,64,768]{2,1,0:T(8,128)(2,1)S(1)}, bf16[4,64,768]{2,1,0:T(8,128)(2,1)S(1)}, u32[]{:S(2)}, u32[]{:S(2)}) collective-permute-start(bf16[4,64,768]{2,1,0:T(8,128)(2,1)S(1)} %get-tuple-element.84), channel_id=1, source_target_pairs={{0,17},{1,16},{2,19},{3,18},{4,21},{5,20},{6,23},{7,22},{8,12},{9,... | collective-permute-start | bytes 1179656 | tf_op jit(solution)/shard_map/ppermute | solution.py:165
  52.8 8.9 %collective-permute-start.13 = (bf16[7,4,64,768]{3,2,1,0:T(8,128)(2,1)S(1)}, bf16[7,4,64,768]{3,2,1,0:T(8,128)(2,1)S(1)}, u32[]{:S(2)}, u32[]{:S(2)}) collective-permute-start(bf16[7,4,64,768]{3,2,1,0:T(8,128)(2,1)S(1)} %get-tuple-element.109), channel_id=1, source_target_pairs={{0,8},{1,9},{2,10},{3,11},{4,12},{5,13},{6,14},{7,15},{8,0},{9,1},... | collective-permute-start | bytes 8257544 | tf_op jit(solution)/shard_map/ppermute | solution.py:165
  52.9 11.5 %collective-permute-start.10 = (bf16[4,64,768]{2,1,0:T(8,128)(2,1)S(1)}, bf16[4,64,768]{2,1,0:T(8,128)(2,1)S(1)}, u32[]{:S(2)}, u32[]{:S(2)}) collective-permute-start(bf16[4,64,768]{2,1,0:T(8,128)(2,1)S(1)} %collective-permute-done.8.ab2_ref.refs_8_), channel_id=1, source_target_pairs={{0,2},{1,3},{2,0},{3,1},{4,6},{5,7},{6,4},{7,5},{8,10},{9,11},{10,... | collective-permute-start | bytes 1179656 | tf_op jit(solution)/shard_map/ppermute | solution.py:165
  54.6 11.9 %collective-permute-start.11 = (bf16[4,64,768]{2,1,0:T(8,128)(2,1)S(1)}, bf16[4,64,768]{2,1,0:T(8,128)(2,1)S(1)}, u32[]{:S(2)}, u32[]{:S(2)}) collective-permute-start(bf16[4,64,768]{2,1,0:T(8,128)(2,1)S(1)} %get-tuple-element.108), channel_id=1, source_target_pairs={{0,16},{1,17},{2,18},{3,19},{4,20},{5,21},{6,22},{7,23},{8,9},{9,8... | collective-permute-start | bytes 1179656 | tf_op jit(solution)/shard_map/ppermute | solution.py:165
  56.1 10.4 %collective-permute-start.12 = (bf16[4,64,768]{2,1,0:T(8,128)(2,1)S(1)}, bf16[4,64,768]{2,1,0:T(8,128)(2,1)S(1)}, u32[]{:S(2)}, u32[]{:S(2)}) collective-permute-start(bf16[4,64,768]{2,1,0:T(8,128)(2,1)S(1)} %get-tuple-element.108), channel_id=1, source_target_pairs={{0,1},{1,0},{2,3},{3,2},{4,5},{5,4},{6,7},{7,6},{8,24},{9,25},{10,... | collective-permute-start | bytes 1179656 | tf_op jit(solution)/shard_map/ppermute | solution.py:165
  66.5 2.2 %collective-permute-start.14 = (bf16[4,64,768]{2,1,0:T(8,128)(2,1)S(1)}, bf16[4,64,768]{2,1,0:T(8,128)(2,1)S(1)}, u32[]{:S(2)}, u32[]{:S(2)}) collective-permute-start(bf16[4,64,768]{2,1,0:T(8,128)(2,1)S(1)} %collective-permute-done.10.refs_1_), channel_id=1, source_target_pairs={{0,8},{1,9},{2,10},{3,11},{4,12},{5,13},{6,14},{7,15},{8,0},{9,1},... | collective-permute-start | bytes 1179656 | tf_op jit(solution)/shard_map/ppermute | solution.py:165
  66.6 2.2 %collective-permute-start.15 = (bf16[4,64,768]{2,1,0:T(8,128)(2,1)S(1)}, bf16[4,64,768]{2,1,0:T(8,128)(2,1)S(1)}, u32[]{:S(2)}, u32[]{:S(2)}) collective-permute-start(bf16[4,64,768]{2,1,0:T(8,128)(2,1)S(1)} %collective-permute-done.11.refs_2_.refs_1_), channel_id=1, source_target_pairs={{0,8},{1,9},{2,10},{3,11},{4,12},{5,13},{6,14},{7,15},{8,0},{9,1},... | collective-permute-start | bytes 1179656 | tf_op jit(solution)/shard_map/ppermute | solution.py:165
  67.0 2.3 %collective-permute-start.16 = (bf16[4,64,768]{2,1,0:T(8,128)(2,1)S(1)}, bf16[4,64,768]{2,1,0:T(8,128)(2,1)S(1)}, u32[]{:S(2)}, u32[]{:S(2)}) collective-permute-start(bf16[4,64,768]{2,1,0:T(8,128)(2,1)S(1)} %collective-permute-done.12.refs_3_.refs_2_), channel_id=1, source_target_pairs={{0,8},{1,9},{2,10},{3,11},{4,12},{5,13},{6,14},{7,15},{8,0},{9,1},... | collective-permute-start | bytes 1179656 | tf_op jit(solution)/shard_map/ppermute | solution.py:165

commit v6 on v5

--- a/solution.py
+++ b/solution.py
@@ -119,9 +119,8 @@
 
 
 def route_second(place_ref, *refs):
-    stack_ref, both_ref, relayed_ref, mixed_ref = refs[6:]
-    ab0_ref, o1_ref, o2_ref = refs[3:6]
-    for slot in range(6):
+    ab0_ref, o1_ref, o2_ref, stack_ref, both_ref, relayed_ref, mixed_ref = refs
+    for slot in range(3):
         stack_ref[slot] = refs[slot][...]
     both_ref[0] = o1_ref[...]
     both_ref[1] = o2_ref[...]
@@ -233,11 +232,19 @@
 
     put("0", packed, "near", [("O", 0)])
 
-    first = [("O", 2), ("A", 0), ("O", 1), ("AB", 0), ("B", 0)]
-    new = [hop_z(packed, 2), hop_a(packed), hop_z(packed, 1), hop_ab(packed), hop_b(packed)]
-    for order, (kind, array) in enumerate(zip(first, new)):
-        put("1" + "abcde"[order], array, "near", [kind])
-    place, weights = fence((place, weights))
+    early = [("O", 0), ("A", 0), ("B", 0)]
+    new = [hop_z(packed, 2), hop_a(packed), hop_z(packed, 1), hop_b(packed)]
+    put("1b", new[1], "near", [("A", 0)])
+    put("1d", new[3], "near", [("B", 0)])
+    totals, place, weights = fence((None, place, weights))
+    totals = add([("near", *kind) for kind in early], None)
+    totals = fence(totals)
+    for order, kind in enumerate(early):
+        put("1f" + "abc"[order], swap(near(*kind)), "far", [kind])
+    put("1e", hop_b(near("A", 0)), "near", [("AB", 0)])
+    put("1a", new[0], "near", [("O", 2)])
+    put("1c", new[2], "near", [("O", 1)])
+    totals = fence(totals)
 
     def route(kernel, operands, counts):
         block = pl.BlockSpec(memory_space=pltpu.VMEM)
@@ -252,20 +259,22 @@
         )(*operands)
         return fence(routed)
 
-    first = [("O", 0), ("A", 0), ("B", 0), ("AB", 0), ("O", 1), ("O", 2)]
+    first = [("AB", 0), ("O", 1), ("O", 2)]
     stack, both, relayed, mixed = route(
-        route_second, [place] + [near(*kind) for kind in first], (6, 2, 2, 1)
+        route_second, [place] + [near(*kind) for kind in first], (3, 2, 2, 1)
     )
     second = [("AB", 1), ("O", 3), ("A", 1), ("A", 2), ("B", 1), ("B", 2), ("AB", 2)]
-    totals = add([("near", *kind) for kind in first], None)
-    put("2a", hop_a(both), "near", second[2:4])
-    put("2b", hop_z(relayed, 1), "near", second[0:2])
+    totals = add(
+        [("near", *kind) for kind in first] + [("far", *kind) for kind in early], totals
+    )
+    put("2a", hop_z(relayed, 1), "near", second[0:2])
+    put("2b", hop_a(both), "near", second[2:4])
     put("2c", hop_b(both), "near", second[4:6])
     put("2d", hop_mixed(mixed), "near", second[6:7])
     put("2e", swap(stack), "far", first)
     totals = fence(totals)
 
-    arrived = [arrays[key] for key in ("2b", "2a", "2c", "2d")]
+    arrived = [arrays[key] for key in ("2a", "2b", "2c", "2d")]
     stack, start = route(route_third, arrived, (7, 1))
     third = [("AB", 3), ("A", 3), ("B", 3)]
     new = [hop_z(near("AB", 2), 1), hop_a(start), hop_b(start)]

time: 72.4 us -> 72.1 us (level)
    ppermute x17 -> x20, starting transfers between devices: 20.5 us -> 19.8 us  [move(): return lax.ppermute(array, AXES, pairs)]
    pallas_call x5 -> x6, Pallas kernels: 13.9 us -> 14.5 us  [add(): pl.pallas_call(functools.partial(add_shards, tuple(names), places, totals...]
    ppermute x17 -> x20, waiting for transfers between devices: 34.5 us -> 34.5 us  [move(): return lax.ppermute(array, AXES, pairs)]
  transfers between devices with their start and end apart: 17 -> 20, of which waited for: 7 -> 10; matrix products, arithmetic and copies ran while one was open for 1% -> 1% of each run, Pallas kernels for 15% -> 16%
where the time goes in v6:
time: 72.1 us; the launch traced here: 72 us
  waiting for transfers between devices  34.5 us (48%)
  starting transfers between devices  19.8 us (27%)
  Pallas kernels  15.4 us (21%)
  local copies, waits for them, and re-layouts  1.78 us (2%)
    ppermute x20, waiting for transfers between devices, move(): return lax.ppermute(array, AXES, pairs)  34.5 us
    ppermute x20, starting transfers between devices, move(): return lax.ppermute(array, AXES, pairs)  19.8 us
    pallas_call x6, Pallas kernels, add(): pl.pallas_call(functools.partial(add_shards, tuple(names), places, totals...  14.5 us
  transfers between devices with their start and end apart: 20, of which 10 were waited for; matrix products, arithmetic and copies ran while one was open for 1% of the time, Pallas kernels for 16%

profile of v6, /device:TPU:0, one launch (start us, length us, event | category | flops | bytes accessed | tf_op | source)
XLA Modules:
  0.0 72.0 jit_solution(14812109042593119711)
XLA Ops:
  0.0 0.0 copy-start
  0.0 1.3 %copy.9 = bf16[2,64,4,3,128]{4,3,0,1,2:T(4,128)(2,1)S(1)} copy(bf16[2,64,4,3,128]{4,1,3,2,0:T(8,128)(2,1)} %bitcast.32) | data formatting | bytes 786432 | tf_op jit(solution)/shard_map/reshape | solution.py:363
  1.4 0.3 reshape.222.refs_0_
  1.7 3.0 %collective-permute-start = (bf16[4,64,768]{2,1,0:T(8,128)(2,1)S(1)}, bf16[4,64,768]{2,1,0:T(8,128)(2,1)S(1)}, u32[]{:S(2)}, u32[]{:S(2)}) collective-permute-start(bf16[4,64,768]{2,1,0:T(8,128)(2,1)S(1)} %reshape.222.refs_0_), channel_id=1, source_target_pairs={{0,16},{1,17},{2,18},{3,19},{4,20},{5,21},{6,22},{7,23},{8,9},{9,8... | collective-permute-start | bytes 1179656 | tf_op jit(solution)/shard_map/ppermute | solution.py:164
  4.7 1.5 %collective-permute-start.1 = (bf16[4,64,768]{2,1,0:T(8,128)(2,1)S(1)}, bf16[4,64,768]{2,1,0:T(8,128)(2,1)S(1)}, u32[]{:S(2)}, u32[]{:S(2)}) collective-permute-start(bf16[4,64,768]{2,1,0:T(8,128)(2,1)S(1)} %reshape.222.refs_0_), channel_id=1, source_target_pairs={{0,1},{1,0},{2,3},{3,2},{4,5},{5,4},{6,7},{7,6},{8,24},{9,25},{10,... | collective-permute-start | bytes 1179656 | tf_op jit(solution)/shard_map/ppermute | solution.py:164
  6.2 2.6 %collective-permute-start.2 = (bf16[4,64,768]{2,1,0:T(8,128)(2,1)S(1)}, bf16[4,64,768]{2,1,0:T(8,128)(2,1)S(1)}, u32[]{:S(2)}, u32[]{:S(2)}) collective-permute-start(bf16[4,64,768]{2,1,0:T(8,128)(2,1)S(1)} %reshape.222.refs_0_), channel_id=1, source_target_pairs={{0,4},{1,5},{2,6},{3,7},{4,0},{5,1},{6,2},{7,3},{8,12},{9,13},{10,... | collective-permute-start | bytes 1179656 | tf_op jit(solution)/shard_map/ppermute | solution.py:164
  8.8 1.6 %collective-permute-start.3 = (bf16[4,64,768]{2,1,0:T(8,128)(2,1)S(1)}, bf16[4,64,768]{2,1,0:T(8,128)(2,1)S(1)}, u32[]{:S(2)}, u32[]{:S(2)}) collective-permute-start(bf16[4,64,768]{2,1,0:T(8,128)(2,1)S(1)} %reshape.222.refs_0_), channel_id=1, source_target_pairs={{0,2},{1,3},{2,0},{3,1},{4,6},{5,7},{6,4},{7,5},{8,10},{9,11},{10,... | collective-permute-start | bytes 1179656 | tf_op jit(solution)/shard_map/ppermute | solution.py:164
  10.4 0.0 copy-done
  10.5 0.1 fusion
  10.6 0.1 stack.44.place_ref
  10.7 0.1 multiply_cosine_fusion
  10.9 3.2 %collective-permute-done.refs_1_.refs_2_ = bf16[4,64,768]{2,1,0:T(8,128)(2,1)S(1)} collective-permute-done((bf16[4,64,768]{2,1,0:T(8,128)(2,1)S(1)}, bf16[4,64,768]{2,1,0:T(8,128)(2,1)S(1)}, u32[]{:S(2)}, u32[]{:S(2)}) %collective-permute-start) | collective-permute-done | bytes 393248 | tf_op jit(solution)/shard_map/ppermute | solution.py:164
  14.1 0.0 collective-permute-done.1.refs_2_.refs_4_.refs_3_
  14.1 1.6 %shard_map.28.refs_9_ = f32[2,2,256,256]{3,2,1,0:T(8,128)S(1)} custom-call(s32[7]{0:T(128)S(1)} %stack.44.place_ref, f32[8,2,128]{2,1,0:T(2,128)S(1)} %maximum_bitcast_fusion.weights_ref, bf16[4,64,768]{2,1,0:T(8,128)(2,1)S(1)} %reshape.222.refs_0_, bf16[4,64,768]{2,1,0:T(8,128)(2,1)S(1)} %collective-permute-done.refs_1_.refs_2_, ...), custom_call_target="tpu_custom_call" | custom-call | flops 603979776 | bytes 3276800 | tf_op jit(solution)/shard_map/pallas_call | solution.py:213
  15.7 1.6 %collective-permute-start.4 = (bf16[4,64,768]{2,1,0:T(8,128)(2,1)S(1)}, bf16[4,64,768]{2,1,0:T(8,128)(2,1)S(1)}, u32[]{:S(2)}, u32[]{:S(2)}) collective-permute-start(bf16[4,64,768]{2,1,0:T(8,128)(2,1)S(1)} %collective-permute-done.refs_1_.refs_2_), channel_id=1, source_target_pairs={{0,1},{1,0},{2,3},{3,2},{4,5},{5,4},{6,7},{7,6},{8,24},{9,25},{10,... | collective-permute-start | bytes 1179656 | tf_op jit(solution)/shard_map/ppermute | solution.py:164
  17.3 0.9 %collective-permute-start.6 = (bf16[4,64,768]{2,1,0:T(8,128)(2,1)S(1)}, bf16[4,64,768]{2,1,0:T(8,128)(2,1)S(1)}, u32[]{:S(2)}, u32[]{:S(2)}) collective-permute-start(bf16[4,64,768]{2,1,0:T(8,128)(2,1)S(1)} %collective-permute-done.refs_1_.refs_2_), channel_id=1, source_target_pairs={{0,8},{1,9},{2,10},{3,11},{4,12},{5,13},{6,14},{7,15},{8,0},{9,1},... | collective-permute-start | bytes 1179656 | tf_op jit(solution)/shard_map/ppermute | solution.py:164
  18.2 0.0 collective-permute-start.5
  18.2 7.8 %collective-permute-done.2.refs_2_.refs_1_.refs_0_ = bf16[4,64,768]{2,1,0:T(8,128)(2,1)S(1)} collective-permute-done((bf16[4,64,768]{2,1,0:T(8,128)(2,1)S(1)}, bf16[4,64,768]{2,1,0:T(8,128)(2,1)S(1)}, u32[]{:S(2)}, u32[]{:S(2)}) %collective-permute-start.2) | collective-permute-done | bytes 393248 | tf_op jit(solution)/shard_map/ppermute | solution.py:164
  25.9 0.0 collective-permute-start.7
  25.9 0.2 collective-permute-done.3.refs_1_.refs_3_.refs_2_
  26.1 0.0 collective-permute-done.4.refs_0_.refs_5_
  26.1 0.0 collective-permute-done.5.refs_6_
  26.1 0.0 collective-permute-done.6.refs_7_
  26.1 1.5 %collective-permute-done.7.refs_8_ = bf16[4,64,768]{2,1,0:T(8,128)(2,1)S(1)} collective-permute-done((bf16[4,64,768]{2,1,0:T(8,128)(2,1)S(1)}, bf16[4,64,768]{2,1,0:T(8,128)(2,1)S(1)}, u32[]{:S(2)}, u32[]{:S(2)}) %collective-permute-start.7) | collective-permute-done | bytes 393248 | tf_op jit(solution)/shard_map/ppermute | solution.py:164
  27.7 0.7 %shard_map.29 = (bf16[3,4,64,768]{3,2,1,0:T(8,128)(2,1)S(1)}, bf16[2,4,64,768]{3,2,1,0:T(8,128)(2,1)S(1)}, bf16[2,4,64,768]{3,2,1,0:T(8,128)(2,1)S(1)}, bf16[4,64,768]{2,1,0:T(8,128)(2,1)S(1)}) custom-call(s32[7]{0:T(128)S(1)} %stack.44.place_ref, bf16[4,64,768]{2,1,0:T(8,128)(2,1)S(1)} %collective-permute-done.4.refs_0_.refs_5_, ...), custom_call_target="tpu_custom_call" | custom-call | tf_op jit(solution)/shard_map/pallas_call | solution.py:253
  28.4 0.2 collective-permute-start.12
  28.6 0.5 collective-permute-start.10
  29.1 0.6 collective-permute-start.8
  29.7 0.5 collective-permute-start.9
  30.2 2.4 %collective-permute-start.11 = (bf16[4,64,768]{2,1,0:T(8,128)(2,1)S(1)}, bf16[4,64,768]{2,1,0:T(8,128)(2,1)S(1)}, u32[]{:S(2)}, u32[]{:S(2)}) collective-permute-start(bf16[4,64,768]{2,1,0:T(8,128)(2,1)S(1)} %get-tuple-element.109), channel_id=1, source_target_pairs={{0,17},{1,16},{2,19},{3,18},{4,21},{5,20},{6,23},{7,22},{8,12},{9,... | collective-permute-start | bytes 1179656 | tf_op jit(solution)/shard_map/ppermute | solution.py:164
  32.7 2.2 %shard_map.30.refs_9_ = f32[2,2,256,256]{3,2,1,0:T(8,128)S(1)} custom-call(s32[7]{0:T(128)S(1)} %stack.44.place_ref, f32[8,2,128]{2,1,0:T(2,128)S(1)} %maximum_bitcast_fusion.weights_ref, bf16[4,64,768]{2,1,0:T(8,128)(2,1)S(1)} %reshape.222.refs_0_, bf16[4,64,768]{2,1,0:T(8,128)(2,1)S(1)} %collective-permute-done.2.refs_2_.refs_1_.refs_0_, ...), custom_call_target="tpu_custom_call" | custom-call | flops 1207959552 | bytes 4456448 | tf_op jit(solution)/shard_map/pallas_call | solution.py:213
  34.9 17.8 %collective-permute-done.11.ab2_ref.refs_7_ = bf16[4,64,768]{2,1,0:T(8,128)(2,1)S(1)} collective-permute-done((bf16[4,64,768]{2,1,0:T(8,128)(2,1)S(1)}, bf16[4,64,768]{2,1,0:T(8,128)(2,1)S(1)}, u32[]{:S(2)}, u32[]{:S(2)}) %collective-permute-start.11) | collective-permute-done | bytes 393248 | tf_op jit(solution)/shard_map/ppermute | solution.py:164
  52.7 0.5 collective-permute-done.10.b12_ref.refs_6_.refs_4_
  53.2 0.0 collective-permute-done.8.z1_ref.refs_4_.refs_2_.refs_0_
  53.2 0.0 collective-permute-done.9.a12_ref.refs_5_.refs_3_
  53.2 0.0 collective-permute-done.12.refs_8_
  53.2 0.2 shard_map.31
  53.4 0.1 collective-permute-start.16
  53.5 1.7 %collective-permute-start.13 = (bf16[4,64,768]{2,1,0:T(8,128)(2,1)S(1)}, bf16[4,64,768]{2,1,0:T(8,128)(2,1)S(1)}, u32[]{:S(2)}, u32[]{:S(2)}) collective-permute-start(bf16[4,64,768]{2,1,0:T(8,128)(2,1)S(1)} %collective-permute-done.11.ab2_ref.refs_7_), channel_id=1, source_target_pairs={{0,2},{1,3},{2,0},{3,1},{4,6},{5,7},{6,4},{7,5},{8,10},{9,11},{10,... | collective-permute-start | bytes 1179656 | tf_op jit(solution)/shard_map/ppermute | solution.py:164
  55.2 1.1 %collective-permute-start.14 = (bf16[4,64,768]{2,1,0:T(8,128)(2,1)S(1)}, bf16[4,64,768]{2,1,0:T(8,128)(2,1)S(1)}, u32[]{:S(2)}, u32[]{:S(2)}) collective-permute-start(bf16[4,64,768]{2,1,0:T(8,128)(2,1)S(1)} %get-tuple-element.132), channel_id=1, source_target_pairs={{0,16},{1,17},{2,18},{3,19},{4,20},{5,21},{6,22},{7,23},{8,9},{9,8... | collective-permute-start | bytes 1179656 | tf_op jit(solution)/shard_map/ppermute | solution.py:164
  56.3 0.9 %collective-permute-start.15 = (bf16[4,64,768]{2,1,0:T(8,128)(2,1)S(1)}, bf16[4,64,768]{2,1,0:T(8,128)(2,1)S(1)}, u32[]{:S(2)}, u32[]{:S(2)}) collective-permute-start(bf16[4,64,768]{2,1,0:T(8,128)(2,1)S(1)} %get-tuple-element.132), channel_id=1, source_target_pairs={{0,1},{1,0},{2,3},{3,2},{4,5},{5,4},{6,7},{7,6},{8,24},{9,25},{10,... | collective-permute-start | bytes 1179656 | tf_op jit(solution)/shard_map/ppermute | solution.py:164
  57.2 3.6 %shard_map.32.refs_6_ = f32[2,2,256,256]{3,2,1,0:T(8,128)S(1)} custom-call(s32[7]{0:T(128)S(1)} %stack.44.place_ref, f32[8,2,128]{2,1,0:T(2,128)S(1)} %maximum_bitcast_fusion.weights_ref, bf16[4,64,768]{2,1,0:T(8,128)(2,1)S(1)} %collective-permute-done.2.refs_2_.refs_1_.refs_0_, bf16[4,64,768]{2,1,0:T(8,128)(2,1)S(1)} %collective-permute-done.refs_1_.refs_2_, ...), custom_call_target="tpu_custom_call" | custom-call | flops 2013265920 | bytes 6029312 | tf_op jit(solution)/shard_map/pallas_call | solution.py:213
  60.9 0.0 collective-permute-done.16.refs_5_
  60.9 2.8 %shard_map.33.refs_4_ = f32[2,2,256,256]{3,2,1,0:T(8,128)S(1)} custom-call(s32[7]{0:T(128)S(1)} %stack.44.place_ref, f32[8,2,128]{2,1,0:T(2,128)S(1)} %maximum_bitcast_fusion.weights_ref, bf16[4,64,768]{2,1,0:T(8,128)(2,1)S(1)} %collective-permute-done.2.refs_2_.refs_1_.refs_0_, bf16[4,64,768]{2,1,0:T(8,128)(2,1)S(1)} %collective-permute-done.3.refs_1_.refs_3_.refs_2_, ...), custom_call_target="tpu_custom_call" | custom-call | flops 1409286144 | bytes 4849664 | tf_op jit(solution)/shard_map/pallas_call | solution.py:213
  63.6 1.4 %collective-permute-done.13.refs_1_ = bf16[4,64,768]{2,1,0:T(8,128)(2,1)S(1)} collective-permute-done((bf16[4,64,768]{2,1,0:T(8,128)(2,1)S(1)}, bf16[4,64,768]{2,1,0:T(8,128)(2,1)S(1)}, u32[]{:S(2)}, u32[]{:S(2)}) %collective-permute-start.13) | collective-permute-done | bytes 393248 | tf_op jit(solution)/shard_map/ppermute | solution.py:164
  65.0 1.2 %collective-permute-done.14.refs_2_.refs_1_ = bf16[4,64,768]{2,1,0:T(8,128)(2,1)S(1)} collective-permute-done((bf16[4,64,768]{2,1,0:T(8,128)(2,1)S(1)}, bf16[4,64,768]{2,1,0:T(8,128)(2,1)S(1)}, u32[]{:S(2)}, u32[]{:S(2)}) %collective-permute-start.14) | collective-permute-done | bytes 393248 | tf_op jit(solution)/shard_map/ppermute | solution.py:164
  66.3 0.0 collective-permute-done.15.refs_3_.refs_2_
  66.3 0.0 collective-permute-start.17
  66.3 0.5 collective-permute-start.18
  66.8 0.0 collective-permute-start.19
  66.8 1.5 %shard_map.34.refs_6_ = f32[2,2,256,256]{3,2,1,0:T(8,128)S(1)} custom-call(s32[7]{0:T(128)S(1)} %stack.44.place_ref, f32[8,2,128]{2,1,0:T(2,128)S(1)} %maximum_bitcast_fusion.weights_ref, bf16[2,4,64,768]{3,2,1,0:T(8,128)(2,1)S(1)} %collective-permute-done.8.z1_ref.refs_4_.refs_2_.refs_0_, bf16[4,64,768]{2,1,0:T(8,128)(2,1)S(1)} %collective-permute-done.13.refs_1_, ...), custom_call_target="tpu_custom_call" | custom-call | flops 603979776 | bytes 3276800 | tf_op jit(solution)/shard_map/pallas_call | solution.py:213
  68.3 0.0 collective-permute-done.17.refs_3_
  68.3 0.2 collective-permute-done.18.refs_4_
  68.6 0.6 collective-permute-done.19.refs_5_
  69.1 2.9 %shard_map.35 = f32[16,64,256]{2,1,0:T(8,128)} custom-call(s32[7]{0:T(128)S(1)} %stack.44.place_ref, f32[8,2,128]{2,1,0:T(2,128)S(1)} %maximum_bitcast_fusion.weights_ref, bf16[2,4,64,768]{3,2,1,0:T(8,128)(2,1)S(1)} %collective-permute-done.8.z1_ref.refs_4_.refs_2_.refs_0_, bf16[4,64,768]{2,1,0:T(8,128)(2,1)S(1)} %collective-permute-done.14.refs_2_.refs_1_, ...), custom_call_target="tpu_custom_call" | custom-call | flops 603979776 | bytes 3276800 | tf_op jit(solution)/shard_map/pallas_call | solution.py:213
  (5 shorter events, 0.1 us)
Async XLA Ops:
  0.0 10.4 %copy-start = (s32[4,3]{1,0:T(4,128)S(1)}, s32[4,3]{1,0:T(4,128)}, u32[]{:S(2)}) copy-start(s32[4,3]{1,0:T(4,128)} %param.3) | copy-start | bytes 148
  1.7 12.4 %collective-permute-start = (bf16[4,64,768]{2,1,0:T(8,128)(2,1)S(1)}, bf16[4,64,768]{2,1,0:T(8,128)(2,1)S(1)}, u32[]{:S(2)}, u32[]{:S(2)}) collective-permute-start(bf16[4,64,768]{2,1,0:T(8,128)(2,1)S(1)} %reshape.222.refs_0_), channel_id=1, source_target_pairs={{0,16},{1,17},{2,18},{3,19},{4,20},{5,21},{6,22},{7,23},{8,9},{9,8... | collective-permute-start | bytes 1179656 | tf_op jit(solution)/shard_map/ppermute | solution.py:164
  4.7 9.4 %collective-permute-start.1 = (bf16[4,64,768]{2,1,0:T(8,128)(2,1)S(1)}, bf16[4,64,768]{2,1,0:T(8,128)(2,1)S(1)}, u32[]{:S(2)}, u32[]{:S(2)}) collective-permute-start(bf16[4,64,768]{2,1,0:T(8,128)(2,1)S(1)} %reshape.222.refs_0_), channel_id=1, source_target_pairs={{0,1},{1,0},{2,3},{3,2},{4,5},{5,4},{6,7},{7,6},{8,24},{9,25},{10,... | collective-permute-start | bytes 1179656 | tf_op jit(solution)/shard_map/ppermute | solution.py:164
  6.2 19.7 %collective-permute-start.2 = (bf16[4,64,768]{2,1,0:T(8,128)(2,1)S(1)}, bf16[4,64,768]{2,1,0:T(8,128)(2,1)S(1)}, u32[]{:S(2)}, u32[]{:S(2)}) collective-permute-start(bf16[4,64,768]{2,1,0:T(8,128)(2,1)S(1)} %reshape.222.refs_0_), channel_id=1, source_target_pairs={{0,4},{1,5},{2,6},{3,7},{4,0},{5,1},{6,2},{7,3},{8,12},{9,13},{10,... | collective-permute-start | bytes 1179656 | tf_op jit(solution)/shard_map/ppermute | solution.py:164
  8.8 17.3 %collective-permute-start.3 = (bf16[4,64,768]{2,1,0:T(8,128)(2,1)S(1)}, bf16[4,64,768]{2,1,0:T(8,128)(2,1)S(1)}, u32[]{:S(2)}, u32[]{:S(2)}) collective-permute-start(bf16[4,64,768]{2,1,0:T(8,128)(2,1)S(1)} %reshape.222.refs_0_), channel_id=1, source_target_pairs={{0,2},{1,3},{2,0},{3,1},{4,6},{5,7},{6,4},{7,5},{8,10},{9,11},{10,... | collective-permute-start | bytes 1179656 | tf_op jit(solution)/shard_map/ppermute | solution.py:164
  15.7 10.5 %collective-permute-start.4 = (bf16[4,64,768]{2,1,0:T(8,128)(2,1)S(1)}, bf16[4,64,768]{2,1,0:T(8,128)(2,1)S(1)}, u32[]{:S(2)}, u32[]{:S(2)}) collective-permute-start(bf16[4,64,768]{2,1,0:T(8,128)(2,1)S(1)} %collective-permute-done.refs_1_.refs_2_), channel_id=1, source_target_pairs={{0,1},{1,0},{2,3},{3,2},{4,5},{5,4},{6,7},{7,6},{8,24},{9,25},{10,... | collective-permute-start | bytes 1179656 | tf_op jit(solution)/shard_map/ppermute | solution.py:164
  17.3 8.8 %collective-permute-start.6 = (bf16[4,64,768]{2,1,0:T(8,128)(2,1)S(1)}, bf16[4,64,768]{2,1,0:T(8,128)(2,1)S(1)}, u32[]{:S(2)}, u32[]{:S(2)}) collective-permute-start(bf16[4,64,768]{2,1,0:T(8,128)(2,1)S(1)} %collective-permute-done.refs_1_.refs_2_), channel_id=1, source_target_pairs={{0,8},{1,9},{2,10},{3,11},{4,12},{5,13},{6,14},{7,15},{8,0},{9,1},... | collective-permute-start | bytes 1179656 | tf_op jit(solution)/shard_map/ppermute | solution.py:164
  18.2 8.0 %collective-permute-start.5 = (bf16[4,64,768]{2,1,0:T(8,128)(2,1)S(1)}, bf16[4,64,768]{2,1,0:T(8,128)(2,1)S(1)}, u32[]{:S(2)}, u32[]{:S(2)}) collective-permute-start(bf16[4,64,768]{2,1,0:T(8,128)(2,1)S(1)} %reshape.222.refs_0_), channel_id=1, source_target_pairs={{0,8},{1,9},{2,10},{3,11},{4,12},{5,13},{6,14},{7,15},{8,0},{9,1},... | collective-permute-start | bytes 1179656 | tf_op jit(solution)/shard_map/ppermute | solution.py:164
  25.9 1.7 %collective-permute-start.7 = (bf16[4,64,768]{2,1,0:T(8,128)(2,1)S(1)}, bf16[4,64,768]{2,1,0:T(8,128)(2,1)S(1)}, u32[]{:S(2)}, u32[]{:S(2)}) collective-permute-start(bf16[4,64,768]{2,1,0:T(8,128)(2,1)S(1)} %collective-permute-done.1.refs_2_.refs_4_.refs_3_), channel_id=1, source_target_pairs={{0,8},{1,9},{2,10},{3,11},{4,12},{5,13},{6,14},{7,15},{8,0},{9,1},... | collective-permute-start | bytes 1179656 | tf_op jit(solution)/shard_map/ppermute | solution.py:164
  28.4 24.8 %collective-permute-start.12 = (bf16[3,4,64,768]{3,2,1,0:T(8,128)(2,1)S(1)}, bf16[3,4,64,768]{3,2,1,0:T(8,128)(2,1)S(1)}, u32[]{:S(2)}, u32[]{:S(2)}) collective-permute-start(bf16[3,4,64,768]{3,2,1,0:T(8,128)(2,1)S(1)} %get-tuple-element.110), channel_id=1, source_target_pairs={{0,8},{1,9},{2,10},{3,11},{4,12},{5,13},{6,14},{7,15},{8,0},{9,1},... | collective-permute-start | bytes 3538952 | tf_op jit(solution)/shard_map/ppermute | solution.py:164
  28.6 24.6 %collective-permute-start.10 = (bf16[2,4,64,768]{3,2,1,0:T(8,128)(2,1)S(1)}, bf16[2,4,64,768]{3,2,1,0:T(8,128)(2,1)S(1)}, u32[]{:S(2)}, u32[]{:S(2)}) collective-permute-start(bf16[2,4,64,768]{3,2,1,0:T(8,128)(2,1)S(1)} %get-tuple-element.108), channel_id=1, source_target_pairs={{0,1},{1,0},{2,3},{3,2},{4,5},{5,4},{6,7},{7,6},{8,24},{9,25},{10,... | collective-permute-start | bytes 2359304 | tf_op jit(solution)/shard_map/ppermute | solution.py:164
  29.1 24.1 %collective-permute-start.8 = (bf16[2,4,64,768]{3,2,1,0:T(8,128)(2,1)S(1)}, bf16[2,4,64,768]{3,2,1,0:T(8,128)(2,1)S(1)}, u32[]{:S(2)}, u32[]{:S(2)}) collective-permute-start(bf16[2,4,64,768]{3,2,1,0:T(8,128)(2,1)S(1)} %get-tuple-element.107), channel_id=1, source_target_pairs={{0,2},{1,3},{2,0},{3,1},{4,6},{5,7},{6,4},{7,5},{8,10},{9,11},{10,... | collective-permute-start | bytes 2359304 | tf_op jit(solution)/shard_map/ppermute | solution.py:164
  29.7 23.5 %collective-permute-start.9 = (bf16[2,4,64,768]{3,2,1,0:T(8,128)(2,1)S(1)}, bf16[2,4,64,768]{3,2,1,0:T(8,128)(2,1)S(1)}, u32[]{:S(2)}, u32[]{:S(2)}) collective-permute-start(bf16[2,4,64,768]{3,2,1,0:T(8,128)(2,1)S(1)} %get-tuple-element.108), channel_id=1, source_target_pairs={{0,16},{1,17},{2,18},{3,19},{4,20},{5,21},{6,22},{7,23},{8,9},{9,8... | collective-permute-start | bytes 2359304 | tf_op jit(solution)/shard_map/ppermute | solution.py:164
  30.2 22.5 %collective-permute-start.11 = (bf16[4,64,768]{2,1,0:T(8,128)(2,1)S(1)}, bf16[4,64,768]{2,1,0:T(8,128)(2,1)S(1)}, u32[]{:S(2)}, u32[]{:S(2)}) collective-permute-start(bf16[4,64,768]{2,1,0:T(8,128)(2,1)S(1)} %get-tuple-element.109), channel_id=1, source_target_pairs={{0,17},{1,16},{2,19},{3,18},{4,21},{5,20},{6,23},{7,22},{8,12},{9,... | collective-permute-start | bytes 1179656 | tf_op jit(solution)/shard_map/ppermute | solution.py:164
  53.4 7.4 %collective-permute-start.16 = (bf16[7,4,64,768]{3,2,1,0:T(8,128)(2,1)S(1)}, bf16[7,4,64,768]{3,2,1,0:T(8,128)(2,1)S(1)}, u32[]{:S(2)}, u32[]{:S(2)}) collective-permute-start(bf16[7,4,64,768]{3,2,1,0:T(8,128)(2,1)S(1)} %get-tuple-element.133), channel_id=1, source_target_pairs={{0,8},{1,9},{2,10},{3,11},{4,12},{5,13},{6,14},{7,15},{8,0},{9,1},... | collective-permute-start | bytes 8257544 | tf_op jit(solution)/shard_map/ppermute | solution.py:164
  53.5 11.5 %collective-permute-start.13 = (bf16[4,64,768]{2,1,0:T(8,128)(2,1)S(1)}, bf16[4,64,768]{2,1,0:T(8,128)(2,1)S(1)}, u32[]{:S(2)}, u32[]{:S(2)}) collective-permute-start(bf16[4,64,768]{2,1,0:T(8,128)(2,1)S(1)} %collective-permute-done.11.ab2_ref.refs_7_), channel_id=1, source_target_pairs={{0,2},{1,3},{2,0},{3,1},{4,6},{5,7},{6,4},{7,5},{8,10},{9,11},{10,... | collective-permute-start | bytes 1179656 | tf_op jit(solution)/shard_map/ppermute | solution.py:164
  55.2 11.0 %collective-permute-start.14 = (bf16[4,64,768]{2,1,0:T(8,128)(2,1)S(1)}, bf16[4,64,768]{2,1,0:T(8,128)(2,1)S(1)}, u32[]{:S(2)}, u32[]{:S(2)}) collective-permute-start(bf16[4,64,768]{2,1,0:T(8,128)(2,1)S(1)} %get-tuple-element.132), channel_id=1, source_target_pairs={{0,16},{1,17},{2,18},{3,19},{4,20},{5,21},{6,22},{7,23},{8,9},{9,8... | collective-permute-start | bytes 1179656 | tf_op jit(solution)/shard_map/ppermute | solution.py:164
  56.3 9.9 %collective-permute-start.15 = (bf16[4,64,768]{2,1,0:T(8,128)(2,1)S(1)}, bf16[4,64,768]{2,1,0:T(8,128)(2,1)S(1)}, u32[]{:S(2)}, u32[]{:S(2)}) collective-permute-start(bf16[4,64,768]{2,1,0:T(8,128)(2,1)S(1)} %get-tuple-element.132), channel_id=1, source_target_pairs={{0,1},{1,0},{2,3},{3,2},{4,5},{5,4},{6,7},{7,6},{8,24},{9,25},{10,... | collective-permute-start | bytes 1179656 | tf_op jit(solution)/shard_map/ppermute | solution.py:164
  66.3 2.0 %collective-permute-start.17 = (bf16[4,64,768]{2,1,0:T(8,128)(2,1)S(1)}, bf16[4,64,768]{2,1,0:T(8,128)(2,1)S(1)}, u32[]{:S(2)}, u32[]{:S(2)}) collective-permute-start(bf16[4,64,768]{2,1,0:T(8,128)(2,1)S(1)} %collective-permute-done.13.refs_1_), channel_id=1, source_target_pairs={{0,8},{1,9},{2,10},{3,11},{4,12},{5,13},{6,14},{7,15},{8,0},{9,1},... | collective-permute-start | bytes 1179656 | tf_op jit(solution)/shard_map/ppermute | solution.py:164
  66.3 2.3 %collective-permute-start.18 = (bf16[4,64,768]{2,1,0:T(8,128)(2,1)S(1)}, bf16[4,64,768]{2,1,0:T(8,128)(2,1)S(1)}, u32[]{:S(2)}, u32[]{:S(2)}) collective-permute-start(bf16[4,64,768]{2,1,0:T(8,128)(2,1)S(1)} %collective-permute-done.14.refs_2_.refs_1_), channel_id=1, source_target_pairs={{0,8},{1,9},{2,10},{3,11},{4,12},{5,13},{6,14},{7,15},{8,0},{9,1},... | collective-permute-start | bytes 1179656 | tf_op jit(solution)/shard_map/ppermute | solution.py:164
  66.8 2.3 %collective-permute-start.19 = (bf16[4,64,768]{2,1,0:T(8,128)(2,1)S(1)}, bf16[4,64,768]{2,1,0:T(8,128)(2,1)S(1)}, u32[]{:S(2)}, u32[]{:S(2)}) collective-permute-start(bf16[4,64,768]{2,1,0:T(8,128)(2,1)S(1)} %collective-permute-done.15.refs_3_.refs_2_), channel_id=1, source_target_pairs={{0,8},{1,9},{2,10},{3,11},{4,12},{5,13},{6,14},{7,15},{8,0},{9,1},... | collective-permute-start | bytes 1179656 | tf_op jit(solution)/shard_map/ppermute | solution.py:164

commit v7 on v5

--- a/solution.py
+++ b/solution.py
@@ -52,10 +52,11 @@
 
 def add_shards(names, where, has_totals, last, place_ref, weights_ref, *refs):
     refs = list(refs)
-    scratch_ref = refs.pop() if last else None
-    left_ref, out_ref = refs.pop(), refs.pop()
-    totals_in = refs.pop() if has_totals else None
-    totals_ref = scratch_ref if last else out_ref
+    if last:
+        far_ref, out_ref, totals_in, left_ref = (refs.pop() for _ in range(4))
+    else:
+        left_ref, out_ref = refs.pop(), refs.pop()
+        totals_in = refs.pop() if has_totals else None
 
     def shard(name):
         index, slot = where[name]
@@ -65,26 +66,28 @@
     columns, per_block, _ = shard(names[0]).shape
     spins = left_ref.shape[2] // (2 * per_block)
 
-    if has_totals:
-        totals_ref[...] = totals_in[...]
+    slots = left_slots(names)
+    if last:
+        far_ref[...] = totals_in[1]
     else:
-        totals_ref[...] = jnp.zeros_like(totals_ref)
-
-    slots = left_slots(names)
-    for slot, (dy, dz) in enumerate(slots):
-        site = jnp.bitwise_xor(level, dz) * flat + jnp.bitwise_xor(beside, dy)
-        if dy == 0:
-            owns = [shard(("near", "O", dz))[first_s + s] for s in range(spins)]
+        if has_totals:
+            out_ref[...] = totals_in[...]
         else:
-            owns = [
-                jnp.where(
-                    core == 0,
-                    shard(("near", "B", dz))[first_s + s],
-                    shard(("near", "A", dz))[first_s + s],
-                )
-                for s in range(spins)
-            ]
-        left_ref[slot, 0], left_ref[slot, 1] = left_sides(owns, weights_ref[site])
+            out_ref[...] = jnp.zeros_like(out_ref)
+        for slot, (dy, dz) in enumerate(slots):
+            site = jnp.bitwise_xor(level, dz) * flat + jnp.bitwise_xor(beside, dy)
+            if dy == 0:
+                owns = [shard(("near", "O", dz))[first_s + s] for s in range(spins)]
+            else:
+                owns = [
+                    jnp.where(
+                        core == 0,
+                        shard(("near", "B", dz))[first_s + s],
+                        shard(("near", "A", dz))[first_s + s],
+                    )
+                    for s in range(spins)
+                ]
+            left_ref[slot, 0], left_ref[slot, 1] = left_sides(owns, weights_ref[site])
 
     for side, kind, dz in names:
         right = shard((side, kind, dz))[...].reshape(columns * per_block, -1)
@@ -94,33 +97,37 @@
             slot = slots.index((dy, dz))
         else:
             slot = slots.index((0, dz)) + dy
-        totals_ref[0 if side == "near" else 1, dx] += product(
-            left_ref[slot, 0], left_ref[slot, 1], right
-        )
+        term = product(left_ref[slot, 0], left_ref[slot, 1], right)
+        if last:
+            far_ref[dx] += term
+        else:
+            out_ref[0 if side == "near" else 1, dx] += term
 
     if last:
+        lane = lax.broadcasted_iota(jnp.int32, (per_block, 2 * per_block), 1)
         for part in range(2):
             for spin in range(spins):
                 top = (part * spins + spin) * per_block
-                for column in range(columns):
-                    across = pl.ds(column * per_block, per_block)
-                    pieces = [
-                        totals_ref[
-                            jnp.bitwise_xor(core, c),
-                            jnp.bitwise_xor(pair, p),
-                            pl.ds(top, per_block),
-                            across,
-                        ]
-                        for p in range(2)
-                        for c in range(2)
-                    ]
-                    row = (spin * columns + column) * 2 + part
-                    out_ref[row] = jnp.concatenate(pieces, 1)
+                for column in range(0, columns, 2):
+                    across = pl.ds(column * per_block, 2 * per_block)
+                    for p in range(2):
+                        dx = jnp.bitwise_xor(pair, p)
+                        near = totals_in[0, dx, pl.ds(top, per_block), across]
+                        far = far_ref[dx, pl.ds(top, per_block), across]
+                        even = jnp.where(core == 0, near, far)
+                        odd = jnp.where(core == 0, far, near)
+                        row = (spin * columns + column) * 2 + part
+                        place = pl.ds(p * 2 * per_block, 2 * per_block)
+                        out_ref[row, :, place] = jnp.where(
+                            lane < per_block, even, pltpu.roll(odd, per_block, 1)
+                        )
+                        out_ref[row + 2, :, place] = jnp.where(
+                            lane < per_block, pltpu.roll(even, per_block, 1), odd
+                        )
 
 
 def route_second(place_ref, *refs):
-    stack_ref, both_ref, relayed_ref, mixed_ref = refs[6:]
-    ab0_ref, o1_ref, o2_ref = refs[3:6]
+    ab0_ref, o1_ref, o2_ref, stack_ref, both_ref, relayed_ref, mixed_ref = refs[3:]
     for slot in range(6):
         stack_ref[slot] = refs[slot][...]
     both_ref[0] = o1_ref[...]
@@ -196,27 +203,32 @@
         key, slot = where[("near", kind, dz)]
         return arrays[key] if slot is None else arrays[key][slot]
 
-    def add(names, totals, last=False):
+    def add(names, totals, keep=False, left=None):
+        last = left is not None
         slots = left_slots(names)
         uses = list(names)
-        for dy, dz in slots:
+        for dy, dz in [] if last else slots:
             uses += [("near", kind, dz) for kind in (("A", "B") if dy else ("O",))]
         keys = sorted({where[name][0] for name in uses})
         places = {name: (keys.index(where[name][0]), where[name][1]) for name in uses}
         operands = [place, weights] + [arrays[key] for key in keys]
-        if totals is not None:
-            operands.append(totals)
+        operands += [each for each in (left, totals) if each is not None]
         total_shape = (2, 2, tall, wide)
-        out = (share, per_block, 4 * per_block) if last else total_shape
-        scratch = [pltpu.VMEM((len(slots), 2, tall, depth), jnp.bfloat16)]
+        left_shape = (len(slots), 2, tall, depth)
+        block = pl.BlockSpec(memory_space=pltpu.VMEM)
+        out_shape = [jax.ShapeDtypeStruct(total_shape, jnp.float32)]
+        scratch = [pltpu.VMEM(left_shape, jnp.bfloat16)]
         if last:
-            scratch.append(pltpu.VMEM(total_shape, jnp.float32))
-        return pl.pallas_call(
+            out_shape = [jax.ShapeDtypeStruct((share, per_block, 4 * per_block), jnp.float32)]
+            scratch = [pltpu.VMEM(total_shape[1:], jnp.float32)]
+        if keep:
+            out_shape.append(jax.ShapeDtypeStruct(left_shape, jnp.bfloat16))
+            scratch = []
+        out = pl.pallas_call(
             functools.partial(add_shards, tuple(names), places, totals is not None, last),
-            in_specs=[pl.BlockSpec(memory_space=pltpu.SMEM)]
-            + [pl.BlockSpec(memory_space=pltpu.VMEM)] * (len(operands) - 1),
-            out_specs=pl.BlockSpec(memory_space=pltpu.VMEM),
-            out_shape=jax.ShapeDtypeStruct(out, jnp.float32),
+            in_specs=[pl.BlockSpec(memory_space=pltpu.SMEM)] + [block] * (len(operands) - 1),
+            out_specs=[block] * len(out_shape),
+            out_shape=out_shape,
             scratch_shapes=scratch,
             compiler_params=pltpu.CompilerParams(vmem_limit_bytes=40 * 1024 * 1024),
             cost_estimate=pl.CostEstimate(
@@ -225,18 +237,20 @@
                 transcendentals=0,
             ),
         )(*operands)
+        return out if keep else out[0]
 
     def fence(totals):
         nonlocal arrays
         arrays, totals = lax.optimization_barrier((arrays, totals))
         return totals
 
-    put("0", packed, "near", [("O", 0)])
-
-    first = [("O", 2), ("A", 0), ("O", 1), ("AB", 0), ("B", 0)]
-    new = [hop_z(packed, 2), hop_a(packed), hop_z(packed, 1), hop_ab(packed), hop_b(packed)]
-    for order, (kind, array) in enumerate(zip(first, new)):
-        put("1" + "abcde"[order], array, "near", [kind])
+    put("9", packed, "near", [("O", 0)])
+
+    put("1a", hop_z(packed, 2), "near", [("O", 2)])
+    put("1b", hop_z(packed, 1), "near", [("O", 1)])
+    put("1c", hop_b(packed), "near", [("B", 0)])
+    put("1d", hop_a(packed), "near", [("A", 0)])
+    put("1e", hop_b(near("A", 0)), "near", [("AB", 0)])
     place, weights = fence((place, weights))
 
     def route(kernel, operands, counts):
@@ -258,14 +272,14 @@
     )
     second = [("AB", 1), ("O", 3), ("A", 1), ("A", 2), ("B", 1), ("B", 2), ("AB", 2)]
     totals = add([("near", *kind) for kind in first], None)
-    put("2a", hop_a(both), "near", second[2:4])
-    put("2b", hop_z(relayed, 1), "near", second[0:2])
+    put("2a", hop_z(relayed, 1), "near", second[0:2])
+    put("2b", hop_a(both), "near", second[2:4])
     put("2c", hop_b(both), "near", second[4:6])
     put("2d", hop_mixed(mixed), "near", second[6:7])
     put("2e", swap(stack), "far", first)
     totals = fence(totals)
 
-    arrived = [arrays[key] for key in ("2b", "2a", "2c", "2d")]
+    arrived = [arrays[key] for key in ("2a", "2b", "2c", "2d")]
     stack, start = route(route_third, arrived, (7, 1))
     third = [("AB", 3), ("A", 3), ("B", 3)]
     new = [hop_z(near("AB", 2), 1), hop_a(start), hop_b(start)]
@@ -277,11 +291,11 @@
     totals = fence(totals)
 
     new = [swap(near(*kind)) for kind in third]
-    totals = add([("near", *kind) for kind in third], totals)
+    totals, left = add([("near", *kind) for kind in third], totals, keep=True)
     for order, (kind, array) in enumerate(zip(third, new)):
         put("4" + "abc"[order], array, "far", [kind])
-    totals = fence(totals)
-    return add([("far", *kind) for kind in third], totals, last=True)
+    totals, left = fence((totals, left))
+    return add([("far", *kind) for kind in third], totals, left=left)
 
 
 def add_terms(place_ref, weights_ref, left_ref, right_ref, field_ref):

time: 72.4 us -> 70.4 us (0.972)
  waiting for transfers between devices: 34.5 us -> 32.4 us
    ppermute x17, waiting for transfers between devices: 34.5 us -> 32.4 us  [move(): return lax.ppermute(array, AXES, pairs)]
  transfers between devices with their start and end apart: 17 -> 17, of which waited for: 7 -> 7; matrix products, arithmetic and copies ran while one was open for 1% -> 1% of each run, Pallas kernels for 15% -> 16%
where the time goes in v7:
time: 70.4 us; the launch traced here: 70.2 us
  waiting for transfers between devices  32.4 us (46%)
  starting transfers between devices  20.9 us (30%)
  Pallas kernels  14.8 us (21%)
  local copies, waits for them, and re-layouts  1.78 us (3%)
    ppermute x17, waiting for transfers between devices, move(): return lax.ppermute(array, AXES, pairs)  32.4 us
    ppermute x17, starting transfers between devices, move(): return lax.ppermute(array, AXES, pairs)  20.9 us
    pallas_call x5, Pallas kernels, add(): pl.pallas_call(functools.partial(add_shards, tuple(names), places, totals...  13.7 us
  transfers between devices with their start and end apart: 17, of which 7 were waited for; matrix products, arithmetic and copies ran while one was open for 1% of the time, Pallas kernels for 16%

profile of v7, /device:TPU:0, one launch (start us, length us, event | category | flops | bytes accessed | tf_op | source)
XLA Modules:
  0.0 70.2 jit_solution(8017985726544532479)
XLA Ops:
  0.0 0.0 copy-start
  0.0 1.3 %copy.9 = bf16[2,64,4,3,128]{4,3,0,1,2:T(4,128)(2,1)S(1)} copy(bf16[2,64,4,3,128]{4,1,3,2,0:T(8,128)(2,1)} %bitcast.32) | data formatting | bytes 786432 | tf_op jit(solution)/shard_map/reshape | solution.py:368
  1.4 0.3 reshape.222.refs_0_.refs_5_.refs_9_
  1.7 3.0 %collective-permute-start.3 = (bf16[4,64,768]{2,1,0:T(8,128)(2,1)S(1)}, bf16[4,64,768]{2,1,0:T(8,128)(2,1)S(1)}, u32[]{:S(2)}, u32[]{:S(2)}) collective-permute-start(bf16[4,64,768]{2,1,0:T(8,128)(2,1)S(1)} %reshape.222.refs_0_.refs_5_.refs_9_), channel_id=1, source_target_pairs={{0,16},{1,17},{2,18},{3,19},{4,20},{5,21},{6,22},{7,23},{8,9},{9,8... | collective-permute-start | bytes 1179656 | tf_op jit(solution)/shard_map/ppermute | solution.py:172
  4.7 2.6 %collective-permute-start = (bf16[4,64,768]{2,1,0:T(8,128)(2,1)S(1)}, bf16[4,64,768]{2,1,0:T(8,128)(2,1)S(1)}, u32[]{:S(2)}, u32[]{:S(2)}) collective-permute-start(bf16[4,64,768]{2,1,0:T(8,128)(2,1)S(1)} %reshape.222.refs_0_.refs_5_.refs_9_), channel_id=1, source_target_pairs={{0,4},{1,5},{2,6},{3,7},{4,0},{5,1},{6,2},{7,3},{8,12},{9,13},{10,... | collective-permute-start | bytes 1179656 | tf_op jit(solution)/shard_map/ppermute | solution.py:172
  7.3 1.6 %collective-permute-start.1 = (bf16[4,64,768]{2,1,0:T(8,128)(2,1)S(1)}, bf16[4,64,768]{2,1,0:T(8,128)(2,1)S(1)}, u32[]{:S(2)}, u32[]{:S(2)}) collective-permute-start(bf16[4,64,768]{2,1,0:T(8,128)(2,1)S(1)} %reshape.222.refs_0_.refs_5_.refs_9_), channel_id=1, source_target_pairs={{0,2},{1,3},{2,0},{3,1},{4,6},{5,7},{6,4},{7,5},{8,10},{9,11},{10,... | collective-permute-start | bytes 1179656 | tf_op jit(solution)/shard_map/ppermute | solution.py:172
  8.9 1.5 %collective-permute-start.2 = (bf16[4,64,768]{2,1,0:T(8,128)(2,1)S(1)}, bf16[4,64,768]{2,1,0:T(8,128)(2,1)S(1)}, u32[]{:S(2)}, u32[]{:S(2)}) collective-permute-start(bf16[4,64,768]{2,1,0:T(8,128)(2,1)S(1)} %reshape.222.refs_0_.refs_5_.refs_9_), channel_id=1, source_target_pairs={{0,1},{1,0},{2,3},{3,2},{4,5},{5,4},{6,7},{7,6},{8,24},{9,25},{10,... | collective-permute-start | bytes 1179656 | tf_op jit(solution)/shard_map/ppermute | solution.py:172
  10.4 0.0 copy-done
  10.4 0.1 fusion
  10.5 0.0 collective-permute-done.3.refs_1_.refs_3_
  10.6 3.4 %collective-permute-start.4 = (bf16[4,64,768]{2,1,0:T(8,128)(2,1)S(1)}, bf16[4,64,768]{2,1,0:T(8,128)(2,1)S(1)}, u32[]{:S(2)}, u32[]{:S(2)}) collective-permute-start(bf16[4,64,768]{2,1,0:T(8,128)(2,1)S(1)} %collective-permute-done.3.refs_1_.refs_3_), channel_id=1, source_target_pairs={{0,1},{1,0},{2,3},{3,2},{4,5},{5,4},{6,7},{7,6},{8,24},{9,25},{10,... | collective-permute-start | bytes 1179656 | tf_op jit(solution)/shard_map/ppermute | solution.py:172
  14.0 0.1 stack.44.place_ref
  14.1 0.1 multiply_cosine_fusion
  14.2 10.5 %collective-permute-done.refs_5_.refs_0_ = bf16[4,64,768]{2,1,0:T(8,128)(2,1)S(1)} collective-permute-done((bf16[4,64,768]{2,1,0:T(8,128)(2,1)S(1)}, bf16[4,64,768]{2,1,0:T(8,128)(2,1)S(1)}, u32[]{:S(2)}, u32[]{:S(2)}) %collective-permute-start) | collective-permute-done | bytes 393248 | tf_op jit(solution)/shard_map/ppermute | solution.py:172
  24.7 0.2 collective-permute-done.1.refs_4_.refs_1_
  24.9 0.0 collective-permute-done.2.refs_2_
  24.9 0.0 collective-permute-done.4.refs_3_.refs_4_
  24.9 0.8 %shard_map.28 = (bf16[6,4,64,768]{3,2,1,0:T(8,128)(2,1)S(1)}, bf16[2,4,64,768]{3,2,1,0:T(8,128)(2,1)S(1)}, bf16[2,4,64,768]{3,2,1,0:T(8,128)(2,1)S(1)}, bf16[4,64,768]{2,1,0:T(8,128)(2,1)S(1)}) custom-call(s32[7]{0:T(128)S(1)} %stack.44.place_ref, bf16[4,64,768]{2,1,0:T(8,128)(2,1)S(1)} %reshape.222.refs_0_.refs_5_.refs_9_, ...), custom_call_target="tpu_custom_call" | custom-call | tf_op jit(solution)/shard_map/pallas_call | solution.py:260
  25.8 0.1 collective-permute-start.9
  25.8 1.5 %collective-permute-start.5 = (bf16[2,4,64,768]{3,2,1,0:T(8,128)(2,1)S(1)}, bf16[2,4,64,768]{3,2,1,0:T(8,128)(2,1)S(1)}, u32[]{:S(2)}, u32[]{:S(2)}) collective-permute-start(bf16[2,4,64,768]{3,2,1,0:T(8,128)(2,1)S(1)} %get-tuple-element.81), channel_id=1, source_target_pairs={{0,2},{1,3},{2,0},{3,1},{4,6},{5,7},{6,4},{7,5},{8,10},{9,11},{10,... | collective-permute-start | bytes 2359304 | tf_op jit(solution)/shard_map/ppermute | solution.py:172
  27.3 1.5 %collective-permute-start.6 = (bf16[2,4,64,768]{3,2,1,0:T(8,128)(2,1)S(1)}, bf16[2,4,64,768]{3,2,1,0:T(8,128)(2,1)S(1)}, u32[]{:S(2)}, u32[]{:S(2)}) collective-permute-start(bf16[2,4,64,768]{3,2,1,0:T(8,128)(2,1)S(1)} %get-tuple-element.82), channel_id=1, source_target_pairs={{0,16},{1,17},{2,18},{3,19},{4,20},{5,21},{6,22},{7,23},{8,9},{9,8... | collective-permute-start | bytes 2359304 | tf_op jit(solution)/shard_map/ppermute | solution.py:172
  28.9 0.5 collective-permute-start.7
  29.3 1.5 %collective-permute-start.8 = (bf16[4,64,768]{2,1,0:T(8,128)(2,1)S(1)}, bf16[4,64,768]{2,1,0:T(8,128)(2,1)S(1)}, u32[]{:S(2)}, u32[]{:S(2)}) collective-permute-start(bf16[4,64,768]{2,1,0:T(8,128)(2,1)S(1)} %get-tuple-element.83), channel_id=1, source_target_pairs={{0,17},{1,16},{2,19},{3,18},{4,21},{5,20},{6,23},{7,22},{8,12},{9,... | collective-permute-start | bytes 1179656 | tf_op jit(solution)/shard_map/ppermute | solution.py:172
  30.9 2.5 %shard_map.29.refs_10_ = f32[2,2,256,256]{3,2,1,0:T(8,128)S(1)} custom-call(s32[7]{0:T(128)S(1)} %stack.44.place_ref, f32[8,2,128]{2,1,0:T(2,128)S(1)} %maximum_bitcast_fusion.weights_ref, bf16[4,64,768]{2,1,0:T(8,128)(2,1)S(1)} %collective-permute-done.refs_5_.refs_0_, bf16[4,64,768]{2,1,0:T(8,128)(2,1)S(1)} %collective-permute-done.1.refs_4_.refs_1_, ...), custom_call_target="tpu_custom_call" | custom-call | flops 1207959552 | bytes 4456448 | tf_op jit(solution)/shard_map/pallas_call | solution.py:227
  33.3 18.6 %collective-permute-done.8.ab2_ref.refs_7_ = bf16[4,64,768]{2,1,0:T(8,128)(2,1)S(1)} collective-permute-done((bf16[4,64,768]{2,1,0:T(8,128)(2,1)S(1)}, bf16[4,64,768]{2,1,0:T(8,128)(2,1)S(1)}, u32[]{:S(2)}, u32[]{:S(2)}) %collective-permute-start.8) | collective-permute-done | bytes 393248 | tf_op jit(solution)/shard_map/ppermute | solution.py:172
  51.9 0.0 collective-permute-done.5.z1_ref.refs_4_.refs_2_.refs_0_
  51.9 0.0 collective-permute-done.6.a12_ref.refs_5_.refs_3_
  51.9 0.0 collective-permute-done.7.b12_ref.refs_6_.refs_4_
  51.9 0.0 collective-permute-done.9.refs_8_
  51.9 0.2 shard_map.30
  52.2 0.1 collective-permute-start.13
  52.2 0.6 collective-permute-start.10
  52.8 1.5 %collective-permute-start.11 = (bf16[4,64,768]{2,1,0:T(8,128)(2,1)S(1)}, bf16[4,64,768]{2,1,0:T(8,128)(2,1)S(1)}, u32[]{:S(2)}, u32[]{:S(2)}) collective-permute-start(bf16[4,64,768]{2,1,0:T(8,128)(2,1)S(1)} %get-tuple-element.107), channel_id=1, source_target_pairs={{0,16},{1,17},{2,18},{3,19},{4,20},{5,21},{6,22},{7,23},{8,9},{9,8... | collective-permute-start | bytes 1179656 | tf_op jit(solution)/shard_map/ppermute | solution.py:172
  54.4 0.9 %collective-permute-start.12 = (bf16[4,64,768]{2,1,0:T(8,128)(2,1)S(1)}, bf16[4,64,768]{2,1,0:T(8,128)(2,1)S(1)}, u32[]{:S(2)}, u32[]{:S(2)}) collective-permute-start(bf16[4,64,768]{2,1,0:T(8,128)(2,1)S(1)} %get-tuple-element.107), channel_id=1, source_target_pairs={{0,1},{1,0},{2,3},{3,2},{4,5},{5,4},{6,7},{7,6},{8,24},{9,25},{10,... | collective-permute-start | bytes 1179656 | tf_op jit(solution)/shard_map/ppermute | solution.py:172
  55.3 4.3 %shard_map.31.refs_6_ = f32[2,2,256,256]{3,2,1,0:T(8,128)S(1)} custom-call(s32[7]{0:T(128)S(1)} %stack.44.place_ref, f32[8,2,128]{2,1,0:T(2,128)S(1)} %maximum_bitcast_fusion.weights_ref, bf16[4,64,768]{2,1,0:T(8,128)(2,1)S(1)} %collective-permute-done.refs_5_.refs_0_, bf16[4,64,768]{2,1,0:T(8,128)(2,1)S(1)} %collective-permute-done.1.refs_4_.refs_1_, ...), custom_call_target="tpu_custom_call" | custom-call | flops 2617245696 | bytes 7208960 | tf_op jit(solution)/shard_map/pallas_call | solution.py:227
  59.6 0.0 collective-permute-done.13.refs_5_
  59.6 2.7 %shard_map.32.refs_4_ = f32[2,2,256,256]{3,2,1,0:T(8,128)S(1)} custom-call(s32[7]{0:T(128)S(1)} %stack.44.place_ref, f32[8,2,128]{2,1,0:T(2,128)S(1)} %maximum_bitcast_fusion.weights_ref, bf16[4,64,768]{2,1,0:T(8,128)(2,1)S(1)} %collective-permute-done.refs_5_.refs_0_, bf16[4,64,768]{2,1,0:T(8,128)(2,1)S(1)} %collective-permute-done.1.refs_4_.refs_1_, ...), custom_call_target="tpu_custom_call" | custom-call | flops 1409286144 | bytes 4849664 | tf_op jit(solution)/shard_map/pallas_call | solution.py:227
  62.4 1.4 %collective-permute-done.10.refs_1_ = bf16[4,64,768]{2,1,0:T(8,128)(2,1)S(1)} collective-permute-done((bf16[4,64,768]{2,1,0:T(8,128)(2,1)S(1)}, bf16[4,64,768]{2,1,0:T(8,128)(2,1)S(1)}, u32[]{:S(2)}, u32[]{:S(2)}) %collective-permute-start.10) | collective-permute-done | bytes 393248 | tf_op jit(solution)/shard_map/ppermute | solution.py:172
  63.8 0.9 %collective-permute-done.11.refs_2_ = bf16[4,64,768]{2,1,0:T(8,128)(2,1)S(1)} collective-permute-done((bf16[4,64,768]{2,1,0:T(8,128)(2,1)S(1)}, bf16[4,64,768]{2,1,0:T(8,128)(2,1)S(1)}, u32[]{:S(2)}, u32[]{:S(2)}) %collective-permute-start.11) | collective-permute-done | bytes 393248 | tf_op jit(solution)/shard_map/ppermute | solution.py:172
  64.7 0.0 collective-permute-done.12.refs_3_
  64.7 0.0 collective-permute-start.14
  64.7 0.5 collective-permute-start.15
  65.2 0.0 collective-permute-start.16
  65.2 1.5 %shard_map.33 = (f32[2,2,256,256]{3,2,1,0:T(8,128)S(1)}, bf16[2,2,256,768]{3,2,1,0:T(8,128)(2,1)S(1)}) custom-call(s32[7]{0:T(128)S(1)} %stack.44.place_ref, f32[8,2,128]{2,1,0:T(2,128)S(1)} %maximum_bitcast_fusion.weights_ref, bf16[2,4,64,768]{3,2,1,0:T(8,128)(2,1)S(1)} %collective-permute-done.5.z1_ref.refs_4_.refs_2_.refs_0_, ...), custom_call_target="tpu_custom_call" | custom-call | flops 603979776 | bytes 3276800 | tf_op jit(solution)/shard_map/pallas_call | solution.py:227
  66.7 0.0 collective-permute-done.14.refs_0_
  66.7 0.2 collective-permute-done.15.refs_1_
  67.0 0.6 collective-permute-done.16.refs_2_
  67.5 2.7 %shard_map.34 = f32[16,64,256]{2,1,0:T(8,128)} custom-call(s32[7]{0:T(128)S(1)} %stack.44.place_ref, f32[8,2,128]{2,1,0:T(2,128)S(1)} %maximum_bitcast_fusion.weights_ref, bf16[4,64,768]{2,1,0:T(8,128)(2,1)S(1)} %collective-permute-done.14.refs_0_, bf16[4,64,768]{2,1,0:T(8,128)(2,1)S(1)} %collective-permute-done.15.refs_1_, ...), custom_call_target="tpu_custom_call" | custom-call | flops 603979776 | bytes 3276800 | tf_op jit(solution)/shard_map/pallas_call | solution.py:227
  (5 shorter events, 0.1 us)
Async XLA Ops:
  0.0 10.4 %copy-start = (s32[4,3]{1,0:T(4,128)S(1)}, s32[4,3]{1,0:T(4,128)}, u32[]{:S(2)}) copy-start(s32[4,3]{1,0:T(4,128)} %param.3) | copy-start | bytes 148
  1.7 8.8 %collective-permute-start.3 = (bf16[4,64,768]{2,1,0:T(8,128)(2,1)S(1)}, bf16[4,64,768]{2,1,0:T(8,128)(2,1)S(1)}, u32[]{:S(2)}, u32[]{:S(2)}) collective-permute-start(bf16[4,64,768]{2,1,0:T(8,128)(2,1)S(1)} %reshape.222.refs_0_.refs_5_.refs_9_), channel_id=1, source_target_pairs={{0,16},{1,17},{2,18},{3,19},{4,20},{5,21},{6,22},{7,23},{8,9},{9,8... | collective-permute-start | bytes 1179656 | tf_op jit(solution)/shard_map/ppermute | solution.py:172
  4.7 20.0 %collective-permute-start = (bf16[4,64,768]{2,1,0:T(8,128)(2,1)S(1)}, bf16[4,64,768]{2,1,0:T(8,128)(2,1)S(1)}, u32[]{:S(2)}, u32[]{:S(2)}) collective-permute-start(bf16[4,64,768]{2,1,0:T(8,128)(2,1)S(1)} %reshape.222.refs_0_.refs_5_.refs_9_), channel_id=1, source_target_pairs={{0,4},{1,5},{2,6},{3,7},{4,0},{5,1},{6,2},{7,3},{8,12},{9,13},{10,... | collective-permute-start | bytes 1179656 | tf_op jit(solution)/shard_map/ppermute | solution.py:172
  7.3 17.6 %collective-permute-start.1 = (bf16[4,64,768]{2,1,0:T(8,128)(2,1)S(1)}, bf16[4,64,768]{2,1,0:T(8,128)(2,1)S(1)}, u32[]{:S(2)}, u32[]{:S(2)}) collective-permute-start(bf16[4,64,768]{2,1,0:T(8,128)(2,1)S(1)} %reshape.222.refs_0_.refs_5_.refs_9_), channel_id=1, source_target_pairs={{0,2},{1,3},{2,0},{3,1},{4,6},{5,7},{6,4},{7,5},{8,10},{9,11},{10,... | collective-permute-start | bytes 1179656 | tf_op jit(solution)/shard_map/ppermute | solution.py:172
  8.9 16.1 %collective-permute-start.2 = (bf16[4,64,768]{2,1,0:T(8,128)(2,1)S(1)}, bf16[4,64,768]{2,1,0:T(8,128)(2,1)S(1)}, u32[]{:S(2)}, u32[]{:S(2)}) collective-permute-start(bf16[4,64,768]{2,1,0:T(8,128)(2,1)S(1)} %reshape.222.refs_0_.refs_5_.refs_9_), channel_id=1, source_target_pairs={{0,1},{1,0},{2,3},{3,2},{4,5},{5,4},{6,7},{7,6},{8,24},{9,25},{10,... | collective-permute-start | bytes 1179656 | tf_op jit(solution)/shard_map/ppermute | solution.py:172
  10.6 14.4 %collective-permute-start.4 = (bf16[4,64,768]{2,1,0:T(8,128)(2,1)S(1)}, bf16[4,64,768]{2,1,0:T(8,128)(2,1)S(1)}, u32[]{:S(2)}, u32[]{:S(2)}) collective-permute-start(bf16[4,64,768]{2,1,0:T(8,128)(2,1)S(1)} %collective-permute-done.3.refs_1_.refs_3_), channel_id=1, source_target_pairs={{0,1},{1,0},{2,3},{3,2},{4,5},{5,4},{6,7},{7,6},{8,24},{9,25},{10,... | collective-permute-start | bytes 1179656 | tf_op jit(solution)/shard_map/ppermute | solution.py:172
  25.8 26.2 %collective-permute-start.9 = (bf16[6,4,64,768]{3,2,1,0:T(8,128)(2,1)S(1)}, bf16[6,4,64,768]{3,2,1,0:T(8,128)(2,1)S(1)}, u32[]{:S(2)}, u32[]{:S(2)}) collective-permute-start(bf16[6,4,64,768]{3,2,1,0:T(8,128)(2,1)S(1)} %get-tuple-element.84), channel_id=1, source_target_pairs={{0,8},{1,9},{2,10},{3,11},{4,12},{5,13},{6,14},{7,15},{8,0},{9,1},... | collective-permute-start | bytes 7077896 | tf_op jit(solution)/shard_map/ppermute | solution.py:172
  25.8 26.1 %collective-permute-start.5 = (bf16[2,4,64,768]{3,2,1,0:T(8,128)(2,1)S(1)}, bf16[2,4,64,768]{3,2,1,0:T(8,128)(2,1)S(1)}, u32[]{:S(2)}, u32[]{:S(2)}) collective-permute-start(bf16[2,4,64,768]{3,2,1,0:T(8,128)(2,1)S(1)} %get-tuple-element.81), channel_id=1, source_target_pairs={{0,2},{1,3},{2,0},{3,1},{4,6},{5,7},{6,4},{7,5},{8,10},{9,11},{10,... | collective-permute-start | bytes 2359304 | tf_op jit(solution)/shard_map/ppermute | solution.py:172
  27.3 24.6 %collective-permute-start.6 = (bf16[2,4,64,768]{3,2,1,0:T(8,128)(2,1)S(1)}, bf16[2,4,64,768]{3,2,1,0:T(8,128)(2,1)S(1)}, u32[]{:S(2)}, u32[]{:S(2)}) collective-permute-start(bf16[2,4,64,768]{3,2,1,0:T(8,128)(2,1)S(1)} %get-tuple-element.82), channel_id=1, source_target_pairs={{0,16},{1,17},{2,18},{3,19},{4,20},{5,21},{6,22},{7,23},{8,9},{9,8... | collective-permute-start | bytes 2359304 | tf_op jit(solution)/shard_map/ppermute | solution.py:172
  28.9 23.1 %collective-permute-start.7 = (bf16[2,4,64,768]{3,2,1,0:T(8,128)(2,1)S(1)}, bf16[2,4,64,768]{3,2,1,0:T(8,128)(2,1)S(1)}, u32[]{:S(2)}, u32[]{:S(2)}) collective-permute-start(bf16[2,4,64,768]{3,2,1,0:T(8,128)(2,1)S(1)} %get-tuple-element.82), channel_id=1, source_target_pairs={{0,1},{1,0},{2,3},{3,2},{4,5},{5,4},{6,7},{7,6},{8,24},{9,25},{10,... | collective-permute-start | bytes 2359304 | tf_op jit(solution)/shard_map/ppermute | solution.py:172
  29.3 22.6 %collective-permute-start.8 = (bf16[4,64,768]{2,1,0:T(8,128)(2,1)S(1)}, bf16[4,64,768]{2,1,0:T(8,128)(2,1)S(1)}, u32[]{:S(2)}, u32[]{:S(2)}) collective-permute-start(bf16[4,64,768]{2,1,0:T(8,128)(2,1)S(1)} %get-tuple-element.83), channel_id=1, source_target_pairs={{0,17},{1,16},{2,19},{3,18},{4,21},{5,20},{6,23},{7,22},{8,12},{9,... | collective-permute-start | bytes 1179656 | tf_op jit(solution)/shard_map/ppermute | solution.py:172
  52.2 7.5 %collective-permute-start.13 = (bf16[7,4,64,768]{3,2,1,0:T(8,128)(2,1)S(1)}, bf16[7,4,64,768]{3,2,1,0:T(8,128)(2,1)S(1)}, u32[]{:S(2)}, u32[]{:S(2)}) collective-permute-start(bf16[7,4,64,768]{3,2,1,0:T(8,128)(2,1)S(1)} %get-tuple-element.108), channel_id=1, source_target_pairs={{0,8},{1,9},{2,10},{3,11},{4,12},{5,13},{6,14},{7,15},{8,0},{9,1},... | collective-permute-start | bytes 8257544 | tf_op jit(solution)/shard_map/ppermute | solution.py:172
  52.2 11.5 %collective-permute-start.10 = (bf16[4,64,768]{2,1,0:T(8,128)(2,1)S(1)}, bf16[4,64,768]{2,1,0:T(8,128)(2,1)S(1)}, u32[]{:S(2)}, u32[]{:S(2)}) collective-permute-start(bf16[4,64,768]{2,1,0:T(8,128)(2,1)S(1)} %collective-permute-done.8.ab2_ref.refs_7_), channel_id=1, source_target_pairs={{0,2},{1,3},{2,0},{3,1},{4,6},{5,7},{6,4},{7,5},{8,10},{9,11},{10,... | collective-permute-start | bytes 1179656 | tf_op jit(solution)/shard_map/ppermute | solution.py:172
  52.8 11.8 %collective-permute-start.11 = (bf16[4,64,768]{2,1,0:T(8,128)(2,1)S(1)}, bf16[4,64,768]{2,1,0:T(8,128)(2,1)S(1)}, u32[]{:S(2)}, u32[]{:S(2)}) collective-permute-start(bf16[4,64,768]{2,1,0:T(8,128)(2,1)S(1)} %get-tuple-element.107), channel_id=1, source_target_pairs={{0,16},{1,17},{2,18},{3,19},{4,20},{5,21},{6,22},{7,23},{8,9},{9,8... | collective-permute-start | bytes 1179656 | tf_op jit(solution)/shard_map/ppermute | solution.py:172
  54.4 10.3 %collective-permute-start.12 = (bf16[4,64,768]{2,1,0:T(8,128)(2,1)S(1)}, bf16[4,64,768]{2,1,0:T(8,128)(2,1)S(1)}, u32[]{:S(2)}, u32[]{:S(2)}) collective-permute-start(bf16[4,64,768]{2,1,0:T(8,128)(2,1)S(1)} %get-tuple-element.107), channel_id=1, source_target_pairs={{0,1},{1,0},{2,3},{3,2},{4,5},{5,4},{6,7},{7,6},{8,24},{9,25},{10,... | collective-permute-start | bytes 1179656 | tf_op jit(solution)/shard_map/ppermute | solution.py:172
  64.7 2.0 %collective-permute-start.14 = (bf16[4,64,768]{2,1,0:T(8,128)(2,1)S(1)}, bf16[4,64,768]{2,1,0:T(8,128)(2,1)S(1)}, u32[]{:S(2)}, u32[]{:S(2)}) collective-permute-start(bf16[4,64,768]{2,1,0:T(8,128)(2,1)S(1)} %collective-permute-done.10.refs_1_), channel_id=1, source_target_pairs={{0,8},{1,9},{2,10},{3,11},{4,12},{5,13},{6,14},{7,15},{8,0},{9,1},... | collective-permute-start | bytes 1179656 | tf_op jit(solution)/shard_map/ppermute | solution.py:172
  64.7 2.3 %collective-permute-start.15 = (bf16[4,64,768]{2,1,0:T(8,128)(2,1)S(1)}, bf16[4,64,768]{2,1,0:T(8,128)(2,1)S(1)}, u32[]{:S(2)}, u32[]{:S(2)}) collective-permute-start(bf16[4,64,768]{2,1,0:T(8,128)(2,1)S(1)} %collective-permute-done.11.refs_2_), channel_id=1, source_target_pairs={{0,8},{1,9},{2,10},{3,11},{4,12},{5,13},{6,14},{7,15},{8,0},{9,1},... | collective-permute-start | bytes 1179656 | tf_op jit(solution)/shard_map/ppermute | solution.py:172
  65.2 2.3 %collective-permute-start.16 = (bf16[4,64,768]{2,1,0:T(8,128)(2,1)S(1)}, bf16[4,64,768]{2,1,0:T(8,128)(2,1)S(1)}, u32[]{:S(2)}, u32[]{:S(2)}) collective-permute-start(bf16[4,64,768]{2,1,0:T(8,128)(2,1)S(1)} %collective-permute-done.12.refs_3_), channel_id=1, source_target_pairs={{0,8},{1,9},{2,10},{3,11},{4,12},{5,13},{6,14},{7,15},{8,0},{9,1},... | collective-permute-start | bytes 1179656 | tf_op jit(solution)/shard_map/ppermute | solution.py:172

commit v8 on v7

--- a/solution.py
+++ b/solution.py
@@ -53,7 +53,7 @@
 def add_shards(names, where, has_totals, last, place_ref, weights_ref, *refs):
     refs = list(refs)
     if last:
-        far_ref, out_ref, totals_in, left_ref = (refs.pop() for _ in range(4))
+        sems, row_ref, far_ref, out_ref, totals_in, left_ref = (refs.pop() for _ in range(6))
     else:
         left_ref, out_ref = refs.pop(), refs.pop()
         totals_in = refs.pop() if has_totals else None
@@ -105,44 +105,54 @@
 
     if last:
         lane = lax.broadcasted_iota(jnp.int32, (per_block, 2 * per_block), 1)
-        for part in range(2):
-            for spin in range(spins):
-                top = (part * spins + spin) * per_block
-                for column in range(0, columns, 2):
-                    across = pl.ds(column * per_block, 2 * per_block)
+        copies = []
+        for spin in range(spins):
+            for column in range(0, columns, 2):
+                first = (spin * columns + column) * 2
+                across = pl.ds(column * per_block, 2 * per_block)
+                for part in range(2):
+                    top = (part * spins + spin) * per_block
                     for p in range(2):
                         dx = jnp.bitwise_xor(pair, p)
                         near = totals_in[0, dx, pl.ds(top, per_block), across]
                         far = far_ref[dx, pl.ds(top, per_block), across]
                         even = jnp.where(core == 0, near, far)
                         odd = jnp.where(core == 0, far, near)
-                        row = (spin * columns + column) * 2 + part
                         place = pl.ds(p * 2 * per_block, 2 * per_block)
-                        out_ref[row, :, place] = jnp.where(
+                        row_ref[first + part, :, place] = jnp.where(
                             lane < per_block, even, pltpu.roll(odd, per_block, 1)
                         )
-                        out_ref[row + 2, :, place] = jnp.where(
+                        row_ref[first + part + 2, :, place] = jnp.where(
                             lane < per_block, pltpu.roll(even, per_block, 1), odd
                         )
+                rows = pl.ds(first, 4)
+                copies.append(
+                    pltpu.make_async_copy(row_ref.at[rows], out_ref.at[rows], sems.at[len(copies)])
+                )
+                copies[-1].start()
+        for copy in copies:
+            copy.wait()
 
 
 def route_second(place_ref, *refs):
-    ab0_ref, o1_ref, o2_ref, stack_ref, both_ref, relayed_ref, mixed_ref = refs[3:]
+    ab0_ref, o1_ref, o2_ref, stack_ref, both_ref, mixed_ref = refs[3:]
     for slot in range(6):
         stack_ref[slot] = refs[slot][...]
     both_ref[0] = o1_ref[...]
     both_ref[1] = o2_ref[...]
-    relayed_ref[0] = ab0_ref[...]
-    relayed_ref[1] = o2_ref[...]
     mixed_ref[...] = jnp.where(place_ref[1] == 0, o2_ref[...], ab0_ref[...])
 
 
-def route_third(z1_ref, a12_ref, b12_ref, ab2_ref, stack_ref, o3_ref):
-    for slot, ref in enumerate((z1_ref, a12_ref, b12_ref)):
-        stack_ref[2 * slot] = ref[0]
-        stack_ref[2 * slot + 1] = ref[1]
-    stack_ref[6] = ab2_ref[...]
-    o3_ref[...] = z1_ref[1]
+def route_third(ab1_ref, o3_ref, ab2_ref, a12_ref, b12_ref, stack_ref):
+    for slot, ref in enumerate((ab1_ref, o3_ref, ab2_ref)):
+        stack_ref[slot] = ref[...]
+    stack_ref[3:5] = a12_ref[...]
+    stack_ref[5:7] = b12_ref[...]
+
+
+def route_last(a3_ref, ab3_ref, stack_ref):
+    stack_ref[0] = a3_ref[...]
+    stack_ref[1] = ab3_ref[...]
 
 
 def left_slots(names):
@@ -218,16 +228,22 @@
         block = pl.BlockSpec(memory_space=pltpu.VMEM)
         out_shape = [jax.ShapeDtypeStruct(total_shape, jnp.float32)]
         scratch = [pltpu.VMEM(left_shape, jnp.bfloat16)]
+        out_specs = [block]
         if last:
             out_shape = [jax.ShapeDtypeStruct((share, per_block, 4 * per_block), jnp.float32)]
-            scratch = [pltpu.VMEM(total_shape[1:], jnp.float32)]
+            out_specs = [pl.BlockSpec(memory_space=pl.ANY)]
+            scratch = [
+                pltpu.VMEM(total_shape[1:], jnp.float32),
+                pltpu.VMEM(out_shape[0].shape, jnp.float32),
+                pltpu.SemaphoreType.DMA((spins * columns // 2,)),
+            ]
         if keep:
             out_shape.append(jax.ShapeDtypeStruct(left_shape, jnp.bfloat16))
-            scratch = []
+            out_specs, scratch = [block] * 2, []
         out = pl.pallas_call(
             functools.partial(add_shards, tuple(names), places, totals is not None, last),
             in_specs=[pl.BlockSpec(memory_space=pltpu.SMEM)] + [block] * (len(operands) - 1),
-            out_specs=[block] * len(out_shape),
+            out_specs=out_specs,
             out_shape=out_shape,
             scratch_shapes=scratch,
             compiler_params=pltpu.CompilerParams(vmem_limit_bytes=40 * 1024 * 1024),
@@ -253,7 +269,7 @@
     put("1e", hop_b(near("A", 0)), "near", [("AB", 0)])
     place, weights = fence((place, weights))
 
-    def route(kernel, operands, counts):
+    def route(kernel, operands, counts, weight=0):
         block = pl.BlockSpec(memory_space=pltpu.VMEM)
         first = pl.BlockSpec(memory_space=pltpu.SMEM) if operands[0] is place else block
         shapes = [(count,) * (count > 1) + packed.shape for count in counts]
@@ -263,37 +279,49 @@
             out_specs=[block] * len(counts),
             out_shape=[jax.ShapeDtypeStruct(shape, packed.dtype) for shape in shapes],
             compiler_params=pltpu.CompilerParams(vmem_limit_bytes=24 * 1024 * 1024),
+            cost_estimate=pl.CostEstimate(flops=weight, bytes_accessed=0, transcendentals=0),
         )(*operands)
         return fence(routed)
 
     first = [("O", 0), ("A", 0), ("B", 0), ("AB", 0), ("O", 1), ("O", 2)]
-    stack, both, relayed, mixed = route(
-        route_second, [place] + [near(*kind) for kind in first], (6, 2, 2, 1)
-    )
-    second = [("AB", 1), ("O", 3), ("A", 1), ("A", 2), ("B", 1), ("B", 2), ("AB", 2)]
+    second = [("AB", 1), ("O", 3), ("AB", 2), ("A", 1), ("A", 2), ("B", 1), ("B", 2)]
+    third = [("A", 3), ("AB", 3), ("B", 3)]
+    stack, both, mixed = route(route_second, [place] + [near(*kind) for kind in first], (6, 2, 1))
     totals = add([("near", *kind) for kind in first], None)
-    put("2a", hop_z(relayed, 1), "near", second[0:2])
-    put("2b", hop_a(both), "near", second[2:4])
-    put("2c", hop_b(both), "near", second[4:6])
-    put("2d", hop_mixed(mixed), "near", second[6:7])
-    put("2e", swap(stack), "far", first)
+    o3, ab2, a12, b12 = hop_z(near("O", 2), 1), hop_mixed(mixed), hop_a(both), hop_b(both)
+    put("2a", swap(stack), "far", first)
     totals = fence(totals)
 
-    arrived = [arrays[key] for key in ("2a", "2b", "2c", "2d")]
-    stack, start = route(route_third, arrived, (7, 1))
-    third = [("AB", 3), ("A", 3), ("B", 3)]
-    new = [hop_z(near("AB", 2), 1), hop_a(start), hop_b(start)]
-    put("3d", swap(stack), "far", second)
-    totals = add([("near", *kind) for kind in second] + [("far", *kind) for kind in first], totals)
+    put("2b", hop_z(near("AB", 0), 1), "near", [("AB", 1)])
+    totals = add([("far", *kind) for kind in first], totals)
+    ab1 = arrays.pop("2b")
+    put("2c", o3, "near", [("O", 3)])
+    put("2d", ab2, "near", [("AB", 2)])
+    totals = fence(totals)
+
+    ab3, a3, o3 = hop_z(near("AB", 2), 1), hop_a(near("O", 3)), near("O", 3)
+    arrays["2b"] = ab1
+    put("2e", a12, "near", [("A", 1), ("A", 2)])
+    put("2f", b12, "near", [("B", 1), ("B", 2)])
+    totals = fence(totals)
+
+    keys = ("2b", "2c", "2d", "2e", "2f")
+    (stack,) = route(route_third, [arrays[key] for key in keys], (7,))
+    b3, far2 = hop_b(near("O", 3)), swap(stack)
+    totals = add([("near", *kind) for kind in second], totals)
+    a3, ab3, totals = lax.optimization_barrier((a3, ab3, totals))
+    (stack,) = route(route_last, [a3, ab3], (2,), weight=10**11)
+    put("3a", stack, "near", third[:2])
+    stack = swap(stack)
+    put("3d", far2, "far", second)
     totals = add([("far", *kind) for kind in second], totals)
-    for order, (kind, array) in enumerate(zip(third, new)):
-        put("3" + "abc"[order], array, "near", [kind])
+    put("3b", b3, "near", third[2:])
     totals = fence(totals)
 
-    new = [swap(near(*kind)) for kind in third]
+    put("4a", stack, "far", third[:2])
+    far3 = swap(near("B", 3))
     totals, left = add([("near", *kind) for kind in third], totals, keep=True)
-    for order, (kind, array) in enumerate(zip(third, new)):
-        put("4" + "abc"[order], array, "far", [kind])
+    put("4b", far3, "far", third[2:])
     totals, left = fence((totals, left))
     return add([("far", *kind) for kind in third], totals, left=left)
 

time: 70.4 us -> 67.4 us (0.957)
  waiting for transfers between devices: 32.4 us -> 26.6 us
  starting transfers between devices: 20.9 us -> 23.1 us
    ppermute x17, waiting for transfers between devices: 32.4 us -> 26.6 us  [move(): return lax.ppermute(array, AXES, pairs)]
    ppermute x17, starting transfers between devices: 20.9 us -> 23.1 us  [move(): return lax.ppermute(array, AXES, pairs)]
    pallas_call x5 -> x6, Pallas kernels: 13.7 us -> 14.3 us  [add(): pl.pallas_call(functools.partial(add_shards, tuple(names), places, totals...]
  transfers between devices with their start and end apart: 17 -> 17, of which waited for: 7 -> 6; matrix products, arithmetic and copies ran while one was open for 1% -> 1% of each run, Pallas kernels for 16% -> 18%
where the time goes in v8:
time: 67.4 us; the launch traced here: 67.3 us
  waiting for transfers between devices  26.6 us (39%)
  starting transfers between devices  23.1 us (34%)
  Pallas kernels  15.3 us (23%)
  local copies, waits for them, and re-layouts  1.78 us (3%)
    ppermute x17, waiting for transfers between devices, move(): return lax.ppermute(array, AXES, pairs)  26.6 us
    ppermute x17, starting transfers between devices, move(): return lax.ppermute(array, AXES, pairs)  23.1 us
    pallas_call x6, Pallas kernels, add(): pl.pallas_call(functools.partial(add_shards, tuple(names), places, totals...  14.3 us
    reshape x1, local copies, waits for them, and re-layouts, shards(): modes.reshape(slots, per_block, 4, 3, site_count)  1.35 us
  transfers between devices with their start and end apart: 17, of which 6 were waited for; matrix products, arithmetic and copies ran while one was open for 1% of the time, Pallas kernels for 18%

profile of v8, /device:TPU:0, one launch (start us, length us, event | category | flops | bytes accessed | tf_op | source)
XLA Modules:
  0.0 67.3 jit_solution(16415435033980854520)
XLA Ops:
  0.0 0.0 copy-start
  0.0 1.3 %copy.9 = bf16[2,64,4,3,128]{4,3,0,1,2:T(4,128)(2,1)S(1)} copy(bf16[2,64,4,3,128]{4,1,3,2,0:T(8,128)(2,1)} %bitcast.32) | data formatting | bytes 786432 | tf_op jit(solution)/shard_map/reshape | solution.py:396
  1.4 0.3 reshape.222.refs_0_.refs_5_
  1.7 3.0 %collective-permute-start.3 = (bf16[4,64,768]{2,1,0:T(8,128)(2,1)S(1)}, bf16[4,64,768]{2,1,0:T(8,128)(2,1)S(1)}, u32[]{:S(2)}, u32[]{:S(2)}) collective-permute-start(bf16[4,64,768]{2,1,0:T(8,128)(2,1)S(1)} %reshape.222.refs_0_.refs_5_), channel_id=1, source_target_pairs={{0,16},{1,17},{2,18},{3,19},{4,20},{5,21},{6,22},{7,23},{8,9},{9,8... | collective-permute-start | bytes 1179656 | tf_op jit(solution)/shard_map/ppermute | solution.py:182
  4.7 2.6 %collective-permute-start = (bf16[4,64,768]{2,1,0:T(8,128)(2,1)S(1)}, bf16[4,64,768]{2,1,0:T(8,128)(2,1)S(1)}, u32[]{:S(2)}, u32[]{:S(2)}) collective-permute-start(bf16[4,64,768]{2,1,0:T(8,128)(2,1)S(1)} %reshape.222.refs_0_.refs_5_), channel_id=1, source_target_pairs={{0,4},{1,5},{2,6},{3,7},{4,0},{5,1},{6,2},{7,3},{8,12},{9,13},{10,... | collective-permute-start | bytes 1179656 | tf_op jit(solution)/shard_map/ppermute | solution.py:182
  7.3 1.6 %collective-permute-start.1 = (bf16[4,64,768]{2,1,0:T(8,128)(2,1)S(1)}, bf16[4,64,768]{2,1,0:T(8,128)(2,1)S(1)}, u32[]{:S(2)}, u32[]{:S(2)}) collective-permute-start(bf16[4,64,768]{2,1,0:T(8,128)(2,1)S(1)} %reshape.222.refs_0_.refs_5_), channel_id=1, source_target_pairs={{0,2},{1,3},{2,0},{3,1},{4,6},{5,7},{6,4},{7,5},{8,10},{9,11},{10,... | collective-permute-start | bytes 1179656 | tf_op jit(solution)/shard_map/ppermute | solution.py:182
  8.9 1.5 %collective-permute-start.2 = (bf16[4,64,768]{2,1,0:T(8,128)(2,1)S(1)}, bf16[4,64,768]{2,1,0:T(8,128)(2,1)S(1)}, u32[]{:S(2)}, u32[]{:S(2)}) collective-permute-start(bf16[4,64,768]{2,1,0:T(8,128)(2,1)S(1)} %reshape.222.refs_0_.refs_5_), channel_id=1, source_target_pairs={{0,1},{1,0},{2,3},{3,2},{4,5},{5,4},{6,7},{7,6},{8,24},{9,25},{10,... | collective-permute-start | bytes 1179656 | tf_op jit(solution)/shard_map/ppermute | solution.py:182
  10.4 0.0 copy-done
  10.4 0.1 fusion
  10.5 0.0 collective-permute-done.3.refs_1_.refs_3_
  10.6 3.4 %collective-permute-start.4 = (bf16[4,64,768]{2,1,0:T(8,128)(2,1)S(1)}, bf16[4,64,768]{2,1,0:T(8,128)(2,1)S(1)}, u32[]{:S(2)}, u32[]{:S(2)}) collective-permute-start(bf16[4,64,768]{2,1,0:T(8,128)(2,1)S(1)} %collective-permute-done.3.refs_1_.refs_3_), channel_id=1, source_target_pairs={{0,1},{1,0},{2,3},{3,2},{4,5},{5,4},{6,7},{7,6},{8,24},{9,25},{10,... | collective-permute-start | bytes 1179656 | tf_op jit(solution)/shard_map/ppermute | solution.py:182
  14.0 0.1 stack.44.place_ref
  14.1 0.1 multiply_cosine_fusion
  14.2 10.5 %collective-permute-done.refs_5_.refs_0_ = bf16[4,64,768]{2,1,0:T(8,128)(2,1)S(1)} collective-permute-done((bf16[4,64,768]{2,1,0:T(8,128)(2,1)S(1)}, bf16[4,64,768]{2,1,0:T(8,128)(2,1)S(1)}, u32[]{:S(2)}, u32[]{:S(2)}) %collective-permute-start) | collective-permute-done | bytes 393248 | tf_op jit(solution)/shard_map/ppermute | solution.py:182
  24.7 0.2 collective-permute-done.1.refs_4_.refs_1_
  24.9 0.0 collective-permute-done.2.refs_2_
  24.9 0.0 collective-permute-done.4.refs_3_.refs_4_
  24.9 0.8 %shard_map.28 = (bf16[6,4,64,768]{3,2,1,0:T(8,128)(2,1)S(1)}, bf16[2,4,64,768]{3,2,1,0:T(8,128)(2,1)S(1)}, bf16[4,64,768]{2,1,0:T(8,128)(2,1)S(1)}) custom-call(s32[7]{0:T(128)S(1)} %stack.44.place_ref, bf16[4,64,768]{2,1,0:T(8,128)(2,1)S(1)} %reshape.222.refs_0_.refs_5_, bf16[4,64,768]{2,1,0:T(8,128)(2,1)S(1)} %collective-permute-done.3.refs_1_.refs_3_, ...), custom_call_target="tpu_custom_call" | custom-call | tf_op jit(solution)/shard_map/pallas_call | solution.py:276
  25.7 0.1 collective-permute-start.5
  25.8 0.5 collective-permute-start.10
  26.3 1.5 %collective-permute-start.9 = (bf16[2,4,64,768]{3,2,1,0:T(8,128)(2,1)S(1)}, bf16[2,4,64,768]{3,2,1,0:T(8,128)(2,1)S(1)}, u32[]{:S(2)}, u32[]{:S(2)}) collective-permute-start(bf16[2,4,64,768]{3,2,1,0:T(8,128)(2,1)S(1)} %get-tuple-element.104), channel_id=1, source_target_pairs={{0,16},{1,17},{2,18},{3,19},{4,20},{5,21},{6,22},{7,23},{8,9},{9,8... | collective-permute-start | bytes 2359304 | tf_op jit(solution)/shard_map/ppermute | solution.py:182
  27.9 1.4 %collective-permute-start.6 = (bf16[4,64,768]{2,1,0:T(8,128)(2,1)S(1)}, bf16[4,64,768]{2,1,0:T(8,128)(2,1)S(1)}, u32[]{:S(2)}, u32[]{:S(2)}) collective-permute-start(bf16[4,64,768]{2,1,0:T(8,128)(2,1)S(1)} %collective-permute-done.refs_5_.refs_0_), channel_id=1, source_target_pairs={{0,2},{1,3},{2,0},{3,1},{4,6},{5,7},{6,4},{7,5},{8,10},{9,11},{10,... | collective-permute-start | bytes 1179656 | tf_op jit(solution)/shard_map/ppermute | solution.py:182
  29.3 1.5 %collective-permute-start.7 = (bf16[4,64,768]{2,1,0:T(8,128)(2,1)S(1)}, bf16[4,64,768]{2,1,0:T(8,128)(2,1)S(1)}, u32[]{:S(2)}, u32[]{:S(2)}) collective-permute-start(bf16[4,64,768]{2,1,0:T(8,128)(2,1)S(1)} %get-tuple-element.97), channel_id=1, source_target_pairs={{0,17},{1,16},{2,19},{3,18},{4,21},{5,20},{6,23},{7,22},{8,12},{9,... | collective-permute-start | bytes 1179656 | tf_op jit(solution)/shard_map/ppermute | solution.py:182
  30.8 2.5 %shard_map.29.refs_6_ = f32[2,2,256,256]{3,2,1,0:T(8,128)S(1)} custom-call(s32[7]{0:T(128)S(1)} %stack.44.place_ref, f32[8,2,128]{2,1,0:T(2,128)S(1)} %maximum_bitcast_fusion.weights_ref, bf16[4,64,768]{2,1,0:T(8,128)(2,1)S(1)} %collective-permute-done.refs_5_.refs_0_, bf16[4,64,768]{2,1,0:T(8,128)(2,1)S(1)} %collective-permute-done.1.refs_4_.refs_1_, ...), custom_call_target="tpu_custom_call" | custom-call | flops 1207959552 | bytes 4456448 | tf_op jit(solution)/shard_map/pallas_call | solution.py:243
  33.3 0.0 collective-permute-done.5.refs_4_
  33.3 0.7 collective-permute-start.8
  33.9 2.5 %shard_map.30.refs_7_ = f32[2,2,256,256]{3,2,1,0:T(8,128)S(1)} custom-call(s32[7]{0:T(128)S(1)} %stack.44.place_ref, f32[8,2,128]{2,1,0:T(2,128)S(1)} %maximum_bitcast_fusion.weights_ref, bf16[4,64,768]{2,1,0:T(8,128)(2,1)S(1)} %collective-permute-done.refs_5_.refs_0_, bf16[4,64,768]{2,1,0:T(8,128)(2,1)S(1)} %collective-permute-done.1.refs_4_.refs_1_, ...), custom_call_target="tpu_custom_call" | custom-call | flops 1207959552 | bytes 4456448 | tf_op jit(solution)/shard_map/pallas_call | solution.py:243
  36.4 7.6 %collective-permute-done.6.o3_ref.refs_3_.refs_2_.refs_0_ = bf16[4,64,768]{2,1,0:T(8,128)(2,1)S(1)} collective-permute-done((bf16[4,64,768]{2,1,0:T(8,128)(2,1)S(1)}, bf16[4,64,768]{2,1,0:T(8,128)(2,1)S(1)}, u32[]{:S(2)}, u32[]{:S(2)}) %collective-permute-start.6) | collective-permute-done | bytes 393248 | tf_op jit(solution)/shard_map/ppermute | solution.py:182
  44.1 5.9 %collective-permute-done.7.ab2_ref.refs_4_ = bf16[4,64,768]{2,1,0:T(8,128)(2,1)S(1)} collective-permute-done((bf16[4,64,768]{2,1,0:T(8,128)(2,1)S(1)}, bf16[4,64,768]{2,1,0:T(8,128)(2,1)S(1)}, u32[]{:S(2)}, u32[]{:S(2)}) %collective-permute-start.7) | collective-permute-done | bytes 393248 | tf_op jit(solution)/shard_map/ppermute | solution.py:182
  49.9 1.5 %collective-permute-start.11 = (bf16[4,64,768]{2,1,0:T(8,128)(2,1)S(1)}, bf16[4,64,768]{2,1,0:T(8,128)(2,1)S(1)}, u32[]{:S(2)}, u32[]{:S(2)}) collective-permute-start(bf16[4,64,768]{2,1,0:T(8,128)(2,1)S(1)} %collective-permute-done.6.o3_ref.refs_3_.refs_2_.refs_0_), channel_id=1, source_target_pairs={{0,16},{1,17},{2,18},{3,19},{4,20},{5,21},{6,22},{7,23},{8,9},{9,8... | collective-permute-start | bytes 1179656 | tf_op jit(solution)/shard_map/ppermute | solution.py:182
  51.5 1.4 %collective-permute-start.12 = (bf16[4,64,768]{2,1,0:T(8,128)(2,1)S(1)}, bf16[4,64,768]{2,1,0:T(8,128)(2,1)S(1)}, u32[]{:S(2)}, u32[]{:S(2)}) collective-permute-start(bf16[4,64,768]{2,1,0:T(8,128)(2,1)S(1)} %collective-permute-done.7.ab2_ref.refs_4_), channel_id=1, source_target_pairs={{0,2},{1,3},{2,0},{3,1},{4,6},{5,7},{6,4},{7,5},{8,10},{9,11},{10,... | collective-permute-start | bytes 1179656 | tf_op jit(solution)/shard_map/ppermute | solution.py:182
  52.9 0.0 collective-permute-done.10.b12_ref.refs_6_.refs_4_
  52.9 0.0 collective-permute-done.9.a12_ref.refs_5_.refs_3_
  52.9 0.0 collective-permute-done.8.ab1_ref.refs_2_
  52.9 0.2 shard_map.31
  53.1 0.1 collective-permute-start.14
  53.2 1.6 %collective-permute-start.13 = (bf16[4,64,768]{2,1,0:T(8,128)(2,1)S(1)}, bf16[4,64,768]{2,1,0:T(8,128)(2,1)S(1)}, u32[]{:S(2)}, u32[]{:S(2)}) collective-permute-start(bf16[4,64,768]{2,1,0:T(8,128)(2,1)S(1)} %collective-permute-done.6.o3_ref.refs_3_.refs_2_.refs_0_), channel_id=1, source_target_pairs={{0,1},{1,0},{2,3},{3,2},{4,5},{5,4},{6,7},{7,6},{8,24},{9,25},{10,... | collective-permute-start | bytes 1179656 | tf_op jit(solution)/shard_map/ppermute | solution.py:182
  54.8 2.6 %shard_map.32.refs_6_ = f32[2,2,256,256]{3,2,1,0:T(8,128)S(1)} custom-call(s32[7]{0:T(128)S(1)} %stack.44.place_ref, f32[8,2,128]{2,1,0:T(2,128)S(1)} %maximum_bitcast_fusion.weights_ref, bf16[4,64,768]{2,1,0:T(8,128)(2,1)S(1)} %collective-permute-done.refs_5_.refs_0_, bf16[4,64,768]{2,1,0:T(8,128)(2,1)S(1)} %collective-permute-done.1.refs_4_.refs_1_, ...), custom_call_target="tpu_custom_call" | custom-call | flops 1409286144 | bytes 4849664 | tf_op jit(solution)/shard_map/pallas_call | solution.py:243
  57.4 1.8 %collective-permute-done.11.a3_ref = bf16[4,64,768]{2,1,0:T(8,128)(2,1)S(1)} collective-permute-done((bf16[4,64,768]{2,1,0:T(8,128)(2,1)S(1)}, bf16[4,64,768]{2,1,0:T(8,128)(2,1)S(1)}, u32[]{:S(2)}, u32[]{:S(2)}) %collective-permute-start.11) | collective-permute-done | bytes 393248 | tf_op jit(solution)/shard_map/ppermute | solution.py:182
  59.2 0.7 collective-permute-done.12.ab3_ref
  59.8 0.1 shard_map.33.refs_1_
  59.9 0.1 collective-permute-start.15
  59.9 0.0 collective-permute-done.14.refs_5_
  60.0 2.6 %shard_map.34.refs_3_ = f32[2,2,256,256]{3,2,1,0:T(8,128)S(1)} custom-call(s32[7]{0:T(128)S(1)} %stack.44.place_ref, f32[8,2,128]{2,1,0:T(2,128)S(1)} %maximum_bitcast_fusion.weights_ref, bf16[4,64,768]{2,1,0:T(8,128)(2,1)S(1)} %collective-permute-done.refs_5_.refs_0_, bf16[4,64,768]{2,1,0:T(8,128)(2,1)S(1)} %collective-permute-done.1.refs_4_.refs_1_, ...), custom_call_target="tpu_custom_call" | custom-call | flops 1409286144 | bytes 4849664 | tf_op jit(solution)/shard_map/pallas_call | solution.py:243
  62.5 0.0 collective-permute-done.13.refs_2_
  62.5 0.6 collective-permute-start.16
  63.1 1.6 %shard_map.35 = (f32[2,2,256,256]{3,2,1,0:T(8,128)S(1)}, bf16[2,2,256,768]{3,2,1,0:T(8,128)(2,1)S(1)}) custom-call(s32[7]{0:T(128)S(1)} %stack.44.place_ref, f32[8,2,128]{2,1,0:T(2,128)S(1)} %maximum_bitcast_fusion.weights_ref, bf16[4,64,768]{2,1,0:T(8,128)(2,1)S(1)} %collective-permute-done.6.o3_ref.refs_3_.refs_2_.refs_0_, ...), custom_call_target="tpu_custom_call" | custom-call | flops 603979776 | bytes 3276800 | tf_op jit(solution)/shard_map/pallas_call | solution.py:243
  64.7 0.0 collective-permute-done.15.refs_0_
  64.7 0.0 collective-permute-done.16.refs_1_
  64.7 2.5 %shard_map.36 = f32[16,64,256]{2,1,0:T(8,128)} custom-call(s32[7]{0:T(128)S(1)} %stack.44.place_ref, f32[8,2,128]{2,1,0:T(2,128)S(1)} %maximum_bitcast_fusion.weights_ref, bf16[2,4,64,768]{3,2,1,0:T(8,128)(2,1)S(1)} %collective-permute-done.15.refs_0_, bf16[4,64,768]{2,1,0:T(8,128)(2,1)S(1)} %collective-permute-done.16.refs_1_, ...), custom_call_target="tpu_custom_call" | custom-call | flops 603979776 | bytes 3276800 | tf_op jit(solution)/shard_map/pallas_call | solution.py:243
  (5 shorter events, 0.1 us)
Async XLA Ops:
  0.0 10.4 %copy-start = (s32[4,3]{1,0:T(4,128)S(1)}, s32[4,3]{1,0:T(4,128)}, u32[]{:S(2)}) copy-start(s32[4,3]{1,0:T(4,128)} %param.3) | copy-start | bytes 148
  1.7 8.8 %collective-permute-start.3 = (bf16[4,64,768]{2,1,0:T(8,128)(2,1)S(1)}, bf16[4,64,768]{2,1,0:T(8,128)(2,1)S(1)}, u32[]{:S(2)}, u32[]{:S(2)}) collective-permute-start(bf16[4,64,768]{2,1,0:T(8,128)(2,1)S(1)} %reshape.222.refs_0_.refs_5_), channel_id=1, source_target_pairs={{0,16},{1,17},{2,18},{3,19},{4,20},{5,21},{6,22},{7,23},{8,9},{9,8... | collective-permute-start | bytes 1179656 | tf_op jit(solution)/shard_map/ppermute | solution.py:182
  4.7 20.0 %collective-permute-start = (bf16[4,64,768]{2,1,0:T(8,128)(2,1)S(1)}, bf16[4,64,768]{2,1,0:T(8,128)(2,1)S(1)}, u32[]{:S(2)}, u32[]{:S(2)}) collective-permute-start(bf16[4,64,768]{2,1,0:T(8,128)(2,1)S(1)} %reshape.222.refs_0_.refs_5_), channel_id=1, source_target_pairs={{0,4},{1,5},{2,6},{3,7},{4,0},{5,1},{6,2},{7,3},{8,12},{9,13},{10,... | collective-permute-start | bytes 1179656 | tf_op jit(solution)/shard_map/ppermute | solution.py:182
  7.3 17.6 %collective-permute-start.1 = (bf16[4,64,768]{2,1,0:T(8,128)(2,1)S(1)}, bf16[4,64,768]{2,1,0:T(8,128)(2,1)S(1)}, u32[]{:S(2)}, u32[]{:S(2)}) collective-permute-start(bf16[4,64,768]{2,1,0:T(8,128)(2,1)S(1)} %reshape.222.refs_0_.refs_5_), channel_id=1, source_target_pairs={{0,2},{1,3},{2,0},{3,1},{4,6},{5,7},{6,4},{7,5},{8,10},{9,11},{10,... | collective-permute-start | bytes 1179656 | tf_op jit(solution)/shard_map/ppermute | solution.py:182
  8.9 16.1 %collective-permute-start.2 = (bf16[4,64,768]{2,1,0:T(8,128)(2,1)S(1)}, bf16[4,64,768]{2,1,0:T(8,128)(2,1)S(1)}, u32[]{:S(2)}, u32[]{:S(2)}) collective-permute-start(bf16[4,64,768]{2,1,0:T(8,128)(2,1)S(1)} %reshape.222.refs_0_.refs_5_), channel_id=1, source_target_pairs={{0,1},{1,0},{2,3},{3,2},{4,5},{5,4},{6,7},{7,6},{8,24},{9,25},{10,... | collective-permute-start | bytes 1179656 | tf_op jit(solution)/shard_map/ppermute | solution.py:182
  10.6 14.4 %collective-permute-start.4 = (bf16[4,64,768]{2,1,0:T(8,128)(2,1)S(1)}, bf16[4,64,768]{2,1,0:T(8,128)(2,1)S(1)}, u32[]{:S(2)}, u32[]{:S(2)}) collective-permute-start(bf16[4,64,768]{2,1,0:T(8,128)(2,1)S(1)} %collective-permute-done.3.refs_1_.refs_3_), channel_id=1, source_target_pairs={{0,1},{1,0},{2,3},{3,2},{4,5},{5,4},{6,7},{7,6},{8,24},{9,25},{10,... | collective-permute-start | bytes 1179656 | tf_op jit(solution)/shard_map/ppermute | solution.py:182
  25.7 7.6 %collective-permute-start.5 = (bf16[6,4,64,768]{3,2,1,0:T(8,128)(2,1)S(1)}, bf16[6,4,64,768]{3,2,1,0:T(8,128)(2,1)S(1)}, u32[]{:S(2)}, u32[]{:S(2)}) collective-permute-start(bf16[6,4,64,768]{3,2,1,0:T(8,128)(2,1)S(1)} %get-tuple-element.89), channel_id=1, source_target_pairs={{0,8},{1,9},{2,10},{3,11},{4,12},{5,13},{6,14},{7,15},{8,0},{9,1},... | collective-permute-start | bytes 7077896 | tf_op jit(solution)/shard_map/ppermute | solution.py:182
  25.8 27.1 %collective-permute-start.10 = (bf16[2,4,64,768]{3,2,1,0:T(8,128)(2,1)S(1)}, bf16[2,4,64,768]{3,2,1,0:T(8,128)(2,1)S(1)}, u32[]{:S(2)}, u32[]{:S(2)}) collective-permute-start(bf16[2,4,64,768]{3,2,1,0:T(8,128)(2,1)S(1)} %get-tuple-element.104), channel_id=1, source_target_pairs={{0,1},{1,0},{2,3},{3,2},{4,5},{5,4},{6,7},{7,6},{8,24},{9,25},{10,... | collective-permute-start | bytes 2359304 | tf_op jit(solution)/shard_map/ppermute | solution.py:182
  26.3 26.6 %collective-permute-start.9 = (bf16[2,4,64,768]{3,2,1,0:T(8,128)(2,1)S(1)}, bf16[2,4,64,768]{3,2,1,0:T(8,128)(2,1)S(1)}, u32[]{:S(2)}, u32[]{:S(2)}) collective-permute-start(bf16[2,4,64,768]{3,2,1,0:T(8,128)(2,1)S(1)} %get-tuple-element.104), channel_id=1, source_target_pairs={{0,16},{1,17},{2,18},{3,19},{4,20},{5,21},{6,22},{7,23},{8,9},{9,8... | collective-permute-start | bytes 2359304 | tf_op jit(solution)/shard_map/ppermute | solution.py:182
  27.9 16.2 %collective-permute-start.6 = (bf16[4,64,768]{2,1,0:T(8,128)(2,1)S(1)}, bf16[4,64,768]{2,1,0:T(8,128)(2,1)S(1)}, u32[]{:S(2)}, u32[]{:S(2)}) collective-permute-start(bf16[4,64,768]{2,1,0:T(8,128)(2,1)S(1)} %collective-permute-done.refs_5_.refs_0_), channel_id=1, source_target_pairs={{0,2},{1,3},{2,0},{3,1},{4,6},{5,7},{6,4},{7,5},{8,10},{9,11},{10,... | collective-permute-start | bytes 1179656 | tf_op jit(solution)/shard_map/ppermute | solution.py:182
  29.3 20.7 %collective-permute-start.7 = (bf16[4,64,768]{2,1,0:T(8,128)(2,1)S(1)}, bf16[4,64,768]{2,1,0:T(8,128)(2,1)S(1)}, u32[]{:S(2)}, u32[]{:S(2)}) collective-permute-start(bf16[4,64,768]{2,1,0:T(8,128)(2,1)S(1)} %get-tuple-element.97), channel_id=1, source_target_pairs={{0,17},{1,16},{2,19},{3,18},{4,21},{5,20},{6,23},{7,22},{8,12},{9,... | collective-permute-start | bytes 1179656 | tf_op jit(solution)/shard_map/ppermute | solution.py:182
  33.3 19.7 %collective-permute-start.8 = (bf16[4,64,768]{2,1,0:T(8,128)(2,1)S(1)}, bf16[4,64,768]{2,1,0:T(8,128)(2,1)S(1)}, u32[]{:S(2)}, u32[]{:S(2)}) collective-permute-start(bf16[4,64,768]{2,1,0:T(8,128)(2,1)S(1)} %collective-permute-done.4.refs_3_.refs_4_), channel_id=1, source_target_pairs={{0,2},{1,3},{2,0},{3,1},{4,6},{5,7},{6,4},{7,5},{8,10},{9,11},{10,... | collective-permute-start | bytes 1179656 | tf_op jit(solution)/shard_map/ppermute | solution.py:182
  49.9 9.2 %collective-permute-start.11 = (bf16[4,64,768]{2,1,0:T(8,128)(2,1)S(1)}, bf16[4,64,768]{2,1,0:T(8,128)(2,1)S(1)}, u32[]{:S(2)}, u32[]{:S(2)}) collective-permute-start(bf16[4,64,768]{2,1,0:T(8,128)(2,1)S(1)} %collective-permute-done.6.o3_ref.refs_3_.refs_2_.refs_0_), channel_id=1, source_target_pairs={{0,16},{1,17},{2,18},{3,19},{4,20},{5,21},{6,22},{7,23},{8,9},{9,8... | collective-permute-start | bytes 1179656 | tf_op jit(solution)/shard_map/ppermute | solution.py:182
  51.5 8.3 %collective-permute-start.12 = (bf16[4,64,768]{2,1,0:T(8,128)(2,1)S(1)}, bf16[4,64,768]{2,1,0:T(8,128)(2,1)S(1)}, u32[]{:S(2)}, u32[]{:S(2)}) collective-permute-start(bf16[4,64,768]{2,1,0:T(8,128)(2,1)S(1)} %collective-permute-done.7.ab2_ref.refs_4_), channel_id=1, source_target_pairs={{0,2},{1,3},{2,0},{3,1},{4,6},{5,7},{6,4},{7,5},{8,10},{9,11},{10,... | collective-permute-start | bytes 1179656 | tf_op jit(solution)/shard_map/ppermute | solution.py:182
  53.1 6.8 %collective-permute-start.14 = (bf16[7,4,64,768]{3,2,1,0:T(8,128)(2,1)S(1)}, bf16[7,4,64,768]{3,2,1,0:T(8,128)(2,1)S(1)}, u32[]{:S(2)}, u32[]{:S(2)}) collective-permute-start(bf16[7,4,64,768]{3,2,1,0:T(8,128)(2,1)S(1)} %shard_map.31), channel_id=1, source_target_pairs={{0,8},{1,9},{2,10},{3,11},{4,12},{5,13},{6,14},{7,15},{8,0},{9,1},... | collective-permute-start | bytes 8257544 | tf_op jit(solution)/shard_map/ppermute | solution.py:182
  53.2 9.3 %collective-permute-start.13 = (bf16[4,64,768]{2,1,0:T(8,128)(2,1)S(1)}, bf16[4,64,768]{2,1,0:T(8,128)(2,1)S(1)}, u32[]{:S(2)}, u32[]{:S(2)}) collective-permute-start(bf16[4,64,768]{2,1,0:T(8,128)(2,1)S(1)} %collective-permute-done.6.o3_ref.refs_3_.refs_2_.refs_0_), channel_id=1, source_target_pairs={{0,1},{1,0},{2,3},{3,2},{4,5},{5,4},{6,7},{7,6},{8,24},{9,25},{10,... | collective-permute-start | bytes 1179656 | tf_op jit(solution)/shard_map/ppermute | solution.py:182
  59.9 4.8 %collective-permute-start.15 = (bf16[2,4,64,768]{3,2,1,0:T(8,128)(2,1)S(1)}, bf16[2,4,64,768]{3,2,1,0:T(8,128)(2,1)S(1)}, u32[]{:S(2)}, u32[]{:S(2)}) collective-permute-start(bf16[2,4,64,768]{3,2,1,0:T(8,128)(2,1)S(1)} %shard_map.33.refs_1_), channel_id=1, source_target_pairs={{0,8},{1,9},{2,10},{3,11},{4,12},{5,13},{6,14},{7,15},{8,0},{9,1},... | collective-permute-start | bytes 2359304 | tf_op jit(solution)/shard_map/ppermute | solution.py:182
  62.5 2.2 %collective-permute-start.16 = (bf16[4,64,768]{2,1,0:T(8,128)(2,1)S(1)}, bf16[4,64,768]{2,1,0:T(8,128)(2,1)S(1)}, u32[]{:S(2)}, u32[]{:S(2)}) collective-permute-start(bf16[4,64,768]{2,1,0:T(8,128)(2,1)S(1)} %collective-permute-done.13.refs_2_), channel_id=1, source_target_pairs={{0,8},{1,9},{2,10},{3,11},{4,12},{5,13},{6,14},{7,15},{8,0},{9,1},... | collective-permute-start | bytes 1179656 | tf_op jit(solution)/shard_map/ppermute | solution.py:182

commit v9 on v8

--- a/solution.py
+++ b/solution.py
@@ -50,7 +50,7 @@
     return term + lax.dot_general(left_sin, right, dims, preferred_element_type=jnp.float32)
 
 
-def add_shards(names, where, has_totals, last, place_ref, weights_ref, *refs):
+def add_shards(names, where, slots, has_totals, last, place_ref, weights_ref, *refs):
     refs = list(refs)
     if last:
         sems, row_ref, far_ref, out_ref, totals_in, left_ref = (refs.pop() for _ in range(6))
@@ -66,7 +66,6 @@
     columns, per_block, _ = shard(names[0]).shape
     spins = left_ref.shape[2] // (2 * per_block)
 
-    slots = left_slots(names)
     if last:
         far_ref[...] = totals_in[1]
     else:
@@ -134,25 +133,25 @@
             copy.wait()
 
 
-def route_second(place_ref, *refs):
-    ab0_ref, o1_ref, o2_ref, stack_ref, both_ref, mixed_ref = refs[3:]
+def route_second(*refs):
+    stack_ref, both_ref = refs[6:]
     for slot in range(6):
         stack_ref[slot] = refs[slot][...]
-    both_ref[0] = o1_ref[...]
-    both_ref[1] = o2_ref[...]
-    mixed_ref[...] = jnp.where(place_ref[1] == 0, o2_ref[...], ab0_ref[...])
-
-
-def route_third(ab1_ref, o3_ref, ab2_ref, a12_ref, b12_ref, stack_ref):
-    for slot, ref in enumerate((ab1_ref, o3_ref, ab2_ref)):
-        stack_ref[slot] = ref[...]
-    stack_ref[3:5] = a12_ref[...]
-    stack_ref[5:7] = b12_ref[...]
-
-
-def route_last(a3_ref, ab3_ref, stack_ref):
+    both_ref[0] = refs[4][...]
+    both_ref[1] = refs[5][...]
+
+
+def route_third(o3_ref, a12_ref, b12_ref, stack_ref):
+    stack_ref[0] = o3_ref[...]
+    stack_ref[1:3] = a12_ref[...]
+    stack_ref[3:5] = b12_ref[...]
+
+
+def route_fourth(a3_ref, ab2_ref, o3_ref, stack_ref, both_ref):
     stack_ref[0] = a3_ref[...]
-    stack_ref[1] = ab3_ref[...]
+    stack_ref[1] = ab2_ref[...]
+    both_ref[0] = a3_ref[...]
+    both_ref[1] = o3_ref[...]
 
 
 def left_slots(names):
@@ -187,16 +186,8 @@
     def hop_b(array):
         return move(array, lambda p, c, z, y: (p, c, z, y ^ 1) if c == 0 else (p ^ 1, c, z, y))
 
-    def hop_ab(array):
-        return move(array, lambda p, c, z, y: (p ^ 1, c, z, y ^ 1))
-
     def hop_z(array, by):
         return move(array, lambda p, c, z, y: (p, c, z ^ by, y))
-
-    def hop_mixed(array):
-        return move(
-            array, lambda p, c, z, y: (p ^ 1, c, z, y ^ 1) if c == 0 else (p, c, z ^ 2, y)
-        )
 
     def swap(array):
         return move(array, lambda p, c, z, y: (p, c ^ 1, z, y))
@@ -213,9 +204,9 @@
         key, slot = where[("near", kind, dz)]
         return arrays[key] if slot is None else arrays[key][slot]
 
-    def add(names, totals, keep=False, left=None):
+    def add(names, totals, keep=False, left=None, slots=None):
         last = left is not None
-        slots = left_slots(names)
+        slots = slots or left_slots(names)
         uses = list(names)
         for dy, dz in [] if last else slots:
             uses += [("near", kind, dz) for kind in (("A", "B") if dy else ("O",))]
@@ -241,7 +232,7 @@
             out_shape.append(jax.ShapeDtypeStruct(left_shape, jnp.bfloat16))
             out_specs, scratch = [block] * 2, []
         out = pl.pallas_call(
-            functools.partial(add_shards, tuple(names), places, totals is not None, last),
+            functools.partial(add_shards, tuple(names), places, slots, totals is not None, last),
             in_specs=[pl.BlockSpec(memory_space=pltpu.SMEM)] + [block] * (len(operands) - 1),
             out_specs=out_specs,
             out_shape=out_shape,
@@ -271,11 +262,10 @@
 
     def route(kernel, operands, counts, weight=0):
         block = pl.BlockSpec(memory_space=pltpu.VMEM)
-        first = pl.BlockSpec(memory_space=pltpu.SMEM) if operands[0] is place else block
         shapes = [(count,) * (count > 1) + packed.shape for count in counts]
         routed = pl.pallas_call(
             kernel,
-            in_specs=[first] + [block] * (len(operands) - 1),
+            in_specs=[block] * len(operands),
             out_specs=[block] * len(counts),
             out_shape=[jax.ShapeDtypeStruct(shape, packed.dtype) for shape in shapes],
             compiler_params=pltpu.CompilerParams(vmem_limit_bytes=24 * 1024 * 1024),
@@ -284,46 +274,49 @@
         return fence(routed)
 
     first = [("O", 0), ("A", 0), ("B", 0), ("AB", 0), ("O", 1), ("O", 2)]
-    second = [("AB", 1), ("O", 3), ("AB", 2), ("A", 1), ("A", 2), ("B", 1), ("B", 2)]
-    third = [("A", 3), ("AB", 3), ("B", 3)]
-    stack, both, mixed = route(route_second, [place] + [near(*kind) for kind in first], (6, 2, 1))
+    second = [("O", 3), ("A", 1), ("A", 2), ("B", 1), ("B", 2)]
+    third = [("A", 3), ("AB", 2)]
+    fourth = [("AB", 3), ("B", 3), ("AB", 1)]
+    stack, both = route(route_second, [near(*kind) for kind in first], (6, 2))
     totals = add([("near", *kind) for kind in first], None)
-    o3, ab2, a12, b12 = hop_z(near("O", 2), 1), hop_mixed(mixed), hop_a(both), hop_b(both)
+    o3, a12, b12 = hop_z(near("O", 2), 1), hop_a(both), hop_b(both)
     put("2a", swap(stack), "far", first)
     totals = fence(totals)
 
-    put("2b", hop_z(near("AB", 0), 1), "near", [("AB", 1)])
+    ab2 = hop_z(near("AB", 0), 2)
     totals = add([("far", *kind) for kind in first], totals)
-    ab1 = arrays.pop("2b")
-    put("2c", o3, "near", [("O", 3)])
-    put("2d", ab2, "near", [("AB", 2)])
+    put("2b", o3, "near", second[:1])
     totals = fence(totals)
 
-    ab3, a3, o3 = hop_z(near("AB", 2), 1), hop_a(near("O", 3)), near("O", 3)
-    arrays["2b"] = ab1
-    put("2e", a12, "near", [("A", 1), ("A", 2)])
-    put("2f", b12, "near", [("B", 1), ("B", 2)])
+    a3 = hop_a(near("O", 3))
+    put("2c", a12, "near", second[1:3])
+    put("2d", b12, "near", second[3:5])
     totals = fence(totals)
 
-    keys = ("2b", "2c", "2d", "2e", "2f")
-    (stack,) = route(route_third, [arrays[key] for key in keys], (7,))
-    b3, far2 = hop_b(near("O", 3)), swap(stack)
-    totals = add([("near", *kind) for kind in second], totals)
-    a3, ab3, totals = lax.optimization_barrier((a3, ab3, totals))
-    (stack,) = route(route_last, [a3, ab3], (2,), weight=10**11)
-    put("3a", stack, "near", third[:2])
-    stack = swap(stack)
+    (stack,) = route(route_third, [arrays[key] for key in ("2b", "2c", "2d")], (5,))
+    far2 = swap(stack)
+    put("3b", ab2, "near", third[1:])
+    totals = add([("near", *kind) for kind in second + third[1:]], totals)
+    a3, totals = lax.optimization_barrier((a3, totals))
+    stack, both = route(route_fourth, [a3, ab2, near("O", 3)], (2, 2), weight=10**11)
+    put("3a", a3, "near", third[:1])
+    totals = fence(totals)
+
+    b3, ab1, far3 = hop_b(both), hop_z(near("AB", 0), 1), swap(stack)
     put("3d", far2, "far", second)
     totals = add([("far", *kind) for kind in second], totals)
-    put("3b", b3, "near", third[2:])
+    put("3e", far3, "far", third)
+    put("4a", b3, "near", fourth[:2])
+    put("4b", ab1, "near", fourth[2:])
     totals = fence(totals)
 
-    put("4a", stack, "far", third[:2])
-    far3 = swap(near("B", 3))
-    totals, left = add([("near", *kind) for kind in third], totals, keep=True)
-    put("4b", far3, "far", third[2:])
+    new = [swap(arrays["4a"]), swap(arrays["4b"])]
+    names = [("near", *kind) for kind in fourth + third[:1]] + [("far", *kind) for kind in third]
+    totals, left = add(names, totals, keep=True)
+    put("5a", new[0], "far", fourth[:2])
+    put("5b", new[1], "far", fourth[2:])
     totals, left = fence((totals, left))
-    return add([("far", *kind) for kind in third], totals, left=left)
+    return add([("far", *kind) for kind in fourth], totals, left=left, slots=left_slots(names))
 
 
 def add_terms(place_ref, weights_ref, left_ref, right_ref, field_ref):

time: 67.4 us -> 71.9 us (1.067)
  waiting for transfers between devices: 26.6 us -> 33.3 us
  starting transfers between devices: 23.1 us -> 20.8 us
    ppermute x17, waiting for transfers between devices: 26.6 us -> 33.3 us  [move(): return lax.ppermute(array, AXES, pairs)]
    ppermute x17, starting transfers between devices: 23.1 us -> 20.8 us  [move(): return lax.ppermute(array, AXES, pairs)]
  transfers between devices with their start and end apart: 17 -> 17, of which waited for: 6 -> 7; matrix products, arithmetic and copies ran while one was open for 1% -> 1% of each run, Pallas kernels for 18% -> 18%
where the time goes in v9:
time: 71.9 us; the launch traced here: 71.8 us
  waiting for transfers between devices  33.3 us (46%)
  starting transfers between devices  20.8 us (29%)
  Pallas kernels  15.5 us (22%)
  local copies, waits for them, and re-layouts  1.78 us (2%)
    ppermute x17, waiting for transfers between devices, move(): return lax.ppermute(array, AXES, pairs)  33.3 us
    ppermute x17, starting transfers between devices, move(): return lax.ppermute(array, AXES, pairs)  20.8 us
    pallas_call x6, Pallas kernels, add(): pl.pallas_call(functools.partial(add_shards, tuple(names), places, slots,...  15 us
  transfers between devices with their start and end apart: 17, of which 7 were waited for; matrix products, arithmetic and copies ran while one was open for 1% of the time, Pallas kernels for 18%

profile of v9, /device:TPU:0, one launch (start us, length us, event | category | flops | bytes accessed | tf_op | source)
XLA Modules:
  0.0 71.8 jit_solution(10289425135075322763)
XLA Ops:
  0.0 0.0 copy-start
  0.0 1.3 %copy.9 = bf16[2,64,4,3,128]{4,3,0,1,2:T(4,128)(2,1)S(1)} copy(bf16[2,64,4,3,128]{4,1,3,2,0:T(8,128)(2,1)} %bitcast.32) | data formatting | bytes 786432 | tf_op jit(solution)/shard_map/reshape | solution.py:389
  1.4 0.3 reshape.222.refs_0_.refs_5_
  1.7 3.0 %collective-permute-start.3 = (bf16[4,64,768]{2,1,0:T(8,128)(2,1)S(1)}, bf16[4,64,768]{2,1,0:T(8,128)(2,1)S(1)}, u32[]{:S(2)}, u32[]{:S(2)}) collective-permute-start(bf16[4,64,768]{2,1,0:T(8,128)(2,1)S(1)} %reshape.222.refs_0_.refs_5_), channel_id=1, source_target_pairs={{0,16},{1,17},{2,18},{3,19},{4,20},{5,21},{6,22},{7,23},{8,9},{9,8... | collective-permute-start | bytes 1179656 | tf_op jit(solution)/shard_map/ppermute | solution.py:181
  4.7 2.6 %collective-permute-start = (bf16[4,64,768]{2,1,0:T(8,128)(2,1)S(1)}, bf16[4,64,768]{2,1,0:T(8,128)(2,1)S(1)}, u32[]{:S(2)}, u32[]{:S(2)}) collective-permute-start(bf16[4,64,768]{2,1,0:T(8,128)(2,1)S(1)} %reshape.222.refs_0_.refs_5_), channel_id=1, source_target_pairs={{0,4},{1,5},{2,6},{3,7},{4,0},{5,1},{6,2},{7,3},{8,12},{9,13},{10,... | collective-permute-start | bytes 1179656 | tf_op jit(solution)/shard_map/ppermute | solution.py:181
  7.3 1.6 %collective-permute-start.1 = (bf16[4,64,768]{2,1,0:T(8,128)(2,1)S(1)}, bf16[4,64,768]{2,1,0:T(8,128)(2,1)S(1)}, u32[]{:S(2)}, u32[]{:S(2)}) collective-permute-start(bf16[4,64,768]{2,1,0:T(8,128)(2,1)S(1)} %reshape.222.refs_0_.refs_5_), channel_id=1, source_target_pairs={{0,2},{1,3},{2,0},{3,1},{4,6},{5,7},{6,4},{7,5},{8,10},{9,11},{10,... | collective-permute-start | bytes 1179656 | tf_op jit(solution)/shard_map/ppermute | solution.py:181
  8.9 1.5 %collective-permute-start.2 = (bf16[4,64,768]{2,1,0:T(8,128)(2,1)S(1)}, bf16[4,64,768]{2,1,0:T(8,128)(2,1)S(1)}, u32[]{:S(2)}, u32[]{:S(2)}) collective-permute-start(bf16[4,64,768]{2,1,0:T(8,128)(2,1)S(1)} %reshape.222.refs_0_.refs_5_), channel_id=1, source_target_pairs={{0,1},{1,0},{2,3},{3,2},{4,5},{5,4},{6,7},{7,6},{8,24},{9,25},{10,... | collective-permute-start | bytes 1179656 | tf_op jit(solution)/shard_map/ppermute | solution.py:181
  10.4 0.0 copy-done
  10.4 0.1 fusion
  10.5 0.0 collective-permute-done.3.refs_1_.refs_3_
  10.6 3.4 %collective-permute-start.4 = (bf16[4,64,768]{2,1,0:T(8,128)(2,1)S(1)}, bf16[4,64,768]{2,1,0:T(8,128)(2,1)S(1)}, u32[]{:S(2)}, u32[]{:S(2)}) collective-permute-start(bf16[4,64,768]{2,1,0:T(8,128)(2,1)S(1)} %collective-permute-done.3.refs_1_.refs_3_), channel_id=1, source_target_pairs={{0,1},{1,0},{2,3},{3,2},{4,5},{5,4},{6,7},{7,6},{8,24},{9,25},{10,... | collective-permute-start | bytes 1179656 | tf_op jit(solution)/shard_map/ppermute | solution.py:181
  14.0 0.1 stack.44.place_ref
  14.1 0.1 multiply_cosine_fusion
  14.2 10.5 %collective-permute-done.refs_5_.refs_0_ = bf16[4,64,768]{2,1,0:T(8,128)(2,1)S(1)} collective-permute-done((bf16[4,64,768]{2,1,0:T(8,128)(2,1)S(1)}, bf16[4,64,768]{2,1,0:T(8,128)(2,1)S(1)}, u32[]{:S(2)}, u32[]{:S(2)}) %collective-permute-start) | collective-permute-done | bytes 393248 | tf_op jit(solution)/shard_map/ppermute | solution.py:181
  24.7 0.2 collective-permute-done.1.refs_4_.refs_1_
  24.9 0.0 collective-permute-done.2.refs_2_
  24.9 0.0 collective-permute-done.4.refs_3_.refs_4_
  24.9 0.2 shard_map.28
  25.1 0.1 collective-permute-start.5
  25.2 1.6 %collective-permute-start.7 = (bf16[2,4,64,768]{3,2,1,0:T(8,128)(2,1)S(1)}, bf16[2,4,64,768]{3,2,1,0:T(8,128)(2,1)S(1)}, u32[]{:S(2)}, u32[]{:S(2)}) collective-permute-start(bf16[2,4,64,768]{3,2,1,0:T(8,128)(2,1)S(1)} %get-tuple-element.113), channel_id=1, source_target_pairs={{0,16},{1,17},{2,18},{3,19},{4,20},{5,21},{6,22},{7,23},{8,9},{9,8... | collective-permute-start | bytes 2359304 | tf_op jit(solution)/shard_map/ppermute | solution.py:181
  26.8 0.5 collective-permute-start.8
  27.3 1.4 %collective-permute-start.6 = (bf16[4,64,768]{2,1,0:T(8,128)(2,1)S(1)}, bf16[4,64,768]{2,1,0:T(8,128)(2,1)S(1)}, u32[]{:S(2)}, u32[]{:S(2)}) collective-permute-start(bf16[4,64,768]{2,1,0:T(8,128)(2,1)S(1)} %collective-permute-done.refs_5_.refs_0_), channel_id=1, source_target_pairs={{0,2},{1,3},{2,0},{3,1},{4,6},{5,7},{6,4},{7,5},{8,10},{9,11},{10,... | collective-permute-start | bytes 1179656 | tf_op jit(solution)/shard_map/ppermute | solution.py:181
  28.7 2.5 %shard_map.29.refs_6_ = f32[2,2,256,256]{3,2,1,0:T(8,128)S(1)} custom-call(s32[7]{0:T(128)S(1)} %stack.44.place_ref, f32[8,2,128]{2,1,0:T(2,128)S(1)} %maximum_bitcast_fusion.weights_ref, bf16[4,64,768]{2,1,0:T(8,128)(2,1)S(1)} %collective-permute-done.refs_5_.refs_0_, bf16[4,64,768]{2,1,0:T(8,128)(2,1)S(1)} %collective-permute-done.1.refs_4_.refs_1_, ...), custom_call_target="tpu_custom_call" | custom-call | flops 1207959552 | bytes 4456448 | tf_op jit(solution)/shard_map/pallas_call | solution.py:234
  31.2 0.0 collective-permute-done.5.refs_4_
  31.2 2.4 %collective-permute-start.9 = (bf16[4,64,768]{2,1,0:T(8,128)(2,1)S(1)}, bf16[4,64,768]{2,1,0:T(8,128)(2,1)S(1)}, u32[]{:S(2)}, u32[]{:S(2)}) collective-permute-start(bf16[4,64,768]{2,1,0:T(8,128)(2,1)S(1)} %collective-permute-done.4.refs_3_.refs_4_), channel_id=1, source_target_pairs={{0,4},{1,5},{2,6},{3,7},{4,0},{5,1},{6,2},{7,3},{8,12},{9,13},{10,... | collective-permute-start | bytes 1179656 | tf_op jit(solution)/shard_map/ppermute | solution.py:181
  33.6 2.5 %shard_map.30.refs_6_ = f32[2,2,256,256]{3,2,1,0:T(8,128)S(1)} custom-call(s32[7]{0:T(128)S(1)} %stack.44.place_ref, f32[8,2,128]{2,1,0:T(2,128)S(1)} %maximum_bitcast_fusion.weights_ref, bf16[4,64,768]{2,1,0:T(8,128)(2,1)S(1)} %collective-permute-done.refs_5_.refs_0_, bf16[4,64,768]{2,1,0:T(8,128)(2,1)S(1)} %collective-permute-done.1.refs_4_.refs_1_, ...), custom_call_target="tpu_custom_call" | custom-call | flops 1207959552 | bytes 4456448 | tf_op jit(solution)/shard_map/pallas_call | solution.py:234
  36.1 7.4 %collective-permute-done.6.o3_ref.refs_2_.refs_0_ = bf16[4,64,768]{2,1,0:T(8,128)(2,1)S(1)} collective-permute-done((bf16[4,64,768]{2,1,0:T(8,128)(2,1)S(1)}, bf16[4,64,768]{2,1,0:T(8,128)(2,1)S(1)}, u32[]{:S(2)}, u32[]{:S(2)}) %collective-permute-start.6) | collective-permute-done | bytes 393248 | tf_op jit(solution)/shard_map/ppermute | solution.py:181
  43.5 0.5 collective-permute-start.10
  44.0 1.4 %collective-permute-done.7.a12_ref.refs_3_.refs_1_ = bf16[2,4,64,768]{3,2,1,0:T(8,128)(2,1)S(1)} collective-permute-done((bf16[2,4,64,768]{3,2,1,0:T(8,128)(2,1)S(1)}, bf16[2,4,64,768]{3,2,1,0:T(8,128)(2,1)S(1)}, u32[]{:S(2)}, u32[]{:S(2)}) %collective-permute-start.7) | collective-permute-done | bytes 786464 | tf_op jit(solution)/shard_map/ppermute | solution.py:181
  45.3 0.0 collective-permute-done.8.b12_ref.refs_4_.refs_2_
  45.3 0.1 shard_map.31
  45.5 0.1 collective-permute-start.11
  45.5 5.7 %collective-permute-done.9.refs_5_.ab2_ref = bf16[4,64,768]{2,1,0:T(8,128)(2,1)S(1)} collective-permute-done((bf16[4,64,768]{2,1,0:T(8,128)(2,1)S(1)}, bf16[4,64,768]{2,1,0:T(8,128)(2,1)S(1)}, u32[]{:S(2)}, u32[]{:S(2)}) %collective-permute-start.9) | collective-permute-done | bytes 393248 | tf_op jit(solution)/shard_map/ppermute | solution.py:181
  51.3 2.6 %shard_map.32.refs_6_ = f32[2,2,256,256]{3,2,1,0:T(8,128)S(1)} custom-call(s32[7]{0:T(128)S(1)} %stack.44.place_ref, f32[8,2,128]{2,1,0:T(2,128)S(1)} %maximum_bitcast_fusion.weights_ref, bf16[4,64,768]{2,1,0:T(8,128)(2,1)S(1)} %collective-permute-done.refs_5_.refs_0_, bf16[4,64,768]{2,1,0:T(8,128)(2,1)S(1)} %collective-permute-done.1.refs_4_.refs_1_, ...), custom_call_target="tpu_custom_call" | custom-call | flops 1207959552 | bytes 4456448 | tf_op jit(solution)/shard_map/pallas_call | solution.py:234
  53.9 0.0 collective-permute-done.10.a3_ref.refs_3_
  53.9 0.1 shard_map.33
  54.0 0.1 collective-permute-start.12
  54.1 1.6 %collective-permute-start.13 = (bf16[2,4,64,768]{3,2,1,0:T(8,128)(2,1)S(1)}, bf16[2,4,64,768]{3,2,1,0:T(8,128)(2,1)S(1)}, u32[]{:S(2)}, u32[]{:S(2)}) collective-permute-start(bf16[2,4,64,768]{3,2,1,0:T(8,128)(2,1)S(1)} %get-tuple-element.147), channel_id=1, source_target_pairs={{0,1},{1,0},{2,3},{3,2},{4,5},{5,4},{6,7},{7,6},{8,24},{9,25},{10,... | collective-permute-start | bytes 2359304 | tf_op jit(solution)/shard_map/ppermute | solution.py:181
  55.7 0.0 collective-permute-start.14
  55.7 0.0 collective-permute-done.11.refs_5_
  55.7 2.3 %shard_map.34.refs_7_ = f32[2,2,256,256]{3,2,1,0:T(8,128)S(1)} custom-call(s32[7]{0:T(128)S(1)} %stack.44.place_ref, f32[8,2,128]{2,1,0:T(2,128)S(1)} %maximum_bitcast_fusion.weights_ref, bf16[4,64,768]{2,1,0:T(8,128)(2,1)S(1)} %collective-permute-done.refs_5_.refs_0_, bf16[4,64,768]{2,1,0:T(8,128)(2,1)S(1)} %collective-permute-done.1.refs_4_.refs_1_, ...), custom_call_target="tpu_custom_call" | custom-call | flops 1006632960 | bytes 4063232 | tf_op jit(solution)/shard_map/pallas_call | solution.py:234
  58.1 7.8 %collective-permute-done.14.refs_6_ = bf16[4,64,768]{2,1,0:T(8,128)(2,1)S(1)} collective-permute-done((bf16[4,64,768]{2,1,0:T(8,128)(2,1)S(1)}, bf16[4,64,768]{2,1,0:T(8,128)(2,1)S(1)}, u32[]{:S(2)}, u32[]{:S(2)}) %collective-permute-start.14) | collective-permute-done | bytes 393248 | tf_op jit(solution)/shard_map/ppermute | solution.py:181
  65.9 0.0 collective-permute-done.12.refs_4_
  65.9 0.3 collective-permute-done.13.refs_5_
  66.2 0.0 collective-permute-start.15
  66.2 0.5 collective-permute-start.16
  66.7 2.5 %shard_map.35 = (f32[2,2,256,256]{3,2,1,0:T(8,128)S(1)}, bf16[4,2,256,768]{3,2,1,0:T(8,128)(2,1)S(1)}) custom-call(s32[7]{0:T(128)S(1)} %stack.44.place_ref, f32[8,2,128]{2,1,0:T(2,128)S(1)} %maximum_bitcast_fusion.weights_ref, bf16[4,64,768]{2,1,0:T(8,128)(2,1)S(1)} %collective-permute-done.6.o3_ref.refs_2_.refs_0_, ...), custom_call_target="tpu_custom_call" | custom-call | flops 1207959552 | bytes 4456448 | tf_op jit(solution)/shard_map/pallas_call | solution.py:234
  69.2 0.0 collective-permute-done.16.refs_1_
  69.2 0.0 collective-permute-done.15.refs_0_
  69.3 2.5 %shard_map.36 = f32[16,64,256]{2,1,0:T(8,128)} custom-call(s32[7]{0:T(128)S(1)} %stack.44.place_ref, f32[8,2,128]{2,1,0:T(2,128)S(1)} %maximum_bitcast_fusion.weights_ref, bf16[2,4,64,768]{3,2,1,0:T(8,128)(2,1)S(1)} %collective-permute-done.15.refs_0_, bf16[4,64,768]{2,1,0:T(8,128)(2,1)S(1)} %collective-permute-done.16.refs_1_, ...), custom_call_target="tpu_custom_call" | custom-call | flops 603979776 | bytes 3276800 | tf_op jit(solution)/shard_map/pallas_call | solution.py:234
  (5 shorter events, 0.1 us)
Async XLA Ops:
  0.0 10.4 %copy-start = (s32[4,3]{1,0:T(4,128)S(1)}, s32[4,3]{1,0:T(4,128)}, u32[]{:S(2)}) copy-start(s32[4,3]{1,0:T(4,128)} %param.3) | copy-start | bytes 148
  1.7 8.8 %collective-permute-start.3 = (bf16[4,64,768]{2,1,0:T(8,128)(2,1)S(1)}, bf16[4,64,768]{2,1,0:T(8,128)(2,1)S(1)}, u32[]{:S(2)}, u32[]{:S(2)}) collective-permute-start(bf16[4,64,768]{2,1,0:T(8,128)(2,1)S(1)} %reshape.222.refs_0_.refs_5_), channel_id=1, source_target_pairs={{0,16},{1,17},{2,18},{3,19},{4,20},{5,21},{6,22},{7,23},{8,9},{9,8... | collective-permute-start | bytes 1179656 | tf_op jit(solution)/shard_map/ppermute | solution.py:181
  4.7 20.0 %collective-permute-start = (bf16[4,64,768]{2,1,0:T(8,128)(2,1)S(1)}, bf16[4,64,768]{2,1,0:T(8,128)(2,1)S(1)}, u32[]{:S(2)}, u32[]{:S(2)}) collective-permute-start(bf16[4,64,768]{2,1,0:T(8,128)(2,1)S(1)} %reshape.222.refs_0_.refs_5_), channel_id=1, source_target_pairs={{0,4},{1,5},{2,6},{3,7},{4,0},{5,1},{6,2},{7,3},{8,12},{9,13},{10,... | collective-permute-start | bytes 1179656 | tf_op jit(solution)/shard_map/ppermute | solution.py:181
  7.3 17.6 %collective-permute-start.1 = (bf16[4,64,768]{2,1,0:T(8,128)(2,1)S(1)}, bf16[4,64,768]{2,1,0:T(8,128)(2,1)S(1)}, u32[]{:S(2)}, u32[]{:S(2)}) collective-permute-start(bf16[4,64,768]{2,1,0:T(8,128)(2,1)S(1)} %reshape.222.refs_0_.refs_5_), channel_id=1, source_target_pairs={{0,2},{1,3},{2,0},{3,1},{4,6},{5,7},{6,4},{7,5},{8,10},{9,11},{10,... | collective-permute-start | bytes 1179656 | tf_op jit(solution)/shard_map/ppermute | solution.py:181
  8.9 16.1 %collective-permute-start.2 = (bf16[4,64,768]{2,1,0:T(8,128)(2,1)S(1)}, bf16[4,64,768]{2,1,0:T(8,128)(2,1)S(1)}, u32[]{:S(2)}, u32[]{:S(2)}) collective-permute-start(bf16[4,64,768]{2,1,0:T(8,128)(2,1)S(1)} %reshape.222.refs_0_.refs_5_), channel_id=1, source_target_pairs={{0,1},{1,0},{2,3},{3,2},{4,5},{5,4},{6,7},{7,6},{8,24},{9,25},{10,... | collective-permute-start | bytes 1179656 | tf_op jit(solution)/shard_map/ppermute | solution.py:181
  10.6 14.4 %collective-permute-start.4 = (bf16[4,64,768]{2,1,0:T(8,128)(2,1)S(1)}, bf16[4,64,768]{2,1,0:T(8,128)(2,1)S(1)}, u32[]{:S(2)}, u32[]{:S(2)}) collective-permute-start(bf16[4,64,768]{2,1,0:T(8,128)(2,1)S(1)} %collective-permute-done.3.refs_1_.refs_3_), channel_id=1, source_target_pairs={{0,1},{1,0},{2,3},{3,2},{4,5},{5,4},{6,7},{7,6},{8,24},{9,25},{10,... | collective-permute-start | bytes 1179656 | tf_op jit(solution)/shard_map/ppermute | solution.py:181
  25.1 6.1 %collective-permute-start.5 = (bf16[6,4,64,768]{3,2,1,0:T(8,128)(2,1)S(1)}, bf16[6,4,64,768]{3,2,1,0:T(8,128)(2,1)S(1)}, u32[]{:S(2)}, u32[]{:S(2)}) collective-permute-start(bf16[6,4,64,768]{3,2,1,0:T(8,128)(2,1)S(1)} %get-tuple-element.99), channel_id=1, source_target_pairs={{0,8},{1,9},{2,10},{3,11},{4,12},{5,13},{6,14},{7,15},{8,0},{9,1},... | collective-permute-start | bytes 7077896 | tf_op jit(solution)/shard_map/ppermute | solution.py:181
  25.2 20.1 %collective-permute-start.7 = (bf16[2,4,64,768]{3,2,1,0:T(8,128)(2,1)S(1)}, bf16[2,4,64,768]{3,2,1,0:T(8,128)(2,1)S(1)}, u32[]{:S(2)}, u32[]{:S(2)}) collective-permute-start(bf16[2,4,64,768]{3,2,1,0:T(8,128)(2,1)S(1)} %get-tuple-element.113), channel_id=1, source_target_pairs={{0,16},{1,17},{2,18},{3,19},{4,20},{5,21},{6,22},{7,23},{8,9},{9,8... | collective-permute-start | bytes 2359304 | tf_op jit(solution)/shard_map/ppermute | solution.py:181
  26.8 18.6 %collective-permute-start.8 = (bf16[2,4,64,768]{3,2,1,0:T(8,128)(2,1)S(1)}, bf16[2,4,64,768]{3,2,1,0:T(8,128)(2,1)S(1)}, u32[]{:S(2)}, u32[]{:S(2)}) collective-permute-start(bf16[2,4,64,768]{3,2,1,0:T(8,128)(2,1)S(1)} %get-tuple-element.113), channel_id=1, source_target_pairs={{0,1},{1,0},{2,3},{3,2},{4,5},{5,4},{6,7},{7,6},{8,24},{9,25},{10,... | collective-permute-start | bytes 2359304 | tf_op jit(solution)/shard_map/ppermute | solution.py:181
  27.3 16.2 %collective-permute-start.6 = (bf16[4,64,768]{2,1,0:T(8,128)(2,1)S(1)}, bf16[4,64,768]{2,1,0:T(8,128)(2,1)S(1)}, u32[]{:S(2)}, u32[]{:S(2)}) collective-permute-start(bf16[4,64,768]{2,1,0:T(8,128)(2,1)S(1)} %collective-permute-done.refs_5_.refs_0_), channel_id=1, source_target_pairs={{0,2},{1,3},{2,0},{3,1},{4,6},{5,7},{6,4},{7,5},{8,10},{9,11},{10,... | collective-permute-start | bytes 1179656 | tf_op jit(solution)/shard_map/ppermute | solution.py:181
  31.2 20.0 %collective-permute-start.9 = (bf16[4,64,768]{2,1,0:T(8,128)(2,1)S(1)}, bf16[4,64,768]{2,1,0:T(8,128)(2,1)S(1)}, u32[]{:S(2)}, u32[]{:S(2)}) collective-permute-start(bf16[4,64,768]{2,1,0:T(8,128)(2,1)S(1)} %collective-permute-done.4.refs_3_.refs_4_), channel_id=1, source_target_pairs={{0,4},{1,5},{2,6},{3,7},{4,0},{5,1},{6,2},{7,3},{8,12},{9,13},{10,... | collective-permute-start | bytes 1179656 | tf_op jit(solution)/shard_map/ppermute | solution.py:181
  43.5 10.4 %collective-permute-start.10 = (bf16[4,64,768]{2,1,0:T(8,128)(2,1)S(1)}, bf16[4,64,768]{2,1,0:T(8,128)(2,1)S(1)}, u32[]{:S(2)}, u32[]{:S(2)}) collective-permute-start(bf16[4,64,768]{2,1,0:T(8,128)(2,1)S(1)} %collective-permute-done.6.o3_ref.refs_2_.refs_0_), channel_id=1, source_target_pairs={{0,16},{1,17},{2,18},{3,19},{4,20},{5,21},{6,22},{7,23},{8,9},{9,8... | collective-permute-start | bytes 1179656 | tf_op jit(solution)/shard_map/ppermute | solution.py:181
  45.5 10.2 %collective-permute-start.11 = (bf16[5,4,64,768]{3,2,1,0:T(8,128)(2,1)S(1)}, bf16[5,4,64,768]{3,2,1,0:T(8,128)(2,1)S(1)}, u32[]{:S(2)}, u32[]{:S(2)}) collective-permute-start(bf16[5,4,64,768]{3,2,1,0:T(8,128)(2,1)S(1)} %shard_map.31), channel_id=1, source_target_pairs={{0,8},{1,9},{2,10},{3,11},{4,12},{5,13},{6,14},{7,15},{8,0},{9,1},... | collective-permute-start | bytes 5898248 | tf_op jit(solution)/shard_map/ppermute | solution.py:181
  54.0 11.9 %collective-permute-start.12 = (bf16[2,4,64,768]{3,2,1,0:T(8,128)(2,1)S(1)}, bf16[2,4,64,768]{3,2,1,0:T(8,128)(2,1)S(1)}, u32[]{:S(2)}, u32[]{:S(2)}) collective-permute-start(bf16[2,4,64,768]{3,2,1,0:T(8,128)(2,1)S(1)} %get-tuple-element.146), channel_id=1, source_target_pairs={{0,8},{1,9},{2,10},{3,11},{4,12},{5,13},{6,14},{7,15},{8,0},{9,1},... | collective-permute-start | bytes 2359304 | tf_op jit(solution)/shard_map/ppermute | solution.py:181
  54.1 12.1 %collective-permute-start.13 = (bf16[2,4,64,768]{3,2,1,0:T(8,128)(2,1)S(1)}, bf16[2,4,64,768]{3,2,1,0:T(8,128)(2,1)S(1)}, u32[]{:S(2)}, u32[]{:S(2)}) collective-permute-start(bf16[2,4,64,768]{3,2,1,0:T(8,128)(2,1)S(1)} %get-tuple-element.147), channel_id=1, source_target_pairs={{0,1},{1,0},{2,3},{3,2},{4,5},{5,4},{6,7},{7,6},{8,24},{9,25},{10,... | collective-permute-start | bytes 2359304 | tf_op jit(solution)/shard_map/ppermute | solution.py:181
  55.7 10.2 %collective-permute-start.14 = (bf16[4,64,768]{2,1,0:T(8,128)(2,1)S(1)}, bf16[4,64,768]{2,1,0:T(8,128)(2,1)S(1)}, u32[]{:S(2)}, u32[]{:S(2)}) collective-permute-start(bf16[4,64,768]{2,1,0:T(8,128)(2,1)S(1)} %collective-permute-done.4.refs_3_.refs_4_), channel_id=1, source_target_pairs={{0,2},{1,3},{2,0},{3,1},{4,6},{5,7},{6,4},{7,5},{8,10},{9,11},{10,... | collective-permute-start | bytes 1179656 | tf_op jit(solution)/shard_map/ppermute | solution.py:181
  66.2 3.1 %collective-permute-start.15 = (bf16[2,4,64,768]{3,2,1,0:T(8,128)(2,1)S(1)}, bf16[2,4,64,768]{3,2,1,0:T(8,128)(2,1)S(1)}, u32[]{:S(2)}, u32[]{:S(2)}) collective-permute-start(bf16[2,4,64,768]{3,2,1,0:T(8,128)(2,1)S(1)} %collective-permute-done.13.refs_5_), channel_id=1, source_target_pairs={{0,8},{1,9},{2,10},{3,11},{4,12},{5,13},{6,14},{7,15},{8,0},{9,1},... | collective-permute-start | bytes 2359304 | tf_op jit(solution)/shard_map/ppermute | solution.py:181
  66.2 3.1 %collective-permute-start.16 = (bf16[4,64,768]{2,1,0:T(8,128)(2,1)S(1)}, bf16[4,64,768]{2,1,0:T(8,128)(2,1)S(1)}, u32[]{:S(2)}, u32[]{:S(2)}) collective-permute-start(bf16[4,64,768]{2,1,0:T(8,128)(2,1)S(1)} %collective-permute-done.14.refs_6_), channel_id=1, source_target_pairs={{0,8},{1,9},{2,10},{3,11},{4,12},{5,13},{6,14},{7,15},{8,0},{9,1},... | collective-permute-start | bytes 1179656 | tf_op jit(solution)/shard_map/ppermute | solution.py:181

commit v10 on v9

--- a/solution.py
+++ b/solution.py
@@ -50,10 +50,14 @@
     return term + lax.dot_general(left_sin, right, dims, preferred_element_type=jnp.float32)
 
 
-def add_shards(names, where, slots, has_totals, last, place_ref, weights_ref, *refs):
+def add_shards(names, where, has_totals, half, last, place_ref, weights_ref, *refs):
     refs = list(refs)
+    if half or last:
+        sems, row_ref = refs.pop(), refs.pop()
     if last:
-        sems, row_ref, far_ref, out_ref, totals_in, left_ref = (refs.pop() for _ in range(6))
+        far_ref, field_ref, _, totals_in, left_ref = (refs.pop() for _ in range(5))
+    elif half:
+        field_ref, left_ref, out_ref, totals_in = (refs.pop() for _ in range(4))
     else:
         left_ref, out_ref = refs.pop(), refs.pop()
         totals_in = refs.pop() if has_totals else None
@@ -66,27 +70,71 @@
     columns, per_block, _ = shard(names[0]).shape
     spins = left_ref.shape[2] // (2 * per_block)
 
+    def send_columns(dx, near, far):
+        lane = lax.broadcasted_iota(jnp.int32, (per_block, 2 * per_block), 1)
+        start = pl.multiple_of(jnp.bitwise_xor(pair, dx) * (2 * per_block), 2 * per_block)
+        copies = []
+        for spin in range(spins):
+            for column in range(0, columns, 2):
+                first = (spin * columns + column) * 2
+                across = slice(column * per_block, (column + 2) * per_block)
+                for part in range(2):
+                    top = (part * spins + spin) * per_block
+                    one = near(slice(top, top + per_block), across)
+                    two = far(slice(top, top + per_block), across)
+                    even = jnp.where(core == 0, one, two)
+                    odd = jnp.where(core == 0, two, one)
+                    row_ref[first + part] = jnp.where(
+                        lane < per_block, even, pltpu.roll(odd, per_block, 1)
+                    )
+                    row_ref[first + part + 2] = jnp.where(
+                        lane < per_block, pltpu.roll(even, per_block, 1), odd
+                    )
+                rows = pl.ds(first, 4)
+                target = field_ref.at[rows, :, pl.ds(start, 2 * per_block)]
+                copies.append(
+                    pltpu.make_async_copy(row_ref.at[rows], target, sems.at[len(copies)])
+                )
+                copies[-1].start()
+        return copies
+
+    slots = left_slots(names)
     if last:
-        far_ref[...] = totals_in[1]
+        far_ref[...] = totals_in[1, 1] + product(
+            left_ref[0, 0], left_ref[0, 1], shard(names[0])[...].reshape(columns * per_block, -1)
+        )
+        copies = send_columns(
+            1, lambda rows, across: totals_in[0, 1, rows, across],
+            lambda rows, across: far_ref[rows, across],
+        )
+        for copy in copies:
+            copy.wait()
+        return
+
+    copies = []
+    if half:
+        copies = send_columns(
+            0, lambda rows, across: totals_in[0, 0, rows, across],
+            lambda rows, across: totals_in[1, 0, rows, across],
+        )
+    if has_totals:
+        out_ref[...] = totals_in[...]
     else:
-        if has_totals:
-            out_ref[...] = totals_in[...]
+        out_ref[...] = jnp.zeros_like(out_ref)
+    for slot, (dy, dz) in enumerate(slots):
+        site = jnp.bitwise_xor(level, dz) * flat + jnp.bitwise_xor(beside, dy)
+        if dy == 0:
+            owns = [shard(("near", "O", dz))[first_s + s] for s in range(spins)]
         else:
-            out_ref[...] = jnp.zeros_like(out_ref)
-        for slot, (dy, dz) in enumerate(slots):
-            site = jnp.bitwise_xor(level, dz) * flat + jnp.bitwise_xor(beside, dy)
-            if dy == 0:
-                owns = [shard(("near", "O", dz))[first_s + s] for s in range(spins)]
-            else:
-                owns = [
-                    jnp.where(
-                        core == 0,
-                        shard(("near", "B", dz))[first_s + s],
-                        shard(("near", "A", dz))[first_s + s],
-                    )
-                    for s in range(spins)
-                ]
-            left_ref[slot, 0], left_ref[slot, 1] = left_sides(owns, weights_ref[site])
+            owns = [
+                jnp.where(
+                    core == 0,
+                    shard(("near", "B", dz))[first_s + s],
+                    shard(("near", "A", dz))[first_s + s],
+                )
+                for s in range(spins)
+            ]
+        left_ref[slot, 0], left_ref[slot, 1] = left_sides(owns, weights_ref[site])
 
     for side, kind, dz in names:
         right = shard((side, kind, dz))[...].reshape(columns * per_block, -1)
@@ -96,41 +144,11 @@
             slot = slots.index((dy, dz))
         else:
             slot = slots.index((0, dz)) + dy
-        term = product(left_ref[slot, 0], left_ref[slot, 1], right)
-        if last:
-            far_ref[dx] += term
-        else:
-            out_ref[0 if side == "near" else 1, dx] += term
-
-    if last:
-        lane = lax.broadcasted_iota(jnp.int32, (per_block, 2 * per_block), 1)
-        copies = []
-        for spin in range(spins):
-            for column in range(0, columns, 2):
-                first = (spin * columns + column) * 2
-                across = pl.ds(column * per_block, 2 * per_block)
-                for part in range(2):
-                    top = (part * spins + spin) * per_block
-                    for p in range(2):
-                        dx = jnp.bitwise_xor(pair, p)
-                        near = totals_in[0, dx, pl.ds(top, per_block), across]
-                        far = far_ref[dx, pl.ds(top, per_block), across]
-                        even = jnp.where(core == 0, near, far)
-                        odd = jnp.where(core == 0, far, near)
-                        place = pl.ds(p * 2 * per_block, 2 * per_block)
-                        row_ref[first + part, :, place] = jnp.where(
-                            lane < per_block, even, pltpu.roll(odd, per_block, 1)
-                        )
-                        row_ref[first + part + 2, :, place] = jnp.where(
-                            lane < per_block, pltpu.roll(even, per_block, 1), odd
-                        )
-                rows = pl.ds(first, 4)
-                copies.append(
-                    pltpu.make_async_copy(row_ref.at[rows], out_ref.at[rows], sems.at[len(copies)])
-                )
-                copies[-1].start()
-        for copy in copies:
-            copy.wait()
+        out_ref[0 if side == "near" else 1, dx] += product(
+            left_ref[slot, 0], left_ref[slot, 1], right
+        )
+    for copy in copies:
+        copy.wait()
 
 
 def route_second(*refs):
@@ -147,11 +165,9 @@
     stack_ref[3:5] = b12_ref[...]
 
 
-def route_fourth(a3_ref, ab2_ref, o3_ref, stack_ref, both_ref):
-    stack_ref[0] = a3_ref[...]
-    stack_ref[1] = ab2_ref[...]
-    both_ref[0] = a3_ref[...]
-    both_ref[1] = o3_ref[...]
+def route_fourth(*refs):
+    for slot in range(4):
+        refs[4][slot] = refs[slot][...]
 
 
 def left_slots(names):
@@ -204,39 +220,43 @@
         key, slot = where[("near", kind, dz)]
         return arrays[key] if slot is None else arrays[key][slot]
 
-    def add(names, totals, keep=False, left=None, slots=None):
+    def add(names, totals, half=False, left=None, field=None):
         last = left is not None
-        slots = slots or left_slots(names)
+        slots = left_slots(names)
         uses = list(names)
         for dy, dz in [] if last else slots:
             uses += [("near", kind, dz) for kind in (("A", "B") if dy else ("O",))]
         keys = sorted({where[name][0] for name in uses})
         places = {name: (keys.index(where[name][0]), where[name][1]) for name in uses}
         operands = [place, weights] + [arrays[key] for key in keys]
-        operands += [each for each in (left, totals) if each is not None]
+        operands += [each for each in (left, totals, field) if each is not None]
         total_shape = (2, 2, tall, wide)
         left_shape = (len(slots), 2, tall, depth)
-        block = pl.BlockSpec(memory_space=pltpu.VMEM)
-        out_shape = [jax.ShapeDtypeStruct(total_shape, jnp.float32)]
-        scratch = [pltpu.VMEM(left_shape, jnp.bfloat16)]
-        out_specs = [block]
+        field_shape = (share, per_block, 4 * per_block)
+        block, apart = (pl.BlockSpec(memory_space=space) for space in (pltpu.VMEM, pltpu.HBM))
+        in_specs = [pl.BlockSpec(memory_space=pltpu.SMEM)] + [block] * (len(operands) - 1)
+        out_shape, out_specs = [jax.ShapeDtypeStruct(total_shape, jnp.float32)], [block]
+        scratch, aliases = [pltpu.VMEM(left_shape, jnp.bfloat16)], {}
+        if half:
+            out_shape.append(jax.ShapeDtypeStruct(left_shape, jnp.bfloat16))
+            out_specs.append(block)
+            scratch = []
         if last:
-            out_shape = [jax.ShapeDtypeStruct((share, per_block, 4 * per_block), jnp.float32)]
-            out_specs = [pl.BlockSpec(memory_space=pl.ANY)]
-            scratch = [
-                pltpu.VMEM(total_shape[1:], jnp.float32),
-                pltpu.VMEM(out_shape[0].shape, jnp.float32),
-                pltpu.SemaphoreType.DMA((spins * columns // 2,)),
-            ]
-        if keep:
-            out_shape.append(jax.ShapeDtypeStruct(left_shape, jnp.bfloat16))
-            out_specs, scratch = [block] * 2, []
+            out_shape, out_specs, scratch = [], [], [pltpu.VMEM(total_shape[2:], jnp.float32)]
+            in_specs[-1] = apart
+            aliases = {len(operands) - 1: 0}
+        if half or last:
+            out_shape.append(jax.ShapeDtypeStruct(field_shape, jnp.float32))
+            out_specs.append(apart)
+            scratch.append(pltpu.VMEM((*field_shape[:2], 2 * per_block), jnp.float32))
+            scratch.append(pltpu.SemaphoreType.DMA((spins * columns // 2,)))
         out = pl.pallas_call(
-            functools.partial(add_shards, tuple(names), places, slots, totals is not None, last),
-            in_specs=[pl.BlockSpec(memory_space=pltpu.SMEM)] + [block] * (len(operands) - 1),
+            functools.partial(add_shards, tuple(names), places, totals is not None, half, last),
+            in_specs=in_specs,
             out_specs=out_specs,
             out_shape=out_shape,
             scratch_shapes=scratch,
+            input_output_aliases=aliases,
             compiler_params=pltpu.CompilerParams(vmem_limit_bytes=40 * 1024 * 1024),
             cost_estimate=pl.CostEstimate(
                 flops=4 * tall * wide * depth * len(names),
@@ -244,7 +264,7 @@
                 transcendentals=0,
             ),
         )(*operands)
-        return out if keep else out[0]
+        return out if half else out[0]
 
     def fence(totals):
         nonlocal arrays
@@ -275,8 +295,8 @@
 
     first = [("O", 0), ("A", 0), ("B", 0), ("AB", 0), ("O", 1), ("O", 2)]
     second = [("O", 3), ("A", 1), ("A", 2), ("B", 1), ("B", 2)]
-    third = [("A", 3), ("AB", 2)]
-    fourth = [("AB", 3), ("B", 3), ("AB", 1)]
+    third = [("A", 3), ("B", 3), ("AB", 1), ("AB", 2)]
+    fourth = [("AB", 3)]
     stack, both = route(route_second, [near(*kind) for kind in first], (6, 2))
     totals = add([("near", *kind) for kind in first], None)
     o3, a12, b12 = hop_z(near("O", 2), 1), hop_a(both), hop_b(both)
@@ -286,37 +306,36 @@
     ab2 = hop_z(near("AB", 0), 2)
     totals = add([("far", *kind) for kind in first], totals)
     put("2b", o3, "near", second[:1])
-    totals = fence(totals)
-
-    a3 = hop_a(near("O", 3))
     put("2c", a12, "near", second[1:3])
     put("2d", b12, "near", second[3:5])
     totals = fence(totals)
 
     (stack,) = route(route_third, [arrays[key] for key in ("2b", "2c", "2d")], (5,))
+    a3, b3, ab1 = hop_a(near("O", 3)), hop_b(near("O", 3)), hop_z(near("AB", 0), 1)
     far2 = swap(stack)
-    put("3b", ab2, "near", third[1:])
-    totals = add([("near", *kind) for kind in second + third[1:]], totals)
-    a3, totals = lax.optimization_barrier((a3, totals))
-    stack, both = route(route_fourth, [a3, ab2, near("O", 3)], (2, 2), weight=10**11)
+    put("3d", ab2, "near", third[3:])
+    totals = add([("near", *kind) for kind in second + third[3:]], totals)
+    a3, b3, ab1, totals = lax.optimization_barrier((a3, b3, ab1, totals))
+    (stack,) = route(route_fourth, [a3, b3, ab1, ab2], (4,), weight=10**11)
     put("3a", a3, "near", third[:1])
+    put("3b", b3, "near", third[1:2])
+    put("3c", ab1, "near", third[2:3])
     totals = fence(totals)
 
-    b3, ab1, far3 = hop_b(both), hop_z(near("AB", 0), 1), swap(stack)
-    put("3d", far2, "far", second)
-    totals = add([("far", *kind) for kind in second], totals)
-    put("3e", far3, "far", third)
-    put("4a", b3, "near", fourth[:2])
-    put("4b", ab1, "near", fourth[2:])
+    ab3, far3 = hop_b(near("A", 3)), swap(stack)
+    put("3e", far2, "far", second)
+    names = [("near", *kind) for kind in third[:3]] + [("far", *kind) for kind in second]
+    totals = add(names, totals)
+    put("3f", far3, "far", third)
+    totals = add([("far", *kind) for kind in third], totals)
+    put("4a", ab3, "near", fourth)
     totals = fence(totals)
 
-    new = [swap(arrays["4a"]), swap(arrays["4b"])]
-    names = [("near", *kind) for kind in fourth + third[:1]] + [("far", *kind) for kind in third]
-    totals, left = add(names, totals, keep=True)
-    put("5a", new[0], "far", fourth[:2])
-    put("5b", new[1], "far", fourth[2:])
-    totals, left = fence((totals, left))
-    return add([("far", *kind) for kind in fourth], totals, left=left, slots=left_slots(names))
+    far4 = swap(arrays["4a"])
+    totals, left, field = add([("near", *kind) for kind in fourth], totals, half=True)
+    put("4b", far4, "far", fourth)
+    totals, left, field = fence((totals, left, field))
+    return add([("far", *kind) for kind in fourth], totals, left=left, field=field)
 
 
 def add_terms(place_ref, weights_ref, left_ref, right_ref, field_ref):

time: 71.9 us -> 71.5 us (level)
  waiting for transfers between devices: 33.3 us -> 29 us
  starting transfers between devices: 20.8 us -> 23 us
  Pallas kernels: 15.5 us -> 17 us
    ppermute x17, waiting for transfers between devices: 33.3 us -> 29 us  [move(): return lax.ppermute(array, AXES, pairs)]
    ppermute x17, starting transfers between devices: 20.8 us -> 23 us  [move(): return lax.ppermute(array, AXES, pairs)]
    pallas_call x6 -> x7, Pallas kernels: 15 us -> 16.6 us  [add(): pl.pallas_call(functools.partial(add_shards, tuple(names), places, totals...]
  transfers between devices with their start and end apart: 17 -> 17, of which waited for: 7 -> 8; matrix products, arithmetic and copies ran while one was open for 1% -> 1% of each run, Pallas kernels for 18% -> 21%
where the time goes in v10:
time: 71.5 us; the launch traced here: 71.3 us
  waiting for transfers between devices  29 us (41%)
  starting transfers between devices  23 us (32%)
  Pallas kernels  17 us (24%)
  local copies, waits for them, and re-layouts  1.78 us (2%)
    ppermute x17, waiting for transfers between devices, move(): return lax.ppermute(array, AXES, pairs)  29 us
    ppermute x17, starting transfers between devices, move(): return lax.ppermute(array, AXES, pairs)  23 us
    pallas_call x7, Pallas kernels, add(): pl.pallas_call(functools.partial(add_shards, tuple(names), places, totals...  16.6 us
  transfers between devices with their start and end apart: 17, of which 8 were waited for; matrix products, arithmetic and copies ran while one was open for 1% of the time, Pallas kernels for 21%

profile of v10, /device:TPU:0, one launch (start us, length us, event | category | flops | bytes accessed | tf_op | source)
XLA Modules:
  0.0 71.3 jit_solution(18261338694906027146)
XLA Ops:
  0.0 0.0 copy-start
  0.0 1.3 %copy.10 = bf16[2,64,4,3,128]{4,3,0,1,2:T(4,128)(2,1)S(1)} copy(bf16[2,64,4,3,128]{4,1,3,2,0:T(8,128)(2,1)} %bitcast.32) | data formatting | bytes 786432 | tf_op jit(solution)/shard_map/reshape | solution.py:408
  1.4 0.3 reshape.222.refs_0_.refs_5_
  1.7 3.0 %collective-permute-start.3 = (bf16[4,64,768]{2,1,0:T(8,128)(2,1)S(1)}, bf16[4,64,768]{2,1,0:T(8,128)(2,1)S(1)}, u32[]{:S(2)}, u32[]{:S(2)}) collective-permute-start(bf16[4,64,768]{2,1,0:T(8,128)(2,1)S(1)} %reshape.222.refs_0_.refs_5_), channel_id=1, source_target_pairs={{0,16},{1,17},{2,18},{3,19},{4,20},{5,21},{6,22},{7,23},{8,9},{9,8... | collective-permute-start | bytes 1179656 | tf_op jit(solution)/shard_map/ppermute | solution.py:197
  4.7 2.6 %collective-permute-start = (bf16[4,64,768]{2,1,0:T(8,128)(2,1)S(1)}, bf16[4,64,768]{2,1,0:T(8,128)(2,1)S(1)}, u32[]{:S(2)}, u32[]{:S(2)}) collective-permute-start(bf16[4,64,768]{2,1,0:T(8,128)(2,1)S(1)} %reshape.222.refs_0_.refs_5_), channel_id=1, source_target_pairs={{0,4},{1,5},{2,6},{3,7},{4,0},{5,1},{6,2},{7,3},{8,12},{9,13},{10,... | collective-permute-start | bytes 1179656 | tf_op jit(solution)/shard_map/ppermute | solution.py:197
  7.3 1.6 %collective-permute-start.1 = (bf16[4,64,768]{2,1,0:T(8,128)(2,1)S(1)}, bf16[4,64,768]{2,1,0:T(8,128)(2,1)S(1)}, u32[]{:S(2)}, u32[]{:S(2)}) collective-permute-start(bf16[4,64,768]{2,1,0:T(8,128)(2,1)S(1)} %reshape.222.refs_0_.refs_5_), channel_id=1, source_target_pairs={{0,2},{1,3},{2,0},{3,1},{4,6},{5,7},{6,4},{7,5},{8,10},{9,11},{10,... | collective-permute-start | bytes 1179656 | tf_op jit(solution)/shard_map/ppermute | solution.py:197
  8.9 1.5 %collective-permute-start.2 = (bf16[4,64,768]{2,1,0:T(8,128)(2,1)S(1)}, bf16[4,64,768]{2,1,0:T(8,128)(2,1)S(1)}, u32[]{:S(2)}, u32[]{:S(2)}) collective-permute-start(bf16[4,64,768]{2,1,0:T(8,128)(2,1)S(1)} %reshape.222.refs_0_.refs_5_), channel_id=1, source_target_pairs={{0,1},{1,0},{2,3},{3,2},{4,5},{5,4},{6,7},{7,6},{8,24},{9,25},{10,... | collective-permute-start | bytes 1179656 | tf_op jit(solution)/shard_map/ppermute | solution.py:197
  10.4 0.0 copy-done
  10.4 0.1 fusion
  10.5 0.0 collective-permute-done.3.refs_1_.refs_3_
  10.6 3.4 %collective-permute-start.4 = (bf16[4,64,768]{2,1,0:T(8,128)(2,1)S(1)}, bf16[4,64,768]{2,1,0:T(8,128)(2,1)S(1)}, u32[]{:S(2)}, u32[]{:S(2)}) collective-permute-start(bf16[4,64,768]{2,1,0:T(8,128)(2,1)S(1)} %collective-permute-done.3.refs_1_.refs_3_), channel_id=1, source_target_pairs={{0,1},{1,0},{2,3},{3,2},{4,5},{5,4},{6,7},{7,6},{8,24},{9,25},{10,... | collective-permute-start | bytes 1179656 | tf_op jit(solution)/shard_map/ppermute | solution.py:197
  14.0 0.1 stack.44.place_ref
  14.1 0.1 multiply_cosine_fusion
  14.2 10.5 %collective-permute-done.refs_5_.refs_0_ = bf16[4,64,768]{2,1,0:T(8,128)(2,1)S(1)} collective-permute-done((bf16[4,64,768]{2,1,0:T(8,128)(2,1)S(1)}, bf16[4,64,768]{2,1,0:T(8,128)(2,1)S(1)}, u32[]{:S(2)}, u32[]{:S(2)}) %collective-permute-start) | collective-permute-done | bytes 393248 | tf_op jit(solution)/shard_map/ppermute | solution.py:197
  24.7 0.2 collective-permute-done.1.refs_4_.refs_1_
  24.9 0.0 collective-permute-done.2.refs_2_
  24.9 0.0 collective-permute-done.4.refs_3_.refs_4_
  24.9 0.2 shard_map.28
  25.1 0.1 collective-permute-start.5
  25.2 1.6 %collective-permute-start.7 = (bf16[2,4,64,768]{3,2,1,0:T(8,128)(2,1)S(1)}, bf16[2,4,64,768]{3,2,1,0:T(8,128)(2,1)S(1)}, u32[]{:S(2)}, u32[]{:S(2)}) collective-permute-start(bf16[2,4,64,768]{3,2,1,0:T(8,128)(2,1)S(1)} %get-tuple-element.98), channel_id=1, source_target_pairs={{0,16},{1,17},{2,18},{3,19},{4,20},{5,21},{6,22},{7,23},{8,9},{9,8... | collective-permute-start | bytes 2359304 | tf_op jit(solution)/shard_map/ppermute | solution.py:197
  26.8 0.5 collective-permute-start.8
  27.3 1.4 %collective-permute-start.6 = (bf16[4,64,768]{2,1,0:T(8,128)(2,1)S(1)}, bf16[4,64,768]{2,1,0:T(8,128)(2,1)S(1)}, u32[]{:S(2)}, u32[]{:S(2)}) collective-permute-start(bf16[4,64,768]{2,1,0:T(8,128)(2,1)S(1)} %collective-permute-done.refs_5_.refs_0_), channel_id=1, source_target_pairs={{0,2},{1,3},{2,0},{3,1},{4,6},{5,7},{6,4},{7,5},{8,10},{9,11},{10,... | collective-permute-start | bytes 1179656 | tf_op jit(solution)/shard_map/ppermute | solution.py:197
  28.7 2.5 %shard_map.29.refs_6_ = f32[2,2,256,256]{3,2,1,0:T(8,128)S(1)} custom-call(s32[7]{0:T(128)S(1)} %stack.44.place_ref, f32[8,2,128]{2,1,0:T(2,128)S(1)} %maximum_bitcast_fusion.weights_ref, bf16[4,64,768]{2,1,0:T(8,128)(2,1)S(1)} %collective-permute-done.refs_5_.refs_0_, bf16[4,64,768]{2,1,0:T(8,128)(2,1)S(1)} %collective-permute-done.1.refs_4_.refs_1_, ...), custom_call_target="tpu_custom_call" | custom-call | flops 1207959552 | bytes 4456448 | tf_op jit(solution)/shard_map/pallas_call | solution.py:253
  31.2 0.0 collective-permute-done.5.refs_4_
  31.2 2.4 %collective-permute-start.9 = (bf16[4,64,768]{2,1,0:T(8,128)(2,1)S(1)}, bf16[4,64,768]{2,1,0:T(8,128)(2,1)S(1)}, u32[]{:S(2)}, u32[]{:S(2)}) collective-permute-start(bf16[4,64,768]{2,1,0:T(8,128)(2,1)S(1)} %collective-permute-done.4.refs_3_.refs_4_), channel_id=1, source_target_pairs={{0,4},{1,5},{2,6},{3,7},{4,0},{5,1},{6,2},{7,3},{8,12},{9,13},{10,... | collective-permute-start | bytes 1179656 | tf_op jit(solution)/shard_map/ppermute | solution.py:197
  33.6 2.5 %shard_map.30.refs_6_ = f32[2,2,256,256]{3,2,1,0:T(8,128)S(1)} custom-call(s32[7]{0:T(128)S(1)} %stack.44.place_ref, f32[8,2,128]{2,1,0:T(2,128)S(1)} %maximum_bitcast_fusion.weights_ref, bf16[4,64,768]{2,1,0:T(8,128)(2,1)S(1)} %collective-permute-done.refs_5_.refs_0_, bf16[4,64,768]{2,1,0:T(8,128)(2,1)S(1)} %collective-permute-done.1.refs_4_.refs_1_, ...), custom_call_target="tpu_custom_call" | custom-call | flops 1207959552 | bytes 4456448 | tf_op jit(solution)/shard_map/pallas_call | solution.py:253
  36.1 7.4 %collective-permute-done.6.o3_ref.refs_2_.refs_0_ = bf16[4,64,768]{2,1,0:T(8,128)(2,1)S(1)} collective-permute-done((bf16[4,64,768]{2,1,0:T(8,128)(2,1)S(1)}, bf16[4,64,768]{2,1,0:T(8,128)(2,1)S(1)}, u32[]{:S(2)}, u32[]{:S(2)}) %collective-permute-start.6) | collective-permute-done | bytes 393248 | tf_op jit(solution)/shard_map/ppermute | solution.py:197
  43.5 1.8 %collective-permute-done.7.a12_ref.refs_3_.refs_1_ = bf16[2,4,64,768]{3,2,1,0:T(8,128)(2,1)S(1)} collective-permute-done((bf16[2,4,64,768]{3,2,1,0:T(8,128)(2,1)S(1)}, bf16[2,4,64,768]{3,2,1,0:T(8,128)(2,1)S(1)}, u32[]{:S(2)}, u32[]{:S(2)}) %collective-permute-start.7) | collective-permute-done | bytes 786464 | tf_op jit(solution)/shard_map/ppermute | solution.py:197
  45.3 0.0 collective-permute-done.8.b12_ref.refs_4_.refs_2_
  45.3 0.1 shard_map.31
  45.5 1.6 %collective-permute-start.10 = (bf16[4,64,768]{2,1,0:T(8,128)(2,1)S(1)}, bf16[4,64,768]{2,1,0:T(8,128)(2,1)S(1)}, u32[]{:S(2)}, u32[]{:S(2)}) collective-permute-start(bf16[4,64,768]{2,1,0:T(8,128)(2,1)S(1)} %collective-permute-done.6.o3_ref.refs_2_.refs_0_), channel_id=1, source_target_pairs={{0,16},{1,17},{2,18},{3,19},{4,20},{5,21},{6,22},{7,23},{8,9},{9,8... | collective-permute-start | bytes 1179656 | tf_op jit(solution)/shard_map/ppermute | solution.py:197
  47.1 0.3 collective-permute-start.11
  47.4 1.4 %collective-permute-start.12 = (bf16[4,64,768]{2,1,0:T(8,128)(2,1)S(1)}, bf16[4,64,768]{2,1,0:T(8,128)(2,1)S(1)}, u32[]{:S(2)}, u32[]{:S(2)}) collective-permute-start(bf16[4,64,768]{2,1,0:T(8,128)(2,1)S(1)} %collective-permute-done.4.refs_3_.refs_4_), channel_id=1, source_target_pairs={{0,2},{1,3},{2,0},{3,1},{4,6},{5,7},{6,4},{7,5},{8,10},{9,11},{10,... | collective-permute-start | bytes 1179656 | tf_op jit(solution)/shard_map/ppermute | solution.py:197
  48.8 0.0 collective-permute-start.13
  48.8 2.6 %collective-permute-done.9.refs_5_.refs_3_ = bf16[4,64,768]{2,1,0:T(8,128)(2,1)S(1)} collective-permute-done((bf16[4,64,768]{2,1,0:T(8,128)(2,1)S(1)}, bf16[4,64,768]{2,1,0:T(8,128)(2,1)S(1)}, u32[]{:S(2)}, u32[]{:S(2)}) %collective-permute-start.9) | collective-permute-done | bytes 393248 | tf_op jit(solution)/shard_map/ppermute | solution.py:197
  51.4 2.6 %shard_map.32.refs_9_ = f32[2,2,256,256]{3,2,1,0:T(8,128)S(1)} custom-call(s32[7]{0:T(128)S(1)} %stack.44.place_ref, f32[8,2,128]{2,1,0:T(2,128)S(1)} %maximum_bitcast_fusion.weights_ref, bf16[4,64,768]{2,1,0:T(8,128)(2,1)S(1)} %collective-permute-done.refs_5_.refs_0_, bf16[4,64,768]{2,1,0:T(8,128)(2,1)S(1)} %collective-permute-done.1.refs_4_.refs_1_, ...), custom_call_target="tpu_custom_call" | custom-call | flops 1207959552 | bytes 4456448 | tf_op jit(solution)/shard_map/pallas_call | solution.py:253
  54.0 3.2 %collective-permute-done.10.refs_0_.refs_5_.refs_3_ = bf16[4,64,768]{2,1,0:T(8,128)(2,1)S(1)} collective-permute-done((bf16[4,64,768]{2,1,0:T(8,128)(2,1)S(1)}, bf16[4,64,768]{2,1,0:T(8,128)(2,1)S(1)}, u32[]{:S(2)}, u32[]{:S(2)}) %collective-permute-start.10) | collective-permute-done | bytes 393248 | tf_op jit(solution)/shard_map/ppermute | solution.py:197
  57.2 0.0 collective-permute-done.11.refs_1_.refs_6_.refs_4_
  57.2 2.5 %collective-permute-done.12.refs_2_.refs_7_ = bf16[4,64,768]{2,1,0:T(8,128)(2,1)S(1)} collective-permute-done((bf16[4,64,768]{2,1,0:T(8,128)(2,1)S(1)}, bf16[4,64,768]{2,1,0:T(8,128)(2,1)S(1)}, u32[]{:S(2)}, u32[]{:S(2)}) %collective-permute-start.12) | collective-permute-done | bytes 393248 | tf_op jit(solution)/shard_map/ppermute | solution.py:197
  59.7 0.1 shard_map.33
  59.8 0.1 collective-permute-start.14
  59.9 1.6 %collective-permute-start.15 = (bf16[4,64,768]{2,1,0:T(8,128)(2,1)S(1)}, bf16[4,64,768]{2,1,0:T(8,128)(2,1)S(1)}, u32[]{:S(2)}, u32[]{:S(2)}) collective-permute-start(bf16[4,64,768]{2,1,0:T(8,128)(2,1)S(1)} %collective-permute-done.10.refs_0_.refs_5_.refs_3_), channel_id=1, source_target_pairs={{0,1},{1,0},{2,3},{3,2},{4,5},{5,4},{6,7},{7,6},{8,24},{9,25},{10,... | collective-permute-start | bytes 1179656 | tf_op jit(solution)/shard_map/ppermute | solution.py:197
  61.5 0.0 collective-permute-done.13.refs_8_
  61.5 3.2 %shard_map.34.refs_6_ = f32[2,2,256,256]{3,2,1,0:T(8,128)S(1)} custom-call(s32[7]{0:T(128)S(1)} %stack.44.place_ref, f32[8,2,128]{2,1,0:T(2,128)S(1)} %maximum_bitcast_fusion.weights_ref, bf16[4,64,768]{2,1,0:T(8,128)(2,1)S(1)} %collective-permute-done.refs_5_.refs_0_, bf16[4,64,768]{2,1,0:T(8,128)(2,1)S(1)} %collective-permute-done.1.refs_4_.refs_1_, ...), custom_call_target="tpu_custom_call" | custom-call | flops 1610612736 | bytes 5242880 | tf_op jit(solution)/shard_map/pallas_call | solution.py:253
  64.7 0.0 collective-permute-done.14.refs_5_
  64.7 2.1 %shard_map.35.refs_3_ = f32[2,2,256,256]{3,2,1,0:T(8,128)S(1)} custom-call(s32[7]{0:T(128)S(1)} %stack.44.place_ref, f32[8,2,128]{2,1,0:T(2,128)S(1)} %maximum_bitcast_fusion.weights_ref, bf16[4,64,768]{2,1,0:T(8,128)(2,1)S(1)} %collective-permute-done.6.o3_ref.refs_2_.refs_0_, bf16[2,4,64,768]{3,2,1,0:T(8,128)(2,1)S(1)} %collective-permute-done.7.a12_ref.refs_3_.refs_1_, ...), custom_call_target="tpu_custom_call" | custom-call | flops 805306368 | bytes 3670016 | tf_op jit(solution)/shard_map/pallas_call | solution.py:253
  66.8 0.9 %collective-permute-done.15.refs_2_ = bf16[4,64,768]{2,1,0:T(8,128)(2,1)S(1)} collective-permute-done((bf16[4,64,768]{2,1,0:T(8,128)(2,1)S(1)}, bf16[4,64,768]{2,1,0:T(8,128)(2,1)S(1)}, u32[]{:S(2)}, u32[]{:S(2)}) %collective-permute-start.15) | collective-permute-done | bytes 393248 | tf_op jit(solution)/shard_map/ppermute | solution.py:197
  67.7 0.0 collective-permute-start.16
  67.7 1.7 %shard_map.36 = (f32[2,2,256,256]{3,2,1,0:T(8,128)S(1)}, bf16[1,2,256,768]{3,2,1,0:T(8,128)(2,1)S(1)}, f32[16,64,256]{2,1,0:T(8,128)}) custom-call(s32[7]{0:T(128)S(1)} %stack.44.place_ref, f32[8,2,128]{2,1,0:T(2,128)S(1)} %maximum_bitcast_fusion.weights_ref, bf16[4,64,768]{2,1,0:T(8,128)(2,1)S(1)} %collective-permute-done.10.refs_0_.refs_5_.refs_3_, ...), custom_call_target="tpu_custom_call" | custom-call | flops 201326592 | bytes 2490368 | tf_op jit(solution)/shard_map/pallas_call | solution.py:253
  69.4 0.0 collective-permute-done.16.refs_0_
  69.5 1.9 %shard_map.37 = f32[16,64,256]{2,1,0:T(8,128)} custom-call(s32[7]{0:T(128)S(1)} %stack.44.place_ref, f32[8,2,128]{2,1,0:T(2,128)S(1)} %maximum_bitcast_fusion.weights_ref, bf16[4,64,768]{2,1,0:T(8,128)(2,1)S(1)} %collective-permute-done.16.refs_0_, bf16[1,2,256,768]{3,2,1,0:T(8,128)(2,1)S(1)} %get-tuple-element.142.refs_1_, ...), custom_call_target="tpu_custom_call", output_to_operand_aliasing={{}: (5, {})} | custom-call | flops 201326592 | bytes 2490368 | tf_op jit(solution)/shard_map/pallas_call | solution.py:253
  (5 shorter events, 0.1 us)
Async XLA Ops:
  0.0 10.4 %copy-start = (s32[4,3]{1,0:T(4,128)S(1)}, s32[4,3]{1,0:T(4,128)}, u32[]{:S(2)}) copy-start(s32[4,3]{1,0:T(4,128)} %param.3) | copy-start | bytes 148
  1.7 8.8 %collective-permute-start.3 = (bf16[4,64,768]{2,1,0:T(8,128)(2,1)S(1)}, bf16[4,64,768]{2,1,0:T(8,128)(2,1)S(1)}, u32[]{:S(2)}, u32[]{:S(2)}) collective-permute-start(bf16[4,64,768]{2,1,0:T(8,128)(2,1)S(1)} %reshape.222.refs_0_.refs_5_), channel_id=1, source_target_pairs={{0,16},{1,17},{2,18},{3,19},{4,20},{5,21},{6,22},{7,23},{8,9},{9,8... | collective-permute-start | bytes 1179656 | tf_op jit(solution)/shard_map/ppermute | solution.py:197
  4.7 20.0 %collective-permute-start = (bf16[4,64,768]{2,1,0:T(8,128)(2,1)S(1)}, bf16[4,64,768]{2,1,0:T(8,128)(2,1)S(1)}, u32[]{:S(2)}, u32[]{:S(2)}) collective-permute-start(bf16[4,64,768]{2,1,0:T(8,128)(2,1)S(1)} %reshape.222.refs_0_.refs_5_), channel_id=1, source_target_pairs={{0,4},{1,5},{2,6},{3,7},{4,0},{5,1},{6,2},{7,3},{8,12},{9,13},{10,... | collective-permute-start | bytes 1179656 | tf_op jit(solution)/shard_map/ppermute | solution.py:197
  7.3 17.6 %collective-permute-start.1 = (bf16[4,64,768]{2,1,0:T(8,128)(2,1)S(1)}, bf16[4,64,768]{2,1,0:T(8,128)(2,1)S(1)}, u32[]{:S(2)}, u32[]{:S(2)}) collective-permute-start(bf16[4,64,768]{2,1,0:T(8,128)(2,1)S(1)} %reshape.222.refs_0_.refs_5_), channel_id=1, source_target_pairs={{0,2},{1,3},{2,0},{3,1},{4,6},{5,7},{6,4},{7,5},{8,10},{9,11},{10,... | collective-permute-start | bytes 1179656 | tf_op jit(solution)/shard_map/ppermute | solution.py:197
  8.9 16.1 %collective-permute-start.2 = (bf16[4,64,768]{2,1,0:T(8,128)(2,1)S(1)}, bf16[4,64,768]{2,1,0:T(8,128)(2,1)S(1)}, u32[]{:S(2)}, u32[]{:S(2)}) collective-permute-start(bf16[4,64,768]{2,1,0:T(8,128)(2,1)S(1)} %reshape.222.refs_0_.refs_5_), channel_id=1, source_target_pairs={{0,1},{1,0},{2,3},{3,2},{4,5},{5,4},{6,7},{7,6},{8,24},{9,25},{10,... | collective-permute-start | bytes 1179656 | tf_op jit(solution)/shard_map/ppermute | solution.py:197
  10.6 14.4 %collective-permute-start.4 = (bf16[4,64,768]{2,1,0:T(8,128)(2,1)S(1)}, bf16[4,64,768]{2,1,0:T(8,128)(2,1)S(1)}, u32[]{:S(2)}, u32[]{:S(2)}) collective-permute-start(bf16[4,64,768]{2,1,0:T(8,128)(2,1)S(1)} %collective-permute-done.3.refs_1_.refs_3_), channel_id=1, source_target_pairs={{0,1},{1,0},{2,3},{3,2},{4,5},{5,4},{6,7},{7,6},{8,24},{9,25},{10,... | collective-permute-start | bytes 1179656 | tf_op jit(solution)/shard_map/ppermute | solution.py:197
  25.1 6.1 %collective-permute-start.5 = (bf16[6,4,64,768]{3,2,1,0:T(8,128)(2,1)S(1)}, bf16[6,4,64,768]{3,2,1,0:T(8,128)(2,1)S(1)}, u32[]{:S(2)}, u32[]{:S(2)}) collective-permute-start(bf16[6,4,64,768]{3,2,1,0:T(8,128)(2,1)S(1)} %get-tuple-element.90), channel_id=1, source_target_pairs={{0,8},{1,9},{2,10},{3,11},{4,12},{5,13},{6,14},{7,15},{8,0},{9,1},... | collective-permute-start | bytes 7077896 | tf_op jit(solution)/shard_map/ppermute | solution.py:197
  25.2 20.1 %collective-permute-start.7 = (bf16[2,4,64,768]{3,2,1,0:T(8,128)(2,1)S(1)}, bf16[2,4,64,768]{3,2,1,0:T(8,128)(2,1)S(1)}, u32[]{:S(2)}, u32[]{:S(2)}) collective-permute-start(bf16[2,4,64,768]{3,2,1,0:T(8,128)(2,1)S(1)} %get-tuple-element.98), channel_id=1, source_target_pairs={{0,16},{1,17},{2,18},{3,19},{4,20},{5,21},{6,22},{7,23},{8,9},{9,8... | collective-permute-start | bytes 2359304 | tf_op jit(solution)/shard_map/ppermute | solution.py:197
  26.8 18.6 %collective-permute-start.8 = (bf16[2,4,64,768]{3,2,1,0:T(8,128)(2,1)S(1)}, bf16[2,4,64,768]{3,2,1,0:T(8,128)(2,1)S(1)}, u32[]{:S(2)}, u32[]{:S(2)}) collective-permute-start(bf16[2,4,64,768]{3,2,1,0:T(8,128)(2,1)S(1)} %get-tuple-element.98), channel_id=1, source_target_pairs={{0,1},{1,0},{2,3},{3,2},{4,5},{5,4},{6,7},{7,6},{8,24},{9,25},{10,... | collective-permute-start | bytes 2359304 | tf_op jit(solution)/shard_map/ppermute | solution.py:197
  27.3 16.2 %collective-permute-start.6 = (bf16[4,64,768]{2,1,0:T(8,128)(2,1)S(1)}, bf16[4,64,768]{2,1,0:T(8,128)(2,1)S(1)}, u32[]{:S(2)}, u32[]{:S(2)}) collective-permute-start(bf16[4,64,768]{2,1,0:T(8,128)(2,1)S(1)} %collective-permute-done.refs_5_.refs_0_), channel_id=1, source_target_pairs={{0,2},{1,3},{2,0},{3,1},{4,6},{5,7},{6,4},{7,5},{8,10},{9,11},{10,... | collective-permute-start | bytes 1179656 | tf_op jit(solution)/shard_map/ppermute | solution.py:197
  31.2 20.1 %collective-permute-start.9 = (bf16[4,64,768]{2,1,0:T(8,128)(2,1)S(1)}, bf16[4,64,768]{2,1,0:T(8,128)(2,1)S(1)}, u32[]{:S(2)}, u32[]{:S(2)}) collective-permute-start(bf16[4,64,768]{2,1,0:T(8,128)(2,1)S(1)} %collective-permute-done.4.refs_3_.refs_4_), channel_id=1, source_target_pairs={{0,4},{1,5},{2,6},{3,7},{4,0},{5,1},{6,2},{7,3},{8,12},{9,13},{10,... | collective-permute-start | bytes 1179656 | tf_op jit(solution)/shard_map/ppermute | solution.py:197
  45.5 11.7 %collective-permute-start.10 = (bf16[4,64,768]{2,1,0:T(8,128)(2,1)S(1)}, bf16[4,64,768]{2,1,0:T(8,128)(2,1)S(1)}, u32[]{:S(2)}, u32[]{:S(2)}) collective-permute-start(bf16[4,64,768]{2,1,0:T(8,128)(2,1)S(1)} %collective-permute-done.6.o3_ref.refs_2_.refs_0_), channel_id=1, source_target_pairs={{0,16},{1,17},{2,18},{3,19},{4,20},{5,21},{6,22},{7,23},{8,9},{9,8... | collective-permute-start | bytes 1179656 | tf_op jit(solution)/shard_map/ppermute | solution.py:197
  47.1 10.1 %collective-permute-start.11 = (bf16[4,64,768]{2,1,0:T(8,128)(2,1)S(1)}, bf16[4,64,768]{2,1,0:T(8,128)(2,1)S(1)}, u32[]{:S(2)}, u32[]{:S(2)}) collective-permute-start(bf16[4,64,768]{2,1,0:T(8,128)(2,1)S(1)} %collective-permute-done.6.o3_ref.refs_2_.refs_0_), channel_id=1, source_target_pairs={{0,1},{1,0},{2,3},{3,2},{4,5},{5,4},{6,7},{7,6},{8,24},{9,25},{10,... | collective-permute-start | bytes 1179656 | tf_op jit(solution)/shard_map/ppermute | solution.py:197
  47.4 12.3 %collective-permute-start.12 = (bf16[4,64,768]{2,1,0:T(8,128)(2,1)S(1)}, bf16[4,64,768]{2,1,0:T(8,128)(2,1)S(1)}, u32[]{:S(2)}, u32[]{:S(2)}) collective-permute-start(bf16[4,64,768]{2,1,0:T(8,128)(2,1)S(1)} %collective-permute-done.4.refs_3_.refs_4_), channel_id=1, source_target_pairs={{0,2},{1,3},{2,0},{3,1},{4,6},{5,7},{6,4},{7,5},{8,10},{9,11},{10,... | collective-permute-start | bytes 1179656 | tf_op jit(solution)/shard_map/ppermute | solution.py:197
  48.8 12.7 %collective-permute-start.13 = (bf16[5,4,64,768]{3,2,1,0:T(8,128)(2,1)S(1)}, bf16[5,4,64,768]{3,2,1,0:T(8,128)(2,1)S(1)}, u32[]{:S(2)}, u32[]{:S(2)}) collective-permute-start(bf16[5,4,64,768]{3,2,1,0:T(8,128)(2,1)S(1)} %shard_map.31), channel_id=1, source_target_pairs={{0,8},{1,9},{2,10},{3,11},{4,12},{5,13},{6,14},{7,15},{8,0},{9,1},... | collective-permute-start | bytes 5898248 | tf_op jit(solution)/shard_map/ppermute | solution.py:197
  59.8 4.9 %collective-permute-start.14 = (bf16[4,4,64,768]{3,2,1,0:T(8,128)(2,1)S(1)}, bf16[4,4,64,768]{3,2,1,0:T(8,128)(2,1)S(1)}, u32[]{:S(2)}, u32[]{:S(2)}) collective-permute-start(bf16[4,4,64,768]{3,2,1,0:T(8,128)(2,1)S(1)} %shard_map.33), channel_id=1, source_target_pairs={{0,8},{1,9},{2,10},{3,11},{4,12},{5,13},{6,14},{7,15},{8,0},{9,1},... | collective-permute-start | bytes 4718600 | tf_op jit(solution)/shard_map/ppermute | solution.py:197
  59.9 7.8 %collective-permute-start.15 = (bf16[4,64,768]{2,1,0:T(8,128)(2,1)S(1)}, bf16[4,64,768]{2,1,0:T(8,128)(2,1)S(1)}, u32[]{:S(2)}, u32[]{:S(2)}) collective-permute-start(bf16[4,64,768]{2,1,0:T(8,128)(2,1)S(1)} %collective-permute-done.10.refs_0_.refs_5_.refs_3_), channel_id=1, source_target_pairs={{0,1},{1,0},{2,3},{3,2},{4,5},{5,4},{6,7},{7,6},{8,24},{9,25},{10,... | collective-permute-start | bytes 1179656 | tf_op jit(solution)/shard_map/ppermute | solution.py:197
  67.7 1.7 %collective-permute-start.16 = (bf16[4,64,768]{2,1,0:T(8,128)(2,1)S(1)}, bf16[4,64,768]{2,1,0:T(8,128)(2,1)S(1)}, u32[]{:S(2)}, u32[]{:S(2)}) collective-permute-start(bf16[4,64,768]{2,1,0:T(8,128)(2,1)S(1)} %collective-permute-done.15.refs_2_), channel_id=1, source_target_pairs={{0,8},{1,9},{2,10},{3,11},{4,12},{5,13},{6,14},{7,15},{8,0},{9,1},... | collective-permute-start | bytes 1179656 | tf_op jit(solution)/shard_map/ppermute | solution.py:197

commit v11 on v8

--- a/solution.py
+++ b/solution.py
@@ -38,16 +38,14 @@
         cosine_rows[1].append(jnp.concatenate([-by_cos[:, half:], by_cos[:, :half]], 1))
         sine_rows[0].append(jnp.concatenate([-by_sin[:, half:], by_sin[:, :half]], 1))
         sine_rows[1].append(-by_sin)
-    return (
-        jnp.concatenate(cosine_rows[0] + cosine_rows[1], 0),
-        jnp.concatenate(sine_rows[0] + sine_rows[1], 0),
-    )
-
-
-def product(left_cos, left_sin, right):
+    return jnp.concatenate(cosine_rows[0] + cosine_rows[1] + sine_rows[0] + sine_rows[1], 0)
+
+
+def product(left, right):
     dims = (((1,), (1,)), ((), ()))
-    term = lax.dot_general(left_cos, right, dims, preferred_element_type=jnp.float32)
-    return term + lax.dot_general(left_sin, right, dims, preferred_element_type=jnp.float32)
+    terms = lax.dot_general(left, right, dims, preferred_element_type=jnp.float32)
+    half = terms.shape[0] // 2
+    return terms[:half] + terms[half:]
 
 
 def add_shards(names, where, has_totals, last, place_ref, weights_ref, *refs):
@@ -64,7 +62,7 @@
 
     pair, core, level, beside, first_s, flat = (place_ref[i] for i in range(6))
     columns, per_block, _ = shard(names[0]).shape
-    spins = left_ref.shape[2] // (2 * per_block)
+    spins = left_ref.shape[1] // (4 * per_block)
 
     slots = left_slots(names)
     if last:
@@ -87,7 +85,7 @@
                     )
                     for s in range(spins)
                 ]
-            left_ref[slot, 0], left_ref[slot, 1] = left_sides(owns, weights_ref[site])
+            left_ref[slot] = left_sides(owns, weights_ref[site])
 
     for side, kind, dz in names:
         right = shard((side, kind, dz))[...].reshape(columns * per_block, -1)
@@ -97,7 +95,7 @@
             slot = slots.index((dy, dz))
         else:
             slot = slots.index((0, dz)) + dy
-        term = product(left_ref[slot, 0], left_ref[slot, 1], right)
+        term = product(left_ref[slot], right)
         if last:
             far_ref[dx] += term
         else:
@@ -140,11 +138,18 @@
         stack_ref[slot] = refs[slot][...]
     both_ref[0] = o1_ref[...]
     both_ref[1] = o2_ref[...]
-    mixed_ref[...] = jnp.where(place_ref[1] == 0, o2_ref[...], ab0_ref[...])
+
+    @pl.when(place_ref[1] == 0)
+    def _():
+        mixed_ref[...] = o2_ref[...]
+
+    @pl.when(place_ref[1] != 0)
+    def _():
+        mixed_ref[...] = ab0_ref[...]
 
 
 def route_third(ab1_ref, o3_ref, ab2_ref, a12_ref, b12_ref, stack_ref):
-    for slot, ref in enumerate((ab1_ref, o3_ref, ab2_ref)):
+    for slot, ref in enumerate((ab1_ref, ab2_ref, o3_ref)):
         stack_ref[slot] = ref[...]
     stack_ref[3:5] = a12_ref[...]
     stack_ref[5:7] = b12_ref[...]
@@ -213,7 +218,7 @@
         key, slot = where[("near", kind, dz)]
         return arrays[key] if slot is None else arrays[key][slot]
 
-    def add(names, totals, keep=False, left=None):
+    def add(names, totals, keep=False, left=None, weight=1):
         last = left is not None
         slots = left_slots(names)
         uses = list(names)
@@ -224,7 +229,7 @@
         operands = [place, weights] + [arrays[key] for key in keys]
         operands += [each for each in (left, totals) if each is not None]
         total_shape = (2, 2, tall, wide)
-        left_shape = (len(slots), 2, tall, depth)
+        left_shape = (len(slots), 2 * tall, depth)
         block = pl.BlockSpec(memory_space=pltpu.VMEM)
         out_shape = [jax.ShapeDtypeStruct(total_shape, jnp.float32)]
         scratch = [pltpu.VMEM(left_shape, jnp.bfloat16)]
@@ -248,7 +253,7 @@
             scratch_shapes=scratch,
             compiler_params=pltpu.CompilerParams(vmem_limit_bytes=40 * 1024 * 1024),
             cost_estimate=pl.CostEstimate(
-                flops=4 * tall * wide * depth * len(names),
+                flops=4 * tall * wide * depth * len(names) * weight,
                 bytes_accessed=wide * depth * 2 * len(names) + 8 * 4 * tall * wide,
                 transcendentals=0,
             ),
@@ -284,7 +289,7 @@
         return fence(routed)
 
     first = [("O", 0), ("A", 0), ("B", 0), ("AB", 0), ("O", 1), ("O", 2)]
-    second = [("AB", 1), ("O", 3), ("AB", 2), ("A", 1), ("A", 2), ("B", 1), ("B", 2)]
+    second = [("AB", 1), ("AB", 2), ("O", 3), ("A", 1), ("A", 2), ("B", 1), ("B", 2)]
     third = [("A", 3), ("AB", 3), ("B", 3)]
     stack, both, mixed = route(route_second, [place] + [near(*kind) for kind in first], (6, 2, 1))
     totals = add([("near", *kind) for kind in first], None)
@@ -300,6 +305,7 @@
     totals = fence(totals)
 
     ab3, a3, o3 = hop_z(near("AB", 2), 1), hop_a(near("O", 3)), near("O", 3)
+    totals = add([("near", "O", 3)], totals, weight=45)
     arrays["2b"] = ab1
     put("2e", a12, "near", [("A", 1), ("A", 2)])
     put("2f", b12, "near", [("B", 1), ("B", 2)])
@@ -308,7 +314,8 @@
     keys = ("2b", "2c", "2d", "2e", "2f")
     (stack,) = route(route_third, [arrays[key] for key in keys], (7,))
     b3, far2 = hop_b(near("O", 3)), swap(stack)
-    totals = add([("near", *kind) for kind in second], totals)
+    names = [("near", *kind) for kind in second if kind != ("O", 3)]
+    totals = add(names, totals)
     a3, ab3, totals = lax.optimization_barrier((a3, ab3, totals))
     (stack,) = route(route_last, [a3, ab3], (2,), weight=10**11)
     put("3a", stack, "near", third[:2])
@@ -334,10 +341,10 @@
     spins = left_ref.shape[2]
     groups, columns, per_block, depth = right_ref.shape[0], *right_ref.shape[2:]
     owns = [left_ref[0, 0, spin] for spin in range(spins)]
-    left_cos, left_sin = left_sides(owns, weights_ref[0])
+    left = left_sides(owns, weights_ref[0])
     for column in range(columns):
         right = right_ref[:, 0, column].reshape(groups * per_block, depth)
-        term = product(left_cos, left_sin, right)
+        term = product(left, right)
         for part in range(2):
             for spin in range(spins):
                 start = (part * spins + spin) * per_block

time: 67.4 us -> 70.6 us (1.047)
  waiting for transfers between devices: 26.6 us -> 31.3 us
  starting transfers between devices: 23.1 us -> 20.9 us
    ppermute x17, waiting for transfers between devices: 26.6 us -> 31.3 us  [move(): return lax.ppermute(array, AXES, pairs)]
    ppermute x17, starting transfers between devices: 23.1 us -> 20.9 us  [move(): return lax.ppermute(array, AXES, pairs)]
    pallas_call x6 -> x7, Pallas kernels: 14.3 us -> 15 us  [add(): pl.pallas_call(functools.partial(add_shards, tuple(names), places, totals...]
  transfers between devices with their start and end apart: 17 -> 17, of which waited for: 6 -> 8; matrix products, arithmetic and copies ran while one was open for 1% -> 1% of each run, Pallas kernels for 18% -> 18%
where the time goes in v11:
time: 70.6 us; the launch traced here: 70.4 us
  waiting for transfers between devices  31.3 us (44%)
  starting transfers between devices  20.9 us (30%)
  Pallas kernels  16 us (23%)
  local copies, waits for them, and re-layouts  1.78 us (3%)
    ppermute x17, waiting for transfers between devices, move(): return lax.ppermute(array, AXES, pairs)  31.3 us
    ppermute x17, starting transfers between devices, move(): return lax.ppermute(array, AXES, pairs)  20.9 us
    pallas_call x7, Pallas kernels, add(): pl.pallas_call(functools.partial(add_shards, tuple(names), places, totals...  15 us
  transfers between devices with their start and end apart: 17, of which 8 were waited for; matrix products, arithmetic and copies ran while one was open for 1% of the time, Pallas kernels for 18%

profile of v11, /device:TPU:0, one launch (start us, length us, event | category | flops | bytes accessed | tf_op | source)
XLA Modules:
  0.0 70.4 jit_solution(6125970074650298218)
XLA Ops:
  0.0 0.0 copy-start
  0.0 1.3 %copy.9 = bf16[2,64,4,3,128]{4,3,0,1,2:T(4,128)(2,1)S(1)} copy(bf16[2,64,4,3,128]{4,1,3,2,0:T(8,128)(2,1)} %bitcast.32) | data formatting | bytes 786432 | tf_op jit(solution)/shard_map/reshape | solution.py:403
  1.4 0.3 reshape.222.refs_0_.refs_5_
  1.7 3.0 %collective-permute-start.3 = (bf16[4,64,768]{2,1,0:T(8,128)(2,1)S(1)}, bf16[4,64,768]{2,1,0:T(8,128)(2,1)S(1)}, u32[]{:S(2)}, u32[]{:S(2)}) collective-permute-start(bf16[4,64,768]{2,1,0:T(8,128)(2,1)S(1)} %reshape.222.refs_0_.refs_5_), channel_id=1, source_target_pairs={{0,16},{1,17},{2,18},{3,19},{4,20},{5,21},{6,22},{7,23},{8,9},{9,8... | collective-permute-start | bytes 1179656 | tf_op jit(solution)/shard_map/ppermute | solution.py:187
  4.7 2.6 %collective-permute-start = (bf16[4,64,768]{2,1,0:T(8,128)(2,1)S(1)}, bf16[4,64,768]{2,1,0:T(8,128)(2,1)S(1)}, u32[]{:S(2)}, u32[]{:S(2)}) collective-permute-start(bf16[4,64,768]{2,1,0:T(8,128)(2,1)S(1)} %reshape.222.refs_0_.refs_5_), channel_id=1, source_target_pairs={{0,4},{1,5},{2,6},{3,7},{4,0},{5,1},{6,2},{7,3},{8,12},{9,13},{10,... | collective-permute-start | bytes 1179656 | tf_op jit(solution)/shard_map/ppermute | solution.py:187
  7.3 1.6 %collective-permute-start.1 = (bf16[4,64,768]{2,1,0:T(8,128)(2,1)S(1)}, bf16[4,64,768]{2,1,0:T(8,128)(2,1)S(1)}, u32[]{:S(2)}, u32[]{:S(2)}) collective-permute-start(bf16[4,64,768]{2,1,0:T(8,128)(2,1)S(1)} %reshape.222.refs_0_.refs_5_), channel_id=1, source_target_pairs={{0,2},{1,3},{2,0},{3,1},{4,6},{5,7},{6,4},{7,5},{8,10},{9,11},{10,... | collective-permute-start | bytes 1179656 | tf_op jit(solution)/shard_map/ppermute | solution.py:187
  8.9 1.5 %collective-permute-start.2 = (bf16[4,64,768]{2,1,0:T(8,128)(2,1)S(1)}, bf16[4,64,768]{2,1,0:T(8,128)(2,1)S(1)}, u32[]{:S(2)}, u32[]{:S(2)}) collective-permute-start(bf16[4,64,768]{2,1,0:T(8,128)(2,1)S(1)} %reshape.222.refs_0_.refs_5_), channel_id=1, source_target_pairs={{0,1},{1,0},{2,3},{3,2},{4,5},{5,4},{6,7},{7,6},{8,24},{9,25},{10,... | collective-permute-start | bytes 1179656 | tf_op jit(solution)/shard_map/ppermute | solution.py:187
  10.4 0.0 copy-done
  10.4 0.1 fusion
  10.5 0.0 collective-permute-done.3.refs_1_.refs_3_
  10.6 3.4 %collective-permute-start.4 = (bf16[4,64,768]{2,1,0:T(8,128)(2,1)S(1)}, bf16[4,64,768]{2,1,0:T(8,128)(2,1)S(1)}, u32[]{:S(2)}, u32[]{:S(2)}) collective-permute-start(bf16[4,64,768]{2,1,0:T(8,128)(2,1)S(1)} %collective-permute-done.3.refs_1_.refs_3_), channel_id=1, source_target_pairs={{0,1},{1,0},{2,3},{3,2},{4,5},{5,4},{6,7},{7,6},{8,24},{9,25},{10,... | collective-permute-start | bytes 1179656 | tf_op jit(solution)/shard_map/ppermute | solution.py:187
  14.0 0.1 stack.44.place_ref
  14.1 0.1 multiply_cosine_fusion
  14.2 10.5 %collective-permute-done.refs_5_.refs_0_ = bf16[4,64,768]{2,1,0:T(8,128)(2,1)S(1)} collective-permute-done((bf16[4,64,768]{2,1,0:T(8,128)(2,1)S(1)}, bf16[4,64,768]{2,1,0:T(8,128)(2,1)S(1)}, u32[]{:S(2)}, u32[]{:S(2)}) %collective-permute-start) | collective-permute-done | bytes 393248 | tf_op jit(solution)/shard_map/ppermute | solution.py:187
  24.7 0.2 collective-permute-done.1.refs_4_.refs_1_
  24.9 0.0 collective-permute-done.2.refs_2_
  24.9 0.0 collective-permute-done.4.refs_3_.refs_4_
  24.9 0.8 %shard_map.28 = (bf16[6,4,64,768]{3,2,1,0:T(8,128)(2,1)S(1)}, bf16[2,4,64,768]{3,2,1,0:T(8,128)(2,1)S(1)}, bf16[4,64,768]{2,1,0:T(8,128)(2,1)S(1)}) custom-call(s32[7]{0:T(128)S(1)} %stack.44.place_ref, bf16[4,64,768]{2,1,0:T(8,128)(2,1)S(1)} %reshape.222.refs_0_.refs_5_, bf16[4,64,768]{2,1,0:T(8,128)(2,1)S(1)} %collective-permute-done.3.refs_1_.refs_3_, ...), custom_call_target="tpu_custom_call" | custom-call | tf_op jit(solution)/shard_map/pallas_call | solution.py:281
  25.7 0.1 collective-permute-start.5
  25.8 1.5 %collective-permute-start.6 = (bf16[4,64,768]{2,1,0:T(8,128)(2,1)S(1)}, bf16[4,64,768]{2,1,0:T(8,128)(2,1)S(1)}, u32[]{:S(2)}, u32[]{:S(2)}) collective-permute-start(bf16[4,64,768]{2,1,0:T(8,128)(2,1)S(1)} %collective-permute-done.refs_5_.refs_0_), channel_id=1, source_target_pairs={{0,2},{1,3},{2,0},{3,1},{4,6},{5,7},{6,4},{7,5},{8,10},{9,11},{10,... | collective-permute-start | bytes 1179656 | tf_op jit(solution)/shard_map/ppermute | solution.py:187
  27.3 1.4 %collective-permute-start.7 = (bf16[4,64,768]{2,1,0:T(8,128)(2,1)S(1)}, bf16[4,64,768]{2,1,0:T(8,128)(2,1)S(1)}, u32[]{:S(2)}, u32[]{:S(2)}) collective-permute-start(bf16[4,64,768]{2,1,0:T(8,128)(2,1)S(1)} %get-tuple-element.97), channel_id=1, source_target_pairs={{0,17},{1,16},{2,19},{3,18},{4,21},{5,20},{6,23},{7,22},{8,12},{9,... | collective-permute-start | bytes 1179656 | tf_op jit(solution)/shard_map/ppermute | solution.py:187
  28.7 1.5 %collective-permute-start.10 = (bf16[2,4,64,768]{3,2,1,0:T(8,128)(2,1)S(1)}, bf16[2,4,64,768]{3,2,1,0:T(8,128)(2,1)S(1)}, u32[]{:S(2)}, u32[]{:S(2)}) collective-permute-start(bf16[2,4,64,768]{3,2,1,0:T(8,128)(2,1)S(1)} %get-tuple-element.104), channel_id=1, source_target_pairs={{0,1},{1,0},{2,3},{3,2},{4,5},{5,4},{6,7},{7,6},{8,24},{9,25},{10,... | collective-permute-start | bytes 2359304 | tf_op jit(solution)/shard_map/ppermute | solution.py:187
  30.3 0.5 collective-permute-start.9
  30.8 2.5 %shard_map.29.refs_6_ = f32[2,2,256,256]{3,2,1,0:T(8,128)S(1)} custom-call(s32[7]{0:T(128)S(1)} %stack.44.place_ref, f32[8,2,128]{2,1,0:T(2,128)S(1)} %maximum_bitcast_fusion.weights_ref, bf16[4,64,768]{2,1,0:T(8,128)(2,1)S(1)} %collective-permute-done.refs_5_.refs_0_, bf16[4,64,768]{2,1,0:T(8,128)(2,1)S(1)} %collective-permute-done.1.refs_4_.refs_1_, ...), custom_call_target="tpu_custom_call" | custom-call | flops 1207959552 | bytes 4456448 | tf_op jit(solution)/shard_map/pallas_call | solution.py:248
  33.3 0.0 collective-permute-done.5.refs_4_
  33.3 0.7 collective-permute-start.8
  33.9 2.5 %shard_map.30.refs_1_ = f32[2,2,256,256]{3,2,1,0:T(8,128)S(1)} custom-call(s32[7]{0:T(128)S(1)} %stack.44.place_ref, f32[8,2,128]{2,1,0:T(2,128)S(1)} %maximum_bitcast_fusion.weights_ref, bf16[4,64,768]{2,1,0:T(8,128)(2,1)S(1)} %collective-permute-done.refs_5_.refs_0_, bf16[4,64,768]{2,1,0:T(8,128)(2,1)S(1)} %collective-permute-done.1.refs_4_.refs_1_, ...), custom_call_target="tpu_custom_call" | custom-call | flops 1207959552 | bytes 4456448 | tf_op jit(solution)/shard_map/pallas_call | solution.py:248
  36.4 5.6 %collective-permute-done.6.refs_0_.o3_ref.refs_2_ = bf16[4,64,768]{2,1,0:T(8,128)(2,1)S(1)} collective-permute-done((bf16[4,64,768]{2,1,0:T(8,128)(2,1)S(1)}, bf16[4,64,768]{2,1,0:T(8,128)(2,1)S(1)}, u32[]{:S(2)}, u32[]{:S(2)}) %collective-permute-start.6) | collective-permute-done | bytes 393248 | tf_op jit(solution)/shard_map/ppermute | solution.py:187
  42.0 0.0 collective-permute-done.7.ab2_ref.refs_3_
  42.0 1.5 %collective-permute-start.11 = (bf16[4,64,768]{2,1,0:T(8,128)(2,1)S(1)}, bf16[4,64,768]{2,1,0:T(8,128)(2,1)S(1)}, u32[]{:S(2)}, u32[]{:S(2)}) collective-permute-start(bf16[4,64,768]{2,1,0:T(8,128)(2,1)S(1)} %collective-permute-done.6.refs_0_.o3_ref.refs_2_), channel_id=1, source_target_pairs={{0,16},{1,17},{2,18},{3,19},{4,20},{5,21},{6,22},{7,23},{8,9},{9,8... | collective-permute-start | bytes 1179656 | tf_op jit(solution)/shard_map/ppermute | solution.py:187
  43.5 0.0 collective-permute-start.12
  43.5 1.0 %shard_map.31.refs_6_ = f32[2,2,256,256]{3,2,1,0:T(8,128)S(1)} custom-call(s32[7]{0:T(128)S(1)} %stack.44.place_ref, f32[8,2,128]{2,1,0:T(2,128)S(1)} %maximum_bitcast_fusion.weights_ref, bf16[4,64,768]{2,1,0:T(8,128)(2,1)S(1)} %collective-permute-done.6.refs_0_.o3_ref.refs_2_, f32[2,2,256,256]{3,2,1,0:T(8,128)S(1)} %shard_map.30.refs_1_), custom_call_target="tpu_custom_call" | custom-call | flops 9059696640 | bytes 2490368 | tf_op jit(solution)/shard_map/pallas_call | solution.py:248
  44.5 7.9 %collective-permute-done.10.b12_ref.refs_5_.refs_4_ = bf16[2,4,64,768]{3,2,1,0:T(8,128)(2,1)S(1)} collective-permute-done((bf16[2,4,64,768]{3,2,1,0:T(8,128)(2,1)S(1)}, bf16[2,4,64,768]{3,2,1,0:T(8,128)(2,1)S(1)}, u32[]{:S(2)}, u32[]{:S(2)}) %collective-permute-start.10) | collective-permute-done | bytes 786464 | tf_op jit(solution)/shard_map/ppermute | solution.py:187
  52.4 0.0 collective-permute-done.9.a12_ref.refs_4_.refs_3_
  52.4 0.0 collective-permute-done.8.ab1_ref.refs_2_
  52.4 0.2 shard_map.32
  52.6 0.7 collective-permute-start.14
  53.3 2.3 %shard_map.33.refs_6_ = f32[2,2,256,256]{3,2,1,0:T(8,128)S(1)} custom-call(s32[7]{0:T(128)S(1)} %stack.44.place_ref, f32[8,2,128]{2,1,0:T(2,128)S(1)} %maximum_bitcast_fusion.weights_ref, bf16[4,64,768]{2,1,0:T(8,128)(2,1)S(1)} %collective-permute-done.refs_5_.refs_0_, bf16[4,64,768]{2,1,0:T(8,128)(2,1)S(1)} %collective-permute-done.1.refs_4_.refs_1_, ...), custom_call_target="tpu_custom_call" | custom-call | flops 1207959552 | bytes 4456448 | tf_op jit(solution)/shard_map/pallas_call | solution.py:248
  55.6 0.5 collective-permute-done.11.a3_ref
  56.1 2.3 %collective-permute-done.12.ab3_ref = bf16[4,64,768]{2,1,0:T(8,128)(2,1)S(1)} collective-permute-done((bf16[4,64,768]{2,1,0:T(8,128)(2,1)S(1)}, bf16[4,64,768]{2,1,0:T(8,128)(2,1)S(1)}, u32[]{:S(2)}, u32[]{:S(2)}) %collective-permute-start.12) | collective-permute-done | bytes 393248 | tf_op jit(solution)/shard_map/ppermute | solution.py:187
  58.4 0.5 collective-permute-start.13
  58.8 0.1 shard_map.34.refs_1_
  58.9 0.5 collective-permute-start.15
  59.4 0.0 collective-permute-done.14.refs_5_
  59.4 2.5 %shard_map.35.refs_3_ = f32[2,2,256,256]{3,2,1,0:T(8,128)S(1)} custom-call(s32[7]{0:T(128)S(1)} %stack.44.place_ref, f32[8,2,128]{2,1,0:T(2,128)S(1)} %maximum_bitcast_fusion.weights_ref, bf16[4,64,768]{2,1,0:T(8,128)(2,1)S(1)} %collective-permute-done.refs_5_.refs_0_, bf16[4,64,768]{2,1,0:T(8,128)(2,1)S(1)} %collective-permute-done.1.refs_4_.refs_1_, ...), custom_call_target="tpu_custom_call" | custom-call | flops 1409286144 | bytes 4849664 | tf_op jit(solution)/shard_map/pallas_call | solution.py:248
  61.9 4.2 %collective-permute-done.13.refs_2_ = bf16[4,64,768]{2,1,0:T(8,128)(2,1)S(1)} collective-permute-done((bf16[4,64,768]{2,1,0:T(8,128)(2,1)S(1)}, bf16[4,64,768]{2,1,0:T(8,128)(2,1)S(1)}, u32[]{:S(2)}, u32[]{:S(2)}) %collective-permute-start.13) | collective-permute-done | bytes 393248 | tf_op jit(solution)/shard_map/ppermute | solution.py:187
  66.2 0.0 collective-permute-start.16
  66.2 1.6 %shard_map.36 = (f32[2,2,256,256]{3,2,1,0:T(8,128)S(1)}, bf16[2,512,768]{2,1,0:T(8,128)(2,1)S(1)}) custom-call(s32[7]{0:T(128)S(1)} %stack.44.place_ref, f32[8,2,128]{2,1,0:T(2,128)S(1)} %maximum_bitcast_fusion.weights_ref, bf16[4,64,768]{2,1,0:T(8,128)(2,1)S(1)} %collective-permute-done.6.refs_0_.o3_ref.refs_2_, ...), custom_call_target="tpu_custom_call" | custom-call | flops 603979776 | bytes 3276800 | tf_op jit(solution)/shard_map/pallas_call | solution.py:248
  67.8 0.0 collective-permute-done.15.refs_0_
  67.8 0.1 collective-permute-done.16.refs_1_
  67.9 2.6 %shard_map.37 = f32[16,64,256]{2,1,0:T(8,128)} custom-call(s32[7]{0:T(128)S(1)} %stack.44.place_ref, f32[8,2,128]{2,1,0:T(2,128)S(1)} %maximum_bitcast_fusion.weights_ref, bf16[2,4,64,768]{3,2,1,0:T(8,128)(2,1)S(1)} %collective-permute-done.15.refs_0_, bf16[4,64,768]{2,1,0:T(8,128)(2,1)S(1)} %collective-permute-done.16.refs_1_, ...), custom_call_target="tpu_custom_call" | custom-call | flops 603979776 | bytes 3276800 | tf_op jit(solution)/shard_map/pallas_call | solution.py:248
  (5 shorter events, 0.1 us)
Async XLA Ops:
  0.0 10.4 %copy-start = (s32[4,3]{1,0:T(4,128)S(1)}, s32[4,3]{1,0:T(4,128)}, u32[]{:S(2)}) copy-start(s32[4,3]{1,0:T(4,128)} %param.3) | copy-start | bytes 148
  1.7 8.8 %collective-permute-start.3 = (bf16[4,64,768]{2,1,0:T(8,128)(2,1)S(1)}, bf16[4,64,768]{2,1,0:T(8,128)(2,1)S(1)}, u32[]{:S(2)}, u32[]{:S(2)}) collective-permute-start(bf16[4,64,768]{2,1,0:T(8,128)(2,1)S(1)} %reshape.222.refs_0_.refs_5_), channel_id=1, source_target_pairs={{0,16},{1,17},{2,18},{3,19},{4,20},{5,21},{6,22},{7,23},{8,9},{9,8... | collective-permute-start | bytes 1179656 | tf_op jit(solution)/shard_map/ppermute | solution.py:187
  4.7 20.0 %collective-permute-start = (bf16[4,64,768]{2,1,0:T(8,128)(2,1)S(1)}, bf16[4,64,768]{2,1,0:T(8,128)(2,1)S(1)}, u32[]{:S(2)}, u32[]{:S(2)}) collective-permute-start(bf16[4,64,768]{2,1,0:T(8,128)(2,1)S(1)} %reshape.222.refs_0_.refs_5_), channel_id=1, source_target_pairs={{0,4},{1,5},{2,6},{3,7},{4,0},{5,1},{6,2},{7,3},{8,12},{9,13},{10,... | collective-permute-start | bytes 1179656 | tf_op jit(solution)/shard_map/ppermute | solution.py:187
  7.3 17.6 %collective-permute-start.1 = (bf16[4,64,768]{2,1,0:T(8,128)(2,1)S(1)}, bf16[4,64,768]{2,1,0:T(8,128)(2,1)S(1)}, u32[]{:S(2)}, u32[]{:S(2)}) collective-permute-start(bf16[4,64,768]{2,1,0:T(8,128)(2,1)S(1)} %reshape.222.refs_0_.refs_5_), channel_id=1, source_target_pairs={{0,2},{1,3},{2,0},{3,1},{4,6},{5,7},{6,4},{7,5},{8,10},{9,11},{10,... | collective-permute-start | bytes 1179656 | tf_op jit(solution)/shard_map/ppermute | solution.py:187
  8.9 16.1 %collective-permute-start.2 = (bf16[4,64,768]{2,1,0:T(8,128)(2,1)S(1)}, bf16[4,64,768]{2,1,0:T(8,128)(2,1)S(1)}, u32[]{:S(2)}, u32[]{:S(2)}) collective-permute-start(bf16[4,64,768]{2,1,0:T(8,128)(2,1)S(1)} %reshape.222.refs_0_.refs_5_), channel_id=1, source_target_pairs={{0,1},{1,0},{2,3},{3,2},{4,5},{5,4},{6,7},{7,6},{8,24},{9,25},{10,... | collective-permute-start | bytes 1179656 | tf_op jit(solution)/shard_map/ppermute | solution.py:187
  10.6 14.4 %collective-permute-start.4 = (bf16[4,64,768]{2,1,0:T(8,128)(2,1)S(1)}, bf16[4,64,768]{2,1,0:T(8,128)(2,1)S(1)}, u32[]{:S(2)}, u32[]{:S(2)}) collective-permute-start(bf16[4,64,768]{2,1,0:T(8,128)(2,1)S(1)} %collective-permute-done.3.refs_1_.refs_3_), channel_id=1, source_target_pairs={{0,1},{1,0},{2,3},{3,2},{4,5},{5,4},{6,7},{7,6},{8,24},{9,25},{10,... | collective-permute-start | bytes 1179656 | tf_op jit(solution)/shard_map/ppermute | solution.py:187
  25.7 7.6 %collective-permute-start.5 = (bf16[6,4,64,768]{3,2,1,0:T(8,128)(2,1)S(1)}, bf16[6,4,64,768]{3,2,1,0:T(8,128)(2,1)S(1)}, u32[]{:S(2)}, u32[]{:S(2)}) collective-permute-start(bf16[6,4,64,768]{3,2,1,0:T(8,128)(2,1)S(1)} %get-tuple-element.89), channel_id=1, source_target_pairs={{0,8},{1,9},{2,10},{3,11},{4,12},{5,13},{6,14},{7,15},{8,0},{9,1},... | collective-permute-start | bytes 7077896 | tf_op jit(solution)/shard_map/ppermute | solution.py:187
  25.8 16.2 %collective-permute-start.6 = (bf16[4,64,768]{2,1,0:T(8,128)(2,1)S(1)}, bf16[4,64,768]{2,1,0:T(8,128)(2,1)S(1)}, u32[]{:S(2)}, u32[]{:S(2)}) collective-permute-start(bf16[4,64,768]{2,1,0:T(8,128)(2,1)S(1)} %collective-permute-done.refs_5_.refs_0_), channel_id=1, source_target_pairs={{0,2},{1,3},{2,0},{3,1},{4,6},{5,7},{6,4},{7,5},{8,10},{9,11},{10,... | collective-permute-start | bytes 1179656 | tf_op jit(solution)/shard_map/ppermute | solution.py:187
  27.3 14.7 %collective-permute-start.7 = (bf16[4,64,768]{2,1,0:T(8,128)(2,1)S(1)}, bf16[4,64,768]{2,1,0:T(8,128)(2,1)S(1)}, u32[]{:S(2)}, u32[]{:S(2)}) collective-permute-start(bf16[4,64,768]{2,1,0:T(8,128)(2,1)S(1)} %get-tuple-element.97), channel_id=1, source_target_pairs={{0,17},{1,16},{2,19},{3,18},{4,21},{5,20},{6,23},{7,22},{8,12},{9,... | collective-permute-start | bytes 1179656 | tf_op jit(solution)/shard_map/ppermute | solution.py:187
  28.7 23.7 %collective-permute-start.10 = (bf16[2,4,64,768]{3,2,1,0:T(8,128)(2,1)S(1)}, bf16[2,4,64,768]{3,2,1,0:T(8,128)(2,1)S(1)}, u32[]{:S(2)}, u32[]{:S(2)}) collective-permute-start(bf16[2,4,64,768]{3,2,1,0:T(8,128)(2,1)S(1)} %get-tuple-element.104), channel_id=1, source_target_pairs={{0,1},{1,0},{2,3},{3,2},{4,5},{5,4},{6,7},{7,6},{8,24},{9,25},{10,... | collective-permute-start | bytes 2359304 | tf_op jit(solution)/shard_map/ppermute | solution.py:187
  30.3 22.2 %collective-permute-start.9 = (bf16[2,4,64,768]{3,2,1,0:T(8,128)(2,1)S(1)}, bf16[2,4,64,768]{3,2,1,0:T(8,128)(2,1)S(1)}, u32[]{:S(2)}, u32[]{:S(2)}) collective-permute-start(bf16[2,4,64,768]{3,2,1,0:T(8,128)(2,1)S(1)} %get-tuple-element.104), channel_id=1, source_target_pairs={{0,16},{1,17},{2,18},{3,19},{4,20},{5,21},{6,22},{7,23},{8,9},{9,8... | collective-permute-start | bytes 2359304 | tf_op jit(solution)/shard_map/ppermute | solution.py:187
  33.3 19.2 %collective-permute-start.8 = (bf16[4,64,768]{2,1,0:T(8,128)(2,1)S(1)}, bf16[4,64,768]{2,1,0:T(8,128)(2,1)S(1)}, u32[]{:S(2)}, u32[]{:S(2)}) collective-permute-start(bf16[4,64,768]{2,1,0:T(8,128)(2,1)S(1)} %collective-permute-done.4.refs_3_.refs_4_), channel_id=1, source_target_pairs={{0,2},{1,3},{2,0},{3,1},{4,6},{5,7},{6,4},{7,5},{8,10},{9,11},{10,... | collective-permute-start | bytes 1179656 | tf_op jit(solution)/shard_map/ppermute | solution.py:187
  42.0 14.1 %collective-permute-start.11 = (bf16[4,64,768]{2,1,0:T(8,128)(2,1)S(1)}, bf16[4,64,768]{2,1,0:T(8,128)(2,1)S(1)}, u32[]{:S(2)}, u32[]{:S(2)}) collective-permute-start(bf16[4,64,768]{2,1,0:T(8,128)(2,1)S(1)} %collective-permute-done.6.refs_0_.o3_ref.refs_2_), channel_id=1, source_target_pairs={{0,16},{1,17},{2,18},{3,19},{4,20},{5,21},{6,22},{7,23},{8,9},{9,8... | collective-permute-start | bytes 1179656 | tf_op jit(solution)/shard_map/ppermute | solution.py:187
  43.5 14.9 %collective-permute-start.12 = (bf16[4,64,768]{2,1,0:T(8,128)(2,1)S(1)}, bf16[4,64,768]{2,1,0:T(8,128)(2,1)S(1)}, u32[]{:S(2)}, u32[]{:S(2)}) collective-permute-start(bf16[4,64,768]{2,1,0:T(8,128)(2,1)S(1)} %collective-permute-done.7.ab2_ref.refs_3_), channel_id=1, source_target_pairs={{0,2},{1,3},{2,0},{3,1},{4,6},{5,7},{6,4},{7,5},{8,10},{9,11},{10,... | collective-permute-start | bytes 1179656 | tf_op jit(solution)/shard_map/ppermute | solution.py:187
  52.6 6.8 %collective-permute-start.14 = (bf16[7,4,64,768]{3,2,1,0:T(8,128)(2,1)S(1)}, bf16[7,4,64,768]{3,2,1,0:T(8,128)(2,1)S(1)}, u32[]{:S(2)}, u32[]{:S(2)}) collective-permute-start(bf16[7,4,64,768]{3,2,1,0:T(8,128)(2,1)S(1)} %shard_map.32), channel_id=1, source_target_pairs={{0,8},{1,9},{2,10},{3,11},{4,12},{5,13},{6,14},{7,15},{8,0},{9,1},... | collective-permute-start | bytes 8257544 | tf_op jit(solution)/shard_map/ppermute | solution.py:187
  58.4 7.8 %collective-permute-start.13 = (bf16[4,64,768]{2,1,0:T(8,128)(2,1)S(1)}, bf16[4,64,768]{2,1,0:T(8,128)(2,1)S(1)}, u32[]{:S(2)}, u32[]{:S(2)}) collective-permute-start(bf16[4,64,768]{2,1,0:T(8,128)(2,1)S(1)} %collective-permute-done.6.refs_0_.o3_ref.refs_2_), channel_id=1, source_target_pairs={{0,1},{1,0},{2,3},{3,2},{4,5},{5,4},{6,7},{7,6},{8,24},{9,25},{10,... | collective-permute-start | bytes 1179656 | tf_op jit(solution)/shard_map/ppermute | solution.py:187
  58.9 8.9 %collective-permute-start.15 = (bf16[2,4,64,768]{3,2,1,0:T(8,128)(2,1)S(1)}, bf16[2,4,64,768]{3,2,1,0:T(8,128)(2,1)S(1)}, u32[]{:S(2)}, u32[]{:S(2)}) collective-permute-start(bf16[2,4,64,768]{3,2,1,0:T(8,128)(2,1)S(1)} %shard_map.34.refs_1_), channel_id=1, source_target_pairs={{0,8},{1,9},{2,10},{3,11},{4,12},{5,13},{6,14},{7,15},{8,0},{9,1},... | collective-permute-start | bytes 2359304 | tf_op jit(solution)/shard_map/ppermute | solution.py:187
  66.2 1.7 %collective-permute-start.16 = (bf16[4,64,768]{2,1,0:T(8,128)(2,1)S(1)}, bf16[4,64,768]{2,1,0:T(8,128)(2,1)S(1)}, u32[]{:S(2)}, u32[]{:S(2)}) collective-permute-start(bf16[4,64,768]{2,1,0:T(8,128)(2,1)S(1)} %collective-permute-done.13.refs_2_), channel_id=1, source_target_pairs={{0,8},{1,9},{2,10},{3,11},{4,12},{5,13},{6,14},{7,15},{8,0},{9,1},... | collective-permute-start | bytes 1179656 | tf_op jit(solution)/shard_map/ppermute | solution.py:187

commit v12 on v11

--- a/solution.py
+++ b/solution.py
@@ -48,7 +48,7 @@
     return terms[:half] + terms[half:]
 
 
-def add_shards(names, where, has_totals, last, place_ref, weights_ref, *refs):
+def add_shards(names, where, has_totals, last, share, weights_ref, *refs):
     refs = list(refs)
     if last:
         sems, row_ref, far_ref, out_ref, totals_in, left_ref = (refs.pop() for _ in range(6))
@@ -60,8 +60,10 @@
         index, slot = where[name]
         return refs[index] if slot is None else refs[index].at[slot]
 
-    pair, core, level, beside, first_s, flat = (place_ref[i] for i in range(6))
+    pair, core, level, beside = (lax.axis_index(name) for name in AXES)
+    flat = lax.axis_size("flat")
     columns, per_block, _ = shard(names[0]).shape
+    first_s = lax.rem(lax.div((level * flat + beside) * (share // 2), 4), 4)
     spins = left_ref.shape[1] // (4 * per_block)
 
     slots = left_slots(names)
@@ -132,18 +134,19 @@
             copy.wait()
 
 
-def route_second(place_ref, *refs):
+def route_second(*refs):
     ab0_ref, o1_ref, o2_ref, stack_ref, both_ref, mixed_ref = refs[3:]
+    core = lax.axis_index("core")
     for slot in range(6):
         stack_ref[slot] = refs[slot][...]
     both_ref[0] = o1_ref[...]
     both_ref[1] = o2_ref[...]
 
-    @pl.when(place_ref[1] == 0)
+    @pl.when(core == 0)
     def _():
         mixed_ref[...] = o2_ref[...]
 
-    @pl.when(place_ref[1] != 0)
+    @pl.when(core != 0)
     def _():
         mixed_ref[...] = ab0_ref[...]
 
@@ -167,7 +170,7 @@
     return sorted(needed, key=lambda slot: (slot[1], slot[0]))
 
 
-def swap_in_windows(packed, place, weights, share):
+def swap_in_windows(packed, weights, share):
     shape = tuple(lax.axis_size(name) for name in AXES)
     columns, per_block, depth = packed.shape
     spins = share // (2 * columns)
@@ -226,7 +229,7 @@
             uses += [("near", kind, dz) for kind in (("A", "B") if dy else ("O",))]
         keys = sorted({where[name][0] for name in uses})
         places = {name: (keys.index(where[name][0]), where[name][1]) for name in uses}
-        operands = [place, weights] + [arrays[key] for key in keys]
+        operands = [weights] + [arrays[key] for key in keys]
         operands += [each for each in (left, totals) if each is not None]
         total_shape = (2, 2, tall, wide)
         left_shape = (len(slots), 2 * tall, depth)
@@ -246,8 +249,8 @@
             out_shape.append(jax.ShapeDtypeStruct(left_shape, jnp.bfloat16))
             out_specs, scratch = [block] * 2, []
         out = pl.pallas_call(
-            functools.partial(add_shards, tuple(names), places, totals is not None, last),
-            in_specs=[pl.BlockSpec(memory_space=pltpu.SMEM)] + [block] * (len(operands) - 1),
+            functools.partial(add_shards, tuple(names), places, totals is not None, last, share),
+            in_specs=[block] * len(operands),
             out_specs=out_specs,
             out_shape=out_shape,
             scratch_shapes=scratch,
@@ -272,15 +275,14 @@
     put("1c", hop_b(packed), "near", [("B", 0)])
     put("1d", hop_a(packed), "near", [("A", 0)])
     put("1e", hop_b(near("A", 0)), "near", [("AB", 0)])
-    place, weights = fence((place, weights))
+    weights = fence(weights)
 
     def route(kernel, operands, counts, weight=0):
         block = pl.BlockSpec(memory_space=pltpu.VMEM)
-        first = pl.BlockSpec(memory_space=pltpu.SMEM) if operands[0] is place else block
         shapes = [(count,) * (count > 1) + packed.shape for count in counts]
         routed = pl.pallas_call(
             kernel,
-            in_specs=[first] + [block] * (len(operands) - 1),
+            in_specs=[block] * len(operands),
             out_specs=[block] * len(counts),
             out_shape=[jax.ShapeDtypeStruct(shape, packed.dtype) for shape in shapes],
             compiler_params=pltpu.CompilerParams(vmem_limit_bytes=24 * 1024 * 1024),
@@ -291,7 +293,7 @@
     first = [("O", 0), ("A", 0), ("B", 0), ("AB", 0), ("O", 1), ("O", 2)]
     second = [("AB", 1), ("AB", 2), ("O", 3), ("A", 1), ("A", 2), ("B", 1), ("B", 2)]
     third = [("A", 3), ("AB", 3), ("B", 3)]
-    stack, both, mixed = route(route_second, [place] + [near(*kind) for kind in first], (6, 2, 1))
+    stack, both, mixed = route(route_second, [near(*kind) for kind in first], (6, 2, 1))
     totals = add([("near", *kind) for kind in first], None)
     o3, ab2, a12, b12 = hop_z(near("O", 2), 1), hop_mixed(mixed), hop_a(both), hop_b(both)
     put("2a", swap(stack), "far", first)
@@ -304,7 +306,7 @@
     put("2d", ab2, "near", [("AB", 2)])
     totals = fence(totals)
 
-    ab3, a3, o3 = hop_z(near("AB", 2), 1), hop_a(near("O", 3)), near("O", 3)
+    ab3, a3, b3 = hop_z(near("AB", 2), 1), hop_a(near("O", 3)), hop_b(near("O", 3))
     totals = add([("near", "O", 3)], totals, weight=45)
     arrays["2b"] = ab1
     put("2e", a12, "near", [("A", 1), ("A", 2)])
@@ -313,7 +315,7 @@
 
     keys = ("2b", "2c", "2d", "2e", "2f")
     (stack,) = route(route_third, [arrays[key] for key in keys], (7,))
-    b3, far2 = hop_b(near("O", 3)), swap(stack)
+    far2 = swap(stack)
     names = [("near", *kind) for kind in second if kind != ("O", 3)]
     totals = add(names, totals)
     a3, ab3, totals = lax.optimization_barrier((a3, ab3, totals))
@@ -408,7 +410,7 @@
     weights = jnp.transpose(weights.reshape(2, sites, site_count), (1, 0, 2))
 
     if (groups, deep, flat) == (2, 4, 2) and share in (8, 16, 32):
-        return swap_in_windows(packed, place, weights, share)
+        return swap_in_windows(packed, weights, share)
     return gather_whole(packed, place, weights, share)
 
 

time: 70.6 us -> 66.1 us (0.936)
  Pallas kernels: 16 us -> 11.4 us
    pallas_call x7, Pallas kernels: 15 us -> 10.9 us  [add(): pl.pallas_call(functools.partial(add_shards, tuple(names), places, totals...]
  transfers between devices with their start and end apart: 17 -> 17, of which waited for: 8 -> 6; matrix products, arithmetic and copies ran while one was open for 1% -> 0% of each run, Pallas kernels for 18% -> 14%
where the time goes in v12:
time: 66.1 us; the launch traced here: 65.9 us
  waiting for transfers between devices  31.4 us (48%)
  starting transfers between devices  21 us (32%)
  Pallas kernels  11.4 us (17%)
  local copies, waits for them, and re-layouts  1.69 us (3%)
    ppermute x17, waiting for transfers between devices, move(): return lax.ppermute(array, AXES, pairs)  31.4 us
    ppermute x17, starting transfers between devices, move(): return lax.ppermute(array, AXES, pairs)  21 us
    pallas_call x7, Pallas kernels, add(): pl.pallas_call(functools.partial(add_shards, tuple(names), places, totals...  10.9 us
    reshape x1, local copies, waits for them, and re-layouts, shards(): modes.reshape(slots, per_block, 4, 3, site_count)  1.35 us
  transfers between devices with their start and end apart: 17, of which 6 were waited for; matrix products, arithmetic and copies ran while one was open for 0% of the time, Pallas kernels for 14%

profile of v12, /device:TPU:0, one launch (start us, length us, event | category | flops | bytes accessed | tf_op | source)
XLA Modules:
  0.0 65.9 jit_solution(8353544081959785870)
XLA Ops:
  0.0 0.0 copy-start
  0.0 1.3 %copy.9 = bf16[2,64,4,3,128]{4,3,0,1,2:T(4,128)(2,1)S(1)} copy(bf16[2,64,4,3,128]{4,1,3,2,0:T(8,128)(2,1)} %bitcast.26) | data formatting | bytes 786432 | tf_op jit(solution)/shard_map/reshape | solution.py:405
  1.4 0.3 reshape.222.refs_0_.refs_5_
  1.7 3.0 %collective-permute-start.3 = (bf16[4,64,768]{2,1,0:T(8,128)(2,1)S(1)}, bf16[4,64,768]{2,1,0:T(8,128)(2,1)S(1)}, u32[]{:S(2)}, u32[]{:S(2)}) collective-permute-start(bf16[4,64,768]{2,1,0:T(8,128)(2,1)S(1)} %reshape.222.refs_0_.refs_5_), channel_id=1, source_target_pairs={{0,16},{1,17},{2,18},{3,19},{4,20},{5,21},{6,22},{7,23},{8,9},{9,8... | collective-permute-start | bytes 1179656 | tf_op jit(solution)/shard_map/ppermute | solution.py:190
  4.7 2.6 %collective-permute-start = (bf16[4,64,768]{2,1,0:T(8,128)(2,1)S(1)}, bf16[4,64,768]{2,1,0:T(8,128)(2,1)S(1)}, u32[]{:S(2)}, u32[]{:S(2)}) collective-permute-start(bf16[4,64,768]{2,1,0:T(8,128)(2,1)S(1)} %reshape.222.refs_0_.refs_5_), channel_id=1, source_target_pairs={{0,4},{1,5},{2,6},{3,7},{4,0},{5,1},{6,2},{7,3},{8,12},{9,13},{10,... | collective-permute-start | bytes 1179656 | tf_op jit(solution)/shard_map/ppermute | solution.py:190
  7.3 1.6 %collective-permute-start.1 = (bf16[4,64,768]{2,1,0:T(8,128)(2,1)S(1)}, bf16[4,64,768]{2,1,0:T(8,128)(2,1)S(1)}, u32[]{:S(2)}, u32[]{:S(2)}) collective-permute-start(bf16[4,64,768]{2,1,0:T(8,128)(2,1)S(1)} %reshape.222.refs_0_.refs_5_), channel_id=1, source_target_pairs={{0,2},{1,3},{2,0},{3,1},{4,6},{5,7},{6,4},{7,5},{8,10},{9,11},{10,... | collective-permute-start | bytes 1179656 | tf_op jit(solution)/shard_map/ppermute | solution.py:190
  8.9 1.5 %collective-permute-start.2 = (bf16[4,64,768]{2,1,0:T(8,128)(2,1)S(1)}, bf16[4,64,768]{2,1,0:T(8,128)(2,1)S(1)}, u32[]{:S(2)}, u32[]{:S(2)}) collective-permute-start(bf16[4,64,768]{2,1,0:T(8,128)(2,1)S(1)} %reshape.222.refs_0_.refs_5_), channel_id=1, source_target_pairs={{0,1},{1,0},{2,3},{3,2},{4,5},{5,4},{6,7},{7,6},{8,24},{9,25},{10,... | collective-permute-start | bytes 1179656 | tf_op jit(solution)/shard_map/ppermute | solution.py:190
  10.4 0.0 copy-done
  10.4 0.1 fusion
  10.5 0.0 collective-permute-done.3.refs_1_.refs_3_
  10.6 3.4 %collective-permute-start.4 = (bf16[4,64,768]{2,1,0:T(8,128)(2,1)S(1)}, bf16[4,64,768]{2,1,0:T(8,128)(2,1)S(1)}, u32[]{:S(2)}, u32[]{:S(2)}) collective-permute-start(bf16[4,64,768]{2,1,0:T(8,128)(2,1)S(1)} %collective-permute-done.3.refs_1_.refs_3_), channel_id=1, source_target_pairs={{0,1},{1,0},{2,3},{3,2},{4,5},{5,4},{6,7},{7,6},{8,24},{9,25},{10,... | collective-permute-start | bytes 1179656 | tf_op jit(solution)/shard_map/ppermute | solution.py:190
  14.0 0.1 multiply_cosine_fusion
  14.1 10.6 %collective-permute-done.refs_5_.refs_0_ = bf16[4,64,768]{2,1,0:T(8,128)(2,1)S(1)} collective-permute-done((bf16[4,64,768]{2,1,0:T(8,128)(2,1)S(1)}, bf16[4,64,768]{2,1,0:T(8,128)(2,1)S(1)}, u32[]{:S(2)}, u32[]{:S(2)}) %collective-permute-start) | collective-permute-done | bytes 393248 | tf_op jit(solution)/shard_map/ppermute | solution.py:190
  24.7 0.2 collective-permute-done.1.refs_4_.refs_1_
  24.9 0.0 collective-permute-done.2.refs_2_
  24.9 0.0 collective-permute-done.4.refs_3_.refs_4_
  24.9 0.2 shard_map.28
  25.2 0.1 collective-permute-start.5
  25.3 1.5 %collective-permute-start.6 = (bf16[4,64,768]{2,1,0:T(8,128)(2,1)S(1)}, bf16[4,64,768]{2,1,0:T(8,128)(2,1)S(1)}, u32[]{:S(2)}, u32[]{:S(2)}) collective-permute-start(bf16[4,64,768]{2,1,0:T(8,128)(2,1)S(1)} %collective-permute-done.refs_5_.refs_0_), channel_id=1, source_target_pairs={{0,2},{1,3},{2,0},{3,1},{4,6},{5,7},{6,4},{7,5},{8,10},{9,11},{10,... | collective-permute-start | bytes 1179656 | tf_op jit(solution)/shard_map/ppermute | solution.py:190
  26.8 1.4 %collective-permute-start.7 = (bf16[4,64,768]{2,1,0:T(8,128)(2,1)S(1)}, bf16[4,64,768]{2,1,0:T(8,128)(2,1)S(1)}, u32[]{:S(2)}, u32[]{:S(2)}) collective-permute-start(bf16[4,64,768]{2,1,0:T(8,128)(2,1)S(1)} %get-tuple-element.95), channel_id=1, source_target_pairs={{0,17},{1,16},{2,19},{3,18},{4,21},{5,20},{6,23},{7,22},{8,12},{9,... | collective-permute-start | bytes 1179656 | tf_op jit(solution)/shard_map/ppermute | solution.py:190
  28.2 1.5 %collective-permute-start.10 = (bf16[2,4,64,768]{3,2,1,0:T(8,128)(2,1)S(1)}, bf16[2,4,64,768]{3,2,1,0:T(8,128)(2,1)S(1)}, u32[]{:S(2)}, u32[]{:S(2)}) collective-permute-start(bf16[2,4,64,768]{3,2,1,0:T(8,128)(2,1)S(1)} %get-tuple-element.102), channel_id=1, source_target_pairs={{0,1},{1,0},{2,3},{3,2},{4,5},{5,4},{6,7},{7,6},{8,24},{9,25},{10,... | collective-permute-start | bytes 2359304 | tf_op jit(solution)/shard_map/ppermute | solution.py:190
  29.7 0.5 collective-permute-start.9
  30.2 1.8 %shard_map.29.refs_6_ = f32[2,2,256,256]{3,2,1,0:T(8,128)S(1)} custom-call(f32[8,2,128]{2,1,0:T(2,128)S(1)} %maximum_bitcast_fusion.weights_ref, bf16[4,64,768]{2,1,0:T(8,128)(2,1)S(1)} %collective-permute-done.refs_5_.refs_0_, bf16[4,64,768]{2,1,0:T(8,128)(2,1)S(1)} %collective-permute-done.1.refs_4_.refs_1_, ...), custom_call_target="tpu_custom_call" | custom-call | flops 1207959552 | bytes 4456448 | tf_op jit(solution)/shard_map/pallas_call | solution.py:251
  32.1 0.0 collective-permute-done.5.refs_4_
  32.1 0.7 collective-permute-start.8
  32.7 1.7 %shard_map.30.refs_1_ = f32[2,2,256,256]{3,2,1,0:T(8,128)S(1)} custom-call(f32[8,2,128]{2,1,0:T(2,128)S(1)} %maximum_bitcast_fusion.weights_ref, bf16[4,64,768]{2,1,0:T(8,128)(2,1)S(1)} %collective-permute-done.refs_5_.refs_0_, bf16[4,64,768]{2,1,0:T(8,128)(2,1)S(1)} %collective-permute-done.1.refs_4_.refs_1_, ...), custom_call_target="tpu_custom_call" | custom-call | flops 1207959552 | bytes 4456448 | tf_op jit(solution)/shard_map/pallas_call | solution.py:251
  34.5 7.0 %collective-permute-done.6.refs_0_.o3_ref.refs_2_ = bf16[4,64,768]{2,1,0:T(8,128)(2,1)S(1)} collective-permute-done((bf16[4,64,768]{2,1,0:T(8,128)(2,1)S(1)}, bf16[4,64,768]{2,1,0:T(8,128)(2,1)S(1)}, u32[]{:S(2)}, u32[]{:S(2)}) %collective-permute-start.6) | collective-permute-done | bytes 393248 | tf_op jit(solution)/shard_map/ppermute | solution.py:190
  41.4 0.0 collective-permute-done.7.ab2_ref.refs_3_
  41.4 1.5 %collective-permute-start.11 = (bf16[4,64,768]{2,1,0:T(8,128)(2,1)S(1)}, bf16[4,64,768]{2,1,0:T(8,128)(2,1)S(1)}, u32[]{:S(2)}, u32[]{:S(2)}) collective-permute-start(bf16[4,64,768]{2,1,0:T(8,128)(2,1)S(1)} %collective-permute-done.6.refs_0_.o3_ref.refs_2_), channel_id=1, source_target_pairs={{0,16},{1,17},{2,18},{3,19},{4,20},{5,21},{6,22},{7,23},{8,9},{9,8... | collective-permute-start | bytes 1179656 | tf_op jit(solution)/shard_map/ppermute | solution.py:190
  42.9 0.0 collective-permute-start.12
  42.9 0.4 shard_map.31.refs_6_
  43.4 8.5 %collective-permute-done.10.b12_ref.refs_5_.refs_4_ = bf16[2,4,64,768]{3,2,1,0:T(8,128)(2,1)S(1)} collective-permute-done((bf16[2,4,64,768]{3,2,1,0:T(8,128)(2,1)S(1)}, bf16[2,4,64,768]{3,2,1,0:T(8,128)(2,1)S(1)}, u32[]{:S(2)}, u32[]{:S(2)}) %collective-permute-start.10) | collective-permute-done | bytes 786464 | tf_op jit(solution)/shard_map/ppermute | solution.py:190
  51.9 1.0 %collective-permute-start.13 = (bf16[4,64,768]{2,1,0:T(8,128)(2,1)S(1)}, bf16[4,64,768]{2,1,0:T(8,128)(2,1)S(1)}, u32[]{:S(2)}, u32[]{:S(2)}) collective-permute-start(bf16[4,64,768]{2,1,0:T(8,128)(2,1)S(1)} %collective-permute-done.6.refs_0_.o3_ref.refs_2_), channel_id=1, source_target_pairs={{0,1},{1,0},{2,3},{3,2},{4,5},{5,4},{6,7},{7,6},{8,24},{9,25},{10,... | collective-permute-start | bytes 1179656 | tf_op jit(solution)/shard_map/ppermute | solution.py:190
  52.9 0.0 collective-permute-done.9.a12_ref.refs_4_.refs_3_
  52.9 0.0 collective-permute-done.8.ab1_ref.refs_2_
  52.9 0.2 shard_map.32
  53.1 0.1 collective-permute-start.14
  53.2 1.7 %shard_map.33.refs_6_ = f32[2,2,256,256]{3,2,1,0:T(8,128)S(1)} custom-call(f32[8,2,128]{2,1,0:T(2,128)S(1)} %maximum_bitcast_fusion.weights_ref, bf16[4,64,768]{2,1,0:T(8,128)(2,1)S(1)} %collective-permute-done.refs_5_.refs_0_, bf16[4,64,768]{2,1,0:T(8,128)(2,1)S(1)} %collective-permute-done.1.refs_4_.refs_1_, ...), custom_call_target="tpu_custom_call" | custom-call | flops 1207959552 | bytes 4456448 | tf_op jit(solution)/shard_map/pallas_call | solution.py:251
  54.9 4.9 %collective-permute-done.11.a3_ref = bf16[4,64,768]{2,1,0:T(8,128)(2,1)S(1)} collective-permute-done((bf16[4,64,768]{2,1,0:T(8,128)(2,1)S(1)}, bf16[4,64,768]{2,1,0:T(8,128)(2,1)S(1)}, u32[]{:S(2)}, u32[]{:S(2)}) %collective-permute-start.11) | collective-permute-done | bytes 393248 | tf_op jit(solution)/shard_map/ppermute | solution.py:190
  59.8 0.0 collective-permute-done.12.ab3_ref
  59.8 0.1 shard_map.34.refs_1_
  59.8 0.1 collective-permute-start.15
  59.9 0.0 collective-permute-done.14.refs_5_
  59.9 2.0 %shard_map.35.refs_3_ = f32[2,2,256,256]{3,2,1,0:T(8,128)S(1)} custom-call(f32[8,2,128]{2,1,0:T(2,128)S(1)} %maximum_bitcast_fusion.weights_ref, bf16[4,64,768]{2,1,0:T(8,128)(2,1)S(1)} %collective-permute-done.refs_5_.refs_0_, bf16[4,64,768]{2,1,0:T(8,128)(2,1)S(1)} %collective-permute-done.1.refs_4_.refs_1_, ...), custom_call_target="tpu_custom_call" | custom-call | flops 1409286144 | bytes 4849664 | tf_op jit(solution)/shard_map/pallas_call | solution.py:251
  61.9 0.0 collective-permute-done.13.refs_2_
  61.9 0.6 collective-permute-start.16
  62.4 1.1 %shard_map.36 = (f32[2,2,256,256]{3,2,1,0:T(8,128)S(1)}, bf16[2,512,768]{2,1,0:T(8,128)(2,1)S(1)}) custom-call(f32[8,2,128]{2,1,0:T(2,128)S(1)} %maximum_bitcast_fusion.weights_ref, bf16[4,64,768]{2,1,0:T(8,128)(2,1)S(1)} %collective-permute-done.6.refs_0_.o3_ref.refs_2_, bf16[2,4,64,768]{3,2,1,0:T(8,128)(2,1)S(1)} %shard_map.34.refs_1_, ...), custom_call_target="tpu_custom_call" | custom-call | flops 603979776 | bytes 3276800 | tf_op jit(solution)/shard_map/pallas_call | solution.py:251
  63.6 0.0 collective-permute-done.15.refs_0_
  63.6 0.2 collective-permute-done.16.refs_1_
  63.8 2.1 %shard_map.37 = f32[16,64,256]{2,1,0:T(8,128)} custom-call(f32[8,2,128]{2,1,0:T(2,128)S(1)} %maximum_bitcast_fusion.weights_ref, bf16[2,4,64,768]{3,2,1,0:T(8,128)(2,1)S(1)} %collective-permute-done.15.refs_0_, bf16[4,64,768]{2,1,0:T(8,128)(2,1)S(1)} %collective-permute-done.16.refs_1_, bf16[2,512,768]{2,1,0:T(8,128)(2,1)S(1)} %get-tuple-element.137.refs_2_, ...), custom_call_target="tpu_custom_call" | custom-call | flops 603979776 | bytes 3276800 | tf_op jit(solution)/shard_map/pallas_call | solution.py:251
  (5 shorter events, 0.1 us)
Async XLA Ops:
  0.0 10.4 %copy-start = (s32[4,3]{1,0:T(4,128)S(1)}, s32[4,3]{1,0:T(4,128)}, u32[]{:S(2)}) copy-start(s32[4,3]{1,0:T(4,128)} %param.3) | copy-start | bytes 148
  1.7 8.8 %collective-permute-start.3 = (bf16[4,64,768]{2,1,0:T(8,128)(2,1)S(1)}, bf16[4,64,768]{2,1,0:T(8,128)(2,1)S(1)}, u32[]{:S(2)}, u32[]{:S(2)}) collective-permute-start(bf16[4,64,768]{2,1,0:T(8,128)(2,1)S(1)} %reshape.222.refs_0_.refs_5_), channel_id=1, source_target_pairs={{0,16},{1,17},{2,18},{3,19},{4,20},{5,21},{6,22},{7,23},{8,9},{9,8... | collective-permute-start | bytes 1179656 | tf_op jit(solution)/shard_map/ppermute | solution.py:190
  4.7 20.0 %collective-permute-start = (bf16[4,64,768]{2,1,0:T(8,128)(2,1)S(1)}, bf16[4,64,768]{2,1,0:T(8,128)(2,1)S(1)}, u32[]{:S(2)}, u32[]{:S(2)}) collective-permute-start(bf16[4,64,768]{2,1,0:T(8,128)(2,1)S(1)} %reshape.222.refs_0_.refs_5_), channel_id=1, source_target_pairs={{0,4},{1,5},{2,6},{3,7},{4,0},{5,1},{6,2},{7,3},{8,12},{9,13},{10,... | collective-permute-start | bytes 1179656 | tf_op jit(solution)/shard_map/ppermute | solution.py:190
  7.3 17.6 %collective-permute-start.1 = (bf16[4,64,768]{2,1,0:T(8,128)(2,1)S(1)}, bf16[4,64,768]{2,1,0:T(8,128)(2,1)S(1)}, u32[]{:S(2)}, u32[]{:S(2)}) collective-permute-start(bf16[4,64,768]{2,1,0:T(8,128)(2,1)S(1)} %reshape.222.refs_0_.refs_5_), channel_id=1, source_target_pairs={{0,2},{1,3},{2,0},{3,1},{4,6},{5,7},{6,4},{7,5},{8,10},{9,11},{10,... | collective-permute-start | bytes 1179656 | tf_op jit(solution)/shard_map/ppermute | solution.py:190
  8.9 16.1 %collective-permute-start.2 = (bf16[4,64,768]{2,1,0:T(8,128)(2,1)S(1)}, bf16[4,64,768]{2,1,0:T(8,128)(2,1)S(1)}, u32[]{:S(2)}, u32[]{:S(2)}) collective-permute-start(bf16[4,64,768]{2,1,0:T(8,128)(2,1)S(1)} %reshape.222.refs_0_.refs_5_), channel_id=1, source_target_pairs={{0,1},{1,0},{2,3},{3,2},{4,5},{5,4},{6,7},{7,6},{8,24},{9,25},{10,... | collective-permute-start | bytes 1179656 | tf_op jit(solution)/shard_map/ppermute | solution.py:190
  10.6 14.4 %collective-permute-start.4 = (bf16[4,64,768]{2,1,0:T(8,128)(2,1)S(1)}, bf16[4,64,768]{2,1,0:T(8,128)(2,1)S(1)}, u32[]{:S(2)}, u32[]{:S(2)}) collective-permute-start(bf16[4,64,768]{2,1,0:T(8,128)(2,1)S(1)} %collective-permute-done.3.refs_1_.refs_3_), channel_id=1, source_target_pairs={{0,1},{1,0},{2,3},{3,2},{4,5},{5,4},{6,7},{7,6},{8,24},{9,25},{10,... | collective-permute-start | bytes 1179656 | tf_op jit(solution)/shard_map/ppermute | solution.py:190
  25.2 6.9 %collective-permute-start.5 = (bf16[6,4,64,768]{3,2,1,0:T(8,128)(2,1)S(1)}, bf16[6,4,64,768]{3,2,1,0:T(8,128)(2,1)S(1)}, u32[]{:S(2)}, u32[]{:S(2)}) collective-permute-start(bf16[6,4,64,768]{3,2,1,0:T(8,128)(2,1)S(1)} %get-tuple-element.87), channel_id=1, source_target_pairs={{0,8},{1,9},{2,10},{3,11},{4,12},{5,13},{6,14},{7,15},{8,0},{9,1},... | collective-permute-start | bytes 7077896 | tf_op jit(solution)/shard_map/ppermute | solution.py:190
  25.3 16.2 %collective-permute-start.6 = (bf16[4,64,768]{2,1,0:T(8,128)(2,1)S(1)}, bf16[4,64,768]{2,1,0:T(8,128)(2,1)S(1)}, u32[]{:S(2)}, u32[]{:S(2)}) collective-permute-start(bf16[4,64,768]{2,1,0:T(8,128)(2,1)S(1)} %collective-permute-done.refs_5_.refs_0_), channel_id=1, source_target_pairs={{0,2},{1,3},{2,0},{3,1},{4,6},{5,7},{6,4},{7,5},{8,10},{9,11},{10,... | collective-permute-start | bytes 1179656 | tf_op jit(solution)/shard_map/ppermute | solution.py:190
  26.8 14.7 %collective-permute-start.7 = (bf16[4,64,768]{2,1,0:T(8,128)(2,1)S(1)}, bf16[4,64,768]{2,1,0:T(8,128)(2,1)S(1)}, u32[]{:S(2)}, u32[]{:S(2)}) collective-permute-start(bf16[4,64,768]{2,1,0:T(8,128)(2,1)S(1)} %get-tuple-element.95), channel_id=1, source_target_pairs={{0,17},{1,16},{2,19},{3,18},{4,21},{5,20},{6,23},{7,22},{8,12},{9,... | collective-permute-start | bytes 1179656 | tf_op jit(solution)/shard_map/ppermute | solution.py:190
  28.2 23.7 %collective-permute-start.10 = (bf16[2,4,64,768]{3,2,1,0:T(8,128)(2,1)S(1)}, bf16[2,4,64,768]{3,2,1,0:T(8,128)(2,1)S(1)}, u32[]{:S(2)}, u32[]{:S(2)}) collective-permute-start(bf16[2,4,64,768]{3,2,1,0:T(8,128)(2,1)S(1)} %get-tuple-element.102), channel_id=1, source_target_pairs={{0,1},{1,0},{2,3},{3,2},{4,5},{5,4},{6,7},{7,6},{8,24},{9,25},{10,... | collective-permute-start | bytes 2359304 | tf_op jit(solution)/shard_map/ppermute | solution.py:190
  29.7 23.2 %collective-permute-start.9 = (bf16[2,4,64,768]{3,2,1,0:T(8,128)(2,1)S(1)}, bf16[2,4,64,768]{3,2,1,0:T(8,128)(2,1)S(1)}, u32[]{:S(2)}, u32[]{:S(2)}) collective-permute-start(bf16[2,4,64,768]{3,2,1,0:T(8,128)(2,1)S(1)} %get-tuple-element.102), channel_id=1, source_target_pairs={{0,16},{1,17},{2,18},{3,19},{4,20},{5,21},{6,22},{7,23},{8,9},{9,8... | collective-permute-start | bytes 2359304 | tf_op jit(solution)/shard_map/ppermute | solution.py:190
  32.1 20.8 %collective-permute-start.8 = (bf16[4,64,768]{2,1,0:T(8,128)(2,1)S(1)}, bf16[4,64,768]{2,1,0:T(8,128)(2,1)S(1)}, u32[]{:S(2)}, u32[]{:S(2)}) collective-permute-start(bf16[4,64,768]{2,1,0:T(8,128)(2,1)S(1)} %collective-permute-done.4.refs_3_.refs_4_), channel_id=1, source_target_pairs={{0,2},{1,3},{2,0},{3,1},{4,6},{5,7},{6,4},{7,5},{8,10},{9,11},{10,... | collective-permute-start | bytes 1179656 | tf_op jit(solution)/shard_map/ppermute | solution.py:190
  41.4 18.3 %collective-permute-start.11 = (bf16[4,64,768]{2,1,0:T(8,128)(2,1)S(1)}, bf16[4,64,768]{2,1,0:T(8,128)(2,1)S(1)}, u32[]{:S(2)}, u32[]{:S(2)}) collective-permute-start(bf16[4,64,768]{2,1,0:T(8,128)(2,1)S(1)} %collective-permute-done.6.refs_0_.o3_ref.refs_2_), channel_id=1, source_target_pairs={{0,16},{1,17},{2,18},{3,19},{4,20},{5,21},{6,22},{7,23},{8,9},{9,8... | collective-permute-start | bytes 1179656 | tf_op jit(solution)/shard_map/ppermute | solution.py:190
  42.9 16.8 %collective-permute-start.12 = (bf16[4,64,768]{2,1,0:T(8,128)(2,1)S(1)}, bf16[4,64,768]{2,1,0:T(8,128)(2,1)S(1)}, u32[]{:S(2)}, u32[]{:S(2)}) collective-permute-start(bf16[4,64,768]{2,1,0:T(8,128)(2,1)S(1)} %collective-permute-done.7.ab2_ref.refs_3_), channel_id=1, source_target_pairs={{0,2},{1,3},{2,0},{3,1},{4,6},{5,7},{6,4},{7,5},{8,10},{9,11},{10,... | collective-permute-start | bytes 1179656 | tf_op jit(solution)/shard_map/ppermute | solution.py:190
  51.9 10.0 %collective-permute-start.13 = (bf16[4,64,768]{2,1,0:T(8,128)(2,1)S(1)}, bf16[4,64,768]{2,1,0:T(8,128)(2,1)S(1)}, u32[]{:S(2)}, u32[]{:S(2)}) collective-permute-start(bf16[4,64,768]{2,1,0:T(8,128)(2,1)S(1)} %collective-permute-done.6.refs_0_.o3_ref.refs_2_), channel_id=1, source_target_pairs={{0,1},{1,0},{2,3},{3,2},{4,5},{5,4},{6,7},{7,6},{8,24},{9,25},{10,... | collective-permute-start | bytes 1179656 | tf_op jit(solution)/shard_map/ppermute | solution.py:190
  53.1 6.8 %collective-permute-start.14 = (bf16[7,4,64,768]{3,2,1,0:T(8,128)(2,1)S(1)}, bf16[7,4,64,768]{3,2,1,0:T(8,128)(2,1)S(1)}, u32[]{:S(2)}, u32[]{:S(2)}) collective-permute-start(bf16[7,4,64,768]{3,2,1,0:T(8,128)(2,1)S(1)} %shard_map.32), channel_id=1, source_target_pairs={{0,8},{1,9},{2,10},{3,11},{4,12},{5,13},{6,14},{7,15},{8,0},{9,1},... | collective-permute-start | bytes 8257544 | tf_op jit(solution)/shard_map/ppermute | solution.py:190
  59.8 3.8 %collective-permute-start.15 = (bf16[2,4,64,768]{3,2,1,0:T(8,128)(2,1)S(1)}, bf16[2,4,64,768]{3,2,1,0:T(8,128)(2,1)S(1)}, u32[]{:S(2)}, u32[]{:S(2)}) collective-permute-start(bf16[2,4,64,768]{3,2,1,0:T(8,128)(2,1)S(1)} %shard_map.34.refs_1_), channel_id=1, source_target_pairs={{0,8},{1,9},{2,10},{3,11},{4,12},{5,13},{6,14},{7,15},{8,0},{9,1},... | collective-permute-start | bytes 2359304 | tf_op jit(solution)/shard_map/ppermute | solution.py:190
  61.9 1.9 %collective-permute-start.16 = (bf16[4,64,768]{2,1,0:T(8,128)(2,1)S(1)}, bf16[4,64,768]{2,1,0:T(8,128)(2,1)S(1)}, u32[]{:S(2)}, u32[]{:S(2)}) collective-permute-start(bf16[4,64,768]{2,1,0:T(8,128)(2,1)S(1)} %collective-permute-done.13.refs_2_), channel_id=1, source_target_pairs={{0,8},{1,9},{2,10},{3,11},{4,12},{5,13},{6,14},{7,15},{8,0},{9,1},... | collective-permute-start | bytes 1179656 | tf_op jit(solution)/shard_map/ppermute | solution.py:190

commit v13 on v12

--- a/solution.py
+++ b/solution.py
@@ -48,49 +48,55 @@
     return terms[:half] + terms[half:]
 
 
-def add_shards(names, where, has_totals, last, share, weights_ref, *refs):
+def add_shards(names, where, slots, has_totals, given, last, share, weights_ref, *refs):
     refs = list(refs)
     if last:
-        sems, row_ref, far_ref, out_ref, totals_in, left_ref = (refs.pop() for _ in range(6))
-    else:
-        left_ref, out_ref = refs.pop(), refs.pop()
-        totals_in = refs.pop() if has_totals else None
+        sems, row_ref, far_ref = (refs.pop() for _ in range(3))
+    left_ref = None if given else refs.pop()
+    out_ref = refs.pop()
+    totals_in = refs.pop() if has_totals else None
+    left_ref = refs.pop() if given else left_ref
 
     def shard(name):
         index, slot = where[name]
         return refs[index] if slot is None else refs[index].at[slot]
 
+    def spin_rows(name, spin):
+        ref = shard(name)
+        tiles = [ref[part, spin * colours + x] for part in range(2) for x in range(colours)]
+        return jnp.concatenate(tiles, 1)
+
     pair, core, level, beside = (lax.axis_index(name) for name in AXES)
     flat = lax.axis_size("flat")
-    columns, per_block, _ = shard(names[0]).shape
+    _, spin_colour, per_block, _ = shard(names[0]).shape
+    columns, colours = 4, spin_colour // 4
     first_s = lax.rem(lax.div((level * flat + beside) * (share // 2), 4), 4)
     spins = left_ref.shape[1] // (4 * per_block)
 
-    slots = left_slots(names)
     if last:
         far_ref[...] = totals_in[1]
+    elif has_totals:
+        out_ref[...] = totals_in[...]
     else:
-        if has_totals:
-            out_ref[...] = totals_in[...]
-        else:
-            out_ref[...] = jnp.zeros_like(out_ref)
+        out_ref[...] = jnp.zeros_like(out_ref)
+    if not given:
         for slot, (dy, dz) in enumerate(slots):
             site = jnp.bitwise_xor(level, dz) * flat + jnp.bitwise_xor(beside, dy)
             if dy == 0:
-                owns = [shard(("near", "O", dz))[first_s + s] for s in range(spins)]
+                owns = [spin_rows(("near", "O", dz), first_s + s) for s in range(spins)]
             else:
                 owns = [
                     jnp.where(
                         core == 0,
-                        shard(("near", "B", dz))[first_s + s],
-                        shard(("near", "A", dz))[first_s + s],
+                        spin_rows(("near", "B", dz), first_s + s),
+                        spin_rows(("near", "A", dz), first_s + s),
                     )
                     for s in range(spins)
                 ]
             left_ref[slot] = left_sides(owns, weights_ref[site])
 
     for side, kind, dz in names:
-        right = shard((side, kind, dz))[...].reshape(columns * per_block, -1)
+        right = jnp.concatenate([spin_rows((side, kind, dz), r) for r in range(columns)], 0)
         turn = core if side == "near" else 1 - core
         dx, dy = {"O": (0, 0), "A": (1 - turn, turn), "B": (turn, 1 - turn), "AB": (1, 1)}[kind]
         if kind in ("O", "AB"):
@@ -170,9 +176,10 @@
     return sorted(needed, key=lambda slot: (slot[1], slot[0]))
 
 
-def swap_in_windows(packed, weights, share):
+def swap_in_windows(own, weights, share):
     shape = tuple(lax.axis_size(name) for name in AXES)
-    columns, per_block, depth = packed.shape
+    columns, per_block = 4, own.shape[2]
+    depth = own.size // (columns * per_block)
     spins = share // (2 * columns)
     tall, wide = 2 * spins * per_block, columns * per_block
     strides = (shape[1] * shape[2] * shape[3], shape[2] * shape[3], shape[3], 1)
@@ -221,11 +228,11 @@
         key, slot = where[("near", kind, dz)]
         return arrays[key] if slot is None else arrays[key][slot]
 
-    def add(names, totals, keep=False, left=None, weight=1):
-        last = left is not None
-        slots = left_slots(names)
+    def add(names, totals, keep=None, left=None, last=False, weight=1):
+        given = left is not None
+        slots, left = left if given else (keep or left_slots(names), None)
         uses = list(names)
-        for dy, dz in [] if last else slots:
+        for dy, dz in [] if given else slots:
             uses += [("near", kind, dz) for kind in (("A", "B") if dy else ("O",))]
         keys = sorted({where[name][0] for name in uses})
         places = {name: (keys.index(where[name][0]), where[name][1]) for name in uses}
@@ -235,7 +242,7 @@
         left_shape = (len(slots), 2 * tall, depth)
         block = pl.BlockSpec(memory_space=pltpu.VMEM)
         out_shape = [jax.ShapeDtypeStruct(total_shape, jnp.float32)]
-        scratch = [pltpu.VMEM(left_shape, jnp.bfloat16)]
+        scratch = [] if given or keep else [pltpu.VMEM(left_shape, jnp.bfloat16)]
         out_specs = [block]
         if last:
             out_shape = [jax.ShapeDtypeStruct((share, per_block, 4 * per_block), jnp.float32)]
@@ -247,9 +254,11 @@
             ]
         if keep:
             out_shape.append(jax.ShapeDtypeStruct(left_shape, jnp.bfloat16))
-            out_specs, scratch = [block] * 2, []
+            out_specs.append(block)
         out = pl.pallas_call(
-            functools.partial(add_shards, tuple(names), places, totals is not None, last, share),
+            functools.partial(
+                add_shards, tuple(names), places, slots, totals is not None, given, last, share
+            ),
             in_specs=[block] * len(operands),
             out_specs=out_specs,
             out_shape=out_shape,
@@ -261,30 +270,30 @@
                 transcendentals=0,
             ),
         )(*operands)
-        return out if keep else out[0]
+        return (out[0], (slots, out[1])) if keep else out[0]
 
     def fence(totals):
         nonlocal arrays
         arrays, totals = lax.optimization_barrier((arrays, totals))
         return totals
 
-    put("9", packed, "near", [("O", 0)])
-
-    put("1a", hop_z(packed, 2), "near", [("O", 2)])
-    put("1b", hop_z(packed, 1), "near", [("O", 1)])
-    put("1c", hop_b(packed), "near", [("B", 0)])
-    put("1d", hop_a(packed), "near", [("A", 0)])
+    put("9", own, "near", [("O", 0)])
+
+    put("1a", hop_z(own, 2), "near", [("O", 2)])
+    put("1b", hop_z(own, 1), "near", [("O", 1)])
+    put("1c", hop_b(own), "near", [("B", 0)])
+    put("1d", hop_a(own), "near", [("A", 0)])
     put("1e", hop_b(near("A", 0)), "near", [("AB", 0)])
     weights = fence(weights)
 
     def route(kernel, operands, counts, weight=0):
         block = pl.BlockSpec(memory_space=pltpu.VMEM)
-        shapes = [(count,) * (count > 1) + packed.shape for count in counts]
+        shapes = [(count,) * (count > 1) + own.shape for count in counts]
         routed = pl.pallas_call(
             kernel,
             in_specs=[block] * len(operands),
             out_specs=[block] * len(counts),
-            out_shape=[jax.ShapeDtypeStruct(shape, packed.dtype) for shape in shapes],
+            out_shape=[jax.ShapeDtypeStruct(shape, own.dtype) for shape in shapes],
             compiler_params=pltpu.CompilerParams(vmem_limit_bytes=24 * 1024 * 1024),
             cost_estimate=pl.CostEstimate(flops=weight, bytes_accessed=0, transcendentals=0),
         )(*operands)
@@ -317,22 +326,23 @@
     (stack,) = route(route_third, [arrays[key] for key in keys], (7,))
     far2 = swap(stack)
     names = [("near", *kind) for kind in second if kind != ("O", 3)]
-    totals = add(names, totals)
+    totals, (slots, left) = add(names, totals, keep=left_slots([("near", *kind) for kind in second]))
     a3, ab3, totals = lax.optimization_barrier((a3, ab3, totals))
     (stack,) = route(route_last, [a3, ab3], (2,), weight=10**11)
     put("3a", stack, "near", third[:2])
     stack = swap(stack)
     put("3d", far2, "far", second)
-    totals = add([("far", *kind) for kind in second], totals)
+    totals = add([("far", *kind) for kind in second], totals, left=(slots, left))
     put("3b", b3, "near", third[2:])
     totals = fence(totals)
 
     put("4a", stack, "far", third[:2])
     far3 = swap(near("B", 3))
-    totals, left = add([("near", *kind) for kind in third], totals, keep=True)
+    names = [("near", *kind) for kind in third]
+    totals, (slots, left) = add(names, totals, keep=left_slots(names))
     put("4b", far3, "far", third[2:])
     totals, left = fence((totals, left))
-    return add([("far", *kind) for kind in third], totals, left=left)
+    return add([("far", *kind) for kind in third], totals, left=(slots, left), last=True)
 
 
 def add_terms(place_ref, weights_ref, left_ref, right_ref, field_ref):
@@ -402,15 +412,15 @@
     place = [lax.axis_index(name) for name in AXES]
     place = jnp.stack(place + [owned // 4 % 4, jnp.int32(flat), owned % 4]).astype(jnp.int32)
 
-    packed = jnp.transpose(modes.reshape(slots, per_block, 4, 3, site_count), (2, 1, 0, 3, 4))
-    packed = packed.reshape(4, per_block, slots * 3 * site_count)
-
     mine = lax.dynamic_slice_in_dim(momenta, owned // 16, 1, 0)
     weights = phase_table(mine, jnp.int32(0), sites * site_count, LEXT)[0]
     weights = jnp.transpose(weights.reshape(2, sites, site_count), (1, 0, 2))
 
-    if (groups, deep, flat) == (2, 4, 2) and share in (8, 16, 32):
-        return swap_in_windows(packed, weights, share)
+    if (groups, deep, flat) == (2, 4, 2) and steps == 1 and share in (8, 16, 32):
+        own = jnp.transpose(modes[:, 0], (0, 2, 1, 3))
+        return swap_in_windows(own, weights, share)
+    packed = jnp.transpose(modes.reshape(slots, per_block, 4, 3, site_count), (2, 1, 0, 3, 4))
+    packed = packed.reshape(4, per_block, slots * 3 * site_count)
     return gather_whole(packed, place, weights, share)
 
 

time: 66.1 us -> 69.5 us (1.051)
  waiting for transfers between devices: 31.4 us -> 37.3 us
  starting transfers between devices: 21 us -> 18.6 us
    ppermute x17, waiting for transfers between devices: 31.4 us -> 37.3 us  [move(): return lax.ppermute(array, AXES, pairs)]
    ppermute x17, starting transfers between devices: 21 us -> 18.6 us  [move(): return lax.ppermute(array, AXES, pairs)]
    unnamed x2 -> x6, local copies, waits for them, and re-layouts: 0.01 us -> 2 us
    reshape x2 -> x0, local copies, waits for them, and re-layouts: 1.69 us -> none  [the longest x1 1.35 us: shards(): modes.reshape(slots, per_block, 4, 3, site_count)]
  transfers between devices with their start and end apart: 17 -> 17, of which waited for: 6 -> 10; matrix products, arithmetic and copies ran while one was open for 0% -> 0% of each run, Pallas kernels for 14% -> 12%
where the time goes in v13:
time: 69.5 us; the launch traced here: 69.3 us
  waiting for transfers between devices  37.3 us (54%)
  starting transfers between devices  18.6 us (27%)
  Pallas kernels  11 us (16%)
  local copies, waits for them, and re-layouts  2 us (3%)
    ppermute x17, waiting for transfers between devices, move(): return lax.ppermute(array, AXES, pairs)  37.3 us
    ppermute x17, starting transfers between devices, move(): return lax.ppermute(array, AXES, pairs)  18.6 us
    pallas_call x7, Pallas kernels, add(): pl.pallas_call(functools.partial(add_shards, tuple(names), places, slots,...  10.5 us
    unnamed x6, local copies, waits for them, and re-layouts  2 us
  transfers between devices with their start and end apart: 17, of which 10 were waited for; matrix products, arithmetic and copies ran while one was open for 0% of the time, Pallas kernels for 12%

profile of v13, /device:TPU:0, one launch (start us, length us, event | category | flops | bytes accessed | tf_op | source)
XLA Modules:
  0.0 69.3 jit_solution(1171189312989867692)
XLA Ops:
  0.0 0.0 copy-start
  0.0 4.0 %collective-permute-start = (bf16[2,12,64,128]{3,2,1,0:T(8,128)(2,1)}, bf16[2,12,64,128]{3,2,1,0:T(8,128)(2,1)S(1)}, u32[]{:S(2)}, u32[]{:S(2)}) collective-permute-start(bf16[2,12,64,128]{3,2,1,0:T(8,128)(2,1)} %bitcast.24), channel_id=1, source_target_pairs={{0,4},{1,5},{2,6},{3,7},{4,0},{5,1},{6,2},{7,3},{8,12},{9,13},{10,... | collective-permute-start | bytes 1179656 | tf_op jit(solution)/shard_map/ppermute | solution.py:197
  4.0 1.6 %collective-permute-start.1 = (bf16[2,12,64,128]{3,2,1,0:T(8,128)(2,1)}, bf16[2,12,64,128]{3,2,1,0:T(8,128)(2,1)S(1)}, u32[]{:S(2)}, u32[]{:S(2)}) collective-permute-start(bf16[2,12,64,128]{3,2,1,0:T(8,128)(2,1)} %bitcast.25), channel_id=1, source_target_pairs={{0,2},{1,3},{2,0},{3,1},{4,6},{5,7},{6,4},{7,5},{8,10},{9,11},{10,... | collective-permute-start | bytes 1179656 | tf_op jit(solution)/shard_map/ppermute | solution.py:197
  5.6 1.5 %collective-permute-start.2 = (bf16[2,12,64,128]{3,2,1,0:T(8,128)(2,1)}, bf16[2,12,64,128]{3,2,1,0:T(8,128)(2,1)S(1)}, u32[]{:S(2)}, u32[]{:S(2)}) collective-permute-start(bf16[2,12,64,128]{3,2,1,0:T(8,128)(2,1)} %bitcast.26), channel_id=1, source_target_pairs={{0,1},{1,0},{2,3},{3,2},{4,5},{5,4},{6,7},{7,6},{8,24},{9,25},{10,... | collective-permute-start | bytes 1179656 | tf_op jit(solution)/shard_map/ppermute | solution.py:197
  7.1 1.5 %collective-permute-start.3 = (bf16[2,12,64,128]{3,2,1,0:T(8,128)(2,1)}, bf16[2,12,64,128]{3,2,1,0:T(8,128)(2,1)S(1)}, u32[]{:S(2)}, u32[]{:S(2)}) collective-permute-start(bf16[2,12,64,128]{3,2,1,0:T(8,128)(2,1)} %bitcast.27), channel_id=1, source_target_pairs={{0,16},{1,17},{2,18},{3,19},{4,20},{5,21},{6,22},{7,23},{8,9},{9,8... | collective-permute-start | bytes 1179656 | tf_op jit(solution)/shard_map/ppermute | solution.py:197
  8.6 0.0 copy-done
  8.7 0.1 fusion
  8.8 7.3 %collective-permute-done.3.refs_1_.refs_3_ = bf16[2,12,64,128]{3,2,1,0:T(8,128)(2,1)S(1)} collective-permute-done((bf16[2,12,64,128]{3,2,1,0:T(8,128)(2,1)}, bf16[2,12,64,128]{3,2,1,0:T(8,128)(2,1)S(1)}, u32[]{:S(2)}, u32[]{:S(2)}) %collective-permute-start.3) | collective-permute-done | bytes 393248 | tf_op jit(solution)/shard_map/ppermute | solution.py:197
  16.1 1.5 %collective-permute-start.4 = (bf16[2,12,64,128]{3,2,1,0:T(8,128)(2,1)S(1)}, bf16[2,12,64,128]{3,2,1,0:T(8,128)(2,1)S(1)}, u32[]{:S(2)}, u32[]{:S(2)}) collective-permute-start(bf16[2,12,64,128]{3,2,1,0:T(8,128)(2,1)S(1)} %collective-permute-done.3.refs_1_.refs_3_), channel_id=1, source_target_pairs={{0,1},{1,0},{2,3},{3,2},{4,5},{5,4},{6,7},{7,6},{8,24},{9,25},{10,... | collective-permute-start | bytes 1179656 | tf_op jit(solution)/shard_map/ppermute | solution.py:197
  17.7 0.1 multiply_cosine_fusion
  17.8 4.1 %collective-permute-done.refs_5_.refs_0_ = bf16[2,12,64,128]{3,2,1,0:T(8,128)(2,1)S(1)} collective-permute-done((bf16[2,12,64,128]{3,2,1,0:T(8,128)(2,1)}, bf16[2,12,64,128]{3,2,1,0:T(8,128)(2,1)S(1)}, u32[]{:S(2)}, u32[]{:S(2)}) %collective-permute-start) | collective-permute-done | bytes 393248 | tf_op jit(solution)/shard_map/ppermute | solution.py:197
  21.9 0.2 collective-permute-done.1.refs_4_.refs_1_
  22.1 0.0 collective-permute-done.2.refs_2_
  22.1 1.8 %collective-permute-done.4.refs_3_.refs_4_ = bf16[2,12,64,128]{3,2,1,0:T(8,128)(2,1)S(1)} collective-permute-done((bf16[2,12,64,128]{3,2,1,0:T(8,128)(2,1)S(1)}, bf16[2,12,64,128]{3,2,1,0:T(8,128)(2,1)S(1)}, u32[]{:S(2)}, u32[]{:S(2)}) %collective-permute-start.4) | collective-permute-done | bytes 393248 | tf_op jit(solution)/shard_map/ppermute | solution.py:197
  23.9 0.0 copy-start.1
  23.9 1.0 %copy-done.1 = bf16[2,1,64,12,128]{4,2,3,1,0:T(8,128)(2,1)S(1)} copy-done((bf16[2,1,64,12,128]{4,2,3,1,0:T(8,128)(2,1)S(1)}, bf16[2,1,64,12,128]{4,2,3,1,0:T(8,128)(2,1)}, u32[]{:S(2)}) %copy-start.1) | copy-done | bytes 393240
  24.9 0.2 shard_map.28
  25.1 0.1 collective-permute-start.5
  25.3 0.5 collective-permute-start.6
  25.7 2.4 %collective-permute-start.7 = (bf16[2,12,64,128]{3,2,1,0:T(8,128)(2,1)S(1)}, bf16[2,12,64,128]{3,2,1,0:T(8,128)(2,1)S(1)}, u32[]{:S(2)}, u32[]{:S(2)}) collective-permute-start(bf16[2,12,64,128]{3,2,1,0:T(8,128)(2,1)S(1)} %get-tuple-element.93), channel_id=1, source_target_pairs={{0,17},{1,16},{2,19},{3,18},{4,21},{5,20},{6,23},{7,22},{8,12},{9,... | collective-permute-start | bytes 1179656 | tf_op jit(solution)/shard_map/ppermute | solution.py:197
  28.2 0.5 collective-permute-start.9
  28.7 0.5 collective-permute-start.10
  29.2 0.0 copy-start.2
  29.2 1.0 %copy-done.2 = bf16[2,1,64,12,128]{4,2,3,1,0:T(8,128)(2,1)S(1)} copy-done((bf16[2,1,64,12,128]{4,2,3,1,0:T(8,128)(2,1)S(1)}, bf16[2,1,64,12,128]{4,2,3,1,0:T(8,128)(2,1)}, u32[]{:S(2)}) %copy-start.2) | copy-done | bytes 393240
  30.2 1.8 %shard_map.29.refs_6_ = f32[2,2,256,256]{3,2,1,0:T(8,128)S(1)} custom-call(f32[8,2,128]{2,1,0:T(2,128)S(1)} %maximum_bitcast_fusion.weights_ref, bf16[2,12,64,128]{3,2,1,0:T(8,128)(2,1)S(1)} %collective-permute-done.refs_5_.refs_0_, bf16[2,12,64,128]{3,2,1,0:T(8,128)(2,1)S(1)} %collective-permute-done.1.refs_4_.refs_1_, ...), custom_call_target="tpu_custom_call" | custom-call | flops 1207959552 | bytes 4456448 | tf_op jit(solution)/shard_map/pallas_call | solution.py:258
  32.0 0.0 collective-permute-done.5.refs_4_
  32.0 1.6 %collective-permute-start.8 = (bf16[2,12,64,128]{3,2,1,0:T(8,128)(2,1)S(1)}, bf16[2,12,64,128]{3,2,1,0:T(8,128)(2,1)S(1)}, u32[]{:S(2)}, u32[]{:S(2)}) collective-permute-start(bf16[2,12,64,128]{3,2,1,0:T(8,128)(2,1)S(1)} %collective-permute-done.4.refs_3_.refs_4_), channel_id=1, source_target_pairs={{0,2},{1,3},{2,0},{3,1},{4,6},{5,7},{6,4},{7,5},{8,10},{9,11},{10,... | collective-permute-start | bytes 1179656 | tf_op jit(solution)/shard_map/ppermute | solution.py:197
  33.7 1.7 %shard_map.30.refs_1_ = f32[2,2,256,256]{3,2,1,0:T(8,128)S(1)} custom-call(f32[8,2,128]{2,1,0:T(2,128)S(1)} %maximum_bitcast_fusion.weights_ref, bf16[2,12,64,128]{3,2,1,0:T(8,128)(2,1)S(1)} %collective-permute-done.refs_5_.refs_0_, bf16[2,12,64,128]{3,2,1,0:T(8,128)(2,1)S(1)} %collective-permute-done.1.refs_4_.refs_1_, ...), custom_call_target="tpu_custom_call" | custom-call | flops 1207959552 | bytes 4456448 | tf_op jit(solution)/shard_map/pallas_call | solution.py:258
  35.4 6.0 %collective-permute-done.6.refs_0_.o3_ref.refs_3_ = bf16[2,12,64,128]{3,2,1,0:T(8,128)(2,1)S(1)} collective-permute-done((bf16[2,12,64,128]{3,2,1,0:T(8,128)(2,1)S(1)}, bf16[2,12,64,128]{3,2,1,0:T(8,128)(2,1)S(1)}, u32[]{:S(2)}, u32[]{:S(2)}) %collective-permute-start.6) | collective-permute-done | bytes 393248 | tf_op jit(solution)/shard_map/ppermute | solution.py:197
  41.4 0.0 collective-permute-done.7.ab2_ref.refs_4_
  41.4 1.5 %collective-permute-start.11 = (bf16[2,12,64,128]{3,2,1,0:T(8,128)(2,1)S(1)}, bf16[2,12,64,128]{3,2,1,0:T(8,128)(2,1)S(1)}, u32[]{:S(2)}, u32[]{:S(2)}) collective-permute-start(bf16[2,12,64,128]{3,2,1,0:T(8,128)(2,1)S(1)} %collective-permute-done.6.refs_0_.o3_ref.refs_3_), channel_id=1, source_target_pairs={{0,16},{1,17},{2,18},{3,19},{4,20},{5,21},{6,22},{7,23},{8,9},{9,8... | collective-permute-start | bytes 1179656 | tf_op jit(solution)/shard_map/ppermute | solution.py:197
  42.9 0.0 collective-permute-start.12
  42.9 0.4 shard_map.31.refs_7_
  43.3 8.0 %collective-permute-done.9.a12_ref.refs_5_ = bf16[2,2,12,64,128]{4,3,2,1,0:T(8,128)(2,1)S(1)} collective-permute-done((bf16[2,2,12,64,128]{4,3,2,1,0:T(8,128)(2,1)S(1)}, bf16[2,2,12,64,128]{4,3,2,1,0:T(8,128)(2,1)S(1)}, u32[]{:S(2)}, u32[]{:S(2)}) %collective-permute-start.9) | collective-permute-done | bytes 786464 | tf_op jit(solution)/shard_map/ppermute | solution.py:197
  51.3 0.5 collective-permute-start.13
  51.8 0.2 collective-permute-done.10.b12_ref.refs_6_
  52.0 0.0 collective-permute-done.8.ab1_ref.refs_2_
  52.0 0.2 shard_map.32
  52.2 1.7 %shard_map.33 = (f32[2,2,256,256]{3,2,1,0:T(8,128)S(1)}, bf16[5,512,768]{2,1,0:T(8,128)(2,1)S(1)}) custom-call(f32[8,2,128]{2,1,0:T(2,128)S(1)} %maximum_bitcast_fusion.weights_ref, bf16[2,12,64,128]{3,2,1,0:T(8,128)(2,1)S(1)} %collective-permute-done.refs_5_.refs_0_, bf16[2,12,64,128]{3,2,1,0:T(8,128)(2,1)S(1)} %collective-permute-done.1.refs_4_.refs_1_, ...), custom_call_target="tpu_custom_call" | custom-call | flops 1207959552 | bytes 4456448 | tf_op jit(solution)/shard_map/pallas_call | solution.py:258
  53.9 4.7 %collective-permute-done.11.a3_ref = bf16[2,12,64,128]{3,2,1,0:T(8,128)(2,1)S(1)} collective-permute-done((bf16[2,12,64,128]{3,2,1,0:T(8,128)(2,1)S(1)}, bf16[2,12,64,128]{3,2,1,0:T(8,128)(2,1)S(1)}, u32[]{:S(2)}, u32[]{:S(2)}) %collective-permute-start.11) | collective-permute-done | bytes 393248 | tf_op jit(solution)/shard_map/ppermute | solution.py:197
  58.6 0.0 collective-permute-done.12.ab3_ref
  58.6 0.0 collective-permute-start.14
  58.6 0.1 shard_map.34.refs_1_
  58.7 0.6 collective-permute-start.15
  59.3 4.5 %collective-permute-done.14.refs_0_ = bf16[7,2,12,64,128]{4,3,2,1,0:T(8,128)(2,1)S(1)} collective-permute-done((bf16[7,2,12,64,128]{4,3,2,1,0:T(8,128)(2,1)S(1)}, bf16[7,2,12,64,128]{4,3,2,1,0:T(8,128)(2,1)S(1)}, u32[]{:S(2)}, u32[]{:S(2)}) %collective-permute-start.14) | collective-permute-done | bytes 2752544 | tf_op jit(solution)/shard_map/ppermute | solution.py:197
  63.7 1.7 %shard_map.35.refs_3_ = f32[2,2,256,256]{3,2,1,0:T(8,128)S(1)} custom-call(f32[8,2,128]{2,1,0:T(2,128)S(1)} %maximum_bitcast_fusion.weights_ref, bf16[7,2,12,64,128]{4,3,2,1,0:T(8,128)(2,1)S(1)} %collective-permute-done.14.refs_0_, bf16[5,512,768]{2,1,0:T(8,128)(2,1)S(1)} %get-tuple-element.123.refs_1_, f32[2,2,256,256]{3,2,1,0:T(8,128)S(1)} %get-tuple-element.124.refs_2_), custom_call_target="tpu_custom_call" | custom-call | flops 1409286144 | bytes 4849664 | tf_op jit(solution)/shard_map/pallas_call | solution.py:258
  65.4 0.0 collective-permute-done.13.refs_2_
  65.4 0.2 collective-permute-start.16
  65.6 1.1 %shard_map.36 = (f32[2,2,256,256]{3,2,1,0:T(8,128)S(1)}, bf16[2,512,768]{2,1,0:T(8,128)(2,1)S(1)}) custom-call(f32[8,2,128]{2,1,0:T(2,128)S(1)} %maximum_bitcast_fusion.weights_ref, bf16[2,12,64,128]{3,2,1,0:T(8,128)(2,1)S(1)} %collective-permute-done.6.refs_0_.o3_ref.refs_3_, bf16[2,2,12,64,128]{4,3,2,1,0:T(8,128)(2,1)S(1)} %shard_map.34.refs_1_, ...), custom_call_target="tpu_custom_call" | custom-call | flops 603979776 | bytes 3276800 | tf_op jit(solution)/shard_map/pallas_call | solution.py:258
  66.7 0.0 collective-permute-done.15.refs_0_
  66.8 0.4 collective-permute-done.16.refs_1_
  67.2 2.1 %shard_map.37 = f32[16,64,256]{2,1,0:T(8,128)} custom-call(f32[8,2,128]{2,1,0:T(2,128)S(1)} %maximum_bitcast_fusion.weights_ref, bf16[2,2,12,64,128]{4,3,2,1,0:T(8,128)(2,1)S(1)} %collective-permute-done.15.refs_0_, bf16[2,12,64,128]{3,2,1,0:T(8,128)(2,1)S(1)} %collective-permute-done.16.refs_1_, bf16[2,512,768]{2,1,0:T(8,128)(2,1)S(1)} %get-tuple-element.133.refs_2_, ...), custom_call_target="tpu_custom_call" | custom-call | flops 603979776 | bytes 3276800 | tf_op jit(solution)/shard_map/pallas_call | solution.py:258
  (5 shorter events, 0.1 us)
Async XLA Ops:
  0.0 8.6 %copy-start = (s32[4,3]{1,0:T(4,128)S(1)}, s32[4,3]{1,0:T(4,128)}, u32[]{:S(2)}) copy-start(s32[4,3]{1,0:T(4,128)} %param.3) | copy-start | bytes 148
  0.0 21.9 %collective-permute-start = (bf16[2,12,64,128]{3,2,1,0:T(8,128)(2,1)}, bf16[2,12,64,128]{3,2,1,0:T(8,128)(2,1)S(1)}, u32[]{:S(2)}, u32[]{:S(2)}) collective-permute-start(bf16[2,12,64,128]{3,2,1,0:T(8,128)(2,1)} %bitcast.24), channel_id=1, source_target_pairs={{0,4},{1,5},{2,6},{3,7},{4,0},{5,1},{6,2},{7,3},{8,12},{9,13},{10,... | collective-permute-start | bytes 1179656 | tf_op jit(solution)/shard_map/ppermute | solution.py:197
  4.0 18.0 %collective-permute-start.1 = (bf16[2,12,64,128]{3,2,1,0:T(8,128)(2,1)}, bf16[2,12,64,128]{3,2,1,0:T(8,128)(2,1)S(1)}, u32[]{:S(2)}, u32[]{:S(2)}) collective-permute-start(bf16[2,12,64,128]{3,2,1,0:T(8,128)(2,1)} %bitcast.25), channel_id=1, source_target_pairs={{0,2},{1,3},{2,0},{3,1},{4,6},{5,7},{6,4},{7,5},{8,10},{9,11},{10,... | collective-permute-start | bytes 1179656 | tf_op jit(solution)/shard_map/ppermute | solution.py:197
  5.6 16.5 %collective-permute-start.2 = (bf16[2,12,64,128]{3,2,1,0:T(8,128)(2,1)}, bf16[2,12,64,128]{3,2,1,0:T(8,128)(2,1)S(1)}, u32[]{:S(2)}, u32[]{:S(2)}) collective-permute-start(bf16[2,12,64,128]{3,2,1,0:T(8,128)(2,1)} %bitcast.26), channel_id=1, source_target_pairs={{0,1},{1,0},{2,3},{3,2},{4,5},{5,4},{6,7},{7,6},{8,24},{9,25},{10,... | collective-permute-start | bytes 1179656 | tf_op jit(solution)/shard_map/ppermute | solution.py:197
  7.1 9.0 %collective-permute-start.3 = (bf16[2,12,64,128]{3,2,1,0:T(8,128)(2,1)}, bf16[2,12,64,128]{3,2,1,0:T(8,128)(2,1)S(1)}, u32[]{:S(2)}, u32[]{:S(2)}) collective-permute-start(bf16[2,12,64,128]{3,2,1,0:T(8,128)(2,1)} %bitcast.27), channel_id=1, source_target_pairs={{0,16},{1,17},{2,18},{3,19},{4,20},{5,21},{6,22},{7,23},{8,9},{9,8... | collective-permute-start | bytes 1179656 | tf_op jit(solution)/shard_map/ppermute | solution.py:197
  16.1 7.8 %collective-permute-start.4 = (bf16[2,12,64,128]{3,2,1,0:T(8,128)(2,1)S(1)}, bf16[2,12,64,128]{3,2,1,0:T(8,128)(2,1)S(1)}, u32[]{:S(2)}, u32[]{:S(2)}) collective-permute-start(bf16[2,12,64,128]{3,2,1,0:T(8,128)(2,1)S(1)} %collective-permute-done.3.refs_1_.refs_3_), channel_id=1, source_target_pairs={{0,1},{1,0},{2,3},{3,2},{4,5},{5,4},{6,7},{7,6},{8,24},{9,25},{10,... | collective-permute-start | bytes 1179656 | tf_op jit(solution)/shard_map/ppermute | solution.py:197
  23.9 1.0 %copy-start.1 = (bf16[2,1,64,12,128]{4,2,3,1,0:T(8,128)(2,1)S(1)}, bf16[2,1,64,12,128]{4,2,3,1,0:T(8,128)(2,1)}, u32[]{:S(2)}) copy-start(bf16[2,1,64,12,128]{4,2,3,1,0:T(8,128)(2,1)} %param.2) | copy-start | bytes 1179652
  25.1 6.9 %collective-permute-start.5 = (bf16[6,2,12,64,128]{4,3,2,1,0:T(8,128)(2,1)S(1)}, bf16[6,2,12,64,128]{4,3,2,1,0:T(8,128)(2,1)S(1)}, u32[]{:S(2)}, u32[]{:S(2)}) collective-permute-start(bf16[6,2,12,64,128]{4,3,2,1,0:T(8,128)(2,1)S(1)} %get-tuple-element.85), channel_id=1, source_target_pairs={{0,8},{1,9},{2,10},{3,11},{4,12},{5,13},{6,14},{7,15},{8,0},{9,1},... | collective-permute-start | bytes 7077896 | tf_op jit(solution)/shard_map/ppermute | solution.py:197
  25.3 16.2 %collective-permute-start.6 = (bf16[2,12,64,128]{3,2,1,0:T(8,128)(2,1)S(1)}, bf16[2,12,64,128]{3,2,1,0:T(8,128)(2,1)S(1)}, u32[]{:S(2)}, u32[]{:S(2)}) collective-permute-start(bf16[2,12,64,128]{3,2,1,0:T(8,128)(2,1)S(1)} %collective-permute-done.refs_5_.refs_0_), channel_id=1, source_target_pairs={{0,2},{1,3},{2,0},{3,1},{4,6},{5,7},{6,4},{7,5},{8,10},{9,11},{10,... | collective-permute-start | bytes 1179656 | tf_op jit(solution)/shard_map/ppermute | solution.py:197
  25.7 15.7 %collective-permute-start.7 = (bf16[2,12,64,128]{3,2,1,0:T(8,128)(2,1)S(1)}, bf16[2,12,64,128]{3,2,1,0:T(8,128)(2,1)S(1)}, u32[]{:S(2)}, u32[]{:S(2)}) collective-permute-start(bf16[2,12,64,128]{3,2,1,0:T(8,128)(2,1)S(1)} %get-tuple-element.93), channel_id=1, source_target_pairs={{0,17},{1,16},{2,19},{3,18},{4,21},{5,20},{6,23},{7,22},{8,12},{9,... | collective-permute-start | bytes 1179656 | tf_op jit(solution)/shard_map/ppermute | solution.py:197
  28.2 23.1 %collective-permute-start.9 = (bf16[2,2,12,64,128]{4,3,2,1,0:T(8,128)(2,1)S(1)}, bf16[2,2,12,64,128]{4,3,2,1,0:T(8,128)(2,1)S(1)}, u32[]{:S(2)}, u32[]{:S(2)}) collective-permute-start(bf16[2,2,12,64,128]{4,3,2,1,0:T(8,128)(2,1)S(1)} %get-tuple-element.100), channel_id=1, source_target_pairs={{0,16},{1,17},{2,18},{3,19},{4,20},{5,21},{6,22},{7,23},{8,9},{9,8... | collective-permute-start | bytes 2359304 | tf_op jit(solution)/shard_map/ppermute | solution.py:197
  28.7 23.3 %collective-permute-start.10 = (bf16[2,2,12,64,128]{4,3,2,1,0:T(8,128)(2,1)S(1)}, bf16[2,2,12,64,128]{4,3,2,1,0:T(8,128)(2,1)S(1)}, u32[]{:S(2)}, u32[]{:S(2)}) collective-permute-start(bf16[2,2,12,64,128]{4,3,2,1,0:T(8,128)(2,1)S(1)} %get-tuple-element.100), channel_id=1, source_target_pairs={{0,1},{1,0},{2,3},{3,2},{4,5},{5,4},{6,7},{7,6},{8,24},{9,25},{10,... | collective-permute-start | bytes 2359304 | tf_op jit(solution)/shard_map/ppermute | solution.py:197
  29.2 1.0 %copy-start.2 = (bf16[2,1,64,12,128]{4,2,3,1,0:T(8,128)(2,1)S(1)}, bf16[2,1,64,12,128]{4,2,3,1,0:T(8,128)(2,1)}, u32[]{:S(2)}) copy-start(bf16[2,1,64,12,128]{4,2,3,1,0:T(8,128)(2,1)} %param.2) | copy-start | bytes 1179652
  32.0 20.0 %collective-permute-start.8 = (bf16[2,12,64,128]{3,2,1,0:T(8,128)(2,1)S(1)}, bf16[2,12,64,128]{3,2,1,0:T(8,128)(2,1)S(1)}, u32[]{:S(2)}, u32[]{:S(2)}) collective-permute-start(bf16[2,12,64,128]{3,2,1,0:T(8,128)(2,1)S(1)} %collective-permute-done.4.refs_3_.refs_4_), channel_id=1, source_target_pairs={{0,2},{1,3},{2,0},{3,1},{4,6},{5,7},{6,4},{7,5},{8,10},{9,11},{10,... | collective-permute-start | bytes 1179656 | tf_op jit(solution)/shard_map/ppermute | solution.py:197
  41.4 17.2 %collective-permute-start.11 = (bf16[2,12,64,128]{3,2,1,0:T(8,128)(2,1)S(1)}, bf16[2,12,64,128]{3,2,1,0:T(8,128)(2,1)S(1)}, u32[]{:S(2)}, u32[]{:S(2)}) collective-permute-start(bf16[2,12,64,128]{3,2,1,0:T(8,128)(2,1)S(1)} %collective-permute-done.6.refs_0_.o3_ref.refs_3_), channel_id=1, source_target_pairs={{0,16},{1,17},{2,18},{3,19},{4,20},{5,21},{6,22},{7,23},{8,9},{9,8... | collective-permute-start | bytes 1179656 | tf_op jit(solution)/shard_map/ppermute | solution.py:197
  42.9 15.7 %collective-permute-start.12 = (bf16[2,12,64,128]{3,2,1,0:T(8,128)(2,1)S(1)}, bf16[2,12,64,128]{3,2,1,0:T(8,128)(2,1)S(1)}, u32[]{:S(2)}, u32[]{:S(2)}) collective-permute-start(bf16[2,12,64,128]{3,2,1,0:T(8,128)(2,1)S(1)} %collective-permute-done.7.ab2_ref.refs_4_), channel_id=1, source_target_pairs={{0,2},{1,3},{2,0},{3,1},{4,6},{5,7},{6,4},{7,5},{8,10},{9,11},{10,... | collective-permute-start | bytes 1179656 | tf_op jit(solution)/shard_map/ppermute | solution.py:197
  51.3 14.1 %collective-permute-start.13 = (bf16[2,12,64,128]{3,2,1,0:T(8,128)(2,1)S(1)}, bf16[2,12,64,128]{3,2,1,0:T(8,128)(2,1)S(1)}, u32[]{:S(2)}, u32[]{:S(2)}) collective-permute-start(bf16[2,12,64,128]{3,2,1,0:T(8,128)(2,1)S(1)} %collective-permute-done.6.refs_0_.o3_ref.refs_3_), channel_id=1, source_target_pairs={{0,1},{1,0},{2,3},{3,2},{4,5},{5,4},{6,7},{7,6},{8,24},{9,25},{10,... | collective-permute-start | bytes 1179656 | tf_op jit(solution)/shard_map/ppermute | solution.py:197
  58.6 5.1 %collective-permute-start.14 = (bf16[7,2,12,64,128]{4,3,2,1,0:T(8,128)(2,1)S(1)}, bf16[7,2,12,64,128]{4,3,2,1,0:T(8,128)(2,1)S(1)}, u32[]{:S(2)}, u32[]{:S(2)}) collective-permute-start(bf16[7,2,12,64,128]{4,3,2,1,0:T(8,128)(2,1)S(1)} %shard_map.32), channel_id=1, source_target_pairs={{0,8},{1,9},{2,10},{3,11},{4,12},{5,13},{6,14},{7,15},{8,0},{9,1},... | collective-permute-start | bytes 8257544 | tf_op jit(solution)/shard_map/ppermute | solution.py:197
  58.7 8.1 %collective-permute-start.15 = (bf16[2,2,12,64,128]{4,3,2,1,0:T(8,128)(2,1)S(1)}, bf16[2,2,12,64,128]{4,3,2,1,0:T(8,128)(2,1)S(1)}, u32[]{:S(2)}, u32[]{:S(2)}) collective-permute-start(bf16[2,2,12,64,128]{4,3,2,1,0:T(8,128)(2,1)S(1)} %shard_map.34.refs_1_), channel_id=1, source_target_pairs={{0,8},{1,9},{2,10},{3,11},{4,12},{5,13},{6,14},{7,15},{8,0},{9,1},... | collective-permute-start | bytes 2359304 | tf_op jit(solution)/shard_map/ppermute | solution.py:197
  65.4 1.8 %collective-permute-start.16 = (bf16[2,12,64,128]{3,2,1,0:T(8,128)(2,1)S(1)}, bf16[2,12,64,128]{3,2,1,0:T(8,128)(2,1)S(1)}, u32[]{:S(2)}, u32[]{:S(2)}) collective-permute-start(bf16[2,12,64,128]{3,2,1,0:T(8,128)(2,1)S(1)} %collective-permute-done.13.refs_2_), channel_id=1, source_target_pairs={{0,8},{1,9},{2,10},{3,11},{4,12},{5,13},{6,14},{7,15},{8,0},{9,1},... | collective-permute-start | bytes 1179656 | tf_op jit(solution)/shard_map/ppermute | solution.py:197

commit v14 on v13

--- a/solution.py
+++ b/solution.py
@@ -138,6 +138,12 @@
                 copies[-1].start()
         for copy in copies:
             copy.wait()
+
+
+def fetch(from_ref, to_ref, sem):
+    copy = pltpu.make_async_copy(from_ref, to_ref, sem)
+    copy.start()
+    copy.wait()
 
 
 def route_second(*refs):
@@ -277,13 +283,19 @@
         arrays, totals = lax.optimization_barrier((arrays, totals))
         return totals
 
-    put("9", own, "near", [("O", 0)])
-
     put("1a", hop_z(own, 2), "near", [("O", 2)])
-    put("1b", hop_z(own, 1), "near", [("O", 1)])
-    put("1c", hop_b(own), "near", [("B", 0)])
-    put("1d", hop_a(own), "near", [("A", 0)])
+    put("1b", hop_a(own), "near", [("A", 0)])
+    put("1c", hop_z(own, 1), "near", [("O", 1)])
+    put("1d", hop_b(own), "near", [("B", 0)])
     put("1e", hop_b(near("A", 0)), "near", [("AB", 0)])
+    held = pl.pallas_call(
+        fetch,
+        in_specs=[pl.BlockSpec(memory_space=pl.ANY)],
+        out_specs=pl.BlockSpec(memory_space=pltpu.VMEM),
+        out_shape=jax.ShapeDtypeStruct(own.shape, own.dtype),
+        scratch_shapes=[pltpu.SemaphoreType.DMA],
+    )(own)
+    put("9", held, "near", [("O", 0)])
     weights = fence(weights)
 
     def route(kernel, operands, counts, weight=0):
@@ -326,13 +338,13 @@
     (stack,) = route(route_third, [arrays[key] for key in keys], (7,))
     far2 = swap(stack)
     names = [("near", *kind) for kind in second if kind != ("O", 3)]
-    totals, (slots, left) = add(names, totals, keep=left_slots([("near", *kind) for kind in second]))
+    totals = add(names, totals)
     a3, ab3, totals = lax.optimization_barrier((a3, ab3, totals))
     (stack,) = route(route_last, [a3, ab3], (2,), weight=10**11)
     put("3a", stack, "near", third[:2])
     stack = swap(stack)
     put("3d", far2, "far", second)
-    totals = add([("far", *kind) for kind in second], totals, left=(slots, left))
+    totals = add([("far", *kind) for kind in second], totals)
     put("3b", b3, "near", third[2:])
     totals = fence(totals)
 

time: 69.5 us -> 65.5 us (0.942)
  waiting for transfers between devices: 37.3 us -> 30 us
  starting transfers between devices: 18.6 us -> 20.9 us
  Pallas kernels: 11 us -> 13 us
  local copies, waits for them, and re-layouts: 2 us -> 1.01 us
    ppermute x17, waiting for transfers between devices: 37.3 us -> 30 us  [move(): return lax.ppermute(array, AXES, pairs)]
    ppermute x17, starting transfers between devices: 18.6 us -> 20.9 us  [move(): return lax.ppermute(array, AXES, pairs)]
    pallas_call x0 -> x1, Pallas kernels: none -> 1.75 us  [swap_in_windows(): pl.pallas_call(fetch, in_specs=[pl.BlockSpec(memory_space=pl.ANY)], out_s...]
    unnamed x6, local copies, waits for them, and re-layouts: 2 us -> 1 us
  transfers between devices with their start and end apart: 17 -> 17, of which waited for: 10 -> 7; matrix products, arithmetic and copies ran while one was open for 0% -> 0% of each run, Pallas kernels for 12% -> 16%
where the time goes in v14:
time: 65.5 us; the launch traced here: 65.4 us
  waiting for transfers between devices  30 us (46%)
  starting transfers between devices  20.9 us (32%)
  Pallas kernels  13 us (20%)
  local copies, waits for them, and re-layouts  1.01 us (2%)
    ppermute x17, waiting for transfers between devices, move(): return lax.ppermute(array, AXES, pairs)  30 us
    ppermute x17, starting transfers between devices, move(): return lax.ppermute(array, AXES, pairs)  20.9 us
    pallas_call x7, Pallas kernels, add(): pl.pallas_call(functools.partial(add_shards, tuple(names), places, slots,...  10.7 us
    pallas_call x1, Pallas kernels, swap_in_windows(): pl.pallas_call(fetch, in_specs=[pl.BlockSpec(memory_space=pl.ANY)], out_s...  1.75 us
  transfers between devices with their start and end apart: 17, of which 7 were waited for; matrix products, arithmetic and copies ran while one was open for 0% of the time, Pallas kernels for 16%

profile of v14, /device:TPU:0, one launch (start us, length us, event | category | flops | bytes accessed | tf_op | source)
XLA Modules:
  0.0 65.4 jit_solution(5935695436965897556)
XLA Ops:
  0.0 0.0 copy-start
  0.0 2.9 %collective-permute-start.1 = (bf16[2,12,64,128]{3,2,1,0:T(8,128)(2,1)}, bf16[2,12,64,128]{3,2,1,0:T(8,128)(2,1)S(1)}, u32[]{:S(2)}, u32[]{:S(2)}) collective-permute-start(bf16[2,12,64,128]{3,2,1,0:T(8,128)(2,1)} %bitcast.24), channel_id=1, source_target_pairs={{0,16},{1,17},{2,18},{3,19},{4,20},{5,21},{6,22},{7,23},{8,9},{9,8... | collective-permute-start | bytes 1179656 | tf_op jit(solution)/shard_map/ppermute | solution.py:203
  2.9 2.6 %collective-permute-start = (bf16[2,12,64,128]{3,2,1,0:T(8,128)(2,1)}, bf16[2,12,64,128]{3,2,1,0:T(8,128)(2,1)S(1)}, u32[]{:S(2)}, u32[]{:S(2)}) collective-permute-start(bf16[2,12,64,128]{3,2,1,0:T(8,128)(2,1)} %bitcast.25), channel_id=1, source_target_pairs={{0,4},{1,5},{2,6},{3,7},{4,0},{5,1},{6,2},{7,3},{8,12},{9,13},{10,... | collective-permute-start | bytes 1179656 | tf_op jit(solution)/shard_map/ppermute | solution.py:203
  5.5 1.6 %collective-permute-start.2 = (bf16[2,12,64,128]{3,2,1,0:T(8,128)(2,1)}, bf16[2,12,64,128]{3,2,1,0:T(8,128)(2,1)S(1)}, u32[]{:S(2)}, u32[]{:S(2)}) collective-permute-start(bf16[2,12,64,128]{3,2,1,0:T(8,128)(2,1)} %bitcast.26), channel_id=1, source_target_pairs={{0,2},{1,3},{2,0},{3,1},{4,6},{5,7},{6,4},{7,5},{8,10},{9,11},{10,... | collective-permute-start | bytes 1179656 | tf_op jit(solution)/shard_map/ppermute | solution.py:203
  7.1 1.5 %collective-permute-start.3 = (bf16[2,12,64,128]{3,2,1,0:T(8,128)(2,1)}, bf16[2,12,64,128]{3,2,1,0:T(8,128)(2,1)S(1)}, u32[]{:S(2)}, u32[]{:S(2)}) collective-permute-start(bf16[2,12,64,128]{3,2,1,0:T(8,128)(2,1)} %bitcast.27), channel_id=1, source_target_pairs={{0,1},{1,0},{2,3},{3,2},{4,5},{5,4},{6,7},{7,6},{8,24},{9,25},{10,... | collective-permute-start | bytes 1179656 | tf_op jit(solution)/shard_map/ppermute | solution.py:203
  8.6 0.0 copy-done
  8.7 0.1 fusion
  8.8 0.2 collective-permute-done.1.refs_1_
  9.0 3.4 %collective-permute-start.4 = (bf16[2,12,64,128]{3,2,1,0:T(8,128)(2,1)S(1)}, bf16[2,12,64,128]{3,2,1,0:T(8,128)(2,1)S(1)}, u32[]{:S(2)}, u32[]{:S(2)}) collective-permute-start(bf16[2,12,64,128]{3,2,1,0:T(8,128)(2,1)S(1)} %collective-permute-done.1.refs_1_), channel_id=1, source_target_pairs={{0,1},{1,0},{2,3},{3,2},{4,5},{5,4},{6,7},{7,6},{8,24},{9,25},{10,... | collective-permute-start | bytes 1179656 | tf_op jit(solution)/shard_map/ppermute | solution.py:203
  12.4 1.7 %shard_map.28.refs_0_.refs_5_ = bf16[2,12,64,128]{3,2,1,0:T(8,128)(2,1)} custom-call(bf16[2,12,64,128]{3,2,1,0:T(8,128)(2,1)} %bitcast.28), custom_call_target="tpu_custom_call" | custom-call | tf_op jit(solution)/shard_map/pallas_call | solution.py:291
  14.2 0.1 multiply_cosine_fusion
  14.3 8.9 %collective-permute-done.refs_5_.refs_0_ = bf16[2,12,64,128]{3,2,1,0:T(8,128)(2,1)S(1)} collective-permute-done((bf16[2,12,64,128]{3,2,1,0:T(8,128)(2,1)}, bf16[2,12,64,128]{3,2,1,0:T(8,128)(2,1)S(1)}, u32[]{:S(2)}, u32[]{:S(2)}) %collective-permute-start) | collective-permute-done | bytes 393248 | tf_op jit(solution)/shard_map/ppermute | solution.py:203
  23.2 0.2 collective-permute-done.2.refs_4_.refs_2_.refs_1_
  23.4 0.0 collective-permute-done.3.refs_2_.refs_3_
  23.4 0.0 collective-permute-done.4.refs_3_.refs_4_
  23.4 0.0 copy-start.1
  23.4 1.0 %copy-done.1 = bf16[2,12,64,128]{3,2,1,0:T(8,128)(2,1)S(1)} copy-done((bf16[2,12,64,128]{3,2,1,0:T(8,128)(2,1)S(1)}, bf16[2,12,64,128]{3,2,1,0:T(8,128)(2,1)}, u32[]{:S(2)}) %copy-start.1) | copy-done | bytes 393240
  24.4 0.0 copy-start.2
  24.4 0.2 shard_map.29
  24.6 0.1 collective-permute-start.5
  24.7 1.5 %collective-permute-start.6 = (bf16[2,12,64,128]{3,2,1,0:T(8,128)(2,1)S(1)}, bf16[2,12,64,128]{3,2,1,0:T(8,128)(2,1)S(1)}, u32[]{:S(2)}, u32[]{:S(2)}) collective-permute-start(bf16[2,12,64,128]{3,2,1,0:T(8,128)(2,1)S(1)} %collective-permute-done.refs_5_.refs_0_), channel_id=1, source_target_pairs={{0,2},{1,3},{2,0},{3,1},{4,6},{5,7},{6,4},{7,5},{8,10},{9,11},{10,... | collective-permute-start | bytes 1179656 | tf_op jit(solution)/shard_map/ppermute | solution.py:203
  26.2 1.4 %collective-permute-start.7 = (bf16[2,12,64,128]{3,2,1,0:T(8,128)(2,1)S(1)}, bf16[2,12,64,128]{3,2,1,0:T(8,128)(2,1)S(1)}, u32[]{:S(2)}, u32[]{:S(2)}) collective-permute-start(bf16[2,12,64,128]{3,2,1,0:T(8,128)(2,1)S(1)} %get-tuple-element.95), channel_id=1, source_target_pairs={{0,17},{1,16},{2,19},{3,18},{4,21},{5,20},{6,23},{7,22},{8,12},{9,... | collective-permute-start | bytes 1179656 | tf_op jit(solution)/shard_map/ppermute | solution.py:203
  27.6 1.5 %collective-permute-start.10 = (bf16[2,2,12,64,128]{4,3,2,1,0:T(8,128)(2,1)S(1)}, bf16[2,2,12,64,128]{4,3,2,1,0:T(8,128)(2,1)S(1)}, u32[]{:S(2)}, u32[]{:S(2)}) collective-permute-start(bf16[2,2,12,64,128]{4,3,2,1,0:T(8,128)(2,1)S(1)} %get-tuple-element.102), channel_id=1, source_target_pairs={{0,1},{1,0},{2,3},{3,2},{4,5},{5,4},{6,7},{7,6},{8,24},{9,25},{10,... | collective-permute-start | bytes 2359304 | tf_op jit(solution)/shard_map/ppermute | solution.py:203
  29.2 0.5 collective-permute-start.9
  29.7 0.0 copy-done.2
  29.7 1.8 %shard_map.30.refs_6_ = f32[2,2,256,256]{3,2,1,0:T(8,128)S(1)} custom-call(f32[8,2,128]{2,1,0:T(2,128)S(1)} %maximum_bitcast_fusion.weights_ref, bf16[2,12,64,128]{3,2,1,0:T(8,128)(2,1)S(1)} %collective-permute-done.refs_5_.refs_0_, bf16[2,12,64,128]{3,2,1,0:T(8,128)(2,1)S(1)} %collective-permute-done.1.refs_1_, ...), custom_call_target="tpu_custom_call" | custom-call | flops 1207959552 | bytes 4456448 | tf_op jit(solution)/shard_map/pallas_call | solution.py:264
  31.5 0.0 collective-permute-done.5.refs_4_
  31.5 0.7 %collective-permute-start.8 = (bf16[2,12,64,128]{3,2,1,0:T(8,128)(2,1)S(1)}, bf16[2,12,64,128]{3,2,1,0:T(8,128)(2,1)S(1)}, u32[]{:S(2)}, u32[]{:S(2)}) collective-permute-start(bf16[2,12,64,128]{3,2,1,0:T(8,128)(2,1)S(1)} %collective-permute-done.4.refs_3_.refs_4_), channel_id=1, source_target_pairs={{0,2},{1,3},{2,0},{3,1},{4,6},{5,7},{6,4},{7,5},{8,10},{9,11},{10,... | collective-permute-start | bytes 1179656 | tf_op jit(solution)/shard_map/ppermute | solution.py:203
  32.2 1.7 %shard_map.31.refs_1_ = f32[2,2,256,256]{3,2,1,0:T(8,128)S(1)} custom-call(f32[8,2,128]{2,1,0:T(2,128)S(1)} %maximum_bitcast_fusion.weights_ref, bf16[2,12,64,128]{3,2,1,0:T(8,128)(2,1)S(1)} %collective-permute-done.refs_5_.refs_0_, bf16[2,12,64,128]{3,2,1,0:T(8,128)(2,1)S(1)} %collective-permute-done.1.refs_1_, ...), custom_call_target="tpu_custom_call" | custom-call | flops 1207959552 | bytes 4456448 | tf_op jit(solution)/shard_map/pallas_call | solution.py:264
  33.9 7.0 %collective-permute-done.6.refs_0_.o3_ref.refs_2_ = bf16[2,12,64,128]{3,2,1,0:T(8,128)(2,1)S(1)} collective-permute-done((bf16[2,12,64,128]{3,2,1,0:T(8,128)(2,1)S(1)}, bf16[2,12,64,128]{3,2,1,0:T(8,128)(2,1)S(1)}, u32[]{:S(2)}, u32[]{:S(2)}) %collective-permute-start.6) | collective-permute-done | bytes 393248 | tf_op jit(solution)/shard_map/ppermute | solution.py:203
  40.9 0.0 collective-permute-done.7.ab2_ref.refs_3_
  40.9 1.5 %collective-permute-start.11 = (bf16[2,12,64,128]{3,2,1,0:T(8,128)(2,1)S(1)}, bf16[2,12,64,128]{3,2,1,0:T(8,128)(2,1)S(1)}, u32[]{:S(2)}, u32[]{:S(2)}) collective-permute-start(bf16[2,12,64,128]{3,2,1,0:T(8,128)(2,1)S(1)} %collective-permute-done.6.refs_0_.o3_ref.refs_2_), channel_id=1, source_target_pairs={{0,16},{1,17},{2,18},{3,19},{4,20},{5,21},{6,22},{7,23},{8,9},{9,8... | collective-permute-start | bytes 1179656 | tf_op jit(solution)/shard_map/ppermute | solution.py:203
  42.4 0.0 collective-permute-start.12
  42.4 0.4 shard_map.32.refs_6_
  42.8 8.5 %collective-permute-done.10.b12_ref.refs_5_.refs_4_ = bf16[2,2,12,64,128]{4,3,2,1,0:T(8,128)(2,1)S(1)} collective-permute-done((bf16[2,2,12,64,128]{4,3,2,1,0:T(8,128)(2,1)S(1)}, bf16[2,2,12,64,128]{4,3,2,1,0:T(8,128)(2,1)S(1)}, u32[]{:S(2)}, u32[]{:S(2)}) %collective-permute-start.10) | collective-permute-done | bytes 786464 | tf_op jit(solution)/shard_map/ppermute | solution.py:203
  51.3 1.0 %collective-permute-start.13 = (bf16[2,12,64,128]{3,2,1,0:T(8,128)(2,1)S(1)}, bf16[2,12,64,128]{3,2,1,0:T(8,128)(2,1)S(1)}, u32[]{:S(2)}, u32[]{:S(2)}) collective-permute-start(bf16[2,12,64,128]{3,2,1,0:T(8,128)(2,1)S(1)} %collective-permute-done.6.refs_0_.o3_ref.refs_2_), channel_id=1, source_target_pairs={{0,1},{1,0},{2,3},{3,2},{4,5},{5,4},{6,7},{7,6},{8,24},{9,25},{10,... | collective-permute-start | bytes 1179656 | tf_op jit(solution)/shard_map/ppermute | solution.py:203
  52.3 0.0 collective-permute-done.9.a12_ref.refs_4_.refs_3_
  52.3 0.0 collective-permute-done.8.ab1_ref.refs_2_
  52.3 0.2 shard_map.33
  52.5 0.1 collective-permute-start.14
  52.6 1.6 %shard_map.34.refs_6_ = f32[2,2,256,256]{3,2,1,0:T(8,128)S(1)} custom-call(f32[8,2,128]{2,1,0:T(2,128)S(1)} %maximum_bitcast_fusion.weights_ref, bf16[2,12,64,128]{3,2,1,0:T(8,128)(2,1)S(1)} %collective-permute-done.refs_5_.refs_0_, bf16[2,12,64,128]{3,2,1,0:T(8,128)(2,1)S(1)} %collective-permute-done.2.refs_4_.refs_2_.refs_1_, ...), custom_call_target="tpu_custom_call" | custom-call | flops 1207959552 | bytes 4456448 | tf_op jit(solution)/shard_map/pallas_call | solution.py:264
  54.2 5.0 %collective-permute-done.11.a3_ref = bf16[2,12,64,128]{3,2,1,0:T(8,128)(2,1)S(1)} collective-permute-done((bf16[2,12,64,128]{3,2,1,0:T(8,128)(2,1)S(1)}, bf16[2,12,64,128]{3,2,1,0:T(8,128)(2,1)S(1)}, u32[]{:S(2)}, u32[]{:S(2)}) %collective-permute-start.11) | collective-permute-done | bytes 393248 | tf_op jit(solution)/shard_map/ppermute | solution.py:203
  59.2 0.0 collective-permute-done.12.ab3_ref
  59.2 0.1 shard_map.35.refs_1_
  59.3 0.1 collective-permute-start.15
  59.3 0.0 collective-permute-done.14.refs_5_
  59.4 2.0 %shard_map.36.refs_3_ = f32[2,2,256,256]{3,2,1,0:T(8,128)S(1)} custom-call(f32[8,2,128]{2,1,0:T(2,128)S(1)} %maximum_bitcast_fusion.weights_ref, bf16[2,12,64,128]{3,2,1,0:T(8,128)(2,1)S(1)} %collective-permute-done.refs_5_.refs_0_, bf16[2,12,64,128]{3,2,1,0:T(8,128)(2,1)S(1)} %collective-permute-done.2.refs_4_.refs_2_.refs_1_, ...), custom_call_target="tpu_custom_call" | custom-call | flops 1409286144 | bytes 4849664 | tf_op jit(solution)/shard_map/pallas_call | solution.py:264
  61.3 0.0 collective-permute-done.13.refs_2_
  61.3 0.6 collective-permute-start.16
  61.9 1.1 %shard_map.37 = (f32[2,2,256,256]{3,2,1,0:T(8,128)S(1)}, bf16[2,512,768]{2,1,0:T(8,128)(2,1)S(1)}) custom-call(f32[8,2,128]{2,1,0:T(2,128)S(1)} %maximum_bitcast_fusion.weights_ref, bf16[2,12,64,128]{3,2,1,0:T(8,128)(2,1)S(1)} %collective-permute-done.6.refs_0_.o3_ref.refs_2_, bf16[2,2,12,64,128]{4,3,2,1,0:T(8,128)(2,1)S(1)} %shard_map.35.refs_1_, ...), custom_call_target="tpu_custom_call" | custom-call | flops 603979776 | bytes 3276800 | tf_op jit(solution)/shard_map/pallas_call | solution.py:264
  63.0 0.0 collective-permute-done.15.refs_0_
  63.0 0.2 collective-permute-done.16.refs_1_
  63.2 2.1 %shard_map.38 = f32[16,64,256]{2,1,0:T(8,128)} custom-call(f32[8,2,128]{2,1,0:T(2,128)S(1)} %maximum_bitcast_fusion.weights_ref, bf16[2,2,12,64,128]{4,3,2,1,0:T(8,128)(2,1)S(1)} %collective-permute-done.15.refs_0_, bf16[2,12,64,128]{3,2,1,0:T(8,128)(2,1)S(1)} %collective-permute-done.16.refs_1_, bf16[2,512,768]{2,1,0:T(8,128)(2,1)S(1)} %get-tuple-element.137.refs_2_, ...), custom_call_target="tpu_custom_call" | custom-call | flops 603979776 | bytes 3276800 | tf_op jit(solution)/shard_map/pallas_call | solution.py:264
  (5 shorter events, 0.1 us)
Async XLA Ops:
  0.0 8.6 %copy-start = (s32[4,3]{1,0:T(4,128)S(1)}, s32[4,3]{1,0:T(4,128)}, u32[]{:S(2)}) copy-start(s32[4,3]{1,0:T(4,128)} %param.3) | copy-start | bytes 148
  0.0 9.0 %collective-permute-start.1 = (bf16[2,12,64,128]{3,2,1,0:T(8,128)(2,1)}, bf16[2,12,64,128]{3,2,1,0:T(8,128)(2,1)S(1)}, u32[]{:S(2)}, u32[]{:S(2)}) collective-permute-start(bf16[2,12,64,128]{3,2,1,0:T(8,128)(2,1)} %bitcast.24), channel_id=1, source_target_pairs={{0,16},{1,17},{2,18},{3,19},{4,20},{5,21},{6,22},{7,23},{8,9},{9,8... | collective-permute-start | bytes 1179656 | tf_op jit(solution)/shard_map/ppermute | solution.py:203
  2.9 20.3 %collective-permute-start = (bf16[2,12,64,128]{3,2,1,0:T(8,128)(2,1)}, bf16[2,12,64,128]{3,2,1,0:T(8,128)(2,1)S(1)}, u32[]{:S(2)}, u32[]{:S(2)}) collective-permute-start(bf16[2,12,64,128]{3,2,1,0:T(8,128)(2,1)} %bitcast.25), channel_id=1, source_target_pairs={{0,4},{1,5},{2,6},{3,7},{4,0},{5,1},{6,2},{7,3},{8,12},{9,13},{10,... | collective-permute-start | bytes 1179656 | tf_op jit(solution)/shard_map/ppermute | solution.py:203
  5.5 17.8 %collective-permute-start.2 = (bf16[2,12,64,128]{3,2,1,0:T(8,128)(2,1)}, bf16[2,12,64,128]{3,2,1,0:T(8,128)(2,1)S(1)}, u32[]{:S(2)}, u32[]{:S(2)}) collective-permute-start(bf16[2,12,64,128]{3,2,1,0:T(8,128)(2,1)} %bitcast.26), channel_id=1, source_target_pairs={{0,2},{1,3},{2,0},{3,1},{4,6},{5,7},{6,4},{7,5},{8,10},{9,11},{10,... | collective-permute-start | bytes 1179656 | tf_op jit(solution)/shard_map/ppermute | solution.py:203
  7.1 16.3 %collective-permute-start.3 = (bf16[2,12,64,128]{3,2,1,0:T(8,128)(2,1)}, bf16[2,12,64,128]{3,2,1,0:T(8,128)(2,1)S(1)}, u32[]{:S(2)}, u32[]{:S(2)}) collective-permute-start(bf16[2,12,64,128]{3,2,1,0:T(8,128)(2,1)} %bitcast.27), channel_id=1, source_target_pairs={{0,1},{1,0},{2,3},{3,2},{4,5},{5,4},{6,7},{7,6},{8,24},{9,25},{10,... | collective-permute-start | bytes 1179656 | tf_op jit(solution)/shard_map/ppermute | solution.py:203
  9.0 14.4 %collective-permute-start.4 = (bf16[2,12,64,128]{3,2,1,0:T(8,128)(2,1)S(1)}, bf16[2,12,64,128]{3,2,1,0:T(8,128)(2,1)S(1)}, u32[]{:S(2)}, u32[]{:S(2)}) collective-permute-start(bf16[2,12,64,128]{3,2,1,0:T(8,128)(2,1)S(1)} %collective-permute-done.1.refs_1_), channel_id=1, source_target_pairs={{0,1},{1,0},{2,3},{3,2},{4,5},{5,4},{6,7},{7,6},{8,24},{9,25},{10,... | collective-permute-start | bytes 1179656 | tf_op jit(solution)/shard_map/ppermute | solution.py:203
  23.4 1.0 %copy-start.1 = (bf16[2,12,64,128]{3,2,1,0:T(8,128)(2,1)S(1)}, bf16[2,12,64,128]{3,2,1,0:T(8,128)(2,1)}, u32[]{:S(2)}) copy-start(bf16[2,12,64,128]{3,2,1,0:T(8,128)(2,1)} %shard_map.28.refs_0_.refs_5_) | copy-start | bytes 1179652
  24.4 5.3 %copy-start.2 = (bf16[2,12,64,128]{3,2,1,0:T(8,128)(2,1)S(1)}, bf16[2,12,64,128]{3,2,1,0:T(8,128)(2,1)}, u32[]{:S(2)}) copy-start(bf16[2,12,64,128]{3,2,1,0:T(8,128)(2,1)} %shard_map.28.refs_0_.refs_5_) | copy-start | bytes 1179652
  24.6 6.9 %collective-permute-start.5 = (bf16[6,2,12,64,128]{4,3,2,1,0:T(8,128)(2,1)S(1)}, bf16[6,2,12,64,128]{4,3,2,1,0:T(8,128)(2,1)S(1)}, u32[]{:S(2)}, u32[]{:S(2)}) collective-permute-start(bf16[6,2,12,64,128]{4,3,2,1,0:T(8,128)(2,1)S(1)} %get-tuple-element.87), channel_id=1, source_target_pairs={{0,8},{1,9},{2,10},{3,11},{4,12},{5,13},{6,14},{7,15},{8,0},{9,1},... | collective-permute-start | bytes 7077896 | tf_op jit(solution)/shard_map/ppermute | solution.py:203
  24.7 16.2 %collective-permute-start.6 = (bf16[2,12,64,128]{3,2,1,0:T(8,128)(2,1)S(1)}, bf16[2,12,64,128]{3,2,1,0:T(8,128)(2,1)S(1)}, u32[]{:S(2)}, u32[]{:S(2)}) collective-permute-start(bf16[2,12,64,128]{3,2,1,0:T(8,128)(2,1)S(1)} %collective-permute-done.refs_5_.refs_0_), channel_id=1, source_target_pairs={{0,2},{1,3},{2,0},{3,1},{4,6},{5,7},{6,4},{7,5},{8,10},{9,11},{10,... | collective-permute-start | bytes 1179656 | tf_op jit(solution)/shard_map/ppermute | solution.py:203
  26.2 14.7 %collective-permute-start.7 = (bf16[2,12,64,128]{3,2,1,0:T(8,128)(2,1)S(1)}, bf16[2,12,64,128]{3,2,1,0:T(8,128)(2,1)S(1)}, u32[]{:S(2)}, u32[]{:S(2)}) collective-permute-start(bf16[2,12,64,128]{3,2,1,0:T(8,128)(2,1)S(1)} %get-tuple-element.95), channel_id=1, source_target_pairs={{0,17},{1,16},{2,19},{3,18},{4,21},{5,20},{6,23},{7,22},{8,12},{9,... | collective-permute-start | bytes 1179656 | tf_op jit(solution)/shard_map/ppermute | solution.py:203
  27.6 23.7 %collective-permute-start.10 = (bf16[2,2,12,64,128]{4,3,2,1,0:T(8,128)(2,1)S(1)}, bf16[2,2,12,64,128]{4,3,2,1,0:T(8,128)(2,1)S(1)}, u32[]{:S(2)}, u32[]{:S(2)}) collective-permute-start(bf16[2,2,12,64,128]{4,3,2,1,0:T(8,128)(2,1)S(1)} %get-tuple-element.102), channel_id=1, source_target_pairs={{0,1},{1,0},{2,3},{3,2},{4,5},{5,4},{6,7},{7,6},{8,24},{9,25},{10,... | collective-permute-start | bytes 2359304 | tf_op jit(solution)/shard_map/ppermute | solution.py:203
  29.2 23.2 %collective-permute-start.9 = (bf16[2,2,12,64,128]{4,3,2,1,0:T(8,128)(2,1)S(1)}, bf16[2,2,12,64,128]{4,3,2,1,0:T(8,128)(2,1)S(1)}, u32[]{:S(2)}, u32[]{:S(2)}) collective-permute-start(bf16[2,2,12,64,128]{4,3,2,1,0:T(8,128)(2,1)S(1)} %get-tuple-element.102), channel_id=1, source_target_pairs={{0,16},{1,17},{2,18},{3,19},{4,20},{5,21},{6,22},{7,23},{8,9},{9,8... | collective-permute-start | bytes 2359304 | tf_op jit(solution)/shard_map/ppermute | solution.py:203
  31.5 20.8 %collective-permute-start.8 = (bf16[2,12,64,128]{3,2,1,0:T(8,128)(2,1)S(1)}, bf16[2,12,64,128]{3,2,1,0:T(8,128)(2,1)S(1)}, u32[]{:S(2)}, u32[]{:S(2)}) collective-permute-start(bf16[2,12,64,128]{3,2,1,0:T(8,128)(2,1)S(1)} %collective-permute-done.4.refs_3_.refs_4_), channel_id=1, source_target_pairs={{0,2},{1,3},{2,0},{3,1},{4,6},{5,7},{6,4},{7,5},{8,10},{9,11},{10,... | collective-permute-start | bytes 1179656 | tf_op jit(solution)/shard_map/ppermute | solution.py:203
  40.9 18.3 %collective-permute-start.11 = (bf16[2,12,64,128]{3,2,1,0:T(8,128)(2,1)S(1)}, bf16[2,12,64,128]{3,2,1,0:T(8,128)(2,1)S(1)}, u32[]{:S(2)}, u32[]{:S(2)}) collective-permute-start(bf16[2,12,64,128]{3,2,1,0:T(8,128)(2,1)S(1)} %collective-permute-done.6.refs_0_.o3_ref.refs_2_), channel_id=1, source_target_pairs={{0,16},{1,17},{2,18},{3,19},{4,20},{5,21},{6,22},{7,23},{8,9},{9,8... | collective-permute-start | bytes 1179656 | tf_op jit(solution)/shard_map/ppermute | solution.py:203
  42.4 16.8 %collective-permute-start.12 = (bf16[2,12,64,128]{3,2,1,0:T(8,128)(2,1)S(1)}, bf16[2,12,64,128]{3,2,1,0:T(8,128)(2,1)S(1)}, u32[]{:S(2)}, u32[]{:S(2)}) collective-permute-start(bf16[2,12,64,128]{3,2,1,0:T(8,128)(2,1)S(1)} %collective-permute-done.7.ab2_ref.refs_3_), channel_id=1, source_target_pairs={{0,2},{1,3},{2,0},{3,1},{4,6},{5,7},{6,4},{7,5},{8,10},{9,11},{10,... | collective-permute-start | bytes 1179656 | tf_op jit(solution)/shard_map/ppermute | solution.py:203
  51.3 10.0 %collective-permute-start.13 = (bf16[2,12,64,128]{3,2,1,0:T(8,128)(2,1)S(1)}, bf16[2,12,64,128]{3,2,1,0:T(8,128)(2,1)S(1)}, u32[]{:S(2)}, u32[]{:S(2)}) collective-permute-start(bf16[2,12,64,128]{3,2,1,0:T(8,128)(2,1)S(1)} %collective-permute-done.6.refs_0_.o3_ref.refs_2_), channel_id=1, source_target_pairs={{0,1},{1,0},{2,3},{3,2},{4,5},{5,4},{6,7},{7,6},{8,24},{9,25},{10,... | collective-permute-start | bytes 1179656 | tf_op jit(solution)/shard_map/ppermute | solution.py:203
  52.5 6.8 %collective-permute-start.14 = (bf16[7,2,12,64,128]{4,3,2,1,0:T(8,128)(2,1)S(1)}, bf16[7,2,12,64,128]{4,3,2,1,0:T(8,128)(2,1)S(1)}, u32[]{:S(2)}, u32[]{:S(2)}) collective-permute-start(bf16[7,2,12,64,128]{4,3,2,1,0:T(8,128)(2,1)S(1)} %shard_map.33), channel_id=1, source_target_pairs={{0,8},{1,9},{2,10},{3,11},{4,12},{5,13},{6,14},{7,15},{8,0},{9,1},... | collective-permute-start | bytes 8257544 | tf_op jit(solution)/shard_map/ppermute | solution.py:203
  59.3 3.8 %collective-permute-start.15 = (bf16[2,2,12,64,128]{4,3,2,1,0:T(8,128)(2,1)S(1)}, bf16[2,2,12,64,128]{4,3,2,1,0:T(8,128)(2,1)S(1)}, u32[]{:S(2)}, u32[]{:S(2)}) collective-permute-start(bf16[2,2,12,64,128]{4,3,2,1,0:T(8,128)(2,1)S(1)} %shard_map.35.refs_1_), channel_id=1, source_target_pairs={{0,8},{1,9},{2,10},{3,11},{4,12},{5,13},{6,14},{7,15},{8,0},{9,1},... | collective-permute-start | bytes 2359304 | tf_op jit(solution)/shard_map/ppermute | solution.py:203
  61.3 1.9 %collective-permute-start.16 = (bf16[2,12,64,128]{3,2,1,0:T(8,128)(2,1)S(1)}, bf16[2,12,64,128]{3,2,1,0:T(8,128)(2,1)S(1)}, u32[]{:S(2)}, u32[]{:S(2)}) collective-permute-start(bf16[2,12,64,128]{3,2,1,0:T(8,128)(2,1)S(1)} %collective-permute-done.13.refs_2_), channel_id=1, source_target_pairs={{0,8},{1,9},{2,10},{3,11},{4,12},{5,13},{6,14},{7,15},{8,0},{9,1},... | collective-permute-start | bytes 1179656 | tf_op jit(solution)/shard_map/ppermute | solution.py:203

commit v15 on v14

--- a/solution.py
+++ b/solution.py
@@ -140,16 +140,10 @@
             copy.wait()
 
 
-def fetch(from_ref, to_ref, sem):
-    copy = pltpu.make_async_copy(from_ref, to_ref, sem)
-    copy.start()
-    copy.wait()
-
-
 def route_second(*refs):
-    ab0_ref, o1_ref, o2_ref, stack_ref, both_ref, mixed_ref = refs[3:]
+    ab0_ref, o1_ref, o2_ref, stack_ref, both_ref, mixed_ref = refs[2:]
     core = lax.axis_index("core")
-    for slot in range(6):
+    for slot in range(5):
         stack_ref[slot] = refs[slot][...]
     both_ref[0] = o1_ref[...]
     both_ref[1] = o2_ref[...]
@@ -288,14 +282,8 @@
     put("1c", hop_z(own, 1), "near", [("O", 1)])
     put("1d", hop_b(own), "near", [("B", 0)])
     put("1e", hop_b(near("A", 0)), "near", [("AB", 0)])
-    held = pl.pallas_call(
-        fetch,
-        in_specs=[pl.BlockSpec(memory_space=pl.ANY)],
-        out_specs=pl.BlockSpec(memory_space=pltpu.VMEM),
-        out_shape=jax.ShapeDtypeStruct(own.shape, own.dtype),
-        scratch_shapes=[pltpu.SemaphoreType.DMA],
-    )(own)
-    put("9", held, "near", [("O", 0)])
+    put("1f", swap(own), "far", [("O", 0)])
+    put("9", own, "near", [("O", 0)])
     weights = fence(weights)
 
     def route(kernel, operands, counts, weight=0):
@@ -314,10 +302,10 @@
     first = [("O", 0), ("A", 0), ("B", 0), ("AB", 0), ("O", 1), ("O", 2)]
     second = [("AB", 1), ("AB", 2), ("O", 3), ("A", 1), ("A", 2), ("B", 1), ("B", 2)]
     third = [("A", 3), ("AB", 3), ("B", 3)]
-    stack, both, mixed = route(route_second, [near(*kind) for kind in first], (6, 2, 1))
+    stack, both, mixed = route(route_second, [near(*kind) for kind in first[1:]], (5, 2, 1))
     totals = add([("near", *kind) for kind in first], None)
     o3, ab2, a12, b12 = hop_z(near("O", 2), 1), hop_mixed(mixed), hop_a(both), hop_b(both)
-    put("2a", swap(stack), "far", first)
+    put("2a", swap(stack), "far", first[1:])
     totals = fence(totals)
 
     put("2b", hop_z(near("AB", 0), 1), "near", [("AB", 1)])

time: 65.5 us -> 63.1 us (0.963)
  Pallas kernels: 13 us -> 11.2 us
  starting transfers between devices: 20.9 us -> 22.1 us
  local copies, waits for them, and re-layouts: 1.01 us -> 0.01 us
  waiting for transfers between devices: 30 us -> 29.2 us
    pallas_call x1 -> x0, Pallas kernels: 1.75 us -> none  [swap_in_windows(): pl.pallas_call(fetch, in_specs=[pl.BlockSpec(memory_space=pl.ANY)], out_s...]
    ppermute x17 -> x18, starting transfers between devices: 20.9 us -> 22.1 us  [move(): return lax.ppermute(array, AXES, pairs)]
    unnamed x6 -> x4, local copies, waits for them, and re-layouts: 1 us -> 0.01 us
    ppermute x17 -> x18, waiting for transfers between devices: 30 us -> 29.2 us  [move(): return lax.ppermute(array, AXES, pairs)]
  transfers between devices with their start and end apart: 17 -> 18, of which waited for: 7 -> 10; matrix products, arithmetic and copies ran while one was open for 0% -> 0% of each run, Pallas kernels for 16% -> 14%
where the time goes in v15:
time: 63.1 us; the launch traced here: 63 us
  waiting for transfers between devices  29.2 us (46%)
  starting transfers between devices  22.1 us (35%)
  Pallas kernels  11.2 us (18%)
    ppermute x18, waiting for transfers between devices, move(): return lax.ppermute(array, AXES, pairs)  29.2 us
    ppermute x18, starting transfers between devices, move(): return lax.ppermute(array, AXES, pairs)  22.1 us
    pallas_call x7, Pallas kernels, add(): pl.pallas_call(functools.partial(add_shards, tuple(names), places, slots,...  10.7 us
  transfers between devices with their start and end apart: 18, of which 10 were waited for; matrix products, arithmetic and copies ran while one was open for 0% of the time, Pallas kernels for 14%

profile of v15, /device:TPU:0, one launch (start us, length us, event | category | flops | bytes accessed | tf_op | source)
XLA Modules:
  0.0 63.0 jit_solution(9897791315316566479)
XLA Ops:
  0.0 0.0 copy-start
  0.0 0.0 copy-start.1
  0.0 2.9 %collective-permute-start.1 = (bf16[2,12,64,128]{3,2,1,0:T(8,128)(2,1)}, bf16[2,12,64,128]{3,2,1,0:T(8,128)(2,1)S(1)}, u32[]{:S(2)}, u32[]{:S(2)}) collective-permute-start(bf16[2,12,64,128]{3,2,1,0:T(8,128)(2,1)} %bitcast.24), channel_id=1, source_target_pairs={{0,16},{1,17},{2,18},{3,19},{4,20},{5,21},{6,22},{7,23},{8,9},{9,8... | collective-permute-start | bytes 1179656 | tf_op jit(solution)/shard_map/ppermute | solution.py:197
  2.9 2.6 %collective-permute-start = (bf16[2,12,64,128]{3,2,1,0:T(8,128)(2,1)}, bf16[2,12,64,128]{3,2,1,0:T(8,128)(2,1)S(1)}, u32[]{:S(2)}, u32[]{:S(2)}) collective-permute-start(bf16[2,12,64,128]{3,2,1,0:T(8,128)(2,1)} %bitcast.25), channel_id=1, source_target_pairs={{0,4},{1,5},{2,6},{3,7},{4,0},{5,1},{6,2},{7,3},{8,12},{9,13},{10,... | collective-permute-start | bytes 1179656 | tf_op jit(solution)/shard_map/ppermute | solution.py:197
  5.5 1.6 %collective-permute-start.2 = (bf16[2,12,64,128]{3,2,1,0:T(8,128)(2,1)}, bf16[2,12,64,128]{3,2,1,0:T(8,128)(2,1)S(1)}, u32[]{:S(2)}, u32[]{:S(2)}) collective-permute-start(bf16[2,12,64,128]{3,2,1,0:T(8,128)(2,1)} %bitcast.26), channel_id=1, source_target_pairs={{0,2},{1,3},{2,0},{3,1},{4,6},{5,7},{6,4},{7,5},{8,10},{9,11},{10,... | collective-permute-start | bytes 1179656 | tf_op jit(solution)/shard_map/ppermute | solution.py:197
  7.1 1.5 %collective-permute-start.3 = (bf16[2,12,64,128]{3,2,1,0:T(8,128)(2,1)}, bf16[2,12,64,128]{3,2,1,0:T(8,128)(2,1)S(1)}, u32[]{:S(2)}, u32[]{:S(2)}) collective-permute-start(bf16[2,12,64,128]{3,2,1,0:T(8,128)(2,1)} %bitcast.27), channel_id=1, source_target_pairs={{0,1},{1,0},{2,3},{3,2},{4,5},{5,4},{6,7},{7,6},{8,24},{9,25},{10,... | collective-permute-start | bytes 1179656 | tf_op jit(solution)/shard_map/ppermute | solution.py:197
  8.6 0.0 collective-permute-start.5
  8.6 0.0 copy-done
  8.7 0.1 fusion
  8.8 0.2 collective-permute-done.1.refs_0_.refs_1_
  9.0 3.4 %collective-permute-start.4 = (bf16[2,12,64,128]{3,2,1,0:T(8,128)(2,1)S(1)}, bf16[2,12,64,128]{3,2,1,0:T(8,128)(2,1)S(1)}, u32[]{:S(2)}, u32[]{:S(2)}) collective-permute-start(bf16[2,12,64,128]{3,2,1,0:T(8,128)(2,1)S(1)} %collective-permute-done.1.refs_0_.refs_1_), channel_id=1, source_target_pairs={{0,1},{1,0},{2,3},{3,2},{4,5},{5,4},{6,7},{7,6},{8,24},{9,25},{10,... | collective-permute-start | bytes 1179656 | tf_op jit(solution)/shard_map/ppermute | solution.py:197
  12.4 0.1 multiply_cosine_fusion
  12.6 10.6 %collective-permute-done.refs_4_.refs_0_ = bf16[2,12,64,128]{3,2,1,0:T(8,128)(2,1)S(1)} collective-permute-done((bf16[2,12,64,128]{3,2,1,0:T(8,128)(2,1)}, bf16[2,12,64,128]{3,2,1,0:T(8,128)(2,1)S(1)}, u32[]{:S(2)}, u32[]{:S(2)}) %collective-permute-start) | collective-permute-done | bytes 393248 | tf_op jit(solution)/shard_map/ppermute | solution.py:197
  23.2 0.2 collective-permute-done.2.refs_3_.refs_2_.refs_1_
  23.4 0.0 collective-permute-done.3.refs_1_.refs_3_
  23.4 0.0 collective-permute-done.5.refs_4_
  23.4 0.0 collective-permute-done.4.refs_2_.refs_4_
  23.4 0.2 shard_map.28
  23.6 0.1 collective-permute-start.6
  23.7 1.5 %collective-permute-start.7 = (bf16[2,12,64,128]{3,2,1,0:T(8,128)(2,1)S(1)}, bf16[2,12,64,128]{3,2,1,0:T(8,128)(2,1)S(1)}, u32[]{:S(2)}, u32[]{:S(2)}) collective-permute-start(bf16[2,12,64,128]{3,2,1,0:T(8,128)(2,1)S(1)} %collective-permute-done.refs_4_.refs_0_), channel_id=1, source_target_pairs={{0,2},{1,3},{2,0},{3,1},{4,6},{5,7},{6,4},{7,5},{8,10},{9,11},{10,... | collective-permute-start | bytes 1179656 | tf_op jit(solution)/shard_map/ppermute | solution.py:197
  25.2 1.4 %collective-permute-start.8 = (bf16[2,12,64,128]{3,2,1,0:T(8,128)(2,1)S(1)}, bf16[2,12,64,128]{3,2,1,0:T(8,128)(2,1)S(1)}, u32[]{:S(2)}, u32[]{:S(2)}) collective-permute-start(bf16[2,12,64,128]{3,2,1,0:T(8,128)(2,1)S(1)} %get-tuple-element.101), channel_id=1, source_target_pairs={{0,17},{1,16},{2,19},{3,18},{4,21},{5,20},{6,23},{7,22},{8,12},{9,... | collective-permute-start | bytes 1179656 | tf_op jit(solution)/shard_map/ppermute | solution.py:197
  26.6 0.5 collective-permute-start.10
  27.2 1.5 %collective-permute-start.11 = (bf16[2,2,12,64,128]{4,3,2,1,0:T(8,128)(2,1)S(1)}, bf16[2,2,12,64,128]{4,3,2,1,0:T(8,128)(2,1)S(1)}, u32[]{:S(2)}, u32[]{:S(2)}) collective-permute-start(bf16[2,2,12,64,128]{4,3,2,1,0:T(8,128)(2,1)S(1)} %get-tuple-element.108), channel_id=1, source_target_pairs={{0,1},{1,0},{2,3},{3,2},{4,5},{5,4},{6,7},{7,6},{8,24},{9,25},{10,... | collective-permute-start | bytes 2359304 | tf_op jit(solution)/shard_map/ppermute | solution.py:197
  28.7 0.0 copy-done.1
  28.7 1.8 %shard_map.29.refs_7_ = f32[2,2,256,256]{3,2,1,0:T(8,128)S(1)} custom-call(f32[8,2,128]{2,1,0:T(2,128)S(1)} %maximum_bitcast_fusion.weights_ref, bf16[2,12,64,128]{3,2,1,0:T(8,128)(2,1)S(1)} %collective-permute-done.refs_4_.refs_0_, bf16[2,12,64,128]{3,2,1,0:T(8,128)(2,1)S(1)} %collective-permute-done.1.refs_0_.refs_1_, ...), custom_call_target="tpu_custom_call" | custom-call | flops 1207959552 | bytes 4456448 | tf_op jit(solution)/shard_map/pallas_call | solution.py:258
  30.5 0.0 collective-permute-done.6.refs_5_
  30.5 0.7 %collective-permute-start.9 = (bf16[2,12,64,128]{3,2,1,0:T(8,128)(2,1)S(1)}, bf16[2,12,64,128]{3,2,1,0:T(8,128)(2,1)S(1)}, u32[]{:S(2)}, u32[]{:S(2)}) collective-permute-start(bf16[2,12,64,128]{3,2,1,0:T(8,128)(2,1)S(1)} %collective-permute-done.4.refs_2_.refs_4_), channel_id=1, source_target_pairs={{0,2},{1,3},{2,0},{3,1},{4,6},{5,7},{6,4},{7,5},{8,10},{9,11},{10,... | collective-permute-start | bytes 1179656 | tf_op jit(solution)/shard_map/ppermute | solution.py:197
  31.1 1.7 %shard_map.30.refs_1_ = f32[2,2,256,256]{3,2,1,0:T(8,128)S(1)} custom-call(f32[8,2,128]{2,1,0:T(2,128)S(1)} %maximum_bitcast_fusion.weights_ref, bf16[2,12,64,128]{3,2,1,0:T(8,128)(2,1)S(1)} %collective-permute-done.refs_4_.refs_0_, bf16[2,12,64,128]{3,2,1,0:T(8,128)(2,1)S(1)} %collective-permute-done.1.refs_0_.refs_1_, ...), custom_call_target="tpu_custom_call" | custom-call | flops 1207959552 | bytes 4456448 | tf_op jit(solution)/shard_map/pallas_call | solution.py:258
  32.9 7.0 %collective-permute-done.7.refs_0_.o3_ref.refs_2_ = bf16[2,12,64,128]{3,2,1,0:T(8,128)(2,1)S(1)} collective-permute-done((bf16[2,12,64,128]{3,2,1,0:T(8,128)(2,1)S(1)}, bf16[2,12,64,128]{3,2,1,0:T(8,128)(2,1)S(1)}, u32[]{:S(2)}, u32[]{:S(2)}) %collective-permute-start.7) | collective-permute-done | bytes 393248 | tf_op jit(solution)/shard_map/ppermute | solution.py:197
  39.9 0.0 collective-permute-done.8.ab2_ref.refs_3_
  39.9 1.5 %collective-permute-start.12 = (bf16[2,12,64,128]{3,2,1,0:T(8,128)(2,1)S(1)}, bf16[2,12,64,128]{3,2,1,0:T(8,128)(2,1)S(1)}, u32[]{:S(2)}, u32[]{:S(2)}) collective-permute-start(bf16[2,12,64,128]{3,2,1,0:T(8,128)(2,1)S(1)} %collective-permute-done.7.refs_0_.o3_ref.refs_2_), channel_id=1, source_target_pairs={{0,16},{1,17},{2,18},{3,19},{4,20},{5,21},{6,22},{7,23},{8,9},{9,8... | collective-permute-start | bytes 1179656 | tf_op jit(solution)/shard_map/ppermute | solution.py:197
  41.4 0.0 collective-permute-start.13
  41.4 0.4 shard_map.31.refs_6_
  41.8 8.0 %collective-permute-done.10.a12_ref.refs_4_.refs_3_ = bf16[2,2,12,64,128]{4,3,2,1,0:T(8,128)(2,1)S(1)} collective-permute-done((bf16[2,2,12,64,128]{4,3,2,1,0:T(8,128)(2,1)S(1)}, bf16[2,2,12,64,128]{4,3,2,1,0:T(8,128)(2,1)S(1)}, u32[]{:S(2)}, u32[]{:S(2)}) %collective-permute-start.10) | collective-permute-done | bytes 786464 | tf_op jit(solution)/shard_map/ppermute | solution.py:197
  49.8 1.5 %collective-permute-start.14 = (bf16[2,12,64,128]{3,2,1,0:T(8,128)(2,1)S(1)}, bf16[2,12,64,128]{3,2,1,0:T(8,128)(2,1)S(1)}, u32[]{:S(2)}, u32[]{:S(2)}) collective-permute-start(bf16[2,12,64,128]{3,2,1,0:T(8,128)(2,1)S(1)} %collective-permute-done.7.refs_0_.o3_ref.refs_2_), channel_id=1, source_target_pairs={{0,1},{1,0},{2,3},{3,2},{4,5},{5,4},{6,7},{7,6},{8,24},{9,25},{10,... | collective-permute-start | bytes 1179656 | tf_op jit(solution)/shard_map/ppermute | solution.py:197
  51.3 0.0 collective-permute-done.11.b12_ref.refs_5_.refs_4_
  51.3 0.0 collective-permute-done.9.ab1_ref.refs_2_
  51.3 0.2 shard_map.32
  51.5 0.8 %collective-permute-start.15 = (bf16[7,2,12,64,128]{4,3,2,1,0:T(8,128)(2,1)S(1)}, bf16[7,2,12,64,128]{4,3,2,1,0:T(8,128)(2,1)S(1)}, u32[]{:S(2)}, u32[]{:S(2)}) collective-permute-start(bf16[7,2,12,64,128]{4,3,2,1,0:T(8,128)(2,1)S(1)} %shard_map.32), channel_id=1, source_target_pairs={{0,8},{1,9},{2,10},{3,11},{4,12},{5,13},{6,14},{7,15},{8,0},{9,1},... | collective-permute-start | bytes 8257544 | tf_op jit(solution)/shard_map/ppermute | solution.py:197
  52.2 1.6 %shard_map.33.refs_6_ = f32[2,2,256,256]{3,2,1,0:T(8,128)S(1)} custom-call(f32[8,2,128]{2,1,0:T(2,128)S(1)} %maximum_bitcast_fusion.weights_ref, bf16[2,12,64,128]{3,2,1,0:T(8,128)(2,1)S(1)} %collective-permute-done.refs_4_.refs_0_, bf16[2,12,64,128]{3,2,1,0:T(8,128)(2,1)S(1)} %collective-permute-done.2.refs_3_.refs_2_.refs_1_, ...), custom_call_target="tpu_custom_call" | custom-call | flops 1207959552 | bytes 4456448 | tf_op jit(solution)/shard_map/pallas_call | solution.py:258
  53.9 0.7 %collective-permute-done.12.a3_ref = bf16[2,12,64,128]{3,2,1,0:T(8,128)(2,1)S(1)} collective-permute-done((bf16[2,12,64,128]{3,2,1,0:T(8,128)(2,1)S(1)}, bf16[2,12,64,128]{3,2,1,0:T(8,128)(2,1)S(1)}, u32[]{:S(2)}, u32[]{:S(2)}) %collective-permute-start.12) | collective-permute-done | bytes 393248 | tf_op jit(solution)/shard_map/ppermute | solution.py:197
  54.5 1.8 %collective-permute-done.13.ab3_ref = bf16[2,12,64,128]{3,2,1,0:T(8,128)(2,1)S(1)} collective-permute-done((bf16[2,12,64,128]{3,2,1,0:T(8,128)(2,1)S(1)}, bf16[2,12,64,128]{3,2,1,0:T(8,128)(2,1)S(1)}, u32[]{:S(2)}, u32[]{:S(2)}) %collective-permute-start.13) | collective-permute-done | bytes 393248 | tf_op jit(solution)/shard_map/ppermute | solution.py:197
  56.3 0.1 shard_map.34.refs_1_
  56.3 0.4 collective-permute-start.16
  56.7 0.2 collective-permute-done.15.refs_5_
  57.0 2.0 %shard_map.35.refs_3_ = f32[2,2,256,256]{3,2,1,0:T(8,128)S(1)} custom-call(f32[8,2,128]{2,1,0:T(2,128)S(1)} %maximum_bitcast_fusion.weights_ref, bf16[2,12,64,128]{3,2,1,0:T(8,128)(2,1)S(1)} %collective-permute-done.refs_4_.refs_0_, bf16[2,12,64,128]{3,2,1,0:T(8,128)(2,1)S(1)} %collective-permute-done.2.refs_3_.refs_2_.refs_1_, ...), custom_call_target="tpu_custom_call" | custom-call | flops 1409286144 | bytes 4849664 | tf_op jit(solution)/shard_map/pallas_call | solution.py:258
  58.9 0.2 collective-permute-done.14.refs_2_
  59.1 0.2 collective-permute-start.17
  59.4 1.1 %shard_map.36 = (f32[2,2,256,256]{3,2,1,0:T(8,128)S(1)}, bf16[2,512,768]{2,1,0:T(8,128)(2,1)S(1)}) custom-call(f32[8,2,128]{2,1,0:T(2,128)S(1)} %maximum_bitcast_fusion.weights_ref, bf16[2,12,64,128]{3,2,1,0:T(8,128)(2,1)S(1)} %collective-permute-done.7.refs_0_.o3_ref.refs_2_, bf16[2,2,12,64,128]{4,3,2,1,0:T(8,128)(2,1)S(1)} %shard_map.34.refs_1_, ...), custom_call_target="tpu_custom_call" | custom-call | flops 603979776 | bytes 3276800 | tf_op jit(solution)/shard_map/pallas_call | solution.py:258
  60.5 0.0 collective-permute-done.16.refs_0_
  60.5 0.4 collective-permute-done.17.refs_1_
  60.9 2.1 %shard_map.37 = f32[16,64,256]{2,1,0:T(8,128)} custom-call(f32[8,2,128]{2,1,0:T(2,128)S(1)} %maximum_bitcast_fusion.weights_ref, bf16[2,2,12,64,128]{4,3,2,1,0:T(8,128)(2,1)S(1)} %collective-permute-done.16.refs_0_, bf16[2,12,64,128]{3,2,1,0:T(8,128)(2,1)S(1)} %collective-permute-done.17.refs_1_, bf16[2,512,768]{2,1,0:T(8,128)(2,1)S(1)} %get-tuple-element.143.refs_2_, ...), custom_call_target="tpu_custom_call" | custom-call | flops 603979776 | bytes 3276800 | tf_op jit(solution)/shard_map/pallas_call | solution.py:258
  (5 shorter events, 0.1 us)
Async XLA Ops:
  0.0 8.6 %copy-start = (s32[4,3]{1,0:T(4,128)S(1)}, s32[4,3]{1,0:T(4,128)}, u32[]{:S(2)}) copy-start(s32[4,3]{1,0:T(4,128)} %param.3) | copy-start | bytes 148
  0.0 28.7 %copy-start.1 = (bf16[2,1,64,12,128]{4,2,3,1,0:T(8,128)(2,1)S(1)}, bf16[2,1,64,12,128]{4,2,3,1,0:T(8,128)(2,1)}, u32[]{:S(2)}) copy-start(bf16[2,1,64,12,128]{4,2,3,1,0:T(8,128)(2,1)} %param.2) | copy-start | bytes 1179652
  0.0 9.0 %collective-permute-start.1 = (bf16[2,12,64,128]{3,2,1,0:T(8,128)(2,1)}, bf16[2,12,64,128]{3,2,1,0:T(8,128)(2,1)S(1)}, u32[]{:S(2)}, u32[]{:S(2)}) collective-permute-start(bf16[2,12,64,128]{3,2,1,0:T(8,128)(2,1)} %bitcast.24), channel_id=1, source_target_pairs={{0,16},{1,17},{2,18},{3,19},{4,20},{5,21},{6,22},{7,23},{8,9},{9,8... | collective-permute-start | bytes 1179656 | tf_op jit(solution)/shard_map/ppermute | solution.py:197
  2.9 20.3 %collective-permute-start = (bf16[2,12,64,128]{3,2,1,0:T(8,128)(2,1)}, bf16[2,12,64,128]{3,2,1,0:T(8,128)(2,1)S(1)}, u32[]{:S(2)}, u32[]{:S(2)}) collective-permute-start(bf16[2,12,64,128]{3,2,1,0:T(8,128)(2,1)} %bitcast.25), channel_id=1, source_target_pairs={{0,4},{1,5},{2,6},{3,7},{4,0},{5,1},{6,2},{7,3},{8,12},{9,13},{10,... | collective-permute-start | bytes 1179656 | tf_op jit(solution)/shard_map/ppermute | solution.py:197
  5.5 17.8 %collective-permute-start.2 = (bf16[2,12,64,128]{3,2,1,0:T(8,128)(2,1)}, bf16[2,12,64,128]{3,2,1,0:T(8,128)(2,1)S(1)}, u32[]{:S(2)}, u32[]{:S(2)}) collective-permute-start(bf16[2,12,64,128]{3,2,1,0:T(8,128)(2,1)} %bitcast.26), channel_id=1, source_target_pairs={{0,2},{1,3},{2,0},{3,1},{4,6},{5,7},{6,4},{7,5},{8,10},{9,11},{10,... | collective-permute-start | bytes 1179656 | tf_op jit(solution)/shard_map/ppermute | solution.py:197
  7.1 16.3 %collective-permute-start.3 = (bf16[2,12,64,128]{3,2,1,0:T(8,128)(2,1)}, bf16[2,12,64,128]{3,2,1,0:T(8,128)(2,1)S(1)}, u32[]{:S(2)}, u32[]{:S(2)}) collective-permute-start(bf16[2,12,64,128]{3,2,1,0:T(8,128)(2,1)} %bitcast.27), channel_id=1, source_target_pairs={{0,1},{1,0},{2,3},{3,2},{4,5},{5,4},{6,7},{7,6},{8,24},{9,25},{10,... | collective-permute-start | bytes 1179656 | tf_op jit(solution)/shard_map/ppermute | solution.py:197
  8.6 14.8 %collective-permute-start.5 = (bf16[2,12,64,128]{3,2,1,0:T(8,128)(2,1)}, bf16[2,12,64,128]{3,2,1,0:T(8,128)(2,1)S(1)}, u32[]{:S(2)}, u32[]{:S(2)}) collective-permute-start(bf16[2,12,64,128]{3,2,1,0:T(8,128)(2,1)} %bitcast.28), channel_id=1, source_target_pairs={{0,8},{1,9},{2,10},{3,11},{4,12},{5,13},{6,14},{7,15},{8,0},{9,1},... | collective-permute-start | bytes 1179656 | tf_op jit(solution)/shard_map/ppermute | solution.py:197
  9.0 14.4 %collective-permute-start.4 = (bf16[2,12,64,128]{3,2,1,0:T(8,128)(2,1)S(1)}, bf16[2,12,64,128]{3,2,1,0:T(8,128)(2,1)S(1)}, u32[]{:S(2)}, u32[]{:S(2)}) collective-permute-start(bf16[2,12,64,128]{3,2,1,0:T(8,128)(2,1)S(1)} %collective-permute-done.1.refs_0_.refs_1_), channel_id=1, source_target_pairs={{0,1},{1,0},{2,3},{3,2},{4,5},{5,4},{6,7},{7,6},{8,24},{9,25},{10,... | collective-permute-start | bytes 1179656 | tf_op jit(solution)/shard_map/ppermute | solution.py:197
  23.6 6.9 %collective-permute-start.6 = (bf16[5,2,12,64,128]{4,3,2,1,0:T(8,128)(2,1)S(1)}, bf16[5,2,12,64,128]{4,3,2,1,0:T(8,128)(2,1)S(1)}, u32[]{:S(2)}, u32[]{:S(2)}) collective-permute-start(bf16[5,2,12,64,128]{4,3,2,1,0:T(8,128)(2,1)S(1)} %get-tuple-element.92), channel_id=1, source_target_pairs={{0,8},{1,9},{2,10},{3,11},{4,12},{5,13},{6,14},{7,15},{8,0},{9,1},... | collective-permute-start | bytes 5898248 | tf_op jit(solution)/shard_map/ppermute | solution.py:197
  23.7 16.2 %collective-permute-start.7 = (bf16[2,12,64,128]{3,2,1,0:T(8,128)(2,1)S(1)}, bf16[2,12,64,128]{3,2,1,0:T(8,128)(2,1)S(1)}, u32[]{:S(2)}, u32[]{:S(2)}) collective-permute-start(bf16[2,12,64,128]{3,2,1,0:T(8,128)(2,1)S(1)} %collective-permute-done.refs_4_.refs_0_), channel_id=1, source_target_pairs={{0,2},{1,3},{2,0},{3,1},{4,6},{5,7},{6,4},{7,5},{8,10},{9,11},{10,... | collective-permute-start | bytes 1179656 | tf_op jit(solution)/shard_map/ppermute | solution.py:197
  25.2 14.7 %collective-permute-start.8 = (bf16[2,12,64,128]{3,2,1,0:T(8,128)(2,1)S(1)}, bf16[2,12,64,128]{3,2,1,0:T(8,128)(2,1)S(1)}, u32[]{:S(2)}, u32[]{:S(2)}) collective-permute-start(bf16[2,12,64,128]{3,2,1,0:T(8,128)(2,1)S(1)} %get-tuple-element.101), channel_id=1, source_target_pairs={{0,17},{1,16},{2,19},{3,18},{4,21},{5,20},{6,23},{7,22},{8,12},{9,... | collective-permute-start | bytes 1179656 | tf_op jit(solution)/shard_map/ppermute | solution.py:197
  26.6 23.1 %collective-permute-start.10 = (bf16[2,2,12,64,128]{4,3,2,1,0:T(8,128)(2,1)S(1)}, bf16[2,2,12,64,128]{4,3,2,1,0:T(8,128)(2,1)S(1)}, u32[]{:S(2)}, u32[]{:S(2)}) collective-permute-start(bf16[2,2,12,64,128]{4,3,2,1,0:T(8,128)(2,1)S(1)} %get-tuple-element.108), channel_id=1, source_target_pairs={{0,16},{1,17},{2,18},{3,19},{4,20},{5,21},{6,22},{7,23},{8,9},{9,8... | collective-permute-start | bytes 2359304 | tf_op jit(solution)/shard_map/ppermute | solution.py:197
  27.2 24.1 %collective-permute-start.11 = (bf16[2,2,12,64,128]{4,3,2,1,0:T(8,128)(2,1)S(1)}, bf16[2,2,12,64,128]{4,3,2,1,0:T(8,128)(2,1)S(1)}, u32[]{:S(2)}, u32[]{:S(2)}) collective-permute-start(bf16[2,2,12,64,128]{4,3,2,1,0:T(8,128)(2,1)S(1)} %get-tuple-element.108), channel_id=1, source_target_pairs={{0,1},{1,0},{2,3},{3,2},{4,5},{5,4},{6,7},{7,6},{8,24},{9,25},{10,... | collective-permute-start | bytes 2359304 | tf_op jit(solution)/shard_map/ppermute | solution.py:197
  30.5 20.8 %collective-permute-start.9 = (bf16[2,12,64,128]{3,2,1,0:T(8,128)(2,1)S(1)}, bf16[2,12,64,128]{3,2,1,0:T(8,128)(2,1)S(1)}, u32[]{:S(2)}, u32[]{:S(2)}) collective-permute-start(bf16[2,12,64,128]{3,2,1,0:T(8,128)(2,1)S(1)} %collective-permute-done.4.refs_2_.refs_4_), channel_id=1, source_target_pairs={{0,2},{1,3},{2,0},{3,1},{4,6},{5,7},{6,4},{7,5},{8,10},{9,11},{10,... | collective-permute-start | bytes 1179656 | tf_op jit(solution)/shard_map/ppermute | solution.py:197
  39.9 14.6 %collective-permute-start.12 = (bf16[2,12,64,128]{3,2,1,0:T(8,128)(2,1)S(1)}, bf16[2,12,64,128]{3,2,1,0:T(8,128)(2,1)S(1)}, u32[]{:S(2)}, u32[]{:S(2)}) collective-permute-start(bf16[2,12,64,128]{3,2,1,0:T(8,128)(2,1)S(1)} %collective-permute-done.7.refs_0_.o3_ref.refs_2_), channel_id=1, source_target_pairs={{0,16},{1,17},{2,18},{3,19},{4,20},{5,21},{6,22},{7,23},{8,9},{9,8... | collective-permute-start | bytes 1179656 | tf_op jit(solution)/shard_map/ppermute | solution.py:197
  41.4 14.9 %collective-permute-start.13 = (bf16[2,12,64,128]{3,2,1,0:T(8,128)(2,1)S(1)}, bf16[2,12,64,128]{3,2,1,0:T(8,128)(2,1)S(1)}, u32[]{:S(2)}, u32[]{:S(2)}) collective-permute-start(bf16[2,12,64,128]{3,2,1,0:T(8,128)(2,1)S(1)} %collective-permute-done.8.ab2_ref.refs_3_), channel_id=1, source_target_pairs={{0,2},{1,3},{2,0},{3,1},{4,6},{5,7},{6,4},{7,5},{8,10},{9,11},{10,... | collective-permute-start | bytes 1179656 | tf_op jit(solution)/shard_map/ppermute | solution.py:197
  49.8 9.4 %collective-permute-start.14 = (bf16[2,12,64,128]{3,2,1,0:T(8,128)(2,1)S(1)}, bf16[2,12,64,128]{3,2,1,0:T(8,128)(2,1)S(1)}, u32[]{:S(2)}, u32[]{:S(2)}) collective-permute-start(bf16[2,12,64,128]{3,2,1,0:T(8,128)(2,1)S(1)} %collective-permute-done.7.refs_0_.o3_ref.refs_2_), channel_id=1, source_target_pairs={{0,1},{1,0},{2,3},{3,2},{4,5},{5,4},{6,7},{7,6},{8,24},{9,25},{10,... | collective-permute-start | bytes 1179656 | tf_op jit(solution)/shard_map/ppermute | solution.py:197
  51.5 5.5 %collective-permute-start.15 = (bf16[7,2,12,64,128]{4,3,2,1,0:T(8,128)(2,1)S(1)}, bf16[7,2,12,64,128]{4,3,2,1,0:T(8,128)(2,1)S(1)}, u32[]{:S(2)}, u32[]{:S(2)}) collective-permute-start(bf16[7,2,12,64,128]{4,3,2,1,0:T(8,128)(2,1)S(1)} %shard_map.32), channel_id=1, source_target_pairs={{0,8},{1,9},{2,10},{3,11},{4,12},{5,13},{6,14},{7,15},{8,0},{9,1},... | collective-permute-start | bytes 8257544 | tf_op jit(solution)/shard_map/ppermute | solution.py:197
  56.3 4.2 %collective-permute-start.16 = (bf16[2,2,12,64,128]{4,3,2,1,0:T(8,128)(2,1)S(1)}, bf16[2,2,12,64,128]{4,3,2,1,0:T(8,128)(2,1)S(1)}, u32[]{:S(2)}, u32[]{:S(2)}) collective-permute-start(bf16[2,2,12,64,128]{4,3,2,1,0:T(8,128)(2,1)S(1)} %shard_map.34.refs_1_), channel_id=1, source_target_pairs={{0,8},{1,9},{2,10},{3,11},{4,12},{5,13},{6,14},{7,15},{8,0},{9,1},... | collective-permute-start | bytes 2359304 | tf_op jit(solution)/shard_map/ppermute | solution.py:197
  59.1 1.7 %collective-permute-start.17 = (bf16[2,12,64,128]{3,2,1,0:T(8,128)(2,1)S(1)}, bf16[2,12,64,128]{3,2,1,0:T(8,128)(2,1)S(1)}, u32[]{:S(2)}, u32[]{:S(2)}) collective-permute-start(bf16[2,12,64,128]{3,2,1,0:T(8,128)(2,1)S(1)} %collective-permute-done.14.refs_2_), channel_id=1, source_target_pairs={{0,8},{1,9},{2,10},{3,11},{4,12},{5,13},{6,14},{7,15},{8,0},{9,1},... | collective-permute-start | bytes 1179656 | tf_op jit(solution)/shard_map/ppermute | solution.py:197

commit v16 on v15

--- a/solution.py
+++ b/solution.py
@@ -157,11 +157,11 @@
         mixed_ref[...] = ab0_ref[...]
 
 
-def route_third(ab1_ref, o3_ref, ab2_ref, a12_ref, b12_ref, stack_ref):
-    for slot, ref in enumerate((ab1_ref, ab2_ref, o3_ref)):
-        stack_ref[slot] = ref[...]
-    stack_ref[3:5] = a12_ref[...]
-    stack_ref[5:7] = b12_ref[...]
+def route_third(*refs):
+    stack_ref = refs[-1]
+    for slot in range(5):
+        stack_ref[slot] = refs[slot][...]
+    stack_ref[5:7] = refs[5][...]
 
 
 def route_last(a3_ref, ab3_ref, stack_ref):
@@ -302,15 +302,17 @@
     first = [("O", 0), ("A", 0), ("B", 0), ("AB", 0), ("O", 1), ("O", 2)]
     second = [("AB", 1), ("AB", 2), ("O", 3), ("A", 1), ("A", 2), ("B", 1), ("B", 2)]
     third = [("A", 3), ("AB", 3), ("B", 3)]
+    a1 = hop_a(near("O", 1))
     stack, both, mixed = route(route_second, [near(*kind) for kind in first[1:]], (5, 2, 1))
     totals = add([("near", *kind) for kind in first], None)
-    o3, ab2, a12, b12 = hop_z(near("O", 2), 1), hop_mixed(mixed), hop_a(both), hop_b(both)
+    o3, ab2, a2, b12 = hop_z(near("O", 2), 1), hop_mixed(mixed), hop_a(near("O", 2)), hop_b(both)
     put("2a", swap(stack), "far", first[1:])
     totals = fence(totals)
 
     put("2b", hop_z(near("AB", 0), 1), "near", [("AB", 1)])
     totals = add([("far", *kind) for kind in first], totals)
     ab1 = arrays.pop("2b")
+    put("2bb", a1, "near", [("A", 1)])
     put("2c", o3, "near", [("O", 3)])
     put("2d", ab2, "near", [("AB", 2)])
     totals = fence(totals)
@@ -318,11 +320,11 @@
     ab3, a3, b3 = hop_z(near("AB", 2), 1), hop_a(near("O", 3)), hop_b(near("O", 3))
     totals = add([("near", "O", 3)], totals, weight=45)
     arrays["2b"] = ab1
-    put("2e", a12, "near", [("A", 1), ("A", 2)])
+    put("2e", a2, "near", [("A", 2)])
     put("2f", b12, "near", [("B", 1), ("B", 2)])
     totals = fence(totals)
 
-    keys = ("2b", "2c", "2d", "2e", "2f")
+    keys = ("2b", "2d", "2c", "2bb", "2e", "2f")
     (stack,) = route(route_third, [arrays[key] for key in keys], (7,))
     far2 = swap(stack)
     names = [("near", *kind) for kind in second if kind != ("O", 3)]

time: 63.1 us -> 64.8 us (1.027)
  starting transfers between devices: 22.1 us -> 24.2 us
    ppermute x18 -> x19, starting transfers between devices: 22.1 us -> 24.2 us  [move(): return lax.ppermute(array, AXES, pairs)]
    ppermute x18 -> x19, waiting for transfers between devices: 29.2 us -> 28.8 us  [move(): return lax.ppermute(array, AXES, pairs)]
  transfers between devices with their start and end apart: 18 -> 19, of which waited for: 10 -> 10; matrix products, arithmetic and copies ran while one was open for 0% -> 0% of each run, Pallas kernels for 14% -> 14%
where the time goes in v16:
time: 64.8 us; the launch traced here: 64.7 us
  waiting for transfers between devices  28.8 us (44%)
  starting transfers between devices  24.2 us (37%)
  Pallas kernels  11.2 us (17%)
    ppermute x19, waiting for transfers between devices, move(): return lax.ppermute(array, AXES, pairs)  28.8 us
    ppermute x19, starting transfers between devices, move(): return lax.ppermute(array, AXES, pairs)  24.2 us
    pallas_call x7, Pallas kernels, add(): pl.pallas_call(functools.partial(add_shards, tuple(names), places, slots,...  10.7 us
  transfers between devices with their start and end apart: 19, of which 10 were waited for; matrix products, arithmetic and copies ran while one was open for 0% of the time, Pallas kernels for 14%

profile of v16, /device:TPU:0, one launch (start us, length us, event | category | flops | bytes accessed | tf_op | source)
XLA Modules:
  0.0 64.7 jit_solution(4249620180938917493)
XLA Ops:
  0.0 0.0 copy-start
  0.0 0.0 copy-start.1
  0.0 2.9 %collective-permute-start.1 = (bf16[2,12,64,128]{3,2,1,0:T(8,128)(2,1)}, bf16[2,12,64,128]{3,2,1,0:T(8,128)(2,1)S(1)}, u32[]{:S(2)}, u32[]{:S(2)}) collective-permute-start(bf16[2,12,64,128]{3,2,1,0:T(8,128)(2,1)} %bitcast.24), channel_id=1, source_target_pairs={{0,16},{1,17},{2,18},{3,19},{4,20},{5,21},{6,22},{7,23},{8,9},{9,8... | collective-permute-start | bytes 1179656 | tf_op jit(solution)/shard_map/ppermute | solution.py:197
  2.9 2.6 %collective-permute-start = (bf16[2,12,64,128]{3,2,1,0:T(8,128)(2,1)}, bf16[2,12,64,128]{3,2,1,0:T(8,128)(2,1)S(1)}, u32[]{:S(2)}, u32[]{:S(2)}) collective-permute-start(bf16[2,12,64,128]{3,2,1,0:T(8,128)(2,1)} %bitcast.25), channel_id=1, source_target_pairs={{0,4},{1,5},{2,6},{3,7},{4,0},{5,1},{6,2},{7,3},{8,12},{9,13},{10,... | collective-permute-start | bytes 1179656 | tf_op jit(solution)/shard_map/ppermute | solution.py:197
  5.5 1.6 %collective-permute-start.2 = (bf16[2,12,64,128]{3,2,1,0:T(8,128)(2,1)}, bf16[2,12,64,128]{3,2,1,0:T(8,128)(2,1)S(1)}, u32[]{:S(2)}, u32[]{:S(2)}) collective-permute-start(bf16[2,12,64,128]{3,2,1,0:T(8,128)(2,1)} %bitcast.26), channel_id=1, source_target_pairs={{0,2},{1,3},{2,0},{3,1},{4,6},{5,7},{6,4},{7,5},{8,10},{9,11},{10,... | collective-permute-start | bytes 1179656 | tf_op jit(solution)/shard_map/ppermute | solution.py:197
  7.1 1.5 %collective-permute-start.3 = (bf16[2,12,64,128]{3,2,1,0:T(8,128)(2,1)}, bf16[2,12,64,128]{3,2,1,0:T(8,128)(2,1)S(1)}, u32[]{:S(2)}, u32[]{:S(2)}) collective-permute-start(bf16[2,12,64,128]{3,2,1,0:T(8,128)(2,1)} %bitcast.27), channel_id=1, source_target_pairs={{0,1},{1,0},{2,3},{3,2},{4,5},{5,4},{6,7},{7,6},{8,24},{9,25},{10,... | collective-permute-start | bytes 1179656 | tf_op jit(solution)/shard_map/ppermute | solution.py:197
  8.6 0.0 collective-permute-start.5
  8.6 0.0 copy-done
  8.7 0.1 fusion
  8.8 0.2 collective-permute-done.1.refs_0_.refs_1_
  9.0 3.4 %collective-permute-start.4 = (bf16[2,12,64,128]{3,2,1,0:T(8,128)(2,1)S(1)}, bf16[2,12,64,128]{3,2,1,0:T(8,128)(2,1)S(1)}, u32[]{:S(2)}, u32[]{:S(2)}) collective-permute-start(bf16[2,12,64,128]{3,2,1,0:T(8,128)(2,1)S(1)} %collective-permute-done.1.refs_0_.refs_1_), channel_id=1, source_target_pairs={{0,1},{1,0},{2,3},{3,2},{4,5},{5,4},{6,7},{7,6},{8,24},{9,25},{10,... | collective-permute-start | bytes 1179656 | tf_op jit(solution)/shard_map/ppermute | solution.py:197
  12.4 0.1 multiply_cosine_fusion
  12.6 10.6 %collective-permute-done.refs_4_.refs_0_ = bf16[2,12,64,128]{3,2,1,0:T(8,128)(2,1)S(1)} collective-permute-done((bf16[2,12,64,128]{3,2,1,0:T(8,128)(2,1)}, bf16[2,12,64,128]{3,2,1,0:T(8,128)(2,1)S(1)}, u32[]{:S(2)}, u32[]{:S(2)}) %collective-permute-start) | collective-permute-done | bytes 393248 | tf_op jit(solution)/shard_map/ppermute | solution.py:197
  23.2 0.2 collective-permute-done.2.refs_3_.refs_2_.refs_1_
  23.4 0.0 collective-permute-done.3.refs_1_.refs_3_
  23.4 0.0 collective-permute-done.5.refs_4_
  23.4 0.0 collective-permute-done.4.refs_2_.refs_4_
  23.4 0.2 shard_map.28
  23.6 0.1 collective-permute-start.6
  23.7 1.5 %collective-permute-start.8 = (bf16[2,12,64,128]{3,2,1,0:T(8,128)(2,1)S(1)}, bf16[2,12,64,128]{3,2,1,0:T(8,128)(2,1)S(1)}, u32[]{:S(2)}, u32[]{:S(2)}) collective-permute-start(bf16[2,12,64,128]{3,2,1,0:T(8,128)(2,1)S(1)} %collective-permute-done.refs_4_.refs_0_), channel_id=1, source_target_pairs={{0,2},{1,3},{2,0},{3,1},{4,6},{5,7},{6,4},{7,5},{8,10},{9,11},{10,... | collective-permute-start | bytes 1179656 | tf_op jit(solution)/shard_map/ppermute | solution.py:197
  25.2 1.4 %collective-permute-start.9 = (bf16[2,12,64,128]{3,2,1,0:T(8,128)(2,1)S(1)}, bf16[2,12,64,128]{3,2,1,0:T(8,128)(2,1)S(1)}, u32[]{:S(2)}, u32[]{:S(2)}) collective-permute-start(bf16[2,12,64,128]{3,2,1,0:T(8,128)(2,1)S(1)} %get-tuple-element.105), channel_id=1, source_target_pairs={{0,17},{1,16},{2,19},{3,18},{4,21},{5,20},{6,23},{7,22},{8,12},{9,... | collective-permute-start | bytes 1179656 | tf_op jit(solution)/shard_map/ppermute | solution.py:197
  26.6 0.5 collective-permute-start.7
  27.2 1.5 %collective-permute-start.11 = (bf16[2,12,64,128]{3,2,1,0:T(8,128)(2,1)S(1)}, bf16[2,12,64,128]{3,2,1,0:T(8,128)(2,1)S(1)}, u32[]{:S(2)}, u32[]{:S(2)}) collective-permute-start(bf16[2,12,64,128]{3,2,1,0:T(8,128)(2,1)S(1)} %collective-permute-done.refs_4_.refs_0_), channel_id=1, source_target_pairs={{0,16},{1,17},{2,18},{3,19},{4,20},{5,21},{6,22},{7,23},{8,9},{9,8... | collective-permute-start | bytes 1179656 | tf_op jit(solution)/shard_map/ppermute | solution.py:197
  28.7 0.0 copy-done.1
  28.7 1.8 %shard_map.29.refs_7_ = f32[2,2,256,256]{3,2,1,0:T(8,128)S(1)} custom-call(f32[8,2,128]{2,1,0:T(2,128)S(1)} %maximum_bitcast_fusion.weights_ref, bf16[2,12,64,128]{3,2,1,0:T(8,128)(2,1)S(1)} %collective-permute-done.refs_4_.refs_0_, bf16[2,12,64,128]{3,2,1,0:T(8,128)(2,1)S(1)} %collective-permute-done.1.refs_0_.refs_1_, ...), custom_call_target="tpu_custom_call" | custom-call | flops 1207959552 | bytes 4456448 | tf_op jit(solution)/shard_map/pallas_call | solution.py:258
  30.4 0.0 collective-permute-done.6.refs_5_
  30.5 1.6 %collective-permute-start.12 = (bf16[2,2,12,64,128]{4,3,2,1,0:T(8,128)(2,1)S(1)}, bf16[2,2,12,64,128]{4,3,2,1,0:T(8,128)(2,1)S(1)}, u32[]{:S(2)}, u32[]{:S(2)}) collective-permute-start(bf16[2,2,12,64,128]{4,3,2,1,0:T(8,128)(2,1)S(1)} %get-tuple-element.113), channel_id=1, source_target_pairs={{0,1},{1,0},{2,3},{3,2},{4,5},{5,4},{6,7},{7,6},{8,24},{9,25},{10,... | collective-permute-start | bytes 2359304 | tf_op jit(solution)/shard_map/ppermute | solution.py:197
  32.0 1.7 %shard_map.30.refs_1_ = f32[2,2,256,256]{3,2,1,0:T(8,128)S(1)} custom-call(f32[8,2,128]{2,1,0:T(2,128)S(1)} %maximum_bitcast_fusion.weights_ref, bf16[2,12,64,128]{3,2,1,0:T(8,128)(2,1)S(1)} %collective-permute-done.refs_4_.refs_0_, bf16[2,12,64,128]{3,2,1,0:T(8,128)(2,1)S(1)} %collective-permute-done.1.refs_0_.refs_1_, ...), custom_call_target="tpu_custom_call" | custom-call | flops 1207959552 | bytes 4456448 | tf_op jit(solution)/shard_map/pallas_call | solution.py:258
  33.8 5.7 %collective-permute-done.8.refs_0_.refs_2_.refs_3_ = bf16[2,12,64,128]{3,2,1,0:T(8,128)(2,1)S(1)} collective-permute-done((bf16[2,12,64,128]{3,2,1,0:T(8,128)(2,1)S(1)}, bf16[2,12,64,128]{3,2,1,0:T(8,128)(2,1)S(1)}, u32[]{:S(2)}, u32[]{:S(2)}) %collective-permute-start.8) | collective-permute-done | bytes 393248 | tf_op jit(solution)/shard_map/ppermute | solution.py:197
  39.4 0.0 collective-permute-start.10
  39.4 0.0 collective-permute-done.9.refs_1_.refs_4_
  39.4 1.5 %collective-permute-done.7.refs_3_.refs_2_ = bf16[2,12,64,128]{3,2,1,0:T(8,128)(2,1)S(1)} collective-permute-done((bf16[2,12,64,128]{3,2,1,0:T(8,128)(2,1)S(1)}, bf16[2,12,64,128]{3,2,1,0:T(8,128)(2,1)S(1)}, u32[]{:S(2)}, u32[]{:S(2)}) %collective-permute-start.7) | collective-permute-done | bytes 393248 | tf_op jit(solution)/shard_map/ppermute | solution.py:197
  40.9 1.5 %collective-permute-start.13 = (bf16[2,12,64,128]{3,2,1,0:T(8,128)(2,1)S(1)}, bf16[2,12,64,128]{3,2,1,0:T(8,128)(2,1)S(1)}, u32[]{:S(2)}, u32[]{:S(2)}) collective-permute-start(bf16[2,12,64,128]{3,2,1,0:T(8,128)(2,1)S(1)} %collective-permute-done.8.refs_0_.refs_2_.refs_3_), channel_id=1, source_target_pairs={{0,16},{1,17},{2,18},{3,19},{4,20},{5,21},{6,22},{7,23},{8,9},{9,8... | collective-permute-start | bytes 1179656 | tf_op jit(solution)/shard_map/ppermute | solution.py:197
  42.4 0.9 %collective-permute-start.14 = (bf16[2,12,64,128]{3,2,1,0:T(8,128)(2,1)S(1)}, bf16[2,12,64,128]{3,2,1,0:T(8,128)(2,1)S(1)}, u32[]{:S(2)}, u32[]{:S(2)}) collective-permute-start(bf16[2,12,64,128]{3,2,1,0:T(8,128)(2,1)S(1)} %collective-permute-done.9.refs_1_.refs_4_), channel_id=1, source_target_pairs={{0,2},{1,3},{2,0},{3,1},{4,6},{5,7},{6,4},{7,5},{8,10},{9,11},{10,... | collective-permute-start | bytes 1179656 | tf_op jit(solution)/shard_map/ppermute | solution.py:197
  43.3 0.4 shard_map.31.refs_7_
  43.8 5.6 %collective-permute-done.11.refs_4_.refs_5_ = bf16[2,12,64,128]{3,2,1,0:T(8,128)(2,1)S(1)} collective-permute-done((bf16[2,12,64,128]{3,2,1,0:T(8,128)(2,1)S(1)}, bf16[2,12,64,128]{3,2,1,0:T(8,128)(2,1)S(1)}, u32[]{:S(2)}, u32[]{:S(2)}) %collective-permute-start.11) | collective-permute-done | bytes 393248 | tf_op jit(solution)/shard_map/ppermute | solution.py:197
  49.4 2.0 %collective-permute-start.15 = (bf16[2,12,64,128]{3,2,1,0:T(8,128)(2,1)S(1)}, bf16[2,12,64,128]{3,2,1,0:T(8,128)(2,1)S(1)}, u32[]{:S(2)}, u32[]{:S(2)}) collective-permute-start(bf16[2,12,64,128]{3,2,1,0:T(8,128)(2,1)S(1)} %collective-permute-done.8.refs_0_.refs_2_.refs_3_), channel_id=1, source_target_pairs={{0,1},{1,0},{2,3},{3,2},{4,5},{5,4},{6,7},{7,6},{8,24},{9,25},{10,... | collective-permute-start | bytes 1179656 | tf_op jit(solution)/shard_map/ppermute | solution.py:197
  51.3 0.0 collective-permute-done.12.refs_5_.refs_6_
  51.3 0.1 collective-permute-done.10.refs_0_.refs_2_
  51.5 0.2 shard_map.32
  51.6 0.6 collective-permute-start.16
  52.2 1.6 %shard_map.33.refs_7_ = f32[2,2,256,256]{3,2,1,0:T(8,128)S(1)} custom-call(f32[8,2,128]{2,1,0:T(2,128)S(1)} %maximum_bitcast_fusion.weights_ref, bf16[2,12,64,128]{3,2,1,0:T(8,128)(2,1)S(1)} %collective-permute-done.refs_4_.refs_0_, bf16[2,12,64,128]{3,2,1,0:T(8,128)(2,1)S(1)} %collective-permute-done.2.refs_3_.refs_2_.refs_1_, ...), custom_call_target="tpu_custom_call" | custom-call | flops 1207959552 | bytes 4456448 | tf_op jit(solution)/shard_map/pallas_call | solution.py:258
  53.8 1.0 %collective-permute-done.13.a3_ref = bf16[2,12,64,128]{3,2,1,0:T(8,128)(2,1)S(1)} collective-permute-done((bf16[2,12,64,128]{3,2,1,0:T(8,128)(2,1)S(1)}, bf16[2,12,64,128]{3,2,1,0:T(8,128)(2,1)S(1)}, u32[]{:S(2)}, u32[]{:S(2)}) %collective-permute-start.13) | collective-permute-done | bytes 393248 | tf_op jit(solution)/shard_map/ppermute | solution.py:197
  54.9 3.6 %collective-permute-done.14.ab3_ref = bf16[2,12,64,128]{3,2,1,0:T(8,128)(2,1)S(1)} collective-permute-done((bf16[2,12,64,128]{3,2,1,0:T(8,128)(2,1)S(1)}, bf16[2,12,64,128]{3,2,1,0:T(8,128)(2,1)S(1)}, u32[]{:S(2)}, u32[]{:S(2)}) %collective-permute-start.14) | collective-permute-done | bytes 393248 | tf_op jit(solution)/shard_map/ppermute | solution.py:197
  58.5 0.1 shard_map.34.refs_1_
  58.6 0.1 collective-permute-start.17
  58.7 0.0 collective-permute-done.16.refs_6_
  58.7 2.0 %shard_map.35.refs_3_ = f32[2,2,256,256]{3,2,1,0:T(8,128)S(1)} custom-call(f32[8,2,128]{2,1,0:T(2,128)S(1)} %maximum_bitcast_fusion.weights_ref, bf16[2,12,64,128]{3,2,1,0:T(8,128)(2,1)S(1)} %collective-permute-done.refs_4_.refs_0_, bf16[2,12,64,128]{3,2,1,0:T(8,128)(2,1)S(1)} %collective-permute-done.2.refs_3_.refs_2_.refs_1_, ...), custom_call_target="tpu_custom_call" | custom-call | flops 1409286144 | bytes 4849664 | tf_op jit(solution)/shard_map/pallas_call | solution.py:258
  60.7 0.0 collective-permute-done.15.refs_2_
  60.7 0.6 collective-permute-start.18
  61.2 1.1 %shard_map.36 = (f32[2,2,256,256]{3,2,1,0:T(8,128)S(1)}, bf16[2,512,768]{2,1,0:T(8,128)(2,1)S(1)}) custom-call(f32[8,2,128]{2,1,0:T(2,128)S(1)} %maximum_bitcast_fusion.weights_ref, bf16[2,12,64,128]{3,2,1,0:T(8,128)(2,1)S(1)} %collective-permute-done.8.refs_0_.refs_2_.refs_3_, bf16[2,2,12,64,128]{4,3,2,1,0:T(8,128)(2,1)S(1)} %shard_map.34.refs_1_, ...), custom_call_target="tpu_custom_call" | custom-call | flops 603979776 | bytes 3276800 | tf_op jit(solution)/shard_map/pallas_call | solution.py:258
  62.4 0.0 collective-permute-done.17.refs_0_
  62.4 0.2 collective-permute-done.18.refs_1_
  62.6 2.1 %shard_map.37 = f32[16,64,256]{2,1,0:T(8,128)} custom-call(f32[8,2,128]{2,1,0:T(2,128)S(1)} %maximum_bitcast_fusion.weights_ref, bf16[2,2,12,64,128]{4,3,2,1,0:T(8,128)(2,1)S(1)} %collective-permute-done.17.refs_0_, bf16[2,12,64,128]{3,2,1,0:T(8,128)(2,1)S(1)} %collective-permute-done.18.refs_1_, bf16[2,512,768]{2,1,0:T(8,128)(2,1)S(1)} %get-tuple-element.151.refs_2_, ...), custom_call_target="tpu_custom_call" | custom-call | flops 603979776 | bytes 3276800 | tf_op jit(solution)/shard_map/pallas_call | solution.py:258
  (5 shorter events, 0.1 us)
Async XLA Ops:
  0.0 8.6 %copy-start = (s32[4,3]{1,0:T(4,128)S(1)}, s32[4,3]{1,0:T(4,128)}, u32[]{:S(2)}) copy-start(s32[4,3]{1,0:T(4,128)} %param.3) | copy-start | bytes 148
  0.0 28.7 %copy-start.1 = (bf16[2,1,64,12,128]{4,2,3,1,0:T(8,128)(2,1)S(1)}, bf16[2,1,64,12,128]{4,2,3,1,0:T(8,128)(2,1)}, u32[]{:S(2)}) copy-start(bf16[2,1,64,12,128]{4,2,3,1,0:T(8,128)(2,1)} %param.2) | copy-start | bytes 1179652
  0.0 9.0 %collective-permute-start.1 = (bf16[2,12,64,128]{3,2,1,0:T(8,128)(2,1)}, bf16[2,12,64,128]{3,2,1,0:T(8,128)(2,1)S(1)}, u32[]{:S(2)}, u32[]{:S(2)}) collective-permute-start(bf16[2,12,64,128]{3,2,1,0:T(8,128)(2,1)} %bitcast.24), channel_id=1, source_target_pairs={{0,16},{1,17},{2,18},{3,19},{4,20},{5,21},{6,22},{7,23},{8,9},{9,8... | collective-permute-start | bytes 1179656 | tf_op jit(solution)/shard_map/ppermute | solution.py:197
  2.9 20.3 %collective-permute-start = (bf16[2,12,64,128]{3,2,1,0:T(8,128)(2,1)}, bf16[2,12,64,128]{3,2,1,0:T(8,128)(2,1)S(1)}, u32[]{:S(2)}, u32[]{:S(2)}) collective-permute-start(bf16[2,12,64,128]{3,2,1,0:T(8,128)(2,1)} %bitcast.25), channel_id=1, source_target_pairs={{0,4},{1,5},{2,6},{3,7},{4,0},{5,1},{6,2},{7,3},{8,12},{9,13},{10,... | collective-permute-start | bytes 1179656 | tf_op jit(solution)/shard_map/ppermute | solution.py:197
  5.5 17.8 %collective-permute-start.2 = (bf16[2,12,64,128]{3,2,1,0:T(8,128)(2,1)}, bf16[2,12,64,128]{3,2,1,0:T(8,128)(2,1)S(1)}, u32[]{:S(2)}, u32[]{:S(2)}) collective-permute-start(bf16[2,12,64,128]{3,2,1,0:T(8,128)(2,1)} %bitcast.26), channel_id=1, source_target_pairs={{0,2},{1,3},{2,0},{3,1},{4,6},{5,7},{6,4},{7,5},{8,10},{9,11},{10,... | collective-permute-start | bytes 1179656 | tf_op jit(solution)/shard_map/ppermute | solution.py:197
  7.1 16.3 %collective-permute-start.3 = (bf16[2,12,64,128]{3,2,1,0:T(8,128)(2,1)}, bf16[2,12,64,128]{3,2,1,0:T(8,128)(2,1)S(1)}, u32[]{:S(2)}, u32[]{:S(2)}) collective-permute-start(bf16[2,12,64,128]{3,2,1,0:T(8,128)(2,1)} %bitcast.27), channel_id=1, source_target_pairs={{0,1},{1,0},{2,3},{3,2},{4,5},{5,4},{6,7},{7,6},{8,24},{9,25},{10,... | collective-permute-start | bytes 1179656 | tf_op jit(solution)/shard_map/ppermute | solution.py:197
  8.6 14.8 %collective-permute-start.5 = (bf16[2,12,64,128]{3,2,1,0:T(8,128)(2,1)}, bf16[2,12,64,128]{3,2,1,0:T(8,128)(2,1)S(1)}, u32[]{:S(2)}, u32[]{:S(2)}) collective-permute-start(bf16[2,12,64,128]{3,2,1,0:T(8,128)(2,1)} %bitcast.28), channel_id=1, source_target_pairs={{0,8},{1,9},{2,10},{3,11},{4,12},{5,13},{6,14},{7,15},{8,0},{9,1},... | collective-permute-start | bytes 1179656 | tf_op jit(solution)/shard_map/ppermute | solution.py:197
  9.0 14.4 %collective-permute-start.4 = (bf16[2,12,64,128]{3,2,1,0:T(8,128)(2,1)S(1)}, bf16[2,12,64,128]{3,2,1,0:T(8,128)(2,1)S(1)}, u32[]{:S(2)}, u32[]{:S(2)}) collective-permute-start(bf16[2,12,64,128]{3,2,1,0:T(8,128)(2,1)S(1)} %collective-permute-done.1.refs_0_.refs_1_), channel_id=1, source_target_pairs={{0,1},{1,0},{2,3},{3,2},{4,5},{5,4},{6,7},{7,6},{8,24},{9,25},{10,... | collective-permute-start | bytes 1179656 | tf_op jit(solution)/shard_map/ppermute | solution.py:197
  23.6 6.8 %collective-permute-start.6 = (bf16[5,2,12,64,128]{4,3,2,1,0:T(8,128)(2,1)S(1)}, bf16[5,2,12,64,128]{4,3,2,1,0:T(8,128)(2,1)S(1)}, u32[]{:S(2)}, u32[]{:S(2)}) collective-permute-start(bf16[5,2,12,64,128]{4,3,2,1,0:T(8,128)(2,1)S(1)} %get-tuple-element.96), channel_id=1, source_target_pairs={{0,8},{1,9},{2,10},{3,11},{4,12},{5,13},{6,14},{7,15},{8,0},{9,1},... | collective-permute-start | bytes 5898248 | tf_op jit(solution)/shard_map/ppermute | solution.py:197
  23.7 15.7 %collective-permute-start.8 = (bf16[2,12,64,128]{3,2,1,0:T(8,128)(2,1)S(1)}, bf16[2,12,64,128]{3,2,1,0:T(8,128)(2,1)S(1)}, u32[]{:S(2)}, u32[]{:S(2)}) collective-permute-start(bf16[2,12,64,128]{3,2,1,0:T(8,128)(2,1)S(1)} %collective-permute-done.refs_4_.refs_0_), channel_id=1, source_target_pairs={{0,2},{1,3},{2,0},{3,1},{4,6},{5,7},{6,4},{7,5},{8,10},{9,11},{10,... | collective-permute-start | bytes 1179656 | tf_op jit(solution)/shard_map/ppermute | solution.py:197
  25.2 14.2 %collective-permute-start.9 = (bf16[2,12,64,128]{3,2,1,0:T(8,128)(2,1)S(1)}, bf16[2,12,64,128]{3,2,1,0:T(8,128)(2,1)S(1)}, u32[]{:S(2)}, u32[]{:S(2)}) collective-permute-start(bf16[2,12,64,128]{3,2,1,0:T(8,128)(2,1)S(1)} %get-tuple-element.105), channel_id=1, source_target_pairs={{0,17},{1,16},{2,19},{3,18},{4,21},{5,20},{6,23},{7,22},{8,12},{9,... | collective-permute-start | bytes 1179656 | tf_op jit(solution)/shard_map/ppermute | solution.py:197
  26.6 14.3 %collective-permute-start.7 = (bf16[2,12,64,128]{3,2,1,0:T(8,128)(2,1)S(1)}, bf16[2,12,64,128]{3,2,1,0:T(8,128)(2,1)S(1)}, u32[]{:S(2)}, u32[]{:S(2)}) collective-permute-start(bf16[2,12,64,128]{3,2,1,0:T(8,128)(2,1)S(1)} %collective-permute-done.2.refs_3_.refs_2_.refs_1_), channel_id=1, source_target_pairs={{0,16},{1,17},{2,18},{3,19},{4,20},{5,21},{6,22},{7,23},{8,9},{9,8... | collective-permute-start | bytes 1179656 | tf_op jit(solution)/shard_map/ppermute | solution.py:197
  27.2 22.2 %collective-permute-start.11 = (bf16[2,12,64,128]{3,2,1,0:T(8,128)(2,1)S(1)}, bf16[2,12,64,128]{3,2,1,0:T(8,128)(2,1)S(1)}, u32[]{:S(2)}, u32[]{:S(2)}) collective-permute-start(bf16[2,12,64,128]{3,2,1,0:T(8,128)(2,1)S(1)} %collective-permute-done.refs_4_.refs_0_), channel_id=1, source_target_pairs={{0,16},{1,17},{2,18},{3,19},{4,20},{5,21},{6,22},{7,23},{8,9},{9,8... | collective-permute-start | bytes 1179656 | tf_op jit(solution)/shard_map/ppermute | solution.py:197
  30.5 20.9 %collective-permute-start.12 = (bf16[2,2,12,64,128]{4,3,2,1,0:T(8,128)(2,1)S(1)}, bf16[2,2,12,64,128]{4,3,2,1,0:T(8,128)(2,1)S(1)}, u32[]{:S(2)}, u32[]{:S(2)}) collective-permute-start(bf16[2,2,12,64,128]{4,3,2,1,0:T(8,128)(2,1)S(1)} %get-tuple-element.113), channel_id=1, source_target_pairs={{0,1},{1,0},{2,3},{3,2},{4,5},{5,4},{6,7},{7,6},{8,24},{9,25},{10,... | collective-permute-start | bytes 2359304 | tf_op jit(solution)/shard_map/ppermute | solution.py:197
  39.4 12.0 %collective-permute-start.10 = (bf16[2,12,64,128]{3,2,1,0:T(8,128)(2,1)S(1)}, bf16[2,12,64,128]{3,2,1,0:T(8,128)(2,1)S(1)}, u32[]{:S(2)}, u32[]{:S(2)}) collective-permute-start(bf16[2,12,64,128]{3,2,1,0:T(8,128)(2,1)S(1)} %collective-permute-done.4.refs_2_.refs_4_), channel_id=1, source_target_pairs={{0,2},{1,3},{2,0},{3,1},{4,6},{5,7},{6,4},{7,5},{8,10},{9,11},{10,... | collective-permute-start | bytes 1179656 | tf_op jit(solution)/shard_map/ppermute | solution.py:197
  40.9 14.0 %collective-permute-start.13 = (bf16[2,12,64,128]{3,2,1,0:T(8,128)(2,1)S(1)}, bf16[2,12,64,128]{3,2,1,0:T(8,128)(2,1)S(1)}, u32[]{:S(2)}, u32[]{:S(2)}) collective-permute-start(bf16[2,12,64,128]{3,2,1,0:T(8,128)(2,1)S(1)} %collective-permute-done.8.refs_0_.refs_2_.refs_3_), channel_id=1, source_target_pairs={{0,16},{1,17},{2,18},{3,19},{4,20},{5,21},{6,22},{7,23},{8,9},{9,8... | collective-permute-start | bytes 1179656 | tf_op jit(solution)/shard_map/ppermute | solution.py:197
  42.4 16.1 %collective-permute-start.14 = (bf16[2,12,64,128]{3,2,1,0:T(8,128)(2,1)S(1)}, bf16[2,12,64,128]{3,2,1,0:T(8,128)(2,1)S(1)}, u32[]{:S(2)}, u32[]{:S(2)}) collective-permute-start(bf16[2,12,64,128]{3,2,1,0:T(8,128)(2,1)S(1)} %collective-permute-done.9.refs_1_.refs_4_), channel_id=1, source_target_pairs={{0,2},{1,3},{2,0},{3,1},{4,6},{5,7},{6,4},{7,5},{8,10},{9,11},{10,... | collective-permute-start | bytes 1179656 | tf_op jit(solution)/shard_map/ppermute | solution.py:197
  49.4 11.3 %collective-permute-start.15 = (bf16[2,12,64,128]{3,2,1,0:T(8,128)(2,1)S(1)}, bf16[2,12,64,128]{3,2,1,0:T(8,128)(2,1)S(1)}, u32[]{:S(2)}, u32[]{:S(2)}) collective-permute-start(bf16[2,12,64,128]{3,2,1,0:T(8,128)(2,1)S(1)} %collective-permute-done.8.refs_0_.refs_2_.refs_3_), channel_id=1, source_target_pairs={{0,1},{1,0},{2,3},{3,2},{4,5},{5,4},{6,7},{7,6},{8,24},{9,25},{10,... | collective-permute-start | bytes 1179656 | tf_op jit(solution)/shard_map/ppermute | solution.py:197
  51.6 7.0 %collective-permute-start.16 = (bf16[7,2,12,64,128]{4,3,2,1,0:T(8,128)(2,1)S(1)}, bf16[7,2,12,64,128]{4,3,2,1,0:T(8,128)(2,1)S(1)}, u32[]{:S(2)}, u32[]{:S(2)}) collective-permute-start(bf16[7,2,12,64,128]{4,3,2,1,0:T(8,128)(2,1)S(1)} %shard_map.32), channel_id=1, source_target_pairs={{0,8},{1,9},{2,10},{3,11},{4,12},{5,13},{6,14},{7,15},{8,0},{9,1},... | collective-permute-start | bytes 8257544 | tf_op jit(solution)/shard_map/ppermute | solution.py:197
  58.6 3.8 %collective-permute-start.17 = (bf16[2,2,12,64,128]{4,3,2,1,0:T(8,128)(2,1)S(1)}, bf16[2,2,12,64,128]{4,3,2,1,0:T(8,128)(2,1)S(1)}, u32[]{:S(2)}, u32[]{:S(2)}) collective-permute-start(bf16[2,2,12,64,128]{4,3,2,1,0:T(8,128)(2,1)S(1)} %shard_map.34.refs_1_), channel_id=1, source_target_pairs={{0,8},{1,9},{2,10},{3,11},{4,12},{5,13},{6,14},{7,15},{8,0},{9,1},... | collective-permute-start | bytes 2359304 | tf_op jit(solution)/shard_map/ppermute | solution.py:197
  60.7 1.9 %collective-permute-start.18 = (bf16[2,12,64,128]{3,2,1,0:T(8,128)(2,1)S(1)}, bf16[2,12,64,128]{3,2,1,0:T(8,128)(2,1)S(1)}, u32[]{:S(2)}, u32[]{:S(2)}) collective-permute-start(bf16[2,12,64,128]{3,2,1,0:T(8,128)(2,1)S(1)} %collective-permute-done.15.refs_2_), channel_id=1, source_target_pairs={{0,8},{1,9},{2,10},{3,11},{4,12},{5,13},{6,14},{7,15},{8,0},{9,1},... | collective-permute-start | bytes 1179656 | tf_op jit(solution)/shard_map/ppermute | solution.py:197

commit v17 on v15

--- a/solution.py
+++ b/solution.py
@@ -141,27 +141,19 @@
 
 
 def route_second(*refs):
-    ab0_ref, o1_ref, o2_ref, stack_ref, both_ref, mixed_ref = refs[2:]
-    core = lax.axis_index("core")
+    o1_ref, o2_ref, stack_ref, both_ref = refs[3:]
     for slot in range(5):
         stack_ref[slot] = refs[slot][...]
     both_ref[0] = o1_ref[...]
     both_ref[1] = o2_ref[...]
 
-    @pl.when(core == 0)
-    def _():
-        mixed_ref[...] = o2_ref[...]
-
-    @pl.when(core != 0)
-    def _():
-        mixed_ref[...] = ab0_ref[...]
-
-
-def route_third(ab1_ref, o3_ref, ab2_ref, a12_ref, b12_ref, stack_ref):
-    for slot, ref in enumerate((ab1_ref, ab2_ref, o3_ref)):
-        stack_ref[slot] = ref[...]
-    stack_ref[3:5] = a12_ref[...]
-    stack_ref[5:7] = b12_ref[...]
+
+def route_third(ab2_ref, o3_ref, a12_ref, b12_ref, stack_ref, a1_ref):
+    stack_ref[0] = ab2_ref[...]
+    stack_ref[1] = o3_ref[...]
+    stack_ref[2:4] = a12_ref[...]
+    stack_ref[4:6] = b12_ref[...]
+    a1_ref[...] = a12_ref[0]
 
 
 def route_last(a3_ref, ab3_ref, stack_ref):
@@ -202,16 +194,8 @@
     def hop_b(array):
         return move(array, lambda p, c, z, y: (p, c, z, y ^ 1) if c == 0 else (p ^ 1, c, z, y))
 
-    def hop_ab(array):
-        return move(array, lambda p, c, z, y: (p ^ 1, c, z, y ^ 1))
-
     def hop_z(array, by):
         return move(array, lambda p, c, z, y: (p, c, z ^ by, y))
-
-    def hop_mixed(array):
-        return move(
-            array, lambda p, c, z, y: (p ^ 1, c, z, y ^ 1) if c == 0 else (p, c, z ^ 2, y)
-        )
 
     def swap(array):
         return move(array, lambda p, c, z, y: (p, c ^ 1, z, y))
@@ -300,49 +284,52 @@
         return fence(routed)
 
     first = [("O", 0), ("A", 0), ("B", 0), ("AB", 0), ("O", 1), ("O", 2)]
-    second = [("AB", 1), ("AB", 2), ("O", 3), ("A", 1), ("A", 2), ("B", 1), ("B", 2)]
-    third = [("A", 3), ("AB", 3), ("B", 3)]
-    stack, both, mixed = route(route_second, [near(*kind) for kind in first[1:]], (5, 2, 1))
+    second = [("AB", 2), ("O", 3), ("A", 1), ("A", 2), ("B", 1), ("B", 2)]
+    third = [("A", 3), ("B", 3)]
+    fourth = [("AB", 3), ("AB", 1)]
+    stack, both = route(route_second, [near(*kind) for kind in first[1:]], (5, 2))
     totals = add([("near", *kind) for kind in first], None)
-    o3, ab2, a12, b12 = hop_z(near("O", 2), 1), hop_mixed(mixed), hop_a(both), hop_b(both)
+    o3, ab2 = hop_z(near("O", 2), 1), hop_z(near("AB", 0), 2)
+    a12, b12 = hop_a(both), hop_b(both)
     put("2a", swap(stack), "far", first[1:])
     totals = fence(totals)
 
-    put("2b", hop_z(near("AB", 0), 1), "near", [("AB", 1)])
     totals = add([("far", *kind) for kind in first], totals)
-    ab1 = arrays.pop("2b")
     put("2c", o3, "near", [("O", 3)])
+    totals = fence(totals)
+
+    a3, b3 = hop_a(near("O", 3)), hop_b(near("O", 3))
+    totals = add([("near", "O", 3)], totals, weight=45)
     put("2d", ab2, "near", [("AB", 2)])
-    totals = fence(totals)
-
-    ab3, a3, b3 = hop_z(near("AB", 2), 1), hop_a(near("O", 3)), hop_b(near("O", 3))
-    totals = add([("near", "O", 3)], totals, weight=45)
-    arrays["2b"] = ab1
     put("2e", a12, "near", [("A", 1), ("A", 2)])
     put("2f", b12, "near", [("B", 1), ("B", 2)])
     totals = fence(totals)
 
-    keys = ("2b", "2c", "2d", "2e", "2f")
-    (stack,) = route(route_third, [arrays[key] for key in keys], (7,))
-    far2 = swap(stack)
+    ab3 = hop_z(near("AB", 2), 1)
+    stack, a1 = route(route_third, [arrays[key] for key in ("2d", "2c", "2e", "2f")], (6, 1))
+    far2, ab1 = swap(stack), hop_b(a1)
     names = [("near", *kind) for kind in second if kind != ("O", 3)]
     totals = add(names, totals)
-    a3, ab3, totals = lax.optimization_barrier((a3, ab3, totals))
-    (stack,) = route(route_last, [a3, ab3], (2,), weight=10**11)
-    put("3a", stack, "near", third[:2])
-    stack = swap(stack)
+    a3, b3, totals = lax.optimization_barrier((a3, b3, totals))
+    (stack,) = route(route_last, [a3, b3], (2,), weight=10**11)
+    put("3a", stack, "near", third)
+    far3 = swap(stack)
     put("3d", far2, "far", second)
-    totals = add([("far", *kind) for kind in second], totals)
-    put("3b", b3, "near", third[2:])
+    names = [("far", *kind) for kind in second] + [("near", *kind) for kind in third]
+    totals = add(names, totals)
+    put("3b", ab3, "near", fourth[:1])
+    put("3c", ab1, "near", fourth[1:])
     totals = fence(totals)
 
-    put("4a", stack, "far", third[:2])
-    far3 = swap(near("B", 3))
-    names = [("near", *kind) for kind in third]
-    totals, (slots, left) = add(names, totals, keep=left_slots(names))
-    put("4b", far3, "far", third[2:])
+    far4 = [swap(near(*kind)) for kind in fourth]
+    names = [("far", *kind) for kind in third + fourth]
+    slots = left_slots(names)
+    totals, (slots, left) = add([("near", *kind) for kind in fourth], totals, keep=slots)
+    put("4a", far3, "far", third)
+    put("4b", far4[0], "far", fourth[:1])
+    put("4c", far4[1], "far", fourth[1:])
     totals, left = fence((totals, left))
-    return add([("far", *kind) for kind in third], totals, left=(slots, left), last=True)
+    return add(names, totals, left=(slots, left), last=True)
 
 
 def add_terms(place_ref, weights_ref, left_ref, right_ref, field_ref):

time: 63.1 us -> 62.9 us (level)
  waiting for transfers between devices: 29.2 us -> 27 us
  local copies, waits for them, and re-layouts: 0.01 us -> 1 us
  starting transfers between devices: 22.1 us -> 22.9 us
    ppermute x18 -> x19, waiting for transfers between devices: 29.2 us -> 27 us  [move(): return lax.ppermute(array, AXES, pairs)]
    unnamed x4, local copies, waits for them, and re-layouts: 0.01 us -> 1 us
    ppermute x18 -> x19, starting transfers between devices: 22.1 us -> 22.9 us  [move(): return lax.ppermute(array, AXES, pairs)]
  transfers between devices with their start and end apart: 18 -> 19, of which waited for: 10 -> 11; matrix products, arithmetic and copies ran while one was open for 0% -> 0% of each run, Pallas kernels for 14% -> 14%
where the time goes in v17:
time: 62.9 us; the launch traced here: 62.8 us
  waiting for transfers between devices  27 us (43%)
  starting transfers between devices  22.9 us (36%)
  Pallas kernels  11.4 us (18%)
  local copies, waits for them, and re-layouts  1 us (2%)
    ppermute x19, waiting for transfers between devices, move(): return lax.ppermute(array, AXES, pairs)  27 us
    ppermute x19, starting transfers between devices, move(): return lax.ppermute(array, AXES, pairs)  22.9 us
    pallas_call x7, Pallas kernels, add(): pl.pallas_call(functools.partial(add_shards, tuple(names), places, slots,...  10.9 us
  transfers between devices with their start and end apart: 19, of which 11 were waited for; matrix products, arithmetic and copies ran while one was open for 0% of the time, Pallas kernels for 14%

profile of v17, /device:TPU:0, one launch (start us, length us, event | category | flops | bytes accessed | tf_op | source)
XLA Modules:
  0.0 62.8 jit_solution(770665412415081450)
XLA Ops:
  0.0 0.0 copy-start
  0.0 4.0 %collective-permute-start = (bf16[2,12,64,128]{3,2,1,0:T(8,128)(2,1)}, bf16[2,12,64,128]{3,2,1,0:T(8,128)(2,1)S(1)}, u32[]{:S(2)}, u32[]{:S(2)}) collective-permute-start(bf16[2,12,64,128]{3,2,1,0:T(8,128)(2,1)} %bitcast.24), channel_id=1, source_target_pairs={{0,4},{1,5},{2,6},{3,7},{4,0},{5,1},{6,2},{7,3},{8,12},{9,13},{10,... | collective-permute-start | bytes 1179656 | tf_op jit(solution)/shard_map/ppermute | solution.py:189
  4.0 1.5 %collective-permute-start.1 = (bf16[2,12,64,128]{3,2,1,0:T(8,128)(2,1)}, bf16[2,12,64,128]{3,2,1,0:T(8,128)(2,1)S(1)}, u32[]{:S(2)}, u32[]{:S(2)}) collective-permute-start(bf16[2,12,64,128]{3,2,1,0:T(8,128)(2,1)} %bitcast.25), channel_id=1, source_target_pairs={{0,16},{1,17},{2,18},{3,19},{4,20},{5,21},{6,22},{7,23},{8,9},{9,8... | collective-permute-start | bytes 1179656 | tf_op jit(solution)/shard_map/ppermute | solution.py:189
  5.5 1.6 %collective-permute-start.2 = (bf16[2,12,64,128]{3,2,1,0:T(8,128)(2,1)}, bf16[2,12,64,128]{3,2,1,0:T(8,128)(2,1)S(1)}, u32[]{:S(2)}, u32[]{:S(2)}) collective-permute-start(bf16[2,12,64,128]{3,2,1,0:T(8,128)(2,1)} %bitcast.26), channel_id=1, source_target_pairs={{0,2},{1,3},{2,0},{3,1},{4,6},{5,7},{6,4},{7,5},{8,10},{9,11},{10,... | collective-permute-start | bytes 1179656 | tf_op jit(solution)/shard_map/ppermute | solution.py:189
  7.1 1.5 %collective-permute-start.3 = (bf16[2,12,64,128]{3,2,1,0:T(8,128)(2,1)}, bf16[2,12,64,128]{3,2,1,0:T(8,128)(2,1)S(1)}, u32[]{:S(2)}, u32[]{:S(2)}) collective-permute-start(bf16[2,12,64,128]{3,2,1,0:T(8,128)(2,1)} %bitcast.27), channel_id=1, source_target_pairs={{0,1},{1,0},{2,3},{3,2},{4,5},{5,4},{6,7},{7,6},{8,24},{9,25},{10,... | collective-permute-start | bytes 1179656 | tf_op jit(solution)/shard_map/ppermute | solution.py:189
  8.6 0.0 collective-permute-start.5
  8.6 0.0 copy-done
  8.7 0.1 fusion
  8.8 6.3 %collective-permute-done.1.refs_0_.refs_1_ = bf16[2,12,64,128]{3,2,1,0:T(8,128)(2,1)S(1)} collective-permute-done((bf16[2,12,64,128]{3,2,1,0:T(8,128)(2,1)}, bf16[2,12,64,128]{3,2,1,0:T(8,128)(2,1)S(1)}, u32[]{:S(2)}, u32[]{:S(2)}) %collective-permute-start.1) | collective-permute-done | bytes 393248 | tf_op jit(solution)/shard_map/ppermute | solution.py:189
  15.1 2.6 %collective-permute-start.4 = (bf16[2,12,64,128]{3,2,1,0:T(8,128)(2,1)S(1)}, bf16[2,12,64,128]{3,2,1,0:T(8,128)(2,1)S(1)}, u32[]{:S(2)}, u32[]{:S(2)}) collective-permute-start(bf16[2,12,64,128]{3,2,1,0:T(8,128)(2,1)S(1)} %collective-permute-done.1.refs_0_.refs_1_), channel_id=1, source_target_pairs={{0,1},{1,0},{2,3},{3,2},{4,5},{5,4},{6,7},{7,6},{8,24},{9,25},{10,... | collective-permute-start | bytes 1179656 | tf_op jit(solution)/shard_map/ppermute | solution.py:189
  17.7 0.1 multiply_cosine_fusion
  17.8 4.1 %collective-permute-done.refs_4_.refs_0_ = bf16[2,12,64,128]{3,2,1,0:T(8,128)(2,1)S(1)} collective-permute-done((bf16[2,12,64,128]{3,2,1,0:T(8,128)(2,1)}, bf16[2,12,64,128]{3,2,1,0:T(8,128)(2,1)S(1)}, u32[]{:S(2)}, u32[]{:S(2)}) %collective-permute-start) | collective-permute-done | bytes 393248 | tf_op jit(solution)/shard_map/ppermute | solution.py:189
  21.9 1.4 %collective-permute-done.2.refs_3_.refs_2_.refs_1_ = bf16[2,12,64,128]{3,2,1,0:T(8,128)(2,1)S(1)} collective-permute-done((bf16[2,12,64,128]{3,2,1,0:T(8,128)(2,1)}, bf16[2,12,64,128]{3,2,1,0:T(8,128)(2,1)S(1)}, u32[]{:S(2)}, u32[]{:S(2)}) %collective-permute-start.2) | collective-permute-done | bytes 393248 | tf_op jit(solution)/shard_map/ppermute | solution.py:189
  23.3 0.0 collective-permute-done.3.refs_1_.refs_3_
  23.3 0.0 collective-permute-done.5.refs_4_
  23.3 0.1 collective-permute-done.4.refs_2_.refs_4_
  23.4 0.2 shard_map.28
  23.6 0.1 collective-permute-start.6
  23.7 2.2 %collective-permute-start.7 = (bf16[2,12,64,128]{3,2,1,0:T(8,128)(2,1)S(1)}, bf16[2,12,64,128]{3,2,1,0:T(8,128)(2,1)S(1)}, u32[]{:S(2)}, u32[]{:S(2)}) collective-permute-start(bf16[2,12,64,128]{3,2,1,0:T(8,128)(2,1)S(1)} %collective-permute-done.refs_4_.refs_0_), channel_id=1, source_target_pairs={{0,2},{1,3},{2,0},{3,1},{4,6},{5,7},{6,4},{7,5},{8,10},{9,11},{10,... | collective-permute-start | bytes 1179656 | tf_op jit(solution)/shard_map/ppermute | solution.py:189
  25.9 1.5 %collective-permute-start.9 = (bf16[2,2,12,64,128]{4,3,2,1,0:T(8,128)(2,1)S(1)}, bf16[2,2,12,64,128]{4,3,2,1,0:T(8,128)(2,1)S(1)}, u32[]{:S(2)}, u32[]{:S(2)}) collective-permute-start(bf16[2,2,12,64,128]{4,3,2,1,0:T(8,128)(2,1)S(1)} %get-tuple-element.105), channel_id=1, source_target_pairs={{0,16},{1,17},{2,18},{3,19},{4,20},{5,21},{6,22},{7,23},{8,9},{9,8... | collective-permute-start | bytes 2359304 | tf_op jit(solution)/shard_map/ppermute | solution.py:189
  27.4 0.6 collective-permute-start.10
  28.0 1.3 %collective-permute-start.8 = (bf16[2,12,64,128]{3,2,1,0:T(8,128)(2,1)S(1)}, bf16[2,12,64,128]{3,2,1,0:T(8,128)(2,1)S(1)}, u32[]{:S(2)}, u32[]{:S(2)}) collective-permute-start(bf16[2,12,64,128]{3,2,1,0:T(8,128)(2,1)S(1)} %collective-permute-done.4.refs_2_.refs_4_), channel_id=1, source_target_pairs={{0,4},{1,5},{2,6},{3,7},{4,0},{5,1},{6,2},{7,3},{8,12},{9,13},{10,... | collective-permute-start | bytes 1179656 | tf_op jit(solution)/shard_map/ppermute | solution.py:189
  29.3 0.0 copy-start.1
  29.3 1.0 %copy-done.1 = bf16[2,1,64,12,128]{4,2,3,1,0:T(8,128)(2,1)S(1)} copy-done((bf16[2,1,64,12,128]{4,2,3,1,0:T(8,128)(2,1)S(1)}, bf16[2,1,64,12,128]{4,2,3,1,0:T(8,128)(2,1)}, u32[]{:S(2)}) %copy-start.1) | copy-done | bytes 393240
  30.3 1.8 %shard_map.29.refs_7_ = f32[2,2,256,256]{3,2,1,0:T(8,128)S(1)} custom-call(f32[8,2,128]{2,1,0:T(2,128)S(1)} %maximum_bitcast_fusion.weights_ref, bf16[2,12,64,128]{3,2,1,0:T(8,128)(2,1)S(1)} %collective-permute-done.refs_4_.refs_0_, bf16[2,12,64,128]{3,2,1,0:T(8,128)(2,1)S(1)} %collective-permute-done.1.refs_0_.refs_1_, ...), custom_call_target="tpu_custom_call" | custom-call | flops 1207959552 | bytes 4456448 | tf_op jit(solution)/shard_map/pallas_call | solution.py:242
  32.0 0.0 collective-permute-done.6.refs_5_
  32.1 1.7 %shard_map.30.refs_1_ = f32[2,2,256,256]{3,2,1,0:T(8,128)S(1)} custom-call(f32[8,2,128]{2,1,0:T(2,128)S(1)} %maximum_bitcast_fusion.weights_ref, bf16[2,12,64,128]{3,2,1,0:T(8,128)(2,1)S(1)} %collective-permute-done.refs_4_.refs_0_, bf16[2,12,64,128]{3,2,1,0:T(8,128)(2,1)S(1)} %collective-permute-done.1.refs_0_.refs_1_, ...), custom_call_target="tpu_custom_call" | custom-call | flops 1207959552 | bytes 4456448 | tf_op jit(solution)/shard_map/pallas_call | solution.py:242
  33.8 6.7 %collective-permute-done.7.refs_0_.o3_ref.refs_2_ = bf16[2,12,64,128]{3,2,1,0:T(8,128)(2,1)S(1)} collective-permute-done((bf16[2,12,64,128]{3,2,1,0:T(8,128)(2,1)S(1)}, bf16[2,12,64,128]{3,2,1,0:T(8,128)(2,1)S(1)}, u32[]{:S(2)}, u32[]{:S(2)}) %collective-permute-start.7) | collective-permute-done | bytes 393248 | tf_op jit(solution)/shard_map/ppermute | solution.py:189
  40.5 2.2 %collective-permute-start.11 = (bf16[2,12,64,128]{3,2,1,0:T(8,128)(2,1)S(1)}, bf16[2,12,64,128]{3,2,1,0:T(8,128)(2,1)S(1)}, u32[]{:S(2)}, u32[]{:S(2)}) collective-permute-start(bf16[2,12,64,128]{3,2,1,0:T(8,128)(2,1)S(1)} %collective-permute-done.7.refs_0_.o3_ref.refs_2_), channel_id=1, source_target_pairs={{0,16},{1,17},{2,18},{3,19},{4,20},{5,21},{6,22},{7,23},{8,9},{9,8... | collective-permute-start | bytes 1179656 | tf_op jit(solution)/shard_map/ppermute | solution.py:189
  42.6 1.5 %collective-permute-start.12 = (bf16[2,12,64,128]{3,2,1,0:T(8,128)(2,1)S(1)}, bf16[2,12,64,128]{3,2,1,0:T(8,128)(2,1)S(1)}, u32[]{:S(2)}, u32[]{:S(2)}) collective-permute-start(bf16[2,12,64,128]{3,2,1,0:T(8,128)(2,1)S(1)} %collective-permute-done.7.refs_0_.o3_ref.refs_2_), channel_id=1, source_target_pairs={{0,1},{1,0},{2,3},{3,2},{4,5},{5,4},{6,7},{7,6},{8,24},{9,25},{10,... | collective-permute-start | bytes 1179656 | tf_op jit(solution)/shard_map/ppermute | solution.py:189
  44.2 0.4 shard_map.31.refs_5_
  44.6 3.4 %collective-permute-done.8.ab2_ref.refs_2_ = bf16[2,12,64,128]{3,2,1,0:T(8,128)(2,1)S(1)} collective-permute-done((bf16[2,12,64,128]{3,2,1,0:T(8,128)(2,1)S(1)}, bf16[2,12,64,128]{3,2,1,0:T(8,128)(2,1)S(1)}, u32[]{:S(2)}, u32[]{:S(2)}) %collective-permute-start.8) | collective-permute-done | bytes 393248 | tf_op jit(solution)/shard_map/ppermute | solution.py:189
  48.0 0.0 collective-permute-done.9.a12_ref.refs_3_.refs_1_
  48.0 0.0 collective-permute-done.10.b12_ref.refs_4_.refs_2_
  48.0 0.0 collective-permute-start.13
  48.0 0.2 shard_map.32
  48.2 1.8 %collective-permute-start.14 = (bf16[2,12,64,128]{3,2,1,0:T(8,128)(2,1)S(1)}, bf16[2,12,64,128]{3,2,1,0:T(8,128)(2,1)S(1)}, u32[]{:S(2)}, u32[]{:S(2)}) collective-permute-start(bf16[2,12,64,128]{3,2,1,0:T(8,128)(2,1)S(1)} %get-tuple-element.130), channel_id=1, source_target_pairs={{0,1},{1,0},{2,3},{3,2},{4,5},{5,4},{6,7},{7,6},{8,24},{9,25},{10,... | collective-permute-start | bytes 1179656 | tf_op jit(solution)/shard_map/ppermute | solution.py:189
  50.0 0.0 collective-permute-start.15
  50.0 1.6 %shard_map.33.refs_7_ = f32[2,2,256,256]{3,2,1,0:T(8,128)S(1)} custom-call(f32[8,2,128]{2,1,0:T(2,128)S(1)} %maximum_bitcast_fusion.weights_ref, bf16[2,12,64,128]{3,2,1,0:T(8,128)(2,1)S(1)} %collective-permute-done.refs_4_.refs_0_, bf16[2,12,64,128]{3,2,1,0:T(8,128)(2,1)S(1)} %collective-permute-done.2.refs_3_.refs_2_.refs_1_, ...), custom_call_target="tpu_custom_call" | custom-call | flops 1006632960 | bytes 4063232 | tf_op jit(solution)/shard_map/pallas_call | solution.py:242
  51.6 3.1 %collective-permute-done.11.a3_ref = bf16[2,12,64,128]{3,2,1,0:T(8,128)(2,1)S(1)} collective-permute-done((bf16[2,12,64,128]{3,2,1,0:T(8,128)(2,1)S(1)}, bf16[2,12,64,128]{3,2,1,0:T(8,128)(2,1)S(1)}, u32[]{:S(2)}, u32[]{:S(2)}) %collective-permute-start.11) | collective-permute-done | bytes 393248 | tf_op jit(solution)/shard_map/ppermute | solution.py:189
  54.8 0.0 collective-permute-done.12.ab3_ref
  54.8 0.1 shard_map.34.refs_5_.refs_3_
  54.8 0.1 collective-permute-start.16
  54.9 0.0 collective-permute-done.15.refs_6_
  54.9 2.3 %shard_map.35.refs_6_ = f32[2,2,256,256]{3,2,1,0:T(8,128)S(1)} custom-call(f32[8,2,128]{2,1,0:T(2,128)S(1)} %maximum_bitcast_fusion.weights_ref, bf16[2,12,64,128]{3,2,1,0:T(8,128)(2,1)S(1)} %collective-permute-done.refs_4_.refs_0_, bf16[2,12,64,128]{3,2,1,0:T(8,128)(2,1)S(1)} %collective-permute-done.2.refs_3_.refs_2_.refs_1_, ...), custom_call_target="tpu_custom_call" | custom-call | flops 1610612736 | bytes 5242880 | tf_op jit(solution)/shard_map/pallas_call | solution.py:242
  57.2 0.5 collective-permute-done.13.refs_4_
  57.8 0.4 collective-permute-done.14.refs_5_
  58.2 0.4 collective-permute-start.17
  58.6 0.1 collective-permute-start.18
  58.7 0.8 %shard_map.36 = (f32[2,2,256,256]{3,2,1,0:T(8,128)S(1)}, bf16[3,512,768]{2,1,0:T(8,128)(2,1)S(1)}) custom-call(f32[8,2,128]{2,1,0:T(2,128)S(1)} %maximum_bitcast_fusion.weights_ref, bf16[2,12,64,128]{3,2,1,0:T(8,128)(2,1)S(1)} %collective-permute-done.7.refs_0_.o3_ref.refs_2_, ...), custom_call_target="tpu_custom_call" | custom-call | flops 402653184 | bytes 2883584 | tf_op jit(solution)/shard_map/pallas_call | solution.py:242
  59.5 0.0 collective-permute-done.16.refs_0_
  59.5 0.4 collective-permute-done.17.refs_1_
  59.9 0.6 collective-permute-done.18.refs_2_
  60.5 2.3 %shard_map.37 = f32[16,64,256]{2,1,0:T(8,128)} custom-call(f32[8,2,128]{2,1,0:T(2,128)S(1)} %maximum_bitcast_fusion.weights_ref, bf16[2,2,12,64,128]{4,3,2,1,0:T(8,128)(2,1)S(1)} %collective-permute-done.16.refs_0_, bf16[2,12,64,128]{3,2,1,0:T(8,128)(2,1)S(1)} %collective-permute-done.17.refs_1_, ...), custom_call_target="tpu_custom_call" | custom-call | flops 805306368 | bytes 3670016 | tf_op jit(solution)/shard_map/pallas_call | solution.py:242
  (5 shorter events, 0.1 us)
Async XLA Ops:
  0.0 8.6 %copy-start = (s32[4,3]{1,0:T(4,128)S(1)}, s32[4,3]{1,0:T(4,128)}, u32[]{:S(2)}) copy-start(s32[4,3]{1,0:T(4,128)} %param.3) | copy-start | bytes 148
  0.0 21.9 %collective-permute-start = (bf16[2,12,64,128]{3,2,1,0:T(8,128)(2,1)}, bf16[2,12,64,128]{3,2,1,0:T(8,128)(2,1)S(1)}, u32[]{:S(2)}, u32[]{:S(2)}) collective-permute-start(bf16[2,12,64,128]{3,2,1,0:T(8,128)(2,1)} %bitcast.24), channel_id=1, source_target_pairs={{0,4},{1,5},{2,6},{3,7},{4,0},{5,1},{6,2},{7,3},{8,12},{9,13},{10,... | collective-permute-start | bytes 1179656 | tf_op jit(solution)/shard_map/ppermute | solution.py:189
  4.0 11.1 %collective-permute-start.1 = (bf16[2,12,64,128]{3,2,1,0:T(8,128)(2,1)}, bf16[2,12,64,128]{3,2,1,0:T(8,128)(2,1)S(1)}, u32[]{:S(2)}, u32[]{:S(2)}) collective-permute-start(bf16[2,12,64,128]{3,2,1,0:T(8,128)(2,1)} %bitcast.25), channel_id=1, source_target_pairs={{0,16},{1,17},{2,18},{3,19},{4,20},{5,21},{6,22},{7,23},{8,9},{9,8... | collective-permute-start | bytes 1179656 | tf_op jit(solution)/shard_map/ppermute | solution.py:189
  5.5 17.8 %collective-permute-start.2 = (bf16[2,12,64,128]{3,2,1,0:T(8,128)(2,1)}, bf16[2,12,64,128]{3,2,1,0:T(8,128)(2,1)S(1)}, u32[]{:S(2)}, u32[]{:S(2)}) collective-permute-start(bf16[2,12,64,128]{3,2,1,0:T(8,128)(2,1)} %bitcast.26), channel_id=1, source_target_pairs={{0,2},{1,3},{2,0},{3,1},{4,6},{5,7},{6,4},{7,5},{8,10},{9,11},{10,... | collective-permute-start | bytes 1179656 | tf_op jit(solution)/shard_map/ppermute | solution.py:189
  7.1 16.2 %collective-permute-start.3 = (bf16[2,12,64,128]{3,2,1,0:T(8,128)(2,1)}, bf16[2,12,64,128]{3,2,1,0:T(8,128)(2,1)S(1)}, u32[]{:S(2)}, u32[]{:S(2)}) collective-permute-start(bf16[2,12,64,128]{3,2,1,0:T(8,128)(2,1)} %bitcast.27), channel_id=1, source_target_pairs={{0,1},{1,0},{2,3},{3,2},{4,5},{5,4},{6,7},{7,6},{8,24},{9,25},{10,... | collective-permute-start | bytes 1179656 | tf_op jit(solution)/shard_map/ppermute | solution.py:189
  8.6 14.7 %collective-permute-start.5 = (bf16[2,12,64,128]{3,2,1,0:T(8,128)(2,1)}, bf16[2,12,64,128]{3,2,1,0:T(8,128)(2,1)S(1)}, u32[]{:S(2)}, u32[]{:S(2)}) collective-permute-start(bf16[2,12,64,128]{3,2,1,0:T(8,128)(2,1)} %bitcast.28), channel_id=1, source_target_pairs={{0,8},{1,9},{2,10},{3,11},{4,12},{5,13},{6,14},{7,15},{8,0},{9,1},... | collective-permute-start | bytes 1179656 | tf_op jit(solution)/shard_map/ppermute | solution.py:189
  15.1 8.3 %collective-permute-start.4 = (bf16[2,12,64,128]{3,2,1,0:T(8,128)(2,1)S(1)}, bf16[2,12,64,128]{3,2,1,0:T(8,128)(2,1)S(1)}, u32[]{:S(2)}, u32[]{:S(2)}) collective-permute-start(bf16[2,12,64,128]{3,2,1,0:T(8,128)(2,1)S(1)} %collective-permute-done.1.refs_0_.refs_1_), channel_id=1, source_target_pairs={{0,1},{1,0},{2,3},{3,2},{4,5},{5,4},{6,7},{7,6},{8,24},{9,25},{10,... | collective-permute-start | bytes 1179656 | tf_op jit(solution)/shard_map/ppermute | solution.py:189
  23.6 8.5 %collective-permute-start.6 = (bf16[5,2,12,64,128]{4,3,2,1,0:T(8,128)(2,1)S(1)}, bf16[5,2,12,64,128]{4,3,2,1,0:T(8,128)(2,1)S(1)}, u32[]{:S(2)}, u32[]{:S(2)}) collective-permute-start(bf16[5,2,12,64,128]{4,3,2,1,0:T(8,128)(2,1)S(1)} %get-tuple-element.92), channel_id=1, source_target_pairs={{0,8},{1,9},{2,10},{3,11},{4,12},{5,13},{6,14},{7,15},{8,0},{9,1},... | collective-permute-start | bytes 5898248 | tf_op jit(solution)/shard_map/ppermute | solution.py:189
  23.7 16.8 %collective-permute-start.7 = (bf16[2,12,64,128]{3,2,1,0:T(8,128)(2,1)S(1)}, bf16[2,12,64,128]{3,2,1,0:T(8,128)(2,1)S(1)}, u32[]{:S(2)}, u32[]{:S(2)}) collective-permute-start(bf16[2,12,64,128]{3,2,1,0:T(8,128)(2,1)S(1)} %collective-permute-done.refs_4_.refs_0_), channel_id=1, source_target_pairs={{0,2},{1,3},{2,0},{3,1},{4,6},{5,7},{6,4},{7,5},{8,10},{9,11},{10,... | collective-permute-start | bytes 1179656 | tf_op jit(solution)/shard_map/ppermute | solution.py:189
  25.9 22.1 %collective-permute-start.9 = (bf16[2,2,12,64,128]{4,3,2,1,0:T(8,128)(2,1)S(1)}, bf16[2,2,12,64,128]{4,3,2,1,0:T(8,128)(2,1)S(1)}, u32[]{:S(2)}, u32[]{:S(2)}) collective-permute-start(bf16[2,2,12,64,128]{4,3,2,1,0:T(8,128)(2,1)S(1)} %get-tuple-element.105), channel_id=1, source_target_pairs={{0,16},{1,17},{2,18},{3,19},{4,20},{5,21},{6,22},{7,23},{8,9},{9,8... | collective-permute-start | bytes 2359304 | tf_op jit(solution)/shard_map/ppermute | solution.py:189
  27.4 20.6 %collective-permute-start.10 = (bf16[2,2,12,64,128]{4,3,2,1,0:T(8,128)(2,1)S(1)}, bf16[2,2,12,64,128]{4,3,2,1,0:T(8,128)(2,1)S(1)}, u32[]{:S(2)}, u32[]{:S(2)}) collective-permute-start(bf16[2,2,12,64,128]{4,3,2,1,0:T(8,128)(2,1)S(1)} %get-tuple-element.105), channel_id=1, source_target_pairs={{0,1},{1,0},{2,3},{3,2},{4,5},{5,4},{6,7},{7,6},{8,24},{9,25},{10,... | collective-permute-start | bytes 2359304 | tf_op jit(solution)/shard_map/ppermute | solution.py:189
  28.0 20.0 %collective-permute-start.8 = (bf16[2,12,64,128]{3,2,1,0:T(8,128)(2,1)S(1)}, bf16[2,12,64,128]{3,2,1,0:T(8,128)(2,1)S(1)}, u32[]{:S(2)}, u32[]{:S(2)}) collective-permute-start(bf16[2,12,64,128]{3,2,1,0:T(8,128)(2,1)S(1)} %collective-permute-done.4.refs_2_.refs_4_), channel_id=1, source_target_pairs={{0,4},{1,5},{2,6},{3,7},{4,0},{5,1},{6,2},{7,3},{8,12},{9,13},{10,... | collective-permute-start | bytes 1179656 | tf_op jit(solution)/shard_map/ppermute | solution.py:189
  29.3 1.0 %copy-start.1 = (bf16[2,1,64,12,128]{4,2,3,1,0:T(8,128)(2,1)S(1)}, bf16[2,1,64,12,128]{4,2,3,1,0:T(8,128)(2,1)}, u32[]{:S(2)}) copy-start(bf16[2,1,64,12,128]{4,2,3,1,0:T(8,128)(2,1)} %param.2) | copy-start | bytes 1179652
  40.5 14.3 %collective-permute-start.11 = (bf16[2,12,64,128]{3,2,1,0:T(8,128)(2,1)S(1)}, bf16[2,12,64,128]{3,2,1,0:T(8,128)(2,1)S(1)}, u32[]{:S(2)}, u32[]{:S(2)}) collective-permute-start(bf16[2,12,64,128]{3,2,1,0:T(8,128)(2,1)S(1)} %collective-permute-done.7.refs_0_.o3_ref.refs_2_), channel_id=1, source_target_pairs={{0,16},{1,17},{2,18},{3,19},{4,20},{5,21},{6,22},{7,23},{8,9},{9,8... | collective-permute-start | bytes 1179656 | tf_op jit(solution)/shard_map/ppermute | solution.py:189
  42.6 12.1 %collective-permute-start.12 = (bf16[2,12,64,128]{3,2,1,0:T(8,128)(2,1)S(1)}, bf16[2,12,64,128]{3,2,1,0:T(8,128)(2,1)S(1)}, u32[]{:S(2)}, u32[]{:S(2)}) collective-permute-start(bf16[2,12,64,128]{3,2,1,0:T(8,128)(2,1)S(1)} %collective-permute-done.7.refs_0_.o3_ref.refs_2_), channel_id=1, source_target_pairs={{0,1},{1,0},{2,3},{3,2},{4,5},{5,4},{6,7},{7,6},{8,24},{9,25},{10,... | collective-permute-start | bytes 1179656 | tf_op jit(solution)/shard_map/ppermute | solution.py:189
  48.0 9.8 %collective-permute-start.13 = (bf16[2,12,64,128]{3,2,1,0:T(8,128)(2,1)S(1)}, bf16[2,12,64,128]{3,2,1,0:T(8,128)(2,1)S(1)}, u32[]{:S(2)}, u32[]{:S(2)}) collective-permute-start(bf16[2,12,64,128]{3,2,1,0:T(8,128)(2,1)S(1)} %collective-permute-done.8.ab2_ref.refs_2_), channel_id=1, source_target_pairs={{0,2},{1,3},{2,0},{3,1},{4,6},{5,7},{6,4},{7,5},{8,10},{9,11},{10,... | collective-permute-start | bytes 1179656 | tf_op jit(solution)/shard_map/ppermute | solution.py:189
  48.2 10.0 %collective-permute-start.14 = (bf16[2,12,64,128]{3,2,1,0:T(8,128)(2,1)S(1)}, bf16[2,12,64,128]{3,2,1,0:T(8,128)(2,1)S(1)}, u32[]{:S(2)}, u32[]{:S(2)}) collective-permute-start(bf16[2,12,64,128]{3,2,1,0:T(8,128)(2,1)S(1)} %get-tuple-element.130), channel_id=1, source_target_pairs={{0,1},{1,0},{2,3},{3,2},{4,5},{5,4},{6,7},{7,6},{8,24},{9,25},{10,... | collective-permute-start | bytes 1179656 | tf_op jit(solution)/shard_map/ppermute | solution.py:189
  50.0 4.9 %collective-permute-start.15 = (bf16[6,2,12,64,128]{4,3,2,1,0:T(8,128)(2,1)S(1)}, bf16[6,2,12,64,128]{4,3,2,1,0:T(8,128)(2,1)S(1)}, u32[]{:S(2)}, u32[]{:S(2)}) collective-permute-start(bf16[6,2,12,64,128]{4,3,2,1,0:T(8,128)(2,1)S(1)} %get-tuple-element.131), channel_id=1, source_target_pairs={{0,8},{1,9},{2,10},{3,11},{4,12},{5,13},{6,14},{7,15},{8,0},{9,1},... | collective-permute-start | bytes 7077896 | tf_op jit(solution)/shard_map/ppermute | solution.py:189
  54.8 4.6 %collective-permute-start.16 = (bf16[2,2,12,64,128]{4,3,2,1,0:T(8,128)(2,1)S(1)}, bf16[2,2,12,64,128]{4,3,2,1,0:T(8,128)(2,1)S(1)}, u32[]{:S(2)}, u32[]{:S(2)}) collective-permute-start(bf16[2,2,12,64,128]{4,3,2,1,0:T(8,128)(2,1)S(1)} %shard_map.34.refs_5_.refs_3_), channel_id=1, source_target_pairs={{0,8},{1,9},{2,10},{3,11},{4,12},{5,13},{6,14},{7,15},{8,0},{9,1},... | collective-permute-start | bytes 2359304 | tf_op jit(solution)/shard_map/ppermute | solution.py:189
  58.2 1.7 %collective-permute-start.17 = (bf16[2,12,64,128]{3,2,1,0:T(8,128)(2,1)S(1)}, bf16[2,12,64,128]{3,2,1,0:T(8,128)(2,1)S(1)}, u32[]{:S(2)}, u32[]{:S(2)}) collective-permute-start(bf16[2,12,64,128]{3,2,1,0:T(8,128)(2,1)S(1)} %collective-permute-done.13.refs_4_), channel_id=1, source_target_pairs={{0,8},{1,9},{2,10},{3,11},{4,12},{5,13},{6,14},{7,15},{8,0},{9,1},... | collective-permute-start | bytes 1179656 | tf_op jit(solution)/shard_map/ppermute | solution.py:189
  58.6 1.9 %collective-permute-start.18 = (bf16[2,12,64,128]{3,2,1,0:T(8,128)(2,1)S(1)}, bf16[2,12,64,128]{3,2,1,0:T(8,128)(2,1)S(1)}, u32[]{:S(2)}, u32[]{:S(2)}) collective-permute-start(bf16[2,12,64,128]{3,2,1,0:T(8,128)(2,1)S(1)} %collective-permute-done.14.refs_5_), channel_id=1, source_target_pairs={{0,8},{1,9},{2,10},{3,11},{4,12},{5,13},{6,14},{7,15},{8,0},{9,1},... | collective-permute-start | bytes 1179656 | tf_op jit(solution)/shard_map/ppermute | solution.py:189

commit v18 on v17

--- a/solution.py
+++ b/solution.py
@@ -48,12 +48,16 @@
     return terms[:half] + terms[half:]
 
 
-def add_shards(names, where, slots, has_totals, given, last, share, weights_ref, *refs):
+def add_shards(names, where, slots, has_totals, given, half, last, share, weights_ref, *refs):
     refs = list(refs)
+    left_ref = None if given else refs.pop()
+    if half:
+        sems, row_ref, left_ref = left_ref, refs.pop(), refs.pop()
+        field_ref = refs.pop()
     if last:
-        sems, row_ref, far_ref = (refs.pop() for _ in range(3))
-    left_ref = None if given else refs.pop()
-    out_ref = refs.pop()
+        sems, row_ref, far_ref, field_ref, _ = (refs.pop() for _ in range(5))
+    else:
+        out_ref = refs.pop()
     totals_in = refs.pop() if has_totals else None
     left_ref = refs.pop() if given else left_ref
 
@@ -73,9 +77,57 @@
     first_s = lax.rem(lax.div((level * flat + beside) * (share // 2), 4), 4)
     spins = left_ref.shape[1] // (4 * per_block)
 
+    def send_columns(dx, near, far):
+        lane = lax.broadcasted_iota(jnp.int32, (per_block, 2 * per_block), 1)
+        start = pl.multiple_of(jnp.bitwise_xor(pair, dx) * (2 * per_block), 2 * per_block)
+        copies = []
+        for spin in range(spins):
+            for column in range(0, columns, 2):
+                first = (spin * columns + column) * 2
+                across = slice(column * per_block, (column + 2) * per_block)
+                for part in range(2):
+                    top = (part * spins + spin) * per_block
+                    one = near(slice(top, top + per_block), across)
+                    two = far(slice(top, top + per_block), across)
+                    even = jnp.where(core == 0, one, two)
+                    odd = jnp.where(core == 0, two, one)
+                    row_ref[first + part] = jnp.where(
+                        lane < per_block, even, pltpu.roll(odd, per_block, 1)
+                    )
+                    row_ref[first + part + 2] = jnp.where(
+                        lane < per_block, pltpu.roll(even, per_block, 1), odd
+                    )
+                four = pl.ds(first, 4)
+                target = field_ref.at[four, :, pl.ds(start, 2 * per_block)]
+                copies.append(
+                    pltpu.make_async_copy(row_ref.at[four], target, sems.at[len(copies)])
+                )
+                copies[-1].start()
+        return copies
+
+    def term(name):
+        side, kind, dz = name
+        right = jnp.concatenate([spin_rows(name, r) for r in range(columns)], 0)
+        turn = core if side == "near" else 1 - core
+        dx, dy = {"O": (0, 0), "A": (1 - turn, turn), "B": (turn, 1 - turn), "AB": (1, 1)}[kind]
+        if kind in ("O", "AB"):
+            slot = slots.index((dy, dz))
+        else:
+            slot = slots.index((0, dz)) + dy
+        return dx, product(left_ref[slot], right)
+
     if last:
-        far_ref[...] = totals_in[1]
-    elif has_totals:
+        far_ref[...] = totals_in[1, 1] + sum(term(name)[1] for name in names)
+        copies = send_columns(
+            1,
+            lambda rows, across: totals_in[0, 1, rows, across],
+            lambda rows, across: far_ref[rows, across],
+        )
+        for copy in copies:
+            copy.wait()
+        return
+
+    if has_totals:
         out_ref[...] = totals_in[...]
     else:
         out_ref[...] = jnp.zeros_like(out_ref)
@@ -94,48 +146,15 @@
                     for s in range(spins)
                 ]
             left_ref[slot] = left_sides(owns, weights_ref[site])
-
-    for side, kind, dz in names:
-        right = jnp.concatenate([spin_rows((side, kind, dz), r) for r in range(columns)], 0)
-        turn = core if side == "near" else 1 - core
-        dx, dy = {"O": (0, 0), "A": (1 - turn, turn), "B": (turn, 1 - turn), "AB": (1, 1)}[kind]
-        if kind in ("O", "AB"):
-            slot = slots.index((dy, dz))
-        else:
-            slot = slots.index((0, dz)) + dy
-        term = product(left_ref[slot], right)
-        if last:
-            far_ref[dx] += term
-        else:
-            out_ref[0 if side == "near" else 1, dx] += term
-
-    if last:
-        lane = lax.broadcasted_iota(jnp.int32, (per_block, 2 * per_block), 1)
-        copies = []
-        for spin in range(spins):
-            for column in range(0, columns, 2):
-                first = (spin * columns + column) * 2
-                across = pl.ds(column * per_block, 2 * per_block)
-                for part in range(2):
-                    top = (part * spins + spin) * per_block
-                    for p in range(2):
-                        dx = jnp.bitwise_xor(pair, p)
-                        near = totals_in[0, dx, pl.ds(top, per_block), across]
-                        far = far_ref[dx, pl.ds(top, per_block), across]
-                        even = jnp.where(core == 0, near, far)
-                        odd = jnp.where(core == 0, far, near)
-                        place = pl.ds(p * 2 * per_block, 2 * per_block)
-                        row_ref[first + part, :, place] = jnp.where(
-                            lane < per_block, even, pltpu.roll(odd, per_block, 1)
-                        )
-                        row_ref[first + part + 2, :, place] = jnp.where(
-                            lane < per_block, pltpu.roll(even, per_block, 1), odd
-                        )
-                rows = pl.ds(first, 4)
-                copies.append(
-                    pltpu.make_async_copy(row_ref.at[rows], out_ref.at[rows], sems.at[len(copies)])
-                )
-                copies[-1].start()
+    for name in names:
+        dx, added = term(name)
+        out_ref[0 if name[0] == "near" else 1, dx] += added
+    if half:
+        copies = send_columns(
+            0,
+            lambda rows, across: out_ref[0, 0, rows, across],
+            lambda rows, across: out_ref[1, 0, rows, across],
+        )
         for copy in copies:
             copy.wait()
 
@@ -212,8 +231,8 @@
         key, slot = where[("near", kind, dz)]
         return arrays[key] if slot is None else arrays[key][slot]
 
-    def add(names, totals, keep=None, left=None, last=False, weight=1):
-        given = left is not None
+    def add(names, totals, keep=None, left=None, half=False, field=None, weight=1):
+        given, last = left is not None, field is not None
         slots, left = left if given else (keep or left_slots(names), None)
         uses = list(names)
         for dy, dz in [] if given else slots:
@@ -221,32 +240,35 @@
         keys = sorted({where[name][0] for name in uses})
         places = {name: (keys.index(where[name][0]), where[name][1]) for name in uses}
         operands = [weights] + [arrays[key] for key in keys]
-        operands += [each for each in (left, totals) if each is not None]
+        operands += [each for each in (left, totals, field) if each is not None]
         total_shape = (2, 2, tall, wide)
         left_shape = (len(slots), 2 * tall, depth)
-        block = pl.BlockSpec(memory_space=pltpu.VMEM)
-        out_shape = [jax.ShapeDtypeStruct(total_shape, jnp.float32)]
-        scratch = [] if given or keep else [pltpu.VMEM(left_shape, jnp.bfloat16)]
-        out_specs = [block]
+        field_shape = (share, per_block, 4 * per_block)
+        block, apart = (pl.BlockSpec(memory_space=space) for space in (pltpu.VMEM, pltpu.HBM))
+        in_specs, outs, scratch, aliases = [block] * len(operands), [], [], {}
         if last:
-            out_shape = [jax.ShapeDtypeStruct((share, per_block, 4 * per_block), jnp.float32)]
-            out_specs = [pl.BlockSpec(memory_space=pl.ANY)]
-            scratch = [
-                pltpu.VMEM(total_shape[1:], jnp.float32),
-                pltpu.VMEM(out_shape[0].shape, jnp.float32),
-                pltpu.SemaphoreType.DMA((spins * columns // 2,)),
-            ]
+            in_specs[-1] = apart
+            aliases = {len(operands) - 1: 0}
+            scratch.append(pltpu.VMEM(total_shape[2:], jnp.float32))
+        else:
+            outs.append((total_shape, jnp.float32, block))
+        if half or last:
+            outs.append((field_shape, jnp.float32, apart))
+            scratch.append(pltpu.VMEM((*field_shape[:2], 2 * per_block), jnp.float32))
+            scratch.append(pltpu.SemaphoreType.DMA((spins * columns // 2,)))
         if keep:
-            out_shape.append(jax.ShapeDtypeStruct(left_shape, jnp.bfloat16))
-            out_specs.append(block)
+            outs.append((left_shape, jnp.bfloat16, block))
+        elif not given:
+            scratch.append(pltpu.VMEM(left_shape, jnp.bfloat16))
         out = pl.pallas_call(
             functools.partial(
-                add_shards, tuple(names), places, slots, totals is not None, given, last, share
+                add_shards, tuple(names), places, slots, totals is not None, given, half, last, share
             ),
-            in_specs=[block] * len(operands),
-            out_specs=out_specs,
-            out_shape=out_shape,
+            in_specs=in_specs,
+            out_specs=[spec for _, _, spec in outs],
+            out_shape=[jax.ShapeDtypeStruct(shape, dtype) for shape, dtype, _ in outs],
             scratch_shapes=scratch,
+            input_output_aliases=aliases,
             compiler_params=pltpu.CompilerParams(vmem_limit_bytes=40 * 1024 * 1024),
             cost_estimate=pl.CostEstimate(
                 flops=4 * tall * wide * depth * len(names) * weight,
@@ -254,7 +276,7 @@
                 transcendentals=0,
             ),
         )(*operands)
-        return (out[0], (slots, out[1])) if keep else out[0]
+        return (*out[:-1], (slots, out[-1])) if keep else out[0]
 
     def fence(totals):
         nonlocal arrays
@@ -316,20 +338,19 @@
     far3 = swap(stack)
     put("3d", far2, "far", second)
     names = [("far", *kind) for kind in second] + [("near", *kind) for kind in third]
-    totals = add(names, totals)
+    totals = add(names, totals, weight=10)
     put("3b", ab3, "near", fourth[:1])
     put("3c", ab1, "near", fourth[1:])
     totals = fence(totals)
 
     far4 = [swap(near(*kind)) for kind in fourth]
-    names = [("far", *kind) for kind in third + fourth]
-    slots = left_slots(names)
-    totals, (slots, left) = add([("near", *kind) for kind in fourth], totals, keep=slots)
     put("4a", far3, "far", third)
+    names = [("far", *kind) for kind in third] + [("near", *kind) for kind in fourth]
+    totals, field, (slots, left) = add(names, totals, keep=left_slots(names), half=True)
     put("4b", far4[0], "far", fourth[:1])
     put("4c", far4[1], "far", fourth[1:])
-    totals, left = fence((totals, left))
-    return add(names, totals, left=(slots, left), last=True)
+    totals, left, field = fence((totals, left, field))
+    return add([("far", *kind) for kind in fourth], totals, left=(slots, left), field=field)
 
 
 def add_terms(place_ref, weights_ref, left_ref, right_ref, field_ref):

time: 62.9 us -> 62.6 us (level)
    ppermute x19, waiting for transfers between devices: 27 us -> 26.4 us  [move(): return lax.ppermute(array, AXES, pairs)]
  transfers between devices with their start and end apart: 19 -> 19, of which waited for: 11 -> 7; matrix products, arithmetic and copies ran while one was open for 0% -> 0% of each run, Pallas kernels for 14% -> 16%
where the time goes in v18:
time: 62.6 us; the launch traced here: 62.5 us
  waiting for transfers between devices  26.4 us (42%)
  starting transfers between devices  22.6 us (36%)
  Pallas kernels  12 us (19%)
  local copies, waits for them, and re-layouts  1 us (2%)
    ppermute x19, waiting for transfers between devices, move(): return lax.ppermute(array, AXES, pairs)  26.4 us
    ppermute x19, starting transfers between devices, move(): return lax.ppermute(array, AXES, pairs)  22.6 us
    pallas_call x7, Pallas kernels, add(): pl.pallas_call(functools.partial(add_shards, tuple(names), places, slots,...  11.6 us
  transfers between devices with their start and end apart: 19, of which 7 were waited for; matrix products, arithmetic and copies ran while one was open for 0% of the time, Pallas kernels for 16%

profile of v18, /device:TPU:0, one launch (start us, length us, event | category | flops | bytes accessed | tf_op | source)
XLA Modules:
  0.0 62.5 jit_solution(16985172460702737980)
XLA Ops:
  0.0 0.0 copy-start
  0.0 2.9 %collective-permute-start.1 = (bf16[2,12,64,128]{3,2,1,0:T(8,128)(2,1)}, bf16[2,12,64,128]{3,2,1,0:T(8,128)(2,1)S(1)}, u32[]{:S(2)}, u32[]{:S(2)}) collective-permute-start(bf16[2,12,64,128]{3,2,1,0:T(8,128)(2,1)} %bitcast.24), channel_id=1, source_target_pairs={{0,16},{1,17},{2,18},{3,19},{4,20},{5,21},{6,22},{7,23},{8,9},{9,8... | collective-permute-start | bytes 1179656 | tf_op jit(solution)/shard_map/ppermute | solution.py:208
  2.9 2.6 %collective-permute-start = (bf16[2,12,64,128]{3,2,1,0:T(8,128)(2,1)}, bf16[2,12,64,128]{3,2,1,0:T(8,128)(2,1)S(1)}, u32[]{:S(2)}, u32[]{:S(2)}) collective-permute-start(bf16[2,12,64,128]{3,2,1,0:T(8,128)(2,1)} %bitcast.25), channel_id=1, source_target_pairs={{0,4},{1,5},{2,6},{3,7},{4,0},{5,1},{6,2},{7,3},{8,12},{9,13},{10,... | collective-permute-start | bytes 1179656 | tf_op jit(solution)/shard_map/ppermute | solution.py:208
  5.5 1.6 %collective-permute-start.2 = (bf16[2,12,64,128]{3,2,1,0:T(8,128)(2,1)}, bf16[2,12,64,128]{3,2,1,0:T(8,128)(2,1)S(1)}, u32[]{:S(2)}, u32[]{:S(2)}) collective-permute-start(bf16[2,12,64,128]{3,2,1,0:T(8,128)(2,1)} %bitcast.26), channel_id=1, source_target_pairs={{0,2},{1,3},{2,0},{3,1},{4,6},{5,7},{6,4},{7,5},{8,10},{9,11},{10,... | collective-permute-start | bytes 1179656 | tf_op jit(solution)/shard_map/ppermute | solution.py:208
  7.1 1.5 %collective-permute-start.3 = (bf16[2,12,64,128]{3,2,1,0:T(8,128)(2,1)}, bf16[2,12,64,128]{3,2,1,0:T(8,128)(2,1)S(1)}, u32[]{:S(2)}, u32[]{:S(2)}) collective-permute-start(bf16[2,12,64,128]{3,2,1,0:T(8,128)(2,1)} %bitcast.27), channel_id=1, source_target_pairs={{0,1},{1,0},{2,3},{3,2},{4,5},{5,4},{6,7},{7,6},{8,24},{9,25},{10,... | collective-permute-start | bytes 1179656 | tf_op jit(solution)/shard_map/ppermute | solution.py:208
  8.6 0.0 collective-permute-start.5
  8.6 0.0 copy-done
  8.7 0.1 fusion
  8.8 0.2 collective-permute-done.1.refs_0_.refs_1_
  9.0 3.4 %collective-permute-start.4 = (bf16[2,12,64,128]{3,2,1,0:T(8,128)(2,1)S(1)}, bf16[2,12,64,128]{3,2,1,0:T(8,128)(2,1)S(1)}, u32[]{:S(2)}, u32[]{:S(2)}) collective-permute-start(bf16[2,12,64,128]{3,2,1,0:T(8,128)(2,1)S(1)} %collective-permute-done.1.refs_0_.refs_1_), channel_id=1, source_target_pairs={{0,1},{1,0},{2,3},{3,2},{4,5},{5,4},{6,7},{7,6},{8,24},{9,25},{10,... | collective-permute-start | bytes 1179656 | tf_op jit(solution)/shard_map/ppermute | solution.py:208
  12.4 0.1 multiply_cosine_fusion
  12.6 10.6 %collective-permute-done.refs_4_.refs_0_ = bf16[2,12,64,128]{3,2,1,0:T(8,128)(2,1)S(1)} collective-permute-done((bf16[2,12,64,128]{3,2,1,0:T(8,128)(2,1)}, bf16[2,12,64,128]{3,2,1,0:T(8,128)(2,1)S(1)}, u32[]{:S(2)}, u32[]{:S(2)}) %collective-permute-start) | collective-permute-done | bytes 393248 | tf_op jit(solution)/shard_map/ppermute | solution.py:208
  23.2 0.2 collective-permute-done.2.refs_3_.refs_2_.refs_1_
  23.4 0.0 collective-permute-done.3.refs_1_.refs_3_
  23.4 0.0 collective-permute-done.5.refs_4_
  23.4 0.0 collective-permute-done.4.refs_2_.refs_4_
  23.4 0.2 shard_map.28
  23.6 0.1 collective-permute-start.6
  23.7 1.5 %collective-permute-start.7 = (bf16[2,12,64,128]{3,2,1,0:T(8,128)(2,1)S(1)}, bf16[2,12,64,128]{3,2,1,0:T(8,128)(2,1)S(1)}, u32[]{:S(2)}, u32[]{:S(2)}) collective-permute-start(bf16[2,12,64,128]{3,2,1,0:T(8,128)(2,1)S(1)} %collective-permute-done.refs_4_.refs_0_), channel_id=1, source_target_pairs={{0,2},{1,3},{2,0},{3,1},{4,6},{5,7},{6,4},{7,5},{8,10},{9,11},{10,... | collective-permute-start | bytes 1179656 | tf_op jit(solution)/shard_map/ppermute | solution.py:208
  25.2 0.5 collective-permute-start.10
  25.7 1.5 %collective-permute-start.9 = (bf16[2,2,12,64,128]{4,3,2,1,0:T(8,128)(2,1)S(1)}, bf16[2,2,12,64,128]{4,3,2,1,0:T(8,128)(2,1)S(1)}, u32[]{:S(2)}, u32[]{:S(2)}) collective-permute-start(bf16[2,2,12,64,128]{4,3,2,1,0:T(8,128)(2,1)S(1)} %get-tuple-element.106), channel_id=1, source_target_pairs={{0,16},{1,17},{2,18},{3,19},{4,20},{5,21},{6,22},{7,23},{8,9},{9,8... | collective-permute-start | bytes 2359304 | tf_op jit(solution)/shard_map/ppermute | solution.py:208
  27.2 2.3 %collective-permute-start.8 = (bf16[2,12,64,128]{3,2,1,0:T(8,128)(2,1)S(1)}, bf16[2,12,64,128]{3,2,1,0:T(8,128)(2,1)S(1)}, u32[]{:S(2)}, u32[]{:S(2)}) collective-permute-start(bf16[2,12,64,128]{3,2,1,0:T(8,128)(2,1)S(1)} %collective-permute-done.4.refs_2_.refs_4_), channel_id=1, source_target_pairs={{0,4},{1,5},{2,6},{3,7},{4,0},{5,1},{6,2},{7,3},{8,12},{9,13},{10,... | collective-permute-start | bytes 1179656 | tf_op jit(solution)/shard_map/ppermute | solution.py:208
  29.5 0.0 copy-start.1
  29.5 1.0 %copy-done.1 = bf16[2,1,64,12,128]{4,2,3,1,0:T(8,128)(2,1)S(1)} copy-done((bf16[2,1,64,12,128]{4,2,3,1,0:T(8,128)(2,1)S(1)}, bf16[2,1,64,12,128]{4,2,3,1,0:T(8,128)(2,1)}, u32[]{:S(2)}) %copy-start.1) | copy-done | bytes 393240
  30.5 1.8 %shard_map.29.refs_7_ = f32[2,2,256,256]{3,2,1,0:T(8,128)S(1)} custom-call(f32[8,2,128]{2,1,0:T(2,128)S(1)} %maximum_bitcast_fusion.weights_ref, bf16[2,12,64,128]{3,2,1,0:T(8,128)(2,1)S(1)} %collective-permute-done.refs_4_.refs_0_, bf16[2,12,64,128]{3,2,1,0:T(8,128)(2,1)S(1)} %collective-permute-done.1.refs_0_.refs_1_, ...), custom_call_target="tpu_custom_call" | custom-call | flops 1207959552 | bytes 4456448 | tf_op jit(solution)/shard_map/pallas_call | solution.py:263
  32.3 0.0 collective-permute-done.6.refs_5_
  32.3 1.7 %shard_map.30.refs_1_ = f32[2,2,256,256]{3,2,1,0:T(8,128)S(1)} custom-call(f32[8,2,128]{2,1,0:T(2,128)S(1)} %maximum_bitcast_fusion.weights_ref, bf16[2,12,64,128]{3,2,1,0:T(8,128)(2,1)S(1)} %collective-permute-done.refs_4_.refs_0_, bf16[2,12,64,128]{3,2,1,0:T(8,128)(2,1)S(1)} %collective-permute-done.1.refs_0_.refs_1_, ...), custom_call_target="tpu_custom_call" | custom-call | flops 1207959552 | bytes 4456448 | tf_op jit(solution)/shard_map/pallas_call | solution.py:263
  34.0 7.6 %collective-permute-done.7.refs_0_.o3_ref.refs_2_ = bf16[2,12,64,128]{3,2,1,0:T(8,128)(2,1)S(1)} collective-permute-done((bf16[2,12,64,128]{3,2,1,0:T(8,128)(2,1)S(1)}, bf16[2,12,64,128]{3,2,1,0:T(8,128)(2,1)S(1)}, u32[]{:S(2)}, u32[]{:S(2)}) %collective-permute-start.7) | collective-permute-done | bytes 393248 | tf_op jit(solution)/shard_map/ppermute | solution.py:208
  41.6 2.4 %collective-permute-start.11 = (bf16[2,12,64,128]{3,2,1,0:T(8,128)(2,1)S(1)}, bf16[2,12,64,128]{3,2,1,0:T(8,128)(2,1)S(1)}, u32[]{:S(2)}, u32[]{:S(2)}) collective-permute-start(bf16[2,12,64,128]{3,2,1,0:T(8,128)(2,1)S(1)} %collective-permute-done.7.refs_0_.o3_ref.refs_2_), channel_id=1, source_target_pairs={{0,16},{1,17},{2,18},{3,19},{4,20},{5,21},{6,22},{7,23},{8,9},{9,8... | collective-permute-start | bytes 1179656 | tf_op jit(solution)/shard_map/ppermute | solution.py:208
  44.1 0.0 collective-permute-start.12
  44.1 0.4 shard_map.31.refs_5_
  44.5 2.7 %collective-permute-done.8.ab2_ref.refs_2_ = bf16[2,12,64,128]{3,2,1,0:T(8,128)(2,1)S(1)} collective-permute-done((bf16[2,12,64,128]{3,2,1,0:T(8,128)(2,1)S(1)}, bf16[2,12,64,128]{3,2,1,0:T(8,128)(2,1)S(1)}, u32[]{:S(2)}, u32[]{:S(2)}) %collective-permute-start.8) | collective-permute-done | bytes 393248 | tf_op jit(solution)/shard_map/ppermute | solution.py:208
  47.2 0.0 collective-permute-done.10.b12_ref.refs_4_.refs_2_
  47.2 0.0 collective-permute-done.9.a12_ref.refs_3_.refs_1_
  47.2 0.0 collective-permute-start.13
  47.2 0.2 shard_map.32
  47.4 0.1 collective-permute-start.15
  47.4 1.6 %collective-permute-start.14 = (bf16[2,12,64,128]{3,2,1,0:T(8,128)(2,1)S(1)}, bf16[2,12,64,128]{3,2,1,0:T(8,128)(2,1)S(1)}, u32[]{:S(2)}, u32[]{:S(2)}) collective-permute-start(bf16[2,12,64,128]{3,2,1,0:T(8,128)(2,1)S(1)} %get-tuple-element.131), channel_id=1, source_target_pairs={{0,1},{1,0},{2,3},{3,2},{4,5},{5,4},{6,7},{7,6},{8,24},{9,25},{10,... | collective-permute-start | bytes 1179656 | tf_op jit(solution)/shard_map/ppermute | solution.py:208
  49.0 1.6 %shard_map.33.refs_7_ = f32[2,2,256,256]{3,2,1,0:T(8,128)S(1)} custom-call(f32[8,2,128]{2,1,0:T(2,128)S(1)} %maximum_bitcast_fusion.weights_ref, bf16[2,12,64,128]{3,2,1,0:T(8,128)(2,1)S(1)} %collective-permute-done.refs_4_.refs_0_, bf16[2,12,64,128]{3,2,1,0:T(8,128)(2,1)S(1)} %collective-permute-done.2.refs_3_.refs_2_.refs_1_, ...), custom_call_target="tpu_custom_call" | custom-call | flops 1006632960 | bytes 4063232 | tf_op jit(solution)/shard_map/pallas_call | solution.py:263
  50.7 3.4 %collective-permute-done.11.a3_ref = bf16[2,12,64,128]{3,2,1,0:T(8,128)(2,1)S(1)} collective-permute-done((bf16[2,12,64,128]{3,2,1,0:T(8,128)(2,1)S(1)}, bf16[2,12,64,128]{3,2,1,0:T(8,128)(2,1)S(1)}, u32[]{:S(2)}, u32[]{:S(2)}) %collective-permute-start.11) | collective-permute-done | bytes 393248 | tf_op jit(solution)/shard_map/ppermute | solution.py:208
  54.0 0.0 collective-permute-done.12.ab3_ref
  54.0 0.1 shard_map.34.refs_5_.refs_3_
  54.1 0.1 collective-permute-start.16
  54.2 0.0 collective-permute-done.15.refs_6_
  54.2 2.3 %shard_map.35.refs_7_ = f32[2,2,256,256]{3,2,1,0:T(8,128)S(1)} custom-call(f32[8,2,128]{2,1,0:T(2,128)S(1)} %maximum_bitcast_fusion.weights_ref, bf16[2,12,64,128]{3,2,1,0:T(8,128)(2,1)S(1)} %collective-permute-done.refs_4_.refs_0_, bf16[2,12,64,128]{3,2,1,0:T(8,128)(2,1)S(1)} %collective-permute-done.2.refs_3_.refs_2_.refs_1_, ...), custom_call_target="tpu_custom_call" | custom-call | flops 16106127360 | bytes 5242880 | tf_op jit(solution)/shard_map/pallas_call | solution.py:263
  56.5 1.7 %collective-permute-done.14.refs_5_ = bf16[2,12,64,128]{3,2,1,0:T(8,128)(2,1)S(1)} collective-permute-done((bf16[2,12,64,128]{3,2,1,0:T(8,128)(2,1)S(1)}, bf16[2,12,64,128]{3,2,1,0:T(8,128)(2,1)S(1)}, u32[]{:S(2)}, u32[]{:S(2)}) %collective-permute-start.14) | collective-permute-done | bytes 393248 | tf_op jit(solution)/shard_map/ppermute | solution.py:208
  58.2 0.0 collective-permute-done.13.refs_4_
  58.2 0.0 collective-permute-start.17
  58.2 0.5 collective-permute-start.18
  58.7 0.0 collective-permute-done.16.refs_6_
  58.7 2.2 %shard_map.36 = (f32[2,2,256,256]{3,2,1,0:T(8,128)S(1)}, f32[16,64,256]{2,1,0:T(8,128)}, bf16[3,512,768]{2,1,0:T(8,128)(2,1)S(1)}) custom-call(f32[8,2,128]{2,1,0:T(2,128)S(1)} %maximum_bitcast_fusion.weights_ref, bf16[2,12,64,128]{3,2,1,0:T(8,128)(2,1)S(1)} %collective-permute-done.7.refs_0_.o3_ref.refs_2_, ...), custom_call_target="tpu_custom_call" | custom-call | flops 805306368 | bytes 3670016 | tf_op jit(solution)/shard_map/pallas_call | solution.py:263
  60.9 0.0 collective-permute-done.17.refs_0_
  60.9 0.0 collective-permute-done.18.refs_1_
  60.9 1.5 %shard_map.37 = f32[16,64,256]{2,1,0:T(8,128)} custom-call(f32[8,2,128]{2,1,0:T(2,128)S(1)} %maximum_bitcast_fusion.weights_ref, bf16[2,12,64,128]{3,2,1,0:T(8,128)(2,1)S(1)} %collective-permute-done.17.refs_0_, bf16[2,12,64,128]{3,2,1,0:T(8,128)(2,1)S(1)} %collective-permute-done.18.refs_1_, ...), custom_call_target="tpu_custom_call", output_to_operand_aliasing={{}: (5, {})} | custom-call | flops 402653184 | bytes 2883584 | tf_op jit(solution)/shard_map/pallas_call | solution.py:263
  (5 shorter events, 0.1 us)
Async XLA Ops:
  0.0 8.6 %copy-start = (s32[4,3]{1,0:T(4,128)S(1)}, s32[4,3]{1,0:T(4,128)}, u32[]{:S(2)}) copy-start(s32[4,3]{1,0:T(4,128)} %param.3) | copy-start | bytes 148
  0.0 9.0 %collective-permute-start.1 = (bf16[2,12,64,128]{3,2,1,0:T(8,128)(2,1)}, bf16[2,12,64,128]{3,2,1,0:T(8,128)(2,1)S(1)}, u32[]{:S(2)}, u32[]{:S(2)}) collective-permute-start(bf16[2,12,64,128]{3,2,1,0:T(8,128)(2,1)} %bitcast.24), channel_id=1, source_target_pairs={{0,16},{1,17},{2,18},{3,19},{4,20},{5,21},{6,22},{7,23},{8,9},{9,8... | collective-permute-start | bytes 1179656 | tf_op jit(solution)/shard_map/ppermute | solution.py:208
  2.9 20.3 %collective-permute-start = (bf16[2,12,64,128]{3,2,1,0:T(8,128)(2,1)}, bf16[2,12,64,128]{3,2,1,0:T(8,128)(2,1)S(1)}, u32[]{:S(2)}, u32[]{:S(2)}) collective-permute-start(bf16[2,12,64,128]{3,2,1,0:T(8,128)(2,1)} %bitcast.25), channel_id=1, source_target_pairs={{0,4},{1,5},{2,6},{3,7},{4,0},{5,1},{6,2},{7,3},{8,12},{9,13},{10,... | collective-permute-start | bytes 1179656 | tf_op jit(solution)/shard_map/ppermute | solution.py:208
  5.5 17.8 %collective-permute-start.2 = (bf16[2,12,64,128]{3,2,1,0:T(8,128)(2,1)}, bf16[2,12,64,128]{3,2,1,0:T(8,128)(2,1)S(1)}, u32[]{:S(2)}, u32[]{:S(2)}) collective-permute-start(bf16[2,12,64,128]{3,2,1,0:T(8,128)(2,1)} %bitcast.26), channel_id=1, source_target_pairs={{0,2},{1,3},{2,0},{3,1},{4,6},{5,7},{6,4},{7,5},{8,10},{9,11},{10,... | collective-permute-start | bytes 1179656 | tf_op jit(solution)/shard_map/ppermute | solution.py:208
  7.1 16.3 %collective-permute-start.3 = (bf16[2,12,64,128]{3,2,1,0:T(8,128)(2,1)}, bf16[2,12,64,128]{3,2,1,0:T(8,128)(2,1)S(1)}, u32[]{:S(2)}, u32[]{:S(2)}) collective-permute-start(bf16[2,12,64,128]{3,2,1,0:T(8,128)(2,1)} %bitcast.27), channel_id=1, source_target_pairs={{0,1},{1,0},{2,3},{3,2},{4,5},{5,4},{6,7},{7,6},{8,24},{9,25},{10,... | collective-permute-start | bytes 1179656 | tf_op jit(solution)/shard_map/ppermute | solution.py:208
  8.6 14.8 %collective-permute-start.5 = (bf16[2,12,64,128]{3,2,1,0:T(8,128)(2,1)}, bf16[2,12,64,128]{3,2,1,0:T(8,128)(2,1)S(1)}, u32[]{:S(2)}, u32[]{:S(2)}) collective-permute-start(bf16[2,12,64,128]{3,2,1,0:T(8,128)(2,1)} %bitcast.28), channel_id=1, source_target_pairs={{0,8},{1,9},{2,10},{3,11},{4,12},{5,13},{6,14},{7,15},{8,0},{9,1},... | collective-permute-start | bytes 1179656 | tf_op jit(solution)/shard_map/ppermute | solution.py:208
  9.0 14.4 %collective-permute-start.4 = (bf16[2,12,64,128]{3,2,1,0:T(8,128)(2,1)S(1)}, bf16[2,12,64,128]{3,2,1,0:T(8,128)(2,1)S(1)}, u32[]{:S(2)}, u32[]{:S(2)}) collective-permute-start(bf16[2,12,64,128]{3,2,1,0:T(8,128)(2,1)S(1)} %collective-permute-done.1.refs_0_.refs_1_), channel_id=1, source_target_pairs={{0,1},{1,0},{2,3},{3,2},{4,5},{5,4},{6,7},{7,6},{8,24},{9,25},{10,... | collective-permute-start | bytes 1179656 | tf_op jit(solution)/shard_map/ppermute | solution.py:208
  23.6 8.7 %collective-permute-start.6 = (bf16[5,2,12,64,128]{4,3,2,1,0:T(8,128)(2,1)S(1)}, bf16[5,2,12,64,128]{4,3,2,1,0:T(8,128)(2,1)S(1)}, u32[]{:S(2)}, u32[]{:S(2)}) collective-permute-start(bf16[5,2,12,64,128]{4,3,2,1,0:T(8,128)(2,1)S(1)} %get-tuple-element.93), channel_id=1, source_target_pairs={{0,8},{1,9},{2,10},{3,11},{4,12},{5,13},{6,14},{7,15},{8,0},{9,1},... | collective-permute-start | bytes 5898248 | tf_op jit(solution)/shard_map/ppermute | solution.py:208
  23.7 18.0 %collective-permute-start.7 = (bf16[2,12,64,128]{3,2,1,0:T(8,128)(2,1)S(1)}, bf16[2,12,64,128]{3,2,1,0:T(8,128)(2,1)S(1)}, u32[]{:S(2)}, u32[]{:S(2)}) collective-permute-start(bf16[2,12,64,128]{3,2,1,0:T(8,128)(2,1)S(1)} %collective-permute-done.refs_4_.refs_0_), channel_id=1, source_target_pairs={{0,2},{1,3},{2,0},{3,1},{4,6},{5,7},{6,4},{7,5},{8,10},{9,11},{10,... | collective-permute-start | bytes 1179656 | tf_op jit(solution)/shard_map/ppermute | solution.py:208
  25.2 22.0 %collective-permute-start.10 = (bf16[2,2,12,64,128]{4,3,2,1,0:T(8,128)(2,1)S(1)}, bf16[2,2,12,64,128]{4,3,2,1,0:T(8,128)(2,1)S(1)}, u32[]{:S(2)}, u32[]{:S(2)}) collective-permute-start(bf16[2,2,12,64,128]{4,3,2,1,0:T(8,128)(2,1)S(1)} %get-tuple-element.106), channel_id=1, source_target_pairs={{0,1},{1,0},{2,3},{3,2},{4,5},{5,4},{6,7},{7,6},{8,24},{9,25},{10,... | collective-permute-start | bytes 2359304 | tf_op jit(solution)/shard_map/ppermute | solution.py:208
  25.7 21.5 %collective-permute-start.9 = (bf16[2,2,12,64,128]{4,3,2,1,0:T(8,128)(2,1)S(1)}, bf16[2,2,12,64,128]{4,3,2,1,0:T(8,128)(2,1)S(1)}, u32[]{:S(2)}, u32[]{:S(2)}) collective-permute-start(bf16[2,2,12,64,128]{4,3,2,1,0:T(8,128)(2,1)S(1)} %get-tuple-element.106), channel_id=1, source_target_pairs={{0,16},{1,17},{2,18},{3,19},{4,20},{5,21},{6,22},{7,23},{8,9},{9,8... | collective-permute-start | bytes 2359304 | tf_op jit(solution)/shard_map/ppermute | solution.py:208
  27.2 20.0 %collective-permute-start.8 = (bf16[2,12,64,128]{3,2,1,0:T(8,128)(2,1)S(1)}, bf16[2,12,64,128]{3,2,1,0:T(8,128)(2,1)S(1)}, u32[]{:S(2)}, u32[]{:S(2)}) collective-permute-start(bf16[2,12,64,128]{3,2,1,0:T(8,128)(2,1)S(1)} %collective-permute-done.4.refs_2_.refs_4_), channel_id=1, source_target_pairs={{0,4},{1,5},{2,6},{3,7},{4,0},{5,1},{6,2},{7,3},{8,12},{9,13},{10,... | collective-permute-start | bytes 1179656 | tf_op jit(solution)/shard_map/ppermute | solution.py:208
  29.5 1.0 %copy-start.1 = (bf16[2,1,64,12,128]{4,2,3,1,0:T(8,128)(2,1)S(1)}, bf16[2,1,64,12,128]{4,2,3,1,0:T(8,128)(2,1)}, u32[]{:S(2)}) copy-start(bf16[2,1,64,12,128]{4,2,3,1,0:T(8,128)(2,1)} %param.2) | copy-start | bytes 1179652
  41.6 12.4 %collective-permute-start.11 = (bf16[2,12,64,128]{3,2,1,0:T(8,128)(2,1)S(1)}, bf16[2,12,64,128]{3,2,1,0:T(8,128)(2,1)S(1)}, u32[]{:S(2)}, u32[]{:S(2)}) collective-permute-start(bf16[2,12,64,128]{3,2,1,0:T(8,128)(2,1)S(1)} %collective-permute-done.7.refs_0_.o3_ref.refs_2_), channel_id=1, source_target_pairs={{0,16},{1,17},{2,18},{3,19},{4,20},{5,21},{6,22},{7,23},{8,9},{9,8... | collective-permute-start | bytes 1179656 | tf_op jit(solution)/shard_map/ppermute | solution.py:208
  44.1 10.0 %collective-permute-start.12 = (bf16[2,12,64,128]{3,2,1,0:T(8,128)(2,1)S(1)}, bf16[2,12,64,128]{3,2,1,0:T(8,128)(2,1)S(1)}, u32[]{:S(2)}, u32[]{:S(2)}) collective-permute-start(bf16[2,12,64,128]{3,2,1,0:T(8,128)(2,1)S(1)} %collective-permute-done.7.refs_0_.o3_ref.refs_2_), channel_id=1, source_target_pairs={{0,1},{1,0},{2,3},{3,2},{4,5},{5,4},{6,7},{7,6},{8,24},{9,25},{10,... | collective-permute-start | bytes 1179656 | tf_op jit(solution)/shard_map/ppermute | solution.py:208
  47.2 11.1 %collective-permute-start.13 = (bf16[2,12,64,128]{3,2,1,0:T(8,128)(2,1)S(1)}, bf16[2,12,64,128]{3,2,1,0:T(8,128)(2,1)S(1)}, u32[]{:S(2)}, u32[]{:S(2)}) collective-permute-start(bf16[2,12,64,128]{3,2,1,0:T(8,128)(2,1)S(1)} %collective-permute-done.8.ab2_ref.refs_2_), channel_id=1, source_target_pairs={{0,2},{1,3},{2,0},{3,1},{4,6},{5,7},{6,4},{7,5},{8,10},{9,11},{10,... | collective-permute-start | bytes 1179656 | tf_op jit(solution)/shard_map/ppermute | solution.py:208
  47.4 6.8 %collective-permute-start.15 = (bf16[6,2,12,64,128]{4,3,2,1,0:T(8,128)(2,1)S(1)}, bf16[6,2,12,64,128]{4,3,2,1,0:T(8,128)(2,1)S(1)}, u32[]{:S(2)}, u32[]{:S(2)}) collective-permute-start(bf16[6,2,12,64,128]{4,3,2,1,0:T(8,128)(2,1)S(1)} %get-tuple-element.132), channel_id=1, source_target_pairs={{0,8},{1,9},{2,10},{3,11},{4,12},{5,13},{6,14},{7,15},{8,0},{9,1},... | collective-permute-start | bytes 7077896 | tf_op jit(solution)/shard_map/ppermute | solution.py:208
  47.4 10.8 %collective-permute-start.14 = (bf16[2,12,64,128]{3,2,1,0:T(8,128)(2,1)S(1)}, bf16[2,12,64,128]{3,2,1,0:T(8,128)(2,1)S(1)}, u32[]{:S(2)}, u32[]{:S(2)}) collective-permute-start(bf16[2,12,64,128]{3,2,1,0:T(8,128)(2,1)S(1)} %get-tuple-element.131), channel_id=1, source_target_pairs={{0,1},{1,0},{2,3},{3,2},{4,5},{5,4},{6,7},{7,6},{8,24},{9,25},{10,... | collective-permute-start | bytes 1179656 | tf_op jit(solution)/shard_map/ppermute | solution.py:208
  54.1 4.7 %collective-permute-start.16 = (bf16[2,2,12,64,128]{4,3,2,1,0:T(8,128)(2,1)S(1)}, bf16[2,2,12,64,128]{4,3,2,1,0:T(8,128)(2,1)S(1)}, u32[]{:S(2)}, u32[]{:S(2)}) collective-permute-start(bf16[2,2,12,64,128]{4,3,2,1,0:T(8,128)(2,1)S(1)} %shard_map.34.refs_5_.refs_3_), channel_id=1, source_target_pairs={{0,8},{1,9},{2,10},{3,11},{4,12},{5,13},{6,14},{7,15},{8,0},{9,1},... | collective-permute-start | bytes 2359304 | tf_op jit(solution)/shard_map/ppermute | solution.py:208
  58.2 2.7 %collective-permute-start.17 = (bf16[2,12,64,128]{3,2,1,0:T(8,128)(2,1)S(1)}, bf16[2,12,64,128]{3,2,1,0:T(8,128)(2,1)S(1)}, u32[]{:S(2)}, u32[]{:S(2)}) collective-permute-start(bf16[2,12,64,128]{3,2,1,0:T(8,128)(2,1)S(1)} %collective-permute-done.13.refs_4_), channel_id=1, source_target_pairs={{0,8},{1,9},{2,10},{3,11},{4,12},{5,13},{6,14},{7,15},{8,0},{9,1},... | collective-permute-start | bytes 1179656 | tf_op jit(solution)/shard_map/ppermute | solution.py:208
  58.2 2.7 %collective-permute-start.18 = (bf16[2,12,64,128]{3,2,1,0:T(8,128)(2,1)S(1)}, bf16[2,12,64,128]{3,2,1,0:T(8,128)(2,1)S(1)}, u32[]{:S(2)}, u32[]{:S(2)}) collective-permute-start(bf16[2,12,64,128]{3,2,1,0:T(8,128)(2,1)S(1)} %collective-permute-done.14.refs_5_), channel_id=1, source_target_pairs={{0,8},{1,9},{2,10},{3,11},{4,12},{5,13},{6,14},{7,15},{8,0},{9,1},... | collective-permute-start | bytes 1179656 | tf_op jit(solution)/shard_map/ppermute | solution.py:208

commit v19 on v18

--- a/solution.py
+++ b/solution.py
@@ -52,8 +52,7 @@
     refs = list(refs)
     left_ref = None if given else refs.pop()
     if half:
-        sems, row_ref, left_ref = left_ref, refs.pop(), refs.pop()
-        field_ref = refs.pop()
+        sems, row_ref, field_ref = (refs.pop() for _ in range(3))
     if last:
         sems, row_ref, far_ref, field_ref, _ = (refs.pop() for _ in range(5))
     else:
@@ -276,7 +275,9 @@
                 transcendentals=0,
             ),
         )(*operands)
-        return (*out[:-1], (slots, out[-1])) if keep else out[0]
+        if keep:
+            return out[0], (slots, out[1])
+        return out if half else out[0]
 
     def fence(totals):
         nonlocal arrays
@@ -339,14 +340,16 @@
     put("3d", far2, "far", second)
     names = [("far", *kind) for kind in second] + [("near", *kind) for kind in third]
     totals = add(names, totals, weight=10)
+    put("3e", far3, "far", third)
+    names = [("far", *kind) for kind in third]
+    totals, field = add(names, totals, half=True)
     put("3b", ab3, "near", fourth[:1])
     put("3c", ab1, "near", fourth[1:])
-    totals = fence(totals)
+    totals, field = fence((totals, field))
 
     far4 = [swap(near(*kind)) for kind in fourth]
-    put("4a", far3, "far", third)
-    names = [("far", *kind) for kind in third] + [("near", *kind) for kind in fourth]
-    totals, field, (slots, left) = add(names, totals, keep=left_slots(names), half=True)
+    names = [("near", *kind) for kind in fourth]
+    totals, (slots, left) = add(names, totals, keep=left_slots(names))
     put("4b", far4[0], "far", fourth[:1])
     put("4c", far4[1], "far", fourth[1:])
     totals, left, field = fence((totals, left, field))

time: 62.6 us -> 63.2 us (level)
  local copies, waits for them, and re-layouts: 1 us -> 0.01 us
  waiting for transfers between devices: 26.4 us -> 27.3 us
    unnamed x4, local copies, waits for them, and re-layouts: 1 us -> 0.01 us
    ppermute x19, waiting for transfers between devices: 26.4 us -> 27.3 us  [move(): return lax.ppermute(array, AXES, pairs)]
    pallas_call x7 -> x8, Pallas kernels: 11.6 us -> 11.9 us  [add(): pl.pallas_call(functools.partial(add_shards, tuple(names), places, slots,...]
  transfers between devices with their start and end apart: 19 -> 19, of which waited for: 7 -> 9; matrix products, arithmetic and copies ran while one was open for 0% -> 0% of each run, Pallas kernels for 16% -> 17%
where the time goes in v19:
time: 63.2 us; the launch traced here: 63.1 us
  waiting for transfers between devices  27.3 us (43%)
  starting transfers between devices  23.1 us (37%)
  Pallas kernels  12.3 us (19%)
    ppermute x19, waiting for transfers between devices, move(): return lax.ppermute(array, AXES, pairs)  27.3 us
    ppermute x19, starting transfers between devices, move(): return lax.ppermute(array, AXES, pairs)  23.1 us
    pallas_call x8, Pallas kernels, add(): pl.pallas_call(functools.partial(add_shards, tuple(names), places, slots,...  11.9 us
  transfers between devices with their start and end apart: 19, of which 9 were waited for; matrix products, arithmetic and copies ran while one was open for 0% of the time, Pallas kernels for 17%

profile of v19, /device:TPU:0, one launch (start us, length us, event | category | flops | bytes accessed | tf_op | source)
XLA Modules:
  0.0 63.1 jit_solution(18445693941966455339)
XLA Ops:
  0.0 0.0 copy-start
  0.0 0.0 copy-start.1
  0.0 4.0 %collective-permute-start = (bf16[2,12,64,128]{3,2,1,0:T(8,128)(2,1)}, bf16[2,12,64,128]{3,2,1,0:T(8,128)(2,1)S(1)}, u32[]{:S(2)}, u32[]{:S(2)}) collective-permute-start(bf16[2,12,64,128]{3,2,1,0:T(8,128)(2,1)} %bitcast.24), channel_id=1, source_target_pairs={{0,4},{1,5},{2,6},{3,7},{4,0},{5,1},{6,2},{7,3},{8,12},{9,13},{10,... | collective-permute-start | bytes 1179656 | tf_op jit(solution)/shard_map/ppermute | solution.py:207
  4.0 1.5 %collective-permute-start.1 = (bf16[2,12,64,128]{3,2,1,0:T(8,128)(2,1)}, bf16[2,12,64,128]{3,2,1,0:T(8,128)(2,1)S(1)}, u32[]{:S(2)}, u32[]{:S(2)}) collective-permute-start(bf16[2,12,64,128]{3,2,1,0:T(8,128)(2,1)} %bitcast.25), channel_id=1, source_target_pairs={{0,16},{1,17},{2,18},{3,19},{4,20},{5,21},{6,22},{7,23},{8,9},{9,8... | collective-permute-start | bytes 1179656 | tf_op jit(solution)/shard_map/ppermute | solution.py:207
  5.5 1.6 %collective-permute-start.2 = (bf16[2,12,64,128]{3,2,1,0:T(8,128)(2,1)}, bf16[2,12,64,128]{3,2,1,0:T(8,128)(2,1)S(1)}, u32[]{:S(2)}, u32[]{:S(2)}) collective-permute-start(bf16[2,12,64,128]{3,2,1,0:T(8,128)(2,1)} %bitcast.26), channel_id=1, source_target_pairs={{0,2},{1,3},{2,0},{3,1},{4,6},{5,7},{6,4},{7,5},{8,10},{9,11},{10,... | collective-permute-start | bytes 1179656 | tf_op jit(solution)/shard_map/ppermute | solution.py:207
  7.1 1.5 %collective-permute-start.3 = (bf16[2,12,64,128]{3,2,1,0:T(8,128)(2,1)}, bf16[2,12,64,128]{3,2,1,0:T(8,128)(2,1)S(1)}, u32[]{:S(2)}, u32[]{:S(2)}) collective-permute-start(bf16[2,12,64,128]{3,2,1,0:T(8,128)(2,1)} %bitcast.27), channel_id=1, source_target_pairs={{0,1},{1,0},{2,3},{3,2},{4,5},{5,4},{6,7},{7,6},{8,24},{9,25},{10,... | collective-permute-start | bytes 1179656 | tf_op jit(solution)/shard_map/ppermute | solution.py:207
  8.6 0.0 collective-permute-start.5
  8.6 0.0 copy-done
  8.7 0.1 fusion
  8.8 6.3 %collective-permute-done.1.refs_0_.refs_1_ = bf16[2,12,64,128]{3,2,1,0:T(8,128)(2,1)S(1)} collective-permute-done((bf16[2,12,64,128]{3,2,1,0:T(8,128)(2,1)}, bf16[2,12,64,128]{3,2,1,0:T(8,128)(2,1)S(1)}, u32[]{:S(2)}, u32[]{:S(2)}) %collective-permute-start.1) | collective-permute-done | bytes 393248 | tf_op jit(solution)/shard_map/ppermute | solution.py:207
  15.1 2.6 %collective-permute-start.4 = (bf16[2,12,64,128]{3,2,1,0:T(8,128)(2,1)S(1)}, bf16[2,12,64,128]{3,2,1,0:T(8,128)(2,1)S(1)}, u32[]{:S(2)}, u32[]{:S(2)}) collective-permute-start(bf16[2,12,64,128]{3,2,1,0:T(8,128)(2,1)S(1)} %collective-permute-done.1.refs_0_.refs_1_), channel_id=1, source_target_pairs={{0,1},{1,0},{2,3},{3,2},{4,5},{5,4},{6,7},{7,6},{8,24},{9,25},{10,... | collective-permute-start | bytes 1179656 | tf_op jit(solution)/shard_map/ppermute | solution.py:207
  17.7 0.1 multiply_cosine_fusion
  17.8 4.1 %collective-permute-done.refs_4_.refs_0_ = bf16[2,12,64,128]{3,2,1,0:T(8,128)(2,1)S(1)} collective-permute-done((bf16[2,12,64,128]{3,2,1,0:T(8,128)(2,1)}, bf16[2,12,64,128]{3,2,1,0:T(8,128)(2,1)S(1)}, u32[]{:S(2)}, u32[]{:S(2)}) %collective-permute-start) | collective-permute-done | bytes 393248 | tf_op jit(solution)/shard_map/ppermute | solution.py:207
  21.9 1.4 %collective-permute-done.2.refs_3_.refs_2_.refs_1_ = bf16[2,12,64,128]{3,2,1,0:T(8,128)(2,1)S(1)} collective-permute-done((bf16[2,12,64,128]{3,2,1,0:T(8,128)(2,1)}, bf16[2,12,64,128]{3,2,1,0:T(8,128)(2,1)S(1)}, u32[]{:S(2)}, u32[]{:S(2)}) %collective-permute-start.2) | collective-permute-done | bytes 393248 | tf_op jit(solution)/shard_map/ppermute | solution.py:207
  23.3 0.0 collective-permute-done.3.refs_1_.refs_3_
  23.3 0.0 collective-permute-done.5.refs_4_
  23.3 0.1 collective-permute-done.4.refs_2_.refs_4_
  23.4 0.2 shard_map.28
  23.6 0.1 collective-permute-start.6
  23.7 2.2 %collective-permute-start.7 = (bf16[2,12,64,128]{3,2,1,0:T(8,128)(2,1)S(1)}, bf16[2,12,64,128]{3,2,1,0:T(8,128)(2,1)S(1)}, u32[]{:S(2)}, u32[]{:S(2)}) collective-permute-start(bf16[2,12,64,128]{3,2,1,0:T(8,128)(2,1)S(1)} %collective-permute-done.refs_4_.refs_0_), channel_id=1, source_target_pairs={{0,2},{1,3},{2,0},{3,1},{4,6},{5,7},{6,4},{7,5},{8,10},{9,11},{10,... | collective-permute-start | bytes 1179656 | tf_op jit(solution)/shard_map/ppermute | solution.py:207
  25.9 1.5 %collective-permute-start.9 = (bf16[2,2,12,64,128]{4,3,2,1,0:T(8,128)(2,1)S(1)}, bf16[2,2,12,64,128]{4,3,2,1,0:T(8,128)(2,1)S(1)}, u32[]{:S(2)}, u32[]{:S(2)}) collective-permute-start(bf16[2,2,12,64,128]{4,3,2,1,0:T(8,128)(2,1)S(1)} %get-tuple-element.107), channel_id=1, source_target_pairs={{0,16},{1,17},{2,18},{3,19},{4,20},{5,21},{6,22},{7,23},{8,9},{9,8... | collective-permute-start | bytes 2359304 | tf_op jit(solution)/shard_map/ppermute | solution.py:207
  27.4 0.6 collective-permute-start.10
  28.0 1.3 %collective-permute-start.8 = (bf16[2,12,64,128]{3,2,1,0:T(8,128)(2,1)S(1)}, bf16[2,12,64,128]{3,2,1,0:T(8,128)(2,1)S(1)}, u32[]{:S(2)}, u32[]{:S(2)}) collective-permute-start(bf16[2,12,64,128]{3,2,1,0:T(8,128)(2,1)S(1)} %collective-permute-done.4.refs_2_.refs_4_), channel_id=1, source_target_pairs={{0,4},{1,5},{2,6},{3,7},{4,0},{5,1},{6,2},{7,3},{8,12},{9,13},{10,... | collective-permute-start | bytes 1179656 | tf_op jit(solution)/shard_map/ppermute | solution.py:207
  29.3 0.0 copy-done.1
  29.3 1.8 %shard_map.29.refs_7_ = f32[2,2,256,256]{3,2,1,0:T(8,128)S(1)} custom-call(f32[8,2,128]{2,1,0:T(2,128)S(1)} %maximum_bitcast_fusion.weights_ref, bf16[2,12,64,128]{3,2,1,0:T(8,128)(2,1)S(1)} %collective-permute-done.refs_4_.refs_0_, bf16[2,12,64,128]{3,2,1,0:T(8,128)(2,1)S(1)} %collective-permute-done.1.refs_0_.refs_1_, ...), custom_call_target="tpu_custom_call" | custom-call | flops 1207959552 | bytes 4456448 | tf_op jit(solution)/shard_map/pallas_call | solution.py:262
  31.1 0.0 collective-permute-done.6.refs_5_
  31.1 1.7 %shard_map.30.refs_1_ = f32[2,2,256,256]{3,2,1,0:T(8,128)S(1)} custom-call(f32[8,2,128]{2,1,0:T(2,128)S(1)} %maximum_bitcast_fusion.weights_ref, bf16[2,12,64,128]{3,2,1,0:T(8,128)(2,1)S(1)} %collective-permute-done.refs_4_.refs_0_, bf16[2,12,64,128]{3,2,1,0:T(8,128)(2,1)S(1)} %collective-permute-done.1.refs_0_.refs_1_, ...), custom_call_target="tpu_custom_call" | custom-call | flops 1207959552 | bytes 4456448 | tf_op jit(solution)/shard_map/pallas_call | solution.py:262
  32.8 7.7 %collective-permute-done.7.refs_0_.o3_ref.refs_2_ = bf16[2,12,64,128]{3,2,1,0:T(8,128)(2,1)S(1)} collective-permute-done((bf16[2,12,64,128]{3,2,1,0:T(8,128)(2,1)S(1)}, bf16[2,12,64,128]{3,2,1,0:T(8,128)(2,1)S(1)}, u32[]{:S(2)}, u32[]{:S(2)}) %collective-permute-start.7) | collective-permute-done | bytes 393248 | tf_op jit(solution)/shard_map/ppermute | solution.py:207
  40.5 2.2 %collective-permute-start.11 = (bf16[2,12,64,128]{3,2,1,0:T(8,128)(2,1)S(1)}, bf16[2,12,64,128]{3,2,1,0:T(8,128)(2,1)S(1)}, u32[]{:S(2)}, u32[]{:S(2)}) collective-permute-start(bf16[2,12,64,128]{3,2,1,0:T(8,128)(2,1)S(1)} %collective-permute-done.7.refs_0_.o3_ref.refs_2_), channel_id=1, source_target_pairs={{0,16},{1,17},{2,18},{3,19},{4,20},{5,21},{6,22},{7,23},{8,9},{9,8... | collective-permute-start | bytes 1179656 | tf_op jit(solution)/shard_map/ppermute | solution.py:207
  42.6 1.5 %collective-permute-start.12 = (bf16[2,12,64,128]{3,2,1,0:T(8,128)(2,1)S(1)}, bf16[2,12,64,128]{3,2,1,0:T(8,128)(2,1)S(1)}, u32[]{:S(2)}, u32[]{:S(2)}) collective-permute-start(bf16[2,12,64,128]{3,2,1,0:T(8,128)(2,1)S(1)} %collective-permute-done.7.refs_0_.o3_ref.refs_2_), channel_id=1, source_target_pairs={{0,1},{1,0},{2,3},{3,2},{4,5},{5,4},{6,7},{7,6},{8,24},{9,25},{10,... | collective-permute-start | bytes 1179656 | tf_op jit(solution)/shard_map/ppermute | solution.py:207
  44.2 0.4 shard_map.31.refs_5_
  44.6 3.4 %collective-permute-done.8.ab2_ref.refs_2_ = bf16[2,12,64,128]{3,2,1,0:T(8,128)(2,1)S(1)} collective-permute-done((bf16[2,12,64,128]{3,2,1,0:T(8,128)(2,1)S(1)}, bf16[2,12,64,128]{3,2,1,0:T(8,128)(2,1)S(1)}, u32[]{:S(2)}, u32[]{:S(2)}) %collective-permute-start.8) | collective-permute-done | bytes 393248 | tf_op jit(solution)/shard_map/ppermute | solution.py:207
  48.0 0.0 collective-permute-done.9.a12_ref.refs_3_.refs_0_
  48.0 0.0 collective-permute-done.10.b12_ref.refs_4_.refs_1_
  48.0 0.0 collective-permute-start.13
  48.0 0.2 shard_map.32
  48.2 1.8 %collective-permute-start.14 = (bf16[2,12,64,128]{3,2,1,0:T(8,128)(2,1)S(1)}, bf16[2,12,64,128]{3,2,1,0:T(8,128)(2,1)S(1)}, u32[]{:S(2)}, u32[]{:S(2)}) collective-permute-start(bf16[2,12,64,128]{3,2,1,0:T(8,128)(2,1)S(1)} %get-tuple-element.132), channel_id=1, source_target_pairs={{0,1},{1,0},{2,3},{3,2},{4,5},{5,4},{6,7},{7,6},{8,24},{9,25},{10,... | collective-permute-start | bytes 1179656 | tf_op jit(solution)/shard_map/ppermute | solution.py:207
  50.0 0.0 collective-permute-start.15
  50.0 1.6 %shard_map.33.refs_7_ = f32[2,2,256,256]{3,2,1,0:T(8,128)S(1)} custom-call(f32[8,2,128]{2,1,0:T(2,128)S(1)} %maximum_bitcast_fusion.weights_ref, bf16[2,12,64,128]{3,2,1,0:T(8,128)(2,1)S(1)} %collective-permute-done.refs_4_.refs_0_, bf16[2,12,64,128]{3,2,1,0:T(8,128)(2,1)S(1)} %collective-permute-done.2.refs_3_.refs_2_.refs_1_, ...), custom_call_target="tpu_custom_call" | custom-call | flops 1006632960 | bytes 4063232 | tf_op jit(solution)/shard_map/pallas_call | solution.py:262
  51.6 3.1 %collective-permute-done.11.a3_ref = bf16[2,12,64,128]{3,2,1,0:T(8,128)(2,1)S(1)} collective-permute-done((bf16[2,12,64,128]{3,2,1,0:T(8,128)(2,1)S(1)}, bf16[2,12,64,128]{3,2,1,0:T(8,128)(2,1)S(1)}, u32[]{:S(2)}, u32[]{:S(2)}) %collective-permute-start.11) | collective-permute-done | bytes 393248 | tf_op jit(solution)/shard_map/ppermute | solution.py:207
  54.8 0.0 collective-permute-done.12.ab3_ref
  54.8 0.1 shard_map.34.refs_5_.refs_1_.refs_2_
  54.8 0.1 collective-permute-start.16
  54.9 0.0 collective-permute-done.15.refs_6_
  54.9 2.3 %shard_map.35.refs_3_ = f32[2,2,256,256]{3,2,1,0:T(8,128)S(1)} custom-call(f32[8,2,128]{2,1,0:T(2,128)S(1)} %maximum_bitcast_fusion.weights_ref, bf16[2,12,64,128]{3,2,1,0:T(8,128)(2,1)S(1)} %collective-permute-done.refs_4_.refs_0_, bf16[2,12,64,128]{3,2,1,0:T(8,128)(2,1)S(1)} %collective-permute-done.2.refs_3_.refs_2_.refs_1_, ...), custom_call_target="tpu_custom_call" | custom-call | flops 16106127360 | bytes 5242880 | tf_op jit(solution)/shard_map/pallas_call | solution.py:262
  57.2 0.0 collective-permute-done.16.refs_2_
  57.2 1.8 %shard_map.36 = (f32[2,2,256,256]{3,2,1,0:T(8,128)S(1)}, f32[16,64,256]{2,1,0:T(8,128)}) custom-call(f32[8,2,128]{2,1,0:T(2,128)S(1)} %maximum_bitcast_fusion.weights_ref, bf16[2,12,64,128]{3,2,1,0:T(8,128)(2,1)S(1)} %collective-permute-done.7.refs_0_.o3_ref.refs_2_, bf16[2,2,12,64,128]{4,3,2,1,0:T(8,128)(2,1)S(1)} %shard_map.34.refs_5_.refs_1_.refs_2_, ...), custom_call_target="tpu_custom_call" | custom-call | flops 402653184 | bytes 2883584 | tf_op jit(solution)/shard_map/pallas_call | solution.py:262
  59.1 0.0 collective-permute-done.13.refs_3_
  59.1 0.0 collective-permute-done.14.refs_4_
  59.1 0.6 collective-permute-start.17
  59.7 0.1 collective-permute-start.18
  59.7 0.6 %shard_map.37 = (f32[2,2,256,256]{3,2,1,0:T(8,128)S(1)}, bf16[2,512,768]{2,1,0:T(8,128)(2,1)S(1)}) custom-call(f32[8,2,128]{2,1,0:T(2,128)S(1)} %maximum_bitcast_fusion.weights_ref, bf16[2,2,12,64,128]{4,3,2,1,0:T(8,128)(2,1)S(1)} %collective-permute-done.9.a12_ref.refs_3_.refs_0_, ...), custom_call_target="tpu_custom_call" | custom-call | flops 402653184 | bytes 2883584 | tf_op jit(solution)/shard_map/pallas_call | solution.py:262
  60.4 0.6 collective-permute-done.17.refs_0_
  61.0 0.6 collective-permute-done.18.refs_1_
  61.6 1.5 %shard_map.38 = f32[16,64,256]{2,1,0:T(8,128)} custom-call(f32[8,2,128]{2,1,0:T(2,128)S(1)} %maximum_bitcast_fusion.weights_ref, bf16[2,12,64,128]{3,2,1,0:T(8,128)(2,1)S(1)} %collective-permute-done.17.refs_0_, bf16[2,12,64,128]{3,2,1,0:T(8,128)(2,1)S(1)} %collective-permute-done.18.refs_1_, ...), custom_call_target="tpu_custom_call", output_to_operand_aliasing={{}: (5, {})} | custom-call | flops 402653184 | bytes 2883584 | tf_op jit(solution)/shard_map/pallas_call | solution.py:262
  (5 shorter events, 0.1 us)
Async XLA Ops:
  0.0 8.6 %copy-start = (s32[4,3]{1,0:T(4,128)S(1)}, s32[4,3]{1,0:T(4,128)}, u32[]{:S(2)}) copy-start(s32[4,3]{1,0:T(4,128)} %param.3) | copy-start | bytes 148
  0.0 29.3 %copy-start.1 = (bf16[2,1,64,12,128]{4,2,3,1,0:T(8,128)(2,1)S(1)}, bf16[2,1,64,12,128]{4,2,3,1,0:T(8,128)(2,1)}, u32[]{:S(2)}) copy-start(bf16[2,1,64,12,128]{4,2,3,1,0:T(8,128)(2,1)} %param.2) | copy-start | bytes 1179652
  0.0 21.9 %collective-permute-start = (bf16[2,12,64,128]{3,2,1,0:T(8,128)(2,1)}, bf16[2,12,64,128]{3,2,1,0:T(8,128)(2,1)S(1)}, u32[]{:S(2)}, u32[]{:S(2)}) collective-permute-start(bf16[2,12,64,128]{3,2,1,0:T(8,128)(2,1)} %bitcast.24), channel_id=1, source_target_pairs={{0,4},{1,5},{2,6},{3,7},{4,0},{5,1},{6,2},{7,3},{8,12},{9,13},{10,... | collective-permute-start | bytes 1179656 | tf_op jit(solution)/shard_map/ppermute | solution.py:207
  4.0 11.1 %collective-permute-start.1 = (bf16[2,12,64,128]{3,2,1,0:T(8,128)(2,1)}, bf16[2,12,64,128]{3,2,1,0:T(8,128)(2,1)S(1)}, u32[]{:S(2)}, u32[]{:S(2)}) collective-permute-start(bf16[2,12,64,128]{3,2,1,0:T(8,128)(2,1)} %bitcast.25), channel_id=1, source_target_pairs={{0,16},{1,17},{2,18},{3,19},{4,20},{5,21},{6,22},{7,23},{8,9},{9,8... | collective-permute-start | bytes 1179656 | tf_op jit(solution)/shard_map/ppermute | solution.py:207
  5.5 17.8 %collective-permute-start.2 = (bf16[2,12,64,128]{3,2,1,0:T(8,128)(2,1)}, bf16[2,12,64,128]{3,2,1,0:T(8,128)(2,1)S(1)}, u32[]{:S(2)}, u32[]{:S(2)}) collective-permute-start(bf16[2,12,64,128]{3,2,1,0:T(8,128)(2,1)} %bitcast.26), channel_id=1, source_target_pairs={{0,2},{1,3},{2,0},{3,1},{4,6},{5,7},{6,4},{7,5},{8,10},{9,11},{10,... | collective-permute-start | bytes 1179656 | tf_op jit(solution)/shard_map/ppermute | solution.py:207
  7.1 16.2 %collective-permute-start.3 = (bf16[2,12,64,128]{3,2,1,0:T(8,128)(2,1)}, bf16[2,12,64,128]{3,2,1,0:T(8,128)(2,1)S(1)}, u32[]{:S(2)}, u32[]{:S(2)}) collective-permute-start(bf16[2,12,64,128]{3,2,1,0:T(8,128)(2,1)} %bitcast.27), channel_id=1, source_target_pairs={{0,1},{1,0},{2,3},{3,2},{4,5},{5,4},{6,7},{7,6},{8,24},{9,25},{10,... | collective-permute-start | bytes 1179656 | tf_op jit(solution)/shard_map/ppermute | solution.py:207
  8.6 14.7 %collective-permute-start.5 = (bf16[2,12,64,128]{3,2,1,0:T(8,128)(2,1)}, bf16[2,12,64,128]{3,2,1,0:T(8,128)(2,1)S(1)}, u32[]{:S(2)}, u32[]{:S(2)}) collective-permute-start(bf16[2,12,64,128]{3,2,1,0:T(8,128)(2,1)} %bitcast.28), channel_id=1, source_target_pairs={{0,8},{1,9},{2,10},{3,11},{4,12},{5,13},{6,14},{7,15},{8,0},{9,1},... | collective-permute-start | bytes 1179656 | tf_op jit(solution)/shard_map/ppermute | solution.py:207
  15.1 8.3 %collective-permute-start.4 = (bf16[2,12,64,128]{3,2,1,0:T(8,128)(2,1)S(1)}, bf16[2,12,64,128]{3,2,1,0:T(8,128)(2,1)S(1)}, u32[]{:S(2)}, u32[]{:S(2)}) collective-permute-start(bf16[2,12,64,128]{3,2,1,0:T(8,128)(2,1)S(1)} %collective-permute-done.1.refs_0_.refs_1_), channel_id=1, source_target_pairs={{0,1},{1,0},{2,3},{3,2},{4,5},{5,4},{6,7},{7,6},{8,24},{9,25},{10,... | collective-permute-start | bytes 1179656 | tf_op jit(solution)/shard_map/ppermute | solution.py:207
  23.6 7.5 %collective-permute-start.6 = (bf16[5,2,12,64,128]{4,3,2,1,0:T(8,128)(2,1)S(1)}, bf16[5,2,12,64,128]{4,3,2,1,0:T(8,128)(2,1)S(1)}, u32[]{:S(2)}, u32[]{:S(2)}) collective-permute-start(bf16[5,2,12,64,128]{4,3,2,1,0:T(8,128)(2,1)S(1)} %get-tuple-element.94), channel_id=1, source_target_pairs={{0,8},{1,9},{2,10},{3,11},{4,12},{5,13},{6,14},{7,15},{8,0},{9,1},... | collective-permute-start | bytes 5898248 | tf_op jit(solution)/shard_map/ppermute | solution.py:207
  23.7 16.8 %collective-permute-start.7 = (bf16[2,12,64,128]{3,2,1,0:T(8,128)(2,1)S(1)}, bf16[2,12,64,128]{3,2,1,0:T(8,128)(2,1)S(1)}, u32[]{:S(2)}, u32[]{:S(2)}) collective-permute-start(bf16[2,12,64,128]{3,2,1,0:T(8,128)(2,1)S(1)} %collective-permute-done.refs_4_.refs_0_), channel_id=1, source_target_pairs={{0,2},{1,3},{2,0},{3,1},{4,6},{5,7},{6,4},{7,5},{8,10},{9,11},{10,... | collective-permute-start | bytes 1179656 | tf_op jit(solution)/shard_map/ppermute | solution.py:207
  25.9 22.1 %collective-permute-start.9 = (bf16[2,2,12,64,128]{4,3,2,1,0:T(8,128)(2,1)S(1)}, bf16[2,2,12,64,128]{4,3,2,1,0:T(8,128)(2,1)S(1)}, u32[]{:S(2)}, u32[]{:S(2)}) collective-permute-start(bf16[2,2,12,64,128]{4,3,2,1,0:T(8,128)(2,1)S(1)} %get-tuple-element.107), channel_id=1, source_target_pairs={{0,16},{1,17},{2,18},{3,19},{4,20},{5,21},{6,22},{7,23},{8,9},{9,8... | collective-permute-start | bytes 2359304 | tf_op jit(solution)/shard_map/ppermute | solution.py:207
  27.4 20.6 %collective-permute-start.10 = (bf16[2,2,12,64,128]{4,3,2,1,0:T(8,128)(2,1)S(1)}, bf16[2,2,12,64,128]{4,3,2,1,0:T(8,128)(2,1)S(1)}, u32[]{:S(2)}, u32[]{:S(2)}) collective-permute-start(bf16[2,2,12,64,128]{4,3,2,1,0:T(8,128)(2,1)S(1)} %get-tuple-element.107), channel_id=1, source_target_pairs={{0,1},{1,0},{2,3},{3,2},{4,5},{5,4},{6,7},{7,6},{8,24},{9,25},{10,... | collective-permute-start | bytes 2359304 | tf_op jit(solution)/shard_map/ppermute | solution.py:207
  28.0 20.0 %collective-permute-start.8 = (bf16[2,12,64,128]{3,2,1,0:T(8,128)(2,1)S(1)}, bf16[2,12,64,128]{3,2,1,0:T(8,128)(2,1)S(1)}, u32[]{:S(2)}, u32[]{:S(2)}) collective-permute-start(bf16[2,12,64,128]{3,2,1,0:T(8,128)(2,1)S(1)} %collective-permute-done.4.refs_2_.refs_4_), channel_id=1, source_target_pairs={{0,4},{1,5},{2,6},{3,7},{4,0},{5,1},{6,2},{7,3},{8,12},{9,13},{10,... | collective-permute-start | bytes 1179656 | tf_op jit(solution)/shard_map/ppermute | solution.py:207
  40.5 14.3 %collective-permute-start.11 = (bf16[2,12,64,128]{3,2,1,0:T(8,128)(2,1)S(1)}, bf16[2,12,64,128]{3,2,1,0:T(8,128)(2,1)S(1)}, u32[]{:S(2)}, u32[]{:S(2)}) collective-permute-start(bf16[2,12,64,128]{3,2,1,0:T(8,128)(2,1)S(1)} %collective-permute-done.7.refs_0_.o3_ref.refs_2_), channel_id=1, source_target_pairs={{0,16},{1,17},{2,18},{3,19},{4,20},{5,21},{6,22},{7,23},{8,9},{9,8... | collective-permute-start | bytes 1179656 | tf_op jit(solution)/shard_map/ppermute | solution.py:207
  42.6 12.1 %collective-permute-start.12 = (bf16[2,12,64,128]{3,2,1,0:T(8,128)(2,1)S(1)}, bf16[2,12,64,128]{3,2,1,0:T(8,128)(2,1)S(1)}, u32[]{:S(2)}, u32[]{:S(2)}) collective-permute-start(bf16[2,12,64,128]{3,2,1,0:T(8,128)(2,1)S(1)} %collective-permute-done.7.refs_0_.o3_ref.refs_2_), channel_id=1, source_target_pairs={{0,1},{1,0},{2,3},{3,2},{4,5},{5,4},{6,7},{7,6},{8,24},{9,25},{10,... | collective-permute-start | bytes 1179656 | tf_op jit(solution)/shard_map/ppermute | solution.py:207
  48.0 11.1 %collective-permute-start.13 = (bf16[2,12,64,128]{3,2,1,0:T(8,128)(2,1)S(1)}, bf16[2,12,64,128]{3,2,1,0:T(8,128)(2,1)S(1)}, u32[]{:S(2)}, u32[]{:S(2)}) collective-permute-start(bf16[2,12,64,128]{3,2,1,0:T(8,128)(2,1)S(1)} %collective-permute-done.8.ab2_ref.refs_2_), channel_id=1, source_target_pairs={{0,2},{1,3},{2,0},{3,1},{4,6},{5,7},{6,4},{7,5},{8,10},{9,11},{10,... | collective-permute-start | bytes 1179656 | tf_op jit(solution)/shard_map/ppermute | solution.py:207
  48.2 10.9 %collective-permute-start.14 = (bf16[2,12,64,128]{3,2,1,0:T(8,128)(2,1)S(1)}, bf16[2,12,64,128]{3,2,1,0:T(8,128)(2,1)S(1)}, u32[]{:S(2)}, u32[]{:S(2)}) collective-permute-start(bf16[2,12,64,128]{3,2,1,0:T(8,128)(2,1)S(1)} %get-tuple-element.132), channel_id=1, source_target_pairs={{0,1},{1,0},{2,3},{3,2},{4,5},{5,4},{6,7},{7,6},{8,24},{9,25},{10,... | collective-permute-start | bytes 1179656 | tf_op jit(solution)/shard_map/ppermute | solution.py:207
  50.0 4.9 %collective-permute-start.15 = (bf16[6,2,12,64,128]{4,3,2,1,0:T(8,128)(2,1)S(1)}, bf16[6,2,12,64,128]{4,3,2,1,0:T(8,128)(2,1)S(1)}, u32[]{:S(2)}, u32[]{:S(2)}) collective-permute-start(bf16[6,2,12,64,128]{4,3,2,1,0:T(8,128)(2,1)S(1)} %get-tuple-element.133), channel_id=1, source_target_pairs={{0,8},{1,9},{2,10},{3,11},{4,12},{5,13},{6,14},{7,15},{8,0},{9,1},... | collective-permute-start | bytes 7077896 | tf_op jit(solution)/shard_map/ppermute | solution.py:207
  54.8 2.4 %collective-permute-start.16 = (bf16[2,2,12,64,128]{4,3,2,1,0:T(8,128)(2,1)S(1)}, bf16[2,2,12,64,128]{4,3,2,1,0:T(8,128)(2,1)S(1)}, u32[]{:S(2)}, u32[]{:S(2)}) collective-permute-start(bf16[2,2,12,64,128]{4,3,2,1,0:T(8,128)(2,1)S(1)} %shard_map.34.refs_5_.refs_1_.refs_2_), channel_id=1, source_target_pairs={{0,8},{1,9},{2,10},{3,11},{4,12},{5,13},{6,14},{7,15},{8,0},{9,1},... | collective-permute-start | bytes 2359304 | tf_op jit(solution)/shard_map/ppermute | solution.py:207
  59.1 1.9 %collective-permute-start.17 = (bf16[2,12,64,128]{3,2,1,0:T(8,128)(2,1)S(1)}, bf16[2,12,64,128]{3,2,1,0:T(8,128)(2,1)S(1)}, u32[]{:S(2)}, u32[]{:S(2)}) collective-permute-start(bf16[2,12,64,128]{3,2,1,0:T(8,128)(2,1)S(1)} %collective-permute-done.13.refs_3_), channel_id=1, source_target_pairs={{0,8},{1,9},{2,10},{3,11},{4,12},{5,13},{6,14},{7,15},{8,0},{9,1},... | collective-permute-start | bytes 1179656 | tf_op jit(solution)/shard_map/ppermute | solution.py:207
  59.7 1.9 %collective-permute-start.18 = (bf16[2,12,64,128]{3,2,1,0:T(8,128)(2,1)S(1)}, bf16[2,12,64,128]{3,2,1,0:T(8,128)(2,1)S(1)}, u32[]{:S(2)}, u32[]{:S(2)}) collective-permute-start(bf16[2,12,64,128]{3,2,1,0:T(8,128)(2,1)S(1)} %collective-permute-done.14.refs_4_), channel_id=1, source_target_pairs={{0,8},{1,9},{2,10},{3,11},{4,12},{5,13},{6,14},{7,15},{8,0},{9,1},... | collective-permute-start | bytes 1179656 | tf_op jit(solution)/shard_map/ppermute | solution.py:207

commit v20 on v18

--- a/solution.py
+++ b/solution.py
@@ -146,17 +146,18 @@
                     for s in range(spins)
                 ]
             left_ref[slot] = left_sides(owns, weights_ref[site])
-    for name in names:
+    copies = []
+    for index, name in enumerate(names):
+        if half and index == half:
+            copies = send_columns(
+                0,
+                lambda rows, across: out_ref[0, 0, rows, across],
+                lambda rows, across: out_ref[1, 0, rows, across],
+            )
         dx, added = term(name)
         out_ref[0 if name[0] == "near" else 1, dx] += added
-    if half:
-        copies = send_columns(
-            0,
-            lambda rows, across: out_ref[0, 0, rows, across],
-            lambda rows, across: out_ref[1, 0, rows, across],
-        )
-        for copy in copies:
-            copy.wait()
+    for copy in copies:
+        copy.wait()
 
 
 def route_second(*refs):
@@ -231,7 +232,7 @@
         key, slot = where[("near", kind, dz)]
         return arrays[key] if slot is None else arrays[key][slot]
 
-    def add(names, totals, keep=None, left=None, half=False, field=None, weight=1):
+    def add(names, totals, keep=None, left=None, half=0, field=None, weight=1):
         given, last = left is not None, field is not None
         slots, left = left if given else (keep or left_slots(names), None)
         uses = list(names)
@@ -346,7 +347,7 @@
     far4 = [swap(near(*kind)) for kind in fourth]
     put("4a", far3, "far", third)
     names = [("far", *kind) for kind in third] + [("near", *kind) for kind in fourth]
-    totals, field, (slots, left) = add(names, totals, keep=left_slots(names), half=True)
+    totals, field, (slots, left) = add(names, totals, keep=left_slots(names), half=len(third))
     put("4b", far4[0], "far", fourth[:1])
     put("4c", far4[1], "far", fourth[1:])
     totals, left, field = fence((totals, left, field))

time: 62.6 us -> 62.6 us (level)
  no operation moved by 1% of the time
where the time goes in v20:
time: 62.6 us; the launch traced here: 62.5 us
  waiting for transfers between devices  26.4 us (42%)
  starting transfers between devices  22.6 us (36%)
  Pallas kernels  12 us (19%)
  local copies, waits for them, and re-layouts  1 us (2%)
    ppermute x19, waiting for transfers between devices, move(): return lax.ppermute(array, AXES, pairs)  26.4 us
    ppermute x19, starting transfers between devices, move(): return lax.ppermute(array, AXES, pairs)  22.6 us
    pallas_call x7, Pallas kernels, add(): pl.pallas_call(functools.partial(add_shards, tuple(names), places, slots,...  11.6 us
  transfers between devices with their start and end apart: 19, of which 7 were waited for; matrix products, arithmetic and copies ran while one was open for 0% of the time, Pallas kernels for 16%

profile of v20, /device:TPU:0, one launch (start us, length us, event | category | flops | bytes accessed | tf_op | source)
XLA Modules:
  0.0 62.5 jit_solution(16985172460702737980)
XLA Ops:
  0.0 0.0 copy-start
  0.0 2.9 %collective-permute-start.1 = (bf16[2,12,64,128]{3,2,1,0:T(8,128)(2,1)}, bf16[2,12,64,128]{3,2,1,0:T(8,128)(2,1)S(1)}, u32[]{:S(2)}, u32[]{:S(2)}) collective-permute-start(bf16[2,12,64,128]{3,2,1,0:T(8,128)(2,1)} %bitcast.24), channel_id=1, source_target_pairs={{0,16},{1,17},{2,18},{3,19},{4,20},{5,21},{6,22},{7,23},{8,9},{9,8... | collective-permute-start | bytes 1179656 | tf_op jit(solution)/shard_map/ppermute | solution.py:209
  2.9 2.6 %collective-permute-start = (bf16[2,12,64,128]{3,2,1,0:T(8,128)(2,1)}, bf16[2,12,64,128]{3,2,1,0:T(8,128)(2,1)S(1)}, u32[]{:S(2)}, u32[]{:S(2)}) collective-permute-start(bf16[2,12,64,128]{3,2,1,0:T(8,128)(2,1)} %bitcast.25), channel_id=1, source_target_pairs={{0,4},{1,5},{2,6},{3,7},{4,0},{5,1},{6,2},{7,3},{8,12},{9,13},{10,... | collective-permute-start | bytes 1179656 | tf_op jit(solution)/shard_map/ppermute | solution.py:209
  5.5 1.6 %collective-permute-start.2 = (bf16[2,12,64,128]{3,2,1,0:T(8,128)(2,1)}, bf16[2,12,64,128]{3,2,1,0:T(8,128)(2,1)S(1)}, u32[]{:S(2)}, u32[]{:S(2)}) collective-permute-start(bf16[2,12,64,128]{3,2,1,0:T(8,128)(2,1)} %bitcast.26), channel_id=1, source_target_pairs={{0,2},{1,3},{2,0},{3,1},{4,6},{5,7},{6,4},{7,5},{8,10},{9,11},{10,... | collective-permute-start | bytes 1179656 | tf_op jit(solution)/shard_map/ppermute | solution.py:209
  7.1 1.5 %collective-permute-start.3 = (bf16[2,12,64,128]{3,2,1,0:T(8,128)(2,1)}, bf16[2,12,64,128]{3,2,1,0:T(8,128)(2,1)S(1)}, u32[]{:S(2)}, u32[]{:S(2)}) collective-permute-start(bf16[2,12,64,128]{3,2,1,0:T(8,128)(2,1)} %bitcast.27), channel_id=1, source_target_pairs={{0,1},{1,0},{2,3},{3,2},{4,5},{5,4},{6,7},{7,6},{8,24},{9,25},{10,... | collective-permute-start | bytes 1179656 | tf_op jit(solution)/shard_map/ppermute | solution.py:209
  8.6 0.0 collective-permute-start.5
  8.6 0.0 copy-done
  8.7 0.1 fusion
  8.8 0.2 collective-permute-done.1.refs_0_.refs_1_
  9.0 3.4 %collective-permute-start.4 = (bf16[2,12,64,128]{3,2,1,0:T(8,128)(2,1)S(1)}, bf16[2,12,64,128]{3,2,1,0:T(8,128)(2,1)S(1)}, u32[]{:S(2)}, u32[]{:S(2)}) collective-permute-start(bf16[2,12,64,128]{3,2,1,0:T(8,128)(2,1)S(1)} %collective-permute-done.1.refs_0_.refs_1_), channel_id=1, source_target_pairs={{0,1},{1,0},{2,3},{3,2},{4,5},{5,4},{6,7},{7,6},{8,24},{9,25},{10,... | collective-permute-start | bytes 1179656 | tf_op jit(solution)/shard_map/ppermute | solution.py:209
  12.4 0.1 multiply_cosine_fusion
  12.6 10.6 %collective-permute-done.refs_4_.refs_0_ = bf16[2,12,64,128]{3,2,1,0:T(8,128)(2,1)S(1)} collective-permute-done((bf16[2,12,64,128]{3,2,1,0:T(8,128)(2,1)}, bf16[2,12,64,128]{3,2,1,0:T(8,128)(2,1)S(1)}, u32[]{:S(2)}, u32[]{:S(2)}) %collective-permute-start) | collective-permute-done | bytes 393248 | tf_op jit(solution)/shard_map/ppermute | solution.py:209
  23.2 0.2 collective-permute-done.2.refs_3_.refs_2_.refs_1_
  23.4 0.0 collective-permute-done.3.refs_1_.refs_3_
  23.4 0.0 collective-permute-done.5.refs_4_
  23.4 0.0 collective-permute-done.4.refs_2_.refs_4_
  23.4 0.2 shard_map.28
  23.6 0.1 collective-permute-start.6
  23.7 1.5 %collective-permute-start.7 = (bf16[2,12,64,128]{3,2,1,0:T(8,128)(2,1)S(1)}, bf16[2,12,64,128]{3,2,1,0:T(8,128)(2,1)S(1)}, u32[]{:S(2)}, u32[]{:S(2)}) collective-permute-start(bf16[2,12,64,128]{3,2,1,0:T(8,128)(2,1)S(1)} %collective-permute-done.refs_4_.refs_0_), channel_id=1, source_target_pairs={{0,2},{1,3},{2,0},{3,1},{4,6},{5,7},{6,4},{7,5},{8,10},{9,11},{10,... | collective-permute-start | bytes 1179656 | tf_op jit(solution)/shard_map/ppermute | solution.py:209
  25.2 0.5 collective-permute-start.10
  25.7 1.5 %collective-permute-start.9 = (bf16[2,2,12,64,128]{4,3,2,1,0:T(8,128)(2,1)S(1)}, bf16[2,2,12,64,128]{4,3,2,1,0:T(8,128)(2,1)S(1)}, u32[]{:S(2)}, u32[]{:S(2)}) collective-permute-start(bf16[2,2,12,64,128]{4,3,2,1,0:T(8,128)(2,1)S(1)} %get-tuple-element.106), channel_id=1, source_target_pairs={{0,16},{1,17},{2,18},{3,19},{4,20},{5,21},{6,22},{7,23},{8,9},{9,8... | collective-permute-start | bytes 2359304 | tf_op jit(solution)/shard_map/ppermute | solution.py:209
  27.2 2.3 %collective-permute-start.8 = (bf16[2,12,64,128]{3,2,1,0:T(8,128)(2,1)S(1)}, bf16[2,12,64,128]{3,2,1,0:T(8,128)(2,1)S(1)}, u32[]{:S(2)}, u32[]{:S(2)}) collective-permute-start(bf16[2,12,64,128]{3,2,1,0:T(8,128)(2,1)S(1)} %collective-permute-done.4.refs_2_.refs_4_), channel_id=1, source_target_pairs={{0,4},{1,5},{2,6},{3,7},{4,0},{5,1},{6,2},{7,3},{8,12},{9,13},{10,... | collective-permute-start | bytes 1179656 | tf_op jit(solution)/shard_map/ppermute | solution.py:209
  29.5 0.0 copy-start.1
  29.5 1.0 %copy-done.1 = bf16[2,1,64,12,128]{4,2,3,1,0:T(8,128)(2,1)S(1)} copy-done((bf16[2,1,64,12,128]{4,2,3,1,0:T(8,128)(2,1)S(1)}, bf16[2,1,64,12,128]{4,2,3,1,0:T(8,128)(2,1)}, u32[]{:S(2)}) %copy-start.1) | copy-done | bytes 393240
  30.5 1.8 %shard_map.29.refs_7_ = f32[2,2,256,256]{3,2,1,0:T(8,128)S(1)} custom-call(f32[8,2,128]{2,1,0:T(2,128)S(1)} %maximum_bitcast_fusion.weights_ref, bf16[2,12,64,128]{3,2,1,0:T(8,128)(2,1)S(1)} %collective-permute-done.refs_4_.refs_0_, bf16[2,12,64,128]{3,2,1,0:T(8,128)(2,1)S(1)} %collective-permute-done.1.refs_0_.refs_1_, ...), custom_call_target="tpu_custom_call" | custom-call | flops 1207959552 | bytes 4456448 | tf_op jit(solution)/shard_map/pallas_call | solution.py:264
  32.3 0.0 collective-permute-done.6.refs_5_
  32.3 1.7 %shard_map.30.refs_1_ = f32[2,2,256,256]{3,2,1,0:T(8,128)S(1)} custom-call(f32[8,2,128]{2,1,0:T(2,128)S(1)} %maximum_bitcast_fusion.weights_ref, bf16[2,12,64,128]{3,2,1,0:T(8,128)(2,1)S(1)} %collective-permute-done.refs_4_.refs_0_, bf16[2,12,64,128]{3,2,1,0:T(8,128)(2,1)S(1)} %collective-permute-done.1.refs_0_.refs_1_, ...), custom_call_target="tpu_custom_call" | custom-call | flops 1207959552 | bytes 4456448 | tf_op jit(solution)/shard_map/pallas_call | solution.py:264
  34.0 7.6 %collective-permute-done.7.refs_0_.o3_ref.refs_2_ = bf16[2,12,64,128]{3,2,1,0:T(8,128)(2,1)S(1)} collective-permute-done((bf16[2,12,64,128]{3,2,1,0:T(8,128)(2,1)S(1)}, bf16[2,12,64,128]{3,2,1,0:T(8,128)(2,1)S(1)}, u32[]{:S(2)}, u32[]{:S(2)}) %collective-permute-start.7) | collective-permute-done | bytes 393248 | tf_op jit(solution)/shard_map/ppermute | solution.py:209
  41.6 2.4 %collective-permute-start.11 = (bf16[2,12,64,128]{3,2,1,0:T(8,128)(2,1)S(1)}, bf16[2,12,64,128]{3,2,1,0:T(8,128)(2,1)S(1)}, u32[]{:S(2)}, u32[]{:S(2)}) collective-permute-start(bf16[2,12,64,128]{3,2,1,0:T(8,128)(2,1)S(1)} %collective-permute-done.7.refs_0_.o3_ref.refs_2_), channel_id=1, source_target_pairs={{0,16},{1,17},{2,18},{3,19},{4,20},{5,21},{6,22},{7,23},{8,9},{9,8... | collective-permute-start | bytes 1179656 | tf_op jit(solution)/shard_map/ppermute | solution.py:209
  44.1 0.0 collective-permute-start.12
  44.1 0.4 shard_map.31.refs_5_
  44.5 2.7 %collective-permute-done.8.ab2_ref.refs_2_ = bf16[2,12,64,128]{3,2,1,0:T(8,128)(2,1)S(1)} collective-permute-done((bf16[2,12,64,128]{3,2,1,0:T(8,128)(2,1)S(1)}, bf16[2,12,64,128]{3,2,1,0:T(8,128)(2,1)S(1)}, u32[]{:S(2)}, u32[]{:S(2)}) %collective-permute-start.8) | collective-permute-done | bytes 393248 | tf_op jit(solution)/shard_map/ppermute | solution.py:209
  47.2 0.0 collective-permute-done.10.b12_ref.refs_4_.refs_2_
  47.2 0.0 collective-permute-done.9.a12_ref.refs_3_.refs_1_
  47.2 0.0 collective-permute-start.13
  47.2 0.2 shard_map.32
  47.4 0.1 collective-permute-start.15
  47.4 1.6 %collective-permute-start.14 = (bf16[2,12,64,128]{3,2,1,0:T(8,128)(2,1)S(1)}, bf16[2,12,64,128]{3,2,1,0:T(8,128)(2,1)S(1)}, u32[]{:S(2)}, u32[]{:S(2)}) collective-permute-start(bf16[2,12,64,128]{3,2,1,0:T(8,128)(2,1)S(1)} %get-tuple-element.131), channel_id=1, source_target_pairs={{0,1},{1,0},{2,3},{3,2},{4,5},{5,4},{6,7},{7,6},{8,24},{9,25},{10,... | collective-permute-start | bytes 1179656 | tf_op jit(solution)/shard_map/ppermute | solution.py:209
  49.0 1.6 %shard_map.33.refs_7_ = f32[2,2,256,256]{3,2,1,0:T(8,128)S(1)} custom-call(f32[8,2,128]{2,1,0:T(2,128)S(1)} %maximum_bitcast_fusion.weights_ref, bf16[2,12,64,128]{3,2,1,0:T(8,128)(2,1)S(1)} %collective-permute-done.refs_4_.refs_0_, bf16[2,12,64,128]{3,2,1,0:T(8,128)(2,1)S(1)} %collective-permute-done.2.refs_3_.refs_2_.refs_1_, ...), custom_call_target="tpu_custom_call" | custom-call | flops 1006632960 | bytes 4063232 | tf_op jit(solution)/shard_map/pallas_call | solution.py:264
  50.7 3.4 %collective-permute-done.11.a3_ref = bf16[2,12,64,128]{3,2,1,0:T(8,128)(2,1)S(1)} collective-permute-done((bf16[2,12,64,128]{3,2,1,0:T(8,128)(2,1)S(1)}, bf16[2,12,64,128]{3,2,1,0:T(8,128)(2,1)S(1)}, u32[]{:S(2)}, u32[]{:S(2)}) %collective-permute-start.11) | collective-permute-done | bytes 393248 | tf_op jit(solution)/shard_map/ppermute | solution.py:209
  54.0 0.0 collective-permute-done.12.ab3_ref
  54.0 0.1 shard_map.34.refs_5_.refs_3_
  54.1 0.1 collective-permute-start.16
  54.2 0.0 collective-permute-done.15.refs_6_
  54.2 2.3 %shard_map.35.refs_7_ = f32[2,2,256,256]{3,2,1,0:T(8,128)S(1)} custom-call(f32[8,2,128]{2,1,0:T(2,128)S(1)} %maximum_bitcast_fusion.weights_ref, bf16[2,12,64,128]{3,2,1,0:T(8,128)(2,1)S(1)} %collective-permute-done.refs_4_.refs_0_, bf16[2,12,64,128]{3,2,1,0:T(8,128)(2,1)S(1)} %collective-permute-done.2.refs_3_.refs_2_.refs_1_, ...), custom_call_target="tpu_custom_call" | custom-call | flops 16106127360 | bytes 5242880 | tf_op jit(solution)/shard_map/pallas_call | solution.py:264
  56.5 1.7 %collective-permute-done.14.refs_5_ = bf16[2,12,64,128]{3,2,1,0:T(8,128)(2,1)S(1)} collective-permute-done((bf16[2,12,64,128]{3,2,1,0:T(8,128)(2,1)S(1)}, bf16[2,12,64,128]{3,2,1,0:T(8,128)(2,1)S(1)}, u32[]{:S(2)}, u32[]{:S(2)}) %collective-permute-start.14) | collective-permute-done | bytes 393248 | tf_op jit(solution)/shard_map/ppermute | solution.py:209
  58.2 0.0 collective-permute-done.13.refs_4_
  58.2 0.0 collective-permute-start.17
  58.2 0.5 collective-permute-start.18
  58.7 0.0 collective-permute-done.16.refs_6_
  58.7 2.2 %shard_map.36 = (f32[2,2,256,256]{3,2,1,0:T(8,128)S(1)}, f32[16,64,256]{2,1,0:T(8,128)}, bf16[3,512,768]{2,1,0:T(8,128)(2,1)S(1)}) custom-call(f32[8,2,128]{2,1,0:T(2,128)S(1)} %maximum_bitcast_fusion.weights_ref, bf16[2,12,64,128]{3,2,1,0:T(8,128)(2,1)S(1)} %collective-permute-done.7.refs_0_.o3_ref.refs_2_, ...), custom_call_target="tpu_custom_call" | custom-call | flops 805306368 | bytes 3670016 | tf_op jit(solution)/shard_map/pallas_call | solution.py:264
  60.9 0.0 collective-permute-done.17.refs_0_
  60.9 0.0 collective-permute-done.18.refs_1_
  60.9 1.5 %shard_map.37 = f32[16,64,256]{2,1,0:T(8,128)} custom-call(f32[8,2,128]{2,1,0:T(2,128)S(1)} %maximum_bitcast_fusion.weights_ref, bf16[2,12,64,128]{3,2,1,0:T(8,128)(2,1)S(1)} %collective-permute-done.17.refs_0_, bf16[2,12,64,128]{3,2,1,0:T(8,128)(2,1)S(1)} %collective-permute-done.18.refs_1_, ...), custom_call_target="tpu_custom_call", output_to_operand_aliasing={{}: (5, {})} | custom-call | flops 402653184 | bytes 2883584 | tf_op jit(solution)/shard_map/pallas_call | solution.py:264
  (5 shorter events, 0.1 us)
Async XLA Ops:
  0.0 8.6 %copy-start = (s32[4,3]{1,0:T(4,128)S(1)}, s32[4,3]{1,0:T(4,128)}, u32[]{:S(2)}) copy-start(s32[4,3]{1,0:T(4,128)} %param.3) | copy-start | bytes 148
  0.0 9.0 %collective-permute-start.1 = (bf16[2,12,64,128]{3,2,1,0:T(8,128)(2,1)}, bf16[2,12,64,128]{3,2,1,0:T(8,128)(2,1)S(1)}, u32[]{:S(2)}, u32[]{:S(2)}) collective-permute-start(bf16[2,12,64,128]{3,2,1,0:T(8,128)(2,1)} %bitcast.24), channel_id=1, source_target_pairs={{0,16},{1,17},{2,18},{3,19},{4,20},{5,21},{6,22},{7,23},{8,9},{9,8... | collective-permute-start | bytes 1179656 | tf_op jit(solution)/shard_map/ppermute | solution.py:209
  2.9 20.3 %collective-permute-start = (bf16[2,12,64,128]{3,2,1,0:T(8,128)(2,1)}, bf16[2,12,64,128]{3,2,1,0:T(8,128)(2,1)S(1)}, u32[]{:S(2)}, u32[]{:S(2)}) collective-permute-start(bf16[2,12,64,128]{3,2,1,0:T(8,128)(2,1)} %bitcast.25), channel_id=1, source_target_pairs={{0,4},{1,5},{2,6},{3,7},{4,0},{5,1},{6,2},{7,3},{8,12},{9,13},{10,... | collective-permute-start | bytes 1179656 | tf_op jit(solution)/shard_map/ppermute | solution.py:209
  5.5 17.8 %collective-permute-start.2 = (bf16[2,12,64,128]{3,2,1,0:T(8,128)(2,1)}, bf16[2,12,64,128]{3,2,1,0:T(8,128)(2,1)S(1)}, u32[]{:S(2)}, u32[]{:S(2)}) collective-permute-start(bf16[2,12,64,128]{3,2,1,0:T(8,128)(2,1)} %bitcast.26), channel_id=1, source_target_pairs={{0,2},{1,3},{2,0},{3,1},{4,6},{5,7},{6,4},{7,5},{8,10},{9,11},{10,... | collective-permute-start | bytes 1179656 | tf_op jit(solution)/shard_map/ppermute | solution.py:209
  7.1 16.3 %collective-permute-start.3 = (bf16[2,12,64,128]{3,2,1,0:T(8,128)(2,1)}, bf16[2,12,64,128]{3,2,1,0:T(8,128)(2,1)S(1)}, u32[]{:S(2)}, u32[]{:S(2)}) collective-permute-start(bf16[2,12,64,128]{3,2,1,0:T(8,128)(2,1)} %bitcast.27), channel_id=1, source_target_pairs={{0,1},{1,0},{2,3},{3,2},{4,5},{5,4},{6,7},{7,6},{8,24},{9,25},{10,... | collective-permute-start | bytes 1179656 | tf_op jit(solution)/shard_map/ppermute | solution.py:209
  8.6 14.8 %collective-permute-start.5 = (bf16[2,12,64,128]{3,2,1,0:T(8,128)(2,1)}, bf16[2,12,64,128]{3,2,1,0:T(8,128)(2,1)S(1)}, u32[]{:S(2)}, u32[]{:S(2)}) collective-permute-start(bf16[2,12,64,128]{3,2,1,0:T(8,128)(2,1)} %bitcast.28), channel_id=1, source_target_pairs={{0,8},{1,9},{2,10},{3,11},{4,12},{5,13},{6,14},{7,15},{8,0},{9,1},... | collective-permute-start | bytes 1179656 | tf_op jit(solution)/shard_map/ppermute | solution.py:209
  9.0 14.4 %collective-permute-start.4 = (bf16[2,12,64,128]{3,2,1,0:T(8,128)(2,1)S(1)}, bf16[2,12,64,128]{3,2,1,0:T(8,128)(2,1)S(1)}, u32[]{:S(2)}, u32[]{:S(2)}) collective-permute-start(bf16[2,12,64,128]{3,2,1,0:T(8,128)(2,1)S(1)} %collective-permute-done.1.refs_0_.refs_1_), channel_id=1, source_target_pairs={{0,1},{1,0},{2,3},{3,2},{4,5},{5,4},{6,7},{7,6},{8,24},{9,25},{10,... | collective-permute-start | bytes 1179656 | tf_op jit(solution)/shard_map/ppermute | solution.py:209
  23.6 8.7 %collective-permute-start.6 = (bf16[5,2,12,64,128]{4,3,2,1,0:T(8,128)(2,1)S(1)}, bf16[5,2,12,64,128]{4,3,2,1,0:T(8,128)(2,1)S(1)}, u32[]{:S(2)}, u32[]{:S(2)}) collective-permute-start(bf16[5,2,12,64,128]{4,3,2,1,0:T(8,128)(2,1)S(1)} %get-tuple-element.93), channel_id=1, source_target_pairs={{0,8},{1,9},{2,10},{3,11},{4,12},{5,13},{6,14},{7,15},{8,0},{9,1},... | collective-permute-start | bytes 5898248 | tf_op jit(solution)/shard_map/ppermute | solution.py:209
  23.7 18.0 %collective-permute-start.7 = (bf16[2,12,64,128]{3,2,1,0:T(8,128)(2,1)S(1)}, bf16[2,12,64,128]{3,2,1,0:T(8,128)(2,1)S(1)}, u32[]{:S(2)}, u32[]{:S(2)}) collective-permute-start(bf16[2,12,64,128]{3,2,1,0:T(8,128)(2,1)S(1)} %collective-permute-done.refs_4_.refs_0_), channel_id=1, source_target_pairs={{0,2},{1,3},{2,0},{3,1},{4,6},{5,7},{6,4},{7,5},{8,10},{9,11},{10,... | collective-permute-start | bytes 1179656 | tf_op jit(solution)/shard_map/ppermute | solution.py:209
  25.2 22.0 %collective-permute-start.10 = (bf16[2,2,12,64,128]{4,3,2,1,0:T(8,128)(2,1)S(1)}, bf16[2,2,12,64,128]{4,3,2,1,0:T(8,128)(2,1)S(1)}, u32[]{:S(2)}, u32[]{:S(2)}) collective-permute-start(bf16[2,2,12,64,128]{4,3,2,1,0:T(8,128)(2,1)S(1)} %get-tuple-element.106), channel_id=1, source_target_pairs={{0,1},{1,0},{2,3},{3,2},{4,5},{5,4},{6,7},{7,6},{8,24},{9,25},{10,... | collective-permute-start | bytes 2359304 | tf_op jit(solution)/shard_map/ppermute | solution.py:209
  25.7 21.5 %collective-permute-start.9 = (bf16[2,2,12,64,128]{4,3,2,1,0:T(8,128)(2,1)S(1)}, bf16[2,2,12,64,128]{4,3,2,1,0:T(8,128)(2,1)S(1)}, u32[]{:S(2)}, u32[]{:S(2)}) collective-permute-start(bf16[2,2,12,64,128]{4,3,2,1,0:T(8,128)(2,1)S(1)} %get-tuple-element.106), channel_id=1, source_target_pairs={{0,16},{1,17},{2,18},{3,19},{4,20},{5,21},{6,22},{7,23},{8,9},{9,8... | collective-permute-start | bytes 2359304 | tf_op jit(solution)/shard_map/ppermute | solution.py:209
  27.2 20.0 %collective-permute-start.8 = (bf16[2,12,64,128]{3,2,1,0:T(8,128)(2,1)S(1)}, bf16[2,12,64,128]{3,2,1,0:T(8,128)(2,1)S(1)}, u32[]{:S(2)}, u32[]{:S(2)}) collective-permute-start(bf16[2,12,64,128]{3,2,1,0:T(8,128)(2,1)S(1)} %collective-permute-done.4.refs_2_.refs_4_), channel_id=1, source_target_pairs={{0,4},{1,5},{2,6},{3,7},{4,0},{5,1},{6,2},{7,3},{8,12},{9,13},{10,... | collective-permute-start | bytes 1179656 | tf_op jit(solution)/shard_map/ppermute | solution.py:209
  29.5 1.0 %copy-start.1 = (bf16[2,1,64,12,128]{4,2,3,1,0:T(8,128)(2,1)S(1)}, bf16[2,1,64,12,128]{4,2,3,1,0:T(8,128)(2,1)}, u32[]{:S(2)}) copy-start(bf16[2,1,64,12,128]{4,2,3,1,0:T(8,128)(2,1)} %param.2) | copy-start | bytes 1179652
  41.6 12.4 %collective-permute-start.11 = (bf16[2,12,64,128]{3,2,1,0:T(8,128)(2,1)S(1)}, bf16[2,12,64,128]{3,2,1,0:T(8,128)(2,1)S(1)}, u32[]{:S(2)}, u32[]{:S(2)}) collective-permute-start(bf16[2,12,64,128]{3,2,1,0:T(8,128)(2,1)S(1)} %collective-permute-done.7.refs_0_.o3_ref.refs_2_), channel_id=1, source_target_pairs={{0,16},{1,17},{2,18},{3,19},{4,20},{5,21},{6,22},{7,23},{8,9},{9,8... | collective-permute-start | bytes 1179656 | tf_op jit(solution)/shard_map/ppermute | solution.py:209
  44.1 10.0 %collective-permute-start.12 = (bf16[2,12,64,128]{3,2,1,0:T(8,128)(2,1)S(1)}, bf16[2,12,64,128]{3,2,1,0:T(8,128)(2,1)S(1)}, u32[]{:S(2)}, u32[]{:S(2)}) collective-permute-start(bf16[2,12,64,128]{3,2,1,0:T(8,128)(2,1)S(1)} %collective-permute-done.7.refs_0_.o3_ref.refs_2_), channel_id=1, source_target_pairs={{0,1},{1,0},{2,3},{3,2},{4,5},{5,4},{6,7},{7,6},{8,24},{9,25},{10,... | collective-permute-start | bytes 1179656 | tf_op jit(solution)/shard_map/ppermute | solution.py:209
  47.2 11.1 %collective-permute-start.13 = (bf16[2,12,64,128]{3,2,1,0:T(8,128)(2,1)S(1)}, bf16[2,12,64,128]{3,2,1,0:T(8,128)(2,1)S(1)}, u32[]{:S(2)}, u32[]{:S(2)}) collective-permute-start(bf16[2,12,64,128]{3,2,1,0:T(8,128)(2,1)S(1)} %collective-permute-done.8.ab2_ref.refs_2_), channel_id=1, source_target_pairs={{0,2},{1,3},{2,0},{3,1},{4,6},{5,7},{6,4},{7,5},{8,10},{9,11},{10,... | collective-permute-start | bytes 1179656 | tf_op jit(solution)/shard_map/ppermute | solution.py:209
  47.4 6.8 %collective-permute-start.15 = (bf16[6,2,12,64,128]{4,3,2,1,0:T(8,128)(2,1)S(1)}, bf16[6,2,12,64,128]{4,3,2,1,0:T(8,128)(2,1)S(1)}, u32[]{:S(2)}, u32[]{:S(2)}) collective-permute-start(bf16[6,2,12,64,128]{4,3,2,1,0:T(8,128)(2,1)S(1)} %get-tuple-element.132), channel_id=1, source_target_pairs={{0,8},{1,9},{2,10},{3,11},{4,12},{5,13},{6,14},{7,15},{8,0},{9,1},... | collective-permute-start | bytes 7077896 | tf_op jit(solution)/shard_map/ppermute | solution.py:209
  47.4 10.8 %collective-permute-start.14 = (bf16[2,12,64,128]{3,2,1,0:T(8,128)(2,1)S(1)}, bf16[2,12,64,128]{3,2,1,0:T(8,128)(2,1)S(1)}, u32[]{:S(2)}, u32[]{:S(2)}) collective-permute-start(bf16[2,12,64,128]{3,2,1,0:T(8,128)(2,1)S(1)} %get-tuple-element.131), channel_id=1, source_target_pairs={{0,1},{1,0},{2,3},{3,2},{4,5},{5,4},{6,7},{7,6},{8,24},{9,25},{10,... | collective-permute-start | bytes 1179656 | tf_op jit(solution)/shard_map/ppermute | solution.py:209
  54.1 4.7 %collective-permute-start.16 = (bf16[2,2,12,64,128]{4,3,2,1,0:T(8,128)(2,1)S(1)}, bf16[2,2,12,64,128]{4,3,2,1,0:T(8,128)(2,1)S(1)}, u32[]{:S(2)}, u32[]{:S(2)}) collective-permute-start(bf16[2,2,12,64,128]{4,3,2,1,0:T(8,128)(2,1)S(1)} %shard_map.34.refs_5_.refs_3_), channel_id=1, source_target_pairs={{0,8},{1,9},{2,10},{3,11},{4,12},{5,13},{6,14},{7,15},{8,0},{9,1},... | collective-permute-start | bytes 2359304 | tf_op jit(solution)/shard_map/ppermute | solution.py:209
  58.2 2.7 %collective-permute-start.17 = (bf16[2,12,64,128]{3,2,1,0:T(8,128)(2,1)S(1)}, bf16[2,12,64,128]{3,2,1,0:T(8,128)(2,1)S(1)}, u32[]{:S(2)}, u32[]{:S(2)}) collective-permute-start(bf16[2,12,64,128]{3,2,1,0:T(8,128)(2,1)S(1)} %collective-permute-done.13.refs_4_), channel_id=1, source_target_pairs={{0,8},{1,9},{2,10},{3,11},{4,12},{5,13},{6,14},{7,15},{8,0},{9,1},... | collective-permute-start | bytes 1179656 | tf_op jit(solution)/shard_map/ppermute | solution.py:209
  58.2 2.7 %collective-permute-start.18 = (bf16[2,12,64,128]{3,2,1,0:T(8,128)(2,1)S(1)}, bf16[2,12,64,128]{3,2,1,0:T(8,128)(2,1)S(1)}, u32[]{:S(2)}, u32[]{:S(2)}) collective-permute-start(bf16[2,12,64,128]{3,2,1,0:T(8,128)(2,1)S(1)} %collective-permute-done.14.refs_5_), channel_id=1, source_target_pairs={{0,8},{1,9},{2,10},{3,11},{4,12},{5,13},{6,14},{7,15},{8,0},{9,1},... | collective-permute-start | bytes 1179656 | tf_op jit(solution)/shard_map/ppermute | solution.py:209

commit v21 on v18

--- a/solution.py
+++ b/solution.py
@@ -321,7 +321,7 @@
     totals = fence(totals)
 
     a3, b3 = hop_a(near("O", 3)), hop_b(near("O", 3))
-    totals = add([("near", "O", 3)], totals, weight=45)
+    totals = add([("near", "O", 3)], totals)
     put("2d", ab2, "near", [("AB", 2)])
     put("2e", a12, "near", [("A", 1), ("A", 2)])
     put("2f", b12, "near", [("B", 1), ("B", 2)])

time: 62.6 us -> 63.8 us (1.019)
  waiting for transfers between devices: 26.4 us -> 27.5 us
    ppermute x19, waiting for transfers between devices: 26.4 us -> 27.5 us  [move(): return lax.ppermute(array, AXES, pairs)]
  transfers between devices with their start and end apart: 19 -> 19, of which waited for: 7 -> 6; matrix products, arithmetic and copies ran while one was open for 0% -> 0% of each run, Pallas kernels for 16% -> 16%
where the time goes in v21:
time: 63.8 us; the launch traced here: 63.6 us
  waiting for transfers between devices  27.5 us (43%)
  starting transfers between devices  22.6 us (35%)
  Pallas kernels  12 us (19%)
  local copies, waits for them, and re-layouts  1.01 us (2%)
    ppermute x19, waiting for transfers between devices, move(): return lax.ppermute(array, AXES, pairs)  27.5 us
    ppermute x19, starting transfers between devices, move(): return lax.ppermute(array, AXES, pairs)  22.6 us
    pallas_call x7, Pallas kernels, add(): pl.pallas_call(functools.partial(add_shards, tuple(names), places, slots,...  11.6 us
  transfers between devices with their start and end apart: 19, of which 6 were waited for; matrix products, arithmetic and copies ran while one was open for 0% of the time, Pallas kernels for 16%

profile of v21, /device:TPU:0, one launch (start us, length us, event | category | flops | bytes accessed | tf_op | source)
XLA Modules:
  0.0 63.6 jit_solution(6304716528571333176)
XLA Ops:
  0.0 0.0 copy-start
  0.0 2.9 %collective-permute-start.1 = (bf16[2,12,64,128]{3,2,1,0:T(8,128)(2,1)}, bf16[2,12,64,128]{3,2,1,0:T(8,128)(2,1)S(1)}, u32[]{:S(2)}, u32[]{:S(2)}) collective-permute-start(bf16[2,12,64,128]{3,2,1,0:T(8,128)(2,1)} %bitcast.24), channel_id=1, source_target_pairs={{0,16},{1,17},{2,18},{3,19},{4,20},{5,21},{6,22},{7,23},{8,9},{9,8... | collective-permute-start | bytes 1179656 | tf_op jit(solution)/shard_map/ppermute | solution.py:208
  2.9 2.6 %collective-permute-start = (bf16[2,12,64,128]{3,2,1,0:T(8,128)(2,1)}, bf16[2,12,64,128]{3,2,1,0:T(8,128)(2,1)S(1)}, u32[]{:S(2)}, u32[]{:S(2)}) collective-permute-start(bf16[2,12,64,128]{3,2,1,0:T(8,128)(2,1)} %bitcast.25), channel_id=1, source_target_pairs={{0,4},{1,5},{2,6},{3,7},{4,0},{5,1},{6,2},{7,3},{8,12},{9,13},{10,... | collective-permute-start | bytes 1179656 | tf_op jit(solution)/shard_map/ppermute | solution.py:208
  5.5 1.6 %collective-permute-start.2 = (bf16[2,12,64,128]{3,2,1,0:T(8,128)(2,1)}, bf16[2,12,64,128]{3,2,1,0:T(8,128)(2,1)S(1)}, u32[]{:S(2)}, u32[]{:S(2)}) collective-permute-start(bf16[2,12,64,128]{3,2,1,0:T(8,128)(2,1)} %bitcast.26), channel_id=1, source_target_pairs={{0,2},{1,3},{2,0},{3,1},{4,6},{5,7},{6,4},{7,5},{8,10},{9,11},{10,... | collective-permute-start | bytes 1179656 | tf_op jit(solution)/shard_map/ppermute | solution.py:208
  7.1 1.5 %collective-permute-start.3 = (bf16[2,12,64,128]{3,2,1,0:T(8,128)(2,1)}, bf16[2,12,64,128]{3,2,1,0:T(8,128)(2,1)S(1)}, u32[]{:S(2)}, u32[]{:S(2)}) collective-permute-start(bf16[2,12,64,128]{3,2,1,0:T(8,128)(2,1)} %bitcast.27), channel_id=1, source_target_pairs={{0,1},{1,0},{2,3},{3,2},{4,5},{5,4},{6,7},{7,6},{8,24},{9,25},{10,... | collective-permute-start | bytes 1179656 | tf_op jit(solution)/shard_map/ppermute | solution.py:208
  8.6 0.0 collective-permute-start.5
  8.6 0.0 copy-done
  8.7 0.1 fusion
  8.8 0.2 collective-permute-done.1.refs_0_.refs_1_
  9.0 3.4 %collective-permute-start.4 = (bf16[2,12,64,128]{3,2,1,0:T(8,128)(2,1)S(1)}, bf16[2,12,64,128]{3,2,1,0:T(8,128)(2,1)S(1)}, u32[]{:S(2)}, u32[]{:S(2)}) collective-permute-start(bf16[2,12,64,128]{3,2,1,0:T(8,128)(2,1)S(1)} %collective-permute-done.1.refs_0_.refs_1_), channel_id=1, source_target_pairs={{0,1},{1,0},{2,3},{3,2},{4,5},{5,4},{6,7},{7,6},{8,24},{9,25},{10,... | collective-permute-start | bytes 1179656 | tf_op jit(solution)/shard_map/ppermute | solution.py:208
  12.4 0.1 multiply_cosine_fusion
  12.6 10.6 %collective-permute-done.refs_4_.refs_0_ = bf16[2,12,64,128]{3,2,1,0:T(8,128)(2,1)S(1)} collective-permute-done((bf16[2,12,64,128]{3,2,1,0:T(8,128)(2,1)}, bf16[2,12,64,128]{3,2,1,0:T(8,128)(2,1)S(1)}, u32[]{:S(2)}, u32[]{:S(2)}) %collective-permute-start) | collective-permute-done | bytes 393248 | tf_op jit(solution)/shard_map/ppermute | solution.py:208
  23.2 0.2 collective-permute-done.2.refs_3_.refs_2_.refs_1_
  23.4 0.0 collective-permute-done.3.refs_1_.refs_3_
  23.4 0.0 collective-permute-done.5.refs_4_
  23.4 0.0 collective-permute-done.4.refs_2_.refs_4_
  23.4 0.0 copy-start.2
  23.4 0.2 shard_map.28
  23.6 0.1 collective-permute-start.6
  23.7 0.5 collective-permute-start.10
  24.2 1.5 %collective-permute-start.9 = (bf16[2,2,12,64,128]{4,3,2,1,0:T(8,128)(2,1)S(1)}, bf16[2,2,12,64,128]{4,3,2,1,0:T(8,128)(2,1)S(1)}, u32[]{:S(2)}, u32[]{:S(2)}) collective-permute-start(bf16[2,2,12,64,128]{4,3,2,1,0:T(8,128)(2,1)S(1)} %get-tuple-element.106), channel_id=1, source_target_pairs={{0,16},{1,17},{2,18},{3,19},{4,20},{5,21},{6,22},{7,23},{8,9},{9,8... | collective-permute-start | bytes 2359304 | tf_op jit(solution)/shard_map/ppermute | solution.py:208
  25.7 1.4 %collective-permute-start.7 = (bf16[2,12,64,128]{3,2,1,0:T(8,128)(2,1)S(1)}, bf16[2,12,64,128]{3,2,1,0:T(8,128)(2,1)S(1)}, u32[]{:S(2)}, u32[]{:S(2)}) collective-permute-start(bf16[2,12,64,128]{3,2,1,0:T(8,128)(2,1)S(1)} %collective-permute-done.refs_4_.refs_0_), channel_id=1, source_target_pairs={{0,2},{1,3},{2,0},{3,1},{4,6},{5,7},{6,4},{7,5},{8,10},{9,11},{10,... | collective-permute-start | bytes 1179656 | tf_op jit(solution)/shard_map/ppermute | solution.py:208
  27.2 2.3 %collective-permute-start.8 = (bf16[2,12,64,128]{3,2,1,0:T(8,128)(2,1)S(1)}, bf16[2,12,64,128]{3,2,1,0:T(8,128)(2,1)S(1)}, u32[]{:S(2)}, u32[]{:S(2)}) collective-permute-start(bf16[2,12,64,128]{3,2,1,0:T(8,128)(2,1)S(1)} %collective-permute-done.4.refs_2_.refs_4_), channel_id=1, source_target_pairs={{0,4},{1,5},{2,6},{3,7},{4,0},{5,1},{6,2},{7,3},{8,12},{9,13},{10,... | collective-permute-start | bytes 1179656 | tf_op jit(solution)/shard_map/ppermute | solution.py:208
  29.5 0.0 copy-start.1
  29.5 1.0 %copy-done.1 = bf16[2,1,64,12,128]{4,2,3,1,0:T(8,128)(2,1)S(1)} copy-done((bf16[2,1,64,12,128]{4,2,3,1,0:T(8,128)(2,1)S(1)}, bf16[2,1,64,12,128]{4,2,3,1,0:T(8,128)(2,1)}, u32[]{:S(2)}) %copy-start.1) | copy-done | bytes 393240
  30.5 1.8 %shard_map.29.refs_7_ = f32[2,2,256,256]{3,2,1,0:T(8,128)S(1)} custom-call(f32[8,2,128]{2,1,0:T(2,128)S(1)} %maximum_bitcast_fusion.weights_ref, bf16[2,12,64,128]{3,2,1,0:T(8,128)(2,1)S(1)} %collective-permute-done.refs_4_.refs_0_, bf16[2,12,64,128]{3,2,1,0:T(8,128)(2,1)S(1)} %collective-permute-done.1.refs_0_.refs_1_, ...), custom_call_target="tpu_custom_call" | custom-call | flops 1207959552 | bytes 4456448 | tf_op jit(solution)/shard_map/pallas_call | solution.py:263
  32.3 0.0 collective-permute-done.6.refs_5_
  32.3 0.0 copy-done.2
  32.3 1.7 %shard_map.30.refs_1_ = f32[2,2,256,256]{3,2,1,0:T(8,128)S(1)} custom-call(f32[8,2,128]{2,1,0:T(2,128)S(1)} %maximum_bitcast_fusion.weights_ref, bf16[2,12,64,128]{3,2,1,0:T(8,128)(2,1)S(1)} %collective-permute-done.refs_4_.refs_0_, bf16[2,12,64,128]{3,2,1,0:T(8,128)(2,1)S(1)} %collective-permute-done.1.refs_0_.refs_1_, ...), custom_call_target="tpu_custom_call" | custom-call | flops 1207959552 | bytes 4456448 | tf_op jit(solution)/shard_map/pallas_call | solution.py:263
  34.0 10.5 %collective-permute-done.7.refs_0_.o3_ref.refs_2_ = bf16[2,12,64,128]{3,2,1,0:T(8,128)(2,1)S(1)} collective-permute-done((bf16[2,12,64,128]{3,2,1,0:T(8,128)(2,1)S(1)}, bf16[2,12,64,128]{3,2,1,0:T(8,128)(2,1)S(1)}, u32[]{:S(2)}, u32[]{:S(2)}) %collective-permute-start.7) | collective-permute-done | bytes 393248 | tf_op jit(solution)/shard_map/ppermute | solution.py:208
  44.5 0.5 collective-permute-start.11
  45.0 1.6 %collective-permute-start.12 = (bf16[2,12,64,128]{3,2,1,0:T(8,128)(2,1)S(1)}, bf16[2,12,64,128]{3,2,1,0:T(8,128)(2,1)S(1)}, u32[]{:S(2)}, u32[]{:S(2)}) collective-permute-start(bf16[2,12,64,128]{3,2,1,0:T(8,128)(2,1)S(1)} %collective-permute-done.7.refs_0_.o3_ref.refs_2_), channel_id=1, source_target_pairs={{0,1},{1,0},{2,3},{3,2},{4,5},{5,4},{6,7},{7,6},{8,24},{9,25},{10,... | collective-permute-start | bytes 1179656 | tf_op jit(solution)/shard_map/ppermute | solution.py:208
  46.6 0.4 shard_map.31.refs_5_
  47.0 0.2 collective-permute-done.8.ab2_ref.refs_2_
  47.2 0.0 collective-permute-done.10.b12_ref.refs_4_.refs_2_
  47.2 0.0 collective-permute-done.9.a12_ref.refs_3_.refs_1_
  47.2 0.0 collective-permute-start.13
  47.2 0.2 shard_map.32
  47.4 0.1 collective-permute-start.15
  47.4 1.6 %collective-permute-start.14 = (bf16[2,12,64,128]{3,2,1,0:T(8,128)(2,1)S(1)}, bf16[2,12,64,128]{3,2,1,0:T(8,128)(2,1)S(1)}, u32[]{:S(2)}, u32[]{:S(2)}) collective-permute-start(bf16[2,12,64,128]{3,2,1,0:T(8,128)(2,1)S(1)} %get-tuple-element.131), channel_id=1, source_target_pairs={{0,1},{1,0},{2,3},{3,2},{4,5},{5,4},{6,7},{7,6},{8,24},{9,25},{10,... | collective-permute-start | bytes 1179656 | tf_op jit(solution)/shard_map/ppermute | solution.py:208
  49.0 1.6 %shard_map.33.refs_7_ = f32[2,2,256,256]{3,2,1,0:T(8,128)S(1)} custom-call(f32[8,2,128]{2,1,0:T(2,128)S(1)} %maximum_bitcast_fusion.weights_ref, bf16[2,12,64,128]{3,2,1,0:T(8,128)(2,1)S(1)} %collective-permute-done.refs_4_.refs_0_, bf16[2,12,64,128]{3,2,1,0:T(8,128)(2,1)S(1)} %collective-permute-done.2.refs_3_.refs_2_.refs_1_, ...), custom_call_target="tpu_custom_call" | custom-call | flops 1006632960 | bytes 4063232 | tf_op jit(solution)/shard_map/pallas_call | solution.py:263
  50.7 5.8 %collective-permute-done.11.a3_ref = bf16[2,12,64,128]{3,2,1,0:T(8,128)(2,1)S(1)} collective-permute-done((bf16[2,12,64,128]{3,2,1,0:T(8,128)(2,1)S(1)}, bf16[2,12,64,128]{3,2,1,0:T(8,128)(2,1)S(1)}, u32[]{:S(2)}, u32[]{:S(2)}) %collective-permute-start.11) | collective-permute-done | bytes 393248 | tf_op jit(solution)/shard_map/ppermute | solution.py:208
  56.5 0.0 collective-permute-done.12.ab3_ref
  56.5 0.1 shard_map.34.refs_5_.refs_3_
  56.5 0.1 collective-permute-start.16
  56.6 0.0 collective-permute-done.15.refs_6_
  56.6 2.3 %shard_map.35.refs_7_ = f32[2,2,256,256]{3,2,1,0:T(8,128)S(1)} custom-call(f32[8,2,128]{2,1,0:T(2,128)S(1)} %maximum_bitcast_fusion.weights_ref, bf16[2,12,64,128]{3,2,1,0:T(8,128)(2,1)S(1)} %collective-permute-done.refs_4_.refs_0_, bf16[2,12,64,128]{3,2,1,0:T(8,128)(2,1)S(1)} %collective-permute-done.2.refs_3_.refs_2_.refs_1_, ...), custom_call_target="tpu_custom_call" | custom-call | flops 16106127360 | bytes 5242880 | tf_op jit(solution)/shard_map/pallas_call | solution.py:263
  58.9 0.0 collective-permute-done.14.refs_5_
  58.9 0.0 collective-permute-done.13.refs_4_
  58.9 0.9 %collective-permute-start.17 = (bf16[2,12,64,128]{3,2,1,0:T(8,128)(2,1)S(1)}, bf16[2,12,64,128]{3,2,1,0:T(8,128)(2,1)S(1)}, u32[]{:S(2)}, u32[]{:S(2)}) collective-permute-start(bf16[2,12,64,128]{3,2,1,0:T(8,128)(2,1)S(1)} %collective-permute-done.13.refs_4_), channel_id=1, source_target_pairs={{0,8},{1,9},{2,10},{3,11},{4,12},{5,13},{6,14},{7,15},{8,0},{9,1},... | collective-permute-start | bytes 1179656 | tf_op jit(solution)/shard_map/ppermute | solution.py:208
  59.8 0.0 collective-permute-start.18
  59.8 0.0 collective-permute-done.16.refs_6_
  59.8 2.2 %shard_map.36 = (f32[2,2,256,256]{3,2,1,0:T(8,128)S(1)}, f32[16,64,256]{2,1,0:T(8,128)}, bf16[3,512,768]{2,1,0:T(8,128)(2,1)S(1)}) custom-call(f32[8,2,128]{2,1,0:T(2,128)S(1)} %maximum_bitcast_fusion.weights_ref, bf16[2,12,64,128]{3,2,1,0:T(8,128)(2,1)S(1)} %collective-permute-done.7.refs_0_.o3_ref.refs_2_, ...), custom_call_target="tpu_custom_call" | custom-call | flops 805306368 | bytes 3670016 | tf_op jit(solution)/shard_map/pallas_call | solution.py:263
  62.0 0.0 collective-permute-done.17.refs_0_
  62.0 0.0 collective-permute-done.18.refs_1_
  62.0 1.5 %shard_map.37 = f32[16,64,256]{2,1,0:T(8,128)} custom-call(f32[8,2,128]{2,1,0:T(2,128)S(1)} %maximum_bitcast_fusion.weights_ref, bf16[2,12,64,128]{3,2,1,0:T(8,128)(2,1)S(1)} %collective-permute-done.17.refs_0_, bf16[2,12,64,128]{3,2,1,0:T(8,128)(2,1)S(1)} %collective-permute-done.18.refs_1_, ...), custom_call_target="tpu_custom_call", output_to_operand_aliasing={{}: (5, {})} | custom-call | flops 402653184 | bytes 2883584 | tf_op jit(solution)/shard_map/pallas_call | solution.py:263
  (5 shorter events, 0.1 us)
Async XLA Ops:
  0.0 8.6 %copy-start = (s32[4,3]{1,0:T(4,128)S(1)}, s32[4,3]{1,0:T(4,128)}, u32[]{:S(2)}) copy-start(s32[4,3]{1,0:T(4,128)} %param.3) | copy-start | bytes 148
  0.0 9.0 %collective-permute-start.1 = (bf16[2,12,64,128]{3,2,1,0:T(8,128)(2,1)}, bf16[2,12,64,128]{3,2,1,0:T(8,128)(2,1)S(1)}, u32[]{:S(2)}, u32[]{:S(2)}) collective-permute-start(bf16[2,12,64,128]{3,2,1,0:T(8,128)(2,1)} %bitcast.24), channel_id=1, source_target_pairs={{0,16},{1,17},{2,18},{3,19},{4,20},{5,21},{6,22},{7,23},{8,9},{9,8... | collective-permute-start | bytes 1179656 | tf_op jit(solution)/shard_map/ppermute | solution.py:208
  2.9 20.3 %collective-permute-start = (bf16[2,12,64,128]{3,2,1,0:T(8,128)(2,1)}, bf16[2,12,64,128]{3,2,1,0:T(8,128)(2,1)S(1)}, u32[]{:S(2)}, u32[]{:S(2)}) collective-permute-start(bf16[2,12,64,128]{3,2,1,0:T(8,128)(2,1)} %bitcast.25), channel_id=1, source_target_pairs={{0,4},{1,5},{2,6},{3,7},{4,0},{5,1},{6,2},{7,3},{8,12},{9,13},{10,... | collective-permute-start | bytes 1179656 | tf_op jit(solution)/shard_map/ppermute | solution.py:208
  5.5 17.8 %collective-permute-start.2 = (bf16[2,12,64,128]{3,2,1,0:T(8,128)(2,1)}, bf16[2,12,64,128]{3,2,1,0:T(8,128)(2,1)S(1)}, u32[]{:S(2)}, u32[]{:S(2)}) collective-permute-start(bf16[2,12,64,128]{3,2,1,0:T(8,128)(2,1)} %bitcast.26), channel_id=1, source_target_pairs={{0,2},{1,3},{2,0},{3,1},{4,6},{5,7},{6,4},{7,5},{8,10},{9,11},{10,... | collective-permute-start | bytes 1179656 | tf_op jit(solution)/shard_map/ppermute | solution.py:208
  7.1 16.3 %collective-permute-start.3 = (bf16[2,12,64,128]{3,2,1,0:T(8,128)(2,1)}, bf16[2,12,64,128]{3,2,1,0:T(8,128)(2,1)S(1)}, u32[]{:S(2)}, u32[]{:S(2)}) collective-permute-start(bf16[2,12,64,128]{3,2,1,0:T(8,128)(2,1)} %bitcast.27), channel_id=1, source_target_pairs={{0,1},{1,0},{2,3},{3,2},{4,5},{5,4},{6,7},{7,6},{8,24},{9,25},{10,... | collective-permute-start | bytes 1179656 | tf_op jit(solution)/shard_map/ppermute | solution.py:208
  8.6 14.8 %collective-permute-start.5 = (bf16[2,12,64,128]{3,2,1,0:T(8,128)(2,1)}, bf16[2,12,64,128]{3,2,1,0:T(8,128)(2,1)S(1)}, u32[]{:S(2)}, u32[]{:S(2)}) collective-permute-start(bf16[2,12,64,128]{3,2,1,0:T(8,128)(2,1)} %bitcast.28), channel_id=1, source_target_pairs={{0,8},{1,9},{2,10},{3,11},{4,12},{5,13},{6,14},{7,15},{8,0},{9,1},... | collective-permute-start | bytes 1179656 | tf_op jit(solution)/shard_map/ppermute | solution.py:208
  9.0 14.4 %collective-permute-start.4 = (bf16[2,12,64,128]{3,2,1,0:T(8,128)(2,1)S(1)}, bf16[2,12,64,128]{3,2,1,0:T(8,128)(2,1)S(1)}, u32[]{:S(2)}, u32[]{:S(2)}) collective-permute-start(bf16[2,12,64,128]{3,2,1,0:T(8,128)(2,1)S(1)} %collective-permute-done.1.refs_0_.refs_1_), channel_id=1, source_target_pairs={{0,1},{1,0},{2,3},{3,2},{4,5},{5,4},{6,7},{7,6},{8,24},{9,25},{10,... | collective-permute-start | bytes 1179656 | tf_op jit(solution)/shard_map/ppermute | solution.py:208
  23.4 8.9 %copy-start.2 = (bf16[2,1,64,12,128]{4,2,3,1,0:T(8,128)(2,1)S(1)}, bf16[2,1,64,12,128]{4,2,3,1,0:T(8,128)(2,1)}, u32[]{:S(2)}) copy-start(bf16[2,1,64,12,128]{4,2,3,1,0:T(8,128)(2,1)} %param.2) | copy-start | bytes 1179652
  23.6 8.7 %collective-permute-start.6 = (bf16[5,2,12,64,128]{4,3,2,1,0:T(8,128)(2,1)S(1)}, bf16[5,2,12,64,128]{4,3,2,1,0:T(8,128)(2,1)S(1)}, u32[]{:S(2)}, u32[]{:S(2)}) collective-permute-start(bf16[5,2,12,64,128]{4,3,2,1,0:T(8,128)(2,1)S(1)} %get-tuple-element.93), channel_id=1, source_target_pairs={{0,8},{1,9},{2,10},{3,11},{4,12},{5,13},{6,14},{7,15},{8,0},{9,1},... | collective-permute-start | bytes 5898248 | tf_op jit(solution)/shard_map/ppermute | solution.py:208
  23.7 23.5 %collective-permute-start.10 = (bf16[2,2,12,64,128]{4,3,2,1,0:T(8,128)(2,1)S(1)}, bf16[2,2,12,64,128]{4,3,2,1,0:T(8,128)(2,1)S(1)}, u32[]{:S(2)}, u32[]{:S(2)}) collective-permute-start(bf16[2,2,12,64,128]{4,3,2,1,0:T(8,128)(2,1)S(1)} %get-tuple-element.106), channel_id=1, source_target_pairs={{0,1},{1,0},{2,3},{3,2},{4,5},{5,4},{6,7},{7,6},{8,24},{9,25},{10,... | collective-permute-start | bytes 2359304 | tf_op jit(solution)/shard_map/ppermute | solution.py:208
  24.2 23.0 %collective-permute-start.9 = (bf16[2,2,12,64,128]{4,3,2,1,0:T(8,128)(2,1)S(1)}, bf16[2,2,12,64,128]{4,3,2,1,0:T(8,128)(2,1)S(1)}, u32[]{:S(2)}, u32[]{:S(2)}) collective-permute-start(bf16[2,2,12,64,128]{4,3,2,1,0:T(8,128)(2,1)S(1)} %get-tuple-element.106), channel_id=1, source_target_pairs={{0,16},{1,17},{2,18},{3,19},{4,20},{5,21},{6,22},{7,23},{8,9},{9,8... | collective-permute-start | bytes 2359304 | tf_op jit(solution)/shard_map/ppermute | solution.py:208
  25.7 18.8 %collective-permute-start.7 = (bf16[2,12,64,128]{3,2,1,0:T(8,128)(2,1)S(1)}, bf16[2,12,64,128]{3,2,1,0:T(8,128)(2,1)S(1)}, u32[]{:S(2)}, u32[]{:S(2)}) collective-permute-start(bf16[2,12,64,128]{3,2,1,0:T(8,128)(2,1)S(1)} %collective-permute-done.refs_4_.refs_0_), channel_id=1, source_target_pairs={{0,2},{1,3},{2,0},{3,1},{4,6},{5,7},{6,4},{7,5},{8,10},{9,11},{10,... | collective-permute-start | bytes 1179656 | tf_op jit(solution)/shard_map/ppermute | solution.py:208
  27.2 20.0 %collective-permute-start.8 = (bf16[2,12,64,128]{3,2,1,0:T(8,128)(2,1)S(1)}, bf16[2,12,64,128]{3,2,1,0:T(8,128)(2,1)S(1)}, u32[]{:S(2)}, u32[]{:S(2)}) collective-permute-start(bf16[2,12,64,128]{3,2,1,0:T(8,128)(2,1)S(1)} %collective-permute-done.4.refs_2_.refs_4_), channel_id=1, source_target_pairs={{0,4},{1,5},{2,6},{3,7},{4,0},{5,1},{6,2},{7,3},{8,12},{9,13},{10,... | collective-permute-start | bytes 1179656 | tf_op jit(solution)/shard_map/ppermute | solution.py:208
  29.5 1.0 %copy-start.1 = (bf16[2,1,64,12,128]{4,2,3,1,0:T(8,128)(2,1)S(1)}, bf16[2,1,64,12,128]{4,2,3,1,0:T(8,128)(2,1)}, u32[]{:S(2)}) copy-start(bf16[2,1,64,12,128]{4,2,3,1,0:T(8,128)(2,1)} %param.2) | copy-start | bytes 1179652
  44.5 11.9 %collective-permute-start.11 = (bf16[2,12,64,128]{3,2,1,0:T(8,128)(2,1)S(1)}, bf16[2,12,64,128]{3,2,1,0:T(8,128)(2,1)S(1)}, u32[]{:S(2)}, u32[]{:S(2)}) collective-permute-start(bf16[2,12,64,128]{3,2,1,0:T(8,128)(2,1)S(1)} %collective-permute-done.7.refs_0_.o3_ref.refs_2_), channel_id=1, source_target_pairs={{0,16},{1,17},{2,18},{3,19},{4,20},{5,21},{6,22},{7,23},{8,9},{9,8... | collective-permute-start | bytes 1179656 | tf_op jit(solution)/shard_map/ppermute | solution.py:208
  45.0 11.5 %collective-permute-start.12 = (bf16[2,12,64,128]{3,2,1,0:T(8,128)(2,1)S(1)}, bf16[2,12,64,128]{3,2,1,0:T(8,128)(2,1)S(1)}, u32[]{:S(2)}, u32[]{:S(2)}) collective-permute-start(bf16[2,12,64,128]{3,2,1,0:T(8,128)(2,1)S(1)} %collective-permute-done.7.refs_0_.o3_ref.refs_2_), channel_id=1, source_target_pairs={{0,1},{1,0},{2,3},{3,2},{4,5},{5,4},{6,7},{7,6},{8,24},{9,25},{10,... | collective-permute-start | bytes 1179656 | tf_op jit(solution)/shard_map/ppermute | solution.py:208
  47.2 11.8 %collective-permute-start.13 = (bf16[2,12,64,128]{3,2,1,0:T(8,128)(2,1)S(1)}, bf16[2,12,64,128]{3,2,1,0:T(8,128)(2,1)S(1)}, u32[]{:S(2)}, u32[]{:S(2)}) collective-permute-start(bf16[2,12,64,128]{3,2,1,0:T(8,128)(2,1)S(1)} %collective-permute-done.8.ab2_ref.refs_2_), channel_id=1, source_target_pairs={{0,2},{1,3},{2,0},{3,1},{4,6},{5,7},{6,4},{7,5},{8,10},{9,11},{10,... | collective-permute-start | bytes 1179656 | tf_op jit(solution)/shard_map/ppermute | solution.py:208
  47.4 9.2 %collective-permute-start.15 = (bf16[6,2,12,64,128]{4,3,2,1,0:T(8,128)(2,1)S(1)}, bf16[6,2,12,64,128]{4,3,2,1,0:T(8,128)(2,1)S(1)}, u32[]{:S(2)}, u32[]{:S(2)}) collective-permute-start(bf16[6,2,12,64,128]{4,3,2,1,0:T(8,128)(2,1)S(1)} %get-tuple-element.132), channel_id=1, source_target_pairs={{0,8},{1,9},{2,10},{3,11},{4,12},{5,13},{6,14},{7,15},{8,0},{9,1},... | collective-permute-start | bytes 7077896 | tf_op jit(solution)/shard_map/ppermute | solution.py:208
  47.4 11.5 %collective-permute-start.14 = (bf16[2,12,64,128]{3,2,1,0:T(8,128)(2,1)S(1)}, bf16[2,12,64,128]{3,2,1,0:T(8,128)(2,1)S(1)}, u32[]{:S(2)}, u32[]{:S(2)}) collective-permute-start(bf16[2,12,64,128]{3,2,1,0:T(8,128)(2,1)S(1)} %get-tuple-element.131), channel_id=1, source_target_pairs={{0,1},{1,0},{2,3},{3,2},{4,5},{5,4},{6,7},{7,6},{8,24},{9,25},{10,... | collective-permute-start | bytes 1179656 | tf_op jit(solution)/shard_map/ppermute | solution.py:208
  56.5 3.3 %collective-permute-start.16 = (bf16[2,2,12,64,128]{4,3,2,1,0:T(8,128)(2,1)S(1)}, bf16[2,2,12,64,128]{4,3,2,1,0:T(8,128)(2,1)S(1)}, u32[]{:S(2)}, u32[]{:S(2)}) collective-permute-start(bf16[2,2,12,64,128]{4,3,2,1,0:T(8,128)(2,1)S(1)} %shard_map.34.refs_5_.refs_3_), channel_id=1, source_target_pairs={{0,8},{1,9},{2,10},{3,11},{4,12},{5,13},{6,14},{7,15},{8,0},{9,1},... | collective-permute-start | bytes 2359304 | tf_op jit(solution)/shard_map/ppermute | solution.py:208
  58.9 3.1 %collective-permute-start.17 = (bf16[2,12,64,128]{3,2,1,0:T(8,128)(2,1)S(1)}, bf16[2,12,64,128]{3,2,1,0:T(8,128)(2,1)S(1)}, u32[]{:S(2)}, u32[]{:S(2)}) collective-permute-start(bf16[2,12,64,128]{3,2,1,0:T(8,128)(2,1)S(1)} %collective-permute-done.13.refs_4_), channel_id=1, source_target_pairs={{0,8},{1,9},{2,10},{3,11},{4,12},{5,13},{6,14},{7,15},{8,0},{9,1},... | collective-permute-start | bytes 1179656 | tf_op jit(solution)/shard_map/ppermute | solution.py:208
  59.8 2.2 %collective-permute-start.18 = (bf16[2,12,64,128]{3,2,1,0:T(8,128)(2,1)S(1)}, bf16[2,12,64,128]{3,2,1,0:T(8,128)(2,1)S(1)}, u32[]{:S(2)}, u32[]{:S(2)}) collective-permute-start(bf16[2,12,64,128]{3,2,1,0:T(8,128)(2,1)S(1)} %collective-permute-done.14.refs_5_), channel_id=1, source_target_pairs={{0,8},{1,9},{2,10},{3,11},{4,12},{5,13},{6,14},{7,15},{8,0},{9,1},... | collective-permute-start | bytes 1179656 | tf_op jit(solution)/shard_map/ppermute | solution.py:208

commit v22 on v20

--- a/solution.py
+++ b/solution.py
@@ -52,8 +52,7 @@
     refs = list(refs)
     left_ref = None if given else refs.pop()
     if half:
-        sems, row_ref, left_ref = left_ref, refs.pop(), refs.pop()
-        field_ref = refs.pop()
+        sems, row_ref, field_ref = (refs.pop() for _ in range(3))
     if last:
         sems, row_ref, far_ref, field_ref, _ = (refs.pop() for _ in range(5))
     else:
@@ -277,7 +276,9 @@
                 transcendentals=0,
             ),
         )(*operands)
-        return (*out[:-1], (slots, out[-1])) if keep else out[0]
+        if keep:
+            return out[0], (slots, out[1])
+        return out if half else out[0]
 
     def fence(totals):
         nonlocal arrays
@@ -339,15 +340,15 @@
     far3 = swap(stack)
     put("3d", far2, "far", second)
     names = [("far", *kind) for kind in second] + [("near", *kind) for kind in third]
-    totals = add(names, totals, weight=10)
+    totals, (slots, left) = add(names, totals, keep=left_slots(names), weight=10)
     put("3b", ab3, "near", fourth[:1])
     put("3c", ab1, "near", fourth[1:])
-    totals = fence(totals)
+    totals, left = fence((totals, left))
 
     far4 = [swap(near(*kind)) for kind in fourth]
     put("4a", far3, "far", third)
     names = [("far", *kind) for kind in third] + [("near", *kind) for kind in fourth]
-    totals, field, (slots, left) = add(names, totals, keep=left_slots(names), half=len(third))
+    totals, field = add(names, totals, left=(slots, left), half=len(third))
     put("4b", far4[0], "far", fourth[:1])
     put("4c", far4[1], "far", fourth[1:])
     totals, left, field = fence((totals, left, field))

time: 62.6 us -> 62.4 us (level)
  transfers between devices with their start and end apart: 19 -> 19, of which waited for: 7 -> 9; matrix products, arithmetic and copies ran while one was open for 0% -> 0% of each run, Pallas kernels for 16% -> 16%
where the time goes in v22:
time: 62.4 us; the launch traced here: 62.3 us
  waiting for transfers between devices  26.1 us (42%)
  starting transfers between devices  22.9 us (37%)
  Pallas kernels  11.8 us (19%)
  local copies, waits for them, and re-layouts  1 us (2%)
    ppermute x19, waiting for transfers between devices, move(): return lax.ppermute(array, AXES, pairs)  26.1 us
    ppermute x19, starting transfers between devices, move(): return lax.ppermute(array, AXES, pairs)  22.9 us
    pallas_call x7, Pallas kernels, add(): pl.pallas_call(functools.partial(add_shards, tuple(names), places, slots,...  11.4 us
  transfers between devices with their start and end apart: 19, of which 9 were waited for; matrix products, arithmetic and copies ran while one was open for 0% of the time, Pallas kernels for 16%

profile of v22, /device:TPU:0, one launch (start us, length us, event | category | flops | bytes accessed | tf_op | source)
XLA Modules:
  0.0 62.3 jit_solution(5056675928417811999)
XLA Ops:
  0.0 0.0 copy-start
  0.0 4.0 %collective-permute-start = (bf16[2,12,64,128]{3,2,1,0:T(8,128)(2,1)}, bf16[2,12,64,128]{3,2,1,0:T(8,128)(2,1)S(1)}, u32[]{:S(2)}, u32[]{:S(2)}) collective-permute-start(bf16[2,12,64,128]{3,2,1,0:T(8,128)(2,1)} %bitcast.24), channel_id=1, source_target_pairs={{0,4},{1,5},{2,6},{3,7},{4,0},{5,1},{6,2},{7,3},{8,12},{9,13},{10,... | collective-permute-start | bytes 1179656 | tf_op jit(solution)/shard_map/ppermute | solution.py:208
  4.0 1.5 %collective-permute-start.1 = (bf16[2,12,64,128]{3,2,1,0:T(8,128)(2,1)}, bf16[2,12,64,128]{3,2,1,0:T(8,128)(2,1)S(1)}, u32[]{:S(2)}, u32[]{:S(2)}) collective-permute-start(bf16[2,12,64,128]{3,2,1,0:T(8,128)(2,1)} %bitcast.25), channel_id=1, source_target_pairs={{0,16},{1,17},{2,18},{3,19},{4,20},{5,21},{6,22},{7,23},{8,9},{9,8... | collective-permute-start | bytes 1179656 | tf_op jit(solution)/shard_map/ppermute | solution.py:208
  5.5 1.6 %collective-permute-start.2 = (bf16[2,12,64,128]{3,2,1,0:T(8,128)(2,1)}, bf16[2,12,64,128]{3,2,1,0:T(8,128)(2,1)S(1)}, u32[]{:S(2)}, u32[]{:S(2)}) collective-permute-start(bf16[2,12,64,128]{3,2,1,0:T(8,128)(2,1)} %bitcast.26), channel_id=1, source_target_pairs={{0,2},{1,3},{2,0},{3,1},{4,6},{5,7},{6,4},{7,5},{8,10},{9,11},{10,... | collective-permute-start | bytes 1179656 | tf_op jit(solution)/shard_map/ppermute | solution.py:208
  7.1 1.5 %collective-permute-start.3 = (bf16[2,12,64,128]{3,2,1,0:T(8,128)(2,1)}, bf16[2,12,64,128]{3,2,1,0:T(8,128)(2,1)S(1)}, u32[]{:S(2)}, u32[]{:S(2)}) collective-permute-start(bf16[2,12,64,128]{3,2,1,0:T(8,128)(2,1)} %bitcast.27), channel_id=1, source_target_pairs={{0,1},{1,0},{2,3},{3,2},{4,5},{5,4},{6,7},{7,6},{8,24},{9,25},{10,... | collective-permute-start | bytes 1179656 | tf_op jit(solution)/shard_map/ppermute | solution.py:208
  8.6 0.0 collective-permute-start.5
  8.6 0.0 copy-done
  8.7 0.1 fusion
  8.8 6.3 %collective-permute-done.1.refs_0_.refs_1_ = bf16[2,12,64,128]{3,2,1,0:T(8,128)(2,1)S(1)} collective-permute-done((bf16[2,12,64,128]{3,2,1,0:T(8,128)(2,1)}, bf16[2,12,64,128]{3,2,1,0:T(8,128)(2,1)S(1)}, u32[]{:S(2)}, u32[]{:S(2)}) %collective-permute-start.1) | collective-permute-done | bytes 393248 | tf_op jit(solution)/shard_map/ppermute | solution.py:208
  15.1 2.6 %collective-permute-start.4 = (bf16[2,12,64,128]{3,2,1,0:T(8,128)(2,1)S(1)}, bf16[2,12,64,128]{3,2,1,0:T(8,128)(2,1)S(1)}, u32[]{:S(2)}, u32[]{:S(2)}) collective-permute-start(bf16[2,12,64,128]{3,2,1,0:T(8,128)(2,1)S(1)} %collective-permute-done.1.refs_0_.refs_1_), channel_id=1, source_target_pairs={{0,1},{1,0},{2,3},{3,2},{4,5},{5,4},{6,7},{7,6},{8,24},{9,25},{10,... | collective-permute-start | bytes 1179656 | tf_op jit(solution)/shard_map/ppermute | solution.py:208
  17.7 0.1 multiply_cosine_fusion
  17.8 4.1 %collective-permute-done.refs_4_.refs_0_ = bf16[2,12,64,128]{3,2,1,0:T(8,128)(2,1)S(1)} collective-permute-done((bf16[2,12,64,128]{3,2,1,0:T(8,128)(2,1)}, bf16[2,12,64,128]{3,2,1,0:T(8,128)(2,1)S(1)}, u32[]{:S(2)}, u32[]{:S(2)}) %collective-permute-start) | collective-permute-done | bytes 393248 | tf_op jit(solution)/shard_map/ppermute | solution.py:208
  21.9 1.4 %collective-permute-done.2.refs_3_.refs_2_.refs_1_ = bf16[2,12,64,128]{3,2,1,0:T(8,128)(2,1)S(1)} collective-permute-done((bf16[2,12,64,128]{3,2,1,0:T(8,128)(2,1)}, bf16[2,12,64,128]{3,2,1,0:T(8,128)(2,1)S(1)}, u32[]{:S(2)}, u32[]{:S(2)}) %collective-permute-start.2) | collective-permute-done | bytes 393248 | tf_op jit(solution)/shard_map/ppermute | solution.py:208
  23.3 0.0 collective-permute-done.3.refs_1_.refs_3_
  23.3 0.0 collective-permute-done.5.refs_4_
  23.3 0.1 collective-permute-done.4.refs_2_.refs_4_
  23.4 0.2 shard_map.28
  23.6 0.1 collective-permute-start.6
  23.7 2.2 %collective-permute-start.7 = (bf16[2,12,64,128]{3,2,1,0:T(8,128)(2,1)S(1)}, bf16[2,12,64,128]{3,2,1,0:T(8,128)(2,1)S(1)}, u32[]{:S(2)}, u32[]{:S(2)}) collective-permute-start(bf16[2,12,64,128]{3,2,1,0:T(8,128)(2,1)S(1)} %collective-permute-done.refs_4_.refs_0_), channel_id=1, source_target_pairs={{0,2},{1,3},{2,0},{3,1},{4,6},{5,7},{6,4},{7,5},{8,10},{9,11},{10,... | collective-permute-start | bytes 1179656 | tf_op jit(solution)/shard_map/ppermute | solution.py:208
  25.9 1.5 %collective-permute-start.9 = (bf16[2,2,12,64,128]{4,3,2,1,0:T(8,128)(2,1)S(1)}, bf16[2,2,12,64,128]{4,3,2,1,0:T(8,128)(2,1)S(1)}, u32[]{:S(2)}, u32[]{:S(2)}) collective-permute-start(bf16[2,2,12,64,128]{4,3,2,1,0:T(8,128)(2,1)S(1)} %get-tuple-element.104), channel_id=1, source_target_pairs={{0,16},{1,17},{2,18},{3,19},{4,20},{5,21},{6,22},{7,23},{8,9},{9,8... | collective-permute-start | bytes 2359304 | tf_op jit(solution)/shard_map/ppermute | solution.py:208
  27.4 0.6 collective-permute-start.10
  28.0 1.3 %collective-permute-start.8 = (bf16[2,12,64,128]{3,2,1,0:T(8,128)(2,1)S(1)}, bf16[2,12,64,128]{3,2,1,0:T(8,128)(2,1)S(1)}, u32[]{:S(2)}, u32[]{:S(2)}) collective-permute-start(bf16[2,12,64,128]{3,2,1,0:T(8,128)(2,1)S(1)} %collective-permute-done.4.refs_2_.refs_4_), channel_id=1, source_target_pairs={{0,4},{1,5},{2,6},{3,7},{4,0},{5,1},{6,2},{7,3},{8,12},{9,13},{10,... | collective-permute-start | bytes 1179656 | tf_op jit(solution)/shard_map/ppermute | solution.py:208
  29.3 0.0 copy-start.1
  29.3 1.0 %copy-done.1 = bf16[2,1,64,12,128]{4,2,3,1,0:T(8,128)(2,1)S(1)} copy-done((bf16[2,1,64,12,128]{4,2,3,1,0:T(8,128)(2,1)S(1)}, bf16[2,1,64,12,128]{4,2,3,1,0:T(8,128)(2,1)}, u32[]{:S(2)}) %copy-start.1) | copy-done | bytes 393240
  30.3 1.8 %shard_map.29.refs_7_ = f32[2,2,256,256]{3,2,1,0:T(8,128)S(1)} custom-call(f32[8,2,128]{2,1,0:T(2,128)S(1)} %maximum_bitcast_fusion.weights_ref, bf16[2,12,64,128]{3,2,1,0:T(8,128)(2,1)S(1)} %collective-permute-done.refs_4_.refs_0_, bf16[2,12,64,128]{3,2,1,0:T(8,128)(2,1)S(1)} %collective-permute-done.1.refs_0_.refs_1_, ...), custom_call_target="tpu_custom_call" | custom-call | flops 1207959552 | bytes 4456448 | tf_op jit(solution)/shard_map/pallas_call | solution.py:263
  32.0 0.0 collective-permute-done.6.refs_5_
  32.1 1.7 %shard_map.30.refs_1_ = f32[2,2,256,256]{3,2,1,0:T(8,128)S(1)} custom-call(f32[8,2,128]{2,1,0:T(2,128)S(1)} %maximum_bitcast_fusion.weights_ref, bf16[2,12,64,128]{3,2,1,0:T(8,128)(2,1)S(1)} %collective-permute-done.refs_4_.refs_0_, bf16[2,12,64,128]{3,2,1,0:T(8,128)(2,1)S(1)} %collective-permute-done.1.refs_0_.refs_1_, ...), custom_call_target="tpu_custom_call" | custom-call | flops 1207959552 | bytes 4456448 | tf_op jit(solution)/shard_map/pallas_call | solution.py:263
  33.8 6.7 %collective-permute-done.7.refs_0_.o3_ref.refs_2_ = bf16[2,12,64,128]{3,2,1,0:T(8,128)(2,1)S(1)} collective-permute-done((bf16[2,12,64,128]{3,2,1,0:T(8,128)(2,1)S(1)}, bf16[2,12,64,128]{3,2,1,0:T(8,128)(2,1)S(1)}, u32[]{:S(2)}, u32[]{:S(2)}) %collective-permute-start.7) | collective-permute-done | bytes 393248 | tf_op jit(solution)/shard_map/ppermute | solution.py:208
  40.5 2.2 %collective-permute-start.11 = (bf16[2,12,64,128]{3,2,1,0:T(8,128)(2,1)S(1)}, bf16[2,12,64,128]{3,2,1,0:T(8,128)(2,1)S(1)}, u32[]{:S(2)}, u32[]{:S(2)}) collective-permute-start(bf16[2,12,64,128]{3,2,1,0:T(8,128)(2,1)S(1)} %collective-permute-done.7.refs_0_.o3_ref.refs_2_), channel_id=1, source_target_pairs={{0,16},{1,17},{2,18},{3,19},{4,20},{5,21},{6,22},{7,23},{8,9},{9,8... | collective-permute-start | bytes 1179656 | tf_op jit(solution)/shard_map/ppermute | solution.py:208
  42.6 1.5 %collective-permute-start.12 = (bf16[2,12,64,128]{3,2,1,0:T(8,128)(2,1)S(1)}, bf16[2,12,64,128]{3,2,1,0:T(8,128)(2,1)S(1)}, u32[]{:S(2)}, u32[]{:S(2)}) collective-permute-start(bf16[2,12,64,128]{3,2,1,0:T(8,128)(2,1)S(1)} %collective-permute-done.7.refs_0_.o3_ref.refs_2_), channel_id=1, source_target_pairs={{0,1},{1,0},{2,3},{3,2},{4,5},{5,4},{6,7},{7,6},{8,24},{9,25},{10,... | collective-permute-start | bytes 1179656 | tf_op jit(solution)/shard_map/ppermute | solution.py:208
  44.2 0.4 shard_map.31.refs_5_
  44.6 3.4 %collective-permute-done.8.ab2_ref.refs_2_ = bf16[2,12,64,128]{3,2,1,0:T(8,128)(2,1)S(1)} collective-permute-done((bf16[2,12,64,128]{3,2,1,0:T(8,128)(2,1)S(1)}, bf16[2,12,64,128]{3,2,1,0:T(8,128)(2,1)S(1)}, u32[]{:S(2)}, u32[]{:S(2)}) %collective-permute-start.8) | collective-permute-done | bytes 393248 | tf_op jit(solution)/shard_map/ppermute | solution.py:208
  48.0 0.0 collective-permute-done.9.a12_ref.refs_3_
  48.0 0.0 collective-permute-done.10.b12_ref.refs_4_
  48.0 0.0 collective-permute-start.13
  48.0 0.2 shard_map.32
  48.2 1.8 %collective-permute-start.14 = (bf16[2,12,64,128]{3,2,1,0:T(8,128)(2,1)S(1)}, bf16[2,12,64,128]{3,2,1,0:T(8,128)(2,1)S(1)}, u32[]{:S(2)}, u32[]{:S(2)}) collective-permute-start(bf16[2,12,64,128]{3,2,1,0:T(8,128)(2,1)S(1)} %get-tuple-element.129), channel_id=1, source_target_pairs={{0,1},{1,0},{2,3},{3,2},{4,5},{5,4},{6,7},{7,6},{8,24},{9,25},{10,... | collective-permute-start | bytes 1179656 | tf_op jit(solution)/shard_map/ppermute | solution.py:208
  50.0 0.0 collective-permute-start.15
  50.0 1.6 %shard_map.33.refs_7_ = f32[2,2,256,256]{3,2,1,0:T(8,128)S(1)} custom-call(f32[8,2,128]{2,1,0:T(2,128)S(1)} %maximum_bitcast_fusion.weights_ref, bf16[2,12,64,128]{3,2,1,0:T(8,128)(2,1)S(1)} %collective-permute-done.refs_4_.refs_0_, bf16[2,12,64,128]{3,2,1,0:T(8,128)(2,1)S(1)} %collective-permute-done.2.refs_3_.refs_2_.refs_1_, ...), custom_call_target="tpu_custom_call" | custom-call | flops 1006632960 | bytes 4063232 | tf_op jit(solution)/shard_map/pallas_call | solution.py:263
  51.6 3.1 %collective-permute-done.11.a3_ref = bf16[2,12,64,128]{3,2,1,0:T(8,128)(2,1)S(1)} collective-permute-done((bf16[2,12,64,128]{3,2,1,0:T(8,128)(2,1)S(1)}, bf16[2,12,64,128]{3,2,1,0:T(8,128)(2,1)S(1)}, u32[]{:S(2)}, u32[]{:S(2)}) %collective-permute-start.11) | collective-permute-done | bytes 393248 | tf_op jit(solution)/shard_map/ppermute | solution.py:208
  54.8 0.0 collective-permute-done.12.ab3_ref
  54.8 0.1 shard_map.34.refs_5_
  54.8 0.1 collective-permute-start.16
  54.9 0.0 collective-permute-done.15.refs_6_
  54.9 2.3 %shard_map.35 = (f32[2,2,256,256]{3,2,1,0:T(8,128)S(1)}, bf16[6,512,768]{2,1,0:T(8,128)(2,1)S(1)}) custom-call(f32[8,2,128]{2,1,0:T(2,128)S(1)} %maximum_bitcast_fusion.weights_ref, bf16[2,12,64,128]{3,2,1,0:T(8,128)(2,1)S(1)} %collective-permute-done.refs_4_.refs_0_, bf16[2,12,64,128]{3,2,1,0:T(8,128)(2,1)S(1)} %collective-permute-done.2.refs_3_.refs_2_.refs_1_, ...), custom_call_target="tpu_custom_call" | custom-call | flops 16106127360 | bytes 5242880 | tf_op jit(solution)/shard_map/pallas_call | solution.py:263
  57.2 0.6 collective-permute-done.13.refs_0_
  57.8 0.4 collective-permute-done.14.refs_1_
  58.2 0.4 collective-permute-start.17
  58.6 0.1 collective-permute-start.18
  58.7 0.0 collective-permute-done.16.refs_2_
  58.7 2.0 %shard_map.36 = (f32[2,2,256,256]{3,2,1,0:T(8,128)S(1)}, f32[16,64,256]{2,1,0:T(8,128)}) custom-call(f32[8,2,128]{2,1,0:T(2,128)S(1)} %maximum_bitcast_fusion.weights_ref, bf16[2,12,64,128]{3,2,1,0:T(8,128)(2,1)S(1)} %collective-permute-done.13.refs_0_, bf16[2,12,64,128]{3,2,1,0:T(8,128)(2,1)S(1)} %collective-permute-done.14.refs_1_, ...), custom_call_target="tpu_custom_call" | custom-call | flops 805306368 | bytes 3670016 | tf_op jit(solution)/shard_map/pallas_call | solution.py:263
  60.7 0.0 collective-permute-done.17.refs_0_
  60.7 0.0 collective-permute-done.18.refs_1_
  60.7 1.5 %shard_map.37 = f32[16,64,256]{2,1,0:T(8,128)} custom-call(f32[8,2,128]{2,1,0:T(2,128)S(1)} %maximum_bitcast_fusion.weights_ref, bf16[2,12,64,128]{3,2,1,0:T(8,128)(2,1)S(1)} %collective-permute-done.17.refs_0_, bf16[2,12,64,128]{3,2,1,0:T(8,128)(2,1)S(1)} %collective-permute-done.18.refs_1_, ...), custom_call_target="tpu_custom_call", output_to_operand_aliasing={{}: (5, {})} | custom-call | flops 402653184 | bytes 2883584 | tf_op jit(solution)/shard_map/pallas_call | solution.py:263
  (5 shorter events, 0.1 us)
Async XLA Ops:
  0.0 8.6 %copy-start = (s32[4,3]{1,0:T(4,128)S(1)}, s32[4,3]{1,0:T(4,128)}, u32[]{:S(2)}) copy-start(s32[4,3]{1,0:T(4,128)} %param.3) | copy-start | bytes 148
  0.0 21.9 %collective-permute-start = (bf16[2,12,64,128]{3,2,1,0:T(8,128)(2,1)}, bf16[2,12,64,128]{3,2,1,0:T(8,128)(2,1)S(1)}, u32[]{:S(2)}, u32[]{:S(2)}) collective-permute-start(bf16[2,12,64,128]{3,2,1,0:T(8,128)(2,1)} %bitcast.24), channel_id=1, source_target_pairs={{0,4},{1,5},{2,6},{3,7},{4,0},{5,1},{6,2},{7,3},{8,12},{9,13},{10,... | collective-permute-start | bytes 1179656 | tf_op jit(solution)/shard_map/ppermute | solution.py:208
  4.0 11.1 %collective-permute-start.1 = (bf16[2,12,64,128]{3,2,1,0:T(8,128)(2,1)}, bf16[2,12,64,128]{3,2,1,0:T(8,128)(2,1)S(1)}, u32[]{:S(2)}, u32[]{:S(2)}) collective-permute-start(bf16[2,12,64,128]{3,2,1,0:T(8,128)(2,1)} %bitcast.25), channel_id=1, source_target_pairs={{0,16},{1,17},{2,18},{3,19},{4,20},{5,21},{6,22},{7,23},{8,9},{9,8... | collective-permute-start | bytes 1179656 | tf_op jit(solution)/shard_map/ppermute | solution.py:208
  5.5 17.8 %collective-permute-start.2 = (bf16[2,12,64,128]{3,2,1,0:T(8,128)(2,1)}, bf16[2,12,64,128]{3,2,1,0:T(8,128)(2,1)S(1)}, u32[]{:S(2)}, u32[]{:S(2)}) collective-permute-start(bf16[2,12,64,128]{3,2,1,0:T(8,128)(2,1)} %bitcast.26), channel_id=1, source_target_pairs={{0,2},{1,3},{2,0},{3,1},{4,6},{5,7},{6,4},{7,5},{8,10},{9,11},{10,... | collective-permute-start | bytes 1179656 | tf_op jit(solution)/shard_map/ppermute | solution.py:208
  7.1 16.2 %collective-permute-start.3 = (bf16[2,12,64,128]{3,2,1,0:T(8,128)(2,1)}, bf16[2,12,64,128]{3,2,1,0:T(8,128)(2,1)S(1)}, u32[]{:S(2)}, u32[]{:S(2)}) collective-permute-start(bf16[2,12,64,128]{3,2,1,0:T(8,128)(2,1)} %bitcast.27), channel_id=1, source_target_pairs={{0,1},{1,0},{2,3},{3,2},{4,5},{5,4},{6,7},{7,6},{8,24},{9,25},{10,... | collective-permute-start | bytes 1179656 | tf_op jit(solution)/shard_map/ppermute | solution.py:208
  8.6 14.7 %collective-permute-start.5 = (bf16[2,12,64,128]{3,2,1,0:T(8,128)(2,1)}, bf16[2,12,64,128]{3,2,1,0:T(8,128)(2,1)S(1)}, u32[]{:S(2)}, u32[]{:S(2)}) collective-permute-start(bf16[2,12,64,128]{3,2,1,0:T(8,128)(2,1)} %bitcast.28), channel_id=1, source_target_pairs={{0,8},{1,9},{2,10},{3,11},{4,12},{5,13},{6,14},{7,15},{8,0},{9,1},... | collective-permute-start | bytes 1179656 | tf_op jit(solution)/shard_map/ppermute | solution.py:208
  15.1 8.3 %collective-permute-start.4 = (bf16[2,12,64,128]{3,2,1,0:T(8,128)(2,1)S(1)}, bf16[2,12,64,128]{3,2,1,0:T(8,128)(2,1)S(1)}, u32[]{:S(2)}, u32[]{:S(2)}) collective-permute-start(bf16[2,12,64,128]{3,2,1,0:T(8,128)(2,1)S(1)} %collective-permute-done.1.refs_0_.refs_1_), channel_id=1, source_target_pairs={{0,1},{1,0},{2,3},{3,2},{4,5},{5,4},{6,7},{7,6},{8,24},{9,25},{10,... | collective-permute-start | bytes 1179656 | tf_op jit(solution)/shard_map/ppermute | solution.py:208
  23.6 8.5 %collective-permute-start.6 = (bf16[5,2,12,64,128]{4,3,2,1,0:T(8,128)(2,1)S(1)}, bf16[5,2,12,64,128]{4,3,2,1,0:T(8,128)(2,1)S(1)}, u32[]{:S(2)}, u32[]{:S(2)}) collective-permute-start(bf16[5,2,12,64,128]{4,3,2,1,0:T(8,128)(2,1)S(1)} %get-tuple-element.91), channel_id=1, source_target_pairs={{0,8},{1,9},{2,10},{3,11},{4,12},{5,13},{6,14},{7,15},{8,0},{9,1},... | collective-permute-start | bytes 5898248 | tf_op jit(solution)/shard_map/ppermute | solution.py:208
  23.7 16.8 %collective-permute-start.7 = (bf16[2,12,64,128]{3,2,1,0:T(8,128)(2,1)S(1)}, bf16[2,12,64,128]{3,2,1,0:T(8,128)(2,1)S(1)}, u32[]{:S(2)}, u32[]{:S(2)}) collective-permute-start(bf16[2,12,64,128]{3,2,1,0:T(8,128)(2,1)S(1)} %collective-permute-done.refs_4_.refs_0_), channel_id=1, source_target_pairs={{0,2},{1,3},{2,0},{3,1},{4,6},{5,7},{6,4},{7,5},{8,10},{9,11},{10,... | collective-permute-start | bytes 1179656 | tf_op jit(solution)/shard_map/ppermute | solution.py:208
  25.9 22.1 %collective-permute-start.9 = (bf16[2,2,12,64,128]{4,3,2,1,0:T(8,128)(2,1)S(1)}, bf16[2,2,12,64,128]{4,3,2,1,0:T(8,128)(2,1)S(1)}, u32[]{:S(2)}, u32[]{:S(2)}) collective-permute-start(bf16[2,2,12,64,128]{4,3,2,1,0:T(8,128)(2,1)S(1)} %get-tuple-element.104), channel_id=1, source_target_pairs={{0,16},{1,17},{2,18},{3,19},{4,20},{5,21},{6,22},{7,23},{8,9},{9,8... | collective-permute-start | bytes 2359304 | tf_op jit(solution)/shard_map/ppermute | solution.py:208
  27.4 20.6 %collective-permute-start.10 = (bf16[2,2,12,64,128]{4,3,2,1,0:T(8,128)(2,1)S(1)}, bf16[2,2,12,64,128]{4,3,2,1,0:T(8,128)(2,1)S(1)}, u32[]{:S(2)}, u32[]{:S(2)}) collective-permute-start(bf16[2,2,12,64,128]{4,3,2,1,0:T(8,128)(2,1)S(1)} %get-tuple-element.104), channel_id=1, source_target_pairs={{0,1},{1,0},{2,3},{3,2},{4,5},{5,4},{6,7},{7,6},{8,24},{9,25},{10,... | collective-permute-start | bytes 2359304 | tf_op jit(solution)/shard_map/ppermute | solution.py:208
  28.0 20.0 %collective-permute-start.8 = (bf16[2,12,64,128]{3,2,1,0:T(8,128)(2,1)S(1)}, bf16[2,12,64,128]{3,2,1,0:T(8,128)(2,1)S(1)}, u32[]{:S(2)}, u32[]{:S(2)}) collective-permute-start(bf16[2,12,64,128]{3,2,1,0:T(8,128)(2,1)S(1)} %collective-permute-done.4.refs_2_.refs_4_), channel_id=1, source_target_pairs={{0,4},{1,5},{2,6},{3,7},{4,0},{5,1},{6,2},{7,3},{8,12},{9,13},{10,... | collective-permute-start | bytes 1179656 | tf_op jit(solution)/shard_map/ppermute | solution.py:208
  29.3 1.0 %copy-start.1 = (bf16[2,1,64,12,128]{4,2,3,1,0:T(8,128)(2,1)S(1)}, bf16[2,1,64,12,128]{4,2,3,1,0:T(8,128)(2,1)}, u32[]{:S(2)}) copy-start(bf16[2,1,64,12,128]{4,2,3,1,0:T(8,128)(2,1)} %param.2) | copy-start | bytes 1179652
  40.5 14.3 %collective-permute-start.11 = (bf16[2,12,64,128]{3,2,1,0:T(8,128)(2,1)S(1)}, bf16[2,12,64,128]{3,2,1,0:T(8,128)(2,1)S(1)}, u32[]{:S(2)}, u32[]{:S(2)}) collective-permute-start(bf16[2,12,64,128]{3,2,1,0:T(8,128)(2,1)S(1)} %collective-permute-done.7.refs_0_.o3_ref.refs_2_), channel_id=1, source_target_pairs={{0,16},{1,17},{2,18},{3,19},{4,20},{5,21},{6,22},{7,23},{8,9},{9,8... | collective-permute-start | bytes 1179656 | tf_op jit(solution)/shard_map/ppermute | solution.py:208
  42.6 12.1 %collective-permute-start.12 = (bf16[2,12,64,128]{3,2,1,0:T(8,128)(2,1)S(1)}, bf16[2,12,64,128]{3,2,1,0:T(8,128)(2,1)S(1)}, u32[]{:S(2)}, u32[]{:S(2)}) collective-permute-start(bf16[2,12,64,128]{3,2,1,0:T(8,128)(2,1)S(1)} %collective-permute-done.7.refs_0_.o3_ref.refs_2_), channel_id=1, source_target_pairs={{0,1},{1,0},{2,3},{3,2},{4,5},{5,4},{6,7},{7,6},{8,24},{9,25},{10,... | collective-permute-start | bytes 1179656 | tf_op jit(solution)/shard_map/ppermute | solution.py:208
  48.0 9.8 %collective-permute-start.13 = (bf16[2,12,64,128]{3,2,1,0:T(8,128)(2,1)S(1)}, bf16[2,12,64,128]{3,2,1,0:T(8,128)(2,1)S(1)}, u32[]{:S(2)}, u32[]{:S(2)}) collective-permute-start(bf16[2,12,64,128]{3,2,1,0:T(8,128)(2,1)S(1)} %collective-permute-done.8.ab2_ref.refs_2_), channel_id=1, source_target_pairs={{0,2},{1,3},{2,0},{3,1},{4,6},{5,7},{6,4},{7,5},{8,10},{9,11},{10,... | collective-permute-start | bytes 1179656 | tf_op jit(solution)/shard_map/ppermute | solution.py:208
  48.2 10.0 %collective-permute-start.14 = (bf16[2,12,64,128]{3,2,1,0:T(8,128)(2,1)S(1)}, bf16[2,12,64,128]{3,2,1,0:T(8,128)(2,1)S(1)}, u32[]{:S(2)}, u32[]{:S(2)}) collective-permute-start(bf16[2,12,64,128]{3,2,1,0:T(8,128)(2,1)S(1)} %get-tuple-element.129), channel_id=1, source_target_pairs={{0,1},{1,0},{2,3},{3,2},{4,5},{5,4},{6,7},{7,6},{8,24},{9,25},{10,... | collective-permute-start | bytes 1179656 | tf_op jit(solution)/shard_map/ppermute | solution.py:208
  50.0 4.9 %collective-permute-start.15 = (bf16[6,2,12,64,128]{4,3,2,1,0:T(8,128)(2,1)S(1)}, bf16[6,2,12,64,128]{4,3,2,1,0:T(8,128)(2,1)S(1)}, u32[]{:S(2)}, u32[]{:S(2)}) collective-permute-start(bf16[6,2,12,64,128]{4,3,2,1,0:T(8,128)(2,1)S(1)} %get-tuple-element.130), channel_id=1, source_target_pairs={{0,8},{1,9},{2,10},{3,11},{4,12},{5,13},{6,14},{7,15},{8,0},{9,1},... | collective-permute-start | bytes 7077896 | tf_op jit(solution)/shard_map/ppermute | solution.py:208
  54.8 3.9 %collective-permute-start.16 = (bf16[2,2,12,64,128]{4,3,2,1,0:T(8,128)(2,1)S(1)}, bf16[2,2,12,64,128]{4,3,2,1,0:T(8,128)(2,1)S(1)}, u32[]{:S(2)}, u32[]{:S(2)}) collective-permute-start(bf16[2,2,12,64,128]{4,3,2,1,0:T(8,128)(2,1)S(1)} %shard_map.34.refs_5_), channel_id=1, source_target_pairs={{0,8},{1,9},{2,10},{3,11},{4,12},{5,13},{6,14},{7,15},{8,0},{9,1},... | collective-permute-start | bytes 2359304 | tf_op jit(solution)/shard_map/ppermute | solution.py:208
  58.2 2.6 %collective-permute-start.17 = (bf16[2,12,64,128]{3,2,1,0:T(8,128)(2,1)S(1)}, bf16[2,12,64,128]{3,2,1,0:T(8,128)(2,1)S(1)}, u32[]{:S(2)}, u32[]{:S(2)}) collective-permute-start(bf16[2,12,64,128]{3,2,1,0:T(8,128)(2,1)S(1)} %collective-permute-done.13.refs_0_), channel_id=1, source_target_pairs={{0,8},{1,9},{2,10},{3,11},{4,12},{5,13},{6,14},{7,15},{8,0},{9,1},... | collective-permute-start | bytes 1179656 | tf_op jit(solution)/shard_map/ppermute | solution.py:208
  58.6 2.2 %collective-permute-start.18 = (bf16[2,12,64,128]{3,2,1,0:T(8,128)(2,1)S(1)}, bf16[2,12,64,128]{3,2,1,0:T(8,128)(2,1)S(1)}, u32[]{:S(2)}, u32[]{:S(2)}) collective-permute-start(bf16[2,12,64,128]{3,2,1,0:T(8,128)(2,1)S(1)} %collective-permute-done.14.refs_1_), channel_id=1, source_target_pairs={{0,8},{1,9},{2,10},{3,11},{4,12},{5,13},{6,14},{7,15},{8,0},{9,1},... | collective-permute-start | bytes 1179656 | tf_op jit(solution)/shard_map/ppermute | solution.py:208

commit v23 on v22

--- a/solution.py
+++ b/solution.py
@@ -79,29 +79,37 @@
     def send_columns(dx, near, far):
         lane = lax.broadcasted_iota(jnp.int32, (per_block, 2 * per_block), 1)
         start = pl.multiple_of(jnp.bitwise_xor(pair, dx) * (2 * per_block), 2 * per_block)
+
+        def place(even, odd):
+            for spin in range(spins):
+                for column in range(0, columns, 2):
+                    first = (spin * columns + column) * 2
+                    across = slice(column * per_block, (column + 2) * per_block)
+                    for part in range(2):
+                        top = (part * spins + spin) * per_block
+                        rows = slice(top, top + per_block)
+                        one, two = even(rows, across), odd(rows, across)
+                        row_ref[first + part] = jnp.where(
+                            lane < per_block, one, pltpu.roll(two, per_block, 1)
+                        )
+                        row_ref[first + part + 2] = jnp.where(
+                            lane < per_block, pltpu.roll(one, per_block, 1), two
+                        )
+
+        @pl.when(core == 0)
+        def _():
+            place(near, far)
+
+        @pl.when(core != 0)
+        def _():
+            place(far, near)
+
         copies = []
-        for spin in range(spins):
-            for column in range(0, columns, 2):
-                first = (spin * columns + column) * 2
-                across = slice(column * per_block, (column + 2) * per_block)
-                for part in range(2):
-                    top = (part * spins + spin) * per_block
-                    one = near(slice(top, top + per_block), across)
-                    two = far(slice(top, top + per_block), across)
-                    even = jnp.where(core == 0, one, two)
-                    odd = jnp.where(core == 0, two, one)
-                    row_ref[first + part] = jnp.where(
-                        lane < per_block, even, pltpu.roll(odd, per_block, 1)
-                    )
-                    row_ref[first + part + 2] = jnp.where(
-                        lane < per_block, pltpu.roll(even, per_block, 1), odd
-                    )
-                four = pl.ds(first, 4)
-                target = field_ref.at[four, :, pl.ds(start, 2 * per_block)]
-                copies.append(
-                    pltpu.make_async_copy(row_ref.at[four], target, sems.at[len(copies)])
-                )
-                copies[-1].start()
+        for index in range(spins * columns // 2):
+            four = pl.ds(4 * index, 4)
+            target = field_ref.at[four, :, pl.ds(start, 2 * per_block)]
+            copies.append(pltpu.make_async_copy(row_ref.at[four], target, sems.at[index]))
+            copies[-1].start()
         return copies
 
     def term(name):

time: 62.4 us -> 63.1 us (1.011)
  Pallas kernels: 11.8 us -> 12.5 us
    pallas_call x7, Pallas kernels: 11.4 us -> 12.1 us  [add(): pl.pallas_call(functools.partial(add_shards, tuple(names), places, slots,...]
  transfers between devices with their start and end apart: 19 -> 19, of which waited for: 9 -> 9; matrix products, arithmetic and copies ran while one was open for 0% -> 0% of each run, Pallas kernels for 16% -> 17%
where the time goes in v23:
time: 63.1 us; the launch traced here: 63 us
  waiting for transfers between devices  26.1 us (41%)
  starting transfers between devices  22.9 us (36%)
  Pallas kernels  12.5 us (20%)
  local copies, waits for them, and re-layouts  1 us (2%)
    ppermute x19, waiting for transfers between devices, move(): return lax.ppermute(array, AXES, pairs)  26.1 us
    ppermute x19, starting transfers between devices, move(): return lax.ppermute(array, AXES, pairs)  22.9 us
    pallas_call x7, Pallas kernels, add(): pl.pallas_call(functools.partial(add_shards, tuple(names), places, slots,...  12.1 us
  transfers between devices with their start and end apart: 19, of which 9 were waited for; matrix products, arithmetic and copies ran while one was open for 0% of the time, Pallas kernels for 17%

profile of v23, /device:TPU:0, one launch (start us, length us, event | category | flops | bytes accessed | tf_op | source)
XLA Modules:
  0.0 63.0 jit_solution(11605807193836000492)
XLA Ops:
  0.0 0.0 copy-start
  0.0 4.0 %collective-permute-start = (bf16[2,12,64,128]{3,2,1,0:T(8,128)(2,1)}, bf16[2,12,64,128]{3,2,1,0:T(8,128)(2,1)S(1)}, u32[]{:S(2)}, u32[]{:S(2)}) collective-permute-start(bf16[2,12,64,128]{3,2,1,0:T(8,128)(2,1)} %bitcast.24), channel_id=1, source_target_pairs={{0,4},{1,5},{2,6},{3,7},{4,0},{5,1},{6,2},{7,3},{8,12},{9,13},{10,... | collective-permute-start | bytes 1179656 | tf_op jit(solution)/shard_map/ppermute | solution.py:216
  4.0 1.5 %collective-permute-start.1 = (bf16[2,12,64,128]{3,2,1,0:T(8,128)(2,1)}, bf16[2,12,64,128]{3,2,1,0:T(8,128)(2,1)S(1)}, u32[]{:S(2)}, u32[]{:S(2)}) collective-permute-start(bf16[2,12,64,128]{3,2,1,0:T(8,128)(2,1)} %bitcast.25), channel_id=1, source_target_pairs={{0,16},{1,17},{2,18},{3,19},{4,20},{5,21},{6,22},{7,23},{8,9},{9,8... | collective-permute-start | bytes 1179656 | tf_op jit(solution)/shard_map/ppermute | solution.py:216
  5.5 1.6 %collective-permute-start.2 = (bf16[2,12,64,128]{3,2,1,0:T(8,128)(2,1)}, bf16[2,12,64,128]{3,2,1,0:T(8,128)(2,1)S(1)}, u32[]{:S(2)}, u32[]{:S(2)}) collective-permute-start(bf16[2,12,64,128]{3,2,1,0:T(8,128)(2,1)} %bitcast.26), channel_id=1, source_target_pairs={{0,2},{1,3},{2,0},{3,1},{4,6},{5,7},{6,4},{7,5},{8,10},{9,11},{10,... | collective-permute-start | bytes 1179656 | tf_op jit(solution)/shard_map/ppermute | solution.py:216
  7.1 1.5 %collective-permute-start.3 = (bf16[2,12,64,128]{3,2,1,0:T(8,128)(2,1)}, bf16[2,12,64,128]{3,2,1,0:T(8,128)(2,1)S(1)}, u32[]{:S(2)}, u32[]{:S(2)}) collective-permute-start(bf16[2,12,64,128]{3,2,1,0:T(8,128)(2,1)} %bitcast.27), channel_id=1, source_target_pairs={{0,1},{1,0},{2,3},{3,2},{4,5},{5,4},{6,7},{7,6},{8,24},{9,25},{10,... | collective-permute-start | bytes 1179656 | tf_op jit(solution)/shard_map/ppermute | solution.py:216
  8.6 0.0 collective-permute-start.5
  8.6 0.0 copy-done
  8.7 0.1 fusion
  8.8 6.3 %collective-permute-done.1.refs_0_.refs_1_ = bf16[2,12,64,128]{3,2,1,0:T(8,128)(2,1)S(1)} collective-permute-done((bf16[2,12,64,128]{3,2,1,0:T(8,128)(2,1)}, bf16[2,12,64,128]{3,2,1,0:T(8,128)(2,1)S(1)}, u32[]{:S(2)}, u32[]{:S(2)}) %collective-permute-start.1) | collective-permute-done | bytes 393248 | tf_op jit(solution)/shard_map/ppermute | solution.py:216
  15.1 2.6 %collective-permute-start.4 = (bf16[2,12,64,128]{3,2,1,0:T(8,128)(2,1)S(1)}, bf16[2,12,64,128]{3,2,1,0:T(8,128)(2,1)S(1)}, u32[]{:S(2)}, u32[]{:S(2)}) collective-permute-start(bf16[2,12,64,128]{3,2,1,0:T(8,128)(2,1)S(1)} %collective-permute-done.1.refs_0_.refs_1_), channel_id=1, source_target_pairs={{0,1},{1,0},{2,3},{3,2},{4,5},{5,4},{6,7},{7,6},{8,24},{9,25},{10,... | collective-permute-start | bytes 1179656 | tf_op jit(solution)/shard_map/ppermute | solution.py:216
  17.7 0.1 multiply_cosine_fusion
  17.8 4.1 %collective-permute-done.refs_4_.refs_0_ = bf16[2,12,64,128]{3,2,1,0:T(8,128)(2,1)S(1)} collective-permute-done((bf16[2,12,64,128]{3,2,1,0:T(8,128)(2,1)}, bf16[2,12,64,128]{3,2,1,0:T(8,128)(2,1)S(1)}, u32[]{:S(2)}, u32[]{:S(2)}) %collective-permute-start) | collective-permute-done | bytes 393248 | tf_op jit(solution)/shard_map/ppermute | solution.py:216
  21.9 1.4 %collective-permute-done.2.refs_3_.refs_2_.refs_1_ = bf16[2,12,64,128]{3,2,1,0:T(8,128)(2,1)S(1)} collective-permute-done((bf16[2,12,64,128]{3,2,1,0:T(8,128)(2,1)}, bf16[2,12,64,128]{3,2,1,0:T(8,128)(2,1)S(1)}, u32[]{:S(2)}, u32[]{:S(2)}) %collective-permute-start.2) | collective-permute-done | bytes 393248 | tf_op jit(solution)/shard_map/ppermute | solution.py:216
  23.3 0.0 collective-permute-done.3.refs_1_.refs_3_
  23.3 0.0 collective-permute-done.5.refs_4_
  23.3 0.1 collective-permute-done.4.refs_2_.refs_4_
  23.4 0.2 shard_map.28
  23.6 0.1 collective-permute-start.6
  23.7 2.2 %collective-permute-start.7 = (bf16[2,12,64,128]{3,2,1,0:T(8,128)(2,1)S(1)}, bf16[2,12,64,128]{3,2,1,0:T(8,128)(2,1)S(1)}, u32[]{:S(2)}, u32[]{:S(2)}) collective-permute-start(bf16[2,12,64,128]{3,2,1,0:T(8,128)(2,1)S(1)} %collective-permute-done.refs_4_.refs_0_), channel_id=1, source_target_pairs={{0,2},{1,3},{2,0},{3,1},{4,6},{5,7},{6,4},{7,5},{8,10},{9,11},{10,... | collective-permute-start | bytes 1179656 | tf_op jit(solution)/shard_map/ppermute | solution.py:216
  25.9 1.5 %collective-permute-start.9 = (bf16[2,2,12,64,128]{4,3,2,1,0:T(8,128)(2,1)S(1)}, bf16[2,2,12,64,128]{4,3,2,1,0:T(8,128)(2,1)S(1)}, u32[]{:S(2)}, u32[]{:S(2)}) collective-permute-start(bf16[2,2,12,64,128]{4,3,2,1,0:T(8,128)(2,1)S(1)} %get-tuple-element.104), channel_id=1, source_target_pairs={{0,16},{1,17},{2,18},{3,19},{4,20},{5,21},{6,22},{7,23},{8,9},{9,8... | collective-permute-start | bytes 2359304 | tf_op jit(solution)/shard_map/ppermute | solution.py:216
  27.4 0.6 collective-permute-start.10
  28.0 1.3 %collective-permute-start.8 = (bf16[2,12,64,128]{3,2,1,0:T(8,128)(2,1)S(1)}, bf16[2,12,64,128]{3,2,1,0:T(8,128)(2,1)S(1)}, u32[]{:S(2)}, u32[]{:S(2)}) collective-permute-start(bf16[2,12,64,128]{3,2,1,0:T(8,128)(2,1)S(1)} %collective-permute-done.4.refs_2_.refs_4_), channel_id=1, source_target_pairs={{0,4},{1,5},{2,6},{3,7},{4,0},{5,1},{6,2},{7,3},{8,12},{9,13},{10,... | collective-permute-start | bytes 1179656 | tf_op jit(solution)/shard_map/ppermute | solution.py:216
  29.3 0.0 copy-start.1
  29.3 1.0 %copy-done.1 = bf16[2,1,64,12,128]{4,2,3,1,0:T(8,128)(2,1)S(1)} copy-done((bf16[2,1,64,12,128]{4,2,3,1,0:T(8,128)(2,1)S(1)}, bf16[2,1,64,12,128]{4,2,3,1,0:T(8,128)(2,1)}, u32[]{:S(2)}) %copy-start.1) | copy-done | bytes 393240
  30.3 1.8 %shard_map.29.refs_7_ = f32[2,2,256,256]{3,2,1,0:T(8,128)S(1)} custom-call(f32[8,2,128]{2,1,0:T(2,128)S(1)} %maximum_bitcast_fusion.weights_ref, bf16[2,12,64,128]{3,2,1,0:T(8,128)(2,1)S(1)} %collective-permute-done.refs_4_.refs_0_, bf16[2,12,64,128]{3,2,1,0:T(8,128)(2,1)S(1)} %collective-permute-done.1.refs_0_.refs_1_, ...), custom_call_target="tpu_custom_call" | custom-call | flops 1207959552 | bytes 4456448 | tf_op jit(solution)/shard_map/pallas_call | solution.py:271
  32.0 0.0 collective-permute-done.6.refs_5_
  32.1 1.7 %shard_map.30.refs_1_ = f32[2,2,256,256]{3,2,1,0:T(8,128)S(1)} custom-call(f32[8,2,128]{2,1,0:T(2,128)S(1)} %maximum_bitcast_fusion.weights_ref, bf16[2,12,64,128]{3,2,1,0:T(8,128)(2,1)S(1)} %collective-permute-done.refs_4_.refs_0_, bf16[2,12,64,128]{3,2,1,0:T(8,128)(2,1)S(1)} %collective-permute-done.1.refs_0_.refs_1_, ...), custom_call_target="tpu_custom_call" | custom-call | flops 1207959552 | bytes 4456448 | tf_op jit(solution)/shard_map/pallas_call | solution.py:271
  33.8 6.7 %collective-permute-done.7.refs_0_.o3_ref.refs_2_ = bf16[2,12,64,128]{3,2,1,0:T(8,128)(2,1)S(1)} collective-permute-done((bf16[2,12,64,128]{3,2,1,0:T(8,128)(2,1)S(1)}, bf16[2,12,64,128]{3,2,1,0:T(8,128)(2,1)S(1)}, u32[]{:S(2)}, u32[]{:S(2)}) %collective-permute-start.7) | collective-permute-done | bytes 393248 | tf_op jit(solution)/shard_map/ppermute | solution.py:216
  40.5 2.2 %collective-permute-start.11 = (bf16[2,12,64,128]{3,2,1,0:T(8,128)(2,1)S(1)}, bf16[2,12,64,128]{3,2,1,0:T(8,128)(2,1)S(1)}, u32[]{:S(2)}, u32[]{:S(2)}) collective-permute-start(bf16[2,12,64,128]{3,2,1,0:T(8,128)(2,1)S(1)} %collective-permute-done.7.refs_0_.o3_ref.refs_2_), channel_id=1, source_target_pairs={{0,16},{1,17},{2,18},{3,19},{4,20},{5,21},{6,22},{7,23},{8,9},{9,8... | collective-permute-start | bytes 1179656 | tf_op jit(solution)/shard_map/ppermute | solution.py:216
  42.6 1.5 %collective-permute-start.12 = (bf16[2,12,64,128]{3,2,1,0:T(8,128)(2,1)S(1)}, bf16[2,12,64,128]{3,2,1,0:T(8,128)(2,1)S(1)}, u32[]{:S(2)}, u32[]{:S(2)}) collective-permute-start(bf16[2,12,64,128]{3,2,1,0:T(8,128)(2,1)S(1)} %collective-permute-done.7.refs_0_.o3_ref.refs_2_), channel_id=1, source_target_pairs={{0,1},{1,0},{2,3},{3,2},{4,5},{5,4},{6,7},{7,6},{8,24},{9,25},{10,... | collective-permute-start | bytes 1179656 | tf_op jit(solution)/shard_map/ppermute | solution.py:216
  44.2 0.4 shard_map.31.refs_5_
  44.6 3.4 %collective-permute-done.8.ab2_ref.refs_2_ = bf16[2,12,64,128]{3,2,1,0:T(8,128)(2,1)S(1)} collective-permute-done((bf16[2,12,64,128]{3,2,1,0:T(8,128)(2,1)S(1)}, bf16[2,12,64,128]{3,2,1,0:T(8,128)(2,1)S(1)}, u32[]{:S(2)}, u32[]{:S(2)}) %collective-permute-start.8) | collective-permute-done | bytes 393248 | tf_op jit(solution)/shard_map/ppermute | solution.py:216
  48.0 0.0 collective-permute-done.9.a12_ref.refs_3_
  48.0 0.0 collective-permute-done.10.b12_ref.refs_4_
  48.0 0.0 collective-permute-start.13
  48.0 0.2 shard_map.32
  48.2 1.8 %collective-permute-start.14 = (bf16[2,12,64,128]{3,2,1,0:T(8,128)(2,1)S(1)}, bf16[2,12,64,128]{3,2,1,0:T(8,128)(2,1)S(1)}, u32[]{:S(2)}, u32[]{:S(2)}) collective-permute-start(bf16[2,12,64,128]{3,2,1,0:T(8,128)(2,1)S(1)} %get-tuple-element.129), channel_id=1, source_target_pairs={{0,1},{1,0},{2,3},{3,2},{4,5},{5,4},{6,7},{7,6},{8,24},{9,25},{10,... | collective-permute-start | bytes 1179656 | tf_op jit(solution)/shard_map/ppermute | solution.py:216
  50.0 0.0 collective-permute-start.15
  50.0 1.6 %shard_map.33.refs_7_ = f32[2,2,256,256]{3,2,1,0:T(8,128)S(1)} custom-call(f32[8,2,128]{2,1,0:T(2,128)S(1)} %maximum_bitcast_fusion.weights_ref, bf16[2,12,64,128]{3,2,1,0:T(8,128)(2,1)S(1)} %collective-permute-done.refs_4_.refs_0_, bf16[2,12,64,128]{3,2,1,0:T(8,128)(2,1)S(1)} %collective-permute-done.2.refs_3_.refs_2_.refs_1_, ...), custom_call_target="tpu_custom_call" | custom-call | flops 1006632960 | bytes 4063232 | tf_op jit(solution)/shard_map/pallas_call | solution.py:271
  51.6 3.1 %collective-permute-done.11.a3_ref = bf16[2,12,64,128]{3,2,1,0:T(8,128)(2,1)S(1)} collective-permute-done((bf16[2,12,64,128]{3,2,1,0:T(8,128)(2,1)S(1)}, bf16[2,12,64,128]{3,2,1,0:T(8,128)(2,1)S(1)}, u32[]{:S(2)}, u32[]{:S(2)}) %collective-permute-start.11) | collective-permute-done | bytes 393248 | tf_op jit(solution)/shard_map/ppermute | solution.py:216
  54.8 0.0 collective-permute-done.12.ab3_ref
  54.8 0.1 shard_map.34.refs_5_
  54.8 0.1 collective-permute-start.16
  54.9 0.0 collective-permute-done.15.refs_6_
  54.9 2.3 %shard_map.35 = (f32[2,2,256,256]{3,2,1,0:T(8,128)S(1)}, bf16[6,512,768]{2,1,0:T(8,128)(2,1)S(1)}) custom-call(f32[8,2,128]{2,1,0:T(2,128)S(1)} %maximum_bitcast_fusion.weights_ref, bf16[2,12,64,128]{3,2,1,0:T(8,128)(2,1)S(1)} %collective-permute-done.refs_4_.refs_0_, bf16[2,12,64,128]{3,2,1,0:T(8,128)(2,1)S(1)} %collective-permute-done.2.refs_3_.refs_2_.refs_1_, ...), custom_call_target="tpu_custom_call" | custom-call | flops 16106127360 | bytes 5242880 | tf_op jit(solution)/shard_map/pallas_call | solution.py:271
  57.2 0.6 collective-permute-done.13.refs_0_
  57.8 0.4 collective-permute-done.14.refs_1_
  58.2 0.4 collective-permute-start.17
  58.6 0.1 collective-permute-start.18
  58.7 0.0 collective-permute-done.16.refs_2_
  58.7 2.6 %shard_map.36 = (f32[2,2,256,256]{3,2,1,0:T(8,128)S(1)}, f32[16,64,256]{2,1,0:T(8,128)}) custom-call(f32[8,2,128]{2,1,0:T(2,128)S(1)} %maximum_bitcast_fusion.weights_ref, bf16[2,12,64,128]{3,2,1,0:T(8,128)(2,1)S(1)} %collective-permute-done.13.refs_0_, bf16[2,12,64,128]{3,2,1,0:T(8,128)(2,1)S(1)} %collective-permute-done.14.refs_1_, ...), custom_call_target="tpu_custom_call" | custom-call | flops 805306368 | bytes 3670016 | tf_op jit(solution)/shard_map/pallas_call | solution.py:271
  61.3 0.0 collective-permute-done.17.refs_0_
  61.3 0.0 collective-permute-done.18.refs_1_
  61.3 1.6 %shard_map.37 = f32[16,64,256]{2,1,0:T(8,128)} custom-call(f32[8,2,128]{2,1,0:T(2,128)S(1)} %maximum_bitcast_fusion.weights_ref, bf16[2,12,64,128]{3,2,1,0:T(8,128)(2,1)S(1)} %collective-permute-done.17.refs_0_, bf16[2,12,64,128]{3,2,1,0:T(8,128)(2,1)S(1)} %collective-permute-done.18.refs_1_, ...), custom_call_target="tpu_custom_call", output_to_operand_aliasing={{}: (5, {})} | custom-call | flops 402653184 | bytes 2883584 | tf_op jit(solution)/shard_map/pallas_call | solution.py:271
  (5 shorter events, 0.1 us)
Async XLA Ops:
  0.0 8.6 %copy-start = (s32[4,3]{1,0:T(4,128)S(1)}, s32[4,3]{1,0:T(4,128)}, u32[]{:S(2)}) copy-start(s32[4,3]{1,0:T(4,128)} %param.3) | copy-start | bytes 148
  0.0 21.9 %collective-permute-start = (bf16[2,12,64,128]{3,2,1,0:T(8,128)(2,1)}, bf16[2,12,64,128]{3,2,1,0:T(8,128)(2,1)S(1)}, u32[]{:S(2)}, u32[]{:S(2)}) collective-permute-start(bf16[2,12,64,128]{3,2,1,0:T(8,128)(2,1)} %bitcast.24), channel_id=1, source_target_pairs={{0,4},{1,5},{2,6},{3,7},{4,0},{5,1},{6,2},{7,3},{8,12},{9,13},{10,... | collective-permute-start | bytes 1179656 | tf_op jit(solution)/shard_map/ppermute | solution.py:216
  4.0 11.1 %collective-permute-start.1 = (bf16[2,12,64,128]{3,2,1,0:T(8,128)(2,1)}, bf16[2,12,64,128]{3,2,1,0:T(8,128)(2,1)S(1)}, u32[]{:S(2)}, u32[]{:S(2)}) collective-permute-start(bf16[2,12,64,128]{3,2,1,0:T(8,128)(2,1)} %bitcast.25), channel_id=1, source_target_pairs={{0,16},{1,17},{2,18},{3,19},{4,20},{5,21},{6,22},{7,23},{8,9},{9,8... | collective-permute-start | bytes 1179656 | tf_op jit(solution)/shard_map/ppermute | solution.py:216
  5.5 17.8 %collective-permute-start.2 = (bf16[2,12,64,128]{3,2,1,0:T(8,128)(2,1)}, bf16[2,12,64,128]{3,2,1,0:T(8,128)(2,1)S(1)}, u32[]{:S(2)}, u32[]{:S(2)}) collective-permute-start(bf16[2,12,64,128]{3,2,1,0:T(8,128)(2,1)} %bitcast.26), channel_id=1, source_target_pairs={{0,2},{1,3},{2,0},{3,1},{4,6},{5,7},{6,4},{7,5},{8,10},{9,11},{10,... | collective-permute-start | bytes 1179656 | tf_op jit(solution)/shard_map/ppermute | solution.py:216
  7.1 16.2 %collective-permute-start.3 = (bf16[2,12,64,128]{3,2,1,0:T(8,128)(2,1)}, bf16[2,12,64,128]{3,2,1,0:T(8,128)(2,1)S(1)}, u32[]{:S(2)}, u32[]{:S(2)}) collective-permute-start(bf16[2,12,64,128]{3,2,1,0:T(8,128)(2,1)} %bitcast.27), channel_id=1, source_target_pairs={{0,1},{1,0},{2,3},{3,2},{4,5},{5,4},{6,7},{7,6},{8,24},{9,25},{10,... | collective-permute-start | bytes 1179656 | tf_op jit(solution)/shard_map/ppermute | solution.py:216
  8.6 14.7 %collective-permute-start.5 = (bf16[2,12,64,128]{3,2,1,0:T(8,128)(2,1)}, bf16[2,12,64,128]{3,2,1,0:T(8,128)(2,1)S(1)}, u32[]{:S(2)}, u32[]{:S(2)}) collective-permute-start(bf16[2,12,64,128]{3,2,1,0:T(8,128)(2,1)} %bitcast.28), channel_id=1, source_target_pairs={{0,8},{1,9},{2,10},{3,11},{4,12},{5,13},{6,14},{7,15},{8,0},{9,1},... | collective-permute-start | bytes 1179656 | tf_op jit(solution)/shard_map/ppermute | solution.py:216
  15.1 8.3 %collective-permute-start.4 = (bf16[2,12,64,128]{3,2,1,0:T(8,128)(2,1)S(1)}, bf16[2,12,64,128]{3,2,1,0:T(8,128)(2,1)S(1)}, u32[]{:S(2)}, u32[]{:S(2)}) collective-permute-start(bf16[2,12,64,128]{3,2,1,0:T(8,128)(2,1)S(1)} %collective-permute-done.1.refs_0_.refs_1_), channel_id=1, source_target_pairs={{0,1},{1,0},{2,3},{3,2},{4,5},{5,4},{6,7},{7,6},{8,24},{9,25},{10,... | collective-permute-start | bytes 1179656 | tf_op jit(solution)/shard_map/ppermute | solution.py:216
  23.6 8.5 %collective-permute-start.6 = (bf16[5,2,12,64,128]{4,3,2,1,0:T(8,128)(2,1)S(1)}, bf16[5,2,12,64,128]{4,3,2,1,0:T(8,128)(2,1)S(1)}, u32[]{:S(2)}, u32[]{:S(2)}) collective-permute-start(bf16[5,2,12,64,128]{4,3,2,1,0:T(8,128)(2,1)S(1)} %get-tuple-element.91), channel_id=1, source_target_pairs={{0,8},{1,9},{2,10},{3,11},{4,12},{5,13},{6,14},{7,15},{8,0},{9,1},... | collective-permute-start | bytes 5898248 | tf_op jit(solution)/shard_map/ppermute | solution.py:216
  23.7 16.8 %collective-permute-start.7 = (bf16[2,12,64,128]{3,2,1,0:T(8,128)(2,1)S(1)}, bf16[2,12,64,128]{3,2,1,0:T(8,128)(2,1)S(1)}, u32[]{:S(2)}, u32[]{:S(2)}) collective-permute-start(bf16[2,12,64,128]{3,2,1,0:T(8,128)(2,1)S(1)} %collective-permute-done.refs_4_.refs_0_), channel_id=1, source_target_pairs={{0,2},{1,3},{2,0},{3,1},{4,6},{5,7},{6,4},{7,5},{8,10},{9,11},{10,... | collective-permute-start | bytes 1179656 | tf_op jit(solution)/shard_map/ppermute | solution.py:216
  25.9 22.1 %collective-permute-start.9 = (bf16[2,2,12,64,128]{4,3,2,1,0:T(8,128)(2,1)S(1)}, bf16[2,2,12,64,128]{4,3,2,1,0:T(8,128)(2,1)S(1)}, u32[]{:S(2)}, u32[]{:S(2)}) collective-permute-start(bf16[2,2,12,64,128]{4,3,2,1,0:T(8,128)(2,1)S(1)} %get-tuple-element.104), channel_id=1, source_target_pairs={{0,16},{1,17},{2,18},{3,19},{4,20},{5,21},{6,22},{7,23},{8,9},{9,8... | collective-permute-start | bytes 2359304 | tf_op jit(solution)/shard_map/ppermute | solution.py:216
  27.4 20.6 %collective-permute-start.10 = (bf16[2,2,12,64,128]{4,3,2,1,0:T(8,128)(2,1)S(1)}, bf16[2,2,12,64,128]{4,3,2,1,0:T(8,128)(2,1)S(1)}, u32[]{:S(2)}, u32[]{:S(2)}) collective-permute-start(bf16[2,2,12,64,128]{4,3,2,1,0:T(8,128)(2,1)S(1)} %get-tuple-element.104), channel_id=1, source_target_pairs={{0,1},{1,0},{2,3},{3,2},{4,5},{5,4},{6,7},{7,6},{8,24},{9,25},{10,... | collective-permute-start | bytes 2359304 | tf_op jit(solution)/shard_map/ppermute | solution.py:216
  28.0 20.0 %collective-permute-start.8 = (bf16[2,12,64,128]{3,2,1,0:T(8,128)(2,1)S(1)}, bf16[2,12,64,128]{3,2,1,0:T(8,128)(2,1)S(1)}, u32[]{:S(2)}, u32[]{:S(2)}) collective-permute-start(bf16[2,12,64,128]{3,2,1,0:T(8,128)(2,1)S(1)} %collective-permute-done.4.refs_2_.refs_4_), channel_id=1, source_target_pairs={{0,4},{1,5},{2,6},{3,7},{4,0},{5,1},{6,2},{7,3},{8,12},{9,13},{10,... | collective-permute-start | bytes 1179656 | tf_op jit(solution)/shard_map/ppermute | solution.py:216
  29.3 1.0 %copy-start.1 = (bf16[2,1,64,12,128]{4,2,3,1,0:T(8,128)(2,1)S(1)}, bf16[2,1,64,12,128]{4,2,3,1,0:T(8,128)(2,1)}, u32[]{:S(2)}) copy-start(bf16[2,1,64,12,128]{4,2,3,1,0:T(8,128)(2,1)} %param.2) | copy-start | bytes 1179652
  40.5 14.3 %collective-permute-start.11 = (bf16[2,12,64,128]{3,2,1,0:T(8,128)(2,1)S(1)}, bf16[2,12,64,128]{3,2,1,0:T(8,128)(2,1)S(1)}, u32[]{:S(2)}, u32[]{:S(2)}) collective-permute-start(bf16[2,12,64,128]{3,2,1,0:T(8,128)(2,1)S(1)} %collective-permute-done.7.refs_0_.o3_ref.refs_2_), channel_id=1, source_target_pairs={{0,16},{1,17},{2,18},{3,19},{4,20},{5,21},{6,22},{7,23},{8,9},{9,8... | collective-permute-start | bytes 1179656 | tf_op jit(solution)/shard_map/ppermute | solution.py:216
  42.6 12.1 %collective-permute-start.12 = (bf16[2,12,64,128]{3,2,1,0:T(8,128)(2,1)S(1)}, bf16[2,12,64,128]{3,2,1,0:T(8,128)(2,1)S(1)}, u32[]{:S(2)}, u32[]{:S(2)}) collective-permute-start(bf16[2,12,64,128]{3,2,1,0:T(8,128)(2,1)S(1)} %collective-permute-done.7.refs_0_.o3_ref.refs_2_), channel_id=1, source_target_pairs={{0,1},{1,0},{2,3},{3,2},{4,5},{5,4},{6,7},{7,6},{8,24},{9,25},{10,... | collective-permute-start | bytes 1179656 | tf_op jit(solution)/shard_map/ppermute | solution.py:216
  48.0 9.8 %collective-permute-start.13 = (bf16[2,12,64,128]{3,2,1,0:T(8,128)(2,1)S(1)}, bf16[2,12,64,128]{3,2,1,0:T(8,128)(2,1)S(1)}, u32[]{:S(2)}, u32[]{:S(2)}) collective-permute-start(bf16[2,12,64,128]{3,2,1,0:T(8,128)(2,1)S(1)} %collective-permute-done.8.ab2_ref.refs_2_), channel_id=1, source_target_pairs={{0,2},{1,3},{2,0},{3,1},{4,6},{5,7},{6,4},{7,5},{8,10},{9,11},{10,... | collective-permute-start | bytes 1179656 | tf_op jit(solution)/shard_map/ppermute | solution.py:216
  48.2 10.0 %collective-permute-start.14 = (bf16[2,12,64,128]{3,2,1,0:T(8,128)(2,1)S(1)}, bf16[2,12,64,128]{3,2,1,0:T(8,128)(2,1)S(1)}, u32[]{:S(2)}, u32[]{:S(2)}) collective-permute-start(bf16[2,12,64,128]{3,2,1,0:T(8,128)(2,1)S(1)} %get-tuple-element.129), channel_id=1, source_target_pairs={{0,1},{1,0},{2,3},{3,2},{4,5},{5,4},{6,7},{7,6},{8,24},{9,25},{10,... | collective-permute-start | bytes 1179656 | tf_op jit(solution)/shard_map/ppermute | solution.py:216
  50.0 4.9 %collective-permute-start.15 = (bf16[6,2,12,64,128]{4,3,2,1,0:T(8,128)(2,1)S(1)}, bf16[6,2,12,64,128]{4,3,2,1,0:T(8,128)(2,1)S(1)}, u32[]{:S(2)}, u32[]{:S(2)}) collective-permute-start(bf16[6,2,12,64,128]{4,3,2,1,0:T(8,128)(2,1)S(1)} %get-tuple-element.130), channel_id=1, source_target_pairs={{0,8},{1,9},{2,10},{3,11},{4,12},{5,13},{6,14},{7,15},{8,0},{9,1},... | collective-permute-start | bytes 7077896 | tf_op jit(solution)/shard_map/ppermute | solution.py:216
  54.8 3.9 %collective-permute-start.16 = (bf16[2,2,12,64,128]{4,3,2,1,0:T(8,128)(2,1)S(1)}, bf16[2,2,12,64,128]{4,3,2,1,0:T(8,128)(2,1)S(1)}, u32[]{:S(2)}, u32[]{:S(2)}) collective-permute-start(bf16[2,2,12,64,128]{4,3,2,1,0:T(8,128)(2,1)S(1)} %shard_map.34.refs_5_), channel_id=1, source_target_pairs={{0,8},{1,9},{2,10},{3,11},{4,12},{5,13},{6,14},{7,15},{8,0},{9,1},... | collective-permute-start | bytes 2359304 | tf_op jit(solution)/shard_map/ppermute | solution.py:216
  58.2 3.1 %collective-permute-start.17 = (bf16[2,12,64,128]{3,2,1,0:T(8,128)(2,1)S(1)}, bf16[2,12,64,128]{3,2,1,0:T(8,128)(2,1)S(1)}, u32[]{:S(2)}, u32[]{:S(2)}) collective-permute-start(bf16[2,12,64,128]{3,2,1,0:T(8,128)(2,1)S(1)} %collective-permute-done.13.refs_0_), channel_id=1, source_target_pairs={{0,8},{1,9},{2,10},{3,11},{4,12},{5,13},{6,14},{7,15},{8,0},{9,1},... | collective-permute-start | bytes 1179656 | tf_op jit(solution)/shard_map/ppermute | solution.py:216
  58.6 2.8 %collective-permute-start.18 = (bf16[2,12,64,128]{3,2,1,0:T(8,128)(2,1)S(1)}, bf16[2,12,64,128]{3,2,1,0:T(8,128)(2,1)S(1)}, u32[]{:S(2)}, u32[]{:S(2)}) collective-permute-start(bf16[2,12,64,128]{3,2,1,0:T(8,128)(2,1)S(1)} %collective-permute-done.14.refs_1_), channel_id=1, source_target_pairs={{0,8},{1,9},{2,10},{3,11},{4,12},{5,13},{6,14},{7,15},{8,0},{9,1},... | collective-permute-start | bytes 1179656 | tf_op jit(solution)/shard_map/ppermute | solution.py:216

commit v24 on v22

--- a/solution.py
+++ b/solution.py
@@ -146,13 +146,13 @@
                 ]
             left_ref[slot] = left_sides(owns, weights_ref[site])
     copies = []
-    for index, name in enumerate(names):
-        if half and index == half:
-            copies = send_columns(
-                0,
-                lambda rows, across: out_ref[0, 0, rows, across],
-                lambda rows, across: out_ref[1, 0, rows, across],
-            )
+    if half:
+        copies = send_columns(
+            0,
+            lambda rows, across: totals_in[0, 0, rows, across],
+            lambda rows, across: totals_in[1, 0, rows, across],
+        )
+    for name in names:
         dx, added = term(name)
         out_ref[0 if name[0] == "near" else 1, dx] += added
     for copy in copies:
@@ -231,7 +231,7 @@
         key, slot = where[("near", kind, dz)]
         return arrays[key] if slot is None else arrays[key][slot]
 
-    def add(names, totals, keep=None, left=None, half=0, field=None, weight=1):
+    def add(names, totals, keep=None, left=None, half=False, field=None, weight=1):
         given, last = left is not None, field is not None
         slots, left = left if given else (keep or left_slots(names), None)
         uses = list(names)
@@ -341,14 +341,16 @@
     put("3d", far2, "far", second)
     names = [("far", *kind) for kind in second] + [("near", *kind) for kind in third]
     totals, (slots, left) = add(names, totals, keep=left_slots(names), weight=10)
+    put("3e", far3, "far", third)
+    totals, left = fence((totals, left))
+    totals = add([("far", *kind) for kind in third], totals, left=(slots, left))
     put("3b", ab3, "near", fourth[:1])
     put("3c", ab1, "near", fourth[1:])
     totals, left = fence((totals, left))
 
     far4 = [swap(near(*kind)) for kind in fourth]
-    put("4a", far3, "far", third)
-    names = [("far", *kind) for kind in third] + [("near", *kind) for kind in fourth]
-    totals, field = add(names, totals, left=(slots, left), half=len(third))
+    names = [("near", *kind) for kind in fourth]
+    totals, field = add(names, totals, left=(slots, left), half=True)
     put("4b", far4[0], "far", fourth[:1])
     put("4c", far4[1], "far", fourth[1:])
     totals, left, field = fence((totals, left, field))

time: 62.4 us -> 62.2 us (level)
    pallas_call x7 -> x8, Pallas kernels: 11.4 us -> 11.4 us  [add(): pl.pallas_call(functools.partial(add_shards, tuple(names), places, slots,...]
  transfers between devices with their start and end apart: 19 -> 19, of which waited for: 9 -> 8; matrix products, arithmetic and copies ran while one was open for 0% -> 0% of each run, Pallas kernels for 16% -> 16%
where the time goes in v24:
time: 62.2 us; the launch traced here: 62 us
  waiting for transfers between devices  26.2 us (42%)
  starting transfers between devices  22.6 us (36%)
  Pallas kernels  11.8 us (19%)
  local copies, waits for them, and re-layouts  1 us (2%)
    ppermute x19, waiting for transfers between devices, move(): return lax.ppermute(array, AXES, pairs)  26.2 us
    ppermute x19, starting transfers between devices, move(): return lax.ppermute(array, AXES, pairs)  22.6 us
    pallas_call x8, Pallas kernels, add(): pl.pallas_call(functools.partial(add_shards, tuple(names), places, slots,...  11.4 us
  transfers between devices with their start and end apart: 19, of which 8 were waited for; matrix products, arithmetic and copies ran while one was open for 0% of the time, Pallas kernels for 16%

profile of v24, /device:TPU:0, one launch (start us, length us, event | category | flops | bytes accessed | tf_op | source)
XLA Modules:
  0.0 62.0 jit_solution(6086250330342066120)
XLA Ops:
  0.0 0.0 copy-start
  0.0 2.9 %collective-permute-start.1 = (bf16[2,12,64,128]{3,2,1,0:T(8,128)(2,1)}, bf16[2,12,64,128]{3,2,1,0:T(8,128)(2,1)S(1)}, u32[]{:S(2)}, u32[]{:S(2)}) collective-permute-start(bf16[2,12,64,128]{3,2,1,0:T(8,128)(2,1)} %bitcast.24), channel_id=1, source_target_pairs={{0,16},{1,17},{2,18},{3,19},{4,20},{5,21},{6,22},{7,23},{8,9},{9,8... | collective-permute-start | bytes 1179656 | tf_op jit(solution)/shard_map/ppermute | solution.py:208
  2.9 2.6 %collective-permute-start = (bf16[2,12,64,128]{3,2,1,0:T(8,128)(2,1)}, bf16[2,12,64,128]{3,2,1,0:T(8,128)(2,1)S(1)}, u32[]{:S(2)}, u32[]{:S(2)}) collective-permute-start(bf16[2,12,64,128]{3,2,1,0:T(8,128)(2,1)} %bitcast.25), channel_id=1, source_target_pairs={{0,4},{1,5},{2,6},{3,7},{4,0},{5,1},{6,2},{7,3},{8,12},{9,13},{10,... | collective-permute-start | bytes 1179656 | tf_op jit(solution)/shard_map/ppermute | solution.py:208
  5.5 1.6 %collective-permute-start.2 = (bf16[2,12,64,128]{3,2,1,0:T(8,128)(2,1)}, bf16[2,12,64,128]{3,2,1,0:T(8,128)(2,1)S(1)}, u32[]{:S(2)}, u32[]{:S(2)}) collective-permute-start(bf16[2,12,64,128]{3,2,1,0:T(8,128)(2,1)} %bitcast.26), channel_id=1, source_target_pairs={{0,2},{1,3},{2,0},{3,1},{4,6},{5,7},{6,4},{7,5},{8,10},{9,11},{10,... | collective-permute-start | bytes 1179656 | tf_op jit(solution)/shard_map/ppermute | solution.py:208
  7.1 1.5 %collective-permute-start.3 = (bf16[2,12,64,128]{3,2,1,0:T(8,128)(2,1)}, bf16[2,12,64,128]{3,2,1,0:T(8,128)(2,1)S(1)}, u32[]{:S(2)}, u32[]{:S(2)}) collective-permute-start(bf16[2,12,64,128]{3,2,1,0:T(8,128)(2,1)} %bitcast.27), channel_id=1, source_target_pairs={{0,1},{1,0},{2,3},{3,2},{4,5},{5,4},{6,7},{7,6},{8,24},{9,25},{10,... | collective-permute-start | bytes 1179656 | tf_op jit(solution)/shard_map/ppermute | solution.py:208
  8.6 0.0 collective-permute-start.5
  8.6 0.0 copy-done
  8.7 0.1 fusion
  8.8 0.2 collective-permute-done.1.refs_0_.refs_1_
  9.0 3.4 %collective-permute-start.4 = (bf16[2,12,64,128]{3,2,1,0:T(8,128)(2,1)S(1)}, bf16[2,12,64,128]{3,2,1,0:T(8,128)(2,1)S(1)}, u32[]{:S(2)}, u32[]{:S(2)}) collective-permute-start(bf16[2,12,64,128]{3,2,1,0:T(8,128)(2,1)S(1)} %collective-permute-done.1.refs_0_.refs_1_), channel_id=1, source_target_pairs={{0,1},{1,0},{2,3},{3,2},{4,5},{5,4},{6,7},{7,6},{8,24},{9,25},{10,... | collective-permute-start | bytes 1179656 | tf_op jit(solution)/shard_map/ppermute | solution.py:208
  12.4 0.1 multiply_cosine_fusion
  12.6 10.6 %collective-permute-done.refs_4_.refs_0_ = bf16[2,12,64,128]{3,2,1,0:T(8,128)(2,1)S(1)} collective-permute-done((bf16[2,12,64,128]{3,2,1,0:T(8,128)(2,1)}, bf16[2,12,64,128]{3,2,1,0:T(8,128)(2,1)S(1)}, u32[]{:S(2)}, u32[]{:S(2)}) %collective-permute-start) | collective-permute-done | bytes 393248 | tf_op jit(solution)/shard_map/ppermute | solution.py:208
  23.2 0.2 collective-permute-done.2.refs_3_.refs_2_.refs_1_
  23.4 0.0 collective-permute-done.3.refs_1_.refs_3_
  23.4 0.0 collective-permute-done.5.refs_4_
  23.4 0.0 collective-permute-done.4.refs_2_.refs_4_
  23.4 0.2 shard_map.28
  23.6 0.1 collective-permute-start.6
  23.7 1.5 %collective-permute-start.7 = (bf16[2,12,64,128]{3,2,1,0:T(8,128)(2,1)S(1)}, bf16[2,12,64,128]{3,2,1,0:T(8,128)(2,1)S(1)}, u32[]{:S(2)}, u32[]{:S(2)}) collective-permute-start(bf16[2,12,64,128]{3,2,1,0:T(8,128)(2,1)S(1)} %collective-permute-done.refs_4_.refs_0_), channel_id=1, source_target_pairs={{0,2},{1,3},{2,0},{3,1},{4,6},{5,7},{6,4},{7,5},{8,10},{9,11},{10,... | collective-permute-start | bytes 1179656 | tf_op jit(solution)/shard_map/ppermute | solution.py:208
  25.2 0.5 collective-permute-start.10
  25.7 1.5 %collective-permute-start.9 = (bf16[2,2,12,64,128]{4,3,2,1,0:T(8,128)(2,1)S(1)}, bf16[2,2,12,64,128]{4,3,2,1,0:T(8,128)(2,1)S(1)}, u32[]{:S(2)}, u32[]{:S(2)}) collective-permute-start(bf16[2,2,12,64,128]{4,3,2,1,0:T(8,128)(2,1)S(1)} %get-tuple-element.107), channel_id=1, source_target_pairs={{0,16},{1,17},{2,18},{3,19},{4,20},{5,21},{6,22},{7,23},{8,9},{9,8... | collective-permute-start | bytes 2359304 | tf_op jit(solution)/shard_map/ppermute | solution.py:208
  27.2 2.3 %collective-permute-start.8 = (bf16[2,12,64,128]{3,2,1,0:T(8,128)(2,1)S(1)}, bf16[2,12,64,128]{3,2,1,0:T(8,128)(2,1)S(1)}, u32[]{:S(2)}, u32[]{:S(2)}) collective-permute-start(bf16[2,12,64,128]{3,2,1,0:T(8,128)(2,1)S(1)} %collective-permute-done.4.refs_2_.refs_4_), channel_id=1, source_target_pairs={{0,4},{1,5},{2,6},{3,7},{4,0},{5,1},{6,2},{7,3},{8,12},{9,13},{10,... | collective-permute-start | bytes 1179656 | tf_op jit(solution)/shard_map/ppermute | solution.py:208
  29.5 0.0 copy-start.1
  29.5 1.0 %copy-done.1 = bf16[2,1,64,12,128]{4,2,3,1,0:T(8,128)(2,1)S(1)} copy-done((bf16[2,1,64,12,128]{4,2,3,1,0:T(8,128)(2,1)S(1)}, bf16[2,1,64,12,128]{4,2,3,1,0:T(8,128)(2,1)}, u32[]{:S(2)}) %copy-start.1) | copy-done | bytes 393240
  30.5 1.8 %shard_map.29.refs_7_ = f32[2,2,256,256]{3,2,1,0:T(8,128)S(1)} custom-call(f32[8,2,128]{2,1,0:T(2,128)S(1)} %maximum_bitcast_fusion.weights_ref, bf16[2,12,64,128]{3,2,1,0:T(8,128)(2,1)S(1)} %collective-permute-done.refs_4_.refs_0_, bf16[2,12,64,128]{3,2,1,0:T(8,128)(2,1)S(1)} %collective-permute-done.1.refs_0_.refs_1_, ...), custom_call_target="tpu_custom_call" | custom-call | flops 1207959552 | bytes 4456448 | tf_op jit(solution)/shard_map/pallas_call | solution.py:263
  32.3 0.0 collective-permute-done.6.refs_5_
  32.3 1.7 %shard_map.30.refs_1_ = f32[2,2,256,256]{3,2,1,0:T(8,128)S(1)} custom-call(f32[8,2,128]{2,1,0:T(2,128)S(1)} %maximum_bitcast_fusion.weights_ref, bf16[2,12,64,128]{3,2,1,0:T(8,128)(2,1)S(1)} %collective-permute-done.refs_4_.refs_0_, bf16[2,12,64,128]{3,2,1,0:T(8,128)(2,1)S(1)} %collective-permute-done.1.refs_0_.refs_1_, ...), custom_call_target="tpu_custom_call" | custom-call | flops 1207959552 | bytes 4456448 | tf_op jit(solution)/shard_map/pallas_call | solution.py:263
  34.0 7.6 %collective-permute-done.7.refs_0_.o3_ref.refs_2_ = bf16[2,12,64,128]{3,2,1,0:T(8,128)(2,1)S(1)} collective-permute-done((bf16[2,12,64,128]{3,2,1,0:T(8,128)(2,1)S(1)}, bf16[2,12,64,128]{3,2,1,0:T(8,128)(2,1)S(1)}, u32[]{:S(2)}, u32[]{:S(2)}) %collective-permute-start.7) | collective-permute-done | bytes 393248 | tf_op jit(solution)/shard_map/ppermute | solution.py:208
  41.6 2.4 %collective-permute-start.13 = (bf16[2,12,64,128]{3,2,1,0:T(8,128)(2,1)S(1)}, bf16[2,12,64,128]{3,2,1,0:T(8,128)(2,1)S(1)}, u32[]{:S(2)}, u32[]{:S(2)}) collective-permute-start(bf16[2,12,64,128]{3,2,1,0:T(8,128)(2,1)S(1)} %collective-permute-done.7.refs_0_.o3_ref.refs_2_), channel_id=1, source_target_pairs={{0,16},{1,17},{2,18},{3,19},{4,20},{5,21},{6,22},{7,23},{8,9},{9,8... | collective-permute-start | bytes 1179656 | tf_op jit(solution)/shard_map/ppermute | solution.py:208
  44.1 0.0 collective-permute-start.14
  44.1 0.4 shard_map.31.refs_5_
  44.5 2.7 %collective-permute-done.8.ab2_ref.refs_2_ = bf16[2,12,64,128]{3,2,1,0:T(8,128)(2,1)S(1)} collective-permute-done((bf16[2,12,64,128]{3,2,1,0:T(8,128)(2,1)S(1)}, bf16[2,12,64,128]{3,2,1,0:T(8,128)(2,1)S(1)}, u32[]{:S(2)}, u32[]{:S(2)}) %collective-permute-start.8) | collective-permute-done | bytes 393248 | tf_op jit(solution)/shard_map/ppermute | solution.py:208
  47.2 0.0 collective-permute-done.10.b12_ref.refs_4_
  47.2 0.0 collective-permute-done.9.a12_ref.refs_3_
  47.2 0.0 collective-permute-start.11
  47.2 0.2 shard_map.32
  47.4 0.1 collective-permute-start.15
  47.4 1.6 %collective-permute-start.12 = (bf16[2,12,64,128]{3,2,1,0:T(8,128)(2,1)S(1)}, bf16[2,12,64,128]{3,2,1,0:T(8,128)(2,1)S(1)}, u32[]{:S(2)}, u32[]{:S(2)}) collective-permute-start(bf16[2,12,64,128]{3,2,1,0:T(8,128)(2,1)S(1)} %get-tuple-element.117), channel_id=1, source_target_pairs={{0,1},{1,0},{2,3},{3,2},{4,5},{5,4},{6,7},{7,6},{8,24},{9,25},{10,... | collective-permute-start | bytes 1179656 | tf_op jit(solution)/shard_map/ppermute | solution.py:208
  49.0 1.6 %shard_map.33.refs_7_ = f32[2,2,256,256]{3,2,1,0:T(8,128)S(1)} custom-call(f32[8,2,128]{2,1,0:T(2,128)S(1)} %maximum_bitcast_fusion.weights_ref, bf16[2,12,64,128]{3,2,1,0:T(8,128)(2,1)S(1)} %collective-permute-done.refs_4_.refs_0_, bf16[2,12,64,128]{3,2,1,0:T(8,128)(2,1)S(1)} %collective-permute-done.2.refs_3_.refs_2_.refs_1_, ...), custom_call_target="tpu_custom_call" | custom-call | flops 1006632960 | bytes 4063232 | tf_op jit(solution)/shard_map/pallas_call | solution.py:263
  50.7 3.4 %collective-permute-done.13.a3_ref = bf16[2,12,64,128]{3,2,1,0:T(8,128)(2,1)S(1)} collective-permute-done((bf16[2,12,64,128]{3,2,1,0:T(8,128)(2,1)S(1)}, bf16[2,12,64,128]{3,2,1,0:T(8,128)(2,1)S(1)}, u32[]{:S(2)}, u32[]{:S(2)}) %collective-permute-start.13) | collective-permute-done | bytes 393248 | tf_op jit(solution)/shard_map/ppermute | solution.py:208
  54.0 0.0 collective-permute-done.14.ab3_ref
  54.0 0.1 shard_map.34.refs_5_
  54.1 0.1 collective-permute-start.16
  54.2 0.0 collective-permute-done.15.refs_6_
  54.2 2.3 %shard_map.35 = (f32[2,2,256,256]{3,2,1,0:T(8,128)S(1)}, bf16[6,512,768]{2,1,0:T(8,128)(2,1)S(1)}) custom-call(f32[8,2,128]{2,1,0:T(2,128)S(1)} %maximum_bitcast_fusion.weights_ref, bf16[2,12,64,128]{3,2,1,0:T(8,128)(2,1)S(1)} %collective-permute-done.refs_4_.refs_0_, bf16[2,12,64,128]{3,2,1,0:T(8,128)(2,1)S(1)} %collective-permute-done.2.refs_3_.refs_2_.refs_1_, ...), custom_call_target="tpu_custom_call" | custom-call | flops 16106127360 | bytes 5242880 | tf_op jit(solution)/shard_map/pallas_call | solution.py:263
  56.5 0.0 collective-permute-done.16.refs_0_
  56.5 0.7 %shard_map.36.refs_3_ = f32[2,2,256,256]{3,2,1,0:T(8,128)S(1)} custom-call(f32[8,2,128]{2,1,0:T(2,128)S(1)} %maximum_bitcast_fusion.weights_ref, bf16[2,2,12,64,128]{4,3,2,1,0:T(8,128)(2,1)S(1)} %collective-permute-done.16.refs_0_, bf16[6,512,768]{2,1,0:T(8,128)(2,1)S(1)} %get-tuple-element.148.refs_1_.refs_2_, f32[2,2,256,256]{3,2,1,0:T(8,128)S(1)} %get-tuple-element.139.refs_2_), custom_call_target="tpu_custom_call" | custom-call | flops 402653184 | bytes 2883584 | tf_op jit(solution)/shard_map/pallas_call | solution.py:263
  57.2 1.0 %collective-permute-done.12.refs_1_ = bf16[2,12,64,128]{3,2,1,0:T(8,128)(2,1)S(1)} collective-permute-done((bf16[2,12,64,128]{3,2,1,0:T(8,128)(2,1)S(1)}, bf16[2,12,64,128]{3,2,1,0:T(8,128)(2,1)S(1)}, u32[]{:S(2)}, u32[]{:S(2)}) %collective-permute-start.12) | collective-permute-done | bytes 393248 | tf_op jit(solution)/shard_map/ppermute | solution.py:208
  58.2 0.0 collective-permute-done.11.refs_0_
  58.2 0.0 collective-permute-start.17
  58.2 0.5 collective-permute-start.18
  58.7 1.3 %shard_map.37 = (f32[2,2,256,256]{3,2,1,0:T(8,128)S(1)}, f32[16,64,256]{2,1,0:T(8,128)}) custom-call(f32[8,2,128]{2,1,0:T(2,128)S(1)} %maximum_bitcast_fusion.weights_ref, bf16[2,12,64,128]{3,2,1,0:T(8,128)(2,1)S(1)} %collective-permute-done.11.refs_0_, bf16[2,12,64,128]{3,2,1,0:T(8,128)(2,1)S(1)} %collective-permute-done.12.refs_1_, ...), custom_call_target="tpu_custom_call" | custom-call | flops 402653184 | bytes 2883584 | tf_op jit(solution)/shard_map/pallas_call | solution.py:263
  60.0 0.0 collective-permute-done.17.refs_0_
  60.0 0.5 collective-permute-done.18.refs_1_
  60.5 1.5 %shard_map.38 = f32[16,64,256]{2,1,0:T(8,128)} custom-call(f32[8,2,128]{2,1,0:T(2,128)S(1)} %maximum_bitcast_fusion.weights_ref, bf16[2,12,64,128]{3,2,1,0:T(8,128)(2,1)S(1)} %collective-permute-done.17.refs_0_, bf16[2,12,64,128]{3,2,1,0:T(8,128)(2,1)S(1)} %collective-permute-done.18.refs_1_, ...), custom_call_target="tpu_custom_call", output_to_operand_aliasing={{}: (5, {})} | custom-call | flops 402653184 | bytes 2883584 | tf_op jit(solution)/shard_map/pallas_call | solution.py:263
  (5 shorter events, 0.1 us)
Async XLA Ops:
  0.0 8.6 %copy-start = (s32[4,3]{1,0:T(4,128)S(1)}, s32[4,3]{1,0:T(4,128)}, u32[]{:S(2)}) copy-start(s32[4,3]{1,0:T(4,128)} %param.3) | copy-start | bytes 148
  0.0 9.0 %collective-permute-start.1 = (bf16[2,12,64,128]{3,2,1,0:T(8,128)(2,1)}, bf16[2,12,64,128]{3,2,1,0:T(8,128)(2,1)S(1)}, u32[]{:S(2)}, u32[]{:S(2)}) collective-permute-start(bf16[2,12,64,128]{3,2,1,0:T(8,128)(2,1)} %bitcast.24), channel_id=1, source_target_pairs={{0,16},{1,17},{2,18},{3,19},{4,20},{5,21},{6,22},{7,23},{8,9},{9,8... | collective-permute-start | bytes 1179656 | tf_op jit(solution)/shard_map/ppermute | solution.py:208
  2.9 20.3 %collective-permute-start = (bf16[2,12,64,128]{3,2,1,0:T(8,128)(2,1)}, bf16[2,12,64,128]{3,2,1,0:T(8,128)(2,1)S(1)}, u32[]{:S(2)}, u32[]{:S(2)}) collective-permute-start(bf16[2,12,64,128]{3,2,1,0:T(8,128)(2,1)} %bitcast.25), channel_id=1, source_target_pairs={{0,4},{1,5},{2,6},{3,7},{4,0},{5,1},{6,2},{7,3},{8,12},{9,13},{10,... | collective-permute-start | bytes 1179656 | tf_op jit(solution)/shard_map/ppermute | solution.py:208
  5.5 17.8 %collective-permute-start.2 = (bf16[2,12,64,128]{3,2,1,0:T(8,128)(2,1)}, bf16[2,12,64,128]{3,2,1,0:T(8,128)(2,1)S(1)}, u32[]{:S(2)}, u32[]{:S(2)}) collective-permute-start(bf16[2,12,64,128]{3,2,1,0:T(8,128)(2,1)} %bitcast.26), channel_id=1, source_target_pairs={{0,2},{1,3},{2,0},{3,1},{4,6},{5,7},{6,4},{7,5},{8,10},{9,11},{10,... | collective-permute-start | bytes 1179656 | tf_op jit(solution)/shard_map/ppermute | solution.py:208
  7.1 16.3 %collective-permute-start.3 = (bf16[2,12,64,128]{3,2,1,0:T(8,128)(2,1)}, bf16[2,12,64,128]{3,2,1,0:T(8,128)(2,1)S(1)}, u32[]{:S(2)}, u32[]{:S(2)}) collective-permute-start(bf16[2,12,64,128]{3,2,1,0:T(8,128)(2,1)} %bitcast.27), channel_id=1, source_target_pairs={{0,1},{1,0},{2,3},{3,2},{4,5},{5,4},{6,7},{7,6},{8,24},{9,25},{10,... | collective-permute-start | bytes 1179656 | tf_op jit(solution)/shard_map/ppermute | solution.py:208
  8.6 14.8 %collective-permute-start.5 = (bf16[2,12,64,128]{3,2,1,0:T(8,128)(2,1)}, bf16[2,12,64,128]{3,2,1,0:T(8,128)(2,1)S(1)}, u32[]{:S(2)}, u32[]{:S(2)}) collective-permute-start(bf16[2,12,64,128]{3,2,1,0:T(8,128)(2,1)} %bitcast.28), channel_id=1, source_target_pairs={{0,8},{1,9},{2,10},{3,11},{4,12},{5,13},{6,14},{7,15},{8,0},{9,1},... | collective-permute-start | bytes 1179656 | tf_op jit(solution)/shard_map/ppermute | solution.py:208
  9.0 14.4 %collective-permute-start.4 = (bf16[2,12,64,128]{3,2,1,0:T(8,128)(2,1)S(1)}, bf16[2,12,64,128]{3,2,1,0:T(8,128)(2,1)S(1)}, u32[]{:S(2)}, u32[]{:S(2)}) collective-permute-start(bf16[2,12,64,128]{3,2,1,0:T(8,128)(2,1)S(1)} %collective-permute-done.1.refs_0_.refs_1_), channel_id=1, source_target_pairs={{0,1},{1,0},{2,3},{3,2},{4,5},{5,4},{6,7},{7,6},{8,24},{9,25},{10,... | collective-permute-start | bytes 1179656 | tf_op jit(solution)/shard_map/ppermute | solution.py:208
  23.6 8.7 %collective-permute-start.6 = (bf16[5,2,12,64,128]{4,3,2,1,0:T(8,128)(2,1)S(1)}, bf16[5,2,12,64,128]{4,3,2,1,0:T(8,128)(2,1)S(1)}, u32[]{:S(2)}, u32[]{:S(2)}) collective-permute-start(bf16[5,2,12,64,128]{4,3,2,1,0:T(8,128)(2,1)S(1)} %get-tuple-element.94), channel_id=1, source_target_pairs={{0,8},{1,9},{2,10},{3,11},{4,12},{5,13},{6,14},{7,15},{8,0},{9,1},... | collective-permute-start | bytes 5898248 | tf_op jit(solution)/shard_map/ppermute | solution.py:208
  23.7 18.0 %collective-permute-start.7 = (bf16[2,12,64,128]{3,2,1,0:T(8,128)(2,1)S(1)}, bf16[2,12,64,128]{3,2,1,0:T(8,128)(2,1)S(1)}, u32[]{:S(2)}, u32[]{:S(2)}) collective-permute-start(bf16[2,12,64,128]{3,2,1,0:T(8,128)(2,1)S(1)} %collective-permute-done.refs_4_.refs_0_), channel_id=1, source_target_pairs={{0,2},{1,3},{2,0},{3,1},{4,6},{5,7},{6,4},{7,5},{8,10},{9,11},{10,... | collective-permute-start | bytes 1179656 | tf_op jit(solution)/shard_map/ppermute | solution.py:208
  25.2 22.0 %collective-permute-start.10 = (bf16[2,2,12,64,128]{4,3,2,1,0:T(8,128)(2,1)S(1)}, bf16[2,2,12,64,128]{4,3,2,1,0:T(8,128)(2,1)S(1)}, u32[]{:S(2)}, u32[]{:S(2)}) collective-permute-start(bf16[2,2,12,64,128]{4,3,2,1,0:T(8,128)(2,1)S(1)} %get-tuple-element.107), channel_id=1, source_target_pairs={{0,1},{1,0},{2,3},{3,2},{4,5},{5,4},{6,7},{7,6},{8,24},{9,25},{10,... | collective-permute-start | bytes 2359304 | tf_op jit(solution)/shard_map/ppermute | solution.py:208
  25.7 21.5 %collective-permute-start.9 = (bf16[2,2,12,64,128]{4,3,2,1,0:T(8,128)(2,1)S(1)}, bf16[2,2,12,64,128]{4,3,2,1,0:T(8,128)(2,1)S(1)}, u32[]{:S(2)}, u32[]{:S(2)}) collective-permute-start(bf16[2,2,12,64,128]{4,3,2,1,0:T(8,128)(2,1)S(1)} %get-tuple-element.107), channel_id=1, source_target_pairs={{0,16},{1,17},{2,18},{3,19},{4,20},{5,21},{6,22},{7,23},{8,9},{9,8... | collective-permute-start | bytes 2359304 | tf_op jit(solution)/shard_map/ppermute | solution.py:208
  27.2 20.0 %collective-permute-start.8 = (bf16[2,12,64,128]{3,2,1,0:T(8,128)(2,1)S(1)}, bf16[2,12,64,128]{3,2,1,0:T(8,128)(2,1)S(1)}, u32[]{:S(2)}, u32[]{:S(2)}) collective-permute-start(bf16[2,12,64,128]{3,2,1,0:T(8,128)(2,1)S(1)} %collective-permute-done.4.refs_2_.refs_4_), channel_id=1, source_target_pairs={{0,4},{1,5},{2,6},{3,7},{4,0},{5,1},{6,2},{7,3},{8,12},{9,13},{10,... | collective-permute-start | bytes 1179656 | tf_op jit(solution)/shard_map/ppermute | solution.py:208
  29.5 1.0 %copy-start.1 = (bf16[2,1,64,12,128]{4,2,3,1,0:T(8,128)(2,1)S(1)}, bf16[2,1,64,12,128]{4,2,3,1,0:T(8,128)(2,1)}, u32[]{:S(2)}) copy-start(bf16[2,1,64,12,128]{4,2,3,1,0:T(8,128)(2,1)} %param.2) | copy-start | bytes 1179652
  41.6 12.4 %collective-permute-start.13 = (bf16[2,12,64,128]{3,2,1,0:T(8,128)(2,1)S(1)}, bf16[2,12,64,128]{3,2,1,0:T(8,128)(2,1)S(1)}, u32[]{:S(2)}, u32[]{:S(2)}) collective-permute-start(bf16[2,12,64,128]{3,2,1,0:T(8,128)(2,1)S(1)} %collective-permute-done.7.refs_0_.o3_ref.refs_2_), channel_id=1, source_target_pairs={{0,16},{1,17},{2,18},{3,19},{4,20},{5,21},{6,22},{7,23},{8,9},{9,8... | collective-permute-start | bytes 1179656 | tf_op jit(solution)/shard_map/ppermute | solution.py:208
  44.1 10.0 %collective-permute-start.14 = (bf16[2,12,64,128]{3,2,1,0:T(8,128)(2,1)S(1)}, bf16[2,12,64,128]{3,2,1,0:T(8,128)(2,1)S(1)}, u32[]{:S(2)}, u32[]{:S(2)}) collective-permute-start(bf16[2,12,64,128]{3,2,1,0:T(8,128)(2,1)S(1)} %collective-permute-done.7.refs_0_.o3_ref.refs_2_), channel_id=1, source_target_pairs={{0,1},{1,0},{2,3},{3,2},{4,5},{5,4},{6,7},{7,6},{8,24},{9,25},{10,... | collective-permute-start | bytes 1179656 | tf_op jit(solution)/shard_map/ppermute | solution.py:208
  47.2 11.1 %collective-permute-start.11 = (bf16[2,12,64,128]{3,2,1,0:T(8,128)(2,1)S(1)}, bf16[2,12,64,128]{3,2,1,0:T(8,128)(2,1)S(1)}, u32[]{:S(2)}, u32[]{:S(2)}) collective-permute-start(bf16[2,12,64,128]{3,2,1,0:T(8,128)(2,1)S(1)} %collective-permute-done.8.ab2_ref.refs_2_), channel_id=1, source_target_pairs={{0,2},{1,3},{2,0},{3,1},{4,6},{5,7},{6,4},{7,5},{8,10},{9,11},{10,... | collective-permute-start | bytes 1179656 | tf_op jit(solution)/shard_map/ppermute | solution.py:208
  47.4 6.8 %collective-permute-start.15 = (bf16[6,2,12,64,128]{4,3,2,1,0:T(8,128)(2,1)S(1)}, bf16[6,2,12,64,128]{4,3,2,1,0:T(8,128)(2,1)S(1)}, u32[]{:S(2)}, u32[]{:S(2)}) collective-permute-start(bf16[6,2,12,64,128]{4,3,2,1,0:T(8,128)(2,1)S(1)} %get-tuple-element.133), channel_id=1, source_target_pairs={{0,8},{1,9},{2,10},{3,11},{4,12},{5,13},{6,14},{7,15},{8,0},{9,1},... | collective-permute-start | bytes 7077896 | tf_op jit(solution)/shard_map/ppermute | solution.py:208
  47.4 10.8 %collective-permute-start.12 = (bf16[2,12,64,128]{3,2,1,0:T(8,128)(2,1)S(1)}, bf16[2,12,64,128]{3,2,1,0:T(8,128)(2,1)S(1)}, u32[]{:S(2)}, u32[]{:S(2)}) collective-permute-start(bf16[2,12,64,128]{3,2,1,0:T(8,128)(2,1)S(1)} %get-tuple-element.117), channel_id=1, source_target_pairs={{0,1},{1,0},{2,3},{3,2},{4,5},{5,4},{6,7},{7,6},{8,24},{9,25},{10,... | collective-permute-start | bytes 1179656 | tf_op jit(solution)/shard_map/ppermute | solution.py:208
  54.1 2.4 %collective-permute-start.16 = (bf16[2,2,12,64,128]{4,3,2,1,0:T(8,128)(2,1)S(1)}, bf16[2,2,12,64,128]{4,3,2,1,0:T(8,128)(2,1)S(1)}, u32[]{:S(2)}, u32[]{:S(2)}) collective-permute-start(bf16[2,2,12,64,128]{4,3,2,1,0:T(8,128)(2,1)S(1)} %shard_map.34.refs_5_), channel_id=1, source_target_pairs={{0,8},{1,9},{2,10},{3,11},{4,12},{5,13},{6,14},{7,15},{8,0},{9,1},... | collective-permute-start | bytes 2359304 | tf_op jit(solution)/shard_map/ppermute | solution.py:208
  58.2 1.8 %collective-permute-start.17 = (bf16[2,12,64,128]{3,2,1,0:T(8,128)(2,1)S(1)}, bf16[2,12,64,128]{3,2,1,0:T(8,128)(2,1)S(1)}, u32[]{:S(2)}, u32[]{:S(2)}) collective-permute-start(bf16[2,12,64,128]{3,2,1,0:T(8,128)(2,1)S(1)} %collective-permute-done.11.refs_0_), channel_id=1, source_target_pairs={{0,8},{1,9},{2,10},{3,11},{4,12},{5,13},{6,14},{7,15},{8,0},{9,1},... | collective-permute-start | bytes 1179656 | tf_op jit(solution)/shard_map/ppermute | solution.py:208
  58.2 2.3 %collective-permute-start.18 = (bf16[2,12,64,128]{3,2,1,0:T(8,128)(2,1)S(1)}, bf16[2,12,64,128]{3,2,1,0:T(8,128)(2,1)S(1)}, u32[]{:S(2)}, u32[]{:S(2)}) collective-permute-start(bf16[2,12,64,128]{3,2,1,0:T(8,128)(2,1)S(1)} %collective-permute-done.12.refs_1_), channel_id=1, source_target_pairs={{0,8},{1,9},{2,10},{3,11},{4,12},{5,13},{6,14},{7,15},{8,0},{9,1},... | collective-permute-start | bytes 1179656 | tf_op jit(solution)/shard_map/ppermute | solution.py:208

commit v25 on v24

--- a/solution.py
+++ b/solution.py
@@ -348,11 +348,11 @@
     put("3c", ab1, "near", fourth[1:])
     totals, left = fence((totals, left))
 
-    far4 = [swap(near(*kind)) for kind in fourth]
+    (stack,) = route(route_last, [near(*kind) for kind in fourth], (2,))
+    far4 = swap(stack)
     names = [("near", *kind) for kind in fourth]
     totals, field = add(names, totals, left=(slots, left), half=True)
-    put("4b", far4[0], "far", fourth[:1])
-    put("4c", far4[1], "far", fourth[1:])
+    put("4b", far4, "far", fourth)
     totals, left, field = fence((totals, left, field))
     return add([("far", *kind) for kind in fourth], totals, left=(slots, left), field=field)
 

time: 62.2 us -> 62.3 us (level)
    ppermute x19 -> x18, waiting for transfers between devices: 26.2 us -> 26.6 us  [move(): return lax.ppermute(array, AXES, pairs)]
    ppermute x19 -> x18, starting transfers between devices: 22.6 us -> 22.2 us  [move(): return lax.ppermute(array, AXES, pairs)]
  transfers between devices with their start and end apart: 19 -> 18, of which waited for: 8 -> 8; matrix products, arithmetic and copies ran while one was open for 0% -> 0% of each run, Pallas kernels for 16% -> 16%
where the time goes in v25:
time: 62.3 us; the launch traced here: 62.1 us
  waiting for transfers between devices  26.6 us (43%)
  starting transfers between devices  22.2 us (36%)
  Pallas kernels  11.9 us (19%)
  local copies, waits for them, and re-layouts  1 us (2%)
    ppermute x18, waiting for transfers between devices, move(): return lax.ppermute(array, AXES, pairs)  26.6 us
    ppermute x18, starting transfers between devices, move(): return lax.ppermute(array, AXES, pairs)  22.2 us
    pallas_call x8, Pallas kernels, add(): pl.pallas_call(functools.partial(add_shards, tuple(names), places, slots,...  11.4 us
  transfers between devices with their start and end apart: 18, of which 8 were waited for; matrix products, arithmetic and copies ran while one was open for 0% of the time, Pallas kernels for 16%

profile of v25, /device:TPU:0, one launch (start us, length us, event | category | flops | bytes accessed | tf_op | source)
XLA Modules:
  0.0 62.1 jit_solution(5202974716912831391)
XLA Ops:
  0.0 0.0 copy-start
  0.0 2.9 %collective-permute-start.1 = (bf16[2,12,64,128]{3,2,1,0:T(8,128)(2,1)}, bf16[2,12,64,128]{3,2,1,0:T(8,128)(2,1)S(1)}, u32[]{:S(2)}, u32[]{:S(2)}) collective-permute-start(bf16[2,12,64,128]{3,2,1,0:T(8,128)(2,1)} %bitcast.24), channel_id=1, source_target_pairs={{0,16},{1,17},{2,18},{3,19},{4,20},{5,21},{6,22},{7,23},{8,9},{9,8... | collective-permute-start | bytes 1179656 | tf_op jit(solution)/shard_map/ppermute | solution.py:208
  2.9 2.6 %collective-permute-start = (bf16[2,12,64,128]{3,2,1,0:T(8,128)(2,1)}, bf16[2,12,64,128]{3,2,1,0:T(8,128)(2,1)S(1)}, u32[]{:S(2)}, u32[]{:S(2)}) collective-permute-start(bf16[2,12,64,128]{3,2,1,0:T(8,128)(2,1)} %bitcast.25), channel_id=1, source_target_pairs={{0,4},{1,5},{2,6},{3,7},{4,0},{5,1},{6,2},{7,3},{8,12},{9,13},{10,... | collective-permute-start | bytes 1179656 | tf_op jit(solution)/shard_map/ppermute | solution.py:208
  5.5 1.6 %collective-permute-start.2 = (bf16[2,12,64,128]{3,2,1,0:T(8,128)(2,1)}, bf16[2,12,64,128]{3,2,1,0:T(8,128)(2,1)S(1)}, u32[]{:S(2)}, u32[]{:S(2)}) collective-permute-start(bf16[2,12,64,128]{3,2,1,0:T(8,128)(2,1)} %bitcast.26), channel_id=1, source_target_pairs={{0,2},{1,3},{2,0},{3,1},{4,6},{5,7},{6,4},{7,5},{8,10},{9,11},{10,... | collective-permute-start | bytes 1179656 | tf_op jit(solution)/shard_map/ppermute | solution.py:208
  7.1 1.5 %collective-permute-start.3 = (bf16[2,12,64,128]{3,2,1,0:T(8,128)(2,1)}, bf16[2,12,64,128]{3,2,1,0:T(8,128)(2,1)S(1)}, u32[]{:S(2)}, u32[]{:S(2)}) collective-permute-start(bf16[2,12,64,128]{3,2,1,0:T(8,128)(2,1)} %bitcast.27), channel_id=1, source_target_pairs={{0,1},{1,0},{2,3},{3,2},{4,5},{5,4},{6,7},{7,6},{8,24},{9,25},{10,... | collective-permute-start | bytes 1179656 | tf_op jit(solution)/shard_map/ppermute | solution.py:208
  8.6 0.0 collective-permute-start.5
  8.6 0.0 copy-done
  8.7 0.1 fusion
  8.8 0.2 collective-permute-done.1.refs_0_.refs_1_
  9.0 3.4 %collective-permute-start.4 = (bf16[2,12,64,128]{3,2,1,0:T(8,128)(2,1)S(1)}, bf16[2,12,64,128]{3,2,1,0:T(8,128)(2,1)S(1)}, u32[]{:S(2)}, u32[]{:S(2)}) collective-permute-start(bf16[2,12,64,128]{3,2,1,0:T(8,128)(2,1)S(1)} %collective-permute-done.1.refs_0_.refs_1_), channel_id=1, source_target_pairs={{0,1},{1,0},{2,3},{3,2},{4,5},{5,4},{6,7},{7,6},{8,24},{9,25},{10,... | collective-permute-start | bytes 1179656 | tf_op jit(solution)/shard_map/ppermute | solution.py:208
  12.4 0.1 multiply_cosine_fusion
  12.6 10.6 %collective-permute-done.refs_4_.refs_0_ = bf16[2,12,64,128]{3,2,1,0:T(8,128)(2,1)S(1)} collective-permute-done((bf16[2,12,64,128]{3,2,1,0:T(8,128)(2,1)}, bf16[2,12,64,128]{3,2,1,0:T(8,128)(2,1)S(1)}, u32[]{:S(2)}, u32[]{:S(2)}) %collective-permute-start) | collective-permute-done | bytes 393248 | tf_op jit(solution)/shard_map/ppermute | solution.py:208
  23.2 0.2 collective-permute-done.2.refs_3_.refs_2_.refs_1_
  23.4 0.0 collective-permute-done.3.refs_1_.refs_3_
  23.4 0.0 collective-permute-done.5.refs_4_
  23.4 0.0 collective-permute-done.4.refs_2_.refs_4_
  23.4 0.2 shard_map.28
  23.6 0.1 collective-permute-start.6
  23.7 1.5 %collective-permute-start.7 = (bf16[2,12,64,128]{3,2,1,0:T(8,128)(2,1)S(1)}, bf16[2,12,64,128]{3,2,1,0:T(8,128)(2,1)S(1)}, u32[]{:S(2)}, u32[]{:S(2)}) collective-permute-start(bf16[2,12,64,128]{3,2,1,0:T(8,128)(2,1)S(1)} %collective-permute-done.refs_4_.refs_0_), channel_id=1, source_target_pairs={{0,2},{1,3},{2,0},{3,1},{4,6},{5,7},{6,4},{7,5},{8,10},{9,11},{10,... | collective-permute-start | bytes 1179656 | tf_op jit(solution)/shard_map/ppermute | solution.py:208
  25.2 0.5 collective-permute-start.10
  25.7 1.5 %collective-permute-start.9 = (bf16[2,2,12,64,128]{4,3,2,1,0:T(8,128)(2,1)S(1)}, bf16[2,2,12,64,128]{4,3,2,1,0:T(8,128)(2,1)S(1)}, u32[]{:S(2)}, u32[]{:S(2)}) collective-permute-start(bf16[2,2,12,64,128]{4,3,2,1,0:T(8,128)(2,1)S(1)} %get-tuple-element.109), channel_id=1, source_target_pairs={{0,16},{1,17},{2,18},{3,19},{4,20},{5,21},{6,22},{7,23},{8,9},{9,8... | collective-permute-start | bytes 2359304 | tf_op jit(solution)/shard_map/ppermute | solution.py:208
  27.2 2.3 %collective-permute-start.8 = (bf16[2,12,64,128]{3,2,1,0:T(8,128)(2,1)S(1)}, bf16[2,12,64,128]{3,2,1,0:T(8,128)(2,1)S(1)}, u32[]{:S(2)}, u32[]{:S(2)}) collective-permute-start(bf16[2,12,64,128]{3,2,1,0:T(8,128)(2,1)S(1)} %collective-permute-done.4.refs_2_.refs_4_), channel_id=1, source_target_pairs={{0,4},{1,5},{2,6},{3,7},{4,0},{5,1},{6,2},{7,3},{8,12},{9,13},{10,... | collective-permute-start | bytes 1179656 | tf_op jit(solution)/shard_map/ppermute | solution.py:208
  29.5 0.0 copy-start.1
  29.5 1.0 %copy-done.1 = bf16[2,1,64,12,128]{4,2,3,1,0:T(8,128)(2,1)S(1)} copy-done((bf16[2,1,64,12,128]{4,2,3,1,0:T(8,128)(2,1)S(1)}, bf16[2,1,64,12,128]{4,2,3,1,0:T(8,128)(2,1)}, u32[]{:S(2)}) %copy-start.1) | copy-done | bytes 393240
  30.5 1.8 %shard_map.29.refs_7_ = f32[2,2,256,256]{3,2,1,0:T(8,128)S(1)} custom-call(f32[8,2,128]{2,1,0:T(2,128)S(1)} %maximum_bitcast_fusion.weights_ref, bf16[2,12,64,128]{3,2,1,0:T(8,128)(2,1)S(1)} %collective-permute-done.refs_4_.refs_0_, bf16[2,12,64,128]{3,2,1,0:T(8,128)(2,1)S(1)} %collective-permute-done.1.refs_0_.refs_1_, ...), custom_call_target="tpu_custom_call" | custom-call | flops 1207959552 | bytes 4456448 | tf_op jit(solution)/shard_map/pallas_call | solution.py:263
  32.3 0.0 collective-permute-done.6.refs_5_
  32.3 1.7 %shard_map.30.refs_1_ = f32[2,2,256,256]{3,2,1,0:T(8,128)S(1)} custom-call(f32[8,2,128]{2,1,0:T(2,128)S(1)} %maximum_bitcast_fusion.weights_ref, bf16[2,12,64,128]{3,2,1,0:T(8,128)(2,1)S(1)} %collective-permute-done.refs_4_.refs_0_, bf16[2,12,64,128]{3,2,1,0:T(8,128)(2,1)S(1)} %collective-permute-done.1.refs_0_.refs_1_, ...), custom_call_target="tpu_custom_call" | custom-call | flops 1207959552 | bytes 4456448 | tf_op jit(solution)/shard_map/pallas_call | solution.py:263
  34.0 7.6 %collective-permute-done.7.refs_0_.o3_ref.refs_2_ = bf16[2,12,64,128]{3,2,1,0:T(8,128)(2,1)S(1)} collective-permute-done((bf16[2,12,64,128]{3,2,1,0:T(8,128)(2,1)S(1)}, bf16[2,12,64,128]{3,2,1,0:T(8,128)(2,1)S(1)}, u32[]{:S(2)}, u32[]{:S(2)}) %collective-permute-start.7) | collective-permute-done | bytes 393248 | tf_op jit(solution)/shard_map/ppermute | solution.py:208
  41.6 2.4 %collective-permute-start.13 = (bf16[2,12,64,128]{3,2,1,0:T(8,128)(2,1)S(1)}, bf16[2,12,64,128]{3,2,1,0:T(8,128)(2,1)S(1)}, u32[]{:S(2)}, u32[]{:S(2)}) collective-permute-start(bf16[2,12,64,128]{3,2,1,0:T(8,128)(2,1)S(1)} %collective-permute-done.7.refs_0_.o3_ref.refs_2_), channel_id=1, source_target_pairs={{0,16},{1,17},{2,18},{3,19},{4,20},{5,21},{6,22},{7,23},{8,9},{9,8... | collective-permute-start | bytes 1179656 | tf_op jit(solution)/shard_map/ppermute | solution.py:208
  44.1 0.0 collective-permute-start.14
  44.1 0.4 shard_map.31.refs_5_
  44.5 2.7 %collective-permute-done.8.ab2_ref.refs_2_ = bf16[2,12,64,128]{3,2,1,0:T(8,128)(2,1)S(1)} collective-permute-done((bf16[2,12,64,128]{3,2,1,0:T(8,128)(2,1)S(1)}, bf16[2,12,64,128]{3,2,1,0:T(8,128)(2,1)S(1)}, u32[]{:S(2)}, u32[]{:S(2)}) %collective-permute-start.8) | collective-permute-done | bytes 393248 | tf_op jit(solution)/shard_map/ppermute | solution.py:208
  47.2 0.0 collective-permute-done.10.b12_ref.refs_4_
  47.2 0.0 collective-permute-done.9.a12_ref.refs_3_
  47.2 0.0 collective-permute-start.11
  47.2 0.2 shard_map.32
  47.4 0.1 collective-permute-start.15
  47.4 1.6 %collective-permute-start.12 = (bf16[2,12,64,128]{3,2,1,0:T(8,128)(2,1)S(1)}, bf16[2,12,64,128]{3,2,1,0:T(8,128)(2,1)S(1)}, u32[]{:S(2)}, u32[]{:S(2)}) collective-permute-start(bf16[2,12,64,128]{3,2,1,0:T(8,128)(2,1)S(1)} %get-tuple-element.119), channel_id=1, source_target_pairs={{0,1},{1,0},{2,3},{3,2},{4,5},{5,4},{6,7},{7,6},{8,24},{9,25},{10,... | collective-permute-start | bytes 1179656 | tf_op jit(solution)/shard_map/ppermute | solution.py:208
  49.0 1.6 %shard_map.33.refs_7_ = f32[2,2,256,256]{3,2,1,0:T(8,128)S(1)} custom-call(f32[8,2,128]{2,1,0:T(2,128)S(1)} %maximum_bitcast_fusion.weights_ref, bf16[2,12,64,128]{3,2,1,0:T(8,128)(2,1)S(1)} %collective-permute-done.refs_4_.refs_0_, bf16[2,12,64,128]{3,2,1,0:T(8,128)(2,1)S(1)} %collective-permute-done.2.refs_3_.refs_2_.refs_1_, ...), custom_call_target="tpu_custom_call" | custom-call | flops 1006632960 | bytes 4063232 | tf_op jit(solution)/shard_map/pallas_call | solution.py:263
  50.7 3.4 %collective-permute-done.13.a3_ref = bf16[2,12,64,128]{3,2,1,0:T(8,128)(2,1)S(1)} collective-permute-done((bf16[2,12,64,128]{3,2,1,0:T(8,128)(2,1)S(1)}, bf16[2,12,64,128]{3,2,1,0:T(8,128)(2,1)S(1)}, u32[]{:S(2)}, u32[]{:S(2)}) %collective-permute-start.13) | collective-permute-done | bytes 393248 | tf_op jit(solution)/shard_map/ppermute | solution.py:208
  54.0 0.0 collective-permute-done.14.ab3_ref
  54.0 0.1 shard_map.34.refs_5_
  54.1 0.1 collective-permute-start.16
  54.2 0.0 collective-permute-done.15.refs_6_
  54.2 2.4 %shard_map.35 = (f32[2,2,256,256]{3,2,1,0:T(8,128)S(1)}, bf16[6,512,768]{2,1,0:T(8,128)(2,1)S(1)}) custom-call(f32[8,2,128]{2,1,0:T(2,128)S(1)} %maximum_bitcast_fusion.weights_ref, bf16[2,12,64,128]{3,2,1,0:T(8,128)(2,1)S(1)} %collective-permute-done.refs_4_.refs_0_, bf16[2,12,64,128]{3,2,1,0:T(8,128)(2,1)S(1)} %collective-permute-done.2.refs_3_.refs_2_.refs_1_, ...), custom_call_target="tpu_custom_call" | custom-call | flops 16106127360 | bytes 5242880 | tf_op jit(solution)/shard_map/pallas_call | solution.py:263
  56.5 0.0 collective-permute-done.16.refs_0_
  56.5 0.7 %shard_map.36.refs_3_ = f32[2,2,256,256]{3,2,1,0:T(8,128)S(1)} custom-call(f32[8,2,128]{2,1,0:T(2,128)S(1)} %maximum_bitcast_fusion.weights_ref, bf16[2,2,12,64,128]{4,3,2,1,0:T(8,128)(2,1)S(1)} %collective-permute-done.16.refs_0_, bf16[6,512,768]{2,1,0:T(8,128)(2,1)S(1)} %get-tuple-element.152.refs_1_.refs_2_, f32[2,2,256,256]{3,2,1,0:T(8,128)S(1)} %get-tuple-element.141.refs_2_), custom_call_target="tpu_custom_call" | custom-call | flops 402653184 | bytes 2883584 | tf_op jit(solution)/shard_map/pallas_call | solution.py:263
  57.2 1.0 %collective-permute-done.12.ab3_ref.refs_1_ = bf16[2,12,64,128]{3,2,1,0:T(8,128)(2,1)S(1)} collective-permute-done((bf16[2,12,64,128]{3,2,1,0:T(8,128)(2,1)S(1)}, bf16[2,12,64,128]{3,2,1,0:T(8,128)(2,1)S(1)}, u32[]{:S(2)}, u32[]{:S(2)}) %collective-permute-start.12) | collective-permute-done | bytes 393248 | tf_op jit(solution)/shard_map/ppermute | solution.py:208
  58.2 0.0 collective-permute-done.11.a3_ref.refs_0_
  58.2 0.1 shard_map.37
  58.3 0.1 collective-permute-start.17
  58.4 1.3 %shard_map.38 = (f32[2,2,256,256]{3,2,1,0:T(8,128)S(1)}, f32[16,64,256]{2,1,0:T(8,128)}) custom-call(f32[8,2,128]{2,1,0:T(2,128)S(1)} %maximum_bitcast_fusion.weights_ref, bf16[2,12,64,128]{3,2,1,0:T(8,128)(2,1)S(1)} %collective-permute-done.11.a3_ref.refs_0_, bf16[2,12,64,128]{3,2,1,0:T(8,128)(2,1)S(1)} %collective-permute-done.12.ab3_ref.refs_1_, ...), custom_call_target="tpu_custom_call" | custom-call | flops 402653184 | bytes 2883584 | tf_op jit(solution)/shard_map/pallas_call | solution.py:263
  59.6 1.0 %collective-permute-done.17.refs_0_ = bf16[2,2,12,64,128]{4,3,2,1,0:T(8,128)(2,1)S(1)} collective-permute-done((bf16[2,2,12,64,128]{4,3,2,1,0:T(8,128)(2,1)S(1)}, bf16[2,2,12,64,128]{4,3,2,1,0:T(8,128)(2,1)S(1)}, u32[]{:S(2)}, u32[]{:S(2)}) %collective-permute-start.17) | collective-permute-done | bytes 786464 | tf_op jit(solution)/shard_map/ppermute | solution.py:208
  60.6 1.5 %shard_map.39 = f32[16,64,256]{2,1,0:T(8,128)} custom-call(f32[8,2,128]{2,1,0:T(2,128)S(1)} %maximum_bitcast_fusion.weights_ref, bf16[2,2,12,64,128]{4,3,2,1,0:T(8,128)(2,1)S(1)} %collective-permute-done.17.refs_0_, bf16[6,512,768]{2,1,0:T(8,128)(2,1)S(1)} %get-tuple-element.152.refs_1_.refs_2_, ...), custom_call_target="tpu_custom_call", output_to_operand_aliasing={{}: (4, {})} | custom-call | flops 402653184 | bytes 2883584 | tf_op jit(solution)/shard_map/pallas_call | solution.py:263
  (5 shorter events, 0.1 us)
Async XLA Ops:
  0.0 8.6 %copy-start = (s32[4,3]{1,0:T(4,128)S(1)}, s32[4,3]{1,0:T(4,128)}, u32[]{:S(2)}) copy-start(s32[4,3]{1,0:T(4,128)} %param.3) | copy-start | bytes 148
  0.0 9.0 %collective-permute-start.1 = (bf16[2,12,64,128]{3,2,1,0:T(8,128)(2,1)}, bf16[2,12,64,128]{3,2,1,0:T(8,128)(2,1)S(1)}, u32[]{:S(2)}, u32[]{:S(2)}) collective-permute-start(bf16[2,12,64,128]{3,2,1,0:T(8,128)(2,1)} %bitcast.24), channel_id=1, source_target_pairs={{0,16},{1,17},{2,18},{3,19},{4,20},{5,21},{6,22},{7,23},{8,9},{9,8... | collective-permute-start | bytes 1179656 | tf_op jit(solution)/shard_map/ppermute | solution.py:208
  2.9 20.3 %collective-permute-start = (bf16[2,12,64,128]{3,2,1,0:T(8,128)(2,1)}, bf16[2,12,64,128]{3,2,1,0:T(8,128)(2,1)S(1)}, u32[]{:S(2)}, u32[]{:S(2)}) collective-permute-start(bf16[2,12,64,128]{3,2,1,0:T(8,128)(2,1)} %bitcast.25), channel_id=1, source_target_pairs={{0,4},{1,5},{2,6},{3,7},{4,0},{5,1},{6,2},{7,3},{8,12},{9,13},{10,... | collective-permute-start | bytes 1179656 | tf_op jit(solution)/shard_map/ppermute | solution.py:208
  5.5 17.8 %collective-permute-start.2 = (bf16[2,12,64,128]{3,2,1,0:T(8,128)(2,1)}, bf16[2,12,64,128]{3,2,1,0:T(8,128)(2,1)S(1)}, u32[]{:S(2)}, u32[]{:S(2)}) collective-permute-start(bf16[2,12,64,128]{3,2,1,0:T(8,128)(2,1)} %bitcast.26), channel_id=1, source_target_pairs={{0,2},{1,3},{2,0},{3,1},{4,6},{5,7},{6,4},{7,5},{8,10},{9,11},{10,... | collective-permute-start | bytes 1179656 | tf_op jit(solution)/shard_map/ppermute | solution.py:208
  7.1 16.3 %collective-permute-start.3 = (bf16[2,12,64,128]{3,2,1,0:T(8,128)(2,1)}, bf16[2,12,64,128]{3,2,1,0:T(8,128)(2,1)S(1)}, u32[]{:S(2)}, u32[]{:S(2)}) collective-permute-start(bf16[2,12,64,128]{3,2,1,0:T(8,128)(2,1)} %bitcast.27), channel_id=1, source_target_pairs={{0,1},{1,0},{2,3},{3,2},{4,5},{5,4},{6,7},{7,6},{8,24},{9,25},{10,... | collective-permute-start | bytes 1179656 | tf_op jit(solution)/shard_map/ppermute | solution.py:208
  8.6 14.8 %collective-permute-start.5 = (bf16[2,12,64,128]{3,2,1,0:T(8,128)(2,1)}, bf16[2,12,64,128]{3,2,1,0:T(8,128)(2,1)S(1)}, u32[]{:S(2)}, u32[]{:S(2)}) collective-permute-start(bf16[2,12,64,128]{3,2,1,0:T(8,128)(2,1)} %bitcast.28), channel_id=1, source_target_pairs={{0,8},{1,9},{2,10},{3,11},{4,12},{5,13},{6,14},{7,15},{8,0},{9,1},... | collective-permute-start | bytes 1179656 | tf_op jit(solution)/shard_map/ppermute | solution.py:208
  9.0 14.4 %collective-permute-start.4 = (bf16[2,12,64,128]{3,2,1,0:T(8,128)(2,1)S(1)}, bf16[2,12,64,128]{3,2,1,0:T(8,128)(2,1)S(1)}, u32[]{:S(2)}, u32[]{:S(2)}) collective-permute-start(bf16[2,12,64,128]{3,2,1,0:T(8,128)(2,1)S(1)} %collective-permute-done.1.refs_0_.refs_1_), channel_id=1, source_target_pairs={{0,1},{1,0},{2,3},{3,2},{4,5},{5,4},{6,7},{7,6},{8,24},{9,25},{10,... | collective-permute-start | bytes 1179656 | tf_op jit(solution)/shard_map/ppermute | solution.py:208
  23.6 8.7 %collective-permute-start.6 = (bf16[5,2,12,64,128]{4,3,2,1,0:T(8,128)(2,1)S(1)}, bf16[5,2,12,64,128]{4,3,2,1,0:T(8,128)(2,1)S(1)}, u32[]{:S(2)}, u32[]{:S(2)}) collective-permute-start(bf16[5,2,12,64,128]{4,3,2,1,0:T(8,128)(2,1)S(1)} %get-tuple-element.96), channel_id=1, source_target_pairs={{0,8},{1,9},{2,10},{3,11},{4,12},{5,13},{6,14},{7,15},{8,0},{9,1},... | collective-permute-start | bytes 5898248 | tf_op jit(solution)/shard_map/ppermute | solution.py:208
  23.7 18.0 %collective-permute-start.7 = (bf16[2,12,64,128]{3,2,1,0:T(8,128)(2,1)S(1)}, bf16[2,12,64,128]{3,2,1,0:T(8,128)(2,1)S(1)}, u32[]{:S(2)}, u32[]{:S(2)}) collective-permute-start(bf16[2,12,64,128]{3,2,1,0:T(8,128)(2,1)S(1)} %collective-permute-done.refs_4_.refs_0_), channel_id=1, source_target_pairs={{0,2},{1,3},{2,0},{3,1},{4,6},{5,7},{6,4},{7,5},{8,10},{9,11},{10,... | collective-permute-start | bytes 1179656 | tf_op jit(solution)/shard_map/ppermute | solution.py:208
  25.2 22.0 %collective-permute-start.10 = (bf16[2,2,12,64,128]{4,3,2,1,0:T(8,128)(2,1)S(1)}, bf16[2,2,12,64,128]{4,3,2,1,0:T(8,128)(2,1)S(1)}, u32[]{:S(2)}, u32[]{:S(2)}) collective-permute-start(bf16[2,2,12,64,128]{4,3,2,1,0:T(8,128)(2,1)S(1)} %get-tuple-element.109), channel_id=1, source_target_pairs={{0,1},{1,0},{2,3},{3,2},{4,5},{5,4},{6,7},{7,6},{8,24},{9,25},{10,... | collective-permute-start | bytes 2359304 | tf_op jit(solution)/shard_map/ppermute | solution.py:208
  25.7 21.5 %collective-permute-start.9 = (bf16[2,2,12,64,128]{4,3,2,1,0:T(8,128)(2,1)S(1)}, bf16[2,2,12,64,128]{4,3,2,1,0:T(8,128)(2,1)S(1)}, u32[]{:S(2)}, u32[]{:S(2)}) collective-permute-start(bf16[2,2,12,64,128]{4,3,2,1,0:T(8,128)(2,1)S(1)} %get-tuple-element.109), channel_id=1, source_target_pairs={{0,16},{1,17},{2,18},{3,19},{4,20},{5,21},{6,22},{7,23},{8,9},{9,8... | collective-permute-start | bytes 2359304 | tf_op jit(solution)/shard_map/ppermute | solution.py:208
  27.2 20.0 %collective-permute-start.8 = (bf16[2,12,64,128]{3,2,1,0:T(8,128)(2,1)S(1)}, bf16[2,12,64,128]{3,2,1,0:T(8,128)(2,1)S(1)}, u32[]{:S(2)}, u32[]{:S(2)}) collective-permute-start(bf16[2,12,64,128]{3,2,1,0:T(8,128)(2,1)S(1)} %collective-permute-done.4.refs_2_.refs_4_), channel_id=1, source_target_pairs={{0,4},{1,5},{2,6},{3,7},{4,0},{5,1},{6,2},{7,3},{8,12},{9,13},{10,... | collective-permute-start | bytes 1179656 | tf_op jit(solution)/shard_map/ppermute | solution.py:208
  29.5 1.0 %copy-start.1 = (bf16[2,1,64,12,128]{4,2,3,1,0:T(8,128)(2,1)S(1)}, bf16[2,1,64,12,128]{4,2,3,1,0:T(8,128)(2,1)}, u32[]{:S(2)}) copy-start(bf16[2,1,64,12,128]{4,2,3,1,0:T(8,128)(2,1)} %param.2) | copy-start | bytes 1179652
  41.6 12.4 %collective-permute-start.13 = (bf16[2,12,64,128]{3,2,1,0:T(8,128)(2,1)S(1)}, bf16[2,12,64,128]{3,2,1,0:T(8,128)(2,1)S(1)}, u32[]{:S(2)}, u32[]{:S(2)}) collective-permute-start(bf16[2,12,64,128]{3,2,1,0:T(8,128)(2,1)S(1)} %collective-permute-done.7.refs_0_.o3_ref.refs_2_), channel_id=1, source_target_pairs={{0,16},{1,17},{2,18},{3,19},{4,20},{5,21},{6,22},{7,23},{8,9},{9,8... | collective-permute-start | bytes 1179656 | tf_op jit(solution)/shard_map/ppermute | solution.py:208
  44.1 10.0 %collective-permute-start.14 = (bf16[2,12,64,128]{3,2,1,0:T(8,128)(2,1)S(1)}, bf16[2,12,64,128]{3,2,1,0:T(8,128)(2,1)S(1)}, u32[]{:S(2)}, u32[]{:S(2)}) collective-permute-start(bf16[2,12,64,128]{3,2,1,0:T(8,128)(2,1)S(1)} %collective-permute-done.7.refs_0_.o3_ref.refs_2_), channel_id=1, source_target_pairs={{0,1},{1,0},{2,3},{3,2},{4,5},{5,4},{6,7},{7,6},{8,24},{9,25},{10,... | collective-permute-start | bytes 1179656 | tf_op jit(solution)/shard_map/ppermute | solution.py:208
  47.2 11.1 %collective-permute-start.11 = (bf16[2,12,64,128]{3,2,1,0:T(8,128)(2,1)S(1)}, bf16[2,12,64,128]{3,2,1,0:T(8,128)(2,1)S(1)}, u32[]{:S(2)}, u32[]{:S(2)}) collective-permute-start(bf16[2,12,64,128]{3,2,1,0:T(8,128)(2,1)S(1)} %collective-permute-done.8.ab2_ref.refs_2_), channel_id=1, source_target_pairs={{0,2},{1,3},{2,0},{3,1},{4,6},{5,7},{6,4},{7,5},{8,10},{9,11},{10,... | collective-permute-start | bytes 1179656 | tf_op jit(solution)/shard_map/ppermute | solution.py:208
  47.4 6.8 %collective-permute-start.15 = (bf16[6,2,12,64,128]{4,3,2,1,0:T(8,128)(2,1)S(1)}, bf16[6,2,12,64,128]{4,3,2,1,0:T(8,128)(2,1)S(1)}, u32[]{:S(2)}, u32[]{:S(2)}) collective-permute-start(bf16[6,2,12,64,128]{4,3,2,1,0:T(8,128)(2,1)S(1)} %get-tuple-element.135), channel_id=1, source_target_pairs={{0,8},{1,9},{2,10},{3,11},{4,12},{5,13},{6,14},{7,15},{8,0},{9,1},... | collective-permute-start | bytes 7077896 | tf_op jit(solution)/shard_map/ppermute | solution.py:208
  47.4 10.8 %collective-permute-start.12 = (bf16[2,12,64,128]{3,2,1,0:T(8,128)(2,1)S(1)}, bf16[2,12,64,128]{3,2,1,0:T(8,128)(2,1)S(1)}, u32[]{:S(2)}, u32[]{:S(2)}) collective-permute-start(bf16[2,12,64,128]{3,2,1,0:T(8,128)(2,1)S(1)} %get-tuple-element.119), channel_id=1, source_target_pairs={{0,1},{1,0},{2,3},{3,2},{4,5},{5,4},{6,7},{7,6},{8,24},{9,25},{10,... | collective-permute-start | bytes 1179656 | tf_op jit(solution)/shard_map/ppermute | solution.py:208
  54.1 2.5 %collective-permute-start.16 = (bf16[2,2,12,64,128]{4,3,2,1,0:T(8,128)(2,1)S(1)}, bf16[2,2,12,64,128]{4,3,2,1,0:T(8,128)(2,1)S(1)}, u32[]{:S(2)}, u32[]{:S(2)}) collective-permute-start(bf16[2,2,12,64,128]{4,3,2,1,0:T(8,128)(2,1)S(1)} %shard_map.34.refs_5_), channel_id=1, source_target_pairs={{0,8},{1,9},{2,10},{3,11},{4,12},{5,13},{6,14},{7,15},{8,0},{9,1},... | collective-permute-start | bytes 2359304 | tf_op jit(solution)/shard_map/ppermute | solution.py:208
  58.3 2.4 %collective-permute-start.17 = (bf16[2,2,12,64,128]{4,3,2,1,0:T(8,128)(2,1)S(1)}, bf16[2,2,12,64,128]{4,3,2,1,0:T(8,128)(2,1)S(1)}, u32[]{:S(2)}, u32[]{:S(2)}) collective-permute-start(bf16[2,2,12,64,128]{4,3,2,1,0:T(8,128)(2,1)S(1)} %shard_map.37), channel_id=1, source_target_pairs={{0,8},{1,9},{2,10},{3,11},{4,12},{5,13},{6,14},{7,15},{8,0},{9,1},... | collective-permute-start | bytes 2359304 | tf_op jit(solution)/shard_map/ppermute | solution.py:208

commit v26 on v24

--- a/solution.py
+++ b/solution.py
@@ -96,12 +96,9 @@
                     row_ref[first + part + 2] = jnp.where(
                         lane < per_block, pltpu.roll(even, per_block, 1), odd
                     )
-                four = pl.ds(first, 4)
-                target = field_ref.at[four, :, pl.ds(start, 2 * per_block)]
-                copies.append(
-                    pltpu.make_async_copy(row_ref.at[four], target, sems.at[len(copies)])
-                )
-                copies[-1].start()
+        target = field_ref.at[:, :, pl.ds(start, 2 * per_block)]
+        copies.append(pltpu.make_async_copy(row_ref, target, sems.at[0]))
+        copies[-1].start()
         return copies
 
     def term(name):

time: 62.2 us -> 62.2 us (level)
  no operation moved by 1% of the time
where the time goes in v26:
time: 62.2 us; the launch traced here: 62.1 us
  waiting for transfers between devices  26 us (42%)
  starting transfers between devices  22.6 us (36%)
  Pallas kernels  11.9 us (19%)
  local copies, waits for them, and re-layouts  1 us (2%)
    ppermute x19, waiting for transfers between devices, move(): return lax.ppermute(array, AXES, pairs)  26 us
    ppermute x19, starting transfers between devices, move(): return lax.ppermute(array, AXES, pairs)  22.6 us
    pallas_call x8, Pallas kernels, add(): pl.pallas_call(functools.partial(add_shards, tuple(names), places, slots,...  11.5 us
  transfers between devices with their start and end apart: 19, of which 8 were waited for; matrix products, arithmetic and copies ran while one was open for 0% of the time, Pallas kernels for 16%

profile of v26, /device:TPU:0, one launch (start us, length us, event | category | flops | bytes accessed | tf_op | source)
XLA Modules:
  0.0 62.1 jit_solution(16040668463279699309)
XLA Ops:
  0.0 0.0 copy-start
  0.0 2.9 %collective-permute-start.1 = (bf16[2,12,64,128]{3,2,1,0:T(8,128)(2,1)}, bf16[2,12,64,128]{3,2,1,0:T(8,128)(2,1)S(1)}, u32[]{:S(2)}, u32[]{:S(2)}) collective-permute-start(bf16[2,12,64,128]{3,2,1,0:T(8,128)(2,1)} %bitcast.24), channel_id=1, source_target_pairs={{0,16},{1,17},{2,18},{3,19},{4,20},{5,21},{6,22},{7,23},{8,9},{9,8... | collective-permute-start | bytes 1179656 | tf_op jit(solution)/shard_map/ppermute | solution.py:205
  2.9 2.6 %collective-permute-start = (bf16[2,12,64,128]{3,2,1,0:T(8,128)(2,1)}, bf16[2,12,64,128]{3,2,1,0:T(8,128)(2,1)S(1)}, u32[]{:S(2)}, u32[]{:S(2)}) collective-permute-start(bf16[2,12,64,128]{3,2,1,0:T(8,128)(2,1)} %bitcast.25), channel_id=1, source_target_pairs={{0,4},{1,5},{2,6},{3,7},{4,0},{5,1},{6,2},{7,3},{8,12},{9,13},{10,... | collective-permute-start | bytes 1179656 | tf_op jit(solution)/shard_map/ppermute | solution.py:205
  5.5 1.6 %collective-permute-start.2 = (bf16[2,12,64,128]{3,2,1,0:T(8,128)(2,1)}, bf16[2,12,64,128]{3,2,1,0:T(8,128)(2,1)S(1)}, u32[]{:S(2)}, u32[]{:S(2)}) collective-permute-start(bf16[2,12,64,128]{3,2,1,0:T(8,128)(2,1)} %bitcast.26), channel_id=1, source_target_pairs={{0,2},{1,3},{2,0},{3,1},{4,6},{5,7},{6,4},{7,5},{8,10},{9,11},{10,... | collective-permute-start | bytes 1179656 | tf_op jit(solution)/shard_map/ppermute | solution.py:205
  7.1 1.5 %collective-permute-start.3 = (bf16[2,12,64,128]{3,2,1,0:T(8,128)(2,1)}, bf16[2,12,64,128]{3,2,1,0:T(8,128)(2,1)S(1)}, u32[]{:S(2)}, u32[]{:S(2)}) collective-permute-start(bf16[2,12,64,128]{3,2,1,0:T(8,128)(2,1)} %bitcast.27), channel_id=1, source_target_pairs={{0,1},{1,0},{2,3},{3,2},{4,5},{5,4},{6,7},{7,6},{8,24},{9,25},{10,... | collective-permute-start | bytes 1179656 | tf_op jit(solution)/shard_map/ppermute | solution.py:205
  8.6 0.0 collective-permute-start.5
  8.6 0.0 copy-done
  8.7 0.1 fusion
  8.8 0.2 collective-permute-done.1.refs_0_.refs_1_
  9.0 3.4 %collective-permute-start.4 = (bf16[2,12,64,128]{3,2,1,0:T(8,128)(2,1)S(1)}, bf16[2,12,64,128]{3,2,1,0:T(8,128)(2,1)S(1)}, u32[]{:S(2)}, u32[]{:S(2)}) collective-permute-start(bf16[2,12,64,128]{3,2,1,0:T(8,128)(2,1)S(1)} %collective-permute-done.1.refs_0_.refs_1_), channel_id=1, source_target_pairs={{0,1},{1,0},{2,3},{3,2},{4,5},{5,4},{6,7},{7,6},{8,24},{9,25},{10,... | collective-permute-start | bytes 1179656 | tf_op jit(solution)/shard_map/ppermute | solution.py:205
  12.4 0.1 multiply_cosine_fusion
  12.6 10.6 %collective-permute-done.refs_4_.refs_0_ = bf16[2,12,64,128]{3,2,1,0:T(8,128)(2,1)S(1)} collective-permute-done((bf16[2,12,64,128]{3,2,1,0:T(8,128)(2,1)}, bf16[2,12,64,128]{3,2,1,0:T(8,128)(2,1)S(1)}, u32[]{:S(2)}, u32[]{:S(2)}) %collective-permute-start) | collective-permute-done | bytes 393248 | tf_op jit(solution)/shard_map/ppermute | solution.py:205
  23.2 0.2 collective-permute-done.2.refs_3_.refs_2_.refs_1_
  23.4 0.0 collective-permute-done.3.refs_1_.refs_3_
  23.4 0.0 collective-permute-done.5.refs_4_
  23.4 0.0 collective-permute-done.4.refs_2_.refs_4_
  23.4 0.2 shard_map.28
  23.6 0.1 collective-permute-start.6
  23.7 1.5 %collective-permute-start.7 = (bf16[2,12,64,128]{3,2,1,0:T(8,128)(2,1)S(1)}, bf16[2,12,64,128]{3,2,1,0:T(8,128)(2,1)S(1)}, u32[]{:S(2)}, u32[]{:S(2)}) collective-permute-start(bf16[2,12,64,128]{3,2,1,0:T(8,128)(2,1)S(1)} %collective-permute-done.refs_4_.refs_0_), channel_id=1, source_target_pairs={{0,2},{1,3},{2,0},{3,1},{4,6},{5,7},{6,4},{7,5},{8,10},{9,11},{10,... | collective-permute-start | bytes 1179656 | tf_op jit(solution)/shard_map/ppermute | solution.py:205
  25.2 0.5 collective-permute-start.10
  25.7 1.5 %collective-permute-start.9 = (bf16[2,2,12,64,128]{4,3,2,1,0:T(8,128)(2,1)S(1)}, bf16[2,2,12,64,128]{4,3,2,1,0:T(8,128)(2,1)S(1)}, u32[]{:S(2)}, u32[]{:S(2)}) collective-permute-start(bf16[2,2,12,64,128]{4,3,2,1,0:T(8,128)(2,1)S(1)} %get-tuple-element.107), channel_id=1, source_target_pairs={{0,16},{1,17},{2,18},{3,19},{4,20},{5,21},{6,22},{7,23},{8,9},{9,8... | collective-permute-start | bytes 2359304 | tf_op jit(solution)/shard_map/ppermute | solution.py:205
  27.2 2.3 %collective-permute-start.8 = (bf16[2,12,64,128]{3,2,1,0:T(8,128)(2,1)S(1)}, bf16[2,12,64,128]{3,2,1,0:T(8,128)(2,1)S(1)}, u32[]{:S(2)}, u32[]{:S(2)}) collective-permute-start(bf16[2,12,64,128]{3,2,1,0:T(8,128)(2,1)S(1)} %collective-permute-done.4.refs_2_.refs_4_), channel_id=1, source_target_pairs={{0,4},{1,5},{2,6},{3,7},{4,0},{5,1},{6,2},{7,3},{8,12},{9,13},{10,... | collective-permute-start | bytes 1179656 | tf_op jit(solution)/shard_map/ppermute | solution.py:205
  29.5 0.0 copy-start.1
  29.5 1.0 %copy-done.1 = bf16[2,1,64,12,128]{4,2,3,1,0:T(8,128)(2,1)S(1)} copy-done((bf16[2,1,64,12,128]{4,2,3,1,0:T(8,128)(2,1)S(1)}, bf16[2,1,64,12,128]{4,2,3,1,0:T(8,128)(2,1)}, u32[]{:S(2)}) %copy-start.1) | copy-done | bytes 393240
  30.5 1.8 %shard_map.29.refs_7_ = f32[2,2,256,256]{3,2,1,0:T(8,128)S(1)} custom-call(f32[8,2,128]{2,1,0:T(2,128)S(1)} %maximum_bitcast_fusion.weights_ref, bf16[2,12,64,128]{3,2,1,0:T(8,128)(2,1)S(1)} %collective-permute-done.refs_4_.refs_0_, bf16[2,12,64,128]{3,2,1,0:T(8,128)(2,1)S(1)} %collective-permute-done.1.refs_0_.refs_1_, ...), custom_call_target="tpu_custom_call" | custom-call | flops 1207959552 | bytes 4456448 | tf_op jit(solution)/shard_map/pallas_call | solution.py:260
  32.3 0.0 collective-permute-done.6.refs_5_
  32.3 1.7 %shard_map.30.refs_1_ = f32[2,2,256,256]{3,2,1,0:T(8,128)S(1)} custom-call(f32[8,2,128]{2,1,0:T(2,128)S(1)} %maximum_bitcast_fusion.weights_ref, bf16[2,12,64,128]{3,2,1,0:T(8,128)(2,1)S(1)} %collective-permute-done.refs_4_.refs_0_, bf16[2,12,64,128]{3,2,1,0:T(8,128)(2,1)S(1)} %collective-permute-done.1.refs_0_.refs_1_, ...), custom_call_target="tpu_custom_call" | custom-call | flops 1207959552 | bytes 4456448 | tf_op jit(solution)/shard_map/pallas_call | solution.py:260
  34.0 7.6 %collective-permute-done.7.refs_0_.o3_ref.refs_2_ = bf16[2,12,64,128]{3,2,1,0:T(8,128)(2,1)S(1)} collective-permute-done((bf16[2,12,64,128]{3,2,1,0:T(8,128)(2,1)S(1)}, bf16[2,12,64,128]{3,2,1,0:T(8,128)(2,1)S(1)}, u32[]{:S(2)}, u32[]{:S(2)}) %collective-permute-start.7) | collective-permute-done | bytes 393248 | tf_op jit(solution)/shard_map/ppermute | solution.py:205
  41.6 2.4 %collective-permute-start.13 = (bf16[2,12,64,128]{3,2,1,0:T(8,128)(2,1)S(1)}, bf16[2,12,64,128]{3,2,1,0:T(8,128)(2,1)S(1)}, u32[]{:S(2)}, u32[]{:S(2)}) collective-permute-start(bf16[2,12,64,128]{3,2,1,0:T(8,128)(2,1)S(1)} %collective-permute-done.7.refs_0_.o3_ref.refs_2_), channel_id=1, source_target_pairs={{0,16},{1,17},{2,18},{3,19},{4,20},{5,21},{6,22},{7,23},{8,9},{9,8... | collective-permute-start | bytes 1179656 | tf_op jit(solution)/shard_map/ppermute | solution.py:205
  44.1 0.0 collective-permute-start.14
  44.1 0.4 shard_map.31.refs_5_
  44.5 2.7 %collective-permute-done.8.ab2_ref.refs_2_ = bf16[2,12,64,128]{3,2,1,0:T(8,128)(2,1)S(1)} collective-permute-done((bf16[2,12,64,128]{3,2,1,0:T(8,128)(2,1)S(1)}, bf16[2,12,64,128]{3,2,1,0:T(8,128)(2,1)S(1)}, u32[]{:S(2)}, u32[]{:S(2)}) %collective-permute-start.8) | collective-permute-done | bytes 393248 | tf_op jit(solution)/shard_map/ppermute | solution.py:205
  47.2 0.0 collective-permute-done.10.b12_ref.refs_4_
  47.2 0.0 collective-permute-done.9.a12_ref.refs_3_
  47.2 0.0 collective-permute-start.11
  47.2 0.2 shard_map.32
  47.4 0.1 collective-permute-start.15
  47.4 1.6 %collective-permute-start.12 = (bf16[2,12,64,128]{3,2,1,0:T(8,128)(2,1)S(1)}, bf16[2,12,64,128]{3,2,1,0:T(8,128)(2,1)S(1)}, u32[]{:S(2)}, u32[]{:S(2)}) collective-permute-start(bf16[2,12,64,128]{3,2,1,0:T(8,128)(2,1)S(1)} %get-tuple-element.117), channel_id=1, source_target_pairs={{0,1},{1,0},{2,3},{3,2},{4,5},{5,4},{6,7},{7,6},{8,24},{9,25},{10,... | collective-permute-start | bytes 1179656 | tf_op jit(solution)/shard_map/ppermute | solution.py:205
  49.0 1.6 %shard_map.33.refs_7_ = f32[2,2,256,256]{3,2,1,0:T(8,128)S(1)} custom-call(f32[8,2,128]{2,1,0:T(2,128)S(1)} %maximum_bitcast_fusion.weights_ref, bf16[2,12,64,128]{3,2,1,0:T(8,128)(2,1)S(1)} %collective-permute-done.refs_4_.refs_0_, bf16[2,12,64,128]{3,2,1,0:T(8,128)(2,1)S(1)} %collective-permute-done.2.refs_3_.refs_2_.refs_1_, ...), custom_call_target="tpu_custom_call" | custom-call | flops 1006632960 | bytes 4063232 | tf_op jit(solution)/shard_map/pallas_call | solution.py:260
  50.7 3.4 %collective-permute-done.13.a3_ref = bf16[2,12,64,128]{3,2,1,0:T(8,128)(2,1)S(1)} collective-permute-done((bf16[2,12,64,128]{3,2,1,0:T(8,128)(2,1)S(1)}, bf16[2,12,64,128]{3,2,1,0:T(8,128)(2,1)S(1)}, u32[]{:S(2)}, u32[]{:S(2)}) %collective-permute-start.13) | collective-permute-done | bytes 393248 | tf_op jit(solution)/shard_map/ppermute | solution.py:205
  54.0 0.0 collective-permute-done.14.ab3_ref
  54.0 0.1 shard_map.34.refs_5_
  54.1 0.1 collective-permute-start.16
  54.2 0.0 collective-permute-done.15.refs_6_
  54.2 2.3 %shard_map.35 = (f32[2,2,256,256]{3,2,1,0:T(8,128)S(1)}, bf16[6,512,768]{2,1,0:T(8,128)(2,1)S(1)}) custom-call(f32[8,2,128]{2,1,0:T(2,128)S(1)} %maximum_bitcast_fusion.weights_ref, bf16[2,12,64,128]{3,2,1,0:T(8,128)(2,1)S(1)} %collective-permute-done.refs_4_.refs_0_, bf16[2,12,64,128]{3,2,1,0:T(8,128)(2,1)S(1)} %collective-permute-done.2.refs_3_.refs_2_.refs_1_, ...), custom_call_target="tpu_custom_call" | custom-call | flops 16106127360 | bytes 5242880 | tf_op jit(solution)/shard_map/pallas_call | solution.py:260
  56.5 0.0 collective-permute-done.16.refs_0_
  56.5 0.7 %shard_map.36.refs_3_ = f32[2,2,256,256]{3,2,1,0:T(8,128)S(1)} custom-call(f32[8,2,128]{2,1,0:T(2,128)S(1)} %maximum_bitcast_fusion.weights_ref, bf16[2,2,12,64,128]{4,3,2,1,0:T(8,128)(2,1)S(1)} %collective-permute-done.16.refs_0_, bf16[6,512,768]{2,1,0:T(8,128)(2,1)S(1)} %get-tuple-element.148.refs_1_.refs_2_, f32[2,2,256,256]{3,2,1,0:T(8,128)S(1)} %get-tuple-element.139.refs_2_), custom_call_target="tpu_custom_call" | custom-call | flops 402653184 | bytes 2883584 | tf_op jit(solution)/shard_map/pallas_call | solution.py:260
  57.2 1.0 %collective-permute-done.12.refs_1_ = bf16[2,12,64,128]{3,2,1,0:T(8,128)(2,1)S(1)} collective-permute-done((bf16[2,12,64,128]{3,2,1,0:T(8,128)(2,1)S(1)}, bf16[2,12,64,128]{3,2,1,0:T(8,128)(2,1)S(1)}, u32[]{:S(2)}, u32[]{:S(2)}) %collective-permute-start.12) | collective-permute-done | bytes 393248 | tf_op jit(solution)/shard_map/ppermute | solution.py:205
  58.2 0.0 collective-permute-done.11.refs_0_
  58.2 0.0 collective-permute-start.17
  58.2 0.5 collective-permute-start.18
  58.7 1.4 %shard_map.37 = (f32[2,2,256,256]{3,2,1,0:T(8,128)S(1)}, f32[16,64,256]{2,1,0:T(8,128)}) custom-call(f32[8,2,128]{2,1,0:T(2,128)S(1)} %maximum_bitcast_fusion.weights_ref, bf16[2,12,64,128]{3,2,1,0:T(8,128)(2,1)S(1)} %collective-permute-done.11.refs_0_, bf16[2,12,64,128]{3,2,1,0:T(8,128)(2,1)S(1)} %collective-permute-done.12.refs_1_, ...), custom_call_target="tpu_custom_call" | custom-call | flops 402653184 | bytes 2883584 | tf_op jit(solution)/shard_map/pallas_call | solution.py:260
  60.1 0.0 collective-permute-done.17.refs_0_
  60.2 0.3 collective-permute-done.18.refs_1_
  60.5 1.6 %shard_map.38 = f32[16,64,256]{2,1,0:T(8,128)} custom-call(f32[8,2,128]{2,1,0:T(2,128)S(1)} %maximum_bitcast_fusion.weights_ref, bf16[2,12,64,128]{3,2,1,0:T(8,128)(2,1)S(1)} %collective-permute-done.17.refs_0_, bf16[2,12,64,128]{3,2,1,0:T(8,128)(2,1)S(1)} %collective-permute-done.18.refs_1_, ...), custom_call_target="tpu_custom_call", output_to_operand_aliasing={{}: (5, {})} | custom-call | flops 402653184 | bytes 2883584 | tf_op jit(solution)/shard_map/pallas_call | solution.py:260
  (5 shorter events, 0.1 us)
Async XLA Ops:
  0.0 8.6 %copy-start = (s32[4,3]{1,0:T(4,128)S(1)}, s32[4,3]{1,0:T(4,128)}, u32[]{:S(2)}) copy-start(s32[4,3]{1,0:T(4,128)} %param.3) | copy-start | bytes 148
  0.0 9.0 %collective-permute-start.1 = (bf16[2,12,64,128]{3,2,1,0:T(8,128)(2,1)}, bf16[2,12,64,128]{3,2,1,0:T(8,128)(2,1)S(1)}, u32[]{:S(2)}, u32[]{:S(2)}) collective-permute-start(bf16[2,12,64,128]{3,2,1,0:T(8,128)(2,1)} %bitcast.24), channel_id=1, source_target_pairs={{0,16},{1,17},{2,18},{3,19},{4,20},{5,21},{6,22},{7,23},{8,9},{9,8... | collective-permute-start | bytes 1179656 | tf_op jit(solution)/shard_map/ppermute | solution.py:205
  2.9 20.3 %collective-permute-start = (bf16[2,12,64,128]{3,2,1,0:T(8,128)(2,1)}, bf16[2,12,64,128]{3,2,1,0:T(8,128)(2,1)S(1)}, u32[]{:S(2)}, u32[]{:S(2)}) collective-permute-start(bf16[2,12,64,128]{3,2,1,0:T(8,128)(2,1)} %bitcast.25), channel_id=1, source_target_pairs={{0,4},{1,5},{2,6},{3,7},{4,0},{5,1},{6,2},{7,3},{8,12},{9,13},{10,... | collective-permute-start | bytes 1179656 | tf_op jit(solution)/shard_map/ppermute | solution.py:205
  5.5 17.8 %collective-permute-start.2 = (bf16[2,12,64,128]{3,2,1,0:T(8,128)(2,1)}, bf16[2,12,64,128]{3,2,1,0:T(8,128)(2,1)S(1)}, u32[]{:S(2)}, u32[]{:S(2)}) collective-permute-start(bf16[2,12,64,128]{3,2,1,0:T(8,128)(2,1)} %bitcast.26), channel_id=1, source_target_pairs={{0,2},{1,3},{2,0},{3,1},{4,6},{5,7},{6,4},{7,5},{8,10},{9,11},{10,... | collective-permute-start | bytes 1179656 | tf_op jit(solution)/shard_map/ppermute | solution.py:205
  7.1 16.3 %collective-permute-start.3 = (bf16[2,12,64,128]{3,2,1,0:T(8,128)(2,1)}, bf16[2,12,64,128]{3,2,1,0:T(8,128)(2,1)S(1)}, u32[]{:S(2)}, u32[]{:S(2)}) collective-permute-start(bf16[2,12,64,128]{3,2,1,0:T(8,128)(2,1)} %bitcast.27), channel_id=1, source_target_pairs={{0,1},{1,0},{2,3},{3,2},{4,5},{5,4},{6,7},{7,6},{8,24},{9,25},{10,... | collective-permute-start | bytes 1179656 | tf_op jit(solution)/shard_map/ppermute | solution.py:205
  8.6 14.8 %collective-permute-start.5 = (bf16[2,12,64,128]{3,2,1,0:T(8,128)(2,1)}, bf16[2,12,64,128]{3,2,1,0:T(8,128)(2,1)S(1)}, u32[]{:S(2)}, u32[]{:S(2)}) collective-permute-start(bf16[2,12,64,128]{3,2,1,0:T(8,128)(2,1)} %bitcast.28), channel_id=1, source_target_pairs={{0,8},{1,9},{2,10},{3,11},{4,12},{5,13},{6,14},{7,15},{8,0},{9,1},... | collective-permute-start | bytes 1179656 | tf_op jit(solution)/shard_map/ppermute | solution.py:205
  9.0 14.4 %collective-permute-start.4 = (bf16[2,12,64,128]{3,2,1,0:T(8,128)(2,1)S(1)}, bf16[2,12,64,128]{3,2,1,0:T(8,128)(2,1)S(1)}, u32[]{:S(2)}, u32[]{:S(2)}) collective-permute-start(bf16[2,12,64,128]{3,2,1,0:T(8,128)(2,1)S(1)} %collective-permute-done.1.refs_0_.refs_1_), channel_id=1, source_target_pairs={{0,1},{1,0},{2,3},{3,2},{4,5},{5,4},{6,7},{7,6},{8,24},{9,25},{10,... | collective-permute-start | bytes 1179656 | tf_op jit(solution)/shard_map/ppermute | solution.py:205
  23.6 8.7 %collective-permute-start.6 = (bf16[5,2,12,64,128]{4,3,2,1,0:T(8,128)(2,1)S(1)}, bf16[5,2,12,64,128]{4,3,2,1,0:T(8,128)(2,1)S(1)}, u32[]{:S(2)}, u32[]{:S(2)}) collective-permute-start(bf16[5,2,12,64,128]{4,3,2,1,0:T(8,128)(2,1)S(1)} %get-tuple-element.94), channel_id=1, source_target_pairs={{0,8},{1,9},{2,10},{3,11},{4,12},{5,13},{6,14},{7,15},{8,0},{9,1},... | collective-permute-start | bytes 5898248 | tf_op jit(solution)/shard_map/ppermute | solution.py:205
  23.7 18.0 %collective-permute-start.7 = (bf16[2,12,64,128]{3,2,1,0:T(8,128)(2,1)S(1)}, bf16[2,12,64,128]{3,2,1,0:T(8,128)(2,1)S(1)}, u32[]{:S(2)}, u32[]{:S(2)}) collective-permute-start(bf16[2,12,64,128]{3,2,1,0:T(8,128)(2,1)S(1)} %collective-permute-done.refs_4_.refs_0_), channel_id=1, source_target_pairs={{0,2},{1,3},{2,0},{3,1},{4,6},{5,7},{6,4},{7,5},{8,10},{9,11},{10,... | collective-permute-start | bytes 1179656 | tf_op jit(solution)/shard_map/ppermute | solution.py:205
  25.2 22.0 %collective-permute-start.10 = (bf16[2,2,12,64,128]{4,3,2,1,0:T(8,128)(2,1)S(1)}, bf16[2,2,12,64,128]{4,3,2,1,0:T(8,128)(2,1)S(1)}, u32[]{:S(2)}, u32[]{:S(2)}) collective-permute-start(bf16[2,2,12,64,128]{4,3,2,1,0:T(8,128)(2,1)S(1)} %get-tuple-element.107), channel_id=1, source_target_pairs={{0,1},{1,0},{2,3},{3,2},{4,5},{5,4},{6,7},{7,6},{8,24},{9,25},{10,... | collective-permute-start | bytes 2359304 | tf_op jit(solution)/shard_map/ppermute | solution.py:205
  25.7 21.5 %collective-permute-start.9 = (bf16[2,2,12,64,128]{4,3,2,1,0:T(8,128)(2,1)S(1)}, bf16[2,2,12,64,128]{4,3,2,1,0:T(8,128)(2,1)S(1)}, u32[]{:S(2)}, u32[]{:S(2)}) collective-permute-start(bf16[2,2,12,64,128]{4,3,2,1,0:T(8,128)(2,1)S(1)} %get-tuple-element.107), channel_id=1, source_target_pairs={{0,16},{1,17},{2,18},{3,19},{4,20},{5,21},{6,22},{7,23},{8,9},{9,8... | collective-permute-start | bytes 2359304 | tf_op jit(solution)/shard_map/ppermute | solution.py:205
  27.2 20.0 %collective-permute-start.8 = (bf16[2,12,64,128]{3,2,1,0:T(8,128)(2,1)S(1)}, bf16[2,12,64,128]{3,2,1,0:T(8,128)(2,1)S(1)}, u32[]{:S(2)}, u32[]{:S(2)}) collective-permute-start(bf16[2,12,64,128]{3,2,1,0:T(8,128)(2,1)S(1)} %collective-permute-done.4.refs_2_.refs_4_), channel_id=1, source_target_pairs={{0,4},{1,5},{2,6},{3,7},{4,0},{5,1},{6,2},{7,3},{8,12},{9,13},{10,... | collective-permute-start | bytes 1179656 | tf_op jit(solution)/shard_map/ppermute | solution.py:205
  29.5 1.0 %copy-start.1 = (bf16[2,1,64,12,128]{4,2,3,1,0:T(8,128)(2,1)S(1)}, bf16[2,1,64,12,128]{4,2,3,1,0:T(8,128)(2,1)}, u32[]{:S(2)}) copy-start(bf16[2,1,64,12,128]{4,2,3,1,0:T(8,128)(2,1)} %param.2) | copy-start | bytes 1179652
  41.6 12.4 %collective-permute-start.13 = (bf16[2,12,64,128]{3,2,1,0:T(8,128)(2,1)S(1)}, bf16[2,12,64,128]{3,2,1,0:T(8,128)(2,1)S(1)}, u32[]{:S(2)}, u32[]{:S(2)}) collective-permute-start(bf16[2,12,64,128]{3,2,1,0:T(8,128)(2,1)S(1)} %collective-permute-done.7.refs_0_.o3_ref.refs_2_), channel_id=1, source_target_pairs={{0,16},{1,17},{2,18},{3,19},{4,20},{5,21},{6,22},{7,23},{8,9},{9,8... | collective-permute-start | bytes 1179656 | tf_op jit(solution)/shard_map/ppermute | solution.py:205
  44.1 10.0 %collective-permute-start.14 = (bf16[2,12,64,128]{3,2,1,0:T(8,128)(2,1)S(1)}, bf16[2,12,64,128]{3,2,1,0:T(8,128)(2,1)S(1)}, u32[]{:S(2)}, u32[]{:S(2)}) collective-permute-start(bf16[2,12,64,128]{3,2,1,0:T(8,128)(2,1)S(1)} %collective-permute-done.7.refs_0_.o3_ref.refs_2_), channel_id=1, source_target_pairs={{0,1},{1,0},{2,3},{3,2},{4,5},{5,4},{6,7},{7,6},{8,24},{9,25},{10,... | collective-permute-start | bytes 1179656 | tf_op jit(solution)/shard_map/ppermute | solution.py:205
  47.2 11.1 %collective-permute-start.11 = (bf16[2,12,64,128]{3,2,1,0:T(8,128)(2,1)S(1)}, bf16[2,12,64,128]{3,2,1,0:T(8,128)(2,1)S(1)}, u32[]{:S(2)}, u32[]{:S(2)}) collective-permute-start(bf16[2,12,64,128]{3,2,1,0:T(8,128)(2,1)S(1)} %collective-permute-done.8.ab2_ref.refs_2_), channel_id=1, source_target_pairs={{0,2},{1,3},{2,0},{3,1},{4,6},{5,7},{6,4},{7,5},{8,10},{9,11},{10,... | collective-permute-start | bytes 1179656 | tf_op jit(solution)/shard_map/ppermute | solution.py:205
  47.4 6.8 %collective-permute-start.15 = (bf16[6,2,12,64,128]{4,3,2,1,0:T(8,128)(2,1)S(1)}, bf16[6,2,12,64,128]{4,3,2,1,0:T(8,128)(2,1)S(1)}, u32[]{:S(2)}, u32[]{:S(2)}) collective-permute-start(bf16[6,2,12,64,128]{4,3,2,1,0:T(8,128)(2,1)S(1)} %get-tuple-element.133), channel_id=1, source_target_pairs={{0,8},{1,9},{2,10},{3,11},{4,12},{5,13},{6,14},{7,15},{8,0},{9,1},... | collective-permute-start | bytes 7077896 | tf_op jit(solution)/shard_map/ppermute | solution.py:205
  47.4 10.8 %collective-permute-start.12 = (bf16[2,12,64,128]{3,2,1,0:T(8,128)(2,1)S(1)}, bf16[2,12,64,128]{3,2,1,0:T(8,128)(2,1)S(1)}, u32[]{:S(2)}, u32[]{:S(2)}) collective-permute-start(bf16[2,12,64,128]{3,2,1,0:T(8,128)(2,1)S(1)} %get-tuple-element.117), channel_id=1, source_target_pairs={{0,1},{1,0},{2,3},{3,2},{4,5},{5,4},{6,7},{7,6},{8,24},{9,25},{10,... | collective-permute-start | bytes 1179656 | tf_op jit(solution)/shard_map/ppermute | solution.py:205
  54.1 2.4 %collective-permute-start.16 = (bf16[2,2,12,64,128]{4,3,2,1,0:T(8,128)(2,1)S(1)}, bf16[2,2,12,64,128]{4,3,2,1,0:T(8,128)(2,1)S(1)}, u32[]{:S(2)}, u32[]{:S(2)}) collective-permute-start(bf16[2,2,12,64,128]{4,3,2,1,0:T(8,128)(2,1)S(1)} %shard_map.34.refs_5_), channel_id=1, source_target_pairs={{0,8},{1,9},{2,10},{3,11},{4,12},{5,13},{6,14},{7,15},{8,0},{9,1},... | collective-permute-start | bytes 2359304 | tf_op jit(solution)/shard_map/ppermute | solution.py:205
  58.2 1.9 %collective-permute-start.17 = (bf16[2,12,64,128]{3,2,1,0:T(8,128)(2,1)S(1)}, bf16[2,12,64,128]{3,2,1,0:T(8,128)(2,1)S(1)}, u32[]{:S(2)}, u32[]{:S(2)}) collective-permute-start(bf16[2,12,64,128]{3,2,1,0:T(8,128)(2,1)S(1)} %collective-permute-done.11.refs_0_), channel_id=1, source_target_pairs={{0,8},{1,9},{2,10},{3,11},{4,12},{5,13},{6,14},{7,15},{8,0},{9,1},... | collective-permute-start | bytes 1179656 | tf_op jit(solution)/shard_map/ppermute | solution.py:205
  58.2 2.3 %collective-permute-start.18 = (bf16[2,12,64,128]{3,2,1,0:T(8,128)(2,1)S(1)}, bf16[2,12,64,128]{3,2,1,0:T(8,128)(2,1)S(1)}, u32[]{:S(2)}, u32[]{:S(2)}) collective-permute-start(bf16[2,12,64,128]{3,2,1,0:T(8,128)(2,1)S(1)} %collective-permute-done.12.refs_1_), channel_id=1, source_target_pairs={{0,8},{1,9},{2,10},{3,11},{4,12},{5,13},{6,14},{7,15},{8,0},{9,1},... | collective-permute-start | bytes 1179656 | tf_op jit(solution)/shard_map/ppermute | solution.py:205
